TPU v7x, 32 devices: a whole 2x2x4 slice. The times are simulated.
32 devices in a mesh: img: 8 (over y, x, core), txt: 4 (over z).
Axes of the slice: x: 2, y: 2, z: 4, core: 2. Of those that a mesh axis runs over, the one named last changes fastest.
Arguments:
- image_embeds: bfloat16 [512, 1152], P(('img', 'txt')), may hold values from -0.1875 to 0.1875
- text_embeds: bfloat16 [512, 1152], P(('txt', 'img')), may hold values from -0.1875 to 0.1875
- pair_ids: int32 [512], P('img'), may hold values from 0 to 511, each once
Outputs:
- image_grad: float32 [512, 1152], P(('img', 'txt'))
- text_grad: float32 [512, 1152], P(('txt', 'img'))
Inputs may be any that keep to these rules, and one draw needn't show every extreme that they name: pair_ids is a permutation of the text rows.
All inputs are finite; a program needn't handle non-finite values.
Results may differ from a plain program's by a relative error of at most 0.0036.
Values may be sent and summed in bfloat16 or wider, within the bound.
No kernel may reach another device: no remote copies, remote signals or barrier semaphores. Data moves between devices by JAX's collectives and lax.ppermute only.
A program may use at most 64 MiB of HBM per device.

v0:
```python
import jax
import jax.numpy as jnp
from jax import lax
from jax.sharding import PartitionSpec as P

scale_logit = 8.0
shift_logit = -4.0
epsilon = 1e-06


def normalize(raw):
    values = raw.astype(jnp.float32)
    inverse = lax.rsqrt(jnp.sum(values * values, axis=-1, keepdims=True) + epsilon)
    return (values * inverse, inverse)


def back_norm(unit, inverse, grad):
    inner = jnp.sum(unit * grad, axis=-1, keepdims=True)
    return inverse * (grad - unit * inner)


def pair_coeff(logit, same):
    label = jnp.where(same, 1.0, -1.0).astype(jnp.float32)
    return (-scale_logit * label * jax.nn.sigmoid(-label * logit)).astype(jnp.bfloat16)


def local(image_embeds, text_embeds, pair_ids):
    img_unit, img_inv = normalize(image_embeds)
    txt_unit, txt_inv = normalize(text_embeds)
    img_low = img_unit.astype(jnp.bfloat16)
    txt_low = txt_unit.astype(jnp.bfloat16)
    img_block = lax.all_gather(img_low, "txt", axis=0, tiled=True)
    own_rows = text_embeds.shape[0]
    txt_rows = own_rows * lax.axis_size("img")
    offset = lax.axis_index("txt") * txt_rows
    piece = lax.all_gather(txt_low, "img", axis=0, tiled=True)
    scores = lax.dot_general(
        img_block, piece, (((1,), (1,)), ((), ())), preferred_element_type=jnp.float32
    )
    logit = scale_logit * scores + shift_logit
    columns = offset + lax.broadcasted_iota(jnp.int32, (1, piece.shape[0]), 1)
    coeff = pair_coeff(logit, pair_ids[:, None] == columns)
    img_acc = jnp.dot(coeff, piece, preferred_element_type=jnp.float32)
    txt_piece = lax.dot_general(
        coeff, img_block, (((0,), (0,)), ((), ())), preferred_element_type=jnp.float32
    )
    img_acc, second = (img_acc, txt_piece)
    txt_part = lax.psum_scatter(second, "img", scatter_dimension=0, tiled=True)
    img_part = lax.psum_scatter(img_acc, "txt", scatter_dimension=0, tiled=True)
    return (back_norm(img_unit, img_inv, img_part), back_norm(txt_unit, txt_inv, txt_part))


def solution(mesh):
    return jax.shard_map(
        local,
        mesh=mesh,
        in_specs=(P(("img", "txt"), None), P(("txt", "img"), None), P("img")),
        out_specs=(P(("img", "txt"), None), P(("txt", "img"), None)),
        check_vma=False,
    )
```

profile of v0, /device:TPU:0, one launch (start us, length us, event | category | flops | bytes accessed | tf_op | source)
XLA Modules:
  0.0 100.0 jit_solution(1796863856120895457)
XLA Ops:
  7.2 0.0 copy-start.1
  7.2 0.0 reduce-scatter.3.cloned.1.call-start
  7.2 0.9 fusion.17
  8.1 0.0 copy-done.1
  8.1 0.1 fusion.21
  8.3 0.0 copy-start
  8.3 0.1 fusion.10
  8.4 0.7 copy-done
  9.1 0.1 fusion.13
  9.1 15.1 %all_gather.6 = bf16[64,1152]{1,0:T(8,128)(2,1)S(1)} all-gather(bf16[16,1152]{1,0:T(8,128)(2,1)S(1)} %fusion.13), channel_id=1, replica_groups=mesh['img'=8,'txt'=4] {'txt'}, dimensions={0}, use_global_device_ids=true | all-gather | bytes 184320 | tf_op jit(solution)/shard_map/all_gather | solution.py:32
  24.3 9.6 %all_gather.7 = bf16[128,1152]{1,0:T(8,128)(2,1)S(1)} all-gather(bf16[16,1152]{1,0:T(8,128)(2,1)S(1)} %fusion.10), channel_id=1, replica_groups=mesh['img'=8,'txt'=4] {'img'}, dimensions={0}, use_global_device_ids=true | all-gather | bytes 331776 | tf_op jit(solution)/shard_map/all_gather | solution.py:36
  33.8 0.3 fusion.7
  34.1 0.9 fusion.22
  35.0 0.0 reduce-scatter.3.cloned.1.call-update
  35.0 0.0 reduce-scatter.5.cloned.1.call-start
  35.1 1.1 %fusion.23 = f32[128,1152]{1,0:T(8,128)} fusion(bf16[64,128]{1,0:T(8,128)(2,1)S(1)} %fusion.7, bf16[64,1152]{1,0:T(8,128)(2,1)S(1)} %all_gather.6), kind=kOutput, calls=%fused_computation.33 | convolution fusion | flops 18874368 | bytes 753664 | tf_op jit(solution)/shard_map/dot_general | solution.py:44
  36.2 0.0 reduce-scatter.5.cloned.1.call-update
  36.2 19.3 %reduce-scatter.3.cloned.1.call-done = f32[16,1152]{1,0:T(8,128)} async-done(((f32[64,1152]{1,0:T(8,128)}), f32[16,1152]{1,0:T(8,128)}) %reduce-scatter.3.cloned.1.call-update) | async-done | bytes 73744 | tf_op jit(solution)/shard_map/reduce_scatter | solution.py:49
  55.5 1.1 %fusion.14 = f32[16]{0:T(128)S(1)} fusion(f32[16,1152]{1,0:T(8,128)} %reduce-scatter.3.cloned.1.call-done, bf16[16,1152]{1,0:T(8,128)(2,1)S(1)} %copy-done, f32[16]{0:T(128)S(1)} %add_rsqrt_fusion.1), kind=kLoop, calls=%fused_computation.19 | loop fusion | flops 73712 | bytes 110720 | tf_op jit(solution)/shard_map/reduce_sum | solution.py:18
  56.7 0.0 copy-done.2
  56.7 0.7 fusion.16
  57.4 33.9 %reduce-scatter.5.cloned.1.call-done = f32[16,1152]{1,0:T(8,128)} async-done(((f32[128,1152]{1,0:T(8,128)}), f32[16,1152]{1,0:T(8,128)}) %reduce-scatter.5.cloned.1.call-update) | async-done | bytes 73744 | tf_op jit(solution)/shard_map/reduce_scatter | solution.py:48
  91.3 1.1 %fusion.18 = f32[16]{0:T(128)S(1)} fusion(f32[16,1152]{1,0:T(8,128)} %reduce-scatter.5.cloned.1.call-done, bf16[16,1152]{1,0:T(8,128)(2,1)S(1)} %copy-done.1, f32[16]{0:T(128)S(1)} %add_rsqrt_fusion), kind=kLoop, calls=%fused_computation.23 | loop fusion | flops 73712 | bytes 110720 | tf_op jit(solution)/shard_map/reduce_sum | solution.py:18
  92.4 0.7 fusion.20
  (8 shorter events, 0.0 us)
Async XLA Ops:
  7.2 1.0 copy-start.1
  7.2 48.3 %reduce-scatter.3.cloned.1.call-start = ((), (), s32[]{:S(2)}) async-start(), calls=%async_computation.2 | async-start | bytes 368640 | tf_op jit(solution)/shard_map/reduce_scatter | solution.py:49
  8.3 0.8 copy-start
  24.3 9.6 %copy-start.4 = (s32[64]{0:T(128)S(1)}, s32[64]{0:T(128)}, u32[]{:S(2)}) copy-start(s32[64]{0:T(128)} %param.5) | copy-start | bytes 772
  35.0 56.2 %reduce-scatter.5.cloned.1.call-start = ((), (), s32[]{:S(2)}) async-start(), calls=%async_computation.3 | async-start | bytes 663552 | tf_op jit(solution)/shard_map/reduce_scatter | solution.py:48
  55.5 1.2 %copy-start.2 = (f32[16,1152]{1,0:T(8,128)S(1)}, f32[16,1152]{1,0:T(8,128)}, u32[]{:S(2)}) copy-start(f32[16,1152]{1,0:T(8,128)} %reduce-scatter.3.cloned.1.call-done) | copy-start | bytes 221188
  91.3 1.1 %copy-start.3 = (f32[16,1152]{1,0:T(8,128)S(1)}, f32[16,1152]{1,0:T(8,128)}, u32[]{:S(2)}) copy-start(f32[16,1152]{1,0:T(8,128)} %reduce-scatter.5.cloned.1.call-done) | copy-start | bytes 221188
Sparse Core Ops, SparseCore 0:
  35.2 20.3 reduce-scatter.2
  58.6 32.6 reduce-scatter.4
where the time goes:
time: 100 us
  waiting for transfers between devices  53.3 us (53%)
  blocking collectives  24.7 us (25%)
  between operations  14.1 us (14%)
  other arithmetic  4.91 us (5%)
  matrix products  2.23 us (2%)
    reduce_scatter x1, waiting for transfers between devices, local(): txt_part = lax.psum_scatter(second, 'img', scatter_dimension=0, tiled=True)  33.9 us
    reduce_scatter x1, waiting for transfers between devices, local(): img_part = lax.psum_scatter(img_acc, 'txt', scatter_dimension=0, tiled=True)  19.3 us
    all_gather x1, blocking collectives, local(): img_block = lax.all_gather(img_low, 'txt', axis=0, tiled=True)  15.1 us
    all_gather x1, blocking collectives, local(): piece = lax.all_gather(txt_low, 'img', axis=0, tiled=True)  9.57 us
    reduce_sum x2, other arithmetic, back_norm(): inner = jnp.sum(unit * grad, axis=-1, keepdims=True)  2.29 us
  transfers between devices with their start and end apart: 2, of which 2 were waited for; matrix products, arithmetic and copies ran while one was open for 3% of the time, Pallas kernels for 0%

commit v1 on v0

v1 whole, which is shorter than its diff:
```python
import jax
import jax.numpy as jnp
from jax import lax
from jax.sharding import PartitionSpec as P

scale_logit = 8.0
shift_logit = -4.0
epsilon = 1e-06


def normalize(raw):
    values = raw.astype(jnp.float32)
    inverse = lax.rsqrt(jnp.sum(values * values, axis=-1, keepdims=True) + epsilon)
    return (values * inverse, inverse)


def back_norm(unit, inverse, grad):
    inner = jnp.sum(unit * grad, axis=-1, keepdims=True)
    return inverse * (grad - unit * inner)


def pair_coeff(logit, same):
    label = jnp.where(same, 1.0, -1.0).astype(jnp.float32)
    return (-scale_logit * label * jax.nn.sigmoid(-label * logit)).astype(jnp.bfloat16)


def swap(block, axis, distance):
    size = lax.axis_size(axis)
    return lax.ppermute(block, axis, [(i, i ^ distance) for i in range(size)])


def local(image_embeds, text_embeds, pair_ids):
    rows = image_embeds.shape[0]
    n_img = lax.axis_size("img")
    n_txt = lax.axis_size("txt")
    me_img = lax.axis_index("img")
    me_txt = lax.axis_index("txt")
    txt_raw = [text_embeds] + [swap(text_embeds, "img", k) for k in range(1, n_img)]
    img_raw = [image_embeds] + [swap(image_embeds, "txt", k) for k in range(1, n_txt)]
    img_owner = jnp.arange(n_txt, dtype=jnp.int32) ^ me_txt
    txt_owner = jnp.arange(n_img, dtype=jnp.int32) ^ me_img
    ids = pair_ids.reshape(n_txt, rows)[img_owner].reshape(-1)
    columns = (
        (me_txt * n_img + txt_owner)[:, None] * rows + jnp.arange(rows, dtype=jnp.int32)[None, :]
    ).reshape(-1)
    img_unit, img_inv = normalize(jnp.concatenate(img_raw))
    txt_unit, txt_inv = normalize(jnp.concatenate(txt_raw))
    img_low = img_unit.astype(jnp.bfloat16)
    txt_low = txt_unit.astype(jnp.bfloat16)
    scores = lax.dot_general(
        img_low, txt_low, (((1,), (1,)), ((), ())), preferred_element_type=jnp.float32
    )
    logit = scale_logit * scores + shift_logit
    coeff = pair_coeff(logit, ids[:, None] == columns[None, :])
    img_part = jnp.dot(coeff, txt_low, preferred_element_type=jnp.float32)
    txt_part = lax.dot_general(
        coeff, img_low, (((0,), (0,)), ((), ())), preferred_element_type=jnp.float32
    )
    txt_send = txt_part.astype(jnp.bfloat16)
    img_send = img_part.astype(jnp.bfloat16)
    txt_got = [swap(txt_send[k * rows:(k + 1) * rows], "img", k) for k in range(1, n_img)]
    img_got = [swap(img_send[k * rows:(k + 1) * rows], "txt", k) for k in range(1, n_txt)]
    txt_sum = txt_part[:rows]
    for block in txt_got:
        txt_sum = txt_sum + block.astype(jnp.float32)
    img_sum = img_part[:rows]
    for block in img_got:
        img_sum = img_sum + block.astype(jnp.float32)
    return (
        back_norm(img_unit[:rows], img_inv[:rows], img_sum),
        back_norm(txt_unit[:rows], txt_inv[:rows], txt_sum),
    )


def solution(mesh):
    return jax.shard_map(
        local,
        mesh=mesh,
        in_specs=(P(("img", "txt"), None), P(("txt", "img"), None), P("img")),
        out_specs=(P(("img", "txt"), None), P(("txt", "img"), None)),
        check_vma=False,
    )
```

time: 100 us -> 47.5 us (0.47)
  waiting for transfers between devices: 53.3 us -> 20.1 us
  blocking collectives: 24.7 us -> 0 us
  starting transfers between devices: 0.08 us -> 20.8 us
  between operations: 14.1 us -> 0.77 us
  other arithmetic: 4.91 us -> 2.31 us
  local copies, waits for them, and re-layouts: 0.71 us -> 2.43 us
  matrix products: 2.23 us -> 0.91 us
    reduce_scatter x2 -> x0, waiting for transfers between devices: 53.2 us -> none  [the longest x1 33.9 us: local(): txt_part = lax.psum_scatter(second, 'img', scatter_dimension=0, tiled=True)]
    all_gather x2 -> x0, blocking collectives: 24.7 us -> none  [the longest x1 15.1 us: local(): img_block = lax.all_gather(img_low, 'txt', axis=0, tiled=True)]
    ppermute x0 -> x20, starting transfers between devices: none -> 20.8 us  [swap(): return lax.ppermute(block, axis, [(i, i ^ distance) for i in range(size)])]
    ppermute x0 -> x20, waiting for transfers between devices: none -> 20.1 us  [swap(): return lax.ppermute(block, axis, [(i, i ^ distance) for i in range(size)])]
    reduce_sum x2, other arithmetic: 2.29 us -> 0.3 us  [back_norm(): inner = jnp.sum(unit * grad, axis=-1, keepdims=True)]
    dot_general x3, matrix products: 2.23 us -> 0.91 us  [the longest x1 0.34 us: local(): lax.dot_general(img_low, txt_low, (((1,), (1,)), ((), ())), preferred_ele...]
  transfers between devices with their start and end apart: 2 -> 20, of which waited for: 2 -> 7; matrix products, arithmetic and copies ran while one was open for 3% -> 7% of each run, Pallas kernels for 0% -> 0%
where the time goes in v1:
time: 47.5 us; the launch traced here: 47.3 us
  starting transfers between devices  20.8 us (44%)
  waiting for transfers between devices  20.1 us (42%)
  local copies, waits for them, and re-layouts  2.43 us (5%)
  other arithmetic  2.31 us (5%)
  matrix products  0.91 us (2%)
  between operations  0.77 us (2%)
    ppermute x20, starting transfers between devices, swap(): return lax.ppermute(block, axis, [(i, i ^ distance) for i in range(size)])  20.8 us
    ppermute x20, waiting for transfers between devices, swap(): return lax.ppermute(block, axis, [(i, i ^ distance) for i in range(size)])  20.1 us
    unnamed x13, local copies, waits for them, and re-layouts  1.58 us
    mul x2, other arithmetic, back_norm(): return inverse * (grad - unit * inner)  1.43 us
  transfers between devices with their start and end apart: 20, of which 7 were waited for; matrix products, arithmetic and copies ran while one was open for 7% of the time, Pallas kernels for 0%

profile of v1, /device:TPU:0, one launch (start us, length us, event | category | flops | bytes accessed | tf_op | source)
XLA Modules:
  0.0 47.3 jit_solution(12516445303304403906)
XLA Ops:
  0.6 4.1 %collective-permute-start.1 = (bf16[16,1152]{1,0:T(8,128)(2,1)}, bf16[16,1152]{1,0:T(8,128)(2,1)S(1)}, u32[]{:S(2)}, u32[]{:S(2)}) collective-permute-start(bf16[16,1152]{1,0:T(8,128)(2,1)} %param.3), channel_id=1, source_target_pairs={{0,2},{1,3},{2,0},{3,1},{4,6},{5,7},{6,4},{7,5},{8,10},{9,11},{10,... | collective-permute-start | bytes 110600 | tf_op jit(solution)/shard_map/ppermute | solution.py:29
  4.7 1.6 %collective-permute-start = (bf16[16,1152]{1,0:T(8,128)(2,1)}, bf16[16,1152]{1,0:T(8,128)(2,1)S(1)}, u32[]{:S(2)}, u32[]{:S(2)}) collective-permute-start(bf16[16,1152]{1,0:T(8,128)(2,1)} %param.3), channel_id=1, source_target_pairs={{0,1},{1,0},{2,3},{3,2},{4,5},{5,4},{6,7},{7,6},{8,9},{9,8},{10,11... | collective-permute-start | bytes 110600 | tf_op jit(solution)/shard_map/ppermute | solution.py:29
  6.3 2.7 %collective-permute-start.8 = (bf16[16,1152]{1,0:T(8,128)(2,1)}, bf16[16,1152]{1,0:T(8,128)(2,1)S(1)}, u32[]{:S(2)}, u32[]{:S(2)}) collective-permute-start(bf16[16,1152]{1,0:T(8,128)(2,1)} %param.4), channel_id=1, source_target_pairs={{0,24},{4,28},{8,16},{12,20},{16,8},{20,12},{24,0},{28,4},{1,25},{... | collective-permute-start | bytes 110600 | tf_op jit(solution)/shard_map/ppermute | solution.py:29
  9.0 0.8 %constant_dynamic-update-slice_fusion.7 = bf16[128,1152]{1,0:T(8,128)(2,1)S(1)} fusion(bf16[16,1152]{1,0:T(8,128)(2,1)} %param.4), kind=kLoop, calls=%fused_computation.46 | loop fusion | bytes 73728
  10.0 0.6 %gather_fusion = s32[4,16]{1,0:T(4,128)S(1)} fusion(s32[4,16]{1,0:T(4,128)S(1)} %reshape.81, s32[1024]{0:T(1024)S(1)} %pad_clamp_fusion), kind=kCustom, calls=%fused_computation | custom fusion | bytes 528 | tf_op jit(solution)/shard_map/gather | solution.py:42
  10.7 0.6 %collective-permute-start.4 = (bf16[16,1152]{1,0:T(8,128)(2,1)S(1)}, bf16[16,1152]{1,0:T(8,128)(2,1)S(1)}, u32[]{:S(2)}, u32[]{:S(2)}) collective-permute-start(bf16[16,1152]{1,0:T(8,128)(2,1)S(1)} %copy-done.1), channel_id=1, source_target_pairs={{0,8},{4,12},{8,0},{12,4},{16,24},{20,28},{24,16},{28,20},{1,9},{5... | collective-permute-start | bytes 110600 | tf_op jit(solution)/shard_map/ppermute | solution.py:29
  11.3 3.4 %collective-permute-done.4 = bf16[16,1152]{1,0:T(8,128)(2,1)S(1)} collective-permute-done((bf16[16,1152]{1,0:T(8,128)(2,1)S(1)}, bf16[16,1152]{1,0:T(8,128)(2,1)S(1)}, u32[]{:S(2)}, u32[]{:S(2)}) %collective-permute-start.4) | collective-permute-done | bytes 36896 | tf_op jit(solution)/shard_map/ppermute | solution.py:29
  14.7 3.4 %collective-permute-done.5 = bf16[16,1152]{1,0:T(8,128)(2,1)S(1)} collective-permute-done((bf16[16,1152]{1,0:T(8,128)(2,1)S(1)}, bf16[16,1152]{1,0:T(8,128)(2,1)S(1)}, u32[]{:S(2)}, u32[]{:S(2)}) %collective-permute-start.5) | collective-permute-done | bytes 36896 | tf_op jit(solution)/shard_map/ppermute | solution.py:29
  18.1 0.5 %collective-permute-start.6 = (bf16[16,1152]{1,0:T(8,128)(2,1)S(1)}, bf16[16,1152]{1,0:T(8,128)(2,1)S(1)}, u32[]{:S(2)}, u32[]{:S(2)}) collective-permute-start(bf16[16,1152]{1,0:T(8,128)(2,1)S(1)} %copy-done.1), channel_id=1, source_target_pairs={{0,16},{4,20},{8,24},{12,28},{16,0},{20,4},{24,8},{28,12},{1,17},{... | collective-permute-start | bytes 110600 | tf_op jit(solution)/shard_map/ppermute | solution.py:29
  18.6 3.4 %collective-permute-done.6 = bf16[16,1152]{1,0:T(8,128)(2,1)S(1)} collective-permute-done((bf16[16,1152]{1,0:T(8,128)(2,1)S(1)}, bf16[16,1152]{1,0:T(8,128)(2,1)S(1)}, u32[]{:S(2)}, u32[]{:S(2)}) %collective-permute-start.6) | collective-permute-done | bytes 36896 | tf_op jit(solution)/shard_map/ppermute | solution.py:29
  22.1 3.4 %collective-permute-done.7 = bf16[16,1152]{1,0:T(8,128)(2,1)S(1)} collective-permute-done((bf16[16,1152]{1,0:T(8,128)(2,1)S(1)}, bf16[16,1152]{1,0:T(8,128)(2,1)S(1)}, u32[]{:S(2)}, u32[]{:S(2)}) %collective-permute-start.7) | collective-permute-done | bytes 36896 | tf_op jit(solution)/shard_map/ppermute | solution.py:29
  25.8 0.7 %copy-done = bf16[16,1152]{1,0:T(8,128)(2,1)S(1)} copy-done((bf16[16,1152]{1,0:T(8,128)(2,1)S(1)}, bf16[16,1152]{1,0:T(8,128)(2,1)}, u32[]{:S(2)}) %copy-start) | copy-done | bytes 36888
  26.7 3.0 %collective-permute-done.9 = bf16[16,1152]{1,0:T(8,128)(2,1)S(1)} collective-permute-done((bf16[16,1152]{1,0:T(8,128)(2,1)S(1)}, bf16[16,1152]{1,0:T(8,128)(2,1)S(1)}, u32[]{:S(2)}, u32[]{:S(2)}) %collective-permute-start.9) | collective-permute-done | bytes 36896 | tf_op jit(solution)/shard_map/ppermute | solution.py:29
  31.3 2.5 %collective-permute-start.18 = (bf16[16,1152]{1,0:T(8,128)(2,1)S(1)}, bf16[16,1152]{1,0:T(8,128)(2,1)S(1)}, u32[]{:S(2)}, u32[]{:S(2)}) collective-permute-start(bf16[16,1152]{1,0:T(8,128)(2,1)S(1)} %get-tuple-element.6), channel_id=1, source_target_pairs={{0,24},{4,28},{8,16},{12,20},{16,8},{20,12},{24,0},{28,4},{1,25},{... | collective-permute-start | bytes 110600 | tf_op jit(solution)/shard_map/ppermute | solution.py:29
  34.2 1.0 %collective-permute-start.16 = (bf16[16,1152]{1,0:T(8,128)(2,1)S(1)}, bf16[16,1152]{1,0:T(8,128)(2,1)S(1)}, u32[]{:S(2)}, u32[]{:S(2)}) collective-permute-start(bf16[16,1152]{1,0:T(8,128)(2,1)S(1)} %get-tuple-element.8), channel_id=1, source_target_pairs={{0,16},{4,20},{8,24},{12,28},{16,0},{20,4},{24,8},{28,12},{1,17},{... | collective-permute-start | bytes 110600 | tf_op jit(solution)/shard_map/ppermute | solution.py:29
  35.6 1.0 %collective-permute-start.15 = (bf16[16,1152]{1,0:T(8,128)(2,1)S(1)}, bf16[16,1152]{1,0:T(8,128)(2,1)S(1)}, u32[]{:S(2)}, u32[]{:S(2)}) collective-permute-start(bf16[16,1152]{1,0:T(8,128)(2,1)S(1)} %get-tuple-element.9), channel_id=1, source_target_pairs={{0,12},{4,8},{8,4},{12,0},{16,28},{20,24},{24,20},{28,16},{1,13},{... | collective-permute-start | bytes 110600 | tf_op jit(solution)/shard_map/ppermute | solution.py:29
  36.6 1.1 %collective-permute-start.14 = (bf16[16,1152]{1,0:T(8,128)(2,1)S(1)}, bf16[16,1152]{1,0:T(8,128)(2,1)S(1)}, u32[]{:S(2)}, u32[]{:S(2)}) collective-permute-start(bf16[16,1152]{1,0:T(8,128)(2,1)S(1)} %get-tuple-element.10), channel_id=1, source_target_pairs={{0,8},{4,12},{8,0},{12,4},{16,24},{20,28},{24,16},{28,20},{1,9},{5... | collective-permute-start | bytes 110600 | tf_op jit(solution)/shard_map/ppermute | solution.py:29
  37.8 0.7 %collective-permute-start.10 = (bf16[16,1152]{1,0:T(8,128)(2,1)S(1)}, bf16[16,1152]{1,0:T(8,128)(2,1)S(1)}, u32[]{:S(2)}, u32[]{:S(2)}) collective-permute-start(bf16[16,1152]{1,0:T(8,128)(2,1)S(1)} %get-tuple-element.11), channel_id=1, source_target_pairs={{0,1},{1,0},{2,3},{3,2},{4,5},{5,4},{6,7},{7,6},{8,9},{9,8},{10,11... | collective-permute-start | bytes 110600 | tf_op jit(solution)/shard_map/ppermute | solution.py:29
  38.5 3.0 %collective-permute-start.12 = (bf16[16,1152]{1,0:T(8,128)(2,1)S(1)}, bf16[16,1152]{1,0:T(8,128)(2,1)S(1)}, u32[]{:S(2)}, u32[]{:S(2)}) collective-permute-start(bf16[16,1152]{1,0:T(8,128)(2,1)S(1)} %get-tuple-element.12), channel_id=1, source_target_pairs={{0,3},{1,2},{2,1},{3,0},{4,7},{5,6},{6,5},{7,4},{8,11},{9,10},{10,... | collective-permute-start | bytes 110600 | tf_op jit(solution)/shard_map/ppermute | solution.py:29
  41.6 0.5 %collective-permute-start.11 = (bf16[16,1152]{1,0:T(8,128)(2,1)S(1)}, bf16[16,1152]{1,0:T(8,128)(2,1)S(1)}, u32[]{:S(2)}, u32[]{:S(2)}) collective-permute-start(bf16[16,1152]{1,0:T(8,128)(2,1)S(1)} %get-tuple-element.13), channel_id=1, source_target_pairs={{0,2},{1,3},{2,0},{3,1},{4,6},{5,7},{6,4},{7,5},{8,10},{9,11},{10,... | collective-permute-start | bytes 110600 | tf_op jit(solution)/shard_map/ppermute | solution.py:29
  42.3 0.7 %subtract_multiply_fusion = f32[16,1152]{1,0:T(8,128)} fusion(f32[16,1152]{1,0:T(8,128)S(1)} %get-tuple-element.3, f32[128,1152]{1,0:T(8,128)S(1)} %convert_multiply_fusion, f32[16]{0:T(128)S(1)} %get-tuple-element.2, f32[16]{0:T(128)S(1)} %bitcast.6), kind=kLoop, calls=%fused_computation.30 | loop fusion | flops 55296 | bytes 221312 | tf_op jit(solution)/shard_map/mul | solution.py:19
  43.0 1.4 %collective-permute-done.12 = bf16[16,1152]{1,0:T(8,128)(2,1)S(1)} collective-permute-done((bf16[16,1152]{1,0:T(8,128)(2,1)S(1)}, bf16[16,1152]{1,0:T(8,128)(2,1)S(1)}, u32[]{:S(2)}, u32[]{:S(2)}) %collective-permute-start.12) | collective-permute-done | bytes 36896 | tf_op jit(solution)/shard_map/ppermute | solution.py:29
  44.4 2.1 %collective-permute-done.11 = bf16[16,1152]{1,0:T(8,128)(2,1)S(1)} collective-permute-done((bf16[16,1152]{1,0:T(8,128)(2,1)S(1)}, bf16[16,1152]{1,0:T(8,128)(2,1)S(1)}, u32[]{:S(2)}, u32[]{:S(2)}) %collective-permute-start.11) | collective-permute-done | bytes 36896 | tf_op jit(solution)/shard_map/ppermute | solution.py:29
  46.6 0.7 %subtract_multiply_fusion.1 = f32[16,1152]{1,0:T(8,128)} fusion(f32[64,1152]{1,0:T(8,128)S(1)} %convert_multiply_fusion.2, f32[16]{0:T(128)S(1)} %multiply_reduce_fusion.1, f32[16]{0:T(128)S(1)} %bitcast.7, bf16[16,1152]{1,0:T(8,128)(2,1)S(1)} %collective-permute-done.12, bf16[16,1152]{1,0:T(8,128)(2,1)S(1)} %collective-permute-done.11, ...), kind=kLoop, calls=%fused_computation.32 | loop fusion | flops 165888 | bytes 331904 | tf_op jit(solution)/shard_map/mul | solution.py:19
  (53 shorter events, 3.5 us)
Async XLA Ops:
  0.6 25.2 %collective-permute-start.1 = (bf16[16,1152]{1,0:T(8,128)(2,1)}, bf16[16,1152]{1,0:T(8,128)(2,1)S(1)}, u32[]{:S(2)}, u32[]{:S(2)}) collective-permute-start(bf16[16,1152]{1,0:T(8,128)(2,1)} %param.3), channel_id=1, source_target_pairs={{0,2},{1,3},{2,0},{3,1},{4,6},{5,7},{6,4},{7,5},{8,10},{9,11},{10,... | collective-permute-start | bytes 110600 | tf_op jit(solution)/shard_map/ppermute | solution.py:29
  4.7 21.1 %collective-permute-start = (bf16[16,1152]{1,0:T(8,128)(2,1)}, bf16[16,1152]{1,0:T(8,128)(2,1)S(1)}, u32[]{:S(2)}, u32[]{:S(2)}) collective-permute-start(bf16[16,1152]{1,0:T(8,128)(2,1)} %param.3), channel_id=1, source_target_pairs={{0,1},{1,0},{2,3},{3,2},{4,5},{5,4},{6,7},{7,6},{8,9},{9,8},{10,11... | collective-permute-start | bytes 110600 | tf_op jit(solution)/shard_map/ppermute | solution.py:29
  6.3 19.5 %collective-permute-start.2 = (bf16[16,1152]{1,0:T(8,128)(2,1)}, bf16[16,1152]{1,0:T(8,128)(2,1)S(1)}, u32[]{:S(2)}, u32[]{:S(2)}) collective-permute-start(bf16[16,1152]{1,0:T(8,128)(2,1)} %param.3), channel_id=1, source_target_pairs={{0,3},{1,2},{2,1},{3,0},{4,7},{5,6},{6,5},{7,4},{8,11},{9,10},{10,... | collective-permute-start | bytes 110600 | tf_op jit(solution)/shard_map/ppermute | solution.py:29
  6.3 19.5 %collective-permute-start.8 = (bf16[16,1152]{1,0:T(8,128)(2,1)}, bf16[16,1152]{1,0:T(8,128)(2,1)S(1)}, u32[]{:S(2)}, u32[]{:S(2)}) collective-permute-start(bf16[16,1152]{1,0:T(8,128)(2,1)} %param.4), channel_id=1, source_target_pairs={{0,24},{4,28},{8,16},{12,20},{16,8},{20,12},{24,0},{28,4},{1,25},{... | collective-permute-start | bytes 110600 | tf_op jit(solution)/shard_map/ppermute | solution.py:29
  9.0 1.7 %collective-permute-start.3 = (bf16[16,1152]{1,0:T(8,128)(2,1)}, bf16[16,1152]{1,0:T(8,128)(2,1)S(1)}, u32[]{:S(2)}, u32[]{:S(2)}) collective-permute-start(bf16[16,1152]{1,0:T(8,128)(2,1)} %param.4), channel_id=1, source_target_pairs={{0,4},{4,0},{8,12},{12,8},{16,20},{20,16},{24,28},{28,24},{1,5},{5... | collective-permute-start | bytes 110600 | tf_op jit(solution)/shard_map/ppermute | solution.py:29
  9.0 0.9 %copy-start.2 = (s32[64]{0:T(128)S(1)}, s32[64]{0:T(128)}, u32[]{:S(2)}) copy-start(s32[64]{0:T(128)} %param.5) | copy-start | bytes 772
  9.8 0.9 %copy-start.1 = (bf16[16,1152]{1,0:T(8,128)(2,1)S(1)}, bf16[16,1152]{1,0:T(8,128)(2,1)}, u32[]{:S(2)}) copy-start(bf16[16,1152]{1,0:T(8,128)(2,1)} %param.4) | copy-start | bytes 110596
  10.7 4.0 %collective-permute-start.4 = (bf16[16,1152]{1,0:T(8,128)(2,1)S(1)}, bf16[16,1152]{1,0:T(8,128)(2,1)S(1)}, u32[]{:S(2)}, u32[]{:S(2)}) collective-permute-start(bf16[16,1152]{1,0:T(8,128)(2,1)S(1)} %copy-done.1), channel_id=1, source_target_pairs={{0,8},{4,12},{8,0},{12,4},{16,24},{20,28},{24,16},{28,20},{1,9},{5... | collective-permute-start | bytes 110600 | tf_op jit(solution)/shard_map/ppermute | solution.py:29
  14.7 3.4 %collective-permute-start.5 = (bf16[16,1152]{1,0:T(8,128)(2,1)S(1)}, bf16[16,1152]{1,0:T(8,128)(2,1)S(1)}, u32[]{:S(2)}, u32[]{:S(2)}) collective-permute-start(bf16[16,1152]{1,0:T(8,128)(2,1)S(1)} %copy-done.1), channel_id=1, source_target_pairs={{0,12},{4,8},{8,4},{12,0},{16,28},{20,24},{24,20},{28,16},{1,13},{... | collective-permute-start | bytes 110600 | tf_op jit(solution)/shard_map/ppermute | solution.py:29
  18.1 4.0 %collective-permute-start.6 = (bf16[16,1152]{1,0:T(8,128)(2,1)S(1)}, bf16[16,1152]{1,0:T(8,128)(2,1)S(1)}, u32[]{:S(2)}, u32[]{:S(2)}) collective-permute-start(bf16[16,1152]{1,0:T(8,128)(2,1)S(1)} %copy-done.1), channel_id=1, source_target_pairs={{0,16},{4,20},{8,24},{12,28},{16,0},{20,4},{24,8},{28,12},{1,17},{... | collective-permute-start | bytes 110600 | tf_op jit(solution)/shard_map/ppermute | solution.py:29
  22.1 3.4 %collective-permute-start.7 = (bf16[16,1152]{1,0:T(8,128)(2,1)S(1)}, bf16[16,1152]{1,0:T(8,128)(2,1)S(1)}, u32[]{:S(2)}, u32[]{:S(2)}) collective-permute-start(bf16[16,1152]{1,0:T(8,128)(2,1)S(1)} %copy-done.1), channel_id=1, source_target_pairs={{0,20},{4,16},{8,28},{12,24},{16,4},{20,0},{24,12},{28,8},{1,21},{... | collective-permute-start | bytes 110600 | tf_op jit(solution)/shard_map/ppermute | solution.py:29
  25.5 4.3 %collective-permute-start.9 = (bf16[16,1152]{1,0:T(8,128)(2,1)S(1)}, bf16[16,1152]{1,0:T(8,128)(2,1)S(1)}, u32[]{:S(2)}, u32[]{:S(2)}) collective-permute-start(bf16[16,1152]{1,0:T(8,128)(2,1)S(1)} %copy-done.1), channel_id=1, source_target_pairs={{0,28},{4,24},{8,20},{12,16},{16,12},{20,8},{24,4},{28,0},{1,29},{... | collective-permute-start | bytes 110600 | tf_op jit(solution)/shard_map/ppermute | solution.py:29
  25.8 0.8 %copy-start = (bf16[16,1152]{1,0:T(8,128)(2,1)S(1)}, bf16[16,1152]{1,0:T(8,128)(2,1)}, u32[]{:S(2)}) copy-start(bf16[16,1152]{1,0:T(8,128)(2,1)} %param.3) | copy-start | bytes 110596
  30.7 4.9 %collective-permute-start.13 = (bf16[16,1152]{1,0:T(8,128)(2,1)S(1)}, bf16[16,1152]{1,0:T(8,128)(2,1)S(1)}, u32[]{:S(2)}, u32[]{:S(2)}) collective-permute-start(bf16[16,1152]{1,0:T(8,128)(2,1)S(1)} %get-tuple-element.4), channel_id=1, source_target_pairs={{0,4},{4,0},{8,12},{12,8},{16,20},{20,16},{24,28},{28,24},{1,5},{5... | collective-permute-start | bytes 110600 | tf_op jit(solution)/shard_map/ppermute | solution.py:29
  30.8 5.8 %collective-permute-start.19 = (bf16[16,1152]{1,0:T(8,128)(2,1)S(1)}, bf16[16,1152]{1,0:T(8,128)(2,1)S(1)}, u32[]{:S(2)}, u32[]{:S(2)}) collective-permute-start(bf16[16,1152]{1,0:T(8,128)(2,1)S(1)} %get-tuple-element.5), channel_id=1, source_target_pairs={{0,28},{4,24},{8,20},{12,16},{16,12},{20,8},{24,4},{28,0},{1,29},{... | collective-permute-start | bytes 110600 | tf_op jit(solution)/shard_map/ppermute | solution.py:29
  31.3 6.5 %collective-permute-start.18 = (bf16[16,1152]{1,0:T(8,128)(2,1)S(1)}, bf16[16,1152]{1,0:T(8,128)(2,1)S(1)}, u32[]{:S(2)}, u32[]{:S(2)}) collective-permute-start(bf16[16,1152]{1,0:T(8,128)(2,1)S(1)} %get-tuple-element.6), channel_id=1, source_target_pairs={{0,24},{4,28},{8,16},{12,20},{16,8},{20,12},{24,0},{28,4},{1,25},{... | collective-permute-start | bytes 110600 | tf_op jit(solution)/shard_map/ppermute | solution.py:29
  33.8 4.7 %collective-permute-start.17 = (bf16[16,1152]{1,0:T(8,128)(2,1)S(1)}, bf16[16,1152]{1,0:T(8,128)(2,1)S(1)}, u32[]{:S(2)}, u32[]{:S(2)}) collective-permute-start(bf16[16,1152]{1,0:T(8,128)(2,1)S(1)} %get-tuple-element.7), channel_id=1, source_target_pairs={{0,20},{4,16},{8,28},{12,24},{16,4},{20,0},{24,12},{28,8},{1,21},{... | collective-permute-start | bytes 110600 | tf_op jit(solution)/shard_map/ppermute | solution.py:29
  34.2 7.3 %collective-permute-start.16 = (bf16[16,1152]{1,0:T(8,128)(2,1)S(1)}, bf16[16,1152]{1,0:T(8,128)(2,1)S(1)}, u32[]{:S(2)}, u32[]{:S(2)}) collective-permute-start(bf16[16,1152]{1,0:T(8,128)(2,1)S(1)} %get-tuple-element.8), channel_id=1, source_target_pairs={{0,16},{4,20},{8,24},{12,28},{16,0},{20,4},{24,8},{28,12},{1,17},{... | collective-permute-start | bytes 110600 | tf_op jit(solution)/shard_map/ppermute | solution.py:29
  35.6 6.5 %collective-permute-start.15 = (bf16[16,1152]{1,0:T(8,128)(2,1)S(1)}, bf16[16,1152]{1,0:T(8,128)(2,1)S(1)}, u32[]{:S(2)}, u32[]{:S(2)}) collective-permute-start(bf16[16,1152]{1,0:T(8,128)(2,1)S(1)} %get-tuple-element.9), channel_id=1, source_target_pairs={{0,12},{4,8},{8,4},{12,0},{16,28},{20,24},{24,20},{28,16},{1,13},{... | collective-permute-start | bytes 110600 | tf_op jit(solution)/shard_map/ppermute | solution.py:29
  36.6 5.5 %collective-permute-start.14 = (bf16[16,1152]{1,0:T(8,128)(2,1)S(1)}, bf16[16,1152]{1,0:T(8,128)(2,1)S(1)}, u32[]{:S(2)}, u32[]{:S(2)}) collective-permute-start(bf16[16,1152]{1,0:T(8,128)(2,1)S(1)} %get-tuple-element.10), channel_id=1, source_target_pairs={{0,8},{4,12},{8,0},{12,4},{16,24},{20,28},{24,16},{28,20},{1,9},{5... | collective-permute-start | bytes 110600 | tf_op jit(solution)/shard_map/ppermute | solution.py:29
  37.8 5.2 %collective-permute-start.10 = (bf16[16,1152]{1,0:T(8,128)(2,1)S(1)}, bf16[16,1152]{1,0:T(8,128)(2,1)S(1)}, u32[]{:S(2)}, u32[]{:S(2)}) collective-permute-start(bf16[16,1152]{1,0:T(8,128)(2,1)S(1)} %get-tuple-element.11), channel_id=1, source_target_pairs={{0,1},{1,0},{2,3},{3,2},{4,5},{5,4},{6,7},{7,6},{8,9},{9,8},{10,11... | collective-permute-start | bytes 110600 | tf_op jit(solution)/shard_map/ppermute | solution.py:29
  38.5 5.8 %collective-permute-start.12 = (bf16[16,1152]{1,0:T(8,128)(2,1)S(1)}, bf16[16,1152]{1,0:T(8,128)(2,1)S(1)}, u32[]{:S(2)}, u32[]{:S(2)}) collective-permute-start(bf16[16,1152]{1,0:T(8,128)(2,1)S(1)} %get-tuple-element.12), channel_id=1, source_target_pairs={{0,3},{1,2},{2,1},{3,0},{4,7},{5,6},{6,5},{7,4},{8,11},{9,10},{10,... | collective-permute-start | bytes 110600 | tf_op jit(solution)/shard_map/ppermute | solution.py:29
  41.6 4.9 %collective-permute-start.11 = (bf16[16,1152]{1,0:T(8,128)(2,1)S(1)}, bf16[16,1152]{1,0:T(8,128)(2,1)S(1)}, u32[]{:S(2)}, u32[]{:S(2)}) collective-permute-start(bf16[16,1152]{1,0:T(8,128)(2,1)S(1)} %get-tuple-element.13), channel_id=1, source_target_pairs={{0,2},{1,3},{2,0},{3,1},{4,6},{5,7},{6,4},{7,5},{8,10},{9,11},{10,... | collective-permute-start | bytes 110600 | tf_op jit(solution)/shard_map/ppermute | solution.py:29

commit v2 on v1

v2 whole, which is shorter than its diff:
```python
import jax
import jax.numpy as jnp
from jax import lax
from jax.sharding import PartitionSpec as P

scale_logit = 8.0
shift_logit = -4.0
epsilon = 1e-06


def normalize(raw):
    values = raw.astype(jnp.float32)
    inverse = lax.rsqrt(jnp.sum(values * values, axis=-1, keepdims=True) + epsilon)
    return (values * inverse, inverse)


def back_norm(unit, inverse, grad):
    inner = jnp.sum(unit * grad, axis=-1, keepdims=True)
    return inverse * (grad - unit * inner)


def pair_coeff(logit, same):
    label = jnp.where(same, 1.0, -1.0).astype(jnp.float32)
    return (-scale_logit * label * jax.nn.sigmoid(-label * logit)).astype(jnp.bfloat16)


def spread(block, axis):
    copies = jnp.broadcast_to(block[None], (lax.axis_size(axis),) + block.shape)
    got = lax.all_to_all(copies, axis, split_axis=0, concat_axis=0)
    return got.reshape(-1, block.shape[1])


def local(image_embeds, text_embeds, pair_ids):
    rows = image_embeds.shape[0]
    n_img = lax.axis_size("img")
    n_txt = lax.axis_size("txt")
    me_img = lax.axis_index("img")
    me_txt = lax.axis_index("txt")
    txt_raw = spread(text_embeds, "img")
    img_raw = spread(image_embeds, "txt")
    columns = me_txt * n_img * rows + jnp.arange(n_img * rows, dtype=jnp.int32)
    img_unit, _ = normalize(img_raw)
    txt_unit, _ = normalize(txt_raw)
    img_low = img_unit.astype(jnp.bfloat16)
    txt_low = txt_unit.astype(jnp.bfloat16)
    scores = lax.dot_general(
        img_low, txt_low, (((1,), (1,)), ((), ())), preferred_element_type=jnp.float32
    )
    logit = scale_logit * scores + shift_logit
    coeff = pair_coeff(logit, pair_ids[:, None] == columns[None, :])
    img_part = jnp.dot(coeff, txt_low, preferred_element_type=jnp.float32)
    txt_part = lax.dot_general(
        coeff, img_low, (((0,), (0,)), ((), ())), preferred_element_type=jnp.float32
    )
    txt_send = txt_part.astype(jnp.bfloat16)
    img_send = img_part.astype(jnp.bfloat16)
    txt_got = lax.all_to_all(txt_send, "img", split_axis=0, concat_axis=0, tiled=True)
    img_got = lax.all_to_all(img_send, "txt", split_axis=0, concat_axis=0, tiled=True)
    txt_sum = jnp.sum(txt_got.reshape(n_img, rows, -1).astype(jnp.float32), axis=0)
    img_sum = jnp.sum(img_got.reshape(n_txt, rows, -1).astype(jnp.float32), axis=0)
    own_img = normalize(image_embeds)
    own_txt = normalize(text_embeds)
    return (back_norm(*own_img, img_sum), back_norm(*own_txt, txt_sum))


def solution(mesh):
    return jax.shard_map(
        local,
        mesh=mesh,
        in_specs=(P(("img", "txt"), None), P(("txt", "img"), None), P("img")),
        out_specs=(P(("img", "txt"), None), P(("txt", "img"), None)),
        check_vma=False,
    )
```

time: 47.5 us -> 50.4 us (1.061); the launches traced: 47.3 us -> 49.7 us
  starting transfers between devices: 20.8 us -> 16.9 us
  waiting for transfers between devices: 20.1 us -> 23.5 us
  matrix products: 0.91 us -> 2.1 us
  local copies, waits for them, and re-layouts: 2.43 us -> 3.6 us
  other arithmetic: 2.31 us -> 2.84 us
    all_to_all x0 -> x4, waiting for transfers between devices: none -> 23.5 us  [the longest x2 12.2 us: spread(): got = lax.all_to_all(copies, axis, split_axis=0, concat_axis=0)]
    ppermute x20 -> x0, starting transfers between devices: 20.8 us -> none  [swap(): return lax.ppermute(block, axis, [(i, i ^ distance) for i in range(size)])]
    ppermute x20 -> x0, waiting for transfers between devices: 20.1 us -> none  [swap(): return lax.ppermute(block, axis, [(i, i ^ distance) for i in range(size)])]
    all_to_all x0 -> x4, starting transfers between devices: none -> 16.9 us  [the longest x2 10.2 us: spread(): got = lax.all_to_all(copies, axis, split_axis=0, concat_axis=0)]
    broadcast_in_dim x0 -> x2, local copies, waits for them, and re-layouts: none -> 2.16 us  [spread(): copies = jnp.broadcast_to(block[None], (lax.axis_size(axis),) + block.shape)]
    dot_general x1, matrix products: 0.3 us -> 0.97 us  [local(): lax.dot_general(coeff, img_low, (((0,), (0,)), ((), ())), preferred_eleme...]
    dot_general x1, matrix products: 0.27 us -> 0.86 us  [local(): img_part = jnp.dot(coeff, txt_low, preferred_element_type=jnp.float32)]
    gather x1 -> x0, local copies, waits for them, and re-layouts: 0.56 us -> none  [local(): ids = pair_ids.reshape(n_txt, rows)[img_owner].reshape(-1)]
  transfers between devices with their start and end apart: 20 -> 4, of which waited for: 7 -> 4; matrix products, arithmetic and copies ran while one was open for 7% -> 5% of each run, Pallas kernels for 0% -> 0%
where the time goes in v2:
time: 50.4 us; the launch traced here: 49.7 us
  waiting for transfers between devices  23.5 us (47%)
  starting transfers between devices  16.9 us (34%)
  local copies, waits for them, and re-layouts  3.6 us (7%)
  other arithmetic  2.84 us (6%)
  matrix products  2.1 us (4%)
  between operations  0.72 us (1%)
    all_to_all x2, waiting for transfers between devices, spread(): got = lax.all_to_all(copies, axis, split_axis=0, concat_axis=0)  12.2 us
    all_to_all x2, starting transfers between devices, spread(): got = lax.all_to_all(copies, axis, split_axis=0, concat_axis=0)  10.2 us
    all_to_all x1, waiting for transfers between devices, local(): lax.all_to_all(txt_send, 'img', split_axis=0, concat_axis=0, tiled=True)  6.28 us
    all_to_all x1, waiting for transfers between devices, local(): lax.all_to_all(img_send, 'txt', split_axis=0, concat_axis=0, tiled=True)  4.97 us
    all_to_all x1, starting transfers between devices, local(): lax.all_to_all(txt_send, 'img', split_axis=0, concat_axis=0, tiled=True)  3.42 us
    all_to_all x1, starting transfers between devices, local(): lax.all_to_all(img_send, 'txt', split_axis=0, concat_axis=0, tiled=True)  3.33 us
    broadcast_in_dim x2, local copies, waits for them, and re-layouts, spread(): copies = jnp.broadcast_to(block[None], (lax.axis_size(axis),) + block.shape)  2.16 us
    mul x2, other arithmetic, back_norm(): return inverse * (grad - unit * inner)  1.44 us
  transfers between devices with their start and end apart: 4, of which 4 were waited for; matrix products, arithmetic and copies ran while one was open for 5% of the time, Pallas kernels for 0%

profile of v2, /device:TPU:0, one launch (start us, length us, event | category | flops | bytes accessed | tf_op | source)
XLA Modules:
  0.0 49.7 jit_solution(13970353564970956670)
XLA Ops:
  0.6 1.4 %broadcast_in_dim.12 = bf16[4,16,1152]{2,1,0:T(8,128)(2,1)} broadcast(bf16[16,1152]{1,0:T(8,128)(2,1)} %param.3), dimensions={1,2} | broadcast | bytes 184320 | tf_op jit(solution)/shard_map/broadcast_in_dim | solution.py:28
  2.1 6.4 %all-to-all-start = ((bf16[4,16,1152]{2,1,0:T(8,128)(2,1)}), bf16[4,16,1152]{2,1,0:T(8,128)(2,1)S(1)}, u32[]{:S(2)}, u32[]{:S(2)}) async-start(bf16[4,16,1152]{2,1,0:T(8,128)(2,1)} %broadcast_in_dim.12), calls=%async_computation | async-start | bytes 294912 | tf_op jit(solution)/shard_map/all_to_all | solution.py:29
  8.5 0.1 fusion.20
  8.7 0.6 %copy-done.1 = bf16[16,1152]{1,0:T(8,128)(2,1)S(1)} copy-done((bf16[16,1152]{1,0:T(8,128)(2,1)S(1)}, bf16[16,1152]{1,0:T(8,128)(2,1)}, u32[]{:S(2)}) %copy-start.1) | copy-done | bytes 36888
  9.3 0.1 fusion.21
  9.4 5.4 %all-to-all-done = bf16[4,16,1152]{2,1,0:T(8,128)(2,1)S(1)} async-done(((bf16[4,16,1152]{2,1,0:T(8,128)(2,1)}), bf16[4,16,1152]{2,1,0:T(8,128)(2,1)S(1)}, u32[]{:S(2)}, u32[]{:S(2)}) %all-to-all-start) | async-done | bytes 147488 | tf_op jit(solution)/shard_map/all_to_all | solution.py:29
  14.8 0.7 %broadcast_in_dim.13 = bf16[8,16,1152]{2,1,0:T(8,128)(2,1)} broadcast(bf16[16,1152]{1,0:T(8,128)(2,1)S(1)} %copy-done.1), dimensions={1,2} | broadcast | bytes 331776 | tf_op jit(solution)/shard_map/broadcast_in_dim | solution.py:28
  15.5 3.7 %all-to-all-start.1 = ((bf16[8,16,1152]{2,1,0:T(8,128)(2,1)}), bf16[8,16,1152]{2,1,0:T(8,128)(2,1)S(1)}, u32[]{:S(2)}, u32[]{:S(2)}) async-start(bf16[8,16,1152]{2,1,0:T(8,128)(2,1)} %broadcast_in_dim.13), calls=%async_computation.1 | async-start | bytes 589824 | tf_op jit(solution)/shard_map/all_to_all | solution.py:29
  19.6 6.9 %all-to-all-done.1 = bf16[8,16,1152]{2,1,0:T(8,128)(2,1)S(1)} async-done(((bf16[8,16,1152]{2,1,0:T(8,128)(2,1)}), bf16[8,16,1152]{2,1,0:T(8,128)(2,1)S(1)}, u32[]{:S(2)}, u32[]{:S(2)}) %all-to-all-start.1) | async-done | bytes 294944 | tf_op jit(solution)/shard_map/all_to_all | solution.py:29
  26.5 0.1 multiply_reduce_fusion
  26.7 0.1 multiply_convert_fusion
  26.9 0.6 %copy-done.2 = s32[64]{0:T(128)S(1)} copy-done((s32[64]{0:T(128)S(1)}, s32[64]{0:T(128)}, u32[]{:S(2)}) %copy-start.2) | copy-done | bytes 280
  27.5 0.3 fusion.7
  27.8 0.1 fusion.8
  27.9 0.9 %convolution_convert_fusion.1 = bf16[64,1152]{1,0:T(8,128)(2,1)} fusion(bf16[64,128]{1,0:T(8,128)(2,1)S(1)} %fusion.7, bf16[128,1152]{1,0:T(8,128)(2,1)S(1)} %fusion.8), kind=kOutput, calls=%fused_computation.1 | convolution fusion | flops 18948096 | bytes 458752 | tf_op jit(solution)/shard_map/dot_general | solution.py:51
  28.8 3.3 %all-to-all-start.2 = ((bf16[4,16,1152]{2,1,0:T(8,128)(2,1)}), bf16[4,16,1152]{2,1,0:T(8,128)(2,1)S(1)}, u32[]{:S(2)}, u32[]{:S(2)}) async-start(bf16[4,16,1152]{2,1,0:T(8,128)(2,1)} %bitcast.3), calls=%async_computation.2 | async-start | bytes 294912 | tf_op jit(solution)/shard_map/all_to_all | solution.py:58
  32.1 1.0 %convolution_convert_fusion = bf16[128,1152]{1,0:T(8,128)(2,1)} fusion(bf16[64,128]{1,0:T(8,128)(2,1)S(1)} %fusion.7, bf16[64,1152]{1,0:T(8,128)(2,1)S(1)} %fusion.9), kind=kOutput, calls=%fused_computation | convolution fusion | flops 19021824 | bytes 458752 | tf_op jit(solution)/shard_map/dot_general | solution.py:52
  33.1 5.0 %all-to-all-done.2 = bf16[4,16,1152]{2,1,0:T(8,128)(2,1)S(1)} async-done(((bf16[4,16,1152]{2,1,0:T(8,128)(2,1)}), bf16[4,16,1152]{2,1,0:T(8,128)(2,1)S(1)}, u32[]{:S(2)}, u32[]{:S(2)}) %all-to-all-start.2) | async-done | bytes 147488 | tf_op jit(solution)/shard_map/all_to_all | solution.py:58
  38.1 3.4 %all-to-all-start.3 = ((bf16[8,16,1152]{2,1,0:T(8,128)(2,1)}), bf16[8,16,1152]{2,1,0:T(8,128)(2,1)S(1)}, u32[]{:S(2)}, u32[]{:S(2)}) async-start(bf16[8,16,1152]{2,1,0:T(8,128)(2,1)} %bitcast.5), calls=%async_computation.3 | async-start | bytes 589824 | tf_op jit(solution)/shard_map/all_to_all | solution.py:57
  41.5 0.2 fusion.17
  41.7 0.7 %fusion.19 = f32[16,1152]{1,0:T(8,128)} fusion(f32[16,1152]{1,0:T(8,128)S(1)} %convert_reduce_fusion.1, bf16[16,1152]{1,0:T(8,128)(2,1)S(1)} %copy-done, f32[16]{0:T(128)S(1)} %fusion.17, f32[16]{0:T(128)S(1)} %add_rsqrt_fusion.3), kind=kLoop, calls=%fused_computation.34 | loop fusion | flops 92160 | bytes 184448 | tf_op jit(solution)/shard_map/mul | solution.py:19
  42.4 6.3 %all-to-all-done.3 = bf16[8,16,1152]{2,1,0:T(8,128)(2,1)S(1)} async-done(((bf16[8,16,1152]{2,1,0:T(8,128)(2,1)}), bf16[8,16,1152]{2,1,0:T(8,128)(2,1)S(1)}, u32[]{:S(2)}, u32[]{:S(2)}) %all-to-all-start.3) | async-done | bytes 294944 | tf_op jit(solution)/shard_map/all_to_all | solution.py:57
  48.8 0.2 fusion.14
  48.9 0.7 %fusion.16 = f32[16,1152]{1,0:T(8,128)} fusion(f32[16,1152]{1,0:T(8,128)S(1)} %convert_reduce_fusion, bf16[16,1152]{1,0:T(8,128)(2,1)S(1)} %copy-done.1, f32[16]{0:T(128)S(1)} %fusion.14, f32[16]{0:T(128)S(1)} %add_rsqrt_fusion.2), kind=kLoop, calls=%fused_computation.31 | loop fusion | flops 92160 | bytes 184448 | tf_op jit(solution)/shard_map/mul | solution.py:19
  (16 shorter events, 0.6 us)
Async XLA Ops:
  2.1 6.5 %copy-start = (bf16[16,1152]{1,0:T(8,128)(2,1)S(1)}, bf16[16,1152]{1,0:T(8,128)(2,1)}, u32[]{:S(2)}) copy-start(bf16[16,1152]{1,0:T(8,128)(2,1)} %param.3) | copy-start | bytes 110596
  2.1 12.7 %all-to-all-start = ((bf16[4,16,1152]{2,1,0:T(8,128)(2,1)}), bf16[4,16,1152]{2,1,0:T(8,128)(2,1)S(1)}, u32[]{:S(2)}, u32[]{:S(2)}) async-start(bf16[4,16,1152]{2,1,0:T(8,128)(2,1)} %broadcast_in_dim.12), calls=%async_computation | async-start | bytes 294912 | tf_op jit(solution)/shard_map/all_to_all | solution.py:29
  8.5 0.8 %copy-start.1 = (bf16[16,1152]{1,0:T(8,128)(2,1)S(1)}, bf16[16,1152]{1,0:T(8,128)(2,1)}, u32[]{:S(2)}) copy-start(bf16[16,1152]{1,0:T(8,128)(2,1)} %param.4) | copy-start | bytes 110596
  15.5 11.0 %all-to-all-start.1 = ((bf16[8,16,1152]{2,1,0:T(8,128)(2,1)}), bf16[8,16,1152]{2,1,0:T(8,128)(2,1)S(1)}, u32[]{:S(2)}, u32[]{:S(2)}) async-start(bf16[8,16,1152]{2,1,0:T(8,128)(2,1)} %broadcast_in_dim.13), calls=%async_computation.1 | async-start | bytes 589824 | tf_op jit(solution)/shard_map/all_to_all | solution.py:29
  26.9 0.7 %copy-start.2 = (s32[64]{0:T(128)S(1)}, s32[64]{0:T(128)}, u32[]{:S(2)}) copy-start(s32[64]{0:T(128)} %param.5) | copy-start | bytes 772
  28.8 9.3 %all-to-all-start.2 = ((bf16[4,16,1152]{2,1,0:T(8,128)(2,1)}), bf16[4,16,1152]{2,1,0:T(8,128)(2,1)S(1)}, u32[]{:S(2)}, u32[]{:S(2)}) async-start(bf16[4,16,1152]{2,1,0:T(8,128)(2,1)} %bitcast.3), calls=%async_computation.2 | async-start | bytes 294912 | tf_op jit(solution)/shard_map/all_to_all | solution.py:58
  38.1 10.6 %all-to-all-start.3 = ((bf16[8,16,1152]{2,1,0:T(8,128)(2,1)}), bf16[8,16,1152]{2,1,0:T(8,128)(2,1)S(1)}, u32[]{:S(2)}, u32[]{:S(2)}) async-start(bf16[8,16,1152]{2,1,0:T(8,128)(2,1)} %bitcast.5), calls=%async_computation.3 | async-start | bytes 589824 | tf_op jit(solution)/shard_map/all_to_all | solution.py:57

commit v3 on v0

v3 whole, which is shorter than its diff:
```python
import functools

import jax
import jax.numpy as jnp
from jax import lax
from jax.experimental import pallas as pl
from jax.experimental.pallas import tpu as pltpu
from jax.sharding import PartitionSpec as P

scale_logit = 8.0
shift_logit = -4.0
epsilon = 1e-06
f32 = jnp.float32
bf16 = jnp.bfloat16


def normalize(raw):
    values = raw.astype(f32)
    inverse = lax.rsqrt(jnp.sum(values * values, axis=-1, keepdims=True) + epsilon)
    return (values * inverse, inverse)


def back_norm(unit, inverse, grad):
    inner = jnp.sum(unit * grad, axis=-1, keepdims=True)
    return inverse * (grad - unit * inner)


def pair_coeff(logit, same):
    label = jnp.where(same, 1.0, -1.0).astype(f32)
    return (-scale_logit * label * jax.nn.sigmoid(-label * logit)).astype(bf16)


def swap(block, axis, distance):
    size = lax.axis_size(axis)
    return lax.ppermute(block, axis, [(i, i ^ distance) for i in range(size)])


def call(kernel, outs, args, scratch=()):
    vmem = pl.BlockSpec(memory_space=pltpu.VMEM)
    sizes = [a.size * a.dtype.itemsize for a in list(args) + list(outs)]
    return pl.pallas_call(
        kernel,
        out_shape=outs,
        in_specs=[vmem] * len(args),
        out_specs=[vmem] * len(outs),
        compiler_params=pltpu.CompilerParams(
            vmem_limit_bytes=min(48 * 2**20, 8 * 2**20 + 6 * sum(sizes))
        ),
    )(*args)


def low_kernel(*refs):
    out_ref = refs[-1]
    rows = refs[0].shape[0]
    for k, ref in enumerate(refs[:-1]):
        out_ref[k * rows:(k + 1) * rows, :] = normalize(ref[...])[0].astype(bf16)


def low_rows(pieces):
    rows, width = pieces[0].shape
    out = jax.ShapeDtypeStruct((len(pieces) * rows, width), bf16)
    return call(low_kernel, [out], pieces)[0]


def coeff_kernel(rows, odd, ids_ref, img_ref, txt_ref, coeff_ref):
    me_img = lax.axis_index("img")
    me_txt = lax.axis_index("txt")
    n_img = lax.axis_size("img")
    height = img_ref.shape[0]
    width = txt_ref.shape[0]
    row = lax.broadcasted_iota(jnp.int32, (height, height), 0)
    source = ((row // rows) ^ me_txt) * rows + row % rows
    here = lax.broadcasted_iota(jnp.int32, (height, height), 1) == source
    ids = jnp.sum(jnp.where(here, ids_ref[...], 0), axis=1, keepdims=True)
    column = lax.broadcasted_iota(jnp.int32, (height, width), 1)
    owner = (2 * (column // rows) + odd) ^ me_img
    same = ids == (me_txt * n_img + owner) * rows + column % rows
    scores = lax.dot_general(
        img_ref[...], txt_ref[...], (((1,), (1,)), ((), ())), preferred_element_type=f32
    )
    coeff_ref[...] = pair_coeff(scale_logit * scores + shift_logit, same)


def pair_block(rows, odd, ids, img_low, txt_low):
    out = jax.ShapeDtypeStruct((img_low.shape[0], txt_low.shape[0]), bf16)
    return call(functools.partial(coeff_kernel, rows, odd), [out], [ids, img_low, txt_low])[0]


def txt_kernel(coeff_ref, img_ref, out_ref):
    out_ref[...] = lax.dot_general(
        coeff_ref[...], img_ref[...], (((0,), (0,)), ((), ())), preferred_element_type=f32
    ).astype(out_ref.dtype)


def txt_part(coeff, img_low, dtype):
    out = jax.ShapeDtypeStruct((coeff.shape[1], img_low.shape[1]), dtype)
    return call(txt_kernel, [out], [coeff, img_low])[0]


def img_kernel(even_ref, odd_ref, txt_even_ref, txt_odd_ref, own_ref, *send_refs):
    rows = own_ref.shape[0]
    part = jnp.dot(even_ref[...], txt_even_ref[...], preferred_element_type=f32)
    part = part + jnp.dot(odd_ref[...], txt_odd_ref[...], preferred_element_type=f32)
    own_ref[...] = part[:rows]
    for k, ref in enumerate(send_refs):
        ref[...] = part[(k + 1) * rows:(k + 2) * rows].astype(bf16)


def add_kernel(own_ref, got_ref, keep_ref, *send_refs):
    rows = keep_ref.shape[0]
    keep_ref[...] = own_ref[:rows, :] + got_ref[:rows, :].astype(f32)
    for k, ref in enumerate(send_refs):
        block = slice((k + 1) * rows, (k + 2) * rows)
        ref[...] = (own_ref[block, :] + got_ref[block, :].astype(f32)).astype(bf16)


def last_kernel(raw_ref, own_ref, *refs):
    total = own_ref[...]
    for ref in refs[:-1]:
        total = total + ref[...].astype(f32)
    refs[-1][...] = back_norm(*normalize(raw_ref[...]), total)


def finish(raw, own, got):
    return call(last_kernel, [jax.ShapeDtypeStruct(raw.shape, f32)], [raw, own, *got])[0]


def local(image_embeds, text_embeds, pair_ids):
    rows, width = image_embeds.shape
    n_img = lax.axis_size("img")
    n_txt = lax.axis_size("txt")
    half = n_img // 2
    piece = jax.ShapeDtypeStruct((rows, width), bf16)
    total = jax.ShapeDtypeStruct((rows, width), f32)
    ids = pair_ids.reshape(1, -1)
    txt_even = low_rows([text_embeds] + [swap(text_embeds, "img", 2 * k) for k in range(1, half)])
    txt_odd = swap(txt_even, "img", 1)
    img_low = low_rows([image_embeds] + [swap(image_embeds, "txt", k) for k in range(1, n_txt)])
    even = pair_block(rows, 0, ids, img_low, txt_even)
    own = txt_part(even, img_low, f32)
    odd = pair_block(rows, 1, ids, img_low, txt_odd)
    got = swap(txt_part(odd, img_low, bf16), "img", 1)
    img_own, *img_send = call(
        img_kernel, [total] + [piece] * (n_txt - 1), [even, odd, txt_even, txt_odd]
    )
    txt_own, *txt_send = call(add_kernel, [total] + [piece] * (half - 1), [own, got])
    img_got = [swap(block, "txt", k + 1) for k, block in enumerate(img_send)]
    txt_got = [swap(block, "img", 2 * k + 2) for k, block in enumerate(txt_send)]
    return finish(image_embeds, img_own, img_got), finish(text_embeds, txt_own, txt_got)


def solution(mesh):
    return jax.shard_map(
        local,
        mesh=mesh,
        in_specs=(P(("img", "txt"), None), P(("txt", "img"), None), P("img")),
        out_specs=(P(("img", "txt"), None), P(("txt", "img"), None)),
        check_vma=False,
    )
```

time: 100 us -> 33.3 us (0.33)
  waiting for transfers between devices: 53.3 us -> 10.7 us
  blocking collectives: 24.7 us -> 0 us
  starting transfers between devices: 0.08 us -> 17.3 us
  between operations: 14.1 us -> 0.74 us
  other arithmetic: 4.91 us -> 0 us
  Pallas kernels: 0 us -> 2.95 us
  matrix products: 2.23 us -> 0 us
    reduce_scatter x2 -> x0, waiting for transfers between devices: 53.2 us -> none  [the longest x1 33.9 us: local(): txt_part = lax.psum_scatter(second, 'img', scatter_dimension=0, tiled=True)]
    all_gather x2 -> x0, blocking collectives: 24.7 us -> none  [the longest x1 15.1 us: local(): img_block = lax.all_gather(img_low, 'txt', axis=0, tiled=True)]
    ppermute x0 -> x14, starting transfers between devices: none -> 17.3 us  [swap(): return lax.ppermute(block, axis, [(i, i ^ distance) for i in range(size)])]
    ppermute x0 -> x14, waiting for transfers between devices: none -> 10.7 us  [swap(): return lax.ppermute(block, axis, [(i, i ^ distance) for i in range(size)])]
    reduce_sum x4 -> x0, other arithmetic: 3.3 us -> none  [the longest x2 2.29 us: back_norm(): inner = jnp.sum(unit * grad, axis=-1, keepdims=True)]
    pallas_call x0 -> x10, Pallas kernels: none -> 2.95 us  [call(): pl.pallas_call(kernel, out_shape=outs, in_specs=[vmem] * len(args), out_s...]
    dot_general x3 -> x0, matrix products: 2.23 us -> none  [the longest x1 1.07 us: local(): lax.dot_general(coeff, img_block, (((0,), (0,)), ((), ())), preferred_ele...]
    mul x2 -> x0, other arithmetic: 1.43 us -> none  [back_norm(): return inverse * (grad - unit * inner)]
  transfers between devices with their start and end apart: 2 -> 14, of which waited for: 2 -> 7; matrix products, arithmetic and copies ran while one was open for 3% -> 0% of each run, Pallas kernels for 0% -> 5%
where the time goes in v3:
time: 33.3 us; the launch traced here: 33.1 us
  starting transfers between devices  17.3 us (52%)
  waiting for transfers between devices  10.7 us (32%)
  Pallas kernels  2.95 us (9%)
  local copies, waits for them, and re-layouts  1.42 us (4%)
  between operations  0.74 us (2%)
    ppermute x14, starting transfers between devices, swap(): return lax.ppermute(block, axis, [(i, i ^ distance) for i in range(size)])  17.3 us
    ppermute x14, waiting for transfers between devices, swap(): return lax.ppermute(block, axis, [(i, i ^ distance) for i in range(size)])  10.7 us
    pallas_call x10, Pallas kernels, call(): pl.pallas_call(kernel, out_shape=outs, in_specs=[vmem] * len(args), out_s...  2.95 us
    unnamed x8, local copies, waits for them, and re-layouts  1.42 us
  transfers between devices with their start and end apart: 14, of which 7 were waited for; matrix products, arithmetic and copies ran while one was open for 0% of the time, Pallas kernels for 5%

profile of v3, /device:TPU:0, one launch (start us, length us, event | category | flops | bytes accessed | tf_op | source)
XLA Modules:
  0.0 33.1 jit_solution(16038235509137281184)
XLA Ops:
  0.6 4.0 %collective-permute-start.5 = (bf16[16,1152]{1,0:T(8,128)(2,1)}, bf16[16,1152]{1,0:T(8,128)(2,1)S(1)}, u32[]{:S(2)}, u32[]{:S(2)}) collective-permute-start(bf16[16,1152]{1,0:T(8,128)(2,1)} %raw_ref.3), channel_id=1, source_target_pairs={{0,24},{4,28},{8,16},{12,20},{16,8},{20,12},{24,0},{28,4},{1,25},{... | collective-permute-start | bytes 110600 | tf_op jit(solution)/shard_map/ppermute | solution.py:35
  4.6 0.5 %collective-permute-start.4 = (bf16[16,1152]{1,0:T(8,128)(2,1)}, bf16[16,1152]{1,0:T(8,128)(2,1)S(1)}, u32[]{:S(2)}, u32[]{:S(2)}) collective-permute-start(bf16[16,1152]{1,0:T(8,128)(2,1)} %raw_ref.3), channel_id=1, source_target_pairs={{0,16},{4,20},{8,24},{12,28},{16,0},{20,4},{24,8},{28,12},{1,17},{... | collective-permute-start | bytes 110600 | tf_op jit(solution)/shard_map/ppermute | solution.py:35
  5.2 1.5 %collective-permute-done.5.refs_3_ = bf16[16,1152]{1,0:T(8,128)(2,1)S(1)} collective-permute-done((bf16[16,1152]{1,0:T(8,128)(2,1)}, bf16[16,1152]{1,0:T(8,128)(2,1)S(1)}, u32[]{:S(2)}, u32[]{:S(2)}) %collective-permute-start.5) | collective-permute-done | bytes 36896 | tf_op jit(solution)/shard_map/ppermute | solution.py:35
  6.7 2.0 %collective-permute-done.4.refs_2_ = bf16[16,1152]{1,0:T(8,128)(2,1)S(1)} collective-permute-done((bf16[16,1152]{1,0:T(8,128)(2,1)}, bf16[16,1152]{1,0:T(8,128)(2,1)S(1)}, u32[]{:S(2)}, u32[]{:S(2)}) %collective-permute-start.4) | collective-permute-done | bytes 36896 | tf_op jit(solution)/shard_map/ppermute | solution.py:35
  8.8 0.5 %collective-permute-done.3.refs_1_ = bf16[16,1152]{1,0:T(8,128)(2,1)S(1)} collective-permute-done((bf16[16,1152]{1,0:T(8,128)(2,1)}, bf16[16,1152]{1,0:T(8,128)(2,1)S(1)}, u32[]{:S(2)}, u32[]{:S(2)}) %collective-permute-start.3) | collective-permute-done | bytes 36896 | tf_op jit(solution)/shard_map/ppermute | solution.py:35
  9.3 0.8 %copy-done.1 = bf16[16,1152]{1,0:T(8,128)(2,1)S(1)} copy-done((bf16[16,1152]{1,0:T(8,128)(2,1)S(1)}, bf16[16,1152]{1,0:T(8,128)(2,1)}, u32[]{:S(2)}) %copy-start.1) | copy-done | bytes 36888
  10.3 3.7 %collective-permute-start.2 = (bf16[16,1152]{1,0:T(8,128)(2,1)S(1)}, bf16[16,1152]{1,0:T(8,128)(2,1)S(1)}, u32[]{:S(2)}, u32[]{:S(2)}) collective-permute-start(bf16[16,1152]{1,0:T(8,128)(2,1)S(1)} %copy-done), channel_id=1, source_target_pairs={{0,3},{1,2},{2,1},{3,0},{4,7},{5,6},{6,5},{7,4},{8,11},{9,10},{10,... | collective-permute-start | bytes 110600 | tf_op jit(solution)/shard_map/ppermute | solution.py:35
  13.9 0.8 %collective-permute-start = (bf16[16,1152]{1,0:T(8,128)(2,1)S(1)}, bf16[16,1152]{1,0:T(8,128)(2,1)S(1)}, u32[]{:S(2)}, u32[]{:S(2)}) collective-permute-start(bf16[16,1152]{1,0:T(8,128)(2,1)S(1)} %copy-done), channel_id=1, source_target_pairs={{0,1},{1,0},{2,3},{3,2},{4,5},{5,4},{6,7},{7,6},{8,9},{9,8},{10,11... | collective-permute-start | bytes 110600 | tf_op jit(solution)/shard_map/ppermute | solution.py:35
  14.7 1.4 %collective-permute-done.2.refs_3_ = bf16[16,1152]{1,0:T(8,128)(2,1)S(1)} collective-permute-done((bf16[16,1152]{1,0:T(8,128)(2,1)S(1)}, bf16[16,1152]{1,0:T(8,128)(2,1)S(1)}, u32[]{:S(2)}, u32[]{:S(2)}) %collective-permute-start.2) | collective-permute-done | bytes 36896 | tf_op jit(solution)/shard_map/ppermute | solution.py:35
  16.1 2.7 %collective-permute-done.1.refs_2_ = bf16[16,1152]{1,0:T(8,128)(2,1)S(1)} collective-permute-done((bf16[16,1152]{1,0:T(8,128)(2,1)S(1)}, bf16[16,1152]{1,0:T(8,128)(2,1)S(1)}, u32[]{:S(2)}, u32[]{:S(2)}) %collective-permute-start.1) | collective-permute-done | bytes 36896 | tf_op jit(solution)/shard_map/ppermute | solution.py:35
  18.9 0.6 %copy-done.3 = s32[64]{0:T(128)S(1)} copy-done((s32[64]{0:T(128)S(1)}, s32[64]{0:T(128)}, u32[]{:S(2)}) %copy-start.3) | copy-done | bytes 280
  19.6 0.2 shard_map.53.odd_ref.coeff_ref
  19.8 0.2 shard_map.57
  20.3 0.2 shard_map.54
  20.5 0.6 %collective-permute-start.7 = (bf16[16,1152]{1,0:T(8,128)(2,1)S(1)}, bf16[16,1152]{1,0:T(8,128)(2,1)S(1)}, u32[]{:S(2)}, u32[]{:S(2)}) collective-permute-start(bf16[16,1152]{1,0:T(8,128)(2,1)S(1)} %get-tuple-element.11), channel_id=1, source_target_pairs={{0,1},{1,0},{2,3},{3,2},{4,5},{5,4},{6,7},{7,6},{8,9},{9,8},{10,11... | collective-permute-start | bytes 110600 | tf_op jit(solution)/shard_map/ppermute | solution.py:35
  21.1 0.2 shard_map.56.own_ref
  21.4 1.8 %collective-permute-start.8 = (bf16[16,1152]{1,0:T(8,128)(2,1)S(1)}, bf16[16,1152]{1,0:T(8,128)(2,1)S(1)}, u32[]{:S(2)}, u32[]{:S(2)}) collective-permute-start(bf16[16,1152]{1,0:T(8,128)(2,1)S(1)} %get-tuple-element.12), channel_id=1, source_target_pairs={{0,2},{1,3},{2,0},{3,1},{4,6},{5,7},{6,4},{7,5},{8,10},{9,11},{10,... | collective-permute-start | bytes 110600 | tf_op jit(solution)/shard_map/ppermute | solution.py:35
  23.2 2.0 %collective-permute-start.9 = (bf16[16,1152]{1,0:T(8,128)(2,1)S(1)}, bf16[16,1152]{1,0:T(8,128)(2,1)S(1)}, u32[]{:S(2)}, u32[]{:S(2)}) collective-permute-start(bf16[16,1152]{1,0:T(8,128)(2,1)S(1)} %get-tuple-element.13), channel_id=1, source_target_pairs={{0,3},{1,2},{2,1},{3,0},{4,7},{5,6},{6,5},{7,4},{8,11},{9,10},{10,... | collective-permute-start | bytes 110600 | tf_op jit(solution)/shard_map/ppermute | solution.py:35
  25.3 0.6 %collective-permute-start.11 = (bf16[16,1152]{1,0:T(8,128)(2,1)S(1)}, bf16[16,1152]{1,0:T(8,128)(2,1)S(1)}, u32[]{:S(2)}, u32[]{:S(2)}) collective-permute-start(bf16[16,1152]{1,0:T(8,128)(2,1)S(1)} %get-tuple-element.15), channel_id=1, source_target_pairs={{0,8},{4,12},{8,0},{12,4},{16,24},{20,28},{24,16},{28,20},{1,9},{5... | collective-permute-start | bytes 110600 | tf_op jit(solution)/shard_map/ppermute | solution.py:35
  25.9 1.5 %collective-permute-start.12 = (bf16[16,1152]{1,0:T(8,128)(2,1)S(1)}, bf16[16,1152]{1,0:T(8,128)(2,1)S(1)}, u32[]{:S(2)}, u32[]{:S(2)}) collective-permute-start(bf16[16,1152]{1,0:T(8,128)(2,1)S(1)} %get-tuple-element.16), channel_id=1, source_target_pairs={{0,16},{4,20},{8,24},{12,28},{16,0},{20,4},{24,8},{28,12},{1,17},{... | collective-permute-start | bytes 110600 | tf_op jit(solution)/shard_map/ppermute | solution.py:35
  27.4 1.4 %collective-permute-start.13 = (bf16[16,1152]{1,0:T(8,128)(2,1)S(1)}, bf16[16,1152]{1,0:T(8,128)(2,1)S(1)}, u32[]{:S(2)}, u32[]{:S(2)}) collective-permute-start(bf16[16,1152]{1,0:T(8,128)(2,1)S(1)} %get-tuple-element.17), channel_id=1, source_target_pairs={{0,24},{4,28},{8,16},{12,20},{16,8},{20,12},{24,0},{28,4},{1,25},{... | collective-permute-start | bytes 110600 | tf_op jit(solution)/shard_map/ppermute | solution.py:35
  29.0 0.8 %shard_map.55 = f32[16,1152]{1,0:T(8,128)} custom-call(bf16[16,1152]{1,0:T(8,128)(2,1)S(1)} %copy-done, f32[16,1152]{1,0:T(8,128)S(1)} %get-tuple-element.10.own_ref, bf16[16,1152]{1,0:T(8,128)(2,1)S(1)} %collective-permute-done.7.refs_0_, bf16[16,1152]{1,0:T(8,128)(2,1)S(1)} %collective-permute-done.8.refs_1_, ...), custom_call_target="tpu_custom_call" | custom-call | tf_op jit(solution)/shard_map/pallas_call | solution.py:41
  29.8 2.4 %collective-permute-done.13.refs_2_ = bf16[16,1152]{1,0:T(8,128)(2,1)S(1)} collective-permute-done((bf16[16,1152]{1,0:T(8,128)(2,1)S(1)}, bf16[16,1152]{1,0:T(8,128)(2,1)S(1)}, u32[]{:S(2)}, u32[]{:S(2)}) %collective-permute-start.13) | collective-permute-done | bytes 36896 | tf_op jit(solution)/shard_map/ppermute | solution.py:35
  32.3 0.8 %shard_map.59 = f32[16,1152]{1,0:T(8,128)} custom-call(bf16[16,1152]{1,0:T(8,128)(2,1)S(1)} %copy-done.2, f32[16,1152]{1,0:T(8,128)S(1)} %get-tuple-element.14.own_ref, bf16[16,1152]{1,0:T(8,128)(2,1)S(1)} %collective-permute-done.11.refs_0_, bf16[16,1152]{1,0:T(8,128)(2,1)S(1)} %collective-permute-done.12.refs_1_, ...), custom_call_target="tpu_custom_call" | custom-call | tf_op jit(solution)/shard_map/pallas_call | solution.py:41
  (22 shorter events, 0.9 us)
Async XLA Ops:
  0.6 9.6 %copy-start = (bf16[16,1152]{1,0:T(8,128)(2,1)S(1)}, bf16[16,1152]{1,0:T(8,128)(2,1)}, u32[]{:S(2)}) copy-start(bf16[16,1152]{1,0:T(8,128)(2,1)} %raw_ref.2) | copy-start | bytes 110596
  0.6 6.1 %collective-permute-start.5 = (bf16[16,1152]{1,0:T(8,128)(2,1)}, bf16[16,1152]{1,0:T(8,128)(2,1)S(1)}, u32[]{:S(2)}, u32[]{:S(2)}) collective-permute-start(bf16[16,1152]{1,0:T(8,128)(2,1)} %raw_ref.3), channel_id=1, source_target_pairs={{0,24},{4,28},{8,16},{12,20},{16,8},{20,12},{24,0},{28,4},{1,25},{... | collective-permute-start | bytes 110600 | tf_op jit(solution)/shard_map/ppermute | solution.py:35
  4.6 4.2 %collective-permute-start.4 = (bf16[16,1152]{1,0:T(8,128)(2,1)}, bf16[16,1152]{1,0:T(8,128)(2,1)S(1)}, u32[]{:S(2)}, u32[]{:S(2)}) collective-permute-start(bf16[16,1152]{1,0:T(8,128)(2,1)} %raw_ref.3), channel_id=1, source_target_pairs={{0,16},{4,20},{8,24},{12,28},{16,0},{20,4},{24,8},{28,12},{1,17},{... | collective-permute-start | bytes 110600 | tf_op jit(solution)/shard_map/ppermute | solution.py:35
  5.1 4.2 %collective-permute-start.3 = (bf16[16,1152]{1,0:T(8,128)(2,1)}, bf16[16,1152]{1,0:T(8,128)(2,1)S(1)}, u32[]{:S(2)}, u32[]{:S(2)}) collective-permute-start(bf16[16,1152]{1,0:T(8,128)(2,1)} %raw_ref.3), channel_id=1, source_target_pairs={{0,8},{4,12},{8,0},{12,4},{16,24},{20,28},{24,16},{28,20},{1,9},{5... | collective-permute-start | bytes 110600 | tf_op jit(solution)/shard_map/ppermute | solution.py:35
  9.3 0.8 %copy-start.1 = (bf16[16,1152]{1,0:T(8,128)(2,1)S(1)}, bf16[16,1152]{1,0:T(8,128)(2,1)}, u32[]{:S(2)}) copy-start(bf16[16,1152]{1,0:T(8,128)(2,1)} %raw_ref.3) | copy-start | bytes 110596
  10.2 8.8 %collective-permute-start.6 = (bf16[64,1152]{1,0:T(8,128)(2,1)S(1)}, bf16[64,1152]{1,0:T(8,128)(2,1)S(1)}, u32[]{:S(2)}, u32[]{:S(2)}) collective-permute-start(bf16[64,1152]{1,0:T(8,128)(2,1)S(1)} %shard_map.51.txt_ref.txt_even_ref), channel_id=1, source_target_pairs={{0,4},{4,0},{8,12},{12,8},{16,20},{20,16},{24,28},{28,24},{1,5},{5... | collective-permute-start | bytes 442376 | tf_op jit(solution)/shard_map/ppermute | solution.py:35
  10.3 5.8 %collective-permute-start.2 = (bf16[16,1152]{1,0:T(8,128)(2,1)S(1)}, bf16[16,1152]{1,0:T(8,128)(2,1)S(1)}, u32[]{:S(2)}, u32[]{:S(2)}) collective-permute-start(bf16[16,1152]{1,0:T(8,128)(2,1)S(1)} %copy-done), channel_id=1, source_target_pairs={{0,3},{1,2},{2,1},{3,0},{4,7},{5,6},{6,5},{7,4},{8,11},{9,10},{10,... | collective-permute-start | bytes 110600 | tf_op jit(solution)/shard_map/ppermute | solution.py:35
  13.9 4.9 %collective-permute-start.1 = (bf16[16,1152]{1,0:T(8,128)(2,1)S(1)}, bf16[16,1152]{1,0:T(8,128)(2,1)S(1)}, u32[]{:S(2)}, u32[]{:S(2)}) collective-permute-start(bf16[16,1152]{1,0:T(8,128)(2,1)S(1)} %copy-done), channel_id=1, source_target_pairs={{0,2},{1,3},{2,0},{3,1},{4,6},{5,7},{6,4},{7,5},{8,10},{9,11},{10,... | collective-permute-start | bytes 110600 | tf_op jit(solution)/shard_map/ppermute | solution.py:35
  13.9 4.9 %collective-permute-start = (bf16[16,1152]{1,0:T(8,128)(2,1)S(1)}, bf16[16,1152]{1,0:T(8,128)(2,1)S(1)}, u32[]{:S(2)}, u32[]{:S(2)}) collective-permute-start(bf16[16,1152]{1,0:T(8,128)(2,1)S(1)} %copy-done), channel_id=1, source_target_pairs={{0,1},{1,0},{2,3},{3,2},{4,5},{5,4},{6,7},{7,6},{8,9},{9,8},{10,11... | collective-permute-start | bytes 110600 | tf_op jit(solution)/shard_map/ppermute | solution.py:35
  18.9 0.7 %copy-start.3 = (s32[64]{0:T(128)S(1)}, s32[64]{0:T(128)}, u32[]{:S(2)}) copy-start(s32[64]{0:T(128)} %param.5) | copy-start | bytes 772
  20.0 5.2 %collective-permute-start.10 = (bf16[64,1152]{1,0:T(8,128)(2,1)S(1)}, bf16[64,1152]{1,0:T(8,128)(2,1)S(1)}, u32[]{:S(2)}, u32[]{:S(2)}) collective-permute-start(bf16[64,1152]{1,0:T(8,128)(2,1)S(1)} %shard_map.57), channel_id=1, source_target_pairs={{0,4},{4,0},{8,12},{12,8},{16,20},{20,16},{24,28},{28,24},{1,5},{5... | collective-permute-start | bytes 442376 | tf_op jit(solution)/shard_map/ppermute | solution.py:35
  20.5 6.9 %collective-permute-start.7 = (bf16[16,1152]{1,0:T(8,128)(2,1)S(1)}, bf16[16,1152]{1,0:T(8,128)(2,1)S(1)}, u32[]{:S(2)}, u32[]{:S(2)}) collective-permute-start(bf16[16,1152]{1,0:T(8,128)(2,1)S(1)} %get-tuple-element.11), channel_id=1, source_target_pairs={{0,1},{1,0},{2,3},{3,2},{4,5},{5,4},{6,7},{7,6},{8,9},{9,8},{10,11... | collective-permute-start | bytes 110600 | tf_op jit(solution)/shard_map/ppermute | solution.py:35
  21.4 7.5 %collective-permute-start.8 = (bf16[16,1152]{1,0:T(8,128)(2,1)S(1)}, bf16[16,1152]{1,0:T(8,128)(2,1)S(1)}, u32[]{:S(2)}, u32[]{:S(2)}) collective-permute-start(bf16[16,1152]{1,0:T(8,128)(2,1)S(1)} %get-tuple-element.12), channel_id=1, source_target_pairs={{0,2},{1,3},{2,0},{3,1},{4,6},{5,7},{6,4},{7,5},{8,10},{9,11},{10,... | collective-permute-start | bytes 110600 | tf_op jit(solution)/shard_map/ppermute | solution.py:35
  23.2 5.8 %collective-permute-start.9 = (bf16[16,1152]{1,0:T(8,128)(2,1)S(1)}, bf16[16,1152]{1,0:T(8,128)(2,1)S(1)}, u32[]{:S(2)}, u32[]{:S(2)}) collective-permute-start(bf16[16,1152]{1,0:T(8,128)(2,1)S(1)} %get-tuple-element.13), channel_id=1, source_target_pairs={{0,3},{1,2},{2,1},{3,0},{4,7},{5,6},{6,5},{7,4},{8,11},{9,10},{10,... | collective-permute-start | bytes 110600 | tf_op jit(solution)/shard_map/ppermute | solution.py:35
  25.3 4.5 %collective-permute-start.11 = (bf16[16,1152]{1,0:T(8,128)(2,1)S(1)}, bf16[16,1152]{1,0:T(8,128)(2,1)S(1)}, u32[]{:S(2)}, u32[]{:S(2)}) collective-permute-start(bf16[16,1152]{1,0:T(8,128)(2,1)S(1)} %get-tuple-element.15), channel_id=1, source_target_pairs={{0,8},{4,12},{8,0},{12,4},{16,24},{20,28},{24,16},{28,20},{1,9},{5... | collective-permute-start | bytes 110600 | tf_op jit(solution)/shard_map/ppermute | solution.py:35
  25.9 4.0 %collective-permute-start.12 = (bf16[16,1152]{1,0:T(8,128)(2,1)S(1)}, bf16[16,1152]{1,0:T(8,128)(2,1)S(1)}, u32[]{:S(2)}, u32[]{:S(2)}) collective-permute-start(bf16[16,1152]{1,0:T(8,128)(2,1)S(1)} %get-tuple-element.16), channel_id=1, source_target_pairs={{0,16},{4,20},{8,24},{12,28},{16,0},{20,4},{24,8},{28,12},{1,17},{... | collective-permute-start | bytes 110600 | tf_op jit(solution)/shard_map/ppermute | solution.py:35
  27.4 4.9 %collective-permute-start.13 = (bf16[16,1152]{1,0:T(8,128)(2,1)S(1)}, bf16[16,1152]{1,0:T(8,128)(2,1)S(1)}, u32[]{:S(2)}, u32[]{:S(2)}) collective-permute-start(bf16[16,1152]{1,0:T(8,128)(2,1)S(1)} %get-tuple-element.17), channel_id=1, source_target_pairs={{0,24},{4,28},{8,16},{12,20},{16,8},{20,12},{24,0},{28,4},{1,25},{... | collective-permute-start | bytes 110600 | tf_op jit(solution)/shard_map/ppermute | solution.py:35
  29.0 3.3 %copy-start.2 = (bf16[16,1152]{1,0:T(8,128)(2,1)S(1)}, bf16[16,1152]{1,0:T(8,128)(2,1)}, u32[]{:S(2)}) copy-start(bf16[16,1152]{1,0:T(8,128)(2,1)} %raw_ref.3) | copy-start | bytes 110596

commit v4 on v3

--- a/solution.py
+++ b/solution.py
@@ -10,6 +10,7 @@
 scale_logit = 8.0
 shift_logit = -4.0
 epsilon = 1e-06
+LONG = pl.CostEstimate(flops=10**10, bytes_accessed=10**7, transcendentals=0)
 f32 = jnp.float32
 bf16 = jnp.bfloat16
 
@@ -35,7 +36,7 @@
     return lax.ppermute(block, axis, [(i, i ^ distance) for i in range(size)])
 
 
-def call(kernel, outs, args, scratch=()):
+def call(kernel, outs, args, cost=None):
     vmem = pl.BlockSpec(memory_space=pltpu.VMEM)
     sizes = [a.size * a.dtype.itemsize for a in list(args) + list(outs)]
     return pl.pallas_call(
@@ -43,6 +44,7 @@
         out_shape=outs,
         in_specs=[vmem] * len(args),
         out_specs=[vmem] * len(outs),
+        cost_estimate=cost,
         compiler_params=pltpu.CompilerParams(
             vmem_limit_bytes=min(48 * 2**20, 8 * 2**20 + 6 * sum(sizes))
         ),
@@ -62,28 +64,38 @@
     return call(low_kernel, [out], pieces)[0]
 
 
-def coeff_kernel(rows, odd, ids_ref, img_ref, txt_ref, coeff_ref):
+def block_coeff(rows, odd, ids, img_low, txt_low):
     me_img = lax.axis_index("img")
     me_txt = lax.axis_index("txt")
     n_img = lax.axis_size("img")
-    height = img_ref.shape[0]
-    width = txt_ref.shape[0]
+    height = img_low.shape[0]
+    width = txt_low.shape[0]
     row = lax.broadcasted_iota(jnp.int32, (height, height), 0)
     source = ((row // rows) ^ me_txt) * rows + row % rows
     here = lax.broadcasted_iota(jnp.int32, (height, height), 1) == source
-    ids = jnp.sum(jnp.where(here, ids_ref[...], 0), axis=1, keepdims=True)
+    ids = jnp.sum(jnp.where(here, ids, 0), axis=1, keepdims=True)
     column = lax.broadcasted_iota(jnp.int32, (height, width), 1)
     owner = (2 * (column // rows) + odd) ^ me_img
     same = ids == (me_txt * n_img + owner) * rows + column % rows
     scores = lax.dot_general(
-        img_ref[...], txt_ref[...], (((1,), (1,)), ((), ())), preferred_element_type=f32
+        img_low, txt_low, (((1,), (1,)), ((), ())), preferred_element_type=f32
     )
-    coeff_ref[...] = pair_coeff(scale_logit * scores + shift_logit, same)
+    return pair_coeff(scale_logit * scores + shift_logit, same)
 
 
-def pair_block(rows, odd, ids, img_low, txt_low):
-    out = jax.ShapeDtypeStruct((img_low.shape[0], txt_low.shape[0]), bf16)
-    return call(functools.partial(coeff_kernel, rows, odd), [out], [ids, img_low, txt_low])[0]
+def even_kernel(ids_ref, txt_ref, *refs):
+    *raw_refs, img_ref, coeff_ref = refs
+    rows = raw_refs[0].shape[0]
+    low_kernel(*raw_refs, img_ref)
+    coeff_ref[...] = block_coeff(rows, 0, ids_ref[...], img_ref[...], txt_ref[...])
+
+
+def odd_kernel(rows, ids_ref, img_ref, txt_ref, coeff_ref, part_ref):
+    coeff = block_coeff(rows, 1, ids_ref[...], img_ref[...], txt_ref[...])
+    coeff_ref[...] = coeff
+    part_ref[...] = lax.dot_general(
+        coeff, img_ref[...], (((0,), (0,)), ((), ())), preferred_element_type=f32
+    ).astype(bf16)
 
 
 def txt_kernel(coeff_ref, img_ref, out_ref):
@@ -135,11 +147,16 @@
     ids = pair_ids.reshape(1, -1)
     txt_even = low_rows([text_embeds] + [swap(text_embeds, "img", 2 * k) for k in range(1, half)])
     txt_odd = swap(txt_even, "img", 1)
-    img_low = low_rows([image_embeds] + [swap(image_embeds, "txt", k) for k in range(1, n_txt)])
-    even = pair_block(rows, 0, ids, img_low, txt_even)
+    img_raw = [image_embeds] + [swap(image_embeds, "txt", k) for k in range(1, n_txt)]
+    low = jax.ShapeDtypeStruct((n_txt * rows, width), bf16)
+    wide = jax.ShapeDtypeStruct((half * rows, width), bf16)
+    coeff = jax.ShapeDtypeStruct((n_txt * rows, half * rows), bf16)
+    img_low, even = call(even_kernel, [low, coeff], [ids, txt_even, *img_raw], LONG)
+    odd, odd_part = call(
+        functools.partial(odd_kernel, rows), [coeff, wide], [ids, img_low, txt_odd]
+    )
+    got = swap(odd_part, "img", 1)
     own = txt_part(even, img_low, f32)
-    odd = pair_block(rows, 1, ids, img_low, txt_odd)
-    got = swap(txt_part(odd, img_low, bf16), "img", 1)
     img_own, *img_send = call(
         img_kernel, [total] + [piece] * (n_txt - 1), [even, odd, txt_even, txt_odd]
     )

time: 33.3 us -> 29.1 us (0.87)
  waiting for transfers between devices: 10.7 us -> 7.07 us
  local copies, waits for them, and re-layouts: 1.42 us -> 0.78 us
    ppermute x14, waiting for transfers between devices: 10.7 us -> 7.07 us  [swap(): return lax.ppermute(block, axis, [(i, i ^ distance) for i in range(size)])]
    unnamed x8, local copies, waits for them, and re-layouts: 1.42 us -> 0.78 us
    pallas_call x10 -> x8, Pallas kernels: 2.95 us -> 2.97 us  [call(): pl.pallas_call(kernel, out_shape=outs, in_specs=[vmem] * len(args), out_s...]
  transfers between devices with their start and end apart: 14 -> 14, of which waited for: 7 -> 4; matrix products, arithmetic and copies ran while one was open for 0% -> 0% of each run, Pallas kernels for 5% -> 6%
where the time goes in v4:
time: 29.1 us; the launch traced here: 28.9 us
  starting transfers between devices  17.4 us (60%)
  waiting for transfers between devices  7.07 us (24%)
  Pallas kernels  2.97 us (10%)
  local copies, waits for them, and re-layouts  0.78 us (3%)
  between operations  0.73 us (3%)
    ppermute x14, starting transfers between devices, swap(): return lax.ppermute(block, axis, [(i, i ^ distance) for i in range(size)])  17.4 us
    ppermute x14, waiting for transfers between devices, swap(): return lax.ppermute(block, axis, [(i, i ^ distance) for i in range(size)])  7.07 us
    pallas_call x8, Pallas kernels, call(): pl.pallas_call(kernel, out_shape=outs, in_specs=[vmem] * len(args), out_s...  2.97 us
    unnamed x8, local copies, waits for them, and re-layouts  0.78 us
  transfers between devices with their start and end apart: 14, of which 4 were waited for; matrix products, arithmetic and copies ran while one was open for 0% of the time, Pallas kernels for 6%

profile of v4, /device:TPU:0, one launch (start us, length us, event | category | flops | bytes accessed | tf_op | source)
XLA Modules:
  0.0 28.9 jit_solution(2710764358921030751)
XLA Ops:
  0.6 4.0 %collective-permute-start.2 = (bf16[16,1152]{1,0:T(8,128)(2,1)}, bf16[16,1152]{1,0:T(8,128)(2,1)S(1)}, u32[]{:S(2)}, u32[]{:S(2)}) collective-permute-start(bf16[16,1152]{1,0:T(8,128)(2,1)} %raw_ref.3), channel_id=1, source_target_pairs={{0,24},{4,28},{8,16},{12,20},{16,8},{20,12},{24,0},{28,4},{1,25},{... | collective-permute-start | bytes 110600 | tf_op jit(solution)/shard_map/ppermute | solution.py:36
  4.6 0.5 %collective-permute-start.1 = (bf16[16,1152]{1,0:T(8,128)(2,1)}, bf16[16,1152]{1,0:T(8,128)(2,1)S(1)}, u32[]{:S(2)}, u32[]{:S(2)}) collective-permute-start(bf16[16,1152]{1,0:T(8,128)(2,1)} %raw_ref.3), channel_id=1, source_target_pairs={{0,16},{4,20},{8,24},{12,28},{16,0},{20,4},{24,8},{28,12},{1,17},{... | collective-permute-start | bytes 110600 | tf_op jit(solution)/shard_map/ppermute | solution.py:36
  5.1 0.1 collective-permute-start
  5.2 4.0 %collective-permute-start.5 = (bf16[16,1152]{1,0:T(8,128)(2,1)}, bf16[16,1152]{1,0:T(8,128)(2,1)S(1)}, u32[]{:S(2)}, u32[]{:S(2)}) collective-permute-start(bf16[16,1152]{1,0:T(8,128)(2,1)} %raw_ref.2), channel_id=1, source_target_pairs={{0,3},{1,2},{2,1},{3,0},{4,7},{5,6},{6,5},{7,4},{8,11},{9,10},{10,... | collective-permute-start | bytes 110600 | tf_op jit(solution)/shard_map/ppermute | solution.py:36
  9.2 0.6 %collective-permute-start.3 = (bf16[16,1152]{1,0:T(8,128)(2,1)}, bf16[16,1152]{1,0:T(8,128)(2,1)S(1)}, u32[]{:S(2)}, u32[]{:S(2)}) collective-permute-start(bf16[16,1152]{1,0:T(8,128)(2,1)} %raw_ref.2), channel_id=1, source_target_pairs={{0,1},{1,0},{2,3},{3,2},{4,5},{5,4},{6,7},{7,6},{8,9},{9,8},{10,11... | collective-permute-start | bytes 110600 | tf_op jit(solution)/shard_map/ppermute | solution.py:36
  9.8 0.8 %copy-done = bf16[16,1152]{1,0:T(8,128)(2,1)S(1)} copy-done((bf16[16,1152]{1,0:T(8,128)(2,1)S(1)}, bf16[16,1152]{1,0:T(8,128)(2,1)}, u32[]{:S(2)}) %copy-start) | copy-done | bytes 36888
  10.6 0.1 shard_map.50.txt_ref.txt_even_ref
  10.7 0.1 collective-permute-start.6
  10.8 0.8 %collective-permute-done.5.refs_3_ = bf16[16,1152]{1,0:T(8,128)(2,1)S(1)} collective-permute-done((bf16[16,1152]{1,0:T(8,128)(2,1)}, bf16[16,1152]{1,0:T(8,128)(2,1)S(1)}, u32[]{:S(2)}, u32[]{:S(2)}) %collective-permute-start.5) | collective-permute-done | bytes 36896 | tf_op jit(solution)/shard_map/ppermute | solution.py:36
  11.5 2.8 %collective-permute-done.4.refs_2_ = bf16[16,1152]{1,0:T(8,128)(2,1)S(1)} collective-permute-done((bf16[16,1152]{1,0:T(8,128)(2,1)}, bf16[16,1152]{1,0:T(8,128)(2,1)S(1)}, u32[]{:S(2)}, u32[]{:S(2)}) %collective-permute-start.4) | collective-permute-done | bytes 36896 | tf_op jit(solution)/shard_map/ppermute | solution.py:36
  14.3 0.3 %shard_map.51 = (bf16[64,1152]{1,0:T(8,128)(2,1)S(1)}, bf16[64,64]{1,0:T(8,128)(2,1)S(1)}) custom-call(s32[1,64]{1,0:T(1,128)S(1)} %bitcast.1, bf16[64,1152]{1,0:T(8,128)(2,1)S(1)} %shard_map.50.txt_ref.txt_even_ref, bf16[16,1152]{1,0:T(8,128)(2,1)S(1)} %copy-done.2, bf16[16,1152]{1,0:T(8,128)(2,1)S(1)} %collective-permute-done.3.refs_1_, ...), custom_call_target="tpu_custom_call" | custom-call | flops 10000000000 | bytes 10000000 | tf_op jit(solution)/shard_map/pallas_call | solution.py:42
  14.6 0.5 %shard_map.52 = (bf16[64,64]{1,0:T(8,128)(2,1)S(1)}, bf16[64,1152]{1,0:T(8,128)(2,1)S(1)}) custom-call(s32[1,64]{1,0:T(1,128)S(1)} %bitcast.2, bf16[64,1152]{1,0:T(8,128)(2,1)S(1)} %get-tuple-element.15.img_ref, bf16[64,1152]{1,0:T(8,128)(2,1)S(1)} %collective-permute-done.6.txt_ref.txt_odd_ref), custom_call_target="tpu_custom_call" | custom-call | tf_op jit(solution)/shard_map/pallas_call | solution.py:42
  15.2 0.2 shard_map.53
  15.4 0.1 collective-permute-start.7
  15.5 0.2 shard_map.55.own_ref
  15.7 2.1 %collective-permute-start.8 = (bf16[16,1152]{1,0:T(8,128)(2,1)S(1)}, bf16[16,1152]{1,0:T(8,128)(2,1)S(1)}, u32[]{:S(2)}, u32[]{:S(2)}) collective-permute-start(bf16[16,1152]{1,0:T(8,128)(2,1)S(1)} %get-tuple-element.19), channel_id=1, source_target_pairs={{0,2},{1,3},{2,0},{3,1},{4,6},{5,7},{6,4},{7,5},{8,10},{9,11},{10,... | collective-permute-start | bytes 110600 | tf_op jit(solution)/shard_map/ppermute | solution.py:36
  17.8 2.3 %collective-permute-start.9 = (bf16[16,1152]{1,0:T(8,128)(2,1)S(1)}, bf16[16,1152]{1,0:T(8,128)(2,1)S(1)}, u32[]{:S(2)}, u32[]{:S(2)}) collective-permute-start(bf16[16,1152]{1,0:T(8,128)(2,1)S(1)} %get-tuple-element.20), channel_id=1, source_target_pairs={{0,3},{1,2},{2,1},{3,0},{4,7},{5,6},{6,5},{7,4},{8,11},{9,10},{10,... | collective-permute-start | bytes 110600 | tf_op jit(solution)/shard_map/ppermute | solution.py:36
  20.2 1.6 %collective-permute-start.11 = (bf16[16,1152]{1,0:T(8,128)(2,1)S(1)}, bf16[16,1152]{1,0:T(8,128)(2,1)S(1)}, u32[]{:S(2)}, u32[]{:S(2)}) collective-permute-start(bf16[16,1152]{1,0:T(8,128)(2,1)S(1)} %get-tuple-element.23), channel_id=1, source_target_pairs={{0,8},{4,12},{8,0},{12,4},{16,24},{20,28},{24,16},{28,20},{1,9},{5... | collective-permute-start | bytes 110600 | tf_op jit(solution)/shard_map/ppermute | solution.py:36
  21.7 1.5 %collective-permute-start.12 = (bf16[16,1152]{1,0:T(8,128)(2,1)S(1)}, bf16[16,1152]{1,0:T(8,128)(2,1)S(1)}, u32[]{:S(2)}, u32[]{:S(2)}) collective-permute-start(bf16[16,1152]{1,0:T(8,128)(2,1)S(1)} %get-tuple-element.24), channel_id=1, source_target_pairs={{0,16},{4,20},{8,24},{12,28},{16,0},{20,4},{24,8},{28,12},{1,17},{... | collective-permute-start | bytes 110600 | tf_op jit(solution)/shard_map/ppermute | solution.py:36
  23.2 0.5 %collective-permute-start.13 = (bf16[16,1152]{1,0:T(8,128)(2,1)S(1)}, bf16[16,1152]{1,0:T(8,128)(2,1)S(1)}, u32[]{:S(2)}, u32[]{:S(2)}) collective-permute-start(bf16[16,1152]{1,0:T(8,128)(2,1)S(1)} %get-tuple-element.25), channel_id=1, source_target_pairs={{0,24},{4,28},{8,16},{12,20},{16,8},{20,12},{24,0},{28,4},{1,25},{... | collective-permute-start | bytes 110600 | tf_op jit(solution)/shard_map/ppermute | solution.py:36
  23.7 0.8 %shard_map.54 = f32[16,1152]{1,0:T(8,128)} custom-call(bf16[16,1152]{1,0:T(8,128)(2,1)S(1)} %copy-done.2, f32[16,1152]{1,0:T(8,128)S(1)} %get-tuple-element.17.own_ref, bf16[16,1152]{1,0:T(8,128)(2,1)S(1)} %collective-permute-done.7.refs_0_, bf16[16,1152]{1,0:T(8,128)(2,1)S(1)} %collective-permute-done.8.refs_1_, ...), custom_call_target="tpu_custom_call" | custom-call | tf_op jit(solution)/shard_map/pallas_call | solution.py:42
  24.6 1.1 %collective-permute-done.12.refs_1_ = bf16[16,1152]{1,0:T(8,128)(2,1)S(1)} collective-permute-done((bf16[16,1152]{1,0:T(8,128)(2,1)S(1)}, bf16[16,1152]{1,0:T(8,128)(2,1)S(1)}, u32[]{:S(2)}, u32[]{:S(2)}) %collective-permute-start.12) | collective-permute-done | bytes 36896 | tf_op jit(solution)/shard_map/ppermute | solution.py:36
  25.7 2.4 %collective-permute-done.13.refs_2_ = bf16[16,1152]{1,0:T(8,128)(2,1)S(1)} collective-permute-done((bf16[16,1152]{1,0:T(8,128)(2,1)S(1)}, bf16[16,1152]{1,0:T(8,128)(2,1)S(1)}, u32[]{:S(2)}, u32[]{:S(2)}) %collective-permute-start.13) | collective-permute-done | bytes 36896 | tf_op jit(solution)/shard_map/ppermute | solution.py:36
  28.1 0.8 %shard_map.57 = f32[16,1152]{1,0:T(8,128)} custom-call(bf16[16,1152]{1,0:T(8,128)(2,1)S(1)} %copy-done.1, f32[16,1152]{1,0:T(8,128)S(1)} %get-tuple-element.22.own_ref, bf16[16,1152]{1,0:T(8,128)(2,1)S(1)} %collective-permute-done.11.refs_0_, bf16[16,1152]{1,0:T(8,128)(2,1)S(1)} %collective-permute-done.12.refs_1_, ...), custom_call_target="tpu_custom_call" | custom-call | tf_op jit(solution)/shard_map/pallas_call | solution.py:42
  (20 shorter events, 0.2 us)
Async XLA Ops:
  0.6 8.6 %collective-permute-start.2 = (bf16[16,1152]{1,0:T(8,128)(2,1)}, bf16[16,1152]{1,0:T(8,128)(2,1)S(1)}, u32[]{:S(2)}, u32[]{:S(2)}) collective-permute-start(bf16[16,1152]{1,0:T(8,128)(2,1)} %raw_ref.3), channel_id=1, source_target_pairs={{0,24},{4,28},{8,16},{12,20},{16,8},{20,12},{24,0},{28,4},{1,25},{... | collective-permute-start | bytes 110600 | tf_op jit(solution)/shard_map/ppermute | solution.py:36
  4.6 5.2 %collective-permute-start.1 = (bf16[16,1152]{1,0:T(8,128)(2,1)}, bf16[16,1152]{1,0:T(8,128)(2,1)S(1)}, u32[]{:S(2)}, u32[]{:S(2)}) collective-permute-start(bf16[16,1152]{1,0:T(8,128)(2,1)} %raw_ref.3), channel_id=1, source_target_pairs={{0,16},{4,20},{8,24},{12,28},{16,0},{20,4},{24,8},{28,12},{1,17},{... | collective-permute-start | bytes 110600 | tf_op jit(solution)/shard_map/ppermute | solution.py:36
  5.1 4.7 %collective-permute-start = (bf16[16,1152]{1,0:T(8,128)(2,1)}, bf16[16,1152]{1,0:T(8,128)(2,1)S(1)}, u32[]{:S(2)}, u32[]{:S(2)}) collective-permute-start(bf16[16,1152]{1,0:T(8,128)(2,1)} %raw_ref.3), channel_id=1, source_target_pairs={{0,8},{4,12},{8,0},{12,4},{16,24},{20,28},{24,16},{28,20},{1,9},{5... | collective-permute-start | bytes 110600 | tf_op jit(solution)/shard_map/ppermute | solution.py:36
  5.2 6.3 %collective-permute-start.5 = (bf16[16,1152]{1,0:T(8,128)(2,1)}, bf16[16,1152]{1,0:T(8,128)(2,1)S(1)}, u32[]{:S(2)}, u32[]{:S(2)}) collective-permute-start(bf16[16,1152]{1,0:T(8,128)(2,1)} %raw_ref.2), channel_id=1, source_target_pairs={{0,3},{1,2},{2,1},{3,0},{4,7},{5,6},{6,5},{7,4},{8,11},{9,10},{10,... | collective-permute-start | bytes 110600 | tf_op jit(solution)/shard_map/ppermute | solution.py:36
  9.2 5.1 %collective-permute-start.4 = (bf16[16,1152]{1,0:T(8,128)(2,1)}, bf16[16,1152]{1,0:T(8,128)(2,1)S(1)}, u32[]{:S(2)}, u32[]{:S(2)}) collective-permute-start(bf16[16,1152]{1,0:T(8,128)(2,1)} %raw_ref.2), channel_id=1, source_target_pairs={{0,2},{1,3},{2,0},{3,1},{4,6},{5,7},{6,4},{7,5},{8,10},{9,11},{10,... | collective-permute-start | bytes 110600 | tf_op jit(solution)/shard_map/ppermute | solution.py:36
  9.2 5.1 %collective-permute-start.3 = (bf16[16,1152]{1,0:T(8,128)(2,1)}, bf16[16,1152]{1,0:T(8,128)(2,1)S(1)}, u32[]{:S(2)}, u32[]{:S(2)}) collective-permute-start(bf16[16,1152]{1,0:T(8,128)(2,1)} %raw_ref.2), channel_id=1, source_target_pairs={{0,1},{1,0},{2,3},{3,2},{4,5},{5,4},{6,7},{7,6},{8,9},{9,8},{10,11... | collective-permute-start | bytes 110600 | tf_op jit(solution)/shard_map/ppermute | solution.py:36
  9.8 0.8 %copy-start = (bf16[16,1152]{1,0:T(8,128)(2,1)S(1)}, bf16[16,1152]{1,0:T(8,128)(2,1)}, u32[]{:S(2)}) copy-start(bf16[16,1152]{1,0:T(8,128)(2,1)} %raw_ref.3) | copy-start | bytes 110596
  10.6 3.7 %copy-start.2 = (bf16[16,1152]{1,0:T(8,128)(2,1)S(1)}, bf16[16,1152]{1,0:T(8,128)(2,1)}, u32[]{:S(2)}) copy-start(bf16[16,1152]{1,0:T(8,128)(2,1)} %raw_ref.2) | copy-start | bytes 110596
  10.7 3.6 %copy-start.3 = (s32[64]{0:T(128)S(1)}, s32[64]{0:T(128)}, u32[]{:S(2)}) copy-start(s32[64]{0:T(128)} %param.5) | copy-start | bytes 772
  10.7 3.9 %collective-permute-start.6 = (bf16[64,1152]{1,0:T(8,128)(2,1)S(1)}, bf16[64,1152]{1,0:T(8,128)(2,1)S(1)}, u32[]{:S(2)}, u32[]{:S(2)}) collective-permute-start(bf16[64,1152]{1,0:T(8,128)(2,1)S(1)} %shard_map.50.txt_ref.txt_even_ref), channel_id=1, source_target_pairs={{0,4},{4,0},{8,12},{12,8},{16,20},{20,16},{24,28},{28,24},{1,5},{5... | collective-permute-start | bytes 442376 | tf_op jit(solution)/shard_map/ppermute | solution.py:36
  15.1 5.0 %collective-permute-start.10 = (bf16[64,1152]{1,0:T(8,128)(2,1)S(1)}, bf16[64,1152]{1,0:T(8,128)(2,1)S(1)}, u32[]{:S(2)}, u32[]{:S(2)}) collective-permute-start(bf16[64,1152]{1,0:T(8,128)(2,1)S(1)} %get-tuple-element.21), channel_id=1, source_target_pairs={{0,4},{4,0},{8,12},{12,8},{16,20},{20,16},{24,28},{28,24},{1,5},{5... | collective-permute-start | bytes 442376 | tf_op jit(solution)/shard_map/ppermute | solution.py:36
  15.4 7.9 %collective-permute-start.7 = (bf16[16,1152]{1,0:T(8,128)(2,1)S(1)}, bf16[16,1152]{1,0:T(8,128)(2,1)S(1)}, u32[]{:S(2)}, u32[]{:S(2)}) collective-permute-start(bf16[16,1152]{1,0:T(8,128)(2,1)S(1)} %get-tuple-element.18), channel_id=1, source_target_pairs={{0,1},{1,0},{2,3},{3,2},{4,5},{5,4},{6,7},{7,6},{8,9},{9,8},{10,11... | collective-permute-start | bytes 110600 | tf_op jit(solution)/shard_map/ppermute | solution.py:36
  15.7 8.0 %collective-permute-start.8 = (bf16[16,1152]{1,0:T(8,128)(2,1)S(1)}, bf16[16,1152]{1,0:T(8,128)(2,1)S(1)}, u32[]{:S(2)}, u32[]{:S(2)}) collective-permute-start(bf16[16,1152]{1,0:T(8,128)(2,1)S(1)} %get-tuple-element.19), channel_id=1, source_target_pairs={{0,2},{1,3},{2,0},{3,1},{4,6},{5,7},{6,4},{7,5},{8,10},{9,11},{10,... | collective-permute-start | bytes 110600 | tf_op jit(solution)/shard_map/ppermute | solution.py:36
  17.8 5.9 %collective-permute-start.9 = (bf16[16,1152]{1,0:T(8,128)(2,1)S(1)}, bf16[16,1152]{1,0:T(8,128)(2,1)S(1)}, u32[]{:S(2)}, u32[]{:S(2)}) collective-permute-start(bf16[16,1152]{1,0:T(8,128)(2,1)S(1)} %get-tuple-element.20), channel_id=1, source_target_pairs={{0,3},{1,2},{2,1},{3,0},{4,7},{5,6},{6,5},{7,4},{8,11},{9,10},{10,... | collective-permute-start | bytes 110600 | tf_op jit(solution)/shard_map/ppermute | solution.py:36
  20.2 4.4 %collective-permute-start.11 = (bf16[16,1152]{1,0:T(8,128)(2,1)S(1)}, bf16[16,1152]{1,0:T(8,128)(2,1)S(1)}, u32[]{:S(2)}, u32[]{:S(2)}) collective-permute-start(bf16[16,1152]{1,0:T(8,128)(2,1)S(1)} %get-tuple-element.23), channel_id=1, source_target_pairs={{0,8},{4,12},{8,0},{12,4},{16,24},{20,28},{24,16},{28,20},{1,9},{5... | collective-permute-start | bytes 110600 | tf_op jit(solution)/shard_map/ppermute | solution.py:36
  21.7 4.0 %collective-permute-start.12 = (bf16[16,1152]{1,0:T(8,128)(2,1)S(1)}, bf16[16,1152]{1,0:T(8,128)(2,1)S(1)}, u32[]{:S(2)}, u32[]{:S(2)}) collective-permute-start(bf16[16,1152]{1,0:T(8,128)(2,1)S(1)} %get-tuple-element.24), channel_id=1, source_target_pairs={{0,16},{4,20},{8,24},{12,28},{16,0},{20,4},{24,8},{28,12},{1,17},{... | collective-permute-start | bytes 110600 | tf_op jit(solution)/shard_map/ppermute | solution.py:36
  23.2 4.9 %collective-permute-start.13 = (bf16[16,1152]{1,0:T(8,128)(2,1)S(1)}, bf16[16,1152]{1,0:T(8,128)(2,1)S(1)}, u32[]{:S(2)}, u32[]{:S(2)}) collective-permute-start(bf16[16,1152]{1,0:T(8,128)(2,1)S(1)} %get-tuple-element.25), channel_id=1, source_target_pairs={{0,24},{4,28},{8,16},{12,20},{16,8},{20,12},{24,0},{28,4},{1,25},{... | collective-permute-start | bytes 110600 | tf_op jit(solution)/shard_map/ppermute | solution.py:36
  23.7 4.4 %copy-start.1 = (bf16[16,1152]{1,0:T(8,128)(2,1)S(1)}, bf16[16,1152]{1,0:T(8,128)(2,1)}, u32[]{:S(2)}) copy-start(bf16[16,1152]{1,0:T(8,128)(2,1)} %raw_ref.3) | copy-start | bytes 110596

commit v5 on v0

v5 whole, which is shorter than its diff:
```python
import functools

import jax
import jax.numpy as jnp
from jax import lax
from jax.experimental import pallas as pl
from jax.experimental.pallas import tpu as pltpu
from jax.sharding import PartitionSpec as P

scale_logit = 8.0
shift_logit = -4.0
epsilon = 1e-06
f32 = jnp.float32
bf16 = jnp.bfloat16
VMEM = pl.BlockSpec(memory_space=pltpu.VMEM)
LONG = pl.CostEstimate(flops=10**10, bytes_accessed=10**7, transcendentals=0)


def normalize(raw):
    values = raw.astype(f32)
    inverse = lax.rsqrt(jnp.sum(values * values, axis=-1, keepdims=True) + epsilon)
    return (values * inverse, inverse)


def back_norm(unit, inverse, grad):
    inner = jnp.sum(unit * grad, axis=-1, keepdims=True)
    return inverse * (grad - unit * inner)


def pair_coeff(logit, same):
    label = jnp.where(same, 1.0, -1.0).astype(f32)
    return (-scale_logit * label * jax.nn.sigmoid(-label * logit)).astype(bf16)


def core_swap(block):
    size = lax.axis_size("img")
    return lax.ppermute(block, "img", [(i, i ^ 1) for i in range(size)])


def chip_swap(block, distance):
    n_img, n_txt = lax.axis_size("img"), lax.axis_size("txt")
    pairs = []
    for img in range(n_img):
        for txt in range(n_txt):
            if img % 2 == 0 and distance < n_img // 2:
                pairs.append((img * n_txt + txt, (img ^ (2 * distance)) * n_txt + txt))
            if img % 2 == 1 and distance < n_txt:
                pairs.append((img * n_txt + txt, img * n_txt + (txt ^ distance)))
    return lax.ppermute(block, ("img", "txt"), pairs)


def is_even():
    return lax.axis_index("img") % 2 == 0


def call(kernel, outs, args, cost=None):
    sizes = [a.size * a.dtype.itemsize for a in list(args) + list(outs)]
    return pl.pallas_call(
        kernel,
        out_shape=outs,
        in_specs=[VMEM] * len(args),
        out_specs=[VMEM] * len(outs),
        cost_estimate=cost,
        compiler_params=pltpu.CompilerParams(
            vmem_limit_bytes=min(48 * 2**20, 8 * 2**20 + 6 * sum(sizes))
        ),
    )(*args)


def sides_kernel(own_ref, txt_ref, img_ref, mine_ref, other_ref, raw_ref):
    rows = txt_ref.shape[0]
    even = is_even()
    own = normalize(own_ref[...])[0].astype(bf16)
    own_txt, own_img = own[:rows], own[rows:]
    far_txt = normalize(txt_ref[...])[0].astype(bf16)
    far_img = normalize(img_ref[...])[0].astype(bf16)
    mine_ref[:rows, :] = jnp.where(even, own_txt, far_img)
    mine_ref[rows:, :] = jnp.where(even, far_txt, own_img)
    other_ref[:rows, :] = jnp.where(even, own_img, far_txt)
    other_ref[rows:, :] = jnp.where(even, far_img, own_txt)
    raw_ref[:rows, :] = jnp.where(even, own_ref[:rows, :], img_ref[...])
    raw_ref[rows:, :] = jnp.where(even, txt_ref[...], own_ref[rows:, :])


def row_ids(rows, ids, far_ids, count):
    me_img = lax.axis_index("img")
    me_txt = lax.axis_index("txt")
    n_img = lax.axis_size("img")
    row = lax.broadcasted_iota(jnp.int32, (count, 1), 0)
    chip, core, j = row // (2 * rows), row // rows % 2, row % rows
    txt_ids = (me_txt * n_img + (((me_img // 2) ^ chip) * 2 + core)) * rows + j
    source = (me_txt ^ chip) * rows + j
    here = lax.broadcasted_iota(jnp.int32, (count, ids.shape[1]), 1) == source
    per_core = jnp.where(core == me_img % 2, ids, far_ids)
    img_ids = jnp.sum(jnp.where(here, per_core, 0), axis=1, keepdims=True)
    return txt_ids, img_ids


def ids_kernel(ids_ref, far_ids_ref, piece_ref, mine_ids_ref, other_ids_ref, out_ref):
    height = piece_ref.shape[0]
    count = mine_ids_ref.shape[0]
    even = is_even()
    txt_ids, img_ids = row_ids(height // 2, ids_ref[...], far_ids_ref[...], count)
    mine_ids_ref[...] = jnp.where(even, txt_ids, img_ids)
    other_ids = jnp.where(even, img_ids, txt_ids)
    diagonal = lax.broadcasted_iota(jnp.int32, (count, count), 0) == lax.broadcasted_iota(
        jnp.int32, (count, count), 1
    )
    other_ids_ref[...] = jnp.sum(jnp.where(diagonal, other_ids, 0), axis=0, keepdims=True)
    out_ref[...] = piece_ref[...]


def part_of(mine_refs, other_refs, mine_ids_ref, other_ids):
    mine = jnp.concatenate([ref[...] for ref in mine_refs], axis=0)
    other = jnp.concatenate([ref[...] for ref in other_refs], axis=0)
    scores = lax.dot_general(
        mine, other, (((1,), (1,)), ((), ())), preferred_element_type=f32
    )
    same = mine_ids_ref[...] == other_ids
    coeff = pair_coeff(scale_logit * scores + shift_logit, same)
    return jnp.dot(coeff, other, preferred_element_type=f32)


def most_kernel(blocks, mine_ids_ref, other_ids_ref, *refs):
    mine_refs, other_refs, part_ref = refs[:blocks], refs[blocks:-1], refs[-1]
    width = (blocks - 1) * mine_refs[0].shape[0]
    part_ref[...] = part_of(mine_refs, other_refs, mine_ids_ref, other_ids_ref[:, :width])


def rest_kernel(blocks, mine_ids_ref, other_ids_ref, part_ref, *refs):
    mine_refs, last_ref, (own_ref, *send_refs) = refs[:blocks], refs[blocks], refs[blocks + 1:]
    height = own_ref.shape[0]
    start = (blocks - 1) * height
    part = part_ref[...] + part_of(
        mine_refs, [last_ref], mine_ids_ref, other_ids_ref[:, start:]
    )
    own_ref[...] = part[:height]
    for k, ref in enumerate(send_refs):
        ref[...] = part[(k + 1) * height:(k + 2) * height].astype(bf16)


def grad_kernel(raw_ref, own_ref, *refs):
    *got_refs, keep_ref, send_ref = refs
    rows = keep_ref.shape[0]
    total = own_ref[...]
    for ref in got_refs:
        total = total + ref[...].astype(f32)
    grad = back_norm(*normalize(raw_ref[...]), total)
    even = is_even()
    keep_ref[...] = jnp.where(even, grad[:rows], grad[rows:])
    send_ref[...] = jnp.where(even, grad[rows:], grad[:rows])


def out_kernel(keep_ref, got_ref, img_ref, txt_ref):
    even = is_even()
    keep, got = keep_ref[...], got_ref[...]
    img_ref[...] = jnp.where(even, got, keep)
    txt_ref[...] = jnp.where(even, keep, got)


def local(image_embeds, text_embeds, pair_ids):
    rows, width = image_embeds.shape
    blocks = max(lax.axis_size("img") // 2, lax.axis_size("txt"))
    pair = jax.ShapeDtypeStruct((2 * rows, width), bf16)
    total = jax.ShapeDtypeStruct((2 * rows, width), f32)
    single = jax.ShapeDtypeStruct((rows, width), f32)
    ids = pair_ids.reshape(1, -1)
    far_txt = core_swap(text_embeds)
    far_img = core_swap(image_embeds)
    far_ids = core_swap(ids)
    near = jnp.concatenate([text_embeds, image_embeds])
    mine, other, raw = call(sides_kernel, [pair] * 3, [near, far_txt, far_img])
    mine = [mine] + [chip_swap(mine, k) for k in range(1, blocks)]
    count = blocks * 2 * rows
    mine_ids, other_ids, first = call(
        ids_kernel,
        [
            jax.ShapeDtypeStruct((count, 1), jnp.int32),
            jax.ShapeDtypeStruct((1, count), jnp.int32),
            pair,
        ],
        [ids, far_ids, mine[1]],
    )
    other = [other] + [core_swap(block) for block in [first] + mine[2:]]
    part = jax.ShapeDtypeStruct((count, width), f32)
    (part,) = call(
        functools.partial(most_kernel, blocks),
        [part],
        [mine_ids, other_ids, *mine, *other[:-1]],
        cost=LONG,
    )
    own, *send = call(
        functools.partial(rest_kernel, blocks),
        [total] + [pair] * (blocks - 1),
        [mine_ids, other_ids, part, *mine, other[-1]],
    )
    got = [chip_swap(block, k + 1) for k, block in enumerate(send)]
    keep, send = call(grad_kernel, [single] * 2, [raw, own, *got])
    return tuple(call(out_kernel, [single] * 2, [keep, core_swap(send)]))


def solution(mesh):
    return jax.shard_map(
        local,
        mesh=mesh,
        in_specs=(P(("img", "txt"), None), P(("txt", "img"), None), P("img")),
        out_specs=(P(("img", "txt"), None), P(("txt", "img"), None)),
        check_vma=False,
    )
```

time: 100 us -> 25.8 us (0.26)
  waiting for transfers between devices: 53.3 us -> 9.38 us
  blocking collectives: 24.7 us -> 0 us
  between operations: 14.1 us -> 0.69 us
  starting transfers between devices: 0.08 us -> 12.4 us
  other arithmetic: 4.91 us -> 0.79 us
  Pallas kernels: 0 us -> 2.34 us
  matrix products: 2.23 us -> 0 us
    reduce_scatter x2 -> x0, waiting for transfers between devices: 53.2 us -> none  [the longest x1 33.9 us: local(): txt_part = lax.psum_scatter(second, 'img', scatter_dimension=0, tiled=True)]
    all_gather x2 -> x0, blocking collectives: 24.7 us -> none  [the longest x1 15.1 us: local(): img_block = lax.all_gather(img_low, 'txt', axis=0, tiled=True)]
    ppermute x0 -> x13, starting transfers between devices: none -> 12.4 us  [the longest x6 10.2 us: chip_swap(): return lax.ppermute(block, ('img', 'txt'), pairs)]
    ppermute x0 -> x13, waiting for transfers between devices: none -> 9.38 us  [the longest x6 6.85 us: chip_swap(): return lax.ppermute(block, ('img', 'txt'), pairs)]
    reduce_sum x4 -> x0, other arithmetic: 3.3 us -> none  [the longest x2 2.29 us: back_norm(): inner = jnp.sum(unit * grad, axis=-1, keepdims=True)]
    pallas_call x0 -> x6, Pallas kernels: none -> 2.34 us  [call(): pl.pallas_call(kernel, out_shape=outs, in_specs=[VMEM] * len(args), out_s...]
    dot_general x3 -> x0, matrix products: 2.23 us -> none  [the longest x1 1.07 us: local(): lax.dot_general(coeff, img_block, (((0,), (0,)), ((), ())), preferred_ele...]
    mul x2 -> x0, other arithmetic: 1.43 us -> none  [back_norm(): return inverse * (grad - unit * inner)]
  transfers between devices with their start and end apart: 2 -> 13, of which waited for: 2 -> 8; matrix products, arithmetic and copies ran while one was open for 3% -> 3% of each run, Pallas kernels for 0% -> 3%
where the time goes in v5:
time: 25.8 us; the launch traced here: 25.6 us
  starting transfers between devices  12.4 us (48%)
  waiting for transfers between devices  9.38 us (36%)
  Pallas kernels  2.34 us (9%)
  other arithmetic  0.79 us (3%)
  between operations  0.69 us (3%)
    ppermute x6, starting transfers between devices, chip_swap(): return lax.ppermute(block, ('img', 'txt'), pairs)  10.2 us
    ppermute x6, waiting for transfers between devices, chip_swap(): return lax.ppermute(block, ('img', 'txt'), pairs)  6.85 us
    ppermute x7, waiting for transfers between devices, core_swap(): return lax.ppermute(block, 'img', [(i, i ^ 1) for i in range(size)])  2.53 us
    pallas_call x6, Pallas kernels, call(): pl.pallas_call(kernel, out_shape=outs, in_specs=[VMEM] * len(args), out_s...  2.34 us
    ppermute x7, starting transfers between devices, core_swap(): return lax.ppermute(block, 'img', [(i, i ^ 1) for i in range(size)])  2.19 us
    concatenate x1, other arithmetic, local(): near = jnp.concatenate([text_embeds, image_embeds])  0.79 us
  transfers between devices with their start and end apart: 13, of which 8 were waited for; matrix products, arithmetic and copies ran while one was open for 3% of the time, Pallas kernels for 3%

profile of v5, /device:TPU:0, one launch (start us, length us, event | category | flops | bytes accessed | tf_op | source)
XLA Modules:
  0.0 25.6 jit_solution(6382639295437413501)
XLA Ops:
  0.6 0.5 %collective-permute-start.1 = (bf16[16,1152]{1,0:T(8,128)(2,1)}, bf16[16,1152]{1,0:T(8,128)(2,1)S(1)}, u32[]{:S(2)}, u32[]{:S(2)}) collective-permute-start(bf16[16,1152]{1,0:T(8,128)(2,1)} %param.3), channel_id=1, source_target_pairs={{0,4},{4,0},{8,12},{12,8},{16,20},{20,16},{24,28},{28,24},{1,5},{5... | collective-permute-start | bytes 110600 | tf_op jit(solution)/shard_map/ppermute | solution.py:37
  1.2 0.8 %pad_maximum_fusion.own_ref = bf16[32,1152]{1,0:T(8,128)(2,1)S(1)} fusion(bf16[16,1152]{1,0:T(8,128)(2,1)} %param.3, bf16[16,1152]{1,0:T(8,128)(2,1)} %param.4), kind=kLoop, calls=%fused_computation | loop fusion | flops 147456 | bytes 147456 | tf_op jit(solution)/shard_map/concatenate | solution.py:171
  2.0 0.2 collective-permute-done.1.img_ref
  2.2 0.3 %collective-permute-done.txt_ref = bf16[16,1152]{1,0:T(8,128)(2,1)S(1)} collective-permute-done((bf16[16,1152]{1,0:T(8,128)(2,1)}, bf16[16,1152]{1,0:T(8,128)(2,1)S(1)}, u32[]{:S(2)}, u32[]{:S(2)}) %collective-permute-start) | collective-permute-done | bytes 36896 | tf_op jit(solution)/shard_map/ppermute | solution.py:37
  2.7 2.7 %collective-permute-start.4 = (bf16[32,1152]{1,0:T(8,128)(2,1)S(1)}, bf16[32,1152]{1,0:T(8,128)(2,1)S(1)}, u32[]{:S(2)}, u32[]{:S(2)}) collective-permute-start(bf16[32,1152]{1,0:T(8,128)(2,1)S(1)} %get-tuple-element.15.refs_0_), channel_id=1, source_target_pairs={{0,16},{1,17},{2,18},{3,19},{4,6},{5,7},{6,4},{7,5},{8,24},{9,25},... | collective-permute-start | bytes 221192 | tf_op jit(solution)/shard_map/ppermute | solution.py:49
  5.5 1.5 %collective-permute-start.3 = (bf16[32,1152]{1,0:T(8,128)(2,1)S(1)}, bf16[32,1152]{1,0:T(8,128)(2,1)S(1)}, u32[]{:S(2)}, u32[]{:S(2)}) collective-permute-start(bf16[32,1152]{1,0:T(8,128)(2,1)S(1)} %get-tuple-element.15.refs_0_), channel_id=1, source_target_pairs={{0,8},{1,9},{2,10},{3,11},{4,5},{5,4},{6,7},{7,6},{8,0},{9,1},{10,... | collective-permute-start | bytes 221192 | tf_op jit(solution)/shard_map/ppermute | solution.py:49
  7.0 0.9 %collective-permute-start.2 = (s32[1,64]{1,0:T(1,128)S(1)}, s32[1,64]{1,0:T(1,128)S(1)}, u32[]{:S(2)}, u32[]{:S(2)}) collective-permute-start(s32[1,64]{1,0:T(1,128)S(1)} %bitcast.1), channel_id=1, source_target_pairs={{0,4},{4,0},{8,12},{12,8},{16,20},{20,16},{24,28},{28,24},{1,5},{5... | collective-permute-start | bytes 776 | tf_op jit(solution)/shard_map/ppermute | solution.py:37
  7.9 2.4 %collective-permute-start.5 = (bf16[32,1152]{1,0:T(8,128)(2,1)S(1)}, bf16[32,1152]{1,0:T(8,128)(2,1)S(1)}, u32[]{:S(2)}, u32[]{:S(2)}) collective-permute-start(bf16[32,1152]{1,0:T(8,128)(2,1)S(1)} %get-tuple-element.15.refs_0_), channel_id=1, source_target_pairs={{0,24},{1,25},{2,26},{3,27},{4,7},{5,6},{6,5},{7,4},{8,16},{9,17},... | collective-permute-start | bytes 221192 | tf_op jit(solution)/shard_map/ppermute | solution.py:49
  10.4 0.4 %collective-permute-start.7 = (bf16[32,1152]{1,0:T(8,128)(2,1)S(1)}, bf16[32,1152]{1,0:T(8,128)(2,1)S(1)}, u32[]{:S(2)}, u32[]{:S(2)}) collective-permute-start(bf16[32,1152]{1,0:T(8,128)(2,1)S(1)} %collective-permute-done.4.refs_2_), channel_id=1, source_target_pairs={{0,4},{4,0},{8,12},{12,8},{16,20},{20,16},{24,28},{28,24},{1,5},{5... | collective-permute-start | bytes 221192 | tf_op jit(solution)/shard_map/ppermute | solution.py:37
  10.8 0.1 shard_map.51
  11.0 0.1 collective-permute-start.6
  11.1 2.1 %collective-permute-done.5.refs_3_ = bf16[32,1152]{1,0:T(8,128)(2,1)S(1)} collective-permute-done((bf16[32,1152]{1,0:T(8,128)(2,1)S(1)}, bf16[32,1152]{1,0:T(8,128)(2,1)S(1)}, u32[]{:S(2)}, u32[]{:S(2)}) %collective-permute-start.5) | collective-permute-done | bytes 73760 | tf_op jit(solution)/shard_map/ppermute | solution.py:49
  13.2 0.5 %shard_map.52.part_ref = f32[128,1152]{1,0:T(8,128)S(1)} custom-call(s32[128,1]{1,0:T(8,128)S(1)} %get-tuple-element.16.mine_ids_ref, s32[1,128]{1,0:T(1,128)S(1)} %get-tuple-element.17.other_ids_ref, bf16[32,1152]{1,0:T(8,128)(2,1)S(1)} %get-tuple-element.15.refs_0_, bf16[32,1152]{1,0:T(8,128)(2,1)S(1)} %collective-permute-done.3.piece_ref.refs_1_, ...), custom_call_target="tpu_custom_call" | custom-call | flops 10000000000 | bytes 10000000 | tf_op jit(solution)/shard_map/pallas_call | solution.py:58
  13.7 0.7 %collective-permute-done.8.refs_4_ = bf16[32,1152]{1,0:T(8,128)(2,1)S(1)} collective-permute-done((bf16[32,1152]{1,0:T(8,128)(2,1)S(1)}, bf16[32,1152]{1,0:T(8,128)(2,1)S(1)}, u32[]{:S(2)}, u32[]{:S(2)}) %collective-permute-start.8) | collective-permute-done | bytes 73760 | tf_op jit(solution)/shard_map/ppermute | solution.py:37
  14.4 0.6 %shard_map.53 = (f32[32,1152]{1,0:T(8,128)S(1)}, bf16[32,1152]{1,0:T(8,128)(2,1)S(1)}, bf16[32,1152]{1,0:T(8,128)(2,1)S(1)}, bf16[32,1152]{1,0:T(8,128)(2,1)S(1)}) custom-call(s32[128,1]{1,0:T(8,128)S(1)} %get-tuple-element.16.mine_ids_ref, s32[1,128]{1,0:T(1,128)S(1)} %get-tuple-element.17.other_ids_ref, f32[128,1152]{1,0:T(8,128)S(1)} %shard_map.52.part_ref, ...), custom_call_target="tpu_custom_call" | custom-call | tf_op jit(solution)/shard_map/pallas_call | solution.py:58
  15.1 1.6 %collective-permute-start.9 = (bf16[32,1152]{1,0:T(8,128)(2,1)S(1)}, bf16[32,1152]{1,0:T(8,128)(2,1)S(1)}, u32[]{:S(2)}, u32[]{:S(2)}) collective-permute-start(bf16[32,1152]{1,0:T(8,128)(2,1)S(1)} %get-tuple-element.21), channel_id=1, source_target_pairs={{0,8},{1,9},{2,10},{3,11},{4,5},{5,4},{6,7},{7,6},{8,0},{9,1},{10,... | collective-permute-start | bytes 221192 | tf_op jit(solution)/shard_map/ppermute | solution.py:49
  16.6 1.5 %collective-permute-start.10 = (bf16[32,1152]{1,0:T(8,128)(2,1)S(1)}, bf16[32,1152]{1,0:T(8,128)(2,1)S(1)}, u32[]{:S(2)}, u32[]{:S(2)}) collective-permute-start(bf16[32,1152]{1,0:T(8,128)(2,1)S(1)} %get-tuple-element.22), channel_id=1, source_target_pairs={{0,16},{1,17},{2,18},{3,19},{4,6},{5,7},{6,4},{7,5},{8,24},{9,25},... | collective-permute-start | bytes 221192 | tf_op jit(solution)/shard_map/ppermute | solution.py:49
  18.2 0.5 %collective-permute-start.11 = (bf16[32,1152]{1,0:T(8,128)(2,1)S(1)}, bf16[32,1152]{1,0:T(8,128)(2,1)S(1)}, u32[]{:S(2)}, u32[]{:S(2)}) collective-permute-start(bf16[32,1152]{1,0:T(8,128)(2,1)S(1)} %get-tuple-element.23), channel_id=1, source_target_pairs={{0,24},{1,25},{2,26},{3,27},{4,7},{5,6},{6,5},{7,4},{8,16},{9,17},... | collective-permute-start | bytes 221192 | tf_op jit(solution)/shard_map/ppermute | solution.py:49
  18.6 0.9 %collective-permute-done.9.refs_0_ = bf16[32,1152]{1,0:T(8,128)(2,1)S(1)} collective-permute-done((bf16[32,1152]{1,0:T(8,128)(2,1)S(1)}, bf16[32,1152]{1,0:T(8,128)(2,1)S(1)}, u32[]{:S(2)}, u32[]{:S(2)}) %collective-permute-start.9) | collective-permute-done | bytes 73760 | tf_op jit(solution)/shard_map/ppermute | solution.py:49
  19.5 1.5 %collective-permute-done.10.refs_1_ = bf16[32,1152]{1,0:T(8,128)(2,1)S(1)} collective-permute-done((bf16[32,1152]{1,0:T(8,128)(2,1)S(1)}, bf16[32,1152]{1,0:T(8,128)(2,1)S(1)}, u32[]{:S(2)}, u32[]{:S(2)}) %collective-permute-start.10) | collective-permute-done | bytes 73760 | tf_op jit(solution)/shard_map/ppermute | solution.py:49
  21.0 2.4 %collective-permute-done.11.refs_2_ = bf16[32,1152]{1,0:T(8,128)(2,1)S(1)} collective-permute-done((bf16[32,1152]{1,0:T(8,128)(2,1)S(1)}, bf16[32,1152]{1,0:T(8,128)(2,1)S(1)}, u32[]{:S(2)}, u32[]{:S(2)}) %collective-permute-start.11) | collective-permute-done | bytes 73760 | tf_op jit(solution)/shard_map/ppermute | solution.py:49
  23.4 0.2 shard_map.54
  23.7 1.3 %collective-permute-done.12.got_ref = f32[16,1152]{1,0:T(8,128)S(1)} collective-permute-done((f32[16,1152]{1,0:T(8,128)S(1)}, f32[16,1152]{1,0:T(8,128)S(1)}, u32[]{:S(2)}, u32[]{:S(2)}) %collective-permute-start.12) | collective-permute-done | bytes 73760 | tf_op jit(solution)/shard_map/ppermute | solution.py:37
  24.9 0.7 %shard_map.55 = (f32[16,1152]{1,0:T(8,128)}, f32[16,1152]{1,0:T(8,128)}) custom-call(f32[16,1152]{1,0:T(8,128)S(1)} %get-tuple-element.24.keep_ref, f32[16,1152]{1,0:T(8,128)S(1)} %collective-permute-done.12.got_ref), custom_call_target="tpu_custom_call" | custom-call | tf_op jit(solution)/shard_map/pallas_call | solution.py:58
  (11 shorter events, 0.3 us)
Async XLA Ops:
  0.6 1.6 %collective-permute-start.1 = (bf16[16,1152]{1,0:T(8,128)(2,1)}, bf16[16,1152]{1,0:T(8,128)(2,1)S(1)}, u32[]{:S(2)}, u32[]{:S(2)}) collective-permute-start(bf16[16,1152]{1,0:T(8,128)(2,1)} %param.3), channel_id=1, source_target_pairs={{0,4},{4,0},{8,12},{12,8},{16,20},{20,16},{24,28},{28,24},{1,5},{5... | collective-permute-start | bytes 110600 | tf_op jit(solution)/shard_map/ppermute | solution.py:37
  1.1 1.4 %collective-permute-start = (bf16[16,1152]{1,0:T(8,128)(2,1)}, bf16[16,1152]{1,0:T(8,128)(2,1)S(1)}, u32[]{:S(2)}, u32[]{:S(2)}) collective-permute-start(bf16[16,1152]{1,0:T(8,128)(2,1)} %param.4), channel_id=1, source_target_pairs={{0,4},{4,0},{8,12},{12,8},{16,20},{20,16},{24,28},{28,24},{1,5},{5... | collective-permute-start | bytes 110600 | tf_op jit(solution)/shard_map/ppermute | solution.py:37
  2.7 4.2 %copy-start = (s32[64]{0:T(128)S(1)}, s32[64]{0:T(128)}, u32[]{:S(2)}) copy-start(s32[64]{0:T(128)} %param.5) | copy-start | bytes 772
  2.7 7.6 %collective-permute-start.4 = (bf16[32,1152]{1,0:T(8,128)(2,1)S(1)}, bf16[32,1152]{1,0:T(8,128)(2,1)S(1)}, u32[]{:S(2)}, u32[]{:S(2)}) collective-permute-start(bf16[32,1152]{1,0:T(8,128)(2,1)S(1)} %get-tuple-element.15.refs_0_), channel_id=1, source_target_pairs={{0,16},{1,17},{2,18},{3,19},{4,6},{5,7},{6,4},{7,5},{8,24},{9,25},... | collective-permute-start | bytes 221192 | tf_op jit(solution)/shard_map/ppermute | solution.py:49
  5.5 5.3 %collective-permute-start.3 = (bf16[32,1152]{1,0:T(8,128)(2,1)S(1)}, bf16[32,1152]{1,0:T(8,128)(2,1)S(1)}, u32[]{:S(2)}, u32[]{:S(2)}) collective-permute-start(bf16[32,1152]{1,0:T(8,128)(2,1)S(1)} %get-tuple-element.15.refs_0_), channel_id=1, source_target_pairs={{0,8},{1,9},{2,10},{3,11},{4,5},{5,4},{6,7},{7,6},{8,0},{9,1},{10,... | collective-permute-start | bytes 221192 | tf_op jit(solution)/shard_map/ppermute | solution.py:49
  7.0 3.8 %collective-permute-start.2 = (s32[1,64]{1,0:T(1,128)S(1)}, s32[1,64]{1,0:T(1,128)S(1)}, u32[]{:S(2)}, u32[]{:S(2)}) collective-permute-start(s32[1,64]{1,0:T(1,128)S(1)} %bitcast.1), channel_id=1, source_target_pairs={{0,4},{4,0},{8,12},{12,8},{16,20},{20,16},{24,28},{28,24},{1,5},{5... | collective-permute-start | bytes 776 | tf_op jit(solution)/shard_map/ppermute | solution.py:37
  7.9 5.3 %collective-permute-start.5 = (bf16[32,1152]{1,0:T(8,128)(2,1)S(1)}, bf16[32,1152]{1,0:T(8,128)(2,1)S(1)}, u32[]{:S(2)}, u32[]{:S(2)}) collective-permute-start(bf16[32,1152]{1,0:T(8,128)(2,1)S(1)} %get-tuple-element.15.refs_0_), channel_id=1, source_target_pairs={{0,24},{1,25},{2,26},{3,27},{4,7},{5,6},{6,5},{7,4},{8,16},{9,17},... | collective-permute-start | bytes 221192 | tf_op jit(solution)/shard_map/ppermute | solution.py:49
  10.4 2.8 %collective-permute-start.7 = (bf16[32,1152]{1,0:T(8,128)(2,1)S(1)}, bf16[32,1152]{1,0:T(8,128)(2,1)S(1)}, u32[]{:S(2)}, u32[]{:S(2)}) collective-permute-start(bf16[32,1152]{1,0:T(8,128)(2,1)S(1)} %collective-permute-done.4.refs_2_), channel_id=1, source_target_pairs={{0,4},{4,0},{8,12},{12,8},{16,20},{20,16},{24,28},{28,24},{1,5},{5... | collective-permute-start | bytes 221192 | tf_op jit(solution)/shard_map/ppermute | solution.py:37
  11.0 2.2 %collective-permute-start.6 = (bf16[32,1152]{1,0:T(8,128)(2,1)S(1)}, bf16[32,1152]{1,0:T(8,128)(2,1)S(1)}, u32[]{:S(2)}, u32[]{:S(2)}) collective-permute-start(bf16[32,1152]{1,0:T(8,128)(2,1)S(1)} %get-tuple-element.19), channel_id=1, source_target_pairs={{0,4},{4,0},{8,12},{12,8},{16,20},{20,16},{24,28},{28,24},{1,5},{5... | collective-permute-start | bytes 221192 | tf_op jit(solution)/shard_map/ppermute | solution.py:37
  13.2 1.3 %collective-permute-start.8 = (bf16[32,1152]{1,0:T(8,128)(2,1)S(1)}, bf16[32,1152]{1,0:T(8,128)(2,1)S(1)}, u32[]{:S(2)}, u32[]{:S(2)}) collective-permute-start(bf16[32,1152]{1,0:T(8,128)(2,1)S(1)} %collective-permute-done.5.refs_3_), channel_id=1, source_target_pairs={{0,4},{4,0},{8,12},{12,8},{16,20},{20,16},{24,28},{28,24},{1,5},{5... | collective-permute-start | bytes 221192 | tf_op jit(solution)/shard_map/ppermute | solution.py:37
  15.1 4.4 %collective-permute-start.9 = (bf16[32,1152]{1,0:T(8,128)(2,1)S(1)}, bf16[32,1152]{1,0:T(8,128)(2,1)S(1)}, u32[]{:S(2)}, u32[]{:S(2)}) collective-permute-start(bf16[32,1152]{1,0:T(8,128)(2,1)S(1)} %get-tuple-element.21), channel_id=1, source_target_pairs={{0,8},{1,9},{2,10},{3,11},{4,5},{5,4},{6,7},{7,6},{8,0},{9,1},{10,... | collective-permute-start | bytes 221192 | tf_op jit(solution)/shard_map/ppermute | solution.py:49
  16.6 4.4 %collective-permute-start.10 = (bf16[32,1152]{1,0:T(8,128)(2,1)S(1)}, bf16[32,1152]{1,0:T(8,128)(2,1)S(1)}, u32[]{:S(2)}, u32[]{:S(2)}) collective-permute-start(bf16[32,1152]{1,0:T(8,128)(2,1)S(1)} %get-tuple-element.22), channel_id=1, source_target_pairs={{0,16},{1,17},{2,18},{3,19},{4,6},{5,7},{6,4},{7,5},{8,24},{9,25},... | collective-permute-start | bytes 221192 | tf_op jit(solution)/shard_map/ppermute | solution.py:49
  18.2 5.3 %collective-permute-start.11 = (bf16[32,1152]{1,0:T(8,128)(2,1)S(1)}, bf16[32,1152]{1,0:T(8,128)(2,1)S(1)}, u32[]{:S(2)}, u32[]{:S(2)}) collective-permute-start(bf16[32,1152]{1,0:T(8,128)(2,1)S(1)} %get-tuple-element.23), channel_id=1, source_target_pairs={{0,24},{1,25},{2,26},{3,27},{4,7},{5,6},{6,5},{7,4},{8,16},{9,17},... | collective-permute-start | bytes 221192 | tf_op jit(solution)/shard_map/ppermute | solution.py:49
  23.6 1.3 %collective-permute-start.12 = (f32[16,1152]{1,0:T(8,128)S(1)}, f32[16,1152]{1,0:T(8,128)S(1)}, u32[]{:S(2)}, u32[]{:S(2)}) collective-permute-start(f32[16,1152]{1,0:T(8,128)S(1)} %get-tuple-element.25), channel_id=1, source_target_pairs={{0,4},{4,0},{8,12},{12,8},{16,20},{20,16},{24,28},{28,24},{1,5},{5... | collective-permute-start | bytes 221192 | tf_op jit(solution)/shard_map/ppermute | solution.py:37

commit v6 on v5

--- a/solution.py
+++ b/solution.py
@@ -87,7 +87,8 @@
     me_txt = lax.axis_index("txt")
     n_img = lax.axis_size("img")
     row = lax.broadcasted_iota(jnp.int32, (count, 1), 0)
-    chip, core, j = row // (2 * rows), row // rows % 2, row % rows
+    block, core, j = row // (2 * rows), row // rows % 2, row % rows
+    chip = jnp.where(block == 0, 0, count // (2 * rows) - block)
     txt_ids = (me_txt * n_img + (((me_img // 2) ^ chip) * 2 + core)) * rows + j
     source = (me_txt ^ chip) * rows + j
     here = lax.broadcasted_iota(jnp.int32, (count, ids.shape[1]), 1) == source
@@ -170,7 +171,8 @@
     far_ids = core_swap(ids)
     near = jnp.concatenate([text_embeds, image_embeds])
     mine, other, raw = call(sides_kernel, [pair] * 3, [near, far_txt, far_img])
-    mine = [mine] + [chip_swap(mine, k) for k in range(1, blocks)]
+    order = list(range(blocks - 1, 0, -1))
+    mine = [mine] + [chip_swap(mine, k) for k in order]
     count = blocks * 2 * rows
     mine_ids, other_ids, first = call(
         ids_kernel,
@@ -194,7 +196,7 @@
         [total] + [pair] * (blocks - 1),
         [mine_ids, other_ids, part, *mine, other[-1]],
     )
-    got = [chip_swap(block, k + 1) for k, block in enumerate(send)]
+    got = [chip_swap(block, k) for k, block in zip(order, send)]
     keep, send = call(grad_kernel, [single] * 2, [raw, own, *got])
     return tuple(call(out_kernel, [single] * 2, [keep, core_swap(send)]))
 

time: 25.8 us -> 23.8 us (0.922)
  waiting for transfers between devices: 9.38 us -> 8.05 us
  starting transfers between devices: 12.4 us -> 11.7 us
    ppermute x6, waiting for transfers between devices: 6.85 us -> 5.47 us  [chip_swap(): return lax.ppermute(block, ('img', 'txt'), pairs)]
    ppermute x6, starting transfers between devices: 10.2 us -> 9.22 us  [chip_swap(): return lax.ppermute(block, ('img', 'txt'), pairs)]
    ppermute x7, starting transfers between devices: 2.19 us -> 2.51 us  [core_swap(): return lax.ppermute(block, 'img', [(i, i ^ 1) for i in range(size)])]
  transfers between devices with their start and end apart: 13 -> 13, of which waited for: 8 -> 9; matrix products, arithmetic and copies ran while one was open for 3% -> 3% of each run, Pallas kernels for 3% -> 3%
where the time goes in v6:
time: 23.8 us; the launch traced here: 23.6 us
  starting transfers between devices  11.7 us (49%)
  waiting for transfers between devices  8.05 us (34%)
  Pallas kernels  2.34 us (10%)
  other arithmetic  0.79 us (3%)
  between operations  0.69 us (3%)
    ppermute x6, starting transfers between devices, chip_swap(): return lax.ppermute(block, ('img', 'txt'), pairs)  9.22 us
    ppermute x6, waiting for transfers between devices, chip_swap(): return lax.ppermute(block, ('img', 'txt'), pairs)  5.47 us
    ppermute x7, waiting for transfers between devices, core_swap(): return lax.ppermute(block, 'img', [(i, i ^ 1) for i in range(size)])  2.58 us
    ppermute x7, starting transfers between devices, core_swap(): return lax.ppermute(block, 'img', [(i, i ^ 1) for i in range(size)])  2.51 us
    pallas_call x6, Pallas kernels, call(): pl.pallas_call(kernel, out_shape=outs, in_specs=[VMEM] * len(args), out_s...  2.34 us
    concatenate x1, other arithmetic, local(): near = jnp.concatenate([text_embeds, image_embeds])  0.79 us
  transfers between devices with their start and end apart: 13, of which 9 were waited for; matrix products, arithmetic and copies ran while one was open for 3% of the time, Pallas kernels for 3%

profile of v6, /device:TPU:0, one launch (start us, length us, event | category | flops | bytes accessed | tf_op | source)
XLA Modules:
  0.0 23.6 jit_solution(15199842032637726523)
XLA Ops:
  0.6 0.5 %collective-permute-start.1 = (bf16[16,1152]{1,0:T(8,128)(2,1)}, bf16[16,1152]{1,0:T(8,128)(2,1)S(1)}, u32[]{:S(2)}, u32[]{:S(2)}) collective-permute-start(bf16[16,1152]{1,0:T(8,128)(2,1)} %param.3), channel_id=1, source_target_pairs={{0,4},{4,0},{8,12},{12,8},{16,20},{20,16},{24,28},{28,24},{1,5},{5... | collective-permute-start | bytes 110600 | tf_op jit(solution)/shard_map/ppermute | solution.py:37
  1.2 0.8 %pad_maximum_fusion.own_ref = bf16[32,1152]{1,0:T(8,128)(2,1)S(1)} fusion(bf16[16,1152]{1,0:T(8,128)(2,1)} %param.3, bf16[16,1152]{1,0:T(8,128)(2,1)} %param.4), kind=kLoop, calls=%fused_computation | loop fusion | flops 147456 | bytes 147456 | tf_op jit(solution)/shard_map/concatenate | solution.py:172
  2.0 0.2 collective-permute-done.1.img_ref
  2.2 0.3 %collective-permute-done.txt_ref = bf16[16,1152]{1,0:T(8,128)(2,1)S(1)} collective-permute-done((bf16[16,1152]{1,0:T(8,128)(2,1)}, bf16[16,1152]{1,0:T(8,128)(2,1)S(1)}, u32[]{:S(2)}, u32[]{:S(2)}) %collective-permute-start) | collective-permute-done | bytes 36896 | tf_op jit(solution)/shard_map/ppermute | solution.py:37
  2.7 2.7 %collective-permute-start.4 = (bf16[32,1152]{1,0:T(8,128)(2,1)S(1)}, bf16[32,1152]{1,0:T(8,128)(2,1)S(1)}, u32[]{:S(2)}, u32[]{:S(2)}) collective-permute-start(bf16[32,1152]{1,0:T(8,128)(2,1)S(1)} %get-tuple-element.15.refs_0_), channel_id=1, source_target_pairs={{0,16},{1,17},{2,18},{3,19},{4,6},{5,7},{6,4},{7,5},{8,24},{9,25},... | collective-permute-start | bytes 221192 | tf_op jit(solution)/shard_map/ppermute | solution.py:49
  5.5 1.4 %collective-permute-start.3 = (bf16[32,1152]{1,0:T(8,128)(2,1)S(1)}, bf16[32,1152]{1,0:T(8,128)(2,1)S(1)}, u32[]{:S(2)}, u32[]{:S(2)}) collective-permute-start(bf16[32,1152]{1,0:T(8,128)(2,1)S(1)} %get-tuple-element.15.refs_0_), channel_id=1, source_target_pairs={{0,24},{1,25},{2,26},{3,27},{4,7},{5,6},{6,5},{7,4},{8,16},{9,17},... | collective-permute-start | bytes 221192 | tf_op jit(solution)/shard_map/ppermute | solution.py:49
  6.9 0.8 %collective-permute-start.2 = (s32[1,64]{1,0:T(1,128)S(1)}, s32[1,64]{1,0:T(1,128)S(1)}, u32[]{:S(2)}, u32[]{:S(2)}) collective-permute-start(s32[1,64]{1,0:T(1,128)S(1)} %bitcast.1), channel_id=1, source_target_pairs={{0,4},{4,0},{8,12},{12,8},{16,20},{20,16},{24,28},{28,24},{1,5},{5... | collective-permute-start | bytes 776 | tf_op jit(solution)/shard_map/ppermute | solution.py:37
  7.7 1.5 %collective-permute-start.5 = (bf16[32,1152]{1,0:T(8,128)(2,1)S(1)}, bf16[32,1152]{1,0:T(8,128)(2,1)S(1)}, u32[]{:S(2)}, u32[]{:S(2)}) collective-permute-start(bf16[32,1152]{1,0:T(8,128)(2,1)S(1)} %get-tuple-element.15.refs_0_), channel_id=1, source_target_pairs={{0,8},{1,9},{2,10},{3,11},{4,5},{5,4},{6,7},{7,6},{8,0},{9,1},{10,... | collective-permute-start | bytes 221192 | tf_op jit(solution)/shard_map/ppermute | solution.py:49
  9.2 1.5 %collective-permute-done.3.piece_ref.refs_1_ = bf16[32,1152]{1,0:T(8,128)(2,1)S(1)} collective-permute-done((bf16[32,1152]{1,0:T(8,128)(2,1)S(1)}, bf16[32,1152]{1,0:T(8,128)(2,1)S(1)}, u32[]{:S(2)}, u32[]{:S(2)}) %collective-permute-start.3) | collective-permute-done | bytes 73760 | tf_op jit(solution)/shard_map/ppermute | solution.py:49
  10.7 0.1 shard_map.51
  10.9 1.0 %collective-permute-start.6 = (bf16[32,1152]{1,0:T(8,128)(2,1)S(1)}, bf16[32,1152]{1,0:T(8,128)(2,1)S(1)}, u32[]{:S(2)}, u32[]{:S(2)}) collective-permute-start(bf16[32,1152]{1,0:T(8,128)(2,1)S(1)} %get-tuple-element.19), channel_id=1, source_target_pairs={{0,4},{4,0},{8,12},{12,8},{16,20},{20,16},{24,28},{28,24},{1,5},{5... | collective-permute-start | bytes 221192 | tf_op jit(solution)/shard_map/ppermute | solution.py:37
  11.9 0.1 collective-permute-done.5.refs_3_
  12.1 0.8 %collective-permute-done.6.refs_5_ = bf16[32,1152]{1,0:T(8,128)(2,1)S(1)} collective-permute-done((bf16[32,1152]{1,0:T(8,128)(2,1)S(1)}, bf16[32,1152]{1,0:T(8,128)(2,1)S(1)}, u32[]{:S(2)}, u32[]{:S(2)}) %collective-permute-start.6) | collective-permute-done | bytes 73760 | tf_op jit(solution)/shard_map/ppermute | solution.py:37
  12.8 0.5 %shard_map.52.part_ref = f32[128,1152]{1,0:T(8,128)S(1)} custom-call(s32[128,1]{1,0:T(8,128)S(1)} %get-tuple-element.16.mine_ids_ref, s32[1,128]{1,0:T(1,128)S(1)} %get-tuple-element.17.other_ids_ref, bf16[32,1152]{1,0:T(8,128)(2,1)S(1)} %get-tuple-element.15.refs_0_, bf16[32,1152]{1,0:T(8,128)(2,1)S(1)} %collective-permute-done.3.piece_ref.refs_1_, ...), custom_call_target="tpu_custom_call" | custom-call | flops 10000000000 | bytes 10000000 | tf_op jit(solution)/shard_map/pallas_call | solution.py:58
  13.4 0.7 %shard_map.53 = (f32[32,1152]{1,0:T(8,128)S(1)}, bf16[32,1152]{1,0:T(8,128)(2,1)S(1)}, bf16[32,1152]{1,0:T(8,128)(2,1)S(1)}, bf16[32,1152]{1,0:T(8,128)(2,1)S(1)}) custom-call(s32[128,1]{1,0:T(8,128)S(1)} %get-tuple-element.16.mine_ids_ref, s32[1,128]{1,0:T(1,128)S(1)} %get-tuple-element.17.other_ids_ref, f32[128,1152]{1,0:T(8,128)S(1)} %shard_map.52.part_ref, ...), custom_call_target="tpu_custom_call" | custom-call | tf_op jit(solution)/shard_map/pallas_call | solution.py:58
  14.0 2.5 %collective-permute-start.9 = (bf16[32,1152]{1,0:T(8,128)(2,1)S(1)}, bf16[32,1152]{1,0:T(8,128)(2,1)S(1)}, u32[]{:S(2)}, u32[]{:S(2)}) collective-permute-start(bf16[32,1152]{1,0:T(8,128)(2,1)S(1)} %get-tuple-element.21), channel_id=1, source_target_pairs={{0,24},{1,25},{2,26},{3,27},{4,7},{5,6},{6,5},{7,4},{8,16},{9,17},... | collective-permute-start | bytes 221192 | tf_op jit(solution)/shard_map/ppermute | solution.py:49
  16.5 0.5 %collective-permute-start.10 = (bf16[32,1152]{1,0:T(8,128)(2,1)S(1)}, bf16[32,1152]{1,0:T(8,128)(2,1)S(1)}, u32[]{:S(2)}, u32[]{:S(2)}) collective-permute-start(bf16[32,1152]{1,0:T(8,128)(2,1)S(1)} %get-tuple-element.22), channel_id=1, source_target_pairs={{0,16},{1,17},{2,18},{3,19},{4,6},{5,7},{6,4},{7,5},{8,24},{9,25},... | collective-permute-start | bytes 221192 | tf_op jit(solution)/shard_map/ppermute | solution.py:49
  17.0 0.5 %collective-permute-start.11 = (bf16[32,1152]{1,0:T(8,128)(2,1)S(1)}, bf16[32,1152]{1,0:T(8,128)(2,1)S(1)}, u32[]{:S(2)}, u32[]{:S(2)}) collective-permute-start(bf16[32,1152]{1,0:T(8,128)(2,1)S(1)} %get-tuple-element.23), channel_id=1, source_target_pairs={{0,8},{1,9},{2,10},{3,11},{4,5},{5,4},{6,7},{7,6},{8,0},{9,1},{10,... | collective-permute-start | bytes 221192 | tf_op jit(solution)/shard_map/ppermute | solution.py:49
  17.6 1.8 %collective-permute-done.9.refs_0_ = bf16[32,1152]{1,0:T(8,128)(2,1)S(1)} collective-permute-done((bf16[32,1152]{1,0:T(8,128)(2,1)S(1)}, bf16[32,1152]{1,0:T(8,128)(2,1)S(1)}, u32[]{:S(2)}, u32[]{:S(2)}) %collective-permute-start.9) | collective-permute-done | bytes 73760 | tf_op jit(solution)/shard_map/ppermute | solution.py:49
  19.3 1.5 %collective-permute-done.10.refs_1_ = bf16[32,1152]{1,0:T(8,128)(2,1)S(1)} collective-permute-done((bf16[32,1152]{1,0:T(8,128)(2,1)S(1)}, bf16[32,1152]{1,0:T(8,128)(2,1)S(1)}, u32[]{:S(2)}, u32[]{:S(2)}) %collective-permute-start.10) | collective-permute-done | bytes 73760 | tf_op jit(solution)/shard_map/ppermute | solution.py:49
  20.9 0.5 %collective-permute-done.11.refs_2_ = bf16[32,1152]{1,0:T(8,128)(2,1)S(1)} collective-permute-done((bf16[32,1152]{1,0:T(8,128)(2,1)S(1)}, bf16[32,1152]{1,0:T(8,128)(2,1)S(1)}, u32[]{:S(2)}, u32[]{:S(2)}) %collective-permute-start.11) | collective-permute-done | bytes 73760 | tf_op jit(solution)/shard_map/ppermute | solution.py:49
  21.4 0.2 shard_map.54
  21.7 1.3 %collective-permute-done.12.got_ref = f32[16,1152]{1,0:T(8,128)S(1)} collective-permute-done((f32[16,1152]{1,0:T(8,128)S(1)}, f32[16,1152]{1,0:T(8,128)S(1)}, u32[]{:S(2)}, u32[]{:S(2)}) %collective-permute-start.12) | collective-permute-done | bytes 73760 | tf_op jit(solution)/shard_map/ppermute | solution.py:37
  22.9 0.7 %shard_map.55 = (f32[16,1152]{1,0:T(8,128)}, f32[16,1152]{1,0:T(8,128)}) custom-call(f32[16,1152]{1,0:T(8,128)S(1)} %get-tuple-element.24.keep_ref, f32[16,1152]{1,0:T(8,128)S(1)} %collective-permute-done.12.got_ref), custom_call_target="tpu_custom_call" | custom-call | tf_op jit(solution)/shard_map/pallas_call | solution.py:58
  (11 shorter events, 0.3 us)
Async XLA Ops:
  0.6 1.6 %collective-permute-start.1 = (bf16[16,1152]{1,0:T(8,128)(2,1)}, bf16[16,1152]{1,0:T(8,128)(2,1)S(1)}, u32[]{:S(2)}, u32[]{:S(2)}) collective-permute-start(bf16[16,1152]{1,0:T(8,128)(2,1)} %param.3), channel_id=1, source_target_pairs={{0,4},{4,0},{8,12},{12,8},{16,20},{20,16},{24,28},{28,24},{1,5},{5... | collective-permute-start | bytes 110600 | tf_op jit(solution)/shard_map/ppermute | solution.py:37
  1.1 1.4 %collective-permute-start = (bf16[16,1152]{1,0:T(8,128)(2,1)}, bf16[16,1152]{1,0:T(8,128)(2,1)S(1)}, u32[]{:S(2)}, u32[]{:S(2)}) collective-permute-start(bf16[16,1152]{1,0:T(8,128)(2,1)} %param.4), channel_id=1, source_target_pairs={{0,4},{4,0},{8,12},{12,8},{16,20},{20,16},{24,28},{28,24},{1,5},{5... | collective-permute-start | bytes 110600 | tf_op jit(solution)/shard_map/ppermute | solution.py:37
  2.7 4.2 %copy-start = (s32[64]{0:T(128)S(1)}, s32[64]{0:T(128)}, u32[]{:S(2)}) copy-start(s32[64]{0:T(128)} %param.5) | copy-start | bytes 772
  2.7 6.5 %collective-permute-start.4 = (bf16[32,1152]{1,0:T(8,128)(2,1)S(1)}, bf16[32,1152]{1,0:T(8,128)(2,1)S(1)}, u32[]{:S(2)}, u32[]{:S(2)}) collective-permute-start(bf16[32,1152]{1,0:T(8,128)(2,1)S(1)} %get-tuple-element.15.refs_0_), channel_id=1, source_target_pairs={{0,16},{1,17},{2,18},{3,19},{4,6},{5,7},{6,4},{7,5},{8,24},{9,25},... | collective-permute-start | bytes 221192 | tf_op jit(solution)/shard_map/ppermute | solution.py:49
  5.5 5.3 %collective-permute-start.3 = (bf16[32,1152]{1,0:T(8,128)(2,1)S(1)}, bf16[32,1152]{1,0:T(8,128)(2,1)S(1)}, u32[]{:S(2)}, u32[]{:S(2)}) collective-permute-start(bf16[32,1152]{1,0:T(8,128)(2,1)S(1)} %get-tuple-element.15.refs_0_), channel_id=1, source_target_pairs={{0,24},{1,25},{2,26},{3,27},{4,7},{5,6},{6,5},{7,4},{8,16},{9,17},... | collective-permute-start | bytes 221192 | tf_op jit(solution)/shard_map/ppermute | solution.py:49
  6.9 2.3 %collective-permute-start.2 = (s32[1,64]{1,0:T(1,128)S(1)}, s32[1,64]{1,0:T(1,128)S(1)}, u32[]{:S(2)}, u32[]{:S(2)}) collective-permute-start(s32[1,64]{1,0:T(1,128)S(1)} %bitcast.1), channel_id=1, source_target_pairs={{0,4},{4,0},{8,12},{12,8},{16,20},{20,16},{24,28},{28,24},{1,5},{5... | collective-permute-start | bytes 776 | tf_op jit(solution)/shard_map/ppermute | solution.py:37
  7.7 4.4 %collective-permute-start.5 = (bf16[32,1152]{1,0:T(8,128)(2,1)S(1)}, bf16[32,1152]{1,0:T(8,128)(2,1)S(1)}, u32[]{:S(2)}, u32[]{:S(2)}) collective-permute-start(bf16[32,1152]{1,0:T(8,128)(2,1)S(1)} %get-tuple-element.15.refs_0_), channel_id=1, source_target_pairs={{0,8},{1,9},{2,10},{3,11},{4,5},{5,4},{6,7},{7,6},{8,0},{9,1},{10,... | collective-permute-start | bytes 221192 | tf_op jit(solution)/shard_map/ppermute | solution.py:49
  9.2 2.9 %collective-permute-start.7 = (bf16[32,1152]{1,0:T(8,128)(2,1)S(1)}, bf16[32,1152]{1,0:T(8,128)(2,1)S(1)}, u32[]{:S(2)}, u32[]{:S(2)}) collective-permute-start(bf16[32,1152]{1,0:T(8,128)(2,1)S(1)} %collective-permute-done.4.refs_2_), channel_id=1, source_target_pairs={{0,4},{4,0},{8,12},{12,8},{16,20},{20,16},{24,28},{28,24},{1,5},{5... | collective-permute-start | bytes 221192 | tf_op jit(solution)/shard_map/ppermute | solution.py:37
  10.9 2.0 %collective-permute-start.6 = (bf16[32,1152]{1,0:T(8,128)(2,1)S(1)}, bf16[32,1152]{1,0:T(8,128)(2,1)S(1)}, u32[]{:S(2)}, u32[]{:S(2)}) collective-permute-start(bf16[32,1152]{1,0:T(8,128)(2,1)S(1)} %get-tuple-element.19), channel_id=1, source_target_pairs={{0,4},{4,0},{8,12},{12,8},{16,20},{20,16},{24,28},{28,24},{1,5},{5... | collective-permute-start | bytes 221192 | tf_op jit(solution)/shard_map/ppermute | solution.py:37
  12.1 1.3 %collective-permute-start.8 = (bf16[32,1152]{1,0:T(8,128)(2,1)S(1)}, bf16[32,1152]{1,0:T(8,128)(2,1)S(1)}, u32[]{:S(2)}, u32[]{:S(2)}) collective-permute-start(bf16[32,1152]{1,0:T(8,128)(2,1)S(1)} %collective-permute-done.5.refs_3_), channel_id=1, source_target_pairs={{0,4},{4,0},{8,12},{12,8},{16,20},{20,16},{24,28},{28,24},{1,5},{5... | collective-permute-start | bytes 221192 | tf_op jit(solution)/shard_map/ppermute | solution.py:37
  14.0 5.3 %collective-permute-start.9 = (bf16[32,1152]{1,0:T(8,128)(2,1)S(1)}, bf16[32,1152]{1,0:T(8,128)(2,1)S(1)}, u32[]{:S(2)}, u32[]{:S(2)}) collective-permute-start(bf16[32,1152]{1,0:T(8,128)(2,1)S(1)} %get-tuple-element.21), channel_id=1, source_target_pairs={{0,24},{1,25},{2,26},{3,27},{4,7},{5,6},{6,5},{7,4},{8,16},{9,17},... | collective-permute-start | bytes 221192 | tf_op jit(solution)/shard_map/ppermute | solution.py:49
  16.5 4.4 %collective-permute-start.10 = (bf16[32,1152]{1,0:T(8,128)(2,1)S(1)}, bf16[32,1152]{1,0:T(8,128)(2,1)S(1)}, u32[]{:S(2)}, u32[]{:S(2)}) collective-permute-start(bf16[32,1152]{1,0:T(8,128)(2,1)S(1)} %get-tuple-element.22), channel_id=1, source_target_pairs={{0,16},{1,17},{2,18},{3,19},{4,6},{5,7},{6,4},{7,5},{8,24},{9,25},... | collective-permute-start | bytes 221192 | tf_op jit(solution)/shard_map/ppermute | solution.py:49
  17.0 4.4 %collective-permute-start.11 = (bf16[32,1152]{1,0:T(8,128)(2,1)S(1)}, bf16[32,1152]{1,0:T(8,128)(2,1)S(1)}, u32[]{:S(2)}, u32[]{:S(2)}) collective-permute-start(bf16[32,1152]{1,0:T(8,128)(2,1)S(1)} %get-tuple-element.23), channel_id=1, source_target_pairs={{0,8},{1,9},{2,10},{3,11},{4,5},{5,4},{6,7},{7,6},{8,0},{9,1},{10,... | collective-permute-start | bytes 221192 | tf_op jit(solution)/shard_map/ppermute | solution.py:49
  21.6 1.3 %collective-permute-start.12 = (f32[16,1152]{1,0:T(8,128)S(1)}, f32[16,1152]{1,0:T(8,128)S(1)}, u32[]{:S(2)}, u32[]{:S(2)}) collective-permute-start(f32[16,1152]{1,0:T(8,128)S(1)} %get-tuple-element.25), channel_id=1, source_target_pairs={{0,4},{4,0},{8,12},{12,8},{16,20},{20,16},{24,28},{28,24},{1,5},{5... | collective-permute-start | bytes 221192 | tf_op jit(solution)/shard_map/ppermute | solution.py:37

commit v7 on v6

--- a/solution.py
+++ b/solution.py
@@ -37,15 +37,15 @@
     return lax.ppermute(block, "img", [(i, i ^ 1) for i in range(size)])
 
 
-def chip_swap(block, distance):
+def chip_swap(block, distance, cross=0):
     n_img, n_txt = lax.axis_size("img"), lax.axis_size("txt")
     pairs = []
     for img in range(n_img):
         for txt in range(n_txt):
             if img % 2 == 0 and distance < n_img // 2:
-                pairs.append((img * n_txt + txt, (img ^ (2 * distance)) * n_txt + txt))
+                pairs.append((img * n_txt + txt, (img ^ (2 * distance) ^ cross) * n_txt + txt))
             if img % 2 == 1 and distance < n_txt:
-                pairs.append((img * n_txt + txt, img * n_txt + (txt ^ distance)))
+                pairs.append((img * n_txt + txt, (img ^ cross) * n_txt + (txt ^ distance)))
     return lax.ppermute(block, ("img", "txt"), pairs)
 
 
@@ -67,7 +67,7 @@
     )(*args)
 
 
-def sides_kernel(own_ref, txt_ref, img_ref, mine_ref, other_ref, raw_ref):
+def sides_kernel(own_ref, txt_ref, img_ref, mine_ref, other_ref):
     rows = txt_ref.shape[0]
     even = is_even()
     own = normalize(own_ref[...])[0].astype(bf16)
@@ -78,8 +78,6 @@
     mine_ref[rows:, :] = jnp.where(even, far_txt, own_img)
     other_ref[:rows, :] = jnp.where(even, own_img, far_txt)
     other_ref[rows:, :] = jnp.where(even, far_img, own_txt)
-    raw_ref[:rows, :] = jnp.where(even, own_ref[:rows, :], img_ref[...])
-    raw_ref[rows:, :] = jnp.where(even, txt_ref[...], own_ref[rows:, :])
 
 
 def row_ids(rows, ids, far_ids, count):
@@ -128,35 +126,51 @@
     part_ref[...] = part_of(mine_refs, other_refs, mine_ids_ref, other_ids_ref[:, :width])
 
 
-def rest_kernel(blocks, mine_ids_ref, other_ids_ref, part_ref, *refs):
-    mine_refs, last_ref, (own_ref, *send_refs) = refs[:blocks], refs[blocks], refs[blocks + 1:]
+def rest_kernel(blocks, split, mine_ids_ref, other_ids_ref, part_ref, *refs):
+    mine_refs, last_ref = refs[:blocks], refs[blocks]
+    own_ref, same_ref, cross_ref, *send_refs = refs[blocks + 1:]
     height = own_ref.shape[0]
+    rows = height // 2
     start = (blocks - 1) * height
     part = part_ref[...] + part_of(
         mine_refs, [last_ref], mine_ids_ref, other_ids_ref[:, start:]
     )
     own_ref[...] = part[:height]
-    for k, ref in enumerate(send_refs):
-        ref[...] = part[(k + 1) * height:(k + 2) * height].astype(bf16)
-
-
-def grad_kernel(raw_ref, own_ref, *refs):
+    whole = [k for k in range(1, blocks) if k != split]
+    for k, ref in zip(whole, send_refs):
+        ref[...] = part[k * height:(k + 1) * height].astype(bf16)
+    block = part[split * height:(split + 1) * height].astype(bf16)
+    even = is_even()
+    same_ref[...] = jnp.where(even, block[:rows], block[rows:])
+    cross_ref[...] = jnp.where(even, block[rows:], block[:rows])
+
+
+def sum_kernel(own_ref, *refs):
     *got_refs, keep_ref, send_ref = refs
     rows = keep_ref.shape[0]
     total = own_ref[...]
     for ref in got_refs:
         total = total + ref[...].astype(f32)
-    grad = back_norm(*normalize(raw_ref[...]), total)
-    even = is_even()
-    keep_ref[...] = jnp.where(even, grad[:rows], grad[rows:])
-    send_ref[...] = jnp.where(even, grad[rows:], grad[:rows])
-
-
-def out_kernel(keep_ref, got_ref, img_ref, txt_ref):
-    even = is_even()
-    keep, got = keep_ref[...], got_ref[...]
+    even = is_even()
+    keep_ref[...] = jnp.where(even, total[:rows], total[rows:])
+    send_ref[...] = jnp.where(even, total[rows:], total[:rows])
+
+
+def keep_kernel(raw_ref, keep_ref, same_ref, cross_ref, grad_ref, rest_ref):
+    rows = keep_ref.shape[0]
+    raw = jnp.where(is_even(), raw_ref[:rows, :], raw_ref[rows:, :])
+    grad_ref[...] = back_norm(*normalize(raw), keep_ref[...] + same_ref[...].astype(f32))
+    rest_ref[...] = cross_ref[...].astype(f32)
+
+
+def out_kernel(raw_ref, grad_ref, rest_ref, got_ref, img_ref, txt_ref):
+    rows = grad_ref.shape[0]
+    even = is_even()
+    raw = jnp.where(even, raw_ref[rows:, :], raw_ref[:rows, :])
+    keep = grad_ref[...]
+    got = back_norm(*normalize(raw), got_ref[...] + rest_ref[...])
+    txt_ref[...] = jnp.where(even, keep, got)
     img_ref[...] = jnp.where(even, got, keep)
-    txt_ref[...] = jnp.where(even, keep, got)
 
 
 def local(image_embeds, text_embeds, pair_ids):
@@ -164,13 +178,14 @@
     blocks = max(lax.axis_size("img") // 2, lax.axis_size("txt"))
     pair = jax.ShapeDtypeStruct((2 * rows, width), bf16)
     total = jax.ShapeDtypeStruct((2 * rows, width), f32)
+    piece = jax.ShapeDtypeStruct((rows, width), bf16)
     single = jax.ShapeDtypeStruct((rows, width), f32)
     ids = pair_ids.reshape(1, -1)
     far_txt = core_swap(text_embeds)
     far_img = core_swap(image_embeds)
     far_ids = core_swap(ids)
     near = jnp.concatenate([text_embeds, image_embeds])
-    mine, other, raw = call(sides_kernel, [pair] * 3, [near, far_txt, far_img])
+    mine, other = call(sides_kernel, [pair] * 2, [near, far_txt, far_img])
     order = list(range(blocks - 1, 0, -1))
     mine = [mine] + [chip_swap(mine, k) for k in order]
     count = blocks * 2 * rows
@@ -191,14 +206,20 @@
         [mine_ids, other_ids, *mine, *other[:-1]],
         cost=LONG,
     )
-    own, *send = call(
-        functools.partial(rest_kernel, blocks),
-        [total] + [pair] * (blocks - 1),
+    split = min(2, blocks - 1)
+    own, same, cross, *send = call(
+        functools.partial(rest_kernel, blocks, split),
+        [total] + [piece] * 2 + [pair] * (blocks - 2),
         [mine_ids, other_ids, part, *mine, other[-1]],
     )
+    far = order.pop(split - 1)
     got = [chip_swap(block, k) for k, block in zip(order, send)]
-    keep, send = call(grad_kernel, [single] * 2, [raw, own, *got])
-    return tuple(call(out_kernel, [single] * 2, [keep, core_swap(send)]))
+    same = chip_swap(same, far)
+    cross = chip_swap(cross, far, cross=1)
+    keep, send = call(sum_kernel, [single] * 2, [own, *got])
+    got = core_swap(send)
+    grad, rest = call(keep_kernel, [single] * 2, [near, keep, same, cross], cost=LONG)
+    return tuple(call(out_kernel, [single] * 2, [near, grad, rest, got]))
 
 
 def solution(mesh):

time: 23.8 us -> 23.9 us (level)
  waiting for transfers between devices: 8.05 us -> 6.41 us
  starting transfers between devices: 11.7 us -> 13.3 us
  other arithmetic: 0.79 us -> 0 us
  local copies, waits for them, and re-layouts: 0.01 us -> 0.79 us
    ppermute x6 -> x7, starting transfers between devices: 9.22 us -> 10.8 us  [chip_swap(): return lax.ppermute(block, ('img', 'txt'), pairs)]
    ppermute x7, waiting for transfers between devices: 2.58 us -> 1.34 us  [core_swap(): return lax.ppermute(block, 'img', [(i, i ^ 1) for i in range(size)])]
    concatenate x1 -> x0, other arithmetic: 0.79 us -> none  [local(): near = jnp.concatenate([text_embeds, image_embeds])]
    unnamed x2 -> x5, local copies, waits for them, and re-layouts: 0.01 us -> 0.78 us
    ppermute x6 -> x7, waiting for transfers between devices: 5.47 us -> 5.07 us  [chip_swap(): return lax.ppermute(block, ('img', 'txt'), pairs)]
    pallas_call x6 -> x7, Pallas kernels: 2.34 us -> 2.55 us  [call(): pl.pallas_call(kernel, out_shape=outs, in_specs=[VMEM] * len(args), out_s...]
  transfers between devices with their start and end apart: 13 -> 14, of which waited for: 9 -> 8; matrix products, arithmetic and copies ran while one was open for 3% -> 3% of each run, Pallas kernels for 3% -> 4%
where the time goes in v7:
time: 23.9 us; the launch traced here: 23.7 us
  starting transfers between devices  13.3 us (56%)
  waiting for transfers between devices  6.41 us (27%)
  Pallas kernels  2.55 us (11%)
  local copies, waits for them, and re-layouts  0.79 us (3%)
  between operations  0.71 us (3%)
    ppermute x7, starting transfers between devices, chip_swap(): return lax.ppermute(block, ('img', 'txt'), pairs)  10.8 us
    ppermute x7, waiting for transfers between devices, chip_swap(): return lax.ppermute(block, ('img', 'txt'), pairs)  5.07 us
    pallas_call x7, Pallas kernels, call(): pl.pallas_call(kernel, out_shape=outs, in_specs=[VMEM] * len(args), out_s...  2.55 us
    ppermute x7, starting transfers between devices, core_swap(): return lax.ppermute(block, 'img', [(i, i ^ 1) for i in range(size)])  2.51 us
    ppermute x7, waiting for transfers between devices, core_swap(): return lax.ppermute(block, 'img', [(i, i ^ 1) for i in range(size)])  1.34 us
    unnamed x5, local copies, waits for them, and re-layouts  0.78 us
  transfers between devices with their start and end apart: 14, of which 8 were waited for; matrix products, arithmetic and copies ran while one was open for 3% of the time, Pallas kernels for 4%

profile of v7, /device:TPU:0, one launch (start us, length us, event | category | flops | bytes accessed | tf_op | source)
XLA Modules:
  0.0 23.7 jit_solution(15291850881419816992)
XLA Ops:
  0.6 0.5 %collective-permute-start.2 = (bf16[16,1152]{1,0:T(8,128)(2,1)}, bf16[16,1152]{1,0:T(8,128)(2,1)S(1)}, u32[]{:S(2)}, u32[]{:S(2)}) collective-permute-start(bf16[16,1152]{1,0:T(8,128)(2,1)} %param.3), channel_id=1, source_target_pairs={{0,4},{4,0},{8,12},{12,8},{16,20},{20,16},{24,28},{28,24},{1,5},{5... | collective-permute-start | bytes 110600 | tf_op jit(solution)/shard_map/ppermute | solution.py:37
  1.2 0.8 %constant_dynamic-update-slice_fusion.1 = bf16[32,1152]{1,0:T(8,128)(2,1)S(1)} fusion(bf16[16,1152]{1,0:T(8,128)(2,1)} %param.4), kind=kLoop, calls=%fused_computation.1 | loop fusion | bytes 73728
  2.0 0.2 collective-permute-done.2.img_ref
  2.2 0.3 %collective-permute-done.1.txt_ref = bf16[16,1152]{1,0:T(8,128)(2,1)S(1)} collective-permute-done((bf16[16,1152]{1,0:T(8,128)(2,1)}, bf16[16,1152]{1,0:T(8,128)(2,1)S(1)}, u32[]{:S(2)}, u32[]{:S(2)}) %collective-permute-start.1) | collective-permute-done | bytes 36896 | tf_op jit(solution)/shard_map/ppermute | solution.py:37
  2.7 2.7 %collective-permute-start.4 = (bf16[32,1152]{1,0:T(8,128)(2,1)S(1)}, bf16[32,1152]{1,0:T(8,128)(2,1)S(1)}, u32[]{:S(2)}, u32[]{:S(2)}) collective-permute-start(bf16[32,1152]{1,0:T(8,128)(2,1)S(1)} %get-tuple-element.16.refs_0_), channel_id=1, source_target_pairs={{0,16},{1,17},{2,18},{3,19},{4,6},{5,7},{6,4},{7,5},{8,24},{9,25},... | collective-permute-start | bytes 221192 | tf_op jit(solution)/shard_map/ppermute | solution.py:49
  5.5 1.4 %collective-permute-start.3 = (bf16[32,1152]{1,0:T(8,128)(2,1)S(1)}, bf16[32,1152]{1,0:T(8,128)(2,1)S(1)}, u32[]{:S(2)}, u32[]{:S(2)}) collective-permute-start(bf16[32,1152]{1,0:T(8,128)(2,1)S(1)} %get-tuple-element.16.refs_0_), channel_id=1, source_target_pairs={{0,24},{1,25},{2,26},{3,27},{4,7},{5,6},{6,5},{7,4},{8,16},{9,17},... | collective-permute-start | bytes 221192 | tf_op jit(solution)/shard_map/ppermute | solution.py:49
  6.9 0.8 %collective-permute-start = (s32[1,64]{1,0:T(1,128)S(1)}, s32[1,64]{1,0:T(1,128)S(1)}, u32[]{:S(2)}, u32[]{:S(2)}) collective-permute-start(s32[1,64]{1,0:T(1,128)S(1)} %bitcast.1), channel_id=1, source_target_pairs={{0,4},{4,0},{8,12},{12,8},{16,20},{20,16},{24,28},{28,24},{1,5},{5... | collective-permute-start | bytes 776 | tf_op jit(solution)/shard_map/ppermute | solution.py:37
  7.7 1.5 %collective-permute-start.5 = (bf16[32,1152]{1,0:T(8,128)(2,1)S(1)}, bf16[32,1152]{1,0:T(8,128)(2,1)S(1)}, u32[]{:S(2)}, u32[]{:S(2)}) collective-permute-start(bf16[32,1152]{1,0:T(8,128)(2,1)S(1)} %get-tuple-element.16.refs_0_), channel_id=1, source_target_pairs={{0,8},{1,9},{2,10},{3,11},{4,5},{5,4},{6,7},{7,6},{8,0},{9,1},{10,... | collective-permute-start | bytes 221192 | tf_op jit(solution)/shard_map/ppermute | solution.py:49
  9.2 1.5 %collective-permute-done.3.piece_ref.refs_1_ = bf16[32,1152]{1,0:T(8,128)(2,1)S(1)} collective-permute-done((bf16[32,1152]{1,0:T(8,128)(2,1)S(1)}, bf16[32,1152]{1,0:T(8,128)(2,1)S(1)}, u32[]{:S(2)}, u32[]{:S(2)}) %collective-permute-start.3) | collective-permute-done | bytes 73760 | tf_op jit(solution)/shard_map/ppermute | solution.py:49
  10.7 0.1 shard_map.51
  10.9 1.0 %collective-permute-start.6 = (bf16[32,1152]{1,0:T(8,128)(2,1)S(1)}, bf16[32,1152]{1,0:T(8,128)(2,1)S(1)}, u32[]{:S(2)}, u32[]{:S(2)}) collective-permute-start(bf16[32,1152]{1,0:T(8,128)(2,1)S(1)} %get-tuple-element.20), channel_id=1, source_target_pairs={{0,4},{4,0},{8,12},{12,8},{16,20},{20,16},{24,28},{28,24},{1,5},{5... | collective-permute-start | bytes 221192 | tf_op jit(solution)/shard_map/ppermute | solution.py:37
  11.9 0.1 collective-permute-done.5.refs_3_
  12.1 0.8 %collective-permute-done.6.refs_5_ = bf16[32,1152]{1,0:T(8,128)(2,1)S(1)} collective-permute-done((bf16[32,1152]{1,0:T(8,128)(2,1)S(1)}, bf16[32,1152]{1,0:T(8,128)(2,1)S(1)}, u32[]{:S(2)}, u32[]{:S(2)}) %collective-permute-start.6) | collective-permute-done | bytes 73760 | tf_op jit(solution)/shard_map/ppermute | solution.py:37
  12.8 0.5 %shard_map.52.part_ref = f32[128,1152]{1,0:T(8,128)S(1)} custom-call(s32[128,1]{1,0:T(8,128)S(1)} %get-tuple-element.17.mine_ids_ref, s32[1,128]{1,0:T(1,128)S(1)} %get-tuple-element.18.other_ids_ref, bf16[32,1152]{1,0:T(8,128)(2,1)S(1)} %get-tuple-element.16.refs_0_, bf16[32,1152]{1,0:T(8,128)(2,1)S(1)} %collective-permute-done.3.piece_ref.refs_1_, ...), custom_call_target="tpu_custom_call" | custom-call | flops 10000000000 | bytes 10000000 | tf_op jit(solution)/shard_map/pallas_call | solution.py:58
  13.4 0.7 %shard_map.53 = (f32[32,1152]{1,0:T(8,128)S(1)}, bf16[16,1152]{1,0:T(8,128)(2,1)S(1)}, bf16[16,1152]{1,0:T(8,128)(2,1)S(1)}, bf16[32,1152]{1,0:T(8,128)(2,1)S(1)}, bf16[32,1152]{1,0:T(8,128)(2,1)S(1)}) custom-call(s32[128,1]{1,0:T(8,128)S(1)} %get-tuple-element.17.mine_ids_ref, s32[1,128]{1,0:T(1,128)S(1)} %get-tuple-element.18.other_ids_ref, ...), custom_call_target="tpu_custom_call" | custom-call | tf_op jit(solution)/shard_map/pallas_call | solution.py:58
  14.0 2.5 %collective-permute-start.9 = (bf16[32,1152]{1,0:T(8,128)(2,1)S(1)}, bf16[32,1152]{1,0:T(8,128)(2,1)S(1)}, u32[]{:S(2)}, u32[]{:S(2)}) collective-permute-start(bf16[32,1152]{1,0:T(8,128)(2,1)S(1)} %get-tuple-element.22), channel_id=1, source_target_pairs={{0,24},{1,25},{2,26},{3,27},{4,7},{5,6},{6,5},{7,4},{8,16},{9,17},... | collective-permute-start | bytes 221192 | tf_op jit(solution)/shard_map/ppermute | solution.py:49
  16.5 0.5 %collective-permute-start.10 = (bf16[32,1152]{1,0:T(8,128)(2,1)S(1)}, bf16[32,1152]{1,0:T(8,128)(2,1)S(1)}, u32[]{:S(2)}, u32[]{:S(2)}) collective-permute-start(bf16[32,1152]{1,0:T(8,128)(2,1)S(1)} %get-tuple-element.23), channel_id=1, source_target_pairs={{0,8},{1,9},{2,10},{3,11},{4,5},{5,4},{6,7},{7,6},{8,0},{9,1},{10,... | collective-permute-start | bytes 221192 | tf_op jit(solution)/shard_map/ppermute | solution.py:49
  17.1 0.5 %collective-permute-start.11 = (bf16[16,1152]{1,0:T(8,128)(2,1)S(1)}, bf16[16,1152]{1,0:T(8,128)(2,1)S(1)}, u32[]{:S(2)}, u32[]{:S(2)}) collective-permute-start(bf16[16,1152]{1,0:T(8,128)(2,1)S(1)} %get-tuple-element.25), channel_id=1, source_target_pairs={{0,16},{1,17},{2,18},{3,19},{4,6},{5,7},{6,4},{7,5},{8,24},{9,25},... | collective-permute-start | bytes 110600 | tf_op jit(solution)/shard_map/ppermute | solution.py:49
  17.6 1.5 %collective-permute-start.12 = (bf16[16,1152]{1,0:T(8,128)(2,1)S(1)}, bf16[16,1152]{1,0:T(8,128)(2,1)S(1)}, u32[]{:S(2)}, u32[]{:S(2)}) collective-permute-start(bf16[16,1152]{1,0:T(8,128)(2,1)S(1)} %get-tuple-element.26), channel_id=1, source_target_pairs={{0,20},{1,21},{2,22},{3,23},{4,2},{5,3},{6,0},{7,1},{8,28},{9,29},... | collective-permute-start | bytes 110600 | tf_op jit(solution)/shard_map/ppermute | solution.py:49
  19.1 0.2 collective-permute-done.9.refs_0_
  19.3 1.5 %collective-permute-done.10.refs_1_ = bf16[32,1152]{1,0:T(8,128)(2,1)S(1)} collective-permute-done((bf16[32,1152]{1,0:T(8,128)(2,1)S(1)}, bf16[32,1152]{1,0:T(8,128)(2,1)S(1)}, u32[]{:S(2)}, u32[]{:S(2)}) %collective-permute-start.10) | collective-permute-done | bytes 73760 | tf_op jit(solution)/shard_map/ppermute | solution.py:49
  21.0 1.6 %collective-permute-done.12.cross_ref = bf16[16,1152]{1,0:T(8,128)(2,1)S(1)} collective-permute-done((bf16[16,1152]{1,0:T(8,128)(2,1)S(1)}, bf16[16,1152]{1,0:T(8,128)(2,1)S(1)}, u32[]{:S(2)}, u32[]{:S(2)}) %collective-permute-start.12) | collective-permute-done | bytes 36896 | tf_op jit(solution)/shard_map/ppermute | solution.py:49
  22.7 0.2 shard_map.55
  22.9 0.9 %shard_map.56 = (f32[16,1152]{1,0:T(8,128)}, f32[16,1152]{1,0:T(8,128)}) custom-call(bf16[32,1152]{1,0:T(8,128)(2,1)S(1)} %constant_dynamic-update-slice_fusion.own_ref.raw_ref, f32[16,1152]{1,0:T(8,128)S(1)} %get-tuple-element.27.grad_ref, f32[16,1152]{1,0:T(8,128)S(1)} %get-tuple-element.28.rest_ref, f32[16,1152]{1,0:T(8,128)S(1)} %collective-permute-done.13.got_ref), custom_call_target="tpu_custom_call" | custom-call | tf_op jit(solution)/shard_map/pallas_call | solution.py:58
  (17 shorter events, 0.4 us)
Async XLA Ops:
  0.6 1.4 %copy-start.1 = (bf16[16,1152]{1,0:T(8,128)(2,1)S(1)}, bf16[16,1152]{1,0:T(8,128)(2,1)}, u32[]{:S(2)}) copy-start(bf16[16,1152]{1,0:T(8,128)(2,1)} %param.3) | copy-start | bytes 110596
  0.6 1.6 %collective-permute-start.2 = (bf16[16,1152]{1,0:T(8,128)(2,1)}, bf16[16,1152]{1,0:T(8,128)(2,1)S(1)}, u32[]{:S(2)}, u32[]{:S(2)}) collective-permute-start(bf16[16,1152]{1,0:T(8,128)(2,1)} %param.3), channel_id=1, source_target_pairs={{0,4},{4,0},{8,12},{12,8},{16,20},{20,16},{24,28},{28,24},{1,5},{5... | collective-permute-start | bytes 110600 | tf_op jit(solution)/shard_map/ppermute | solution.py:37
  1.2 1.4 %collective-permute-start.1 = (bf16[16,1152]{1,0:T(8,128)(2,1)}, bf16[16,1152]{1,0:T(8,128)(2,1)S(1)}, u32[]{:S(2)}, u32[]{:S(2)}) collective-permute-start(bf16[16,1152]{1,0:T(8,128)(2,1)} %param.4), channel_id=1, source_target_pairs={{0,4},{4,0},{8,12},{12,8},{16,20},{20,16},{24,28},{28,24},{1,5},{5... | collective-permute-start | bytes 110600 | tf_op jit(solution)/shard_map/ppermute | solution.py:37
  2.7 4.2 %copy-start = (s32[64]{0:T(128)S(1)}, s32[64]{0:T(128)}, u32[]{:S(2)}) copy-start(s32[64]{0:T(128)} %param.5) | copy-start | bytes 772
  2.7 6.5 %collective-permute-start.4 = (bf16[32,1152]{1,0:T(8,128)(2,1)S(1)}, bf16[32,1152]{1,0:T(8,128)(2,1)S(1)}, u32[]{:S(2)}, u32[]{:S(2)}) collective-permute-start(bf16[32,1152]{1,0:T(8,128)(2,1)S(1)} %get-tuple-element.16.refs_0_), channel_id=1, source_target_pairs={{0,16},{1,17},{2,18},{3,19},{4,6},{5,7},{6,4},{7,5},{8,24},{9,25},... | collective-permute-start | bytes 221192 | tf_op jit(solution)/shard_map/ppermute | solution.py:49
  5.5 5.3 %collective-permute-start.3 = (bf16[32,1152]{1,0:T(8,128)(2,1)S(1)}, bf16[32,1152]{1,0:T(8,128)(2,1)S(1)}, u32[]{:S(2)}, u32[]{:S(2)}) collective-permute-start(bf16[32,1152]{1,0:T(8,128)(2,1)S(1)} %get-tuple-element.16.refs_0_), channel_id=1, source_target_pairs={{0,24},{1,25},{2,26},{3,27},{4,7},{5,6},{6,5},{7,4},{8,16},{9,17},... | collective-permute-start | bytes 221192 | tf_op jit(solution)/shard_map/ppermute | solution.py:49
  6.9 2.3 %collective-permute-start = (s32[1,64]{1,0:T(1,128)S(1)}, s32[1,64]{1,0:T(1,128)S(1)}, u32[]{:S(2)}, u32[]{:S(2)}) collective-permute-start(s32[1,64]{1,0:T(1,128)S(1)} %bitcast.1), channel_id=1, source_target_pairs={{0,4},{4,0},{8,12},{12,8},{16,20},{20,16},{24,28},{28,24},{1,5},{5... | collective-permute-start | bytes 776 | tf_op jit(solution)/shard_map/ppermute | solution.py:37
  7.7 4.4 %collective-permute-start.5 = (bf16[32,1152]{1,0:T(8,128)(2,1)S(1)}, bf16[32,1152]{1,0:T(8,128)(2,1)S(1)}, u32[]{:S(2)}, u32[]{:S(2)}) collective-permute-start(bf16[32,1152]{1,0:T(8,128)(2,1)S(1)} %get-tuple-element.16.refs_0_), channel_id=1, source_target_pairs={{0,8},{1,9},{2,10},{3,11},{4,5},{5,4},{6,7},{7,6},{8,0},{9,1},{10,... | collective-permute-start | bytes 221192 | tf_op jit(solution)/shard_map/ppermute | solution.py:49
  9.2 2.9 %collective-permute-start.7 = (bf16[32,1152]{1,0:T(8,128)(2,1)S(1)}, bf16[32,1152]{1,0:T(8,128)(2,1)S(1)}, u32[]{:S(2)}, u32[]{:S(2)}) collective-permute-start(bf16[32,1152]{1,0:T(8,128)(2,1)S(1)} %collective-permute-done.4.refs_2_), channel_id=1, source_target_pairs={{0,4},{4,0},{8,12},{12,8},{16,20},{20,16},{24,28},{28,24},{1,5},{5... | collective-permute-start | bytes 221192 | tf_op jit(solution)/shard_map/ppermute | solution.py:37
  10.9 2.0 %collective-permute-start.6 = (bf16[32,1152]{1,0:T(8,128)(2,1)S(1)}, bf16[32,1152]{1,0:T(8,128)(2,1)S(1)}, u32[]{:S(2)}, u32[]{:S(2)}) collective-permute-start(bf16[32,1152]{1,0:T(8,128)(2,1)S(1)} %get-tuple-element.20), channel_id=1, source_target_pairs={{0,4},{4,0},{8,12},{12,8},{16,20},{20,16},{24,28},{28,24},{1,5},{5... | collective-permute-start | bytes 221192 | tf_op jit(solution)/shard_map/ppermute | solution.py:37
  12.1 1.3 %collective-permute-start.8 = (bf16[32,1152]{1,0:T(8,128)(2,1)S(1)}, bf16[32,1152]{1,0:T(8,128)(2,1)S(1)}, u32[]{:S(2)}, u32[]{:S(2)}) collective-permute-start(bf16[32,1152]{1,0:T(8,128)(2,1)S(1)} %collective-permute-done.5.refs_3_), channel_id=1, source_target_pairs={{0,4},{4,0},{8,12},{12,8},{16,20},{20,16},{24,28},{28,24},{1,5},{5... | collective-permute-start | bytes 221192 | tf_op jit(solution)/shard_map/ppermute | solution.py:37
  14.0 5.3 %collective-permute-start.9 = (bf16[32,1152]{1,0:T(8,128)(2,1)S(1)}, bf16[32,1152]{1,0:T(8,128)(2,1)S(1)}, u32[]{:S(2)}, u32[]{:S(2)}) collective-permute-start(bf16[32,1152]{1,0:T(8,128)(2,1)S(1)} %get-tuple-element.22), channel_id=1, source_target_pairs={{0,24},{1,25},{2,26},{3,27},{4,7},{5,6},{6,5},{7,4},{8,16},{9,17},... | collective-permute-start | bytes 221192 | tf_op jit(solution)/shard_map/ppermute | solution.py:49
  16.5 4.4 %collective-permute-start.10 = (bf16[32,1152]{1,0:T(8,128)(2,1)S(1)}, bf16[32,1152]{1,0:T(8,128)(2,1)S(1)}, u32[]{:S(2)}, u32[]{:S(2)}) collective-permute-start(bf16[32,1152]{1,0:T(8,128)(2,1)S(1)} %get-tuple-element.23), channel_id=1, source_target_pairs={{0,8},{1,9},{2,10},{3,11},{4,5},{5,4},{6,7},{7,6},{8,0},{9,1},{10,... | collective-permute-start | bytes 221192 | tf_op jit(solution)/shard_map/ppermute | solution.py:49
  17.1 4.0 %collective-permute-start.11 = (bf16[16,1152]{1,0:T(8,128)(2,1)S(1)}, bf16[16,1152]{1,0:T(8,128)(2,1)S(1)}, u32[]{:S(2)}, u32[]{:S(2)}) collective-permute-start(bf16[16,1152]{1,0:T(8,128)(2,1)S(1)} %get-tuple-element.25), channel_id=1, source_target_pairs={{0,16},{1,17},{2,18},{3,19},{4,6},{5,7},{6,4},{7,5},{8,24},{9,25},... | collective-permute-start | bytes 110600 | tf_op jit(solution)/shard_map/ppermute | solution.py:49
  17.6 5.1 %collective-permute-start.12 = (bf16[16,1152]{1,0:T(8,128)(2,1)S(1)}, bf16[16,1152]{1,0:T(8,128)(2,1)S(1)}, u32[]{:S(2)}, u32[]{:S(2)}) collective-permute-start(bf16[16,1152]{1,0:T(8,128)(2,1)S(1)} %get-tuple-element.26), channel_id=1, source_target_pairs={{0,20},{1,21},{2,22},{3,23},{4,2},{5,3},{6,0},{7,1},{8,28},{9,29},... | collective-permute-start | bytes 110600 | tf_op jit(solution)/shard_map/ppermute | solution.py:49
  20.9 1.9 %collective-permute-start.13 = (f32[16,1152]{1,0:T(8,128)S(1)}, f32[16,1152]{1,0:T(8,128)S(1)}, u32[]{:S(2)}, u32[]{:S(2)}) collective-permute-start(f32[16,1152]{1,0:T(8,128)S(1)} %get-tuple-element.29), channel_id=1, source_target_pairs={{0,4},{4,0},{8,12},{12,8},{16,20},{20,16},{24,28},{28,24},{1,5},{5... | collective-permute-start | bytes 221192 | tf_op jit(solution)/shard_map/ppermute | solution.py:37

commit v8 on v7

--- a/solution.py
+++ b/solution.py
@@ -95,35 +95,39 @@
     return txt_ids, img_ids
 
 
-def ids_kernel(ids_ref, far_ids_ref, piece_ref, mine_ids_ref, other_ids_ref, out_ref):
-    height = piece_ref.shape[0]
-    count = mine_ids_ref.shape[0]
-    even = is_even()
-    txt_ids, img_ids = row_ids(height // 2, ids_ref[...], far_ids_ref[...], count)
-    mine_ids_ref[...] = jnp.where(even, txt_ids, img_ids)
+def side_ids(rows, ids, far_ids, count):
+    even = is_even()
+    txt_ids, img_ids = row_ids(rows, ids, far_ids, count)
     other_ids = jnp.where(even, img_ids, txt_ids)
     diagonal = lax.broadcasted_iota(jnp.int32, (count, count), 0) == lax.broadcasted_iota(
         jnp.int32, (count, count), 1
     )
-    other_ids_ref[...] = jnp.sum(jnp.where(diagonal, other_ids, 0), axis=0, keepdims=True)
-    out_ref[...] = piece_ref[...]
-
-
-def part_of(mine_refs, other_refs, mine_ids_ref, other_ids):
+    other_ids = jnp.sum(jnp.where(diagonal, other_ids, 0), axis=0, keepdims=True)
+    return jnp.where(even, txt_ids, img_ids), other_ids
+
+
+def part_of(mine_refs, other_refs, mine_ids, other_ids):
     mine = jnp.concatenate([ref[...] for ref in mine_refs], axis=0)
     other = jnp.concatenate([ref[...] for ref in other_refs], axis=0)
     scores = lax.dot_general(
         mine, other, (((1,), (1,)), ((), ())), preferred_element_type=f32
     )
-    same = mine_ids_ref[...] == other_ids
+    same = mine_ids == other_ids
     coeff = pair_coeff(scale_logit * scores + shift_logit, same)
     return jnp.dot(coeff, other, preferred_element_type=f32)
 
 
-def most_kernel(blocks, mine_ids_ref, other_ids_ref, *refs):
-    mine_refs, other_refs, part_ref = refs[:blocks], refs[blocks:-1], refs[-1]
-    width = (blocks - 1) * mine_refs[0].shape[0]
-    part_ref[...] = part_of(mine_refs, other_refs, mine_ids_ref, other_ids_ref[:, :width])
+def most_kernel(blocks, ids_ref, far_ids_ref, *refs):
+    mine_refs, other_refs = refs[:blocks], refs[blocks:-3]
+    part_ref, mine_ids_ref, other_ids_ref = refs[-3:]
+    height = mine_refs[0].shape[0]
+    mine_ids, other_ids = side_ids(
+        height // 2, ids_ref[...], far_ids_ref[...], blocks * height
+    )
+    mine_ids_ref[...] = mine_ids
+    other_ids_ref[...] = other_ids
+    width = (blocks - 1) * height
+    part_ref[...] = part_of(mine_refs, other_refs, mine_ids, other_ids[:, :width])
 
 
 def rest_kernel(blocks, split, mine_ids_ref, other_ids_ref, part_ref, *refs):
@@ -133,7 +137,7 @@
     rows = height // 2
     start = (blocks - 1) * height
     part = part_ref[...] + part_of(
-        mine_refs, [last_ref], mine_ids_ref, other_ids_ref[:, start:]
+        mine_refs, [last_ref], mine_ids_ref[...], other_ids_ref[:, start:]
     )
     own_ref[...] = part[:height]
     whole = [k for k in range(1, blocks) if k != split]
@@ -158,7 +162,7 @@
 
 def keep_kernel(raw_ref, keep_ref, same_ref, cross_ref, grad_ref, rest_ref):
     rows = keep_ref.shape[0]
-    raw = jnp.where(is_even(), raw_ref[:rows, :], raw_ref[rows:, :])
+    raw = jnp.where(is_even(), raw_ref[:rows, :], raw_ref[rows:2 * rows, :])
     grad_ref[...] = back_norm(*normalize(raw), keep_ref[...] + same_ref[...].astype(f32))
     rest_ref[...] = cross_ref[...].astype(f32)
 
@@ -166,7 +170,7 @@
 def out_kernel(raw_ref, grad_ref, rest_ref, got_ref, img_ref, txt_ref):
     rows = grad_ref.shape[0]
     even = is_even()
-    raw = jnp.where(even, raw_ref[rows:, :], raw_ref[:rows, :])
+    raw = jnp.where(even, raw_ref[rows:2 * rows, :], raw_ref[:rows, :])
     keep = grad_ref[...]
     got = back_norm(*normalize(raw), got_ref[...] + rest_ref[...])
     txt_ref[...] = jnp.where(even, keep, got)
@@ -188,22 +192,16 @@
     mine, other = call(sides_kernel, [pair] * 2, [near, far_txt, far_img])
     order = list(range(blocks - 1, 0, -1))
     mine = [mine] + [chip_swap(mine, k) for k in order]
+    other = [other] + [core_swap(block) for block in mine[1:]]
     count = blocks * 2 * rows
-    mine_ids, other_ids, first = call(
-        ids_kernel,
+    part, mine_ids, other_ids = call(
+        functools.partial(most_kernel, blocks),
         [
+            jax.ShapeDtypeStruct((count, width), f32),
             jax.ShapeDtypeStruct((count, 1), jnp.int32),
             jax.ShapeDtypeStruct((1, count), jnp.int32),
-            pair,
         ],
-        [ids, far_ids, mine[1]],
-    )
-    other = [other] + [core_swap(block) for block in [first] + mine[2:]]
-    part = jax.ShapeDtypeStruct((count, width), f32)
-    (part,) = call(
-        functools.partial(most_kernel, blocks),
-        [part],
-        [mine_ids, other_ids, *mine, *other[:-1]],
+        [ids, far_ids, *mine, *other[:-1]],
         cost=LONG,
     )
     split = min(2, blocks - 1)

time: 23.9 us -> 23.9 us (level)
  waiting for transfers between devices: 6.41 us -> 7.9 us
  starting transfers between devices: 13.3 us -> 11.9 us
    ppermute x7, waiting for transfers between devices: 5.07 us -> 6.72 us  [chip_swap(): return lax.ppermute(block, ('img', 'txt'), pairs)]
    ppermute x7, starting transfers between devices: 10.8 us -> 9.23 us  [chip_swap(): return lax.ppermute(block, ('img', 'txt'), pairs)]
    pallas_call x7 -> x6, Pallas kernels: 2.55 us -> 2.41 us  [call(): pl.pallas_call(kernel, out_shape=outs, in_specs=[VMEM] * len(args), out_s...]
  transfers between devices with their start and end apart: 14 -> 14, of which waited for: 8 -> 8; matrix products, arithmetic and copies ran while one was open for 3% -> 3% of each run, Pallas kernels for 4% -> 3%
where the time goes in v8:
time: 23.9 us; the launch traced here: 23.7 us
  starting transfers between devices  11.9 us (50%)
  waiting for transfers between devices  7.9 us (33%)
  Pallas kernels  2.41 us (10%)
  local copies, waits for them, and re-layouts  0.79 us (3%)
  between operations  0.71 us (3%)
    ppermute x7, starting transfers between devices, chip_swap(): return lax.ppermute(block, ('img', 'txt'), pairs)  9.23 us
    ppermute x7, waiting for transfers between devices, chip_swap(): return lax.ppermute(block, ('img', 'txt'), pairs)  6.72 us
    ppermute x7, starting transfers between devices, core_swap(): return lax.ppermute(block, 'img', [(i, i ^ 1) for i in range(size)])  2.7 us
    pallas_call x6, Pallas kernels, call(): pl.pallas_call(kernel, out_shape=outs, in_specs=[VMEM] * len(args), out_s...  2.41 us
    ppermute x7, waiting for transfers between devices, core_swap(): return lax.ppermute(block, 'img', [(i, i ^ 1) for i in range(size)])  1.18 us
    unnamed x5, local copies, waits for them, and re-layouts  0.78 us
  transfers between devices with their start and end apart: 14, of which 8 were waited for; matrix products, arithmetic and copies ran while one was open for 3% of the time, Pallas kernels for 3%

profile of v8, /device:TPU:0, one launch (start us, length us, event | category | flops | bytes accessed | tf_op | source)
XLA Modules:
  0.0 23.7 jit_solution(10192692222164163406)
XLA Ops:
  0.6 0.5 %collective-permute-start.2 = (bf16[16,1152]{1,0:T(8,128)(2,1)}, bf16[16,1152]{1,0:T(8,128)(2,1)S(1)}, u32[]{:S(2)}, u32[]{:S(2)}) collective-permute-start(bf16[16,1152]{1,0:T(8,128)(2,1)} %param.3), channel_id=1, source_target_pairs={{0,4},{4,0},{8,12},{12,8},{16,20},{20,16},{24,28},{28,24},{1,5},{5... | collective-permute-start | bytes 110600 | tf_op jit(solution)/shard_map/ppermute | solution.py:37
  1.2 0.8 %constant_dynamic-update-slice_fusion.1 = bf16[32,1152]{1,0:T(8,128)(2,1)S(1)} fusion(bf16[16,1152]{1,0:T(8,128)(2,1)} %param.4), kind=kLoop, calls=%fused_computation.1 | loop fusion | bytes 73728
  2.0 0.2 collective-permute-done.2.img_ref
  2.2 0.3 %collective-permute-done.1.txt_ref = bf16[16,1152]{1,0:T(8,128)(2,1)S(1)} collective-permute-done((bf16[16,1152]{1,0:T(8,128)(2,1)}, bf16[16,1152]{1,0:T(8,128)(2,1)S(1)}, u32[]{:S(2)}, u32[]{:S(2)}) %collective-permute-start.1) | collective-permute-done | bytes 36896 | tf_op jit(solution)/shard_map/ppermute | solution.py:37
  2.6 0.1 shard_map.50
  2.7 2.7 %collective-permute-start.4 = (bf16[32,1152]{1,0:T(8,128)(2,1)S(1)}, bf16[32,1152]{1,0:T(8,128)(2,1)S(1)}, u32[]{:S(2)}, u32[]{:S(2)}) collective-permute-start(bf16[32,1152]{1,0:T(8,128)(2,1)S(1)} %get-tuple-element.16.refs_0_), channel_id=1, source_target_pairs={{0,16},{1,17},{2,18},{3,19},{4,6},{5,7},{6,4},{7,5},{8,24},{9,25},... | collective-permute-start | bytes 221192 | tf_op jit(solution)/shard_map/ppermute | solution.py:49
  5.5 1.4 %collective-permute-start.3 = (bf16[32,1152]{1,0:T(8,128)(2,1)S(1)}, bf16[32,1152]{1,0:T(8,128)(2,1)S(1)}, u32[]{:S(2)}, u32[]{:S(2)}) collective-permute-start(bf16[32,1152]{1,0:T(8,128)(2,1)S(1)} %get-tuple-element.16.refs_0_), channel_id=1, source_target_pairs={{0,24},{1,25},{2,26},{3,27},{4,7},{5,6},{6,5},{7,4},{8,16},{9,17},... | collective-permute-start | bytes 221192 | tf_op jit(solution)/shard_map/ppermute | solution.py:49
  7.0 0.8 %collective-permute-done.4.refs_2_ = bf16[32,1152]{1,0:T(8,128)(2,1)S(1)} collective-permute-done((bf16[32,1152]{1,0:T(8,128)(2,1)S(1)}, bf16[32,1152]{1,0:T(8,128)(2,1)S(1)}, u32[]{:S(2)}, u32[]{:S(2)}) %collective-permute-start.4) | collective-permute-done | bytes 73760 | tf_op jit(solution)/shard_map/ppermute | solution.py:49
  7.8 0.5 %collective-permute-start.7 = (bf16[32,1152]{1,0:T(8,128)(2,1)S(1)}, bf16[32,1152]{1,0:T(8,128)(2,1)S(1)}, u32[]{:S(2)}, u32[]{:S(2)}) collective-permute-start(bf16[32,1152]{1,0:T(8,128)(2,1)S(1)} %collective-permute-done.4.refs_2_), channel_id=1, source_target_pairs={{0,4},{4,0},{8,12},{12,8},{16,20},{20,16},{24,28},{28,24},{1,5},{5... | collective-permute-start | bytes 221192 | tf_op jit(solution)/shard_map/ppermute | solution.py:37
  8.4 2.4 %collective-permute-done.3.refs_1_ = bf16[32,1152]{1,0:T(8,128)(2,1)S(1)} collective-permute-done((bf16[32,1152]{1,0:T(8,128)(2,1)S(1)}, bf16[32,1152]{1,0:T(8,128)(2,1)S(1)}, u32[]{:S(2)}, u32[]{:S(2)}) %collective-permute-start.3) | collective-permute-done | bytes 73760 | tf_op jit(solution)/shard_map/ppermute | solution.py:49
  10.7 1.0 %collective-permute-start.6 = (bf16[32,1152]{1,0:T(8,128)(2,1)S(1)}, bf16[32,1152]{1,0:T(8,128)(2,1)S(1)}, u32[]{:S(2)}, u32[]{:S(2)}) collective-permute-start(bf16[32,1152]{1,0:T(8,128)(2,1)S(1)} %collective-permute-done.3.refs_1_), channel_id=1, source_target_pairs={{0,4},{4,0},{8,12},{12,8},{16,20},{20,16},{24,28},{28,24},{1,5},{5... | collective-permute-start | bytes 221192 | tf_op jit(solution)/shard_map/ppermute | solution.py:37
  11.7 0.5 %collective-permute-start.8 = (bf16[32,1152]{1,0:T(8,128)(2,1)S(1)}, bf16[32,1152]{1,0:T(8,128)(2,1)S(1)}, u32[]{:S(2)}, u32[]{:S(2)}) collective-permute-start(bf16[32,1152]{1,0:T(8,128)(2,1)S(1)} %collective-permute-done.5.refs_3_), channel_id=1, source_target_pairs={{0,4},{4,0},{8,12},{12,8},{16,20},{20,16},{24,28},{28,24},{1,5},{5... | collective-permute-start | bytes 221192 | tf_op jit(solution)/shard_map/ppermute | solution.py:37
  12.2 0.6 %collective-permute-done.far_ids_ref = s32[1,64]{1,0:T(1,128)S(1)} collective-permute-done((s32[1,64]{1,0:T(1,128)S(1)}, s32[1,64]{1,0:T(1,128)S(1)}, u32[]{:S(2)}, u32[]{:S(2)}) %collective-permute-start) | collective-permute-done | bytes 288 | tf_op jit(solution)/shard_map/ppermute | solution.py:37
  12.8 0.5 %shard_map.51 = (f32[128,1152]{1,0:T(8,128)S(1)}, s32[128,1]{1,0:T(8,128)S(1)}, s32[1,128]{1,0:T(1,128)S(1)}) custom-call(s32[1,64]{1,0:T(1,128)S(1)} %bitcast.2, s32[1,64]{1,0:T(1,128)S(1)} %collective-permute-done.far_ids_ref, bf16[32,1152]{1,0:T(8,128)(2,1)S(1)} %get-tuple-element.16.refs_0_, bf16[32,1152]{1,0:T(8,128)(2,1)S(1)} %collective-permute-done.3.refs_1_, ...), custom_call_target="tpu_custom_call" | custom-call | flops 10000000000 | bytes 10000000 | tf_op jit(solution)/shard_map/pallas_call | solution.py:58
  13.4 0.7 %shard_map.52 = (f32[32,1152]{1,0:T(8,128)S(1)}, bf16[16,1152]{1,0:T(8,128)(2,1)S(1)}, bf16[16,1152]{1,0:T(8,128)(2,1)S(1)}, bf16[32,1152]{1,0:T(8,128)(2,1)S(1)}, bf16[32,1152]{1,0:T(8,128)(2,1)S(1)}) custom-call(s32[128,1]{1,0:T(8,128)S(1)} %get-tuple-element.18.mine_ids_ref, s32[1,128]{1,0:T(1,128)S(1)} %get-tuple-element.19.other_ids_ref, ...), custom_call_target="tpu_custom_call" | custom-call | tf_op jit(solution)/shard_map/pallas_call | solution.py:58
  14.0 2.5 %collective-permute-start.9 = (bf16[32,1152]{1,0:T(8,128)(2,1)S(1)}, bf16[32,1152]{1,0:T(8,128)(2,1)S(1)}, u32[]{:S(2)}, u32[]{:S(2)}) collective-permute-start(bf16[32,1152]{1,0:T(8,128)(2,1)S(1)} %get-tuple-element.22), channel_id=1, source_target_pairs={{0,24},{1,25},{2,26},{3,27},{4,7},{5,6},{6,5},{7,4},{8,16},{9,17},... | collective-permute-start | bytes 221192 | tf_op jit(solution)/shard_map/ppermute | solution.py:49
  16.5 0.5 %collective-permute-start.10 = (bf16[32,1152]{1,0:T(8,128)(2,1)S(1)}, bf16[32,1152]{1,0:T(8,128)(2,1)S(1)}, u32[]{:S(2)}, u32[]{:S(2)}) collective-permute-start(bf16[32,1152]{1,0:T(8,128)(2,1)S(1)} %get-tuple-element.23), channel_id=1, source_target_pairs={{0,8},{1,9},{2,10},{3,11},{4,5},{5,4},{6,7},{7,6},{8,0},{9,1},{10,... | collective-permute-start | bytes 221192 | tf_op jit(solution)/shard_map/ppermute | solution.py:49
  17.1 0.5 %collective-permute-start.11 = (bf16[16,1152]{1,0:T(8,128)(2,1)S(1)}, bf16[16,1152]{1,0:T(8,128)(2,1)S(1)}, u32[]{:S(2)}, u32[]{:S(2)}) collective-permute-start(bf16[16,1152]{1,0:T(8,128)(2,1)S(1)} %get-tuple-element.25), channel_id=1, source_target_pairs={{0,16},{1,17},{2,18},{3,19},{4,6},{5,7},{6,4},{7,5},{8,24},{9,25},... | collective-permute-start | bytes 110600 | tf_op jit(solution)/shard_map/ppermute | solution.py:49
  17.6 1.4 %collective-permute-start.12 = (bf16[16,1152]{1,0:T(8,128)(2,1)S(1)}, bf16[16,1152]{1,0:T(8,128)(2,1)S(1)}, u32[]{:S(2)}, u32[]{:S(2)}) collective-permute-start(bf16[16,1152]{1,0:T(8,128)(2,1)S(1)} %get-tuple-element.26), channel_id=1, source_target_pairs={{0,20},{1,21},{2,22},{3,23},{4,2},{5,3},{6,0},{7,1},{8,28},{9,29},... | collective-permute-start | bytes 110600 | tf_op jit(solution)/shard_map/ppermute | solution.py:49
  19.0 0.4 %collective-permute-done.9.refs_0_ = bf16[32,1152]{1,0:T(8,128)(2,1)S(1)} collective-permute-done((bf16[32,1152]{1,0:T(8,128)(2,1)S(1)}, bf16[32,1152]{1,0:T(8,128)(2,1)S(1)}, u32[]{:S(2)}, u32[]{:S(2)}) %collective-permute-start.9) | collective-permute-done | bytes 73760 | tf_op jit(solution)/shard_map/ppermute | solution.py:49
  19.3 1.5 %collective-permute-done.10.refs_1_ = bf16[32,1152]{1,0:T(8,128)(2,1)S(1)} collective-permute-done((bf16[32,1152]{1,0:T(8,128)(2,1)S(1)}, bf16[32,1152]{1,0:T(8,128)(2,1)S(1)}, u32[]{:S(2)}, u32[]{:S(2)}) %collective-permute-start.10) | collective-permute-done | bytes 73760 | tf_op jit(solution)/shard_map/ppermute | solution.py:49
  21.0 1.6 %collective-permute-done.12.cross_ref = bf16[16,1152]{1,0:T(8,128)(2,1)S(1)} collective-permute-done((bf16[16,1152]{1,0:T(8,128)(2,1)S(1)}, bf16[16,1152]{1,0:T(8,128)(2,1)S(1)}, u32[]{:S(2)}, u32[]{:S(2)}) %collective-permute-start.12) | collective-permute-done | bytes 36896 | tf_op jit(solution)/shard_map/ppermute | solution.py:49
  22.7 0.2 shard_map.54
  22.9 0.9 %shard_map.55 = (f32[16,1152]{1,0:T(8,128)}, f32[16,1152]{1,0:T(8,128)}) custom-call(bf16[32,1152]{1,0:T(8,128)(2,1)S(1)} %constant_dynamic-update-slice_fusion.own_ref.raw_ref, f32[16,1152]{1,0:T(8,128)S(1)} %get-tuple-element.27.grad_ref, f32[16,1152]{1,0:T(8,128)S(1)} %get-tuple-element.28.rest_ref, f32[16,1152]{1,0:T(8,128)S(1)} %collective-permute-done.13.got_ref), custom_call_target="tpu_custom_call" | custom-call | tf_op jit(solution)/shard_map/pallas_call | solution.py:58
  (16 shorter events, 0.4 us)
Async XLA Ops:
  0.6 1.4 %copy-start.1 = (bf16[16,1152]{1,0:T(8,128)(2,1)S(1)}, bf16[16,1152]{1,0:T(8,128)(2,1)}, u32[]{:S(2)}) copy-start(bf16[16,1152]{1,0:T(8,128)(2,1)} %param.3) | copy-start | bytes 110596
  0.6 1.6 %collective-permute-start.2 = (bf16[16,1152]{1,0:T(8,128)(2,1)}, bf16[16,1152]{1,0:T(8,128)(2,1)S(1)}, u32[]{:S(2)}, u32[]{:S(2)}) collective-permute-start(bf16[16,1152]{1,0:T(8,128)(2,1)} %param.3), channel_id=1, source_target_pairs={{0,4},{4,0},{8,12},{12,8},{16,20},{20,16},{24,28},{28,24},{1,5},{5... | collective-permute-start | bytes 110600 | tf_op jit(solution)/shard_map/ppermute | solution.py:37
  1.2 1.4 %collective-permute-start.1 = (bf16[16,1152]{1,0:T(8,128)(2,1)}, bf16[16,1152]{1,0:T(8,128)(2,1)S(1)}, u32[]{:S(2)}, u32[]{:S(2)}) collective-permute-start(bf16[16,1152]{1,0:T(8,128)(2,1)} %param.4), channel_id=1, source_target_pairs={{0,4},{4,0},{8,12},{12,8},{16,20},{20,16},{24,28},{28,24},{1,5},{5... | collective-permute-start | bytes 110600 | tf_op jit(solution)/shard_map/ppermute | solution.py:37
  2.7 9.0 %copy-start = (s32[64]{0:T(128)S(1)}, s32[64]{0:T(128)}, u32[]{:S(2)}) copy-start(s32[64]{0:T(128)} %param.5) | copy-start | bytes 772
  2.7 5.1 %collective-permute-start.4 = (bf16[32,1152]{1,0:T(8,128)(2,1)S(1)}, bf16[32,1152]{1,0:T(8,128)(2,1)S(1)}, u32[]{:S(2)}, u32[]{:S(2)}) collective-permute-start(bf16[32,1152]{1,0:T(8,128)(2,1)S(1)} %get-tuple-element.16.refs_0_), channel_id=1, source_target_pairs={{0,16},{1,17},{2,18},{3,19},{4,6},{5,7},{6,4},{7,5},{8,24},{9,25},... | collective-permute-start | bytes 221192 | tf_op jit(solution)/shard_map/ppermute | solution.py:49
  5.5 5.3 %collective-permute-start.3 = (bf16[32,1152]{1,0:T(8,128)(2,1)S(1)}, bf16[32,1152]{1,0:T(8,128)(2,1)S(1)}, u32[]{:S(2)}, u32[]{:S(2)}) collective-permute-start(bf16[32,1152]{1,0:T(8,128)(2,1)S(1)} %get-tuple-element.16.refs_0_), channel_id=1, source_target_pairs={{0,24},{1,25},{2,26},{3,27},{4,7},{5,6},{6,5},{7,4},{8,16},{9,17},... | collective-permute-start | bytes 221192 | tf_op jit(solution)/shard_map/ppermute | solution.py:49
  6.9 4.8 %collective-permute-start.5 = (bf16[32,1152]{1,0:T(8,128)(2,1)S(1)}, bf16[32,1152]{1,0:T(8,128)(2,1)S(1)}, u32[]{:S(2)}, u32[]{:S(2)}) collective-permute-start(bf16[32,1152]{1,0:T(8,128)(2,1)S(1)} %get-tuple-element.16.refs_0_), channel_id=1, source_target_pairs={{0,8},{1,9},{2,10},{3,11},{4,5},{5,4},{6,7},{7,6},{8,0},{9,1},{10,... | collective-permute-start | bytes 221192 | tf_op jit(solution)/shard_map/ppermute | solution.py:49
  7.8 5.0 %collective-permute-start.7 = (bf16[32,1152]{1,0:T(8,128)(2,1)S(1)}, bf16[32,1152]{1,0:T(8,128)(2,1)S(1)}, u32[]{:S(2)}, u32[]{:S(2)}) collective-permute-start(bf16[32,1152]{1,0:T(8,128)(2,1)S(1)} %collective-permute-done.4.refs_2_), channel_id=1, source_target_pairs={{0,4},{4,0},{8,12},{12,8},{16,20},{20,16},{24,28},{28,24},{1,5},{5... | collective-permute-start | bytes 221192 | tf_op jit(solution)/shard_map/ppermute | solution.py:37
  10.7 2.1 %collective-permute-start.6 = (bf16[32,1152]{1,0:T(8,128)(2,1)S(1)}, bf16[32,1152]{1,0:T(8,128)(2,1)S(1)}, u32[]{:S(2)}, u32[]{:S(2)}) collective-permute-start(bf16[32,1152]{1,0:T(8,128)(2,1)S(1)} %collective-permute-done.3.refs_1_), channel_id=1, source_target_pairs={{0,4},{4,0},{8,12},{12,8},{16,20},{20,16},{24,28},{28,24},{1,5},{5... | collective-permute-start | bytes 221192 | tf_op jit(solution)/shard_map/ppermute | solution.py:37
  11.7 1.1 %collective-permute-start = (s32[1,64]{1,0:T(1,128)S(1)}, s32[1,64]{1,0:T(1,128)S(1)}, u32[]{:S(2)}, u32[]{:S(2)}) collective-permute-start(s32[1,64]{1,0:T(1,128)S(1)} %bitcast.1), channel_id=1, source_target_pairs={{0,4},{4,0},{8,12},{12,8},{16,20},{20,16},{24,28},{28,24},{1,5},{5... | collective-permute-start | bytes 776 | tf_op jit(solution)/shard_map/ppermute | solution.py:37
  11.7 1.7 %collective-permute-start.8 = (bf16[32,1152]{1,0:T(8,128)(2,1)S(1)}, bf16[32,1152]{1,0:T(8,128)(2,1)S(1)}, u32[]{:S(2)}, u32[]{:S(2)}) collective-permute-start(bf16[32,1152]{1,0:T(8,128)(2,1)S(1)} %collective-permute-done.5.refs_3_), channel_id=1, source_target_pairs={{0,4},{4,0},{8,12},{12,8},{16,20},{20,16},{24,28},{28,24},{1,5},{5... | collective-permute-start | bytes 221192 | tf_op jit(solution)/shard_map/ppermute | solution.py:37
  14.0 5.3 %collective-permute-start.9 = (bf16[32,1152]{1,0:T(8,128)(2,1)S(1)}, bf16[32,1152]{1,0:T(8,128)(2,1)S(1)}, u32[]{:S(2)}, u32[]{:S(2)}) collective-permute-start(bf16[32,1152]{1,0:T(8,128)(2,1)S(1)} %get-tuple-element.22), channel_id=1, source_target_pairs={{0,24},{1,25},{2,26},{3,27},{4,7},{5,6},{6,5},{7,4},{8,16},{9,17},... | collective-permute-start | bytes 221192 | tf_op jit(solution)/shard_map/ppermute | solution.py:49
  16.5 4.4 %collective-permute-start.10 = (bf16[32,1152]{1,0:T(8,128)(2,1)S(1)}, bf16[32,1152]{1,0:T(8,128)(2,1)S(1)}, u32[]{:S(2)}, u32[]{:S(2)}) collective-permute-start(bf16[32,1152]{1,0:T(8,128)(2,1)S(1)} %get-tuple-element.23), channel_id=1, source_target_pairs={{0,8},{1,9},{2,10},{3,11},{4,5},{5,4},{6,7},{7,6},{8,0},{9,1},{10,... | collective-permute-start | bytes 221192 | tf_op jit(solution)/shard_map/ppermute | solution.py:49
  17.1 4.0 %collective-permute-start.11 = (bf16[16,1152]{1,0:T(8,128)(2,1)S(1)}, bf16[16,1152]{1,0:T(8,128)(2,1)S(1)}, u32[]{:S(2)}, u32[]{:S(2)}) collective-permute-start(bf16[16,1152]{1,0:T(8,128)(2,1)S(1)} %get-tuple-element.25), channel_id=1, source_target_pairs={{0,16},{1,17},{2,18},{3,19},{4,6},{5,7},{6,4},{7,5},{8,24},{9,25},... | collective-permute-start | bytes 110600 | tf_op jit(solution)/shard_map/ppermute | solution.py:49
  17.6 5.1 %collective-permute-start.12 = (bf16[16,1152]{1,0:T(8,128)(2,1)S(1)}, bf16[16,1152]{1,0:T(8,128)(2,1)S(1)}, u32[]{:S(2)}, u32[]{:S(2)}) collective-permute-start(bf16[16,1152]{1,0:T(8,128)(2,1)S(1)} %get-tuple-element.26), channel_id=1, source_target_pairs={{0,20},{1,21},{2,22},{3,23},{4,2},{5,3},{6,0},{7,1},{8,28},{9,29},... | collective-permute-start | bytes 110600 | tf_op jit(solution)/shard_map/ppermute | solution.py:49
  20.9 1.9 %collective-permute-start.13 = (f32[16,1152]{1,0:T(8,128)S(1)}, f32[16,1152]{1,0:T(8,128)S(1)}, u32[]{:S(2)}, u32[]{:S(2)}) collective-permute-start(f32[16,1152]{1,0:T(8,128)S(1)} %get-tuple-element.29), channel_id=1, source_target_pairs={{0,4},{4,0},{8,12},{12,8},{16,20},{20,16},{24,28},{28,24},{1,5},{5... | collective-permute-start | bytes 221192 | tf_op jit(solution)/shard_map/ppermute | solution.py:37

commit v9 on v8

--- a/solution.py
+++ b/solution.py
@@ -14,6 +14,7 @@
 bf16 = jnp.bfloat16
 VMEM = pl.BlockSpec(memory_space=pltpu.VMEM)
 LONG = pl.CostEstimate(flops=10**10, bytes_accessed=10**7, transcendentals=0)
+SHORT = pl.CostEstimate(flops=2 * 10**8, bytes_accessed=10**5, transcendentals=0)
 
 
 def normalize(raw):
@@ -106,39 +107,26 @@
     return jnp.where(even, txt_ids, img_ids), other_ids
 
 
-def part_of(mine_refs, other_refs, mine_ids, other_ids):
+def scores_of(mine_refs, other_refs):
     mine = jnp.concatenate([ref[...] for ref in mine_refs], axis=0)
     other = jnp.concatenate([ref[...] for ref in other_refs], axis=0)
-    scores = lax.dot_general(
-        mine, other, (((1,), (1,)), ((), ())), preferred_element_type=f32
-    )
-    same = mine_ids == other_ids
-    coeff = pair_coeff(scale_logit * scores + shift_logit, same)
-    return jnp.dot(coeff, other, preferred_element_type=f32)
-
-
-def most_kernel(blocks, ids_ref, far_ids_ref, *refs):
-    mine_refs, other_refs = refs[:blocks], refs[blocks:-3]
-    part_ref, mine_ids_ref, other_ids_ref = refs[-3:]
-    height = mine_refs[0].shape[0]
-    mine_ids, other_ids = side_ids(
-        height // 2, ids_ref[...], far_ids_ref[...], blocks * height
-    )
-    mine_ids_ref[...] = mine_ids
-    other_ids_ref[...] = other_ids
-    width = (blocks - 1) * height
-    part_ref[...] = part_of(mine_refs, other_refs, mine_ids, other_ids[:, :width])
-
-
-def rest_kernel(blocks, split, mine_ids_ref, other_ids_ref, part_ref, *refs):
-    mine_refs, last_ref = refs[:blocks], refs[blocks]
-    own_ref, same_ref, cross_ref, *send_refs = refs[blocks + 1:]
+    return lax.dot_general(mine, other, (((1,), (1,)), ((), ())), preferred_element_type=f32)
+
+
+def most_kernel(blocks, *refs):
+    refs[-1][...] = scores_of(refs[:blocks], refs[blocks:-1])
+
+
+def rest_kernel(blocks, split, ids_ref, far_ids_ref, most_ref, *refs):
+    mine_refs, other_refs = refs[:blocks], refs[blocks:2 * blocks]
+    own_ref, same_ref, cross_ref, *send_refs = refs[2 * blocks:]
     height = own_ref.shape[0]
     rows = height // 2
-    start = (blocks - 1) * height
-    part = part_ref[...] + part_of(
-        mine_refs, [last_ref], mine_ids_ref[...], other_ids_ref[:, start:]
-    )
+    mine_ids, other_ids = side_ids(rows, ids_ref[...], far_ids_ref[...], blocks * height)
+    scores = jnp.concatenate([most_ref[...], scores_of(mine_refs, other_refs[-1:])], axis=1)
+    coeff = pair_coeff(scale_logit * scores + shift_logit, mine_ids == other_ids)
+    other = jnp.concatenate([ref[...] for ref in other_refs], axis=0)
+    part = jnp.dot(coeff, other, preferred_element_type=f32)
     own_ref[...] = part[:height]
     whole = [k for k in range(1, blocks) if k != split]
     for k, ref in zip(whole, send_refs):
@@ -160,19 +148,24 @@
     send_ref[...] = jnp.where(even, total[rows:], total[:rows])
 
 
-def keep_kernel(raw_ref, keep_ref, same_ref, cross_ref, grad_ref, rest_ref):
+def keep_kernel(raw_ref, keep_ref, same_ref, grad_ref, unit_ref, inverse_ref):
     rows = keep_ref.shape[0]
-    raw = jnp.where(is_even(), raw_ref[:rows, :], raw_ref[rows:2 * rows, :])
-    grad_ref[...] = back_norm(*normalize(raw), keep_ref[...] + same_ref[...].astype(f32))
-    rest_ref[...] = cross_ref[...].astype(f32)
-
-
-def out_kernel(raw_ref, grad_ref, rest_ref, got_ref, img_ref, txt_ref):
-    rows = grad_ref.shape[0]
-    even = is_even()
-    raw = jnp.where(even, raw_ref[rows:2 * rows, :], raw_ref[:rows, :])
+    even = is_even()
+    unit, inverse = normalize(raw_ref[...])
+    grad_ref[...] = back_norm(
+        jnp.where(even, unit[:rows], unit[rows:]),
+        jnp.where(even, inverse[:rows], inverse[rows:]),
+        keep_ref[...] + same_ref[...].astype(f32),
+    )
+    unit_ref[...] = jnp.where(even, unit[rows:], unit[:rows])
+    inverse_ref[...] = jnp.where(even, inverse[rows:], inverse[:rows])
+
+
+def out_kernel(grad_ref, unit_ref, inverse_ref, cross_ref, got_ref, img_ref, txt_ref):
+    even = is_even()
+    total = got_ref[...] + cross_ref[...].astype(f32)
     keep = grad_ref[...]
-    got = back_norm(*normalize(raw), got_ref[...] + rest_ref[...])
+    got = back_norm(unit_ref[...], inverse_ref[...], total)
     txt_ref[...] = jnp.where(even, keep, got)
     img_ref[...] = jnp.where(even, got, keep)
 
@@ -187,28 +180,23 @@
     ids = pair_ids.reshape(1, -1)
     far_txt = core_swap(text_embeds)
     far_img = core_swap(image_embeds)
-    far_ids = core_swap(ids)
     near = jnp.concatenate([text_embeds, image_embeds])
     mine, other = call(sides_kernel, [pair] * 2, [near, far_txt, far_img])
     order = list(range(blocks - 1, 0, -1))
     mine = [mine] + [chip_swap(mine, k) for k in order]
     other = [other] + [core_swap(block) for block in mine[1:]]
     count = blocks * 2 * rows
-    part, mine_ids, other_ids = call(
+    (most,) = call(
         functools.partial(most_kernel, blocks),
-        [
-            jax.ShapeDtypeStruct((count, width), f32),
-            jax.ShapeDtypeStruct((count, 1), jnp.int32),
-            jax.ShapeDtypeStruct((1, count), jnp.int32),
-        ],
-        [ids, far_ids, *mine, *other[:-1]],
-        cost=LONG,
+        [jax.ShapeDtypeStruct((count, count - 2 * rows), f32)],
+        [*mine, *other[:-1]],
+        cost=SHORT,
     )
     split = min(2, blocks - 1)
     own, same, cross, *send = call(
         functools.partial(rest_kernel, blocks, split),
         [total] + [piece] * 2 + [pair] * (blocks - 2),
-        [mine_ids, other_ids, part, *mine, other[-1]],
+        [ids, core_swap(ids), most, *mine, *other],
     )
     far = order.pop(split - 1)
     got = [chip_swap(block, k) for k, block in zip(order, send)]
@@ -216,8 +204,9 @@
     cross = chip_swap(cross, far, cross=1)
     keep, send = call(sum_kernel, [single] * 2, [own, *got])
     got = core_swap(send)
-    grad, rest = call(keep_kernel, [single] * 2, [near, keep, same, cross], cost=LONG)
-    return tuple(call(out_kernel, [single] * 2, [near, grad, rest, got]))
+    column = jax.ShapeDtypeStruct((rows, 1), f32)
+    kept = call(keep_kernel, [single, single, column], [near, keep, same], cost=LONG)
+    return tuple(call(out_kernel, [single] * 2, [*kept, cross, got]))
 
 
 def solution(mesh):

time: 23.9 us -> 22.8 us (0.954)
  waiting for transfers between devices: 7.9 us -> 7.19 us
  Pallas kernels: 2.41 us -> 1.92 us
    ppermute x7, waiting for transfers between devices: 6.72 us -> 5.64 us  [chip_swap(): return lax.ppermute(block, ('img', 'txt'), pairs)]
    pallas_call x6, Pallas kernels: 2.41 us -> 1.92 us  [call(): pl.pallas_call(kernel, out_shape=outs, in_specs=[VMEM] * len(args), out_s...]
    ppermute x7, waiting for transfers between devices: 1.18 us -> 1.54 us  [core_swap(): return lax.ppermute(block, 'img', [(i, i ^ 1) for i in range(size)])]
  transfers between devices with their start and end apart: 14 -> 14, of which waited for: 8 -> 10; matrix products, arithmetic and copies ran while one was open for 3% -> 3% of each run, Pallas kernels for 3% -> 2%
where the time goes in v9:
time: 22.8 us; the launch traced here: 22.6 us
  starting transfers between devices  12 us (53%)
  waiting for transfers between devices  7.19 us (32%)
  Pallas kernels  1.92 us (8%)
  local copies, waits for them, and re-layouts  0.79 us (3%)
  between operations  0.7 us (3%)
    ppermute x7, starting transfers between devices, chip_swap(): return lax.ppermute(block, ('img', 'txt'), pairs)  9.32 us
    ppermute x7, waiting for transfers between devices, chip_swap(): return lax.ppermute(block, ('img', 'txt'), pairs)  5.64 us
    ppermute x7, starting transfers between devices, core_swap(): return lax.ppermute(block, 'img', [(i, i ^ 1) for i in range(size)])  2.7 us
    pallas_call x6, Pallas kernels, call(): pl.pallas_call(kernel, out_shape=outs, in_specs=[VMEM] * len(args), out_s...  1.92 us
    ppermute x7, waiting for transfers between devices, core_swap(): return lax.ppermute(block, 'img', [(i, i ^ 1) for i in range(size)])  1.54 us
    unnamed x5, local copies, waits for them, and re-layouts  0.78 us
  transfers between devices with their start and end apart: 14, of which 10 were waited for; matrix products, arithmetic and copies ran while one was open for 3% of the time, Pallas kernels for 2%

profile of v9, /device:TPU:0, one launch (start us, length us, event | category | flops | bytes accessed | tf_op | source)
XLA Modules:
  0.0 22.6 jit_solution(5608850939494892772)
XLA Ops:
  0.6 0.5 %collective-permute-start.2 = (bf16[16,1152]{1,0:T(8,128)(2,1)}, bf16[16,1152]{1,0:T(8,128)(2,1)S(1)}, u32[]{:S(2)}, u32[]{:S(2)}) collective-permute-start(bf16[16,1152]{1,0:T(8,128)(2,1)} %param.3), channel_id=1, source_target_pairs={{0,4},{4,0},{8,12},{12,8},{16,20},{20,16},{24,28},{28,24},{1,5},{5... | collective-permute-start | bytes 110600 | tf_op jit(solution)/shard_map/ppermute | solution.py:38
  1.2 0.8 %constant_dynamic-update-slice_fusion.1 = bf16[32,1152]{1,0:T(8,128)(2,1)S(1)} fusion(bf16[16,1152]{1,0:T(8,128)(2,1)} %param.4), kind=kLoop, calls=%fused_computation.1 | loop fusion | bytes 73728
  2.0 0.2 collective-permute-done.2.img_ref
  2.2 0.3 %collective-permute-done.1.txt_ref = bf16[16,1152]{1,0:T(8,128)(2,1)S(1)} collective-permute-done((bf16[16,1152]{1,0:T(8,128)(2,1)}, bf16[16,1152]{1,0:T(8,128)(2,1)S(1)}, u32[]{:S(2)}, u32[]{:S(2)}) %collective-permute-start.1) | collective-permute-done | bytes 36896 | tf_op jit(solution)/shard_map/ppermute | solution.py:38
  2.7 2.7 %collective-permute-start.4 = (bf16[32,1152]{1,0:T(8,128)(2,1)S(1)}, bf16[32,1152]{1,0:T(8,128)(2,1)S(1)}, u32[]{:S(2)}, u32[]{:S(2)}) collective-permute-start(bf16[32,1152]{1,0:T(8,128)(2,1)S(1)} %get-tuple-element.14.refs_0_), channel_id=1, source_target_pairs={{0,16},{1,17},{2,18},{3,19},{4,6},{5,7},{6,4},{7,5},{8,24},{9,25},... | collective-permute-start | bytes 221192 | tf_op jit(solution)/shard_map/ppermute | solution.py:50
  5.5 1.4 %collective-permute-start.3 = (bf16[32,1152]{1,0:T(8,128)(2,1)S(1)}, bf16[32,1152]{1,0:T(8,128)(2,1)S(1)}, u32[]{:S(2)}, u32[]{:S(2)}) collective-permute-start(bf16[32,1152]{1,0:T(8,128)(2,1)S(1)} %get-tuple-element.14.refs_0_), channel_id=1, source_target_pairs={{0,24},{1,25},{2,26},{3,27},{4,7},{5,6},{6,5},{7,4},{8,16},{9,17},... | collective-permute-start | bytes 221192 | tf_op jit(solution)/shard_map/ppermute | solution.py:50
  7.0 0.8 %collective-permute-done.4.refs_2_ = bf16[32,1152]{1,0:T(8,128)(2,1)S(1)} collective-permute-done((bf16[32,1152]{1,0:T(8,128)(2,1)S(1)}, bf16[32,1152]{1,0:T(8,128)(2,1)S(1)}, u32[]{:S(2)}, u32[]{:S(2)}) %collective-permute-start.4) | collective-permute-done | bytes 73760 | tf_op jit(solution)/shard_map/ppermute | solution.py:50
  7.8 0.5 %collective-permute-start.7 = (bf16[32,1152]{1,0:T(8,128)(2,1)S(1)}, bf16[32,1152]{1,0:T(8,128)(2,1)S(1)}, u32[]{:S(2)}, u32[]{:S(2)}) collective-permute-start(bf16[32,1152]{1,0:T(8,128)(2,1)S(1)} %collective-permute-done.4.refs_2_), channel_id=1, source_target_pairs={{0,4},{4,0},{8,12},{12,8},{16,20},{20,16},{24,28},{28,24},{1,5},{5... | collective-permute-start | bytes 221192 | tf_op jit(solution)/shard_map/ppermute | solution.py:38
  8.4 2.4 %collective-permute-done.3.refs_1_ = bf16[32,1152]{1,0:T(8,128)(2,1)S(1)} collective-permute-done((bf16[32,1152]{1,0:T(8,128)(2,1)S(1)}, bf16[32,1152]{1,0:T(8,128)(2,1)S(1)}, u32[]{:S(2)}, u32[]{:S(2)}) %collective-permute-start.3) | collective-permute-done | bytes 73760 | tf_op jit(solution)/shard_map/ppermute | solution.py:50
  10.7 1.0 %collective-permute-start.6 = (bf16[32,1152]{1,0:T(8,128)(2,1)S(1)}, bf16[32,1152]{1,0:T(8,128)(2,1)S(1)}, u32[]{:S(2)}, u32[]{:S(2)}) collective-permute-start(bf16[32,1152]{1,0:T(8,128)(2,1)S(1)} %collective-permute-done.3.refs_1_), channel_id=1, source_target_pairs={{0,4},{4,0},{8,12},{12,8},{16,20},{20,16},{24,28},{28,24},{1,5},{5... | collective-permute-start | bytes 221192 | tf_op jit(solution)/shard_map/ppermute | solution.py:38
  11.7 0.5 %collective-permute-start = (s32[1,64]{1,0:T(1,128)S(1)}, s32[1,64]{1,0:T(1,128)S(1)}, u32[]{:S(2)}, u32[]{:S(2)}) collective-permute-start(s32[1,64]{1,0:T(1,128)S(1)} %bitcast.1), channel_id=1, source_target_pairs={{0,4},{4,0},{8,12},{12,8},{16,20},{20,16},{24,28},{28,24},{1,5},{5... | collective-permute-start | bytes 776 | tf_op jit(solution)/shard_map/ppermute | solution.py:38
  12.2 0.4 %collective-permute-done.6.refs_5_ = bf16[32,1152]{1,0:T(8,128)(2,1)S(1)} collective-permute-done((bf16[32,1152]{1,0:T(8,128)(2,1)S(1)}, bf16[32,1152]{1,0:T(8,128)(2,1)S(1)}, u32[]{:S(2)}, u32[]{:S(2)}) %collective-permute-start.6) | collective-permute-done | bytes 73760 | tf_op jit(solution)/shard_map/ppermute | solution.py:38
  12.6 0.2 %shard_map.51.most_ref = f32[128,96]{1,0:T(8,128)S(1)} custom-call(bf16[32,1152]{1,0:T(8,128)(2,1)S(1)} %get-tuple-element.14.refs_0_, bf16[32,1152]{1,0:T(8,128)(2,1)S(1)} %collective-permute-done.3.refs_1_, bf16[32,1152]{1,0:T(8,128)(2,1)S(1)} %collective-permute-done.4.refs_2_, bf16[32,1152]{1,0:T(8,128)(2,1)S(1)} %collective-permute-done.5.refs_3_, ...), custom_call_target="tpu_custom_call" | custom-call | flops 200000000 | bytes 100000 | tf_op jit(solution)/shard_map/pallas_call | solution.py:59
  13.0 0.6 %shard_map.52 = (f32[32,1152]{1,0:T(8,128)S(1)}, bf16[16,1152]{1,0:T(8,128)(2,1)S(1)}, bf16[16,1152]{1,0:T(8,128)(2,1)S(1)}, bf16[32,1152]{1,0:T(8,128)(2,1)S(1)}, bf16[32,1152]{1,0:T(8,128)(2,1)S(1)}) custom-call(s32[1,64]{1,0:T(1,128)S(1)} %bitcast.2, s32[1,64]{1,0:T(1,128)S(1)} %collective-permute-done.far_ids_ref, f32[128,96]{1,0:T(8,128)S(1)} %shard_map.51.most_ref, ...), custom_call_target="tpu_custom_call" | custom-call | tf_op jit(solution)/shard_map/pallas_call | solution.py:59
  13.6 2.5 %collective-permute-start.9 = (bf16[32,1152]{1,0:T(8,128)(2,1)S(1)}, bf16[32,1152]{1,0:T(8,128)(2,1)S(1)}, u32[]{:S(2)}, u32[]{:S(2)}) collective-permute-start(bf16[32,1152]{1,0:T(8,128)(2,1)S(1)} %get-tuple-element.17), channel_id=1, source_target_pairs={{0,24},{1,25},{2,26},{3,27},{4,7},{5,6},{6,5},{7,4},{8,16},{9,17},... | collective-permute-start | bytes 221192 | tf_op jit(solution)/shard_map/ppermute | solution.py:50
  16.1 0.5 %collective-permute-start.10 = (bf16[32,1152]{1,0:T(8,128)(2,1)S(1)}, bf16[32,1152]{1,0:T(8,128)(2,1)S(1)}, u32[]{:S(2)}, u32[]{:S(2)}) collective-permute-start(bf16[32,1152]{1,0:T(8,128)(2,1)S(1)} %get-tuple-element.18), channel_id=1, source_target_pairs={{0,8},{1,9},{2,10},{3,11},{4,5},{5,4},{6,7},{7,6},{8,0},{9,1},{10,... | collective-permute-start | bytes 221192 | tf_op jit(solution)/shard_map/ppermute | solution.py:50
  16.7 0.5 %collective-permute-start.11 = (bf16[16,1152]{1,0:T(8,128)(2,1)S(1)}, bf16[16,1152]{1,0:T(8,128)(2,1)S(1)}, u32[]{:S(2)}, u32[]{:S(2)}) collective-permute-start(bf16[16,1152]{1,0:T(8,128)(2,1)S(1)} %get-tuple-element.20), channel_id=1, source_target_pairs={{0,16},{1,17},{2,18},{3,19},{4,6},{5,7},{6,4},{7,5},{8,24},{9,25},... | collective-permute-start | bytes 110600 | tf_op jit(solution)/shard_map/ppermute | solution.py:50
  17.2 1.5 %collective-permute-start.12 = (bf16[16,1152]{1,0:T(8,128)(2,1)S(1)}, bf16[16,1152]{1,0:T(8,128)(2,1)S(1)}, u32[]{:S(2)}, u32[]{:S(2)}) collective-permute-start(bf16[16,1152]{1,0:T(8,128)(2,1)S(1)} %get-tuple-element.24), channel_id=1, source_target_pairs={{0,20},{1,21},{2,22},{3,23},{4,2},{5,3},{6,0},{7,1},{8,28},{9,29},... | collective-permute-start | bytes 110600 | tf_op jit(solution)/shard_map/ppermute | solution.py:50
  18.7 0.3 %collective-permute-done.9.refs_0_ = bf16[32,1152]{1,0:T(8,128)(2,1)S(1)} collective-permute-done((bf16[32,1152]{1,0:T(8,128)(2,1)S(1)}, bf16[32,1152]{1,0:T(8,128)(2,1)S(1)}, u32[]{:S(2)}, u32[]{:S(2)}) %collective-permute-start.9) | collective-permute-done | bytes 73760 | tf_op jit(solution)/shard_map/ppermute | solution.py:50
  18.9 1.5 %collective-permute-done.10.refs_1_ = bf16[32,1152]{1,0:T(8,128)(2,1)S(1)} collective-permute-done((bf16[32,1152]{1,0:T(8,128)(2,1)S(1)}, bf16[32,1152]{1,0:T(8,128)(2,1)S(1)}, u32[]{:S(2)}, u32[]{:S(2)}) %collective-permute-start.10) | collective-permute-done | bytes 73760 | tf_op jit(solution)/shard_map/ppermute | solution.py:50
  20.6 0.2 shard_map.54
  20.8 0.6 %collective-permute-done.12.cross_ref = bf16[16,1152]{1,0:T(8,128)(2,1)S(1)} collective-permute-done((bf16[16,1152]{1,0:T(8,128)(2,1)S(1)}, bf16[16,1152]{1,0:T(8,128)(2,1)S(1)}, u32[]{:S(2)}, u32[]{:S(2)}) %collective-permute-start.12) | collective-permute-done | bytes 36896 | tf_op jit(solution)/shard_map/ppermute | solution.py:50
  21.5 0.4 %collective-permute-done.13.got_ref = f32[16,1152]{1,0:T(8,128)S(1)} collective-permute-done((f32[16,1152]{1,0:T(8,128)S(1)}, f32[16,1152]{1,0:T(8,128)S(1)}, u32[]{:S(2)}, u32[]{:S(2)}) %collective-permute-start.13) | collective-permute-done | bytes 73760 | tf_op jit(solution)/shard_map/ppermute | solution.py:38
  21.9 0.8 %shard_map.55 = (f32[16,1152]{1,0:T(8,128)}, f32[16,1152]{1,0:T(8,128)}) custom-call(f32[16,1152]{1,0:T(8,128)S(1)} %get-tuple-element.21.grad_ref, f32[16,1152]{1,0:T(8,128)S(1)} %get-tuple-element.22.unit_ref, f32[16,1]{1,0:T(8,128)S(1)} %get-tuple-element.23.inverse_ref, bf16[16,1152]{1,0:T(8,128)(2,1)S(1)} %collective-permute-done.12.cross_ref, ...), custom_call_target="tpu_custom_call" | custom-call | tf_op jit(solution)/shard_map/pallas_call | solution.py:59
  (16 shorter events, 0.7 us)
Async XLA Ops:
  0.6 1.4 %copy-start.1 = (bf16[16,1152]{1,0:T(8,128)(2,1)S(1)}, bf16[16,1152]{1,0:T(8,128)(2,1)}, u32[]{:S(2)}) copy-start(bf16[16,1152]{1,0:T(8,128)(2,1)} %param.3) | copy-start | bytes 110596
  0.6 1.6 %collective-permute-start.2 = (bf16[16,1152]{1,0:T(8,128)(2,1)}, bf16[16,1152]{1,0:T(8,128)(2,1)S(1)}, u32[]{:S(2)}, u32[]{:S(2)}) collective-permute-start(bf16[16,1152]{1,0:T(8,128)(2,1)} %param.3), channel_id=1, source_target_pairs={{0,4},{4,0},{8,12},{12,8},{16,20},{20,16},{24,28},{28,24},{1,5},{5... | collective-permute-start | bytes 110600 | tf_op jit(solution)/shard_map/ppermute | solution.py:38
  1.2 1.4 %collective-permute-start.1 = (bf16[16,1152]{1,0:T(8,128)(2,1)}, bf16[16,1152]{1,0:T(8,128)(2,1)S(1)}, u32[]{:S(2)}, u32[]{:S(2)}) collective-permute-start(bf16[16,1152]{1,0:T(8,128)(2,1)} %param.4), channel_id=1, source_target_pairs={{0,4},{4,0},{8,12},{12,8},{16,20},{20,16},{24,28},{28,24},{1,5},{5... | collective-permute-start | bytes 110600 | tf_op jit(solution)/shard_map/ppermute | solution.py:38
  2.7 9.0 %copy-start = (s32[64]{0:T(128)S(1)}, s32[64]{0:T(128)}, u32[]{:S(2)}) copy-start(s32[64]{0:T(128)} %param.5) | copy-start | bytes 772
  2.7 5.1 %collective-permute-start.4 = (bf16[32,1152]{1,0:T(8,128)(2,1)S(1)}, bf16[32,1152]{1,0:T(8,128)(2,1)S(1)}, u32[]{:S(2)}, u32[]{:S(2)}) collective-permute-start(bf16[32,1152]{1,0:T(8,128)(2,1)S(1)} %get-tuple-element.14.refs_0_), channel_id=1, source_target_pairs={{0,16},{1,17},{2,18},{3,19},{4,6},{5,7},{6,4},{7,5},{8,24},{9,25},... | collective-permute-start | bytes 221192 | tf_op jit(solution)/shard_map/ppermute | solution.py:50
  5.5 5.3 %collective-permute-start.3 = (bf16[32,1152]{1,0:T(8,128)(2,1)S(1)}, bf16[32,1152]{1,0:T(8,128)(2,1)S(1)}, u32[]{:S(2)}, u32[]{:S(2)}) collective-permute-start(bf16[32,1152]{1,0:T(8,128)(2,1)S(1)} %get-tuple-element.14.refs_0_), channel_id=1, source_target_pairs={{0,24},{1,25},{2,26},{3,27},{4,7},{5,6},{6,5},{7,4},{8,16},{9,17},... | collective-permute-start | bytes 221192 | tf_op jit(solution)/shard_map/ppermute | solution.py:50
  6.9 4.8 %collective-permute-start.5 = (bf16[32,1152]{1,0:T(8,128)(2,1)S(1)}, bf16[32,1152]{1,0:T(8,128)(2,1)S(1)}, u32[]{:S(2)}, u32[]{:S(2)}) collective-permute-start(bf16[32,1152]{1,0:T(8,128)(2,1)S(1)} %get-tuple-element.14.refs_0_), channel_id=1, source_target_pairs={{0,8},{1,9},{2,10},{3,11},{4,5},{5,4},{6,7},{7,6},{8,0},{9,1},{10,... | collective-permute-start | bytes 221192 | tf_op jit(solution)/shard_map/ppermute | solution.py:50
  7.8 4.4 %collective-permute-start.7 = (bf16[32,1152]{1,0:T(8,128)(2,1)S(1)}, bf16[32,1152]{1,0:T(8,128)(2,1)S(1)}, u32[]{:S(2)}, u32[]{:S(2)}) collective-permute-start(bf16[32,1152]{1,0:T(8,128)(2,1)S(1)} %collective-permute-done.4.refs_2_), channel_id=1, source_target_pairs={{0,4},{4,0},{8,12},{12,8},{16,20},{20,16},{24,28},{28,24},{1,5},{5... | collective-permute-start | bytes 221192 | tf_op jit(solution)/shard_map/ppermute | solution.py:38
  10.7 1.9 %collective-permute-start.6 = (bf16[32,1152]{1,0:T(8,128)(2,1)S(1)}, bf16[32,1152]{1,0:T(8,128)(2,1)S(1)}, u32[]{:S(2)}, u32[]{:S(2)}) collective-permute-start(bf16[32,1152]{1,0:T(8,128)(2,1)S(1)} %collective-permute-done.3.refs_1_), channel_id=1, source_target_pairs={{0,4},{4,0},{8,12},{12,8},{16,20},{20,16},{24,28},{28,24},{1,5},{5... | collective-permute-start | bytes 221192 | tf_op jit(solution)/shard_map/ppermute | solution.py:38
  11.7 1.3 %collective-permute-start.8 = (bf16[32,1152]{1,0:T(8,128)(2,1)S(1)}, bf16[32,1152]{1,0:T(8,128)(2,1)S(1)}, u32[]{:S(2)}, u32[]{:S(2)}) collective-permute-start(bf16[32,1152]{1,0:T(8,128)(2,1)S(1)} %collective-permute-done.5.refs_3_), channel_id=1, source_target_pairs={{0,4},{4,0},{8,12},{12,8},{16,20},{20,16},{24,28},{28,24},{1,5},{5... | collective-permute-start | bytes 221192 | tf_op jit(solution)/shard_map/ppermute | solution.py:38
  11.7 1.3 %collective-permute-start = (s32[1,64]{1,0:T(1,128)S(1)}, s32[1,64]{1,0:T(1,128)S(1)}, u32[]{:S(2)}, u32[]{:S(2)}) collective-permute-start(s32[1,64]{1,0:T(1,128)S(1)} %bitcast.1), channel_id=1, source_target_pairs={{0,4},{4,0},{8,12},{12,8},{16,20},{20,16},{24,28},{28,24},{1,5},{5... | collective-permute-start | bytes 776 | tf_op jit(solution)/shard_map/ppermute | solution.py:38
  13.6 5.3 %collective-permute-start.9 = (bf16[32,1152]{1,0:T(8,128)(2,1)S(1)}, bf16[32,1152]{1,0:T(8,128)(2,1)S(1)}, u32[]{:S(2)}, u32[]{:S(2)}) collective-permute-start(bf16[32,1152]{1,0:T(8,128)(2,1)S(1)} %get-tuple-element.17), channel_id=1, source_target_pairs={{0,24},{1,25},{2,26},{3,27},{4,7},{5,6},{6,5},{7,4},{8,16},{9,17},... | collective-permute-start | bytes 221192 | tf_op jit(solution)/shard_map/ppermute | solution.py:50
  16.1 4.4 %collective-permute-start.10 = (bf16[32,1152]{1,0:T(8,128)(2,1)S(1)}, bf16[32,1152]{1,0:T(8,128)(2,1)S(1)}, u32[]{:S(2)}, u32[]{:S(2)}) collective-permute-start(bf16[32,1152]{1,0:T(8,128)(2,1)S(1)} %get-tuple-element.18), channel_id=1, source_target_pairs={{0,8},{1,9},{2,10},{3,11},{4,5},{5,4},{6,7},{7,6},{8,0},{9,1},{10,... | collective-permute-start | bytes 221192 | tf_op jit(solution)/shard_map/ppermute | solution.py:50
  16.7 4.0 %collective-permute-start.11 = (bf16[16,1152]{1,0:T(8,128)(2,1)S(1)}, bf16[16,1152]{1,0:T(8,128)(2,1)S(1)}, u32[]{:S(2)}, u32[]{:S(2)}) collective-permute-start(bf16[16,1152]{1,0:T(8,128)(2,1)S(1)} %get-tuple-element.20), channel_id=1, source_target_pairs={{0,16},{1,17},{2,18},{3,19},{4,6},{5,7},{6,4},{7,5},{8,24},{9,25},... | collective-permute-start | bytes 110600 | tf_op jit(solution)/shard_map/ppermute | solution.py:50
  17.2 4.3 %collective-permute-start.12 = (bf16[16,1152]{1,0:T(8,128)(2,1)S(1)}, bf16[16,1152]{1,0:T(8,128)(2,1)S(1)}, u32[]{:S(2)}, u32[]{:S(2)}) collective-permute-start(bf16[16,1152]{1,0:T(8,128)(2,1)S(1)} %get-tuple-element.24), channel_id=1, source_target_pairs={{0,20},{1,21},{2,22},{3,23},{4,2},{5,3},{6,0},{7,1},{8,28},{9,29},... | collective-permute-start | bytes 110600 | tf_op jit(solution)/shard_map/ppermute | solution.py:50
  20.5 1.3 %collective-permute-start.13 = (f32[16,1152]{1,0:T(8,128)S(1)}, f32[16,1152]{1,0:T(8,128)S(1)}, u32[]{:S(2)}, u32[]{:S(2)}) collective-permute-start(f32[16,1152]{1,0:T(8,128)S(1)} %get-tuple-element.25), channel_id=1, source_target_pairs={{0,4},{4,0},{8,12},{12,8},{16,20},{20,16},{24,28},{28,24},{1,5},{5... | collective-permute-start | bytes 221192 | tf_op jit(solution)/shard_map/ppermute | solution.py:38

commit v10 on v9

--- a/solution.py
+++ b/solution.py
@@ -14,7 +14,6 @@
 bf16 = jnp.bfloat16
 VMEM = pl.BlockSpec(memory_space=pltpu.VMEM)
 LONG = pl.CostEstimate(flops=10**10, bytes_accessed=10**7, transcendentals=0)
-SHORT = pl.CostEstimate(flops=2 * 10**8, bytes_accessed=10**5, transcendentals=0)
 
 
 def normalize(raw):
@@ -79,6 +78,17 @@
     mine_ref[rows:, :] = jnp.where(even, far_txt, own_img)
     other_ref[:rows, :] = jnp.where(even, own_img, far_txt)
     other_ref[rows:, :] = jnp.where(even, far_img, own_txt)
+
+
+def pack_kernel(ids_ref, piece_ref, out_ref):
+    height = piece_ref.shape[0]
+    tile = out_ref.shape[0] - height
+    count = ids_ref.shape[1]
+    out_ref[:height, :] = piece_ref[...]
+    ids = ids_ref[...]
+    high = lax.broadcasted_iota(jnp.int32, (tile, count), 0) == 0
+    out_ref[height:, :] = jnp.zeros((tile, out_ref.shape[1]), bf16)
+    out_ref[height:, :count] = jnp.where(high, ids // 256, ids % 256).astype(f32).astype(bf16)
 
 
 def row_ids(rows, ids, far_ids, count):
@@ -117,12 +127,15 @@
     refs[-1][...] = scores_of(refs[:blocks], refs[blocks:-1])
 
 
-def rest_kernel(blocks, split, ids_ref, far_ids_ref, most_ref, *refs):
-    mine_refs, other_refs = refs[:blocks], refs[blocks:2 * blocks]
+def rest_kernel(blocks, split, ids_ref, most_ref, *refs):
+    mine_refs, (*other_refs, last_ref) = refs[:blocks], refs[blocks:2 * blocks]
     own_ref, same_ref, cross_ref, *send_refs = refs[2 * blocks:]
     height = own_ref.shape[0]
     rows = height // 2
-    mine_ids, other_ids = side_ids(rows, ids_ref[...], far_ids_ref[...], blocks * height)
+    code = last_ref[height:, :ids_ref.shape[1]].astype(f32)
+    far_ids = (code[0:1] * 256.0 + code[1:2]).astype(jnp.int32)
+    mine_ids, other_ids = side_ids(rows, ids_ref[...], far_ids, blocks * height)
+    other_refs = [*other_refs, last_ref.at[:height, :]]
     scores = jnp.concatenate([most_ref[...], scores_of(mine_refs, other_refs[-1:])], axis=1)
     coeff = pair_coeff(scale_logit * scores + shift_logit, mine_ids == other_ids)
     other = jnp.concatenate([ref[...] for ref in other_refs], axis=0)
@@ -184,19 +197,21 @@
     mine, other = call(sides_kernel, [pair] * 2, [near, far_txt, far_img])
     order = list(range(blocks - 1, 0, -1))
     mine = [mine] + [chip_swap(mine, k) for k in order]
-    other = [other] + [core_swap(block) for block in mine[1:]]
+    packed = jax.ShapeDtypeStruct((3 * rows, width), bf16)
+    (packed,) = call(pack_kernel, [packed], [ids, mine[-1]])
+    other = [other] + [core_swap(block) for block in [*mine[1:-1], packed]]
     count = blocks * 2 * rows
     (most,) = call(
         functools.partial(most_kernel, blocks),
         [jax.ShapeDtypeStruct((count, count - 2 * rows), f32)],
         [*mine, *other[:-1]],
-        cost=SHORT,
+        cost=LONG,
     )
     split = min(2, blocks - 1)
     own, same, cross, *send = call(
         functools.partial(rest_kernel, blocks, split),
         [total] + [piece] * 2 + [pair] * (blocks - 2),
-        [ids, core_swap(ids), most, *mine, *other],
+        [ids, most, *mine, *other],
     )
     far = order.pop(split - 1)
     got = [chip_swap(block, k) for k, block in zip(order, send)]

time: 22.8 us -> 22.9 us (level)
  waiting for transfers between devices: 7.19 us -> 7.8 us
  starting transfers between devices: 12 us -> 11.4 us
    ppermute x7 -> x6, waiting for transfers between devices: 1.54 us -> 2 us  [core_swap(): return lax.ppermute(block, 'img', [(i, i ^ 1) for i in range(size)])]
    ppermute x7 -> x6, starting transfers between devices: 2.7 us -> 2.26 us  [core_swap(): return lax.ppermute(block, 'img', [(i, i ^ 1) for i in range(size)])]
    pallas_call x6 -> x7, Pallas kernels: 1.92 us -> 1.96 us  [call(): pl.pallas_call(kernel, out_shape=outs, in_specs=[VMEM] * len(args), out_s...]
  transfers between devices with their start and end apart: 14 -> 13, of which waited for: 10 -> 10; matrix products, arithmetic and copies ran while one was open for 3% -> 3% of each run, Pallas kernels for 2% -> 2%
where the time goes in v10:
time: 22.9 us; the launch traced here: 22.7 us
  starting transfers between devices  11.4 us (50%)
  waiting for transfers between devices  7.8 us (34%)
  Pallas kernels  1.96 us (9%)
  local copies, waits for them, and re-layouts  0.79 us (3%)
  between operations  0.71 us (3%)
    ppermute x7, starting transfers between devices, chip_swap(): return lax.ppermute(block, ('img', 'txt'), pairs)  9.17 us
    ppermute x7, waiting for transfers between devices, chip_swap(): return lax.ppermute(block, ('img', 'txt'), pairs)  5.8 us
    ppermute x6, starting transfers between devices, core_swap(): return lax.ppermute(block, 'img', [(i, i ^ 1) for i in range(size)])  2.26 us
    ppermute x6, waiting for transfers between devices, core_swap(): return lax.ppermute(block, 'img', [(i, i ^ 1) for i in range(size)])  2 us
    pallas_call x7, Pallas kernels, call(): pl.pallas_call(kernel, out_shape=outs, in_specs=[VMEM] * len(args), out_s...  1.96 us
    unnamed x5, local copies, waits for them, and re-layouts  0.78 us
  transfers between devices with their start and end apart: 13, of which 10 were waited for; matrix products, arithmetic and copies ran while one was open for 3% of the time, Pallas kernels for 2%

profile of v10, /device:TPU:0, one launch (start us, length us, event | category | flops | bytes accessed | tf_op | source)
XLA Modules:
  0.0 22.7 jit_solution(7563476517798611940)
XLA Ops:
  0.6 0.5 %collective-permute-start.1 = (bf16[16,1152]{1,0:T(8,128)(2,1)}, bf16[16,1152]{1,0:T(8,128)(2,1)S(1)}, u32[]{:S(2)}, u32[]{:S(2)}) collective-permute-start(bf16[16,1152]{1,0:T(8,128)(2,1)} %param.3), channel_id=1, source_target_pairs={{0,4},{4,0},{8,12},{12,8},{16,20},{20,16},{24,28},{28,24},{1,5},{5... | collective-permute-start | bytes 110600 | tf_op jit(solution)/shard_map/ppermute | solution.py:37
  1.2 0.8 %constant_dynamic-update-slice_fusion.1 = bf16[32,1152]{1,0:T(8,128)(2,1)S(1)} fusion(bf16[16,1152]{1,0:T(8,128)(2,1)} %param.4), kind=kLoop, calls=%fused_computation.1 | loop fusion | bytes 73728
  2.0 0.2 collective-permute-done.1.img_ref
  2.2 0.3 %collective-permute-done.txt_ref = bf16[16,1152]{1,0:T(8,128)(2,1)S(1)} collective-permute-done((bf16[16,1152]{1,0:T(8,128)(2,1)}, bf16[16,1152]{1,0:T(8,128)(2,1)S(1)}, u32[]{:S(2)}, u32[]{:S(2)}) %collective-permute-start) | collective-permute-done | bytes 36896 | tf_op jit(solution)/shard_map/ppermute | solution.py:37
  2.7 2.7 %collective-permute-start.3 = (bf16[32,1152]{1,0:T(8,128)(2,1)S(1)}, bf16[32,1152]{1,0:T(8,128)(2,1)S(1)}, u32[]{:S(2)}, u32[]{:S(2)}) collective-permute-start(bf16[32,1152]{1,0:T(8,128)(2,1)S(1)} %get-tuple-element.14.refs_0_), channel_id=1, source_target_pairs={{0,16},{1,17},{2,18},{3,19},{4,6},{5,7},{6,4},{7,5},{8,24},{9,25},... | collective-permute-start | bytes 221192 | tf_op jit(solution)/shard_map/ppermute | solution.py:49
  5.5 1.4 %collective-permute-start.2 = (bf16[32,1152]{1,0:T(8,128)(2,1)S(1)}, bf16[32,1152]{1,0:T(8,128)(2,1)S(1)}, u32[]{:S(2)}, u32[]{:S(2)}) collective-permute-start(bf16[32,1152]{1,0:T(8,128)(2,1)S(1)} %get-tuple-element.14.refs_0_), channel_id=1, source_target_pairs={{0,24},{1,25},{2,26},{3,27},{4,7},{5,6},{6,5},{7,4},{8,16},{9,17},... | collective-permute-start | bytes 221192 | tf_op jit(solution)/shard_map/ppermute | solution.py:49
  7.0 0.8 %collective-permute-done.3.refs_2_ = bf16[32,1152]{1,0:T(8,128)(2,1)S(1)} collective-permute-done((bf16[32,1152]{1,0:T(8,128)(2,1)S(1)}, bf16[32,1152]{1,0:T(8,128)(2,1)S(1)}, u32[]{:S(2)}, u32[]{:S(2)}) %collective-permute-start.3) | collective-permute-done | bytes 73760 | tf_op jit(solution)/shard_map/ppermute | solution.py:49
  7.8 0.5 %collective-permute-start.6 = (bf16[32,1152]{1,0:T(8,128)(2,1)S(1)}, bf16[32,1152]{1,0:T(8,128)(2,1)S(1)}, u32[]{:S(2)}, u32[]{:S(2)}) collective-permute-start(bf16[32,1152]{1,0:T(8,128)(2,1)S(1)} %collective-permute-done.3.refs_2_), channel_id=1, source_target_pairs={{0,4},{4,0},{8,12},{12,8},{16,20},{20,16},{24,28},{28,24},{1,5},{5... | collective-permute-start | bytes 221192 | tf_op jit(solution)/shard_map/ppermute | solution.py:37
  8.4 2.4 %collective-permute-done.2.refs_1_ = bf16[32,1152]{1,0:T(8,128)(2,1)S(1)} collective-permute-done((bf16[32,1152]{1,0:T(8,128)(2,1)S(1)}, bf16[32,1152]{1,0:T(8,128)(2,1)S(1)}, u32[]{:S(2)}, u32[]{:S(2)}) %collective-permute-start.2) | collective-permute-done | bytes 73760 | tf_op jit(solution)/shard_map/ppermute | solution.py:49
  10.7 1.0 %collective-permute-start.5 = (bf16[32,1152]{1,0:T(8,128)(2,1)S(1)}, bf16[32,1152]{1,0:T(8,128)(2,1)S(1)}, u32[]{:S(2)}, u32[]{:S(2)}) collective-permute-start(bf16[32,1152]{1,0:T(8,128)(2,1)S(1)} %collective-permute-done.2.refs_1_), channel_id=1, source_target_pairs={{0,4},{4,0},{8,12},{12,8},{16,20},{20,16},{24,28},{28,24},{1,5},{5... | collective-permute-start | bytes 221192 | tf_op jit(solution)/shard_map/ppermute | solution.py:37
  11.8 0.8 %collective-permute-done.5.refs_5_ = bf16[32,1152]{1,0:T(8,128)(2,1)S(1)} collective-permute-done((bf16[32,1152]{1,0:T(8,128)(2,1)S(1)}, bf16[32,1152]{1,0:T(8,128)(2,1)S(1)}, u32[]{:S(2)}, u32[]{:S(2)}) %collective-permute-start.5) | collective-permute-done | bytes 73760 | tf_op jit(solution)/shard_map/ppermute | solution.py:37
  12.6 0.2 %shard_map.51.most_ref = f32[128,96]{1,0:T(8,128)S(1)} custom-call(bf16[32,1152]{1,0:T(8,128)(2,1)S(1)} %get-tuple-element.14.refs_0_, bf16[32,1152]{1,0:T(8,128)(2,1)S(1)} %collective-permute-done.2.refs_1_, bf16[32,1152]{1,0:T(8,128)(2,1)S(1)} %collective-permute-done.3.refs_2_, bf16[32,1152]{1,0:T(8,128)(2,1)S(1)} %collective-permute-done.4.refs_3_.piece_ref, ...), custom_call_target="tpu_custom_call" | custom-call | flops 10000000000 | bytes 10000000 | tf_op jit(solution)/shard_map/pallas_call | solution.py:58
  12.8 0.3 %collective-permute-done.7.refs_7_ = bf16[48,1152]{1,0:T(8,128)(2,1)S(1)} collective-permute-done((bf16[48,1152]{1,0:T(8,128)(2,1)S(1)}, bf16[48,1152]{1,0:T(8,128)(2,1)S(1)}, u32[]{:S(2)}, u32[]{:S(2)}) %collective-permute-start.7) | collective-permute-done | bytes 110624 | tf_op jit(solution)/shard_map/ppermute | solution.py:37
  13.1 0.6 %shard_map.53 = (f32[32,1152]{1,0:T(8,128)S(1)}, bf16[16,1152]{1,0:T(8,128)(2,1)S(1)}, bf16[16,1152]{1,0:T(8,128)(2,1)S(1)}, bf16[32,1152]{1,0:T(8,128)(2,1)S(1)}, bf16[32,1152]{1,0:T(8,128)(2,1)S(1)}) custom-call(s32[1,64]{1,0:T(1,128)S(1)} %bitcast.2, f32[128,96]{1,0:T(8,128)S(1)} %shard_map.51.most_ref, bf16[32,1152]{1,0:T(8,128)(2,1)S(1)} %get-tuple-element.14.refs_0_, ...), custom_call_target="tpu_custom_call" | custom-call | tf_op jit(solution)/shard_map/pallas_call | solution.py:58
  13.7 2.5 %collective-permute-start.8 = (bf16[32,1152]{1,0:T(8,128)(2,1)S(1)}, bf16[32,1152]{1,0:T(8,128)(2,1)S(1)}, u32[]{:S(2)}, u32[]{:S(2)}) collective-permute-start(bf16[32,1152]{1,0:T(8,128)(2,1)S(1)} %get-tuple-element.17), channel_id=1, source_target_pairs={{0,24},{1,25},{2,26},{3,27},{4,7},{5,6},{6,5},{7,4},{8,16},{9,17},... | collective-permute-start | bytes 221192 | tf_op jit(solution)/shard_map/ppermute | solution.py:49
  16.2 0.5 %collective-permute-start.9 = (bf16[32,1152]{1,0:T(8,128)(2,1)S(1)}, bf16[32,1152]{1,0:T(8,128)(2,1)S(1)}, u32[]{:S(2)}, u32[]{:S(2)}) collective-permute-start(bf16[32,1152]{1,0:T(8,128)(2,1)S(1)} %get-tuple-element.18), channel_id=1, source_target_pairs={{0,8},{1,9},{2,10},{3,11},{4,5},{5,4},{6,7},{7,6},{8,0},{9,1},{10,... | collective-permute-start | bytes 221192 | tf_op jit(solution)/shard_map/ppermute | solution.py:49
  16.7 0.5 %collective-permute-start.10 = (bf16[16,1152]{1,0:T(8,128)(2,1)S(1)}, bf16[16,1152]{1,0:T(8,128)(2,1)S(1)}, u32[]{:S(2)}, u32[]{:S(2)}) collective-permute-start(bf16[16,1152]{1,0:T(8,128)(2,1)S(1)} %get-tuple-element.20), channel_id=1, source_target_pairs={{0,16},{1,17},{2,18},{3,19},{4,6},{5,7},{6,4},{7,5},{8,24},{9,25},... | collective-permute-start | bytes 110600 | tf_op jit(solution)/shard_map/ppermute | solution.py:49
  17.2 1.3 %collective-permute-start.11 = (bf16[16,1152]{1,0:T(8,128)(2,1)S(1)}, bf16[16,1152]{1,0:T(8,128)(2,1)S(1)}, u32[]{:S(2)}, u32[]{:S(2)}) collective-permute-start(bf16[16,1152]{1,0:T(8,128)(2,1)S(1)} %get-tuple-element.24), channel_id=1, source_target_pairs={{0,20},{1,21},{2,22},{3,23},{4,2},{5,3},{6,0},{7,1},{8,28},{9,29},... | collective-permute-start | bytes 110600 | tf_op jit(solution)/shard_map/ppermute | solution.py:49
  18.6 0.4 %collective-permute-done.8.refs_0_ = bf16[32,1152]{1,0:T(8,128)(2,1)S(1)} collective-permute-done((bf16[32,1152]{1,0:T(8,128)(2,1)S(1)}, bf16[32,1152]{1,0:T(8,128)(2,1)S(1)}, u32[]{:S(2)}, u32[]{:S(2)}) %collective-permute-start.8) | collective-permute-done | bytes 73760 | tf_op jit(solution)/shard_map/ppermute | solution.py:49
  19.0 1.5 %collective-permute-done.9.refs_1_ = bf16[32,1152]{1,0:T(8,128)(2,1)S(1)} collective-permute-done((bf16[32,1152]{1,0:T(8,128)(2,1)S(1)}, bf16[32,1152]{1,0:T(8,128)(2,1)S(1)}, u32[]{:S(2)}, u32[]{:S(2)}) %collective-permute-start.9) | collective-permute-done | bytes 73760 | tf_op jit(solution)/shard_map/ppermute | solution.py:49
  20.7 0.2 shard_map.55
  20.9 0.6 %collective-permute-done.11.cross_ref = bf16[16,1152]{1,0:T(8,128)(2,1)S(1)} collective-permute-done((bf16[16,1152]{1,0:T(8,128)(2,1)S(1)}, bf16[16,1152]{1,0:T(8,128)(2,1)S(1)}, u32[]{:S(2)}, u32[]{:S(2)}) %collective-permute-start.11) | collective-permute-done | bytes 36896 | tf_op jit(solution)/shard_map/ppermute | solution.py:49
  21.5 0.4 %collective-permute-done.12.got_ref = f32[16,1152]{1,0:T(8,128)S(1)} collective-permute-done((f32[16,1152]{1,0:T(8,128)S(1)}, f32[16,1152]{1,0:T(8,128)S(1)}, u32[]{:S(2)}, u32[]{:S(2)}) %collective-permute-start.12) | collective-permute-done | bytes 73760 | tf_op jit(solution)/shard_map/ppermute | solution.py:37
  21.9 0.8 %shard_map.56 = (f32[16,1152]{1,0:T(8,128)}, f32[16,1152]{1,0:T(8,128)}) custom-call(f32[16,1152]{1,0:T(8,128)S(1)} %get-tuple-element.21.grad_ref, f32[16,1152]{1,0:T(8,128)S(1)} %get-tuple-element.22.unit_ref, f32[16,1]{1,0:T(8,128)S(1)} %get-tuple-element.23.inverse_ref, bf16[16,1152]{1,0:T(8,128)(2,1)S(1)} %collective-permute-done.11.cross_ref, ...), custom_call_target="tpu_custom_call" | custom-call | tf_op jit(solution)/shard_map/pallas_call | solution.py:58
  (15 shorter events, 0.6 us)
Async XLA Ops:
  0.6 1.4 %copy-start.1 = (bf16[16,1152]{1,0:T(8,128)(2,1)S(1)}, bf16[16,1152]{1,0:T(8,128)(2,1)}, u32[]{:S(2)}) copy-start(bf16[16,1152]{1,0:T(8,128)(2,1)} %param.3) | copy-start | bytes 110596
  0.6 1.6 %collective-permute-start.1 = (bf16[16,1152]{1,0:T(8,128)(2,1)}, bf16[16,1152]{1,0:T(8,128)(2,1)S(1)}, u32[]{:S(2)}, u32[]{:S(2)}) collective-permute-start(bf16[16,1152]{1,0:T(8,128)(2,1)} %param.3), channel_id=1, source_target_pairs={{0,4},{4,0},{8,12},{12,8},{16,20},{20,16},{24,28},{28,24},{1,5},{5... | collective-permute-start | bytes 110600 | tf_op jit(solution)/shard_map/ppermute | solution.py:37
  1.2 1.4 %collective-permute-start = (bf16[16,1152]{1,0:T(8,128)(2,1)}, bf16[16,1152]{1,0:T(8,128)(2,1)S(1)}, u32[]{:S(2)}, u32[]{:S(2)}) collective-permute-start(bf16[16,1152]{1,0:T(8,128)(2,1)} %param.4), channel_id=1, source_target_pairs={{0,4},{4,0},{8,12},{12,8},{16,20},{20,16},{24,28},{28,24},{1,5},{5... | collective-permute-start | bytes 110600 | tf_op jit(solution)/shard_map/ppermute | solution.py:37
  2.7 9.0 %copy-start = (s32[64]{0:T(128)S(1)}, s32[64]{0:T(128)}, u32[]{:S(2)}) copy-start(s32[64]{0:T(128)} %param.5) | copy-start | bytes 772
  2.7 5.1 %collective-permute-start.3 = (bf16[32,1152]{1,0:T(8,128)(2,1)S(1)}, bf16[32,1152]{1,0:T(8,128)(2,1)S(1)}, u32[]{:S(2)}, u32[]{:S(2)}) collective-permute-start(bf16[32,1152]{1,0:T(8,128)(2,1)S(1)} %get-tuple-element.14.refs_0_), channel_id=1, source_target_pairs={{0,16},{1,17},{2,18},{3,19},{4,6},{5,7},{6,4},{7,5},{8,24},{9,25},... | collective-permute-start | bytes 221192 | tf_op jit(solution)/shard_map/ppermute | solution.py:49
  5.5 5.3 %collective-permute-start.2 = (bf16[32,1152]{1,0:T(8,128)(2,1)S(1)}, bf16[32,1152]{1,0:T(8,128)(2,1)S(1)}, u32[]{:S(2)}, u32[]{:S(2)}) collective-permute-start(bf16[32,1152]{1,0:T(8,128)(2,1)S(1)} %get-tuple-element.14.refs_0_), channel_id=1, source_target_pairs={{0,24},{1,25},{2,26},{3,27},{4,7},{5,6},{6,5},{7,4},{8,16},{9,17},... | collective-permute-start | bytes 221192 | tf_op jit(solution)/shard_map/ppermute | solution.py:49
  6.9 4.8 %collective-permute-start.4 = (bf16[32,1152]{1,0:T(8,128)(2,1)S(1)}, bf16[32,1152]{1,0:T(8,128)(2,1)S(1)}, u32[]{:S(2)}, u32[]{:S(2)}) collective-permute-start(bf16[32,1152]{1,0:T(8,128)(2,1)S(1)} %get-tuple-element.14.refs_0_), channel_id=1, source_target_pairs={{0,8},{1,9},{2,10},{3,11},{4,5},{5,4},{6,7},{7,6},{8,0},{9,1},{10,... | collective-permute-start | bytes 221192 | tf_op jit(solution)/shard_map/ppermute | solution.py:49
  7.8 4.0 %collective-permute-start.6 = (bf16[32,1152]{1,0:T(8,128)(2,1)S(1)}, bf16[32,1152]{1,0:T(8,128)(2,1)S(1)}, u32[]{:S(2)}, u32[]{:S(2)}) collective-permute-start(bf16[32,1152]{1,0:T(8,128)(2,1)S(1)} %collective-permute-done.3.refs_2_), channel_id=1, source_target_pairs={{0,4},{4,0},{8,12},{12,8},{16,20},{20,16},{24,28},{28,24},{1,5},{5... | collective-permute-start | bytes 221192 | tf_op jit(solution)/shard_map/ppermute | solution.py:37
  10.7 1.9 %collective-permute-start.5 = (bf16[32,1152]{1,0:T(8,128)(2,1)S(1)}, bf16[32,1152]{1,0:T(8,128)(2,1)S(1)}, u32[]{:S(2)}, u32[]{:S(2)}) collective-permute-start(bf16[32,1152]{1,0:T(8,128)(2,1)S(1)} %collective-permute-done.2.refs_1_), channel_id=1, source_target_pairs={{0,4},{4,0},{8,12},{12,8},{16,20},{20,16},{24,28},{28,24},{1,5},{5... | collective-permute-start | bytes 221192 | tf_op jit(solution)/shard_map/ppermute | solution.py:37
  11.7 1.4 %collective-permute-start.7 = (bf16[48,1152]{1,0:T(8,128)(2,1)S(1)}, bf16[48,1152]{1,0:T(8,128)(2,1)S(1)}, u32[]{:S(2)}, u32[]{:S(2)}) collective-permute-start(bf16[48,1152]{1,0:T(8,128)(2,1)S(1)} %shard_map.52), channel_id=1, source_target_pairs={{0,4},{4,0},{8,12},{12,8},{16,20},{20,16},{24,28},{28,24},{1,5},{5... | collective-permute-start | bytes 331784 | tf_op jit(solution)/shard_map/ppermute | solution.py:37
  13.7 5.3 %collective-permute-start.8 = (bf16[32,1152]{1,0:T(8,128)(2,1)S(1)}, bf16[32,1152]{1,0:T(8,128)(2,1)S(1)}, u32[]{:S(2)}, u32[]{:S(2)}) collective-permute-start(bf16[32,1152]{1,0:T(8,128)(2,1)S(1)} %get-tuple-element.17), channel_id=1, source_target_pairs={{0,24},{1,25},{2,26},{3,27},{4,7},{5,6},{6,5},{7,4},{8,16},{9,17},... | collective-permute-start | bytes 221192 | tf_op jit(solution)/shard_map/ppermute | solution.py:49
  16.2 4.4 %collective-permute-start.9 = (bf16[32,1152]{1,0:T(8,128)(2,1)S(1)}, bf16[32,1152]{1,0:T(8,128)(2,1)S(1)}, u32[]{:S(2)}, u32[]{:S(2)}) collective-permute-start(bf16[32,1152]{1,0:T(8,128)(2,1)S(1)} %get-tuple-element.18), channel_id=1, source_target_pairs={{0,8},{1,9},{2,10},{3,11},{4,5},{5,4},{6,7},{7,6},{8,0},{9,1},{10,... | collective-permute-start | bytes 221192 | tf_op jit(solution)/shard_map/ppermute | solution.py:49
  16.7 4.0 %collective-permute-start.10 = (bf16[16,1152]{1,0:T(8,128)(2,1)S(1)}, bf16[16,1152]{1,0:T(8,128)(2,1)S(1)}, u32[]{:S(2)}, u32[]{:S(2)}) collective-permute-start(bf16[16,1152]{1,0:T(8,128)(2,1)S(1)} %get-tuple-element.20), channel_id=1, source_target_pairs={{0,16},{1,17},{2,18},{3,19},{4,6},{5,7},{6,4},{7,5},{8,24},{9,25},... | collective-permute-start | bytes 110600 | tf_op jit(solution)/shard_map/ppermute | solution.py:49
  17.2 4.3 %collective-permute-start.11 = (bf16[16,1152]{1,0:T(8,128)(2,1)S(1)}, bf16[16,1152]{1,0:T(8,128)(2,1)S(1)}, u32[]{:S(2)}, u32[]{:S(2)}) collective-permute-start(bf16[16,1152]{1,0:T(8,128)(2,1)S(1)} %get-tuple-element.24), channel_id=1, source_target_pairs={{0,20},{1,21},{2,22},{3,23},{4,2},{5,3},{6,0},{7,1},{8,28},{9,29},... | collective-permute-start | bytes 110600 | tf_op jit(solution)/shard_map/ppermute | solution.py:49
  20.6 1.3 %collective-permute-start.12 = (f32[16,1152]{1,0:T(8,128)S(1)}, f32[16,1152]{1,0:T(8,128)S(1)}, u32[]{:S(2)}, u32[]{:S(2)}) collective-permute-start(f32[16,1152]{1,0:T(8,128)S(1)} %get-tuple-element.25), channel_id=1, source_target_pairs={{0,4},{4,0},{8,12},{12,8},{16,20},{20,16},{24,28},{28,24},{1,5},{5... | collective-permute-start | bytes 221192 | tf_op jit(solution)/shard_map/ppermute | solution.py:37

commit v11 on v10

--- a/solution.py
+++ b/solution.py
@@ -10,6 +10,7 @@
 scale_logit = 8.0
 shift_logit = -4.0
 epsilon = 1e-06
+LANES = 128
 f32 = jnp.float32
 bf16 = jnp.bfloat16
 VMEM = pl.BlockSpec(memory_space=pltpu.VMEM)
@@ -81,14 +82,32 @@
 
 
 def pack_kernel(ids_ref, piece_ref, out_ref):
-    height = piece_ref.shape[0]
-    tile = out_ref.shape[0] - height
+    height, width = piece_ref.shape
+    tiles = width // LANES
     count = ids_ref.shape[1]
-    out_ref[:height, :] = piece_ref[...]
-    ids = ids_ref[...]
-    high = lax.broadcasted_iota(jnp.int32, (tile, count), 0) == 0
-    out_ref[height:, :] = jnp.zeros((tile, out_ref.shape[1]), bf16)
-    out_ref[height:, :count] = jnp.where(high, ids // 256, ids % 256).astype(f32).astype(bf16)
+    for k in range(tiles):
+        out_ref[k * height:(k + 1) * height, :] = piece_ref[:, k * LANES:(k + 1) * LANES]
+    rest = out_ref.shape[0] - tiles * height
+    row = lax.broadcasted_iota(jnp.int32, (rest, LANES), 0)
+    code = jnp.zeros((rest, LANES), f32)
+    for k in range(0, count, LANES):
+        ids = ids_ref[:, k:k + LANES]
+        if ids.shape[1] < LANES:
+            ids = jnp.concatenate([ids, jnp.zeros((1, LANES - ids.shape[1]), ids.dtype)], axis=1)
+        code = jnp.where(row == 2 * k // LANES, (ids // 256).astype(f32), code)
+        code = jnp.where(row == 2 * k // LANES + 1, (ids % 256).astype(f32), code)
+    out_ref[tiles * height:, :] = code.astype(bf16)
+
+
+def unpack(ref, height, width, count):
+    tiles = width // LANES
+    piece = jnp.concatenate(
+        [ref[k * height:(k + 1) * height, :] for k in range(tiles)], axis=1
+    )
+    code = ref[tiles * height:, :].astype(f32)
+    ids = [code[k:k + 1] * 256.0 + code[k + 1:k + 2] for k in range(0, 2 * count // LANES or 2, 2)]
+    ids = jnp.concatenate(ids, axis=1)[:, :count].astype(jnp.int32)
+    return piece, ids
 
 
 def row_ids(rows, ids, far_ids, count):
@@ -117,28 +136,26 @@
     return jnp.where(even, txt_ids, img_ids), other_ids
 
 
-def scores_of(mine_refs, other_refs):
+def scores_of(mine_refs, other):
     mine = jnp.concatenate([ref[...] for ref in mine_refs], axis=0)
-    other = jnp.concatenate([ref[...] for ref in other_refs], axis=0)
     return lax.dot_general(mine, other, (((1,), (1,)), ((), ())), preferred_element_type=f32)
 
 
 def most_kernel(blocks, *refs):
-    refs[-1][...] = scores_of(refs[:blocks], refs[blocks:-1])
+    other = jnp.concatenate([ref[...] for ref in refs[blocks:-1]], axis=0)
+    refs[-1][...] = scores_of(refs[:blocks], other)
 
 
 def rest_kernel(blocks, split, ids_ref, most_ref, *refs):
     mine_refs, (*other_refs, last_ref) = refs[:blocks], refs[blocks:2 * blocks]
     own_ref, same_ref, cross_ref, *send_refs = refs[2 * blocks:]
-    height = own_ref.shape[0]
+    height, width = own_ref.shape
     rows = height // 2
-    code = last_ref[height:, :ids_ref.shape[1]].astype(f32)
-    far_ids = (code[0:1] * 256.0 + code[1:2]).astype(jnp.int32)
+    last, far_ids = unpack(last_ref, height, width, ids_ref.shape[1])
     mine_ids, other_ids = side_ids(rows, ids_ref[...], far_ids, blocks * height)
-    other_refs = [*other_refs, last_ref.at[:height, :]]
-    scores = jnp.concatenate([most_ref[...], scores_of(mine_refs, other_refs[-1:])], axis=1)
+    scores = jnp.concatenate([most_ref[...], scores_of(mine_refs, last)], axis=1)
     coeff = pair_coeff(scale_logit * scores + shift_logit, mine_ids == other_ids)
-    other = jnp.concatenate([ref[...] for ref in other_refs], axis=0)
+    other = jnp.concatenate([*[ref[...] for ref in other_refs], last], axis=0)
     part = jnp.dot(coeff, other, preferred_element_type=f32)
     own_ref[...] = part[:height]
     whole = [k for k in range(1, blocks) if k != split]
@@ -158,7 +175,7 @@
         total = total + ref[...].astype(f32)
     even = is_even()
     keep_ref[...] = jnp.where(even, total[:rows], total[rows:])
-    send_ref[...] = jnp.where(even, total[rows:], total[:rows])
+    send_ref[...] = jnp.where(even, total[rows:], total[:rows]).astype(bf16)
 
 
 def keep_kernel(raw_ref, keep_ref, same_ref, grad_ref, unit_ref, inverse_ref):
@@ -176,7 +193,7 @@
 
 def out_kernel(grad_ref, unit_ref, inverse_ref, cross_ref, got_ref, img_ref, txt_ref):
     even = is_even()
-    total = got_ref[...] + cross_ref[...].astype(f32)
+    total = got_ref[...].astype(f32) + cross_ref[...].astype(f32)
     keep = grad_ref[...]
     got = back_norm(unit_ref[...], inverse_ref[...], total)
     txt_ref[...] = jnp.where(even, keep, got)
@@ -197,7 +214,7 @@
     mine, other = call(sides_kernel, [pair] * 2, [near, far_txt, far_img])
     order = list(range(blocks - 1, 0, -1))
     mine = [mine] + [chip_swap(mine, k) for k in order]
-    packed = jax.ShapeDtypeStruct((3 * rows, width), bf16)
+    packed = jax.ShapeDtypeStruct((2 * rows * (width // LANES) + 16, LANES), bf16)
     (packed,) = call(pack_kernel, [packed], [ids, mine[-1]])
     other = [other] + [core_swap(block) for block in [*mine[1:-1], packed]]
     count = blocks * 2 * rows
@@ -217,7 +234,7 @@
     got = [chip_swap(block, k) for k, block in zip(order, send)]
     same = chip_swap(same, far)
     cross = chip_swap(cross, far, cross=1)
-    keep, send = call(sum_kernel, [single] * 2, [own, *got])
+    keep, send = call(sum_kernel, [single, piece], [own, *got])
     got = core_swap(send)
     column = jax.ShapeDtypeStruct((rows, 1), f32)
     kept = call(keep_kernel, [single, single, column], [near, keep, same], cost=LONG)

time: 22.9 us -> 22.8 us (level)
  no operation moved by 1% of the time
where the time goes in v11:
time: 22.8 us; the launch traced here: 22.6 us
  starting transfers between devices  11.4 us (50%)
  waiting for transfers between devices  7.7 us (34%)
  Pallas kernels  1.96 us (9%)
  local copies, waits for them, and re-layouts  0.79 us (3%)
  between operations  0.71 us (3%)
    ppermute x7, starting transfers between devices, chip_swap(): return lax.ppermute(block, ('img', 'txt'), pairs)  9.18 us
    ppermute x7, waiting for transfers between devices, chip_swap(): return lax.ppermute(block, ('img', 'txt'), pairs)  5.8 us
    ppermute x6, starting transfers between devices, core_swap(): return lax.ppermute(block, 'img', [(i, i ^ 1) for i in range(size)])  2.26 us
    pallas_call x7, Pallas kernels, call(): pl.pallas_call(kernel, out_shape=outs, in_specs=[VMEM] * len(args), out_s...  1.96 us
    ppermute x6, waiting for transfers between devices, core_swap(): return lax.ppermute(block, 'img', [(i, i ^ 1) for i in range(size)])  1.9 us
    unnamed x5, local copies, waits for them, and re-layouts  0.78 us
  transfers between devices with their start and end apart: 13, of which 10 were waited for; matrix products, arithmetic and copies ran while one was open for 3% of the time, Pallas kernels for 2%

profile of v11, /device:TPU:0, one launch (start us, length us, event | category | flops | bytes accessed | tf_op | source)
XLA Modules:
  0.0 22.6 jit_solution(11718908230453324211)
XLA Ops:
  0.6 0.5 %collective-permute-start.1 = (bf16[16,1152]{1,0:T(8,128)(2,1)}, bf16[16,1152]{1,0:T(8,128)(2,1)S(1)}, u32[]{:S(2)}, u32[]{:S(2)}) collective-permute-start(bf16[16,1152]{1,0:T(8,128)(2,1)} %param.3), channel_id=1, source_target_pairs={{0,4},{4,0},{8,12},{12,8},{16,20},{20,16},{24,28},{28,24},{1,5},{5... | collective-permute-start | bytes 110600 | tf_op jit(solution)/shard_map/ppermute | solution.py:38
  1.2 0.8 %constant_dynamic-update-slice_fusion.1 = bf16[32,1152]{1,0:T(8,128)(2,1)S(1)} fusion(bf16[16,1152]{1,0:T(8,128)(2,1)} %param.4), kind=kLoop, calls=%fused_computation.1 | loop fusion | bytes 73728
  2.0 0.2 collective-permute-done.1.img_ref
  2.2 0.3 %collective-permute-done.txt_ref = bf16[16,1152]{1,0:T(8,128)(2,1)S(1)} collective-permute-done((bf16[16,1152]{1,0:T(8,128)(2,1)}, bf16[16,1152]{1,0:T(8,128)(2,1)S(1)}, u32[]{:S(2)}, u32[]{:S(2)}) %collective-permute-start) | collective-permute-done | bytes 36896 | tf_op jit(solution)/shard_map/ppermute | solution.py:38
  2.7 2.7 %collective-permute-start.3 = (bf16[32,1152]{1,0:T(8,128)(2,1)S(1)}, bf16[32,1152]{1,0:T(8,128)(2,1)S(1)}, u32[]{:S(2)}, u32[]{:S(2)}) collective-permute-start(bf16[32,1152]{1,0:T(8,128)(2,1)S(1)} %get-tuple-element.14.refs_0_), channel_id=1, source_target_pairs={{0,16},{1,17},{2,18},{3,19},{4,6},{5,7},{6,4},{7,5},{8,24},{9,25},... | collective-permute-start | bytes 221192 | tf_op jit(solution)/shard_map/ppermute | solution.py:50
  5.5 1.4 %collective-permute-start.2 = (bf16[32,1152]{1,0:T(8,128)(2,1)S(1)}, bf16[32,1152]{1,0:T(8,128)(2,1)S(1)}, u32[]{:S(2)}, u32[]{:S(2)}) collective-permute-start(bf16[32,1152]{1,0:T(8,128)(2,1)S(1)} %get-tuple-element.14.refs_0_), channel_id=1, source_target_pairs={{0,24},{1,25},{2,26},{3,27},{4,7},{5,6},{6,5},{7,4},{8,16},{9,17},... | collective-permute-start | bytes 221192 | tf_op jit(solution)/shard_map/ppermute | solution.py:50
  7.0 0.8 %collective-permute-done.3.refs_2_ = bf16[32,1152]{1,0:T(8,128)(2,1)S(1)} collective-permute-done((bf16[32,1152]{1,0:T(8,128)(2,1)S(1)}, bf16[32,1152]{1,0:T(8,128)(2,1)S(1)}, u32[]{:S(2)}, u32[]{:S(2)}) %collective-permute-start.3) | collective-permute-done | bytes 73760 | tf_op jit(solution)/shard_map/ppermute | solution.py:50
  7.8 0.5 %collective-permute-start.6 = (bf16[32,1152]{1,0:T(8,128)(2,1)S(1)}, bf16[32,1152]{1,0:T(8,128)(2,1)S(1)}, u32[]{:S(2)}, u32[]{:S(2)}) collective-permute-start(bf16[32,1152]{1,0:T(8,128)(2,1)S(1)} %collective-permute-done.3.refs_2_), channel_id=1, source_target_pairs={{0,4},{4,0},{8,12},{12,8},{16,20},{20,16},{24,28},{28,24},{1,5},{5... | collective-permute-start | bytes 221192 | tf_op jit(solution)/shard_map/ppermute | solution.py:38
  8.4 2.4 %collective-permute-done.2.refs_1_ = bf16[32,1152]{1,0:T(8,128)(2,1)S(1)} collective-permute-done((bf16[32,1152]{1,0:T(8,128)(2,1)S(1)}, bf16[32,1152]{1,0:T(8,128)(2,1)S(1)}, u32[]{:S(2)}, u32[]{:S(2)}) %collective-permute-start.2) | collective-permute-done | bytes 73760 | tf_op jit(solution)/shard_map/ppermute | solution.py:50
  10.7 1.0 %collective-permute-start.5 = (bf16[32,1152]{1,0:T(8,128)(2,1)S(1)}, bf16[32,1152]{1,0:T(8,128)(2,1)S(1)}, u32[]{:S(2)}, u32[]{:S(2)}) collective-permute-start(bf16[32,1152]{1,0:T(8,128)(2,1)S(1)} %collective-permute-done.2.refs_1_), channel_id=1, source_target_pairs={{0,4},{4,0},{8,12},{12,8},{16,20},{20,16},{24,28},{28,24},{1,5},{5... | collective-permute-start | bytes 221192 | tf_op jit(solution)/shard_map/ppermute | solution.py:38
  11.8 0.8 %collective-permute-done.5.refs_5_ = bf16[32,1152]{1,0:T(8,128)(2,1)S(1)} collective-permute-done((bf16[32,1152]{1,0:T(8,128)(2,1)S(1)}, bf16[32,1152]{1,0:T(8,128)(2,1)S(1)}, u32[]{:S(2)}, u32[]{:S(2)}) %collective-permute-start.5) | collective-permute-done | bytes 73760 | tf_op jit(solution)/shard_map/ppermute | solution.py:38
  12.6 0.2 %shard_map.51.most_ref = f32[128,96]{1,0:T(8,128)S(1)} custom-call(bf16[32,1152]{1,0:T(8,128)(2,1)S(1)} %get-tuple-element.14.refs_0_, bf16[32,1152]{1,0:T(8,128)(2,1)S(1)} %collective-permute-done.2.refs_1_, bf16[32,1152]{1,0:T(8,128)(2,1)S(1)} %collective-permute-done.3.refs_2_, bf16[32,1152]{1,0:T(8,128)(2,1)S(1)} %collective-permute-done.4.refs_3_.piece_ref, ...), custom_call_target="tpu_custom_call" | custom-call | flops 10000000000 | bytes 10000000 | tf_op jit(solution)/shard_map/pallas_call | solution.py:59
  12.8 0.2 collective-permute-done.7.refs_7_
  13.1 0.6 %shard_map.53 = (f32[32,1152]{1,0:T(8,128)S(1)}, bf16[16,1152]{1,0:T(8,128)(2,1)S(1)}, bf16[16,1152]{1,0:T(8,128)(2,1)S(1)}, bf16[32,1152]{1,0:T(8,128)(2,1)S(1)}, bf16[32,1152]{1,0:T(8,128)(2,1)S(1)}) custom-call(s32[1,64]{1,0:T(1,128)S(1)} %bitcast.2, f32[128,96]{1,0:T(8,128)S(1)} %shard_map.51.most_ref, bf16[32,1152]{1,0:T(8,128)(2,1)S(1)} %get-tuple-element.14.refs_0_, ...), custom_call_target="tpu_custom_call" | custom-call | tf_op jit(solution)/shard_map/pallas_call | solution.py:59
  13.7 2.5 %collective-permute-start.8 = (bf16[32,1152]{1,0:T(8,128)(2,1)S(1)}, bf16[32,1152]{1,0:T(8,128)(2,1)S(1)}, u32[]{:S(2)}, u32[]{:S(2)}) collective-permute-start(bf16[32,1152]{1,0:T(8,128)(2,1)S(1)} %get-tuple-element.17), channel_id=1, source_target_pairs={{0,24},{1,25},{2,26},{3,27},{4,7},{5,6},{6,5},{7,4},{8,16},{9,17},... | collective-permute-start | bytes 221192 | tf_op jit(solution)/shard_map/ppermute | solution.py:50
  16.2 0.5 %collective-permute-start.9 = (bf16[32,1152]{1,0:T(8,128)(2,1)S(1)}, bf16[32,1152]{1,0:T(8,128)(2,1)S(1)}, u32[]{:S(2)}, u32[]{:S(2)}) collective-permute-start(bf16[32,1152]{1,0:T(8,128)(2,1)S(1)} %get-tuple-element.18), channel_id=1, source_target_pairs={{0,8},{1,9},{2,10},{3,11},{4,5},{5,4},{6,7},{7,6},{8,0},{9,1},{10,... | collective-permute-start | bytes 221192 | tf_op jit(solution)/shard_map/ppermute | solution.py:50
  16.7 0.5 %collective-permute-start.10 = (bf16[16,1152]{1,0:T(8,128)(2,1)S(1)}, bf16[16,1152]{1,0:T(8,128)(2,1)S(1)}, u32[]{:S(2)}, u32[]{:S(2)}) collective-permute-start(bf16[16,1152]{1,0:T(8,128)(2,1)S(1)} %get-tuple-element.20), channel_id=1, source_target_pairs={{0,16},{1,17},{2,18},{3,19},{4,6},{5,7},{6,4},{7,5},{8,24},{9,25},... | collective-permute-start | bytes 110600 | tf_op jit(solution)/shard_map/ppermute | solution.py:50
  17.2 1.3 %collective-permute-start.11 = (bf16[16,1152]{1,0:T(8,128)(2,1)S(1)}, bf16[16,1152]{1,0:T(8,128)(2,1)S(1)}, u32[]{:S(2)}, u32[]{:S(2)}) collective-permute-start(bf16[16,1152]{1,0:T(8,128)(2,1)S(1)} %get-tuple-element.24), channel_id=1, source_target_pairs={{0,20},{1,21},{2,22},{3,23},{4,2},{5,3},{6,0},{7,1},{8,28},{9,29},... | collective-permute-start | bytes 110600 | tf_op jit(solution)/shard_map/ppermute | solution.py:50
  18.5 0.4 %collective-permute-done.8.refs_0_ = bf16[32,1152]{1,0:T(8,128)(2,1)S(1)} collective-permute-done((bf16[32,1152]{1,0:T(8,128)(2,1)S(1)}, bf16[32,1152]{1,0:T(8,128)(2,1)S(1)}, u32[]{:S(2)}, u32[]{:S(2)}) %collective-permute-start.8) | collective-permute-done | bytes 73760 | tf_op jit(solution)/shard_map/ppermute | solution.py:50
  19.0 1.5 %collective-permute-done.9.refs_1_ = bf16[32,1152]{1,0:T(8,128)(2,1)S(1)} collective-permute-done((bf16[32,1152]{1,0:T(8,128)(2,1)S(1)}, bf16[32,1152]{1,0:T(8,128)(2,1)S(1)}, u32[]{:S(2)}, u32[]{:S(2)}) %collective-permute-start.9) | collective-permute-done | bytes 73760 | tf_op jit(solution)/shard_map/ppermute | solution.py:50
  20.7 0.2 shard_map.55
  20.9 0.6 %collective-permute-done.11.cross_ref = bf16[16,1152]{1,0:T(8,128)(2,1)S(1)} collective-permute-done((bf16[16,1152]{1,0:T(8,128)(2,1)S(1)}, bf16[16,1152]{1,0:T(8,128)(2,1)S(1)}, u32[]{:S(2)}, u32[]{:S(2)}) %collective-permute-start.11) | collective-permute-done | bytes 36896 | tf_op jit(solution)/shard_map/ppermute | solution.py:50
  21.5 0.3 %collective-permute-done.12.got_ref = bf16[16,1152]{1,0:T(8,128)(2,1)S(1)} collective-permute-done((bf16[16,1152]{1,0:T(8,128)(2,1)S(1)}, bf16[16,1152]{1,0:T(8,128)(2,1)S(1)}, u32[]{:S(2)}, u32[]{:S(2)}) %collective-permute-start.12) | collective-permute-done | bytes 36896 | tf_op jit(solution)/shard_map/ppermute | solution.py:38
  21.8 0.8 %shard_map.56 = (f32[16,1152]{1,0:T(8,128)}, f32[16,1152]{1,0:T(8,128)}) custom-call(f32[16,1152]{1,0:T(8,128)S(1)} %get-tuple-element.21.grad_ref, f32[16,1152]{1,0:T(8,128)S(1)} %get-tuple-element.22.unit_ref, f32[16,1]{1,0:T(8,128)S(1)} %get-tuple-element.23.inverse_ref, bf16[16,1152]{1,0:T(8,128)(2,1)S(1)} %collective-permute-done.11.cross_ref, ...), custom_call_target="tpu_custom_call" | custom-call | tf_op jit(solution)/shard_map/pallas_call | solution.py:59
  (15 shorter events, 0.6 us)
Async XLA Ops:
  0.6 1.4 %copy-start.1 = (bf16[16,1152]{1,0:T(8,128)(2,1)S(1)}, bf16[16,1152]{1,0:T(8,128)(2,1)}, u32[]{:S(2)}) copy-start(bf16[16,1152]{1,0:T(8,128)(2,1)} %param.3) | copy-start | bytes 110596
  0.6 1.6 %collective-permute-start.1 = (bf16[16,1152]{1,0:T(8,128)(2,1)}, bf16[16,1152]{1,0:T(8,128)(2,1)S(1)}, u32[]{:S(2)}, u32[]{:S(2)}) collective-permute-start(bf16[16,1152]{1,0:T(8,128)(2,1)} %param.3), channel_id=1, source_target_pairs={{0,4},{4,0},{8,12},{12,8},{16,20},{20,16},{24,28},{28,24},{1,5},{5... | collective-permute-start | bytes 110600 | tf_op jit(solution)/shard_map/ppermute | solution.py:38
  1.2 1.4 %collective-permute-start = (bf16[16,1152]{1,0:T(8,128)(2,1)}, bf16[16,1152]{1,0:T(8,128)(2,1)S(1)}, u32[]{:S(2)}, u32[]{:S(2)}) collective-permute-start(bf16[16,1152]{1,0:T(8,128)(2,1)} %param.4), channel_id=1, source_target_pairs={{0,4},{4,0},{8,12},{12,8},{16,20},{20,16},{24,28},{28,24},{1,5},{5... | collective-permute-start | bytes 110600 | tf_op jit(solution)/shard_map/ppermute | solution.py:38
  2.7 9.0 %copy-start = (s32[64]{0:T(128)S(1)}, s32[64]{0:T(128)}, u32[]{:S(2)}) copy-start(s32[64]{0:T(128)} %param.5) | copy-start | bytes 772
  2.7 5.1 %collective-permute-start.3 = (bf16[32,1152]{1,0:T(8,128)(2,1)S(1)}, bf16[32,1152]{1,0:T(8,128)(2,1)S(1)}, u32[]{:S(2)}, u32[]{:S(2)}) collective-permute-start(bf16[32,1152]{1,0:T(8,128)(2,1)S(1)} %get-tuple-element.14.refs_0_), channel_id=1, source_target_pairs={{0,16},{1,17},{2,18},{3,19},{4,6},{5,7},{6,4},{7,5},{8,24},{9,25},... | collective-permute-start | bytes 221192 | tf_op jit(solution)/shard_map/ppermute | solution.py:50
  5.5 5.3 %collective-permute-start.2 = (bf16[32,1152]{1,0:T(8,128)(2,1)S(1)}, bf16[32,1152]{1,0:T(8,128)(2,1)S(1)}, u32[]{:S(2)}, u32[]{:S(2)}) collective-permute-start(bf16[32,1152]{1,0:T(8,128)(2,1)S(1)} %get-tuple-element.14.refs_0_), channel_id=1, source_target_pairs={{0,24},{1,25},{2,26},{3,27},{4,7},{5,6},{6,5},{7,4},{8,16},{9,17},... | collective-permute-start | bytes 221192 | tf_op jit(solution)/shard_map/ppermute | solution.py:50
  6.9 4.8 %collective-permute-start.4 = (bf16[32,1152]{1,0:T(8,128)(2,1)S(1)}, bf16[32,1152]{1,0:T(8,128)(2,1)S(1)}, u32[]{:S(2)}, u32[]{:S(2)}) collective-permute-start(bf16[32,1152]{1,0:T(8,128)(2,1)S(1)} %get-tuple-element.14.refs_0_), channel_id=1, source_target_pairs={{0,8},{1,9},{2,10},{3,11},{4,5},{5,4},{6,7},{7,6},{8,0},{9,1},{10,... | collective-permute-start | bytes 221192 | tf_op jit(solution)/shard_map/ppermute | solution.py:50
  7.8 4.0 %collective-permute-start.6 = (bf16[32,1152]{1,0:T(8,128)(2,1)S(1)}, bf16[32,1152]{1,0:T(8,128)(2,1)S(1)}, u32[]{:S(2)}, u32[]{:S(2)}) collective-permute-start(bf16[32,1152]{1,0:T(8,128)(2,1)S(1)} %collective-permute-done.3.refs_2_), channel_id=1, source_target_pairs={{0,4},{4,0},{8,12},{12,8},{16,20},{20,16},{24,28},{28,24},{1,5},{5... | collective-permute-start | bytes 221192 | tf_op jit(solution)/shard_map/ppermute | solution.py:38
  10.7 1.9 %collective-permute-start.5 = (bf16[32,1152]{1,0:T(8,128)(2,1)S(1)}, bf16[32,1152]{1,0:T(8,128)(2,1)S(1)}, u32[]{:S(2)}, u32[]{:S(2)}) collective-permute-start(bf16[32,1152]{1,0:T(8,128)(2,1)S(1)} %collective-permute-done.2.refs_1_), channel_id=1, source_target_pairs={{0,4},{4,0},{8,12},{12,8},{16,20},{20,16},{24,28},{28,24},{1,5},{5... | collective-permute-start | bytes 221192 | tf_op jit(solution)/shard_map/ppermute | solution.py:38
  11.7 1.3 %collective-permute-start.7 = (bf16[304,128]{1,0:T(8,128)(2,1)S(1)}, bf16[304,128]{1,0:T(8,128)(2,1)S(1)}, u32[]{:S(2)}, u32[]{:S(2)}) collective-permute-start(bf16[304,128]{1,0:T(8,128)(2,1)S(1)} %shard_map.52), channel_id=1, source_target_pairs={{0,4},{4,0},{8,12},{12,8},{16,20},{20,16},{24,28},{28,24},{1,5},{5... | collective-permute-start | bytes 233480 | tf_op jit(solution)/shard_map/ppermute | solution.py:38
  13.7 5.3 %collective-permute-start.8 = (bf16[32,1152]{1,0:T(8,128)(2,1)S(1)}, bf16[32,1152]{1,0:T(8,128)(2,1)S(1)}, u32[]{:S(2)}, u32[]{:S(2)}) collective-permute-start(bf16[32,1152]{1,0:T(8,128)(2,1)S(1)} %get-tuple-element.17), channel_id=1, source_target_pairs={{0,24},{1,25},{2,26},{3,27},{4,7},{5,6},{6,5},{7,4},{8,16},{9,17},... | collective-permute-start | bytes 221192 | tf_op jit(solution)/shard_map/ppermute | solution.py:50
  16.2 4.4 %collective-permute-start.9 = (bf16[32,1152]{1,0:T(8,128)(2,1)S(1)}, bf16[32,1152]{1,0:T(8,128)(2,1)S(1)}, u32[]{:S(2)}, u32[]{:S(2)}) collective-permute-start(bf16[32,1152]{1,0:T(8,128)(2,1)S(1)} %get-tuple-element.18), channel_id=1, source_target_pairs={{0,8},{1,9},{2,10},{3,11},{4,5},{5,4},{6,7},{7,6},{8,0},{9,1},{10,... | collective-permute-start | bytes 221192 | tf_op jit(solution)/shard_map/ppermute | solution.py:50
  16.7 4.0 %collective-permute-start.10 = (bf16[16,1152]{1,0:T(8,128)(2,1)S(1)}, bf16[16,1152]{1,0:T(8,128)(2,1)S(1)}, u32[]{:S(2)}, u32[]{:S(2)}) collective-permute-start(bf16[16,1152]{1,0:T(8,128)(2,1)S(1)} %get-tuple-element.20), channel_id=1, source_target_pairs={{0,16},{1,17},{2,18},{3,19},{4,6},{5,7},{6,4},{7,5},{8,24},{9,25},... | collective-permute-start | bytes 110600 | tf_op jit(solution)/shard_map/ppermute | solution.py:50
  17.2 4.3 %collective-permute-start.11 = (bf16[16,1152]{1,0:T(8,128)(2,1)S(1)}, bf16[16,1152]{1,0:T(8,128)(2,1)S(1)}, u32[]{:S(2)}, u32[]{:S(2)}) collective-permute-start(bf16[16,1152]{1,0:T(8,128)(2,1)S(1)} %get-tuple-element.24), channel_id=1, source_target_pairs={{0,20},{1,21},{2,22},{3,23},{4,2},{5,3},{6,0},{7,1},{8,28},{9,29},... | collective-permute-start | bytes 110600 | tf_op jit(solution)/shard_map/ppermute | solution.py:50
  20.6 1.3 %collective-permute-start.12 = (bf16[16,1152]{1,0:T(8,128)(2,1)S(1)}, bf16[16,1152]{1,0:T(8,128)(2,1)S(1)}, u32[]{:S(2)}, u32[]{:S(2)}) collective-permute-start(bf16[16,1152]{1,0:T(8,128)(2,1)S(1)} %get-tuple-element.25), channel_id=1, source_target_pairs={{0,4},{4,0},{8,12},{12,8},{16,20},{20,16},{24,28},{28,24},{1,5},{5... | collective-permute-start | bytes 110600 | tf_op jit(solution)/shard_map/ppermute | solution.py:38

commit v12 on v11

--- a/solution.py
+++ b/solution.py
@@ -224,7 +224,7 @@
         [*mine, *other[:-1]],
         cost=LONG,
     )
-    split = min(2, blocks - 1)
+    split = blocks - 1
     own, same, cross, *send = call(
         functools.partial(rest_kernel, blocks, split),
         [total] + [piece] * 2 + [pair] * (blocks - 2),

time: 22.8 us -> 22.9 us (level)
  starting transfers between devices: 11.4 us -> 11.9 us
  waiting for transfers between devices: 7.7 us -> 7.39 us
    ppermute x7, waiting for transfers between devices: 5.8 us -> 5.27 us  [chip_swap(): return lax.ppermute(block, ('img', 'txt'), pairs)]
    ppermute x6, starting transfers between devices: 2.26 us -> 2.71 us  [core_swap(): return lax.ppermute(block, 'img', [(i, i ^ 1) for i in range(size)])]
where the time goes in v12:
time: 22.9 us; the launch traced here: 22.7 us
  starting transfers between devices  11.9 us (52%)
  waiting for transfers between devices  7.39 us (32%)
  Pallas kernels  1.96 us (9%)
  local copies, waits for them, and re-layouts  0.79 us (3%)
  between operations  0.7 us (3%)
    ppermute x7, starting transfers between devices, chip_swap(): return lax.ppermute(block, ('img', 'txt'), pairs)  9.15 us
    ppermute x7, waiting for transfers between devices, chip_swap(): return lax.ppermute(block, ('img', 'txt'), pairs)  5.27 us
    ppermute x6, starting transfers between devices, core_swap(): return lax.ppermute(block, 'img', [(i, i ^ 1) for i in range(size)])  2.71 us
    ppermute x6, waiting for transfers between devices, core_swap(): return lax.ppermute(block, 'img', [(i, i ^ 1) for i in range(size)])  2.12 us
    pallas_call x7, Pallas kernels, call(): pl.pallas_call(kernel, out_shape=outs, in_specs=[VMEM] * len(args), out_s...  1.96 us
    unnamed x5, local copies, waits for them, and re-layouts  0.78 us
  transfers between devices with their start and end apart: 13, of which 10 were waited for; matrix products, arithmetic and copies ran while one was open for 3% of the time, Pallas kernels for 2%

profile of v12, /device:TPU:0, one launch (start us, length us, event | category | flops | bytes accessed | tf_op | source)
XLA Modules:
  0.0 22.7 jit_solution(10544899120739731965)
XLA Ops:
  0.6 0.5 %collective-permute-start.1 = (bf16[16,1152]{1,0:T(8,128)(2,1)}, bf16[16,1152]{1,0:T(8,128)(2,1)S(1)}, u32[]{:S(2)}, u32[]{:S(2)}) collective-permute-start(bf16[16,1152]{1,0:T(8,128)(2,1)} %param.3), channel_id=1, source_target_pairs={{0,4},{4,0},{8,12},{12,8},{16,20},{20,16},{24,28},{28,24},{1,5},{5... | collective-permute-start | bytes 110600 | tf_op jit(solution)/shard_map/ppermute | solution.py:38
  1.2 0.8 %constant_dynamic-update-slice_fusion.1 = bf16[32,1152]{1,0:T(8,128)(2,1)S(1)} fusion(bf16[16,1152]{1,0:T(8,128)(2,1)} %param.4), kind=kLoop, calls=%fused_computation.1 | loop fusion | bytes 73728
  2.0 0.2 collective-permute-done.1.img_ref
  2.2 0.3 %collective-permute-done.txt_ref = bf16[16,1152]{1,0:T(8,128)(2,1)S(1)} collective-permute-done((bf16[16,1152]{1,0:T(8,128)(2,1)}, bf16[16,1152]{1,0:T(8,128)(2,1)S(1)}, u32[]{:S(2)}, u32[]{:S(2)}) %collective-permute-start) | collective-permute-done | bytes 36896 | tf_op jit(solution)/shard_map/ppermute | solution.py:38
  2.7 2.7 %collective-permute-start.3 = (bf16[32,1152]{1,0:T(8,128)(2,1)S(1)}, bf16[32,1152]{1,0:T(8,128)(2,1)S(1)}, u32[]{:S(2)}, u32[]{:S(2)}) collective-permute-start(bf16[32,1152]{1,0:T(8,128)(2,1)S(1)} %get-tuple-element.14.refs_0_), channel_id=1, source_target_pairs={{0,16},{1,17},{2,18},{3,19},{4,6},{5,7},{6,4},{7,5},{8,24},{9,25},... | collective-permute-start | bytes 221192 | tf_op jit(solution)/shard_map/ppermute | solution.py:50
  5.5 1.4 %collective-permute-start.2 = (bf16[32,1152]{1,0:T(8,128)(2,1)S(1)}, bf16[32,1152]{1,0:T(8,128)(2,1)S(1)}, u32[]{:S(2)}, u32[]{:S(2)}) collective-permute-start(bf16[32,1152]{1,0:T(8,128)(2,1)S(1)} %get-tuple-element.14.refs_0_), channel_id=1, source_target_pairs={{0,24},{1,25},{2,26},{3,27},{4,7},{5,6},{6,5},{7,4},{8,16},{9,17},... | collective-permute-start | bytes 221192 | tf_op jit(solution)/shard_map/ppermute | solution.py:50
  7.0 0.8 %collective-permute-done.3.refs_2_ = bf16[32,1152]{1,0:T(8,128)(2,1)S(1)} collective-permute-done((bf16[32,1152]{1,0:T(8,128)(2,1)S(1)}, bf16[32,1152]{1,0:T(8,128)(2,1)S(1)}, u32[]{:S(2)}, u32[]{:S(2)}) %collective-permute-start.3) | collective-permute-done | bytes 73760 | tf_op jit(solution)/shard_map/ppermute | solution.py:50
  7.8 0.5 %collective-permute-start.6 = (bf16[32,1152]{1,0:T(8,128)(2,1)S(1)}, bf16[32,1152]{1,0:T(8,128)(2,1)S(1)}, u32[]{:S(2)}, u32[]{:S(2)}) collective-permute-start(bf16[32,1152]{1,0:T(8,128)(2,1)S(1)} %collective-permute-done.3.refs_2_), channel_id=1, source_target_pairs={{0,4},{4,0},{8,12},{12,8},{16,20},{20,16},{24,28},{28,24},{1,5},{5... | collective-permute-start | bytes 221192 | tf_op jit(solution)/shard_map/ppermute | solution.py:38
  8.4 2.4 %collective-permute-done.2.refs_1_ = bf16[32,1152]{1,0:T(8,128)(2,1)S(1)} collective-permute-done((bf16[32,1152]{1,0:T(8,128)(2,1)S(1)}, bf16[32,1152]{1,0:T(8,128)(2,1)S(1)}, u32[]{:S(2)}, u32[]{:S(2)}) %collective-permute-start.2) | collective-permute-done | bytes 73760 | tf_op jit(solution)/shard_map/ppermute | solution.py:50
  10.7 1.0 %collective-permute-start.5 = (bf16[32,1152]{1,0:T(8,128)(2,1)S(1)}, bf16[32,1152]{1,0:T(8,128)(2,1)S(1)}, u32[]{:S(2)}, u32[]{:S(2)}) collective-permute-start(bf16[32,1152]{1,0:T(8,128)(2,1)S(1)} %collective-permute-done.2.refs_1_), channel_id=1, source_target_pairs={{0,4},{4,0},{8,12},{12,8},{16,20},{20,16},{24,28},{28,24},{1,5},{5... | collective-permute-start | bytes 221192 | tf_op jit(solution)/shard_map/ppermute | solution.py:38
  11.8 0.8 %collective-permute-done.5.refs_5_ = bf16[32,1152]{1,0:T(8,128)(2,1)S(1)} collective-permute-done((bf16[32,1152]{1,0:T(8,128)(2,1)S(1)}, bf16[32,1152]{1,0:T(8,128)(2,1)S(1)}, u32[]{:S(2)}, u32[]{:S(2)}) %collective-permute-start.5) | collective-permute-done | bytes 73760 | tf_op jit(solution)/shard_map/ppermute | solution.py:38
  12.6 0.2 %shard_map.51.most_ref = f32[128,96]{1,0:T(8,128)S(1)} custom-call(bf16[32,1152]{1,0:T(8,128)(2,1)S(1)} %get-tuple-element.14.refs_0_, bf16[32,1152]{1,0:T(8,128)(2,1)S(1)} %collective-permute-done.2.refs_1_, bf16[32,1152]{1,0:T(8,128)(2,1)S(1)} %collective-permute-done.3.refs_2_, bf16[32,1152]{1,0:T(8,128)(2,1)S(1)} %collective-permute-done.4.refs_3_.piece_ref, ...), custom_call_target="tpu_custom_call" | custom-call | flops 10000000000 | bytes 10000000 | tf_op jit(solution)/shard_map/pallas_call | solution.py:59
  12.8 0.2 collective-permute-done.7.refs_7_
  13.1 0.6 %shard_map.53 = (f32[32,1152]{1,0:T(8,128)S(1)}, bf16[16,1152]{1,0:T(8,128)(2,1)S(1)}, bf16[16,1152]{1,0:T(8,128)(2,1)S(1)}, bf16[32,1152]{1,0:T(8,128)(2,1)S(1)}, bf16[32,1152]{1,0:T(8,128)(2,1)S(1)}) custom-call(s32[1,64]{1,0:T(1,128)S(1)} %bitcast.2, f32[128,96]{1,0:T(8,128)S(1)} %shard_map.51.most_ref, bf16[32,1152]{1,0:T(8,128)(2,1)S(1)} %get-tuple-element.14.refs_0_, ...), custom_call_target="tpu_custom_call" | custom-call | tf_op jit(solution)/shard_map/pallas_call | solution.py:59
  13.7 2.5 %collective-permute-start.8 = (bf16[32,1152]{1,0:T(8,128)(2,1)S(1)}, bf16[32,1152]{1,0:T(8,128)(2,1)S(1)}, u32[]{:S(2)}, u32[]{:S(2)}) collective-permute-start(bf16[32,1152]{1,0:T(8,128)(2,1)S(1)} %get-tuple-element.17), channel_id=1, source_target_pairs={{0,24},{1,25},{2,26},{3,27},{4,7},{5,6},{6,5},{7,4},{8,16},{9,17},... | collective-permute-start | bytes 221192 | tf_op jit(solution)/shard_map/ppermute | solution.py:50
  16.2 0.5 %collective-permute-start.9 = (bf16[32,1152]{1,0:T(8,128)(2,1)S(1)}, bf16[32,1152]{1,0:T(8,128)(2,1)S(1)}, u32[]{:S(2)}, u32[]{:S(2)}) collective-permute-start(bf16[32,1152]{1,0:T(8,128)(2,1)S(1)} %get-tuple-element.18), channel_id=1, source_target_pairs={{0,16},{1,17},{2,18},{3,19},{4,6},{5,7},{6,4},{7,5},{8,24},{9,25},... | collective-permute-start | bytes 221192 | tf_op jit(solution)/shard_map/ppermute | solution.py:50
  16.7 0.5 %collective-permute-start.10 = (bf16[16,1152]{1,0:T(8,128)(2,1)S(1)}, bf16[16,1152]{1,0:T(8,128)(2,1)S(1)}, u32[]{:S(2)}, u32[]{:S(2)}) collective-permute-start(bf16[16,1152]{1,0:T(8,128)(2,1)S(1)} %get-tuple-element.20), channel_id=1, source_target_pairs={{0,8},{1,9},{2,10},{3,11},{4,5},{5,4},{6,7},{7,6},{8,0},{9,1},{10,... | collective-permute-start | bytes 110600 | tf_op jit(solution)/shard_map/ppermute | solution.py:50
  17.2 1.3 %collective-permute-start.11 = (bf16[16,1152]{1,0:T(8,128)(2,1)S(1)}, bf16[16,1152]{1,0:T(8,128)(2,1)S(1)}, u32[]{:S(2)}, u32[]{:S(2)}) collective-permute-start(bf16[16,1152]{1,0:T(8,128)(2,1)S(1)} %get-tuple-element.24), channel_id=1, source_target_pairs={{0,12},{1,13},{2,14},{3,15},{4,1},{5,0},{6,3},{7,2},{8,4},{9,5},{1... | collective-permute-start | bytes 110600 | tf_op jit(solution)/shard_map/ppermute | solution.py:50
  18.5 0.5 %collective-permute-done.8.refs_0_ = bf16[32,1152]{1,0:T(8,128)(2,1)S(1)} collective-permute-done((bf16[32,1152]{1,0:T(8,128)(2,1)S(1)}, bf16[32,1152]{1,0:T(8,128)(2,1)S(1)}, u32[]{:S(2)}, u32[]{:S(2)}) %collective-permute-start.8) | collective-permute-done | bytes 73760 | tf_op jit(solution)/shard_map/ppermute | solution.py:50
  19.0 1.5 %collective-permute-done.9.refs_1_ = bf16[32,1152]{1,0:T(8,128)(2,1)S(1)} collective-permute-done((bf16[32,1152]{1,0:T(8,128)(2,1)S(1)}, bf16[32,1152]{1,0:T(8,128)(2,1)S(1)}, u32[]{:S(2)}, u32[]{:S(2)}) %collective-permute-start.9) | collective-permute-done | bytes 73760 | tf_op jit(solution)/shard_map/ppermute | solution.py:50
  20.6 0.5 %collective-permute-start.12 = (bf16[16,1152]{1,0:T(8,128)(2,1)S(1)}, bf16[16,1152]{1,0:T(8,128)(2,1)S(1)}, u32[]{:S(2)}, u32[]{:S(2)}) collective-permute-start(bf16[16,1152]{1,0:T(8,128)(2,1)S(1)} %get-tuple-element.25), channel_id=1, source_target_pairs={{0,4},{4,0},{8,12},{12,8},{16,20},{20,16},{24,28},{28,24},{1,5},{5... | collective-permute-start | bytes 110600 | tf_op jit(solution)/shard_map/ppermute | solution.py:38
  21.1 0.2 shard_map.55
  21.4 0.6 %collective-permute-done.12.got_ref = bf16[16,1152]{1,0:T(8,128)(2,1)S(1)} collective-permute-done((bf16[16,1152]{1,0:T(8,128)(2,1)S(1)}, bf16[16,1152]{1,0:T(8,128)(2,1)S(1)}, u32[]{:S(2)}, u32[]{:S(2)}) %collective-permute-start.12) | collective-permute-done | bytes 36896 | tf_op jit(solution)/shard_map/ppermute | solution.py:38
  21.9 0.8 %shard_map.56 = (f32[16,1152]{1,0:T(8,128)}, f32[16,1152]{1,0:T(8,128)}) custom-call(f32[16,1152]{1,0:T(8,128)S(1)} %get-tuple-element.21.grad_ref, f32[16,1152]{1,0:T(8,128)S(1)} %get-tuple-element.22.unit_ref, f32[16,1]{1,0:T(8,128)S(1)} %get-tuple-element.23.inverse_ref, bf16[16,1152]{1,0:T(8,128)(2,1)S(1)} %collective-permute-done.11.cross_ref, ...), custom_call_target="tpu_custom_call" | custom-call | tf_op jit(solution)/shard_map/pallas_call | solution.py:59
  (15 shorter events, 0.6 us)
Async XLA Ops:
  0.6 1.4 %copy-start.1 = (bf16[16,1152]{1,0:T(8,128)(2,1)S(1)}, bf16[16,1152]{1,0:T(8,128)(2,1)}, u32[]{:S(2)}) copy-start(bf16[16,1152]{1,0:T(8,128)(2,1)} %param.3) | copy-start | bytes 110596
  0.6 1.6 %collective-permute-start.1 = (bf16[16,1152]{1,0:T(8,128)(2,1)}, bf16[16,1152]{1,0:T(8,128)(2,1)S(1)}, u32[]{:S(2)}, u32[]{:S(2)}) collective-permute-start(bf16[16,1152]{1,0:T(8,128)(2,1)} %param.3), channel_id=1, source_target_pairs={{0,4},{4,0},{8,12},{12,8},{16,20},{20,16},{24,28},{28,24},{1,5},{5... | collective-permute-start | bytes 110600 | tf_op jit(solution)/shard_map/ppermute | solution.py:38
  1.2 1.4 %collective-permute-start = (bf16[16,1152]{1,0:T(8,128)(2,1)}, bf16[16,1152]{1,0:T(8,128)(2,1)S(1)}, u32[]{:S(2)}, u32[]{:S(2)}) collective-permute-start(bf16[16,1152]{1,0:T(8,128)(2,1)} %param.4), channel_id=1, source_target_pairs={{0,4},{4,0},{8,12},{12,8},{16,20},{20,16},{24,28},{28,24},{1,5},{5... | collective-permute-start | bytes 110600 | tf_op jit(solution)/shard_map/ppermute | solution.py:38
  2.7 9.0 %copy-start = (s32[64]{0:T(128)S(1)}, s32[64]{0:T(128)}, u32[]{:S(2)}) copy-start(s32[64]{0:T(128)} %param.5) | copy-start | bytes 772
  2.7 5.1 %collective-permute-start.3 = (bf16[32,1152]{1,0:T(8,128)(2,1)S(1)}, bf16[32,1152]{1,0:T(8,128)(2,1)S(1)}, u32[]{:S(2)}, u32[]{:S(2)}) collective-permute-start(bf16[32,1152]{1,0:T(8,128)(2,1)S(1)} %get-tuple-element.14.refs_0_), channel_id=1, source_target_pairs={{0,16},{1,17},{2,18},{3,19},{4,6},{5,7},{6,4},{7,5},{8,24},{9,25},... | collective-permute-start | bytes 221192 | tf_op jit(solution)/shard_map/ppermute | solution.py:50
  5.5 5.3 %collective-permute-start.2 = (bf16[32,1152]{1,0:T(8,128)(2,1)S(1)}, bf16[32,1152]{1,0:T(8,128)(2,1)S(1)}, u32[]{:S(2)}, u32[]{:S(2)}) collective-permute-start(bf16[32,1152]{1,0:T(8,128)(2,1)S(1)} %get-tuple-element.14.refs_0_), channel_id=1, source_target_pairs={{0,24},{1,25},{2,26},{3,27},{4,7},{5,6},{6,5},{7,4},{8,16},{9,17},... | collective-permute-start | bytes 221192 | tf_op jit(solution)/shard_map/ppermute | solution.py:50
  6.9 4.8 %collective-permute-start.4 = (bf16[32,1152]{1,0:T(8,128)(2,1)S(1)}, bf16[32,1152]{1,0:T(8,128)(2,1)S(1)}, u32[]{:S(2)}, u32[]{:S(2)}) collective-permute-start(bf16[32,1152]{1,0:T(8,128)(2,1)S(1)} %get-tuple-element.14.refs_0_), channel_id=1, source_target_pairs={{0,8},{1,9},{2,10},{3,11},{4,5},{5,4},{6,7},{7,6},{8,0},{9,1},{10,... | collective-permute-start | bytes 221192 | tf_op jit(solution)/shard_map/ppermute | solution.py:50
  7.8 4.0 %collective-permute-start.6 = (bf16[32,1152]{1,0:T(8,128)(2,1)S(1)}, bf16[32,1152]{1,0:T(8,128)(2,1)S(1)}, u32[]{:S(2)}, u32[]{:S(2)}) collective-permute-start(bf16[32,1152]{1,0:T(8,128)(2,1)S(1)} %collective-permute-done.3.refs_2_), channel_id=1, source_target_pairs={{0,4},{4,0},{8,12},{12,8},{16,20},{20,16},{24,28},{28,24},{1,5},{5... | collective-permute-start | bytes 221192 | tf_op jit(solution)/shard_map/ppermute | solution.py:38
  10.7 1.9 %collective-permute-start.5 = (bf16[32,1152]{1,0:T(8,128)(2,1)S(1)}, bf16[32,1152]{1,0:T(8,128)(2,1)S(1)}, u32[]{:S(2)}, u32[]{:S(2)}) collective-permute-start(bf16[32,1152]{1,0:T(8,128)(2,1)S(1)} %collective-permute-done.2.refs_1_), channel_id=1, source_target_pairs={{0,4},{4,0},{8,12},{12,8},{16,20},{20,16},{24,28},{28,24},{1,5},{5... | collective-permute-start | bytes 221192 | tf_op jit(solution)/shard_map/ppermute | solution.py:38
  11.7 1.3 %collective-permute-start.7 = (bf16[304,128]{1,0:T(8,128)(2,1)S(1)}, bf16[304,128]{1,0:T(8,128)(2,1)S(1)}, u32[]{:S(2)}, u32[]{:S(2)}) collective-permute-start(bf16[304,128]{1,0:T(8,128)(2,1)S(1)} %shard_map.52), channel_id=1, source_target_pairs={{0,4},{4,0},{8,12},{12,8},{16,20},{20,16},{24,28},{28,24},{1,5},{5... | collective-permute-start | bytes 233480 | tf_op jit(solution)/shard_map/ppermute | solution.py:38
  13.7 5.3 %collective-permute-start.8 = (bf16[32,1152]{1,0:T(8,128)(2,1)S(1)}, bf16[32,1152]{1,0:T(8,128)(2,1)S(1)}, u32[]{:S(2)}, u32[]{:S(2)}) collective-permute-start(bf16[32,1152]{1,0:T(8,128)(2,1)S(1)} %get-tuple-element.17), channel_id=1, source_target_pairs={{0,24},{1,25},{2,26},{3,27},{4,7},{5,6},{6,5},{7,4},{8,16},{9,17},... | collective-permute-start | bytes 221192 | tf_op jit(solution)/shard_map/ppermute | solution.py:50
  16.2 4.4 %collective-permute-start.9 = (bf16[32,1152]{1,0:T(8,128)(2,1)S(1)}, bf16[32,1152]{1,0:T(8,128)(2,1)S(1)}, u32[]{:S(2)}, u32[]{:S(2)}) collective-permute-start(bf16[32,1152]{1,0:T(8,128)(2,1)S(1)} %get-tuple-element.18), channel_id=1, source_target_pairs={{0,16},{1,17},{2,18},{3,19},{4,6},{5,7},{6,4},{7,5},{8,24},{9,25},... | collective-permute-start | bytes 221192 | tf_op jit(solution)/shard_map/ppermute | solution.py:50
  16.7 4.4 %collective-permute-start.10 = (bf16[16,1152]{1,0:T(8,128)(2,1)S(1)}, bf16[16,1152]{1,0:T(8,128)(2,1)S(1)}, u32[]{:S(2)}, u32[]{:S(2)}) collective-permute-start(bf16[16,1152]{1,0:T(8,128)(2,1)S(1)} %get-tuple-element.20), channel_id=1, source_target_pairs={{0,8},{1,9},{2,10},{3,11},{4,5},{5,4},{6,7},{7,6},{8,0},{9,1},{10,... | collective-permute-start | bytes 110600 | tf_op jit(solution)/shard_map/ppermute | solution.py:50
  17.2 4.2 %collective-permute-start.11 = (bf16[16,1152]{1,0:T(8,128)(2,1)S(1)}, bf16[16,1152]{1,0:T(8,128)(2,1)S(1)}, u32[]{:S(2)}, u32[]{:S(2)}) collective-permute-start(bf16[16,1152]{1,0:T(8,128)(2,1)S(1)} %get-tuple-element.24), channel_id=1, source_target_pairs={{0,12},{1,13},{2,14},{3,15},{4,1},{5,0},{6,3},{7,2},{8,4},{9,5},{1... | collective-permute-start | bytes 110600 | tf_op jit(solution)/shard_map/ppermute | solution.py:50
  20.6 1.4 %collective-permute-start.12 = (bf16[16,1152]{1,0:T(8,128)(2,1)S(1)}, bf16[16,1152]{1,0:T(8,128)(2,1)S(1)}, u32[]{:S(2)}, u32[]{:S(2)}) collective-permute-start(bf16[16,1152]{1,0:T(8,128)(2,1)S(1)} %get-tuple-element.25), channel_id=1, source_target_pairs={{0,4},{4,0},{8,12},{12,8},{16,20},{20,16},{24,28},{28,24},{1,5},{5... | collective-permute-start | bytes 110600 | tf_op jit(solution)/shard_map/ppermute | solution.py:38

commit v13 on v11

--- a/solution.py
+++ b/solution.py
@@ -231,7 +231,7 @@
         [ids, most, *mine, *other],
     )
     far = order.pop(split - 1)
-    got = [chip_swap(block, k) for k, block in zip(order, send)]
+    got = [chip_swap(block, k) for k, block in zip(order, send)][::-1]
     same = chip_swap(same, far)
     cross = chip_swap(cross, far, cross=1)
     keep, send = call(sum_kernel, [single, piece], [own, *got])

time: 22.8 us -> 22.7 us (level)
  waiting for transfers between devices: 7.7 us -> 8.04 us
  starting transfers between devices: 11.4 us -> 11.1 us
    ppermute x7, waiting for transfers between devices: 5.8 us -> 6.28 us  [chip_swap(): return lax.ppermute(block, ('img', 'txt'), pairs)]
    ppermute x7, starting transfers between devices: 9.18 us -> 8.79 us  [chip_swap(): return lax.ppermute(block, ('img', 'txt'), pairs)]
where the time goes in v13:
time: 22.7 us; the launch traced here: 22.6 us
  starting transfers between devices  11.1 us (49%)
  waiting for transfers between devices  8.04 us (35%)
  Pallas kernels  1.96 us (9%)
  local copies, waits for them, and re-layouts  0.79 us (3%)
  between operations  0.71 us (3%)
    ppermute x7, starting transfers between devices, chip_swap(): return lax.ppermute(block, ('img', 'txt'), pairs)  8.79 us
    ppermute x7, waiting for transfers between devices, chip_swap(): return lax.ppermute(block, ('img', 'txt'), pairs)  6.28 us
    ppermute x6, starting transfers between devices, core_swap(): return lax.ppermute(block, 'img', [(i, i ^ 1) for i in range(size)])  2.26 us
    pallas_call x7, Pallas kernels, call(): pl.pallas_call(kernel, out_shape=outs, in_specs=[VMEM] * len(args), out_s...  1.96 us
    ppermute x6, waiting for transfers between devices, core_swap(): return lax.ppermute(block, 'img', [(i, i ^ 1) for i in range(size)])  1.76 us
    unnamed x5, local copies, waits for them, and re-layouts  0.78 us
  transfers between devices with their start and end apart: 13, of which 10 were waited for; matrix products, arithmetic and copies ran while one was open for 3% of the time, Pallas kernels for 2%

profile of v13, /device:TPU:0, one launch (start us, length us, event | category | flops | bytes accessed | tf_op | source)
XLA Modules:
  0.0 22.6 jit_solution(6752662612105059583)
XLA Ops:
  0.6 0.5 %collective-permute-start.1 = (bf16[16,1152]{1,0:T(8,128)(2,1)}, bf16[16,1152]{1,0:T(8,128)(2,1)S(1)}, u32[]{:S(2)}, u32[]{:S(2)}) collective-permute-start(bf16[16,1152]{1,0:T(8,128)(2,1)} %param.3), channel_id=1, source_target_pairs={{0,4},{4,0},{8,12},{12,8},{16,20},{20,16},{24,28},{28,24},{1,5},{5... | collective-permute-start | bytes 110600 | tf_op jit(solution)/shard_map/ppermute | solution.py:38
  1.2 0.8 %constant_dynamic-update-slice_fusion.1 = bf16[32,1152]{1,0:T(8,128)(2,1)S(1)} fusion(bf16[16,1152]{1,0:T(8,128)(2,1)} %param.4), kind=kLoop, calls=%fused_computation.1 | loop fusion | bytes 73728
  2.0 0.2 collective-permute-done.1.img_ref
  2.2 0.3 %collective-permute-done.txt_ref = bf16[16,1152]{1,0:T(8,128)(2,1)S(1)} collective-permute-done((bf16[16,1152]{1,0:T(8,128)(2,1)}, bf16[16,1152]{1,0:T(8,128)(2,1)S(1)}, u32[]{:S(2)}, u32[]{:S(2)}) %collective-permute-start) | collective-permute-done | bytes 36896 | tf_op jit(solution)/shard_map/ppermute | solution.py:38
  2.7 2.7 %collective-permute-start.3 = (bf16[32,1152]{1,0:T(8,128)(2,1)S(1)}, bf16[32,1152]{1,0:T(8,128)(2,1)S(1)}, u32[]{:S(2)}, u32[]{:S(2)}) collective-permute-start(bf16[32,1152]{1,0:T(8,128)(2,1)S(1)} %get-tuple-element.14.refs_0_), channel_id=1, source_target_pairs={{0,16},{1,17},{2,18},{3,19},{4,6},{5,7},{6,4},{7,5},{8,24},{9,25},... | collective-permute-start | bytes 221192 | tf_op jit(solution)/shard_map/ppermute | solution.py:50
  5.5 1.4 %collective-permute-start.2 = (bf16[32,1152]{1,0:T(8,128)(2,1)S(1)}, bf16[32,1152]{1,0:T(8,128)(2,1)S(1)}, u32[]{:S(2)}, u32[]{:S(2)}) collective-permute-start(bf16[32,1152]{1,0:T(8,128)(2,1)S(1)} %get-tuple-element.14.refs_0_), channel_id=1, source_target_pairs={{0,24},{1,25},{2,26},{3,27},{4,7},{5,6},{6,5},{7,4},{8,16},{9,17},... | collective-permute-start | bytes 221192 | tf_op jit(solution)/shard_map/ppermute | solution.py:50
  7.0 0.8 %collective-permute-done.3.refs_2_ = bf16[32,1152]{1,0:T(8,128)(2,1)S(1)} collective-permute-done((bf16[32,1152]{1,0:T(8,128)(2,1)S(1)}, bf16[32,1152]{1,0:T(8,128)(2,1)S(1)}, u32[]{:S(2)}, u32[]{:S(2)}) %collective-permute-start.3) | collective-permute-done | bytes 73760 | tf_op jit(solution)/shard_map/ppermute | solution.py:50
  7.8 0.5 %collective-permute-start.6 = (bf16[32,1152]{1,0:T(8,128)(2,1)S(1)}, bf16[32,1152]{1,0:T(8,128)(2,1)S(1)}, u32[]{:S(2)}, u32[]{:S(2)}) collective-permute-start(bf16[32,1152]{1,0:T(8,128)(2,1)S(1)} %collective-permute-done.3.refs_2_), channel_id=1, source_target_pairs={{0,4},{4,0},{8,12},{12,8},{16,20},{20,16},{24,28},{28,24},{1,5},{5... | collective-permute-start | bytes 221192 | tf_op jit(solution)/shard_map/ppermute | solution.py:38
  8.4 2.4 %collective-permute-done.2.refs_1_ = bf16[32,1152]{1,0:T(8,128)(2,1)S(1)} collective-permute-done((bf16[32,1152]{1,0:T(8,128)(2,1)S(1)}, bf16[32,1152]{1,0:T(8,128)(2,1)S(1)}, u32[]{:S(2)}, u32[]{:S(2)}) %collective-permute-start.2) | collective-permute-done | bytes 73760 | tf_op jit(solution)/shard_map/ppermute | solution.py:50
  10.7 1.0 %collective-permute-start.5 = (bf16[32,1152]{1,0:T(8,128)(2,1)S(1)}, bf16[32,1152]{1,0:T(8,128)(2,1)S(1)}, u32[]{:S(2)}, u32[]{:S(2)}) collective-permute-start(bf16[32,1152]{1,0:T(8,128)(2,1)S(1)} %collective-permute-done.2.refs_1_), channel_id=1, source_target_pairs={{0,4},{4,0},{8,12},{12,8},{16,20},{20,16},{24,28},{28,24},{1,5},{5... | collective-permute-start | bytes 221192 | tf_op jit(solution)/shard_map/ppermute | solution.py:38
  11.8 0.8 %collective-permute-done.5.refs_5_ = bf16[32,1152]{1,0:T(8,128)(2,1)S(1)} collective-permute-done((bf16[32,1152]{1,0:T(8,128)(2,1)S(1)}, bf16[32,1152]{1,0:T(8,128)(2,1)S(1)}, u32[]{:S(2)}, u32[]{:S(2)}) %collective-permute-start.5) | collective-permute-done | bytes 73760 | tf_op jit(solution)/shard_map/ppermute | solution.py:38
  12.6 0.2 %shard_map.51.most_ref = f32[128,96]{1,0:T(8,128)S(1)} custom-call(bf16[32,1152]{1,0:T(8,128)(2,1)S(1)} %get-tuple-element.14.refs_0_, bf16[32,1152]{1,0:T(8,128)(2,1)S(1)} %collective-permute-done.2.refs_1_, bf16[32,1152]{1,0:T(8,128)(2,1)S(1)} %collective-permute-done.3.refs_2_, bf16[32,1152]{1,0:T(8,128)(2,1)S(1)} %collective-permute-done.4.refs_3_.piece_ref, ...), custom_call_target="tpu_custom_call" | custom-call | flops 10000000000 | bytes 10000000 | tf_op jit(solution)/shard_map/pallas_call | solution.py:59
  12.8 0.2 collective-permute-done.7.refs_7_
  13.1 0.6 %shard_map.53 = (f32[32,1152]{1,0:T(8,128)S(1)}, bf16[16,1152]{1,0:T(8,128)(2,1)S(1)}, bf16[16,1152]{1,0:T(8,128)(2,1)S(1)}, bf16[32,1152]{1,0:T(8,128)(2,1)S(1)}, bf16[32,1152]{1,0:T(8,128)(2,1)S(1)}) custom-call(s32[1,64]{1,0:T(1,128)S(1)} %bitcast.2, f32[128,96]{1,0:T(8,128)S(1)} %shard_map.51.most_ref, bf16[32,1152]{1,0:T(8,128)(2,1)S(1)} %get-tuple-element.14.refs_0_, ...), custom_call_target="tpu_custom_call" | custom-call | tf_op jit(solution)/shard_map/pallas_call | solution.py:59
  13.7 1.6 %collective-permute-start.8 = (bf16[32,1152]{1,0:T(8,128)(2,1)S(1)}, bf16[32,1152]{1,0:T(8,128)(2,1)S(1)}, u32[]{:S(2)}, u32[]{:S(2)}) collective-permute-start(bf16[32,1152]{1,0:T(8,128)(2,1)S(1)} %get-tuple-element.17), channel_id=1, source_target_pairs={{0,8},{1,9},{2,10},{3,11},{4,5},{5,4},{6,7},{7,6},{8,0},{9,1},{10,... | collective-permute-start | bytes 221192 | tf_op jit(solution)/shard_map/ppermute | solution.py:50
  15.2 1.5 %collective-permute-start.9 = (bf16[32,1152]{1,0:T(8,128)(2,1)S(1)}, bf16[32,1152]{1,0:T(8,128)(2,1)S(1)}, u32[]{:S(2)}, u32[]{:S(2)}) collective-permute-start(bf16[32,1152]{1,0:T(8,128)(2,1)S(1)} %get-tuple-element.18), channel_id=1, source_target_pairs={{0,24},{1,25},{2,26},{3,27},{4,7},{5,6},{6,5},{7,4},{8,16},{9,17},... | collective-permute-start | bytes 221192 | tf_op jit(solution)/shard_map/ppermute | solution.py:50
  16.7 0.5 %collective-permute-start.10 = (bf16[16,1152]{1,0:T(8,128)(2,1)S(1)}, bf16[16,1152]{1,0:T(8,128)(2,1)S(1)}, u32[]{:S(2)}, u32[]{:S(2)}) collective-permute-start(bf16[16,1152]{1,0:T(8,128)(2,1)S(1)} %get-tuple-element.20), channel_id=1, source_target_pairs={{0,16},{1,17},{2,18},{3,19},{4,6},{5,7},{6,4},{7,5},{8,24},{9,25},... | collective-permute-start | bytes 110600 | tf_op jit(solution)/shard_map/ppermute | solution.py:50
  17.2 1.0 %collective-permute-start.11 = (bf16[16,1152]{1,0:T(8,128)(2,1)S(1)}, bf16[16,1152]{1,0:T(8,128)(2,1)S(1)}, u32[]{:S(2)}, u32[]{:S(2)}) collective-permute-start(bf16[16,1152]{1,0:T(8,128)(2,1)S(1)} %get-tuple-element.24), channel_id=1, source_target_pairs={{0,20},{1,21},{2,22},{3,23},{4,2},{5,3},{6,0},{7,1},{8,28},{9,29},... | collective-permute-start | bytes 110600 | tf_op jit(solution)/shard_map/ppermute | solution.py:50
  18.2 2.3 %collective-permute-done.9.refs_1_ = bf16[32,1152]{1,0:T(8,128)(2,1)S(1)} collective-permute-done((bf16[32,1152]{1,0:T(8,128)(2,1)S(1)}, bf16[32,1152]{1,0:T(8,128)(2,1)S(1)}, u32[]{:S(2)}, u32[]{:S(2)}) %collective-permute-start.9) | collective-permute-done | bytes 73760 | tf_op jit(solution)/shard_map/ppermute | solution.py:50
  20.6 0.3 %collective-permute-done.10.same_ref = bf16[16,1152]{1,0:T(8,128)(2,1)S(1)} collective-permute-done((bf16[16,1152]{1,0:T(8,128)(2,1)S(1)}, bf16[16,1152]{1,0:T(8,128)(2,1)S(1)}, u32[]{:S(2)}, u32[]{:S(2)}) %collective-permute-start.10) | collective-permute-done | bytes 36896 | tf_op jit(solution)/shard_map/ppermute | solution.py:50
  20.9 0.2 shard_map.55
  21.1 0.5 %collective-permute-done.11.cross_ref = bf16[16,1152]{1,0:T(8,128)(2,1)S(1)} collective-permute-done((bf16[16,1152]{1,0:T(8,128)(2,1)S(1)}, bf16[16,1152]{1,0:T(8,128)(2,1)S(1)}, u32[]{:S(2)}, u32[]{:S(2)}) %collective-permute-start.11) | collective-permute-done | bytes 36896 | tf_op jit(solution)/shard_map/ppermute | solution.py:50
  21.6 0.2 collective-permute-done.12.got_ref
  21.8 0.8 %shard_map.56 = (f32[16,1152]{1,0:T(8,128)}, f32[16,1152]{1,0:T(8,128)}) custom-call(f32[16,1152]{1,0:T(8,128)S(1)} %get-tuple-element.21.grad_ref, f32[16,1152]{1,0:T(8,128)S(1)} %get-tuple-element.22.unit_ref, f32[16,1]{1,0:T(8,128)S(1)} %get-tuple-element.23.inverse_ref, bf16[16,1152]{1,0:T(8,128)(2,1)S(1)} %collective-permute-done.11.cross_ref, ...), custom_call_target="tpu_custom_call" | custom-call | tf_op jit(solution)/shard_map/pallas_call | solution.py:59
  (15 shorter events, 0.5 us)
Async XLA Ops:
  0.6 1.4 %copy-start.1 = (bf16[16,1152]{1,0:T(8,128)(2,1)S(1)}, bf16[16,1152]{1,0:T(8,128)(2,1)}, u32[]{:S(2)}) copy-start(bf16[16,1152]{1,0:T(8,128)(2,1)} %param.3) | copy-start | bytes 110596
  0.6 1.6 %collective-permute-start.1 = (bf16[16,1152]{1,0:T(8,128)(2,1)}, bf16[16,1152]{1,0:T(8,128)(2,1)S(1)}, u32[]{:S(2)}, u32[]{:S(2)}) collective-permute-start(bf16[16,1152]{1,0:T(8,128)(2,1)} %param.3), channel_id=1, source_target_pairs={{0,4},{4,0},{8,12},{12,8},{16,20},{20,16},{24,28},{28,24},{1,5},{5... | collective-permute-start | bytes 110600 | tf_op jit(solution)/shard_map/ppermute | solution.py:38
  1.2 1.4 %collective-permute-start = (bf16[16,1152]{1,0:T(8,128)(2,1)}, bf16[16,1152]{1,0:T(8,128)(2,1)S(1)}, u32[]{:S(2)}, u32[]{:S(2)}) collective-permute-start(bf16[16,1152]{1,0:T(8,128)(2,1)} %param.4), channel_id=1, source_target_pairs={{0,4},{4,0},{8,12},{12,8},{16,20},{20,16},{24,28},{28,24},{1,5},{5... | collective-permute-start | bytes 110600 | tf_op jit(solution)/shard_map/ppermute | solution.py:38
  2.7 9.0 %copy-start = (s32[64]{0:T(128)S(1)}, s32[64]{0:T(128)}, u32[]{:S(2)}) copy-start(s32[64]{0:T(128)} %param.5) | copy-start | bytes 772
  2.7 5.1 %collective-permute-start.3 = (bf16[32,1152]{1,0:T(8,128)(2,1)S(1)}, bf16[32,1152]{1,0:T(8,128)(2,1)S(1)}, u32[]{:S(2)}, u32[]{:S(2)}) collective-permute-start(bf16[32,1152]{1,0:T(8,128)(2,1)S(1)} %get-tuple-element.14.refs_0_), channel_id=1, source_target_pairs={{0,16},{1,17},{2,18},{3,19},{4,6},{5,7},{6,4},{7,5},{8,24},{9,25},... | collective-permute-start | bytes 221192 | tf_op jit(solution)/shard_map/ppermute | solution.py:50
  5.5 5.3 %collective-permute-start.2 = (bf16[32,1152]{1,0:T(8,128)(2,1)S(1)}, bf16[32,1152]{1,0:T(8,128)(2,1)S(1)}, u32[]{:S(2)}, u32[]{:S(2)}) collective-permute-start(bf16[32,1152]{1,0:T(8,128)(2,1)S(1)} %get-tuple-element.14.refs_0_), channel_id=1, source_target_pairs={{0,24},{1,25},{2,26},{3,27},{4,7},{5,6},{6,5},{7,4},{8,16},{9,17},... | collective-permute-start | bytes 221192 | tf_op jit(solution)/shard_map/ppermute | solution.py:50
  6.9 4.8 %collective-permute-start.4 = (bf16[32,1152]{1,0:T(8,128)(2,1)S(1)}, bf16[32,1152]{1,0:T(8,128)(2,1)S(1)}, u32[]{:S(2)}, u32[]{:S(2)}) collective-permute-start(bf16[32,1152]{1,0:T(8,128)(2,1)S(1)} %get-tuple-element.14.refs_0_), channel_id=1, source_target_pairs={{0,8},{1,9},{2,10},{3,11},{4,5},{5,4},{6,7},{7,6},{8,0},{9,1},{10,... | collective-permute-start | bytes 221192 | tf_op jit(solution)/shard_map/ppermute | solution.py:50
  7.8 4.0 %collective-permute-start.6 = (bf16[32,1152]{1,0:T(8,128)(2,1)S(1)}, bf16[32,1152]{1,0:T(8,128)(2,1)S(1)}, u32[]{:S(2)}, u32[]{:S(2)}) collective-permute-start(bf16[32,1152]{1,0:T(8,128)(2,1)S(1)} %collective-permute-done.3.refs_2_), channel_id=1, source_target_pairs={{0,4},{4,0},{8,12},{12,8},{16,20},{20,16},{24,28},{28,24},{1,5},{5... | collective-permute-start | bytes 221192 | tf_op jit(solution)/shard_map/ppermute | solution.py:38
  10.7 1.9 %collective-permute-start.5 = (bf16[32,1152]{1,0:T(8,128)(2,1)S(1)}, bf16[32,1152]{1,0:T(8,128)(2,1)S(1)}, u32[]{:S(2)}, u32[]{:S(2)}) collective-permute-start(bf16[32,1152]{1,0:T(8,128)(2,1)S(1)} %collective-permute-done.2.refs_1_), channel_id=1, source_target_pairs={{0,4},{4,0},{8,12},{12,8},{16,20},{20,16},{24,28},{28,24},{1,5},{5... | collective-permute-start | bytes 221192 | tf_op jit(solution)/shard_map/ppermute | solution.py:38
  11.7 1.3 %collective-permute-start.7 = (bf16[304,128]{1,0:T(8,128)(2,1)S(1)}, bf16[304,128]{1,0:T(8,128)(2,1)S(1)}, u32[]{:S(2)}, u32[]{:S(2)}) collective-permute-start(bf16[304,128]{1,0:T(8,128)(2,1)S(1)} %shard_map.52), channel_id=1, source_target_pairs={{0,4},{4,0},{8,12},{12,8},{16,20},{20,16},{24,28},{28,24},{1,5},{5... | collective-permute-start | bytes 233480 | tf_op jit(solution)/shard_map/ppermute | solution.py:38
  13.7 4.5 %collective-permute-start.8 = (bf16[32,1152]{1,0:T(8,128)(2,1)S(1)}, bf16[32,1152]{1,0:T(8,128)(2,1)S(1)}, u32[]{:S(2)}, u32[]{:S(2)}) collective-permute-start(bf16[32,1152]{1,0:T(8,128)(2,1)S(1)} %get-tuple-element.17), channel_id=1, source_target_pairs={{0,8},{1,9},{2,10},{3,11},{4,5},{5,4},{6,7},{7,6},{8,0},{9,1},{10,... | collective-permute-start | bytes 221192 | tf_op jit(solution)/shard_map/ppermute | solution.py:50
  15.2 5.3 %collective-permute-start.9 = (bf16[32,1152]{1,0:T(8,128)(2,1)S(1)}, bf16[32,1152]{1,0:T(8,128)(2,1)S(1)}, u32[]{:S(2)}, u32[]{:S(2)}) collective-permute-start(bf16[32,1152]{1,0:T(8,128)(2,1)S(1)} %get-tuple-element.18), channel_id=1, source_target_pairs={{0,24},{1,25},{2,26},{3,27},{4,7},{5,6},{6,5},{7,4},{8,16},{9,17},... | collective-permute-start | bytes 221192 | tf_op jit(solution)/shard_map/ppermute | solution.py:50
  16.7 4.2 %collective-permute-start.10 = (bf16[16,1152]{1,0:T(8,128)(2,1)S(1)}, bf16[16,1152]{1,0:T(8,128)(2,1)S(1)}, u32[]{:S(2)}, u32[]{:S(2)}) collective-permute-start(bf16[16,1152]{1,0:T(8,128)(2,1)S(1)} %get-tuple-element.20), channel_id=1, source_target_pairs={{0,16},{1,17},{2,18},{3,19},{4,6},{5,7},{6,4},{7,5},{8,24},{9,25},... | collective-permute-start | bytes 110600 | tf_op jit(solution)/shard_map/ppermute | solution.py:50
  17.2 4.4 %collective-permute-start.11 = (bf16[16,1152]{1,0:T(8,128)(2,1)S(1)}, bf16[16,1152]{1,0:T(8,128)(2,1)S(1)}, u32[]{:S(2)}, u32[]{:S(2)}) collective-permute-start(bf16[16,1152]{1,0:T(8,128)(2,1)S(1)} %get-tuple-element.24), channel_id=1, source_target_pairs={{0,20},{1,21},{2,22},{3,23},{4,2},{5,3},{6,0},{7,1},{8,28},{9,29},... | collective-permute-start | bytes 110600 | tf_op jit(solution)/shard_map/ppermute | solution.py:50
  20.5 1.3 %collective-permute-start.12 = (bf16[16,1152]{1,0:T(8,128)(2,1)S(1)}, bf16[16,1152]{1,0:T(8,128)(2,1)S(1)}, u32[]{:S(2)}, u32[]{:S(2)}) collective-permute-start(bf16[16,1152]{1,0:T(8,128)(2,1)S(1)} %get-tuple-element.25), channel_id=1, source_target_pairs={{0,4},{4,0},{8,12},{12,8},{16,20},{20,16},{24,28},{28,24},{1,5},{5... | collective-permute-start | bytes 110600 | tf_op jit(solution)/shard_map/ppermute | solution.py:38

commit v14 on v12

--- a/solution.py
+++ b/solution.py
@@ -116,7 +116,10 @@
     n_img = lax.axis_size("img")
     row = lax.broadcasted_iota(jnp.int32, (count, 1), 0)
     block, core, j = row // (2 * rows), row // rows % 2, row % rows
-    chip = jnp.where(block == 0, 0, count // (2 * rows) - block)
+    blocks = count // (2 * rows)
+    chip = jnp.where(block == 0, 0, blocks - block)
+    if blocks > 2:
+        chip = jnp.where(block == 1, blocks - 2, jnp.where(block == 2, blocks - 1, chip))
     txt_ids = (me_txt * n_img + (((me_img // 2) ^ chip) * 2 + core)) * rows + j
     source = (me_txt ^ chip) * rows + j
     here = lax.broadcasted_iota(jnp.int32, (count, ids.shape[1]), 1) == source
@@ -213,6 +216,7 @@
     near = jnp.concatenate([text_embeds, image_embeds])
     mine, other = call(sides_kernel, [pair] * 2, [near, far_txt, far_img])
     order = list(range(blocks - 1, 0, -1))
+    order[:2] = order[1::-1]
     mine = [mine] + [chip_swap(mine, k) for k in order]
     packed = jax.ShapeDtypeStruct((2 * rows * (width // LANES) + 16, LANES), bf16)
     (packed,) = call(pack_kernel, [packed], [ids, mine[-1]])
@@ -224,7 +228,7 @@
         [*mine, *other[:-1]],
         cost=LONG,
     )
-    split = blocks - 1
+    split = 1
     own, same, cross, *send = call(
         functools.partial(rest_kernel, blocks, split),
         [total] + [piece] * 2 + [pair] * (blocks - 2),

time: 22.9 us -> 22.8 us (level)
  starting transfers between devices: 11.9 us -> 11.6 us
    ppermute x7, waiting for transfers between devices: 5.27 us -> 5.71 us  [chip_swap(): return lax.ppermute(block, ('img', 'txt'), pairs)]
    ppermute x6, starting transfers between devices: 2.71 us -> 2.35 us  [core_swap(): return lax.ppermute(block, 'img', [(i, i ^ 1) for i in range(size)])]
where the time goes in v14:
time: 22.8 us; the launch traced here: 22.6 us
  starting transfers between devices  11.6 us (51%)
  waiting for transfers between devices  7.61 us (33%)
  Pallas kernels  1.96 us (9%)
  local copies, waits for them, and re-layouts  0.79 us (3%)
  between operations  0.71 us (3%)
    ppermute x7, starting transfers between devices, chip_swap(): return lax.ppermute(block, ('img', 'txt'), pairs)  9.21 us
    ppermute x7, waiting for transfers between devices, chip_swap(): return lax.ppermute(block, ('img', 'txt'), pairs)  5.71 us
    ppermute x6, starting transfers between devices, core_swap(): return lax.ppermute(block, 'img', [(i, i ^ 1) for i in range(size)])  2.35 us
    pallas_call x7, Pallas kernels, call(): pl.pallas_call(kernel, out_shape=outs, in_specs=[VMEM] * len(args), out_s...  1.96 us
    ppermute x6, waiting for transfers between devices, core_swap(): return lax.ppermute(block, 'img', [(i, i ^ 1) for i in range(size)])  1.9 us
    unnamed x5, local copies, waits for them, and re-layouts  0.78 us
  transfers between devices with their start and end apart: 13, of which 10 were waited for; matrix products, arithmetic and copies ran while one was open for 3% of the time, Pallas kernels for 2%

profile of v14, /device:TPU:0, one launch (start us, length us, event | category | flops | bytes accessed | tf_op | source)
XLA Modules:
  0.0 22.6 jit_solution(2192924359699994265)
XLA Ops:
  0.6 0.5 %collective-permute-start.1 = (bf16[16,1152]{1,0:T(8,128)(2,1)}, bf16[16,1152]{1,0:T(8,128)(2,1)S(1)}, u32[]{:S(2)}, u32[]{:S(2)}) collective-permute-start(bf16[16,1152]{1,0:T(8,128)(2,1)} %param.3), channel_id=1, source_target_pairs={{0,4},{4,0},{8,12},{12,8},{16,20},{20,16},{24,28},{28,24},{1,5},{5... | collective-permute-start | bytes 110600 | tf_op jit(solution)/shard_map/ppermute | solution.py:38
  1.2 0.8 %constant_dynamic-update-slice_fusion.1 = bf16[32,1152]{1,0:T(8,128)(2,1)S(1)} fusion(bf16[16,1152]{1,0:T(8,128)(2,1)} %param.4), kind=kLoop, calls=%fused_computation.1 | loop fusion | bytes 73728
  2.0 0.2 collective-permute-done.1.img_ref
  2.2 0.3 %collective-permute-done.txt_ref = bf16[16,1152]{1,0:T(8,128)(2,1)S(1)} collective-permute-done((bf16[16,1152]{1,0:T(8,128)(2,1)}, bf16[16,1152]{1,0:T(8,128)(2,1)S(1)}, u32[]{:S(2)}, u32[]{:S(2)}) %collective-permute-start) | collective-permute-done | bytes 36896 | tf_op jit(solution)/shard_map/ppermute | solution.py:38
  2.7 3.7 %collective-permute-start.3 = (bf16[32,1152]{1,0:T(8,128)(2,1)S(1)}, bf16[32,1152]{1,0:T(8,128)(2,1)S(1)}, u32[]{:S(2)}, u32[]{:S(2)}) collective-permute-start(bf16[32,1152]{1,0:T(8,128)(2,1)S(1)} %get-tuple-element.14.refs_0_), channel_id=1, source_target_pairs={{0,24},{1,25},{2,26},{3,27},{4,7},{5,6},{6,5},{7,4},{8,16},{9,17},... | collective-permute-start | bytes 221192 | tf_op jit(solution)/shard_map/ppermute | solution.py:50
  6.4 0.5 %collective-permute-start.2 = (bf16[32,1152]{1,0:T(8,128)(2,1)S(1)}, bf16[32,1152]{1,0:T(8,128)(2,1)S(1)}, u32[]{:S(2)}, u32[]{:S(2)}) collective-permute-start(bf16[32,1152]{1,0:T(8,128)(2,1)S(1)} %get-tuple-element.14.refs_0_), channel_id=1, source_target_pairs={{0,16},{1,17},{2,18},{3,19},{4,6},{5,7},{6,4},{7,5},{8,24},{9,25},... | collective-permute-start | bytes 221192 | tf_op jit(solution)/shard_map/ppermute | solution.py:50
  7.0 1.7 %collective-permute-done.3.refs_2_ = bf16[32,1152]{1,0:T(8,128)(2,1)S(1)} collective-permute-done((bf16[32,1152]{1,0:T(8,128)(2,1)S(1)}, bf16[32,1152]{1,0:T(8,128)(2,1)S(1)}, u32[]{:S(2)}, u32[]{:S(2)}) %collective-permute-start.3) | collective-permute-done | bytes 73760 | tf_op jit(solution)/shard_map/ppermute | solution.py:50
  8.7 0.6 %collective-permute-start.6 = (bf16[32,1152]{1,0:T(8,128)(2,1)S(1)}, bf16[32,1152]{1,0:T(8,128)(2,1)S(1)}, u32[]{:S(2)}, u32[]{:S(2)}) collective-permute-start(bf16[32,1152]{1,0:T(8,128)(2,1)S(1)} %collective-permute-done.3.refs_2_), channel_id=1, source_target_pairs={{0,4},{4,0},{8,12},{12,8},{16,20},{20,16},{24,28},{28,24},{1,5},{5... | collective-permute-start | bytes 221192 | tf_op jit(solution)/shard_map/ppermute | solution.py:38
  9.4 1.4 %collective-permute-done.2.refs_1_ = bf16[32,1152]{1,0:T(8,128)(2,1)S(1)} collective-permute-done((bf16[32,1152]{1,0:T(8,128)(2,1)S(1)}, bf16[32,1152]{1,0:T(8,128)(2,1)S(1)}, u32[]{:S(2)}, u32[]{:S(2)}) %collective-permute-start.2) | collective-permute-done | bytes 73760 | tf_op jit(solution)/shard_map/ppermute | solution.py:50
  10.7 1.0 %collective-permute-start.5 = (bf16[32,1152]{1,0:T(8,128)(2,1)S(1)}, bf16[32,1152]{1,0:T(8,128)(2,1)S(1)}, u32[]{:S(2)}, u32[]{:S(2)}) collective-permute-start(bf16[32,1152]{1,0:T(8,128)(2,1)S(1)} %collective-permute-done.2.refs_1_), channel_id=1, source_target_pairs={{0,4},{4,0},{8,12},{12,8},{16,20},{20,16},{24,28},{28,24},{1,5},{5... | collective-permute-start | bytes 221192 | tf_op jit(solution)/shard_map/ppermute | solution.py:38
  11.8 0.8 %collective-permute-done.5.refs_5_ = bf16[32,1152]{1,0:T(8,128)(2,1)S(1)} collective-permute-done((bf16[32,1152]{1,0:T(8,128)(2,1)S(1)}, bf16[32,1152]{1,0:T(8,128)(2,1)S(1)}, u32[]{:S(2)}, u32[]{:S(2)}) %collective-permute-start.5) | collective-permute-done | bytes 73760 | tf_op jit(solution)/shard_map/ppermute | solution.py:38
  12.6 0.2 %shard_map.51.most_ref = f32[128,96]{1,0:T(8,128)S(1)} custom-call(bf16[32,1152]{1,0:T(8,128)(2,1)S(1)} %get-tuple-element.14.refs_0_, bf16[32,1152]{1,0:T(8,128)(2,1)S(1)} %collective-permute-done.2.refs_1_, bf16[32,1152]{1,0:T(8,128)(2,1)S(1)} %collective-permute-done.3.refs_2_, bf16[32,1152]{1,0:T(8,128)(2,1)S(1)} %collective-permute-done.4.refs_3_.piece_ref, ...), custom_call_target="tpu_custom_call" | custom-call | flops 10000000000 | bytes 10000000 | tf_op jit(solution)/shard_map/pallas_call | solution.py:59
  12.9 0.2 collective-permute-done.7.refs_7_
  13.1 0.6 %shard_map.53 = (f32[32,1152]{1,0:T(8,128)S(1)}, bf16[16,1152]{1,0:T(8,128)(2,1)S(1)}, bf16[16,1152]{1,0:T(8,128)(2,1)S(1)}, bf16[32,1152]{1,0:T(8,128)(2,1)S(1)}, bf16[32,1152]{1,0:T(8,128)(2,1)S(1)}) custom-call(s32[1,64]{1,0:T(1,128)S(1)} %bitcast.2, f32[128,96]{1,0:T(8,128)S(1)} %shard_map.51.most_ref, bf16[32,1152]{1,0:T(8,128)(2,1)S(1)} %get-tuple-element.14.refs_0_, ...), custom_call_target="tpu_custom_call" | custom-call | tf_op jit(solution)/shard_map/pallas_call | solution.py:59
  13.7 2.5 %collective-permute-start.8 = (bf16[32,1152]{1,0:T(8,128)(2,1)S(1)}, bf16[32,1152]{1,0:T(8,128)(2,1)S(1)}, u32[]{:S(2)}, u32[]{:S(2)}) collective-permute-start(bf16[32,1152]{1,0:T(8,128)(2,1)S(1)} %get-tuple-element.17), channel_id=1, source_target_pairs={{0,24},{1,25},{2,26},{3,27},{4,7},{5,6},{6,5},{7,4},{8,16},{9,17},... | collective-permute-start | bytes 221192 | tf_op jit(solution)/shard_map/ppermute | solution.py:50
  16.2 0.5 %collective-permute-start.9 = (bf16[32,1152]{1,0:T(8,128)(2,1)S(1)}, bf16[32,1152]{1,0:T(8,128)(2,1)S(1)}, u32[]{:S(2)}, u32[]{:S(2)}) collective-permute-start(bf16[32,1152]{1,0:T(8,128)(2,1)S(1)} %get-tuple-element.18), channel_id=1, source_target_pairs={{0,8},{1,9},{2,10},{3,11},{4,5},{5,4},{6,7},{7,6},{8,0},{9,1},{10,... | collective-permute-start | bytes 221192 | tf_op jit(solution)/shard_map/ppermute | solution.py:50
  16.7 0.5 %collective-permute-start.10 = (bf16[16,1152]{1,0:T(8,128)(2,1)S(1)}, bf16[16,1152]{1,0:T(8,128)(2,1)S(1)}, u32[]{:S(2)}, u32[]{:S(2)}) collective-permute-start(bf16[16,1152]{1,0:T(8,128)(2,1)S(1)} %get-tuple-element.20), channel_id=1, source_target_pairs={{0,16},{1,17},{2,18},{3,19},{4,6},{5,7},{6,4},{7,5},{8,24},{9,25},... | collective-permute-start | bytes 110600 | tf_op jit(solution)/shard_map/ppermute | solution.py:50
  17.2 1.3 %collective-permute-start.11 = (bf16[16,1152]{1,0:T(8,128)(2,1)S(1)}, bf16[16,1152]{1,0:T(8,128)(2,1)S(1)}, u32[]{:S(2)}, u32[]{:S(2)}) collective-permute-start(bf16[16,1152]{1,0:T(8,128)(2,1)S(1)} %get-tuple-element.24), channel_id=1, source_target_pairs={{0,20},{1,21},{2,22},{3,23},{4,2},{5,3},{6,0},{7,1},{8,28},{9,29},... | collective-permute-start | bytes 110600 | tf_op jit(solution)/shard_map/ppermute | solution.py:50
  18.6 0.4 %collective-permute-done.8.refs_0_ = bf16[32,1152]{1,0:T(8,128)(2,1)S(1)} collective-permute-done((bf16[32,1152]{1,0:T(8,128)(2,1)S(1)}, bf16[32,1152]{1,0:T(8,128)(2,1)S(1)}, u32[]{:S(2)}, u32[]{:S(2)}) %collective-permute-start.8) | collective-permute-done | bytes 73760 | tf_op jit(solution)/shard_map/ppermute | solution.py:50
  19.0 1.5 %collective-permute-done.9.refs_1_ = bf16[32,1152]{1,0:T(8,128)(2,1)S(1)} collective-permute-done((bf16[32,1152]{1,0:T(8,128)(2,1)S(1)}, bf16[32,1152]{1,0:T(8,128)(2,1)S(1)}, u32[]{:S(2)}, u32[]{:S(2)}) %collective-permute-start.9) | collective-permute-done | bytes 73760 | tf_op jit(solution)/shard_map/ppermute | solution.py:50
  20.7 0.2 shard_map.55
  20.9 0.6 %collective-permute-done.11.cross_ref = bf16[16,1152]{1,0:T(8,128)(2,1)S(1)} collective-permute-done((bf16[16,1152]{1,0:T(8,128)(2,1)S(1)}, bf16[16,1152]{1,0:T(8,128)(2,1)S(1)}, u32[]{:S(2)}, u32[]{:S(2)}) %collective-permute-start.11) | collective-permute-done | bytes 36896 | tf_op jit(solution)/shard_map/ppermute | solution.py:50
  21.5 0.3 %collective-permute-done.12.got_ref = bf16[16,1152]{1,0:T(8,128)(2,1)S(1)} collective-permute-done((bf16[16,1152]{1,0:T(8,128)(2,1)S(1)}, bf16[16,1152]{1,0:T(8,128)(2,1)S(1)}, u32[]{:S(2)}, u32[]{:S(2)}) %collective-permute-start.12) | collective-permute-done | bytes 36896 | tf_op jit(solution)/shard_map/ppermute | solution.py:38
  21.9 0.8 %shard_map.56 = (f32[16,1152]{1,0:T(8,128)}, f32[16,1152]{1,0:T(8,128)}) custom-call(f32[16,1152]{1,0:T(8,128)S(1)} %get-tuple-element.21.grad_ref, f32[16,1152]{1,0:T(8,128)S(1)} %get-tuple-element.22.unit_ref, f32[16,1]{1,0:T(8,128)S(1)} %get-tuple-element.23.inverse_ref, bf16[16,1152]{1,0:T(8,128)(2,1)S(1)} %collective-permute-done.11.cross_ref, ...), custom_call_target="tpu_custom_call" | custom-call | tf_op jit(solution)/shard_map/pallas_call | solution.py:59
  (15 shorter events, 0.6 us)
Async XLA Ops:
  0.6 1.4 %copy-start.1 = (bf16[16,1152]{1,0:T(8,128)(2,1)S(1)}, bf16[16,1152]{1,0:T(8,128)(2,1)}, u32[]{:S(2)}) copy-start(bf16[16,1152]{1,0:T(8,128)(2,1)} %param.3) | copy-start | bytes 110596
  0.6 1.6 %collective-permute-start.1 = (bf16[16,1152]{1,0:T(8,128)(2,1)}, bf16[16,1152]{1,0:T(8,128)(2,1)S(1)}, u32[]{:S(2)}, u32[]{:S(2)}) collective-permute-start(bf16[16,1152]{1,0:T(8,128)(2,1)} %param.3), channel_id=1, source_target_pairs={{0,4},{4,0},{8,12},{12,8},{16,20},{20,16},{24,28},{28,24},{1,5},{5... | collective-permute-start | bytes 110600 | tf_op jit(solution)/shard_map/ppermute | solution.py:38
  1.2 1.4 %collective-permute-start = (bf16[16,1152]{1,0:T(8,128)(2,1)}, bf16[16,1152]{1,0:T(8,128)(2,1)S(1)}, u32[]{:S(2)}, u32[]{:S(2)}) collective-permute-start(bf16[16,1152]{1,0:T(8,128)(2,1)} %param.4), channel_id=1, source_target_pairs={{0,4},{4,0},{8,12},{12,8},{16,20},{20,16},{24,28},{28,24},{1,5},{5... | collective-permute-start | bytes 110600 | tf_op jit(solution)/shard_map/ppermute | solution.py:38
  2.7 9.0 %copy-start = (s32[64]{0:T(128)S(1)}, s32[64]{0:T(128)}, u32[]{:S(2)}) copy-start(s32[64]{0:T(128)} %param.5) | copy-start | bytes 772
  2.7 6.0 %collective-permute-start.3 = (bf16[32,1152]{1,0:T(8,128)(2,1)S(1)}, bf16[32,1152]{1,0:T(8,128)(2,1)S(1)}, u32[]{:S(2)}, u32[]{:S(2)}) collective-permute-start(bf16[32,1152]{1,0:T(8,128)(2,1)S(1)} %get-tuple-element.14.refs_0_), channel_id=1, source_target_pairs={{0,24},{1,25},{2,26},{3,27},{4,7},{5,6},{6,5},{7,4},{8,16},{9,17},... | collective-permute-start | bytes 221192 | tf_op jit(solution)/shard_map/ppermute | solution.py:50
  6.4 4.4 %collective-permute-start.2 = (bf16[32,1152]{1,0:T(8,128)(2,1)S(1)}, bf16[32,1152]{1,0:T(8,128)(2,1)S(1)}, u32[]{:S(2)}, u32[]{:S(2)}) collective-permute-start(bf16[32,1152]{1,0:T(8,128)(2,1)S(1)} %get-tuple-element.14.refs_0_), channel_id=1, source_target_pairs={{0,16},{1,17},{2,18},{3,19},{4,6},{5,7},{6,4},{7,5},{8,24},{9,25},... | collective-permute-start | bytes 221192 | tf_op jit(solution)/shard_map/ppermute | solution.py:50
  6.9 4.8 %collective-permute-start.4 = (bf16[32,1152]{1,0:T(8,128)(2,1)S(1)}, bf16[32,1152]{1,0:T(8,128)(2,1)S(1)}, u32[]{:S(2)}, u32[]{:S(2)}) collective-permute-start(bf16[32,1152]{1,0:T(8,128)(2,1)S(1)} %get-tuple-element.14.refs_0_), channel_id=1, source_target_pairs={{0,8},{1,9},{2,10},{3,11},{4,5},{5,4},{6,7},{7,6},{8,0},{9,1},{10,... | collective-permute-start | bytes 221192 | tf_op jit(solution)/shard_map/ppermute | solution.py:50
  8.7 3.1 %collective-permute-start.6 = (bf16[32,1152]{1,0:T(8,128)(2,1)S(1)}, bf16[32,1152]{1,0:T(8,128)(2,1)S(1)}, u32[]{:S(2)}, u32[]{:S(2)}) collective-permute-start(bf16[32,1152]{1,0:T(8,128)(2,1)S(1)} %collective-permute-done.3.refs_2_), channel_id=1, source_target_pairs={{0,4},{4,0},{8,12},{12,8},{16,20},{20,16},{24,28},{28,24},{1,5},{5... | collective-permute-start | bytes 221192 | tf_op jit(solution)/shard_map/ppermute | solution.py:38
  10.7 1.9 %collective-permute-start.5 = (bf16[32,1152]{1,0:T(8,128)(2,1)S(1)}, bf16[32,1152]{1,0:T(8,128)(2,1)S(1)}, u32[]{:S(2)}, u32[]{:S(2)}) collective-permute-start(bf16[32,1152]{1,0:T(8,128)(2,1)S(1)} %collective-permute-done.2.refs_1_), channel_id=1, source_target_pairs={{0,4},{4,0},{8,12},{12,8},{16,20},{20,16},{24,28},{28,24},{1,5},{5... | collective-permute-start | bytes 221192 | tf_op jit(solution)/shard_map/ppermute | solution.py:38
  11.8 1.3 %collective-permute-start.7 = (bf16[304,128]{1,0:T(8,128)(2,1)S(1)}, bf16[304,128]{1,0:T(8,128)(2,1)S(1)}, u32[]{:S(2)}, u32[]{:S(2)}) collective-permute-start(bf16[304,128]{1,0:T(8,128)(2,1)S(1)} %shard_map.52), channel_id=1, source_target_pairs={{0,4},{4,0},{8,12},{12,8},{16,20},{20,16},{24,28},{28,24},{1,5},{5... | collective-permute-start | bytes 233480 | tf_op jit(solution)/shard_map/ppermute | solution.py:38
  13.7 5.3 %collective-permute-start.8 = (bf16[32,1152]{1,0:T(8,128)(2,1)S(1)}, bf16[32,1152]{1,0:T(8,128)(2,1)S(1)}, u32[]{:S(2)}, u32[]{:S(2)}) collective-permute-start(bf16[32,1152]{1,0:T(8,128)(2,1)S(1)} %get-tuple-element.17), channel_id=1, source_target_pairs={{0,24},{1,25},{2,26},{3,27},{4,7},{5,6},{6,5},{7,4},{8,16},{9,17},... | collective-permute-start | bytes 221192 | tf_op jit(solution)/shard_map/ppermute | solution.py:50
  16.2 4.4 %collective-permute-start.9 = (bf16[32,1152]{1,0:T(8,128)(2,1)S(1)}, bf16[32,1152]{1,0:T(8,128)(2,1)S(1)}, u32[]{:S(2)}, u32[]{:S(2)}) collective-permute-start(bf16[32,1152]{1,0:T(8,128)(2,1)S(1)} %get-tuple-element.18), channel_id=1, source_target_pairs={{0,8},{1,9},{2,10},{3,11},{4,5},{5,4},{6,7},{7,6},{8,0},{9,1},{10,... | collective-permute-start | bytes 221192 | tf_op jit(solution)/shard_map/ppermute | solution.py:50
  16.7 4.0 %collective-permute-start.10 = (bf16[16,1152]{1,0:T(8,128)(2,1)S(1)}, bf16[16,1152]{1,0:T(8,128)(2,1)S(1)}, u32[]{:S(2)}, u32[]{:S(2)}) collective-permute-start(bf16[16,1152]{1,0:T(8,128)(2,1)S(1)} %get-tuple-element.20), channel_id=1, source_target_pairs={{0,16},{1,17},{2,18},{3,19},{4,6},{5,7},{6,4},{7,5},{8,24},{9,25},... | collective-permute-start | bytes 110600 | tf_op jit(solution)/shard_map/ppermute | solution.py:50
  17.2 4.3 %collective-permute-start.11 = (bf16[16,1152]{1,0:T(8,128)(2,1)S(1)}, bf16[16,1152]{1,0:T(8,128)(2,1)S(1)}, u32[]{:S(2)}, u32[]{:S(2)}) collective-permute-start(bf16[16,1152]{1,0:T(8,128)(2,1)S(1)} %get-tuple-element.24), channel_id=1, source_target_pairs={{0,20},{1,21},{2,22},{3,23},{4,2},{5,3},{6,0},{7,1},{8,28},{9,29},... | collective-permute-start | bytes 110600 | tf_op jit(solution)/shard_map/ppermute | solution.py:50
  20.6 1.3 %collective-permute-start.12 = (bf16[16,1152]{1,0:T(8,128)(2,1)S(1)}, bf16[16,1152]{1,0:T(8,128)(2,1)S(1)}, u32[]{:S(2)}, u32[]{:S(2)}) collective-permute-start(bf16[16,1152]{1,0:T(8,128)(2,1)S(1)} %get-tuple-element.25), channel_id=1, source_target_pairs={{0,4},{4,0},{8,12},{12,8},{16,20},{20,16},{24,28},{28,24},{1,5},{5... | collective-permute-start | bytes 110600 | tf_op jit(solution)/shard_map/ppermute | solution.py:38

commit v15 on v11

--- a/solution.py
+++ b/solution.py
@@ -11,6 +11,7 @@
 shift_logit = -4.0
 epsilon = 1e-06
 LANES = 128
+TXT_CORE = 1
 f32 = jnp.float32
 bf16 = jnp.bfloat16
 VMEM = pl.BlockSpec(memory_space=pltpu.VMEM)
@@ -43,11 +44,15 @@
     pairs = []
     for img in range(n_img):
         for txt in range(n_txt):
-            if img % 2 == 0 and distance < n_img // 2:
+            if img % 2 == TXT_CORE and distance < n_img // 2:
                 pairs.append((img * n_txt + txt, (img ^ (2 * distance) ^ cross) * n_txt + txt))
-            if img % 2 == 1 and distance < n_txt:
+            if img % 2 != TXT_CORE and distance < n_txt:
                 pairs.append((img * n_txt + txt, (img ^ cross) * n_txt + (txt ^ distance)))
     return lax.ppermute(block, ("img", "txt"), pairs)
+
+
+def is_txt():
+    return lax.axis_index("img") % 2 == TXT_CORE
 
 
 def is_even():
@@ -70,15 +75,18 @@
 
 def sides_kernel(own_ref, txt_ref, img_ref, mine_ref, other_ref):
     rows = txt_ref.shape[0]
-    even = is_even()
+    even, txt = is_even(), is_txt()
     own = normalize(own_ref[...])[0].astype(bf16)
-    own_txt, own_img = own[:rows], own[rows:]
     far_txt = normalize(txt_ref[...])[0].astype(bf16)
     far_img = normalize(img_ref[...])[0].astype(bf16)
-    mine_ref[:rows, :] = jnp.where(even, own_txt, far_img)
-    mine_ref[rows:, :] = jnp.where(even, far_txt, own_img)
-    other_ref[:rows, :] = jnp.where(even, own_img, far_txt)
-    other_ref[rows:, :] = jnp.where(even, far_img, own_txt)
+    mine_own = jnp.where(txt, own[:rows], own[rows:])
+    mine_far = jnp.where(txt, far_txt, far_img)
+    other_own = jnp.where(txt, own[rows:], own[:rows])
+    other_far = jnp.where(txt, far_img, far_txt)
+    mine_ref[:rows, :] = jnp.where(even, mine_own, mine_far)
+    mine_ref[rows:, :] = jnp.where(even, mine_far, mine_own)
+    other_ref[:rows, :] = jnp.where(even, other_own, other_far)
+    other_ref[rows:, :] = jnp.where(even, other_far, other_own)
 
 
 def pack_kernel(ids_ref, piece_ref, out_ref):
@@ -126,14 +134,14 @@
 
 
 def side_ids(rows, ids, far_ids, count):
-    even = is_even()
+    txt = is_txt()
     txt_ids, img_ids = row_ids(rows, ids, far_ids, count)
-    other_ids = jnp.where(even, img_ids, txt_ids)
+    other_ids = jnp.where(txt, img_ids, txt_ids)
     diagonal = lax.broadcasted_iota(jnp.int32, (count, count), 0) == lax.broadcasted_iota(
         jnp.int32, (count, count), 1
     )
     other_ids = jnp.sum(jnp.where(diagonal, other_ids, 0), axis=0, keepdims=True)
-    return jnp.where(even, txt_ids, img_ids), other_ids
+    return jnp.where(txt, txt_ids, img_ids), other_ids
 
 
 def scores_of(mine_refs, other):
@@ -180,24 +188,24 @@
 
 def keep_kernel(raw_ref, keep_ref, same_ref, grad_ref, unit_ref, inverse_ref):
     rows = keep_ref.shape[0]
-    even = is_even()
+    txt = is_txt()
     unit, inverse = normalize(raw_ref[...])
     grad_ref[...] = back_norm(
-        jnp.where(even, unit[:rows], unit[rows:]),
-        jnp.where(even, inverse[:rows], inverse[rows:]),
+        jnp.where(txt, unit[:rows], unit[rows:]),
+        jnp.where(txt, inverse[:rows], inverse[rows:]),
         keep_ref[...] + same_ref[...].astype(f32),
     )
-    unit_ref[...] = jnp.where(even, unit[rows:], unit[:rows])
-    inverse_ref[...] = jnp.where(even, inverse[rows:], inverse[:rows])
+    unit_ref[...] = jnp.where(txt, unit[rows:], unit[:rows])
+    inverse_ref[...] = jnp.where(txt, inverse[rows:], inverse[:rows])
 
 
 def out_kernel(grad_ref, unit_ref, inverse_ref, cross_ref, got_ref, img_ref, txt_ref):
-    even = is_even()
+    txt = is_txt()
     total = got_ref[...].astype(f32) + cross_ref[...].astype(f32)
     keep = grad_ref[...]
     got = back_norm(unit_ref[...], inverse_ref[...], total)
-    txt_ref[...] = jnp.where(even, keep, got)
-    img_ref[...] = jnp.where(even, got, keep)
+    txt_ref[...] = jnp.where(txt, keep, got)
+    img_ref[...] = jnp.where(txt, got, keep)
 
 
 def local(image_embeds, text_embeds, pair_ids):

time: 22.8 us -> 25.1 us (1.10)
  waiting for transfers between devices: 7.7 us -> 10.5 us
  starting transfers between devices: 11.4 us -> 10.9 us
    ppermute x7, waiting for transfers between devices: 5.8 us -> 8.25 us  [chip_swap(): return lax.ppermute(block, ('img', 'txt'), pairs)]
    ppermute x6, starting transfers between devices: 2.26 us -> 1.02 us  [core_swap(): return lax.ppermute(block, 'img', [(i, i ^ 1) for i in range(size)])]
    ppermute x7, starting transfers between devices: 9.18 us -> 9.84 us  [chip_swap(): return lax.ppermute(block, ('img', 'txt'), pairs)]
    ppermute x6, waiting for transfers between devices: 1.9 us -> 2.28 us  [core_swap(): return lax.ppermute(block, 'img', [(i, i ^ 1) for i in range(size)])]
where the time goes in v15:
time: 25.1 us; the launch traced here: 24.9 us
  starting transfers between devices  10.9 us (43%)
  waiting for transfers between devices  10.5 us (42%)
  Pallas kernels  1.98 us (8%)
  local copies, waits for them, and re-layouts  0.79 us (3%)
  between operations  0.71 us (3%)
    ppermute x7, starting transfers between devices, chip_swap(): return lax.ppermute(block, ('img', 'txt'), pairs)  9.84 us
    ppermute x7, waiting for transfers between devices, chip_swap(): return lax.ppermute(block, ('img', 'txt'), pairs)  8.25 us
    ppermute x6, waiting for transfers between devices, core_swap(): return lax.ppermute(block, 'img', [(i, i ^ 1) for i in range(size)])  2.28 us
    pallas_call x7, Pallas kernels, call(): pl.pallas_call(kernel, out_shape=outs, in_specs=[VMEM] * len(args), out_s...  1.98 us
    ppermute x6, starting transfers between devices, core_swap(): return lax.ppermute(block, 'img', [(i, i ^ 1) for i in range(size)])  1.02 us
    unnamed x5, local copies, waits for them, and re-layouts  0.78 us
  transfers between devices with their start and end apart: 13, of which 10 were waited for; matrix products, arithmetic and copies ran while one was open for 3% of the time, Pallas kernels for 2%

profile of v15, /device:TPU:0, one launch (start us, length us, event | category | flops | bytes accessed | tf_op | source)
XLA Modules:
  0.0 24.9 jit_solution(9829297397158075903)
XLA Ops:
  0.6 0.5 %collective-permute-start.1 = (bf16[16,1152]{1,0:T(8,128)(2,1)}, bf16[16,1152]{1,0:T(8,128)(2,1)S(1)}, u32[]{:S(2)}, u32[]{:S(2)}) collective-permute-start(bf16[16,1152]{1,0:T(8,128)(2,1)} %param.3), channel_id=1, source_target_pairs={{0,4},{4,0},{8,12},{12,8},{16,20},{20,16},{24,28},{28,24},{1,5},{5... | collective-permute-start | bytes 110600 | tf_op jit(solution)/shard_map/ppermute | solution.py:39
  1.2 0.1 collective-permute-start
  1.2 0.8 %constant_dynamic-update-slice_fusion.1 = bf16[32,1152]{1,0:T(8,128)(2,1)S(1)} fusion(bf16[16,1152]{1,0:T(8,128)(2,1)} %param.4), kind=kLoop, calls=%fused_computation.1 | loop fusion | bytes 73728
  2.0 0.2 collective-permute-done.1.img_ref
  2.2 0.3 %collective-permute-done.txt_ref = bf16[16,1152]{1,0:T(8,128)(2,1)S(1)} collective-permute-done((bf16[16,1152]{1,0:T(8,128)(2,1)}, bf16[16,1152]{1,0:T(8,128)(2,1)S(1)}, u32[]{:S(2)}, u32[]{:S(2)}) %collective-permute-start) | collective-permute-done | bytes 36896 | tf_op jit(solution)/shard_map/ppermute | solution.py:39
  2.6 0.1 shard_map.50
  2.7 3.8 %collective-permute-start.3 = (bf16[32,1152]{1,0:T(8,128)(2,1)S(1)}, bf16[32,1152]{1,0:T(8,128)(2,1)S(1)}, u32[]{:S(2)}, u32[]{:S(2)}) collective-permute-start(bf16[32,1152]{1,0:T(8,128)(2,1)S(1)} %get-tuple-element.14.refs_0_), channel_id=1, source_target_pairs={{0,2},{1,3},{2,0},{3,1},{4,20},{5,21},{6,22},{7,23},{8,10},{9,11},... | collective-permute-start | bytes 221192 | tf_op jit(solution)/shard_map/ppermute | solution.py:51
  6.5 1.3 %collective-permute-start.2 = (bf16[32,1152]{1,0:T(8,128)(2,1)S(1)}, bf16[32,1152]{1,0:T(8,128)(2,1)S(1)}, u32[]{:S(2)}, u32[]{:S(2)}) collective-permute-start(bf16[32,1152]{1,0:T(8,128)(2,1)S(1)} %get-tuple-element.14.refs_0_), channel_id=1, source_target_pairs={{0,3},{1,2},{2,1},{3,0},{4,28},{5,29},{6,30},{7,31},{8,11},{9,10},... | collective-permute-start | bytes 221192 | tf_op jit(solution)/shard_map/ppermute | solution.py:51
  7.9 0.2 collective-permute-start.4
  8.1 0.8 %collective-permute-done.3.refs_2_ = bf16[32,1152]{1,0:T(8,128)(2,1)S(1)} collective-permute-done((bf16[32,1152]{1,0:T(8,128)(2,1)S(1)}, bf16[32,1152]{1,0:T(8,128)(2,1)S(1)}, u32[]{:S(2)}, u32[]{:S(2)}) %collective-permute-start.3) | collective-permute-done | bytes 73760 | tf_op jit(solution)/shard_map/ppermute | solution.py:51
  8.9 3.9 %collective-permute-done.2.refs_1_ = bf16[32,1152]{1,0:T(8,128)(2,1)S(1)} collective-permute-done((bf16[32,1152]{1,0:T(8,128)(2,1)S(1)}, bf16[32,1152]{1,0:T(8,128)(2,1)S(1)}, u32[]{:S(2)}, u32[]{:S(2)}) %collective-permute-start.2) | collective-permute-done | bytes 73760 | tf_op jit(solution)/shard_map/ppermute | solution.py:51
  12.8 0.2 collective-permute-done.4.refs_3_.piece_ref
  13.1 0.3 %collective-permute-start.7 = (bf16[304,128]{1,0:T(8,128)(2,1)S(1)}, bf16[304,128]{1,0:T(8,128)(2,1)S(1)}, u32[]{:S(2)}, u32[]{:S(2)}) collective-permute-start(bf16[304,128]{1,0:T(8,128)(2,1)S(1)} %shard_map.52), channel_id=1, source_target_pairs={{0,4},{4,0},{8,12},{12,8},{16,20},{20,16},{24,28},{28,24},{1,5},{5... | collective-permute-start | bytes 233480 | tf_op jit(solution)/shard_map/ppermute | solution.py:39
  13.4 0.7 %collective-permute-done.5.refs_5_ = bf16[32,1152]{1,0:T(8,128)(2,1)S(1)} collective-permute-done((bf16[32,1152]{1,0:T(8,128)(2,1)S(1)}, bf16[32,1152]{1,0:T(8,128)(2,1)S(1)}, u32[]{:S(2)}, u32[]{:S(2)}) %collective-permute-start.5) | collective-permute-done | bytes 73760 | tf_op jit(solution)/shard_map/ppermute | solution.py:39
  14.1 0.2 shard_map.51.most_ref
  14.3 0.1 collective-permute-done.7.refs_7_
  14.4 0.6 %shard_map.53 = (f32[32,1152]{1,0:T(8,128)S(1)}, bf16[16,1152]{1,0:T(8,128)(2,1)S(1)}, bf16[16,1152]{1,0:T(8,128)(2,1)S(1)}, bf16[32,1152]{1,0:T(8,128)(2,1)S(1)}, bf16[32,1152]{1,0:T(8,128)(2,1)S(1)}) custom-call(s32[1,64]{1,0:T(1,128)S(1)} %bitcast.2, f32[128,96]{1,0:T(8,128)S(1)} %shard_map.51.most_ref, bf16[32,1152]{1,0:T(8,128)(2,1)S(1)} %get-tuple-element.14.refs_0_, ...), custom_call_target="tpu_custom_call" | custom-call | tf_op jit(solution)/shard_map/pallas_call | solution.py:64
  15.0 2.1 %collective-permute-start.8 = (bf16[32,1152]{1,0:T(8,128)(2,1)S(1)}, bf16[32,1152]{1,0:T(8,128)(2,1)S(1)}, u32[]{:S(2)}, u32[]{:S(2)}) collective-permute-start(bf16[32,1152]{1,0:T(8,128)(2,1)S(1)} %get-tuple-element.17), channel_id=1, source_target_pairs={{0,3},{1,2},{2,1},{3,0},{4,28},{5,29},{6,30},{7,31},{8,11},{9,10},... | collective-permute-start | bytes 221192 | tf_op jit(solution)/shard_map/ppermute | solution.py:51
  17.1 2.4 %collective-permute-start.10 = (bf16[16,1152]{1,0:T(8,128)(2,1)S(1)}, bf16[16,1152]{1,0:T(8,128)(2,1)S(1)}, u32[]{:S(2)}, u32[]{:S(2)}) collective-permute-start(bf16[16,1152]{1,0:T(8,128)(2,1)S(1)} %get-tuple-element.20), channel_id=1, source_target_pairs={{0,2},{1,3},{2,0},{3,1},{4,20},{5,21},{6,22},{7,23},{8,10},{9,11},... | collective-permute-start | bytes 110600 | tf_op jit(solution)/shard_map/ppermute | solution.py:51
  19.5 1.8 %collective-permute-done.8.refs_0_ = bf16[32,1152]{1,0:T(8,128)(2,1)S(1)} collective-permute-done((bf16[32,1152]{1,0:T(8,128)(2,1)S(1)}, bf16[32,1152]{1,0:T(8,128)(2,1)S(1)}, u32[]{:S(2)}, u32[]{:S(2)}) %collective-permute-start.8) | collective-permute-done | bytes 73760 | tf_op jit(solution)/shard_map/ppermute | solution.py:51
  21.3 1.5 %collective-permute-done.9.refs_1_ = bf16[32,1152]{1,0:T(8,128)(2,1)S(1)} collective-permute-done((bf16[32,1152]{1,0:T(8,128)(2,1)S(1)}, bf16[32,1152]{1,0:T(8,128)(2,1)S(1)}, u32[]{:S(2)}, u32[]{:S(2)}) %collective-permute-start.9) | collective-permute-done | bytes 73760 | tf_op jit(solution)/shard_map/ppermute | solution.py:51
  22.9 0.2 shard_map.55
  23.1 1.0 %collective-permute-done.12.got_ref = bf16[16,1152]{1,0:T(8,128)(2,1)S(1)} collective-permute-done((bf16[16,1152]{1,0:T(8,128)(2,1)S(1)}, bf16[16,1152]{1,0:T(8,128)(2,1)S(1)}, u32[]{:S(2)}, u32[]{:S(2)}) %collective-permute-start.12) | collective-permute-done | bytes 36896 | tf_op jit(solution)/shard_map/ppermute | solution.py:39
  24.1 0.8 %shard_map.56 = (f32[16,1152]{1,0:T(8,128)}, f32[16,1152]{1,0:T(8,128)}) custom-call(f32[16,1152]{1,0:T(8,128)S(1)} %get-tuple-element.21.grad_ref, f32[16,1152]{1,0:T(8,128)S(1)} %get-tuple-element.22.unit_ref, f32[16,1]{1,0:T(8,128)S(1)} %get-tuple-element.23.inverse_ref, bf16[16,1152]{1,0:T(8,128)(2,1)S(1)} %collective-permute-done.11.cross_ref, ...), custom_call_target="tpu_custom_call" | custom-call | tf_op jit(solution)/shard_map/pallas_call | solution.py:64
  (15 shorter events, 0.2 us)
Async XLA Ops:
  0.6 1.4 %copy-start.1 = (bf16[16,1152]{1,0:T(8,128)(2,1)S(1)}, bf16[16,1152]{1,0:T(8,128)(2,1)}, u32[]{:S(2)}) copy-start(bf16[16,1152]{1,0:T(8,128)(2,1)} %param.3) | copy-start | bytes 110596
  0.6 1.6 %collective-permute-start.1 = (bf16[16,1152]{1,0:T(8,128)(2,1)}, bf16[16,1152]{1,0:T(8,128)(2,1)S(1)}, u32[]{:S(2)}, u32[]{:S(2)}) collective-permute-start(bf16[16,1152]{1,0:T(8,128)(2,1)} %param.3), channel_id=1, source_target_pairs={{0,4},{4,0},{8,12},{12,8},{16,20},{20,16},{24,28},{28,24},{1,5},{5... | collective-permute-start | bytes 110600 | tf_op jit(solution)/shard_map/ppermute | solution.py:39
  1.2 1.4 %collective-permute-start = (bf16[16,1152]{1,0:T(8,128)(2,1)}, bf16[16,1152]{1,0:T(8,128)(2,1)S(1)}, u32[]{:S(2)}, u32[]{:S(2)}) collective-permute-start(bf16[16,1152]{1,0:T(8,128)(2,1)} %param.4), channel_id=1, source_target_pairs={{0,4},{4,0},{8,12},{12,8},{16,20},{20,16},{24,28},{28,24},{1,5},{5... | collective-permute-start | bytes 110600 | tf_op jit(solution)/shard_map/ppermute | solution.py:39
  2.7 10.3 %copy-start = (s32[64]{0:T(128)S(1)}, s32[64]{0:T(128)}, u32[]{:S(2)}) copy-start(s32[64]{0:T(128)} %param.5) | copy-start | bytes 772
  2.7 6.1 %collective-permute-start.3 = (bf16[32,1152]{1,0:T(8,128)(2,1)S(1)}, bf16[32,1152]{1,0:T(8,128)(2,1)S(1)}, u32[]{:S(2)}, u32[]{:S(2)}) collective-permute-start(bf16[32,1152]{1,0:T(8,128)(2,1)S(1)} %get-tuple-element.14.refs_0_), channel_id=1, source_target_pairs={{0,2},{1,3},{2,0},{3,1},{4,20},{5,21},{6,22},{7,23},{8,10},{9,11},... | collective-permute-start | bytes 221192 | tf_op jit(solution)/shard_map/ppermute | solution.py:51
  6.5 6.3 %collective-permute-start.2 = (bf16[32,1152]{1,0:T(8,128)(2,1)S(1)}, bf16[32,1152]{1,0:T(8,128)(2,1)S(1)}, u32[]{:S(2)}, u32[]{:S(2)}) collective-permute-start(bf16[32,1152]{1,0:T(8,128)(2,1)S(1)} %get-tuple-element.14.refs_0_), channel_id=1, source_target_pairs={{0,3},{1,2},{2,1},{3,0},{4,28},{5,29},{6,30},{7,31},{8,11},{9,10},... | collective-permute-start | bytes 221192 | tf_op jit(solution)/shard_map/ppermute | solution.py:51
  7.9 5.1 %collective-permute-start.4 = (bf16[32,1152]{1,0:T(8,128)(2,1)S(1)}, bf16[32,1152]{1,0:T(8,128)(2,1)S(1)}, u32[]{:S(2)}, u32[]{:S(2)}) collective-permute-start(bf16[32,1152]{1,0:T(8,128)(2,1)S(1)} %get-tuple-element.14.refs_0_), channel_id=1, source_target_pairs={{0,1},{1,0},{2,3},{3,2},{4,12},{5,13},{6,14},{7,15},{8,9},{9,8},{1... | collective-permute-start | bytes 221192 | tf_op jit(solution)/shard_map/ppermute | solution.py:51
  8.9 4.5 %collective-permute-start.6 = (bf16[32,1152]{1,0:T(8,128)(2,1)S(1)}, bf16[32,1152]{1,0:T(8,128)(2,1)S(1)}, u32[]{:S(2)}, u32[]{:S(2)}) collective-permute-start(bf16[32,1152]{1,0:T(8,128)(2,1)S(1)} %collective-permute-done.3.refs_2_), channel_id=1, source_target_pairs={{0,4},{4,0},{8,12},{12,8},{16,20},{20,16},{24,28},{28,24},{1,5},{5... | collective-permute-start | bytes 221192 | tf_op jit(solution)/shard_map/ppermute | solution.py:39
  12.8 1.3 %collective-permute-start.5 = (bf16[32,1152]{1,0:T(8,128)(2,1)S(1)}, bf16[32,1152]{1,0:T(8,128)(2,1)S(1)}, u32[]{:S(2)}, u32[]{:S(2)}) collective-permute-start(bf16[32,1152]{1,0:T(8,128)(2,1)S(1)} %collective-permute-done.2.refs_1_), channel_id=1, source_target_pairs={{0,4},{4,0},{8,12},{12,8},{16,20},{20,16},{24,28},{28,24},{1,5},{5... | collective-permute-start | bytes 221192 | tf_op jit(solution)/shard_map/ppermute | solution.py:39
  13.1 1.3 %collective-permute-start.7 = (bf16[304,128]{1,0:T(8,128)(2,1)S(1)}, bf16[304,128]{1,0:T(8,128)(2,1)S(1)}, u32[]{:S(2)}, u32[]{:S(2)}) collective-permute-start(bf16[304,128]{1,0:T(8,128)(2,1)S(1)} %shard_map.52), channel_id=1, source_target_pairs={{0,4},{4,0},{8,12},{12,8},{16,20},{20,16},{24,28},{28,24},{1,5},{5... | collective-permute-start | bytes 233480 | tf_op jit(solution)/shard_map/ppermute | solution.py:39
  15.0 6.3 %collective-permute-start.8 = (bf16[32,1152]{1,0:T(8,128)(2,1)S(1)}, bf16[32,1152]{1,0:T(8,128)(2,1)S(1)}, u32[]{:S(2)}, u32[]{:S(2)}) collective-permute-start(bf16[32,1152]{1,0:T(8,128)(2,1)S(1)} %get-tuple-element.17), channel_id=1, source_target_pairs={{0,3},{1,2},{2,1},{3,0},{4,28},{5,29},{6,30},{7,31},{8,11},{9,10},... | collective-permute-start | bytes 221192 | tf_op jit(solution)/shard_map/ppermute | solution.py:51
  17.1 5.7 %collective-permute-start.9 = (bf16[32,1152]{1,0:T(8,128)(2,1)S(1)}, bf16[32,1152]{1,0:T(8,128)(2,1)S(1)}, u32[]{:S(2)}, u32[]{:S(2)}) collective-permute-start(bf16[32,1152]{1,0:T(8,128)(2,1)S(1)} %get-tuple-element.18), channel_id=1, source_target_pairs={{0,1},{1,0},{2,3},{3,2},{4,12},{5,13},{6,14},{7,15},{8,9},{9,8},{1... | collective-permute-start | bytes 221192 | tf_op jit(solution)/shard_map/ppermute | solution.py:51
  17.1 5.8 %collective-permute-start.10 = (bf16[16,1152]{1,0:T(8,128)(2,1)S(1)}, bf16[16,1152]{1,0:T(8,128)(2,1)S(1)}, u32[]{:S(2)}, u32[]{:S(2)}) collective-permute-start(bf16[16,1152]{1,0:T(8,128)(2,1)S(1)} %get-tuple-element.20), channel_id=1, source_target_pairs={{0,2},{1,3},{2,0},{3,1},{4,20},{5,21},{6,22},{7,23},{8,10},{9,11},... | collective-permute-start | bytes 110600 | tf_op jit(solution)/shard_map/ppermute | solution.py:51
  19.4 3.7 %collective-permute-start.11 = (bf16[16,1152]{1,0:T(8,128)(2,1)S(1)}, bf16[16,1152]{1,0:T(8,128)(2,1)S(1)}, u32[]{:S(2)}, u32[]{:S(2)}) collective-permute-start(bf16[16,1152]{1,0:T(8,128)(2,1)S(1)} %get-tuple-element.24), channel_id=1, source_target_pairs={{0,6},{1,7},{2,4},{3,5},{4,16},{5,17},{6,18},{7,19},{8,14},{9,15},... | collective-permute-start | bytes 110600 | tf_op jit(solution)/shard_map/ppermute | solution.py:51
  22.8 1.3 %collective-permute-start.12 = (bf16[16,1152]{1,0:T(8,128)(2,1)S(1)}, bf16[16,1152]{1,0:T(8,128)(2,1)S(1)}, u32[]{:S(2)}, u32[]{:S(2)}) collective-permute-start(bf16[16,1152]{1,0:T(8,128)(2,1)S(1)} %get-tuple-element.25), channel_id=1, source_target_pairs={{0,4},{4,0},{8,12},{12,8},{16,20},{20,16},{24,28},{28,24},{1,5},{5... | collective-permute-start | bytes 110600 | tf_op jit(solution)/shard_map/ppermute | solution.py:39

commit v16 on v9

--- a/solution.py
+++ b/solution.py
@@ -14,7 +14,6 @@
 bf16 = jnp.bfloat16
 VMEM = pl.BlockSpec(memory_space=pltpu.VMEM)
 LONG = pl.CostEstimate(flops=10**10, bytes_accessed=10**7, transcendentals=0)
-SHORT = pl.CostEstimate(flops=2 * 10**8, bytes_accessed=10**5, transcendentals=0)
 
 
 def normalize(raw):
@@ -113,17 +112,13 @@
     return lax.dot_general(mine, other, (((1,), (1,)), ((), ())), preferred_element_type=f32)
 
 
-def most_kernel(blocks, *refs):
-    refs[-1][...] = scores_of(refs[:blocks], refs[blocks:-1])
-
-
-def rest_kernel(blocks, split, ids_ref, far_ids_ref, most_ref, *refs):
+def pair_kernel(blocks, split, ids_ref, far_ids_ref, *refs):
     mine_refs, other_refs = refs[:blocks], refs[blocks:2 * blocks]
     own_ref, same_ref, cross_ref, *send_refs = refs[2 * blocks:]
     height = own_ref.shape[0]
     rows = height // 2
     mine_ids, other_ids = side_ids(rows, ids_ref[...], far_ids_ref[...], blocks * height)
-    scores = jnp.concatenate([most_ref[...], scores_of(mine_refs, other_refs[-1:])], axis=1)
+    scores = scores_of(mine_refs, other_refs)
     coeff = pair_coeff(scale_logit * scores + shift_logit, mine_ids == other_ids)
     other = jnp.concatenate([ref[...] for ref in other_refs], axis=0)
     part = jnp.dot(coeff, other, preferred_element_type=f32)
@@ -145,7 +140,7 @@
         total = total + ref[...].astype(f32)
     even = is_even()
     keep_ref[...] = jnp.where(even, total[:rows], total[rows:])
-    send_ref[...] = jnp.where(even, total[rows:], total[:rows])
+    send_ref[...] = jnp.where(even, total[rows:], total[:rows]).astype(bf16)
 
 
 def keep_kernel(raw_ref, keep_ref, same_ref, grad_ref, unit_ref, inverse_ref):
@@ -163,7 +158,7 @@
 
 def out_kernel(grad_ref, unit_ref, inverse_ref, cross_ref, got_ref, img_ref, txt_ref):
     even = is_even()
-    total = got_ref[...] + cross_ref[...].astype(f32)
+    total = got_ref[...].astype(f32) + cross_ref[...].astype(f32)
     keep = grad_ref[...]
     got = back_norm(unit_ref[...], inverse_ref[...], total)
     txt_ref[...] = jnp.where(even, keep, got)
@@ -184,25 +179,18 @@
     mine, other = call(sides_kernel, [pair] * 2, [near, far_txt, far_img])
     order = list(range(blocks - 1, 0, -1))
     mine = [mine] + [chip_swap(mine, k) for k in order]
-    other = [other] + [core_swap(block) for block in mine[1:]]
-    count = blocks * 2 * rows
-    (most,) = call(
-        functools.partial(most_kernel, blocks),
-        [jax.ShapeDtypeStruct((count, count - 2 * rows), f32)],
-        [*mine, *other[:-1]],
-        cost=SHORT,
-    )
+    other = [other, *[core_swap(block) for block in mine[1:-1]], chip_swap(mine[0], 1, cross=1)]
     split = min(2, blocks - 1)
     own, same, cross, *send = call(
-        functools.partial(rest_kernel, blocks, split),
+        functools.partial(pair_kernel, blocks, split),
         [total] + [piece] * 2 + [pair] * (blocks - 2),
-        [ids, core_swap(ids), most, *mine, *other],
+        [ids, core_swap(ids), *mine, *other],
     )
     far = order.pop(split - 1)
     got = [chip_swap(block, k) for k, block in zip(order, send)]
     same = chip_swap(same, far)
     cross = chip_swap(cross, far, cross=1)
-    keep, send = call(sum_kernel, [single] * 2, [own, *got])
+    keep, send = call(sum_kernel, [single, piece], [own, *got])
     got = core_swap(send)
     column = jax.ShapeDtypeStruct((rows, 1), f32)
     kept = call(keep_kernel, [single, single, column], [near, keep, same], cost=LONG)

time: 22.8 us -> 23.1 us (1.013)
  starting transfers between devices: 12 us -> 12.9 us
  Pallas kernels: 1.92 us -> 1.66 us
  waiting for transfers between devices: 7.19 us -> 6.95 us
    ppermute x7 -> x8, starting transfers between devices: 9.32 us -> 11.2 us  [chip_swap(): return lax.ppermute(block, ('img', 'txt'), pairs)]
    ppermute x7 -> x6, starting transfers between devices: 2.7 us -> 1.63 us  [core_swap(): return lax.ppermute(block, 'img', [(i, i ^ 1) for i in range(size)])]
    ppermute x7 -> x8, waiting for transfers between devices: 5.64 us -> 5.26 us  [chip_swap(): return lax.ppermute(block, ('img', 'txt'), pairs)]
    pallas_call x6 -> x5, Pallas kernels: 1.92 us -> 1.66 us  [call(): pl.pallas_call(kernel, out_shape=outs, in_specs=[VMEM] * len(args), out_s...]
    ppermute x7 -> x6, waiting for transfers between devices: 1.54 us -> 1.69 us  [core_swap(): return lax.ppermute(block, 'img', [(i, i ^ 1) for i in range(size)])]
  transfers between devices with their start and end apart: 14 -> 14, of which waited for: 10 -> 9; matrix products, arithmetic and copies ran while one was open for 3% -> 3% of each run, Pallas kernels for 2% -> 1%
where the time goes in v16:
time: 23.1 us; the launch traced here: 22.9 us
  starting transfers between devices  12.9 us (56%)
  waiting for transfers between devices  6.95 us (30%)
  Pallas kernels  1.66 us (7%)
  local copies, waits for them, and re-layouts  0.79 us (3%)
  between operations  0.69 us (3%)
    ppermute x8, starting transfers between devices, chip_swap(): return lax.ppermute(block, ('img', 'txt'), pairs)  11.2 us
    ppermute x8, waiting for transfers between devices, chip_swap(): return lax.ppermute(block, ('img', 'txt'), pairs)  5.26 us
    ppermute x6, waiting for transfers between devices, core_swap(): return lax.ppermute(block, 'img', [(i, i ^ 1) for i in range(size)])  1.69 us
    pallas_call x5, Pallas kernels, call(): pl.pallas_call(kernel, out_shape=outs, in_specs=[VMEM] * len(args), out_s...  1.66 us
    ppermute x6, starting transfers between devices, core_swap(): return lax.ppermute(block, 'img', [(i, i ^ 1) for i in range(size)])  1.63 us
    unnamed x5, local copies, waits for them, and re-layouts  0.78 us
  transfers between devices with their start and end apart: 14, of which 9 were waited for; matrix products, arithmetic and copies ran while one was open for 3% of the time, Pallas kernels for 1%

profile of v16, /device:TPU:0, one launch (start us, length us, event | category | flops | bytes accessed | tf_op | source)
XLA Modules:
  0.0 22.9 jit_solution(13294218222381352776)
XLA Ops:
  0.6 0.5 %collective-permute-start.2 = (bf16[16,1152]{1,0:T(8,128)(2,1)}, bf16[16,1152]{1,0:T(8,128)(2,1)S(1)}, u32[]{:S(2)}, u32[]{:S(2)}) collective-permute-start(bf16[16,1152]{1,0:T(8,128)(2,1)} %param.3), channel_id=1, source_target_pairs={{0,4},{4,0},{8,12},{12,8},{16,20},{20,16},{24,28},{28,24},{1,5},{5... | collective-permute-start | bytes 110600 | tf_op jit(solution)/shard_map/ppermute | solution.py:37
  1.2 0.8 %constant_dynamic-update-slice_fusion.1 = bf16[32,1152]{1,0:T(8,128)(2,1)S(1)} fusion(bf16[16,1152]{1,0:T(8,128)(2,1)} %param.4), kind=kLoop, calls=%fused_computation.1 | loop fusion | bytes 73728
  2.0 0.2 collective-permute-done.2.img_ref
  2.2 0.3 %collective-permute-done.1.txt_ref = bf16[16,1152]{1,0:T(8,128)(2,1)S(1)} collective-permute-done((bf16[16,1152]{1,0:T(8,128)(2,1)}, bf16[16,1152]{1,0:T(8,128)(2,1)S(1)}, u32[]{:S(2)}, u32[]{:S(2)}) %collective-permute-start.1) | collective-permute-done | bytes 36896 | tf_op jit(solution)/shard_map/ppermute | solution.py:37
  2.6 0.1 shard_map.50
  2.7 2.7 %collective-permute-start.4 = (bf16[32,1152]{1,0:T(8,128)(2,1)S(1)}, bf16[32,1152]{1,0:T(8,128)(2,1)S(1)}, u32[]{:S(2)}, u32[]{:S(2)}) collective-permute-start(bf16[32,1152]{1,0:T(8,128)(2,1)S(1)} %get-tuple-element.14.refs_0_), channel_id=1, source_target_pairs={{0,16},{1,17},{2,18},{3,19},{4,6},{5,7},{6,4},{7,5},{8,24},{9,25},... | collective-permute-start | bytes 221192 | tf_op jit(solution)/shard_map/ppermute | solution.py:49
  5.5 1.4 %collective-permute-start.3 = (bf16[32,1152]{1,0:T(8,128)(2,1)S(1)}, bf16[32,1152]{1,0:T(8,128)(2,1)S(1)}, u32[]{:S(2)}, u32[]{:S(2)}) collective-permute-start(bf16[32,1152]{1,0:T(8,128)(2,1)S(1)} %get-tuple-element.14.refs_0_), channel_id=1, source_target_pairs={{0,24},{1,25},{2,26},{3,27},{4,7},{5,6},{6,5},{7,4},{8,16},{9,17},... | collective-permute-start | bytes 221192 | tf_op jit(solution)/shard_map/ppermute | solution.py:49
  6.9 1.9 %collective-permute-start.8 = (bf16[32,1152]{1,0:T(8,128)(2,1)S(1)}, bf16[32,1152]{1,0:T(8,128)(2,1)S(1)}, u32[]{:S(2)}, u32[]{:S(2)}) collective-permute-start(bf16[32,1152]{1,0:T(8,128)(2,1)S(1)} %get-tuple-element.14.refs_0_), channel_id=1, source_target_pairs={{0,12},{1,13},{2,14},{3,15},{4,1},{5,0},{6,3},{7,2},{8,4},{9,5},{1... | collective-permute-start | bytes 221192 | tf_op jit(solution)/shard_map/ppermute | solution.py:49
  8.8 0.5 %collective-permute-start.5 = (bf16[32,1152]{1,0:T(8,128)(2,1)S(1)}, bf16[32,1152]{1,0:T(8,128)(2,1)S(1)}, u32[]{:S(2)}, u32[]{:S(2)}) collective-permute-start(bf16[32,1152]{1,0:T(8,128)(2,1)S(1)} %get-tuple-element.14.refs_0_), channel_id=1, source_target_pairs={{0,8},{1,9},{2,10},{3,11},{4,5},{5,4},{6,7},{7,6},{8,0},{9,1},{10,... | collective-permute-start | bytes 221192 | tf_op jit(solution)/shard_map/ppermute | solution.py:49
  9.3 1.4 %collective-permute-done.3.refs_1_ = bf16[32,1152]{1,0:T(8,128)(2,1)S(1)} collective-permute-done((bf16[32,1152]{1,0:T(8,128)(2,1)S(1)}, bf16[32,1152]{1,0:T(8,128)(2,1)S(1)}, u32[]{:S(2)}, u32[]{:S(2)}) %collective-permute-start.3) | collective-permute-done | bytes 73760 | tf_op jit(solution)/shard_map/ppermute | solution.py:49
  10.7 1.0 %collective-permute-start.6 = (bf16[32,1152]{1,0:T(8,128)(2,1)S(1)}, bf16[32,1152]{1,0:T(8,128)(2,1)S(1)}, u32[]{:S(2)}, u32[]{:S(2)}) collective-permute-start(bf16[32,1152]{1,0:T(8,128)(2,1)S(1)} %collective-permute-done.3.refs_1_), channel_id=1, source_target_pairs={{0,4},{4,0},{8,12},{12,8},{16,20},{20,16},{24,28},{28,24},{1,5},{5... | collective-permute-start | bytes 221192 | tf_op jit(solution)/shard_map/ppermute | solution.py:37
  11.7 1.1 %collective-permute-done.far_ids_ref = s32[1,64]{1,0:T(1,128)S(1)} collective-permute-done((s32[1,64]{1,0:T(1,128)S(1)}, s32[1,64]{1,0:T(1,128)S(1)}, u32[]{:S(2)}, u32[]{:S(2)}) %collective-permute-start) | collective-permute-done | bytes 288 | tf_op jit(solution)/shard_map/ppermute | solution.py:37
  12.8 0.3 %collective-permute-done.5.refs_3_ = bf16[32,1152]{1,0:T(8,128)(2,1)S(1)} collective-permute-done((bf16[32,1152]{1,0:T(8,128)(2,1)S(1)}, bf16[32,1152]{1,0:T(8,128)(2,1)S(1)}, u32[]{:S(2)}, u32[]{:S(2)}) %collective-permute-start.5) | collective-permute-done | bytes 73760 | tf_op jit(solution)/shard_map/ppermute | solution.py:49
  13.2 0.5 %shard_map.51 = (f32[32,1152]{1,0:T(8,128)S(1)}, bf16[16,1152]{1,0:T(8,128)(2,1)S(1)}, bf16[16,1152]{1,0:T(8,128)(2,1)S(1)}, bf16[32,1152]{1,0:T(8,128)(2,1)S(1)}, bf16[32,1152]{1,0:T(8,128)(2,1)S(1)}) custom-call(s32[1,64]{1,0:T(1,128)S(1)} %bitcast.2, s32[1,64]{1,0:T(1,128)S(1)} %collective-permute-done.far_ids_ref, ...), custom_call_target="tpu_custom_call" | custom-call | tf_op jit(solution)/shard_map/pallas_call | solution.py:58
  13.7 2.2 %collective-permute-start.9 = (bf16[32,1152]{1,0:T(8,128)(2,1)S(1)}, bf16[32,1152]{1,0:T(8,128)(2,1)S(1)}, u32[]{:S(2)}, u32[]{:S(2)}) collective-permute-start(bf16[32,1152]{1,0:T(8,128)(2,1)S(1)} %get-tuple-element.17), channel_id=1, source_target_pairs={{0,24},{1,25},{2,26},{3,27},{4,7},{5,6},{6,5},{7,4},{8,16},{9,17},... | collective-permute-start | bytes 221192 | tf_op jit(solution)/shard_map/ppermute | solution.py:49
  15.9 0.8 %collective-permute-start.10 = (bf16[32,1152]{1,0:T(8,128)(2,1)S(1)}, bf16[32,1152]{1,0:T(8,128)(2,1)S(1)}, u32[]{:S(2)}, u32[]{:S(2)}) collective-permute-start(bf16[32,1152]{1,0:T(8,128)(2,1)S(1)} %get-tuple-element.18), channel_id=1, source_target_pairs={{0,8},{1,9},{2,10},{3,11},{4,5},{5,4},{6,7},{7,6},{8,0},{9,1},{10,... | collective-permute-start | bytes 221192 | tf_op jit(solution)/shard_map/ppermute | solution.py:49
  16.7 0.5 %collective-permute-start.11 = (bf16[16,1152]{1,0:T(8,128)(2,1)S(1)}, bf16[16,1152]{1,0:T(8,128)(2,1)S(1)}, u32[]{:S(2)}, u32[]{:S(2)}) collective-permute-start(bf16[16,1152]{1,0:T(8,128)(2,1)S(1)} %get-tuple-element.20), channel_id=1, source_target_pairs={{0,16},{1,17},{2,18},{3,19},{4,6},{5,7},{6,4},{7,5},{8,24},{9,25},... | collective-permute-start | bytes 110600 | tf_op jit(solution)/shard_map/ppermute | solution.py:49
  17.3 1.1 %collective-permute-start.12 = (bf16[16,1152]{1,0:T(8,128)(2,1)S(1)}, bf16[16,1152]{1,0:T(8,128)(2,1)S(1)}, u32[]{:S(2)}, u32[]{:S(2)}) collective-permute-start(bf16[16,1152]{1,0:T(8,128)(2,1)S(1)} %get-tuple-element.24), channel_id=1, source_target_pairs={{0,20},{1,21},{2,22},{3,23},{4,2},{5,3},{6,0},{7,1},{8,28},{9,29},... | collective-permute-start | bytes 110600 | tf_op jit(solution)/shard_map/ppermute | solution.py:49
  18.3 0.7 %collective-permute-done.9.refs_0_ = bf16[32,1152]{1,0:T(8,128)(2,1)S(1)} collective-permute-done((bf16[32,1152]{1,0:T(8,128)(2,1)S(1)}, bf16[32,1152]{1,0:T(8,128)(2,1)S(1)}, u32[]{:S(2)}, u32[]{:S(2)}) %collective-permute-start.9) | collective-permute-done | bytes 73760 | tf_op jit(solution)/shard_map/ppermute | solution.py:49
  19.0 1.2 %collective-permute-done.10.refs_1_ = bf16[32,1152]{1,0:T(8,128)(2,1)S(1)} collective-permute-done((bf16[32,1152]{1,0:T(8,128)(2,1)S(1)}, bf16[32,1152]{1,0:T(8,128)(2,1)S(1)}, u32[]{:S(2)}, u32[]{:S(2)}) %collective-permute-start.10) | collective-permute-done | bytes 73760 | tf_op jit(solution)/shard_map/ppermute | solution.py:49
  20.4 0.3 %collective-permute-done.11.same_ref = bf16[16,1152]{1,0:T(8,128)(2,1)S(1)} collective-permute-done((bf16[16,1152]{1,0:T(8,128)(2,1)S(1)}, bf16[16,1152]{1,0:T(8,128)(2,1)S(1)}, u32[]{:S(2)}, u32[]{:S(2)}) %collective-permute-start.11) | collective-permute-done | bytes 36896 | tf_op jit(solution)/shard_map/ppermute | solution.py:49
  20.7 0.2 shard_map.53
  20.9 1.3 %collective-permute-done.12.cross_ref = bf16[16,1152]{1,0:T(8,128)(2,1)S(1)} collective-permute-done((bf16[16,1152]{1,0:T(8,128)(2,1)S(1)}, bf16[16,1152]{1,0:T(8,128)(2,1)S(1)}, u32[]{:S(2)}, u32[]{:S(2)}) %collective-permute-start.12) | collective-permute-done | bytes 36896 | tf_op jit(solution)/shard_map/ppermute | solution.py:49
  22.2 0.8 %shard_map.54 = (f32[16,1152]{1,0:T(8,128)}, f32[16,1152]{1,0:T(8,128)}) custom-call(f32[16,1152]{1,0:T(8,128)S(1)} %get-tuple-element.21.grad_ref, f32[16,1152]{1,0:T(8,128)S(1)} %get-tuple-element.22.unit_ref, f32[16,1]{1,0:T(8,128)S(1)} %get-tuple-element.23.inverse_ref, bf16[16,1152]{1,0:T(8,128)(2,1)S(1)} %collective-permute-done.12.cross_ref, ...), custom_call_target="tpu_custom_call" | custom-call | tf_op jit(solution)/shard_map/pallas_call | solution.py:58
  (15 shorter events, 0.2 us)
Async XLA Ops:
  0.6 1.4 %copy-start.1 = (bf16[16,1152]{1,0:T(8,128)(2,1)S(1)}, bf16[16,1152]{1,0:T(8,128)(2,1)}, u32[]{:S(2)}) copy-start(bf16[16,1152]{1,0:T(8,128)(2,1)} %param.3) | copy-start | bytes 110596
  0.6 1.6 %collective-permute-start.2 = (bf16[16,1152]{1,0:T(8,128)(2,1)}, bf16[16,1152]{1,0:T(8,128)(2,1)S(1)}, u32[]{:S(2)}, u32[]{:S(2)}) collective-permute-start(bf16[16,1152]{1,0:T(8,128)(2,1)} %param.3), channel_id=1, source_target_pairs={{0,4},{4,0},{8,12},{12,8},{16,20},{20,16},{24,28},{28,24},{1,5},{5... | collective-permute-start | bytes 110600 | tf_op jit(solution)/shard_map/ppermute | solution.py:37
  1.2 1.4 %collective-permute-start.1 = (bf16[16,1152]{1,0:T(8,128)(2,1)}, bf16[16,1152]{1,0:T(8,128)(2,1)S(1)}, u32[]{:S(2)}, u32[]{:S(2)}) collective-permute-start(bf16[16,1152]{1,0:T(8,128)(2,1)} %param.4), channel_id=1, source_target_pairs={{0,4},{4,0},{8,12},{12,8},{16,20},{20,16},{24,28},{28,24},{1,5},{5... | collective-permute-start | bytes 110600 | tf_op jit(solution)/shard_map/ppermute | solution.py:37
  2.7 9.0 %copy-start = (s32[64]{0:T(128)S(1)}, s32[64]{0:T(128)}, u32[]{:S(2)}) copy-start(s32[64]{0:T(128)} %param.5) | copy-start | bytes 772
  2.7 6.6 %collective-permute-start.4 = (bf16[32,1152]{1,0:T(8,128)(2,1)S(1)}, bf16[32,1152]{1,0:T(8,128)(2,1)S(1)}, u32[]{:S(2)}, u32[]{:S(2)}) collective-permute-start(bf16[32,1152]{1,0:T(8,128)(2,1)S(1)} %get-tuple-element.14.refs_0_), channel_id=1, source_target_pairs={{0,16},{1,17},{2,18},{3,19},{4,6},{5,7},{6,4},{7,5},{8,24},{9,25},... | collective-permute-start | bytes 221192 | tf_op jit(solution)/shard_map/ppermute | solution.py:49
  5.5 5.3 %collective-permute-start.3 = (bf16[32,1152]{1,0:T(8,128)(2,1)S(1)}, bf16[32,1152]{1,0:T(8,128)(2,1)S(1)}, u32[]{:S(2)}, u32[]{:S(2)}) collective-permute-start(bf16[32,1152]{1,0:T(8,128)(2,1)S(1)} %get-tuple-element.14.refs_0_), channel_id=1, source_target_pairs={{0,24},{1,25},{2,26},{3,27},{4,7},{5,6},{6,5},{7,4},{8,16},{9,17},... | collective-permute-start | bytes 221192 | tf_op jit(solution)/shard_map/ppermute | solution.py:49
  6.9 5.9 %collective-permute-start.8 = (bf16[32,1152]{1,0:T(8,128)(2,1)S(1)}, bf16[32,1152]{1,0:T(8,128)(2,1)S(1)}, u32[]{:S(2)}, u32[]{:S(2)}) collective-permute-start(bf16[32,1152]{1,0:T(8,128)(2,1)S(1)} %get-tuple-element.14.refs_0_), channel_id=1, source_target_pairs={{0,12},{1,13},{2,14},{3,15},{4,1},{5,0},{6,3},{7,2},{8,4},{9,5},{1... | collective-permute-start | bytes 221192 | tf_op jit(solution)/shard_map/ppermute | solution.py:49
  8.8 4.4 %collective-permute-start.5 = (bf16[32,1152]{1,0:T(8,128)(2,1)S(1)}, bf16[32,1152]{1,0:T(8,128)(2,1)S(1)}, u32[]{:S(2)}, u32[]{:S(2)}) collective-permute-start(bf16[32,1152]{1,0:T(8,128)(2,1)S(1)} %get-tuple-element.14.refs_0_), channel_id=1, source_target_pairs={{0,8},{1,9},{2,10},{3,11},{4,5},{5,4},{6,7},{7,6},{8,0},{9,1},{10,... | collective-permute-start | bytes 221192 | tf_op jit(solution)/shard_map/ppermute | solution.py:49
  9.3 3.8 %collective-permute-start.7 = (bf16[32,1152]{1,0:T(8,128)(2,1)S(1)}, bf16[32,1152]{1,0:T(8,128)(2,1)S(1)}, u32[]{:S(2)}, u32[]{:S(2)}) collective-permute-start(bf16[32,1152]{1,0:T(8,128)(2,1)S(1)} %collective-permute-done.4.refs_2_), channel_id=1, source_target_pairs={{0,4},{4,0},{8,12},{12,8},{16,20},{20,16},{24,28},{28,24},{1,5},{5... | collective-permute-start | bytes 221192 | tf_op jit(solution)/shard_map/ppermute | solution.py:37
  10.7 2.4 %collective-permute-start.6 = (bf16[32,1152]{1,0:T(8,128)(2,1)S(1)}, bf16[32,1152]{1,0:T(8,128)(2,1)S(1)}, u32[]{:S(2)}, u32[]{:S(2)}) collective-permute-start(bf16[32,1152]{1,0:T(8,128)(2,1)S(1)} %collective-permute-done.3.refs_1_), channel_id=1, source_target_pairs={{0,4},{4,0},{8,12},{12,8},{16,20},{20,16},{24,28},{28,24},{1,5},{5... | collective-permute-start | bytes 221192 | tf_op jit(solution)/shard_map/ppermute | solution.py:37
  11.7 1.1 %collective-permute-start = (s32[1,64]{1,0:T(1,128)S(1)}, s32[1,64]{1,0:T(1,128)S(1)}, u32[]{:S(2)}, u32[]{:S(2)}) collective-permute-start(s32[1,64]{1,0:T(1,128)S(1)} %bitcast.1), channel_id=1, source_target_pairs={{0,4},{4,0},{8,12},{12,8},{16,20},{20,16},{24,28},{28,24},{1,5},{5... | collective-permute-start | bytes 776 | tf_op jit(solution)/shard_map/ppermute | solution.py:37
  13.7 5.3 %collective-permute-start.9 = (bf16[32,1152]{1,0:T(8,128)(2,1)S(1)}, bf16[32,1152]{1,0:T(8,128)(2,1)S(1)}, u32[]{:S(2)}, u32[]{:S(2)}) collective-permute-start(bf16[32,1152]{1,0:T(8,128)(2,1)S(1)} %get-tuple-element.17), channel_id=1, source_target_pairs={{0,24},{1,25},{2,26},{3,27},{4,7},{5,6},{6,5},{7,4},{8,16},{9,17},... | collective-permute-start | bytes 221192 | tf_op jit(solution)/shard_map/ppermute | solution.py:49
  15.9 4.4 %collective-permute-start.10 = (bf16[32,1152]{1,0:T(8,128)(2,1)S(1)}, bf16[32,1152]{1,0:T(8,128)(2,1)S(1)}, u32[]{:S(2)}, u32[]{:S(2)}) collective-permute-start(bf16[32,1152]{1,0:T(8,128)(2,1)S(1)} %get-tuple-element.18), channel_id=1, source_target_pairs={{0,8},{1,9},{2,10},{3,11},{4,5},{5,4},{6,7},{7,6},{8,0},{9,1},{10,... | collective-permute-start | bytes 221192 | tf_op jit(solution)/shard_map/ppermute | solution.py:49
  16.7 4.0 %collective-permute-start.11 = (bf16[16,1152]{1,0:T(8,128)(2,1)S(1)}, bf16[16,1152]{1,0:T(8,128)(2,1)S(1)}, u32[]{:S(2)}, u32[]{:S(2)}) collective-permute-start(bf16[16,1152]{1,0:T(8,128)(2,1)S(1)} %get-tuple-element.20), channel_id=1, source_target_pairs={{0,16},{1,17},{2,18},{3,19},{4,6},{5,7},{6,4},{7,5},{8,24},{9,25},... | collective-permute-start | bytes 110600 | tf_op jit(solution)/shard_map/ppermute | solution.py:49
  17.3 4.9 %collective-permute-start.12 = (bf16[16,1152]{1,0:T(8,128)(2,1)S(1)}, bf16[16,1152]{1,0:T(8,128)(2,1)S(1)}, u32[]{:S(2)}, u32[]{:S(2)}) collective-permute-start(bf16[16,1152]{1,0:T(8,128)(2,1)S(1)} %get-tuple-element.24), channel_id=1, source_target_pairs={{0,20},{1,21},{2,22},{3,23},{4,2},{5,3},{6,0},{7,1},{8,28},{9,29},... | collective-permute-start | bytes 110600 | tf_op jit(solution)/shard_map/ppermute | solution.py:49
  20.3 1.9 %collective-permute-start.13 = (bf16[16,1152]{1,0:T(8,128)(2,1)S(1)}, bf16[16,1152]{1,0:T(8,128)(2,1)S(1)}, u32[]{:S(2)}, u32[]{:S(2)}) collective-permute-start(bf16[16,1152]{1,0:T(8,128)(2,1)S(1)} %get-tuple-element.25), channel_id=1, source_target_pairs={{0,4},{4,0},{8,12},{12,8},{16,20},{20,16},{24,28},{28,24},{1,5},{5... | collective-permute-start | bytes 110600 | tf_op jit(solution)/shard_map/ppermute | solution.py:37

commit v17 on v16

--- a/solution.py
+++ b/solution.py
@@ -143,26 +143,19 @@
     send_ref[...] = jnp.where(even, total[rows:], total[:rows]).astype(bf16)
 
 
-def keep_kernel(raw_ref, keep_ref, same_ref, grad_ref, unit_ref, inverse_ref):
+def unit_kernel(raw_ref, cross_ref, unit_ref, inverse_ref, rest_ref):
+    unit_ref[...], inverse_ref[...] = normalize(raw_ref[...])
+    rest_ref[...] = cross_ref[...].astype(f32)
+
+
+def out_kernel(unit_ref, inverse_ref, rest_ref, keep_ref, same_ref, got_ref, img_ref, txt_ref):
     rows = keep_ref.shape[0]
     even = is_even()
-    unit, inverse = normalize(raw_ref[...])
-    grad_ref[...] = back_norm(
-        jnp.where(even, unit[:rows], unit[rows:]),
-        jnp.where(even, inverse[:rows], inverse[rows:]),
-        keep_ref[...] + same_ref[...].astype(f32),
-    )
-    unit_ref[...] = jnp.where(even, unit[rows:], unit[:rows])
-    inverse_ref[...] = jnp.where(even, inverse[rows:], inverse[:rows])
-
-
-def out_kernel(grad_ref, unit_ref, inverse_ref, cross_ref, got_ref, img_ref, txt_ref):
-    even = is_even()
-    total = got_ref[...].astype(f32) + cross_ref[...].astype(f32)
-    keep = grad_ref[...]
-    got = back_norm(unit_ref[...], inverse_ref[...], total)
-    txt_ref[...] = jnp.where(even, keep, got)
-    img_ref[...] = jnp.where(even, got, keep)
+    keep = keep_ref[...] + same_ref[...].astype(f32)
+    got = got_ref[...].astype(f32) + rest_ref[...]
+    unit, inverse = unit_ref[...], inverse_ref[...]
+    txt_ref[...] = back_norm(unit[:rows], inverse[:rows], jnp.where(even, keep, got))
+    img_ref[...] = back_norm(unit[rows:], inverse[rows:], jnp.where(even, got, keep))
 
 
 def local(image_embeds, text_embeds, pair_ids):
@@ -188,13 +181,13 @@
     )
     far = order.pop(split - 1)
     got = [chip_swap(block, k) for k, block in zip(order, send)]
+    cross = chip_swap(cross, far, cross=1)
     same = chip_swap(same, far)
-    cross = chip_swap(cross, far, cross=1)
     keep, send = call(sum_kernel, [single, piece], [own, *got])
     got = core_swap(send)
-    column = jax.ShapeDtypeStruct((rows, 1), f32)
-    kept = call(keep_kernel, [single, single, column], [near, keep, same], cost=LONG)
-    return tuple(call(out_kernel, [single] * 2, [*kept, cross, got]))
+    column = jax.ShapeDtypeStruct((2 * rows, 1), f32)
+    ready = call(unit_kernel, [total, column, single], [near, cross], cost=LONG)
+    return tuple(call(out_kernel, [single] * 2, [*ready, keep, same, got]))
 
 
 def solution(mesh):

time: 23.1 us -> 22.7 us (0.983)
  starting transfers between devices: 12.9 us -> 12.5 us
    ppermute x8, starting transfers between devices: 11.2 us -> 10.8 us  [chip_swap(): return lax.ppermute(block, ('img', 'txt'), pairs)]
    ppermute x8, waiting for transfers between devices: 5.26 us -> 5.02 us  [chip_swap(): return lax.ppermute(block, ('img', 'txt'), pairs)]
where the time goes in v17:
time: 22.7 us; the launch traced here: 22.3 us
  starting transfers between devices  12.5 us (55%)
  waiting for transfers between devices  6.81 us (30%)
  Pallas kernels  1.57 us (7%)
  local copies, waits for them, and re-layouts  0.79 us (3%)
  between operations  0.7 us (3%)
    ppermute x8, starting transfers between devices, chip_swap(): return lax.ppermute(block, ('img', 'txt'), pairs)  10.8 us
    ppermute x8, waiting for transfers between devices, chip_swap(): return lax.ppermute(block, ('img', 'txt'), pairs)  5.02 us
    ppermute x6, waiting for transfers between devices, core_swap(): return lax.ppermute(block, 'img', [(i, i ^ 1) for i in range(size)])  1.79 us
    ppermute x6, starting transfers between devices, core_swap(): return lax.ppermute(block, 'img', [(i, i ^ 1) for i in range(size)])  1.63 us
    pallas_call x5, Pallas kernels, call(): pl.pallas_call(kernel, out_shape=outs, in_specs=[VMEM] * len(args), out_s...  1.57 us
    unnamed x5, local copies, waits for them, and re-layouts  0.78 us
  transfers between devices with their start and end apart: 14, of which 9 were waited for; matrix products, arithmetic and copies ran while one was open for 3% of the time, Pallas kernels for 1%

profile of v17, /device:TPU:0, one launch (start us, length us, event | category | flops | bytes accessed | tf_op | source)
XLA Modules:
  0.0 22.3 jit_solution(5139687351034258445)
XLA Ops:
  0.6 0.5 %collective-permute-start.2 = (bf16[16,1152]{1,0:T(8,128)(2,1)}, bf16[16,1152]{1,0:T(8,128)(2,1)S(1)}, u32[]{:S(2)}, u32[]{:S(2)}) collective-permute-start(bf16[16,1152]{1,0:T(8,128)(2,1)} %param.3), channel_id=1, source_target_pairs={{0,4},{4,0},{8,12},{12,8},{16,20},{20,16},{24,28},{28,24},{1,5},{5... | collective-permute-start | bytes 110600 | tf_op jit(solution)/shard_map/ppermute | solution.py:37
  1.2 0.1 collective-permute-start.1
  1.2 0.8 %constant_dynamic-update-slice_fusion.1 = bf16[32,1152]{1,0:T(8,128)(2,1)S(1)} fusion(bf16[16,1152]{1,0:T(8,128)(2,1)} %param.4), kind=kLoop, calls=%fused_computation.1 | loop fusion | bytes 73728
  2.0 0.2 collective-permute-done.2.img_ref
  2.2 0.3 %collective-permute-done.1.txt_ref = bf16[16,1152]{1,0:T(8,128)(2,1)S(1)} collective-permute-done((bf16[16,1152]{1,0:T(8,128)(2,1)}, bf16[16,1152]{1,0:T(8,128)(2,1)S(1)}, u32[]{:S(2)}, u32[]{:S(2)}) %collective-permute-start.1) | collective-permute-done | bytes 36896 | tf_op jit(solution)/shard_map/ppermute | solution.py:37
  2.6 0.1 shard_map.50
  2.7 2.7 %collective-permute-start.4 = (bf16[32,1152]{1,0:T(8,128)(2,1)S(1)}, bf16[32,1152]{1,0:T(8,128)(2,1)S(1)}, u32[]{:S(2)}, u32[]{:S(2)}) collective-permute-start(bf16[32,1152]{1,0:T(8,128)(2,1)S(1)} %get-tuple-element.14.refs_0_), channel_id=1, source_target_pairs={{0,16},{1,17},{2,18},{3,19},{4,6},{5,7},{6,4},{7,5},{8,24},{9,25},... | collective-permute-start | bytes 221192 | tf_op jit(solution)/shard_map/ppermute | solution.py:49
  5.5 1.4 %collective-permute-start.3 = (bf16[32,1152]{1,0:T(8,128)(2,1)S(1)}, bf16[32,1152]{1,0:T(8,128)(2,1)S(1)}, u32[]{:S(2)}, u32[]{:S(2)}) collective-permute-start(bf16[32,1152]{1,0:T(8,128)(2,1)S(1)} %get-tuple-element.14.refs_0_), channel_id=1, source_target_pairs={{0,24},{1,25},{2,26},{3,27},{4,7},{5,6},{6,5},{7,4},{8,16},{9,17},... | collective-permute-start | bytes 221192 | tf_op jit(solution)/shard_map/ppermute | solution.py:49
  6.9 1.9 %collective-permute-start.8 = (bf16[32,1152]{1,0:T(8,128)(2,1)S(1)}, bf16[32,1152]{1,0:T(8,128)(2,1)S(1)}, u32[]{:S(2)}, u32[]{:S(2)}) collective-permute-start(bf16[32,1152]{1,0:T(8,128)(2,1)S(1)} %get-tuple-element.14.refs_0_), channel_id=1, source_target_pairs={{0,12},{1,13},{2,14},{3,15},{4,1},{5,0},{6,3},{7,2},{8,4},{9,5},{1... | collective-permute-start | bytes 221192 | tf_op jit(solution)/shard_map/ppermute | solution.py:49
  8.8 0.5 %collective-permute-start.5 = (bf16[32,1152]{1,0:T(8,128)(2,1)S(1)}, bf16[32,1152]{1,0:T(8,128)(2,1)S(1)}, u32[]{:S(2)}, u32[]{:S(2)}) collective-permute-start(bf16[32,1152]{1,0:T(8,128)(2,1)S(1)} %get-tuple-element.14.refs_0_), channel_id=1, source_target_pairs={{0,8},{1,9},{2,10},{3,11},{4,5},{5,4},{6,7},{7,6},{8,0},{9,1},{10,... | collective-permute-start | bytes 221192 | tf_op jit(solution)/shard_map/ppermute | solution.py:49
  9.3 1.4 %collective-permute-done.3.refs_1_ = bf16[32,1152]{1,0:T(8,128)(2,1)S(1)} collective-permute-done((bf16[32,1152]{1,0:T(8,128)(2,1)S(1)}, bf16[32,1152]{1,0:T(8,128)(2,1)S(1)}, u32[]{:S(2)}, u32[]{:S(2)}) %collective-permute-start.3) | collective-permute-done | bytes 73760 | tf_op jit(solution)/shard_map/ppermute | solution.py:49
  10.7 1.0 %collective-permute-start.6 = (bf16[32,1152]{1,0:T(8,128)(2,1)S(1)}, bf16[32,1152]{1,0:T(8,128)(2,1)S(1)}, u32[]{:S(2)}, u32[]{:S(2)}) collective-permute-start(bf16[32,1152]{1,0:T(8,128)(2,1)S(1)} %collective-permute-done.3.refs_1_), channel_id=1, source_target_pairs={{0,4},{4,0},{8,12},{12,8},{16,20},{20,16},{24,28},{28,24},{1,5},{5... | collective-permute-start | bytes 221192 | tf_op jit(solution)/shard_map/ppermute | solution.py:37
  11.7 1.1 %collective-permute-done.far_ids_ref = s32[1,64]{1,0:T(1,128)S(1)} collective-permute-done((s32[1,64]{1,0:T(1,128)S(1)}, s32[1,64]{1,0:T(1,128)S(1)}, u32[]{:S(2)}, u32[]{:S(2)}) %collective-permute-start) | collective-permute-done | bytes 288 | tf_op jit(solution)/shard_map/ppermute | solution.py:37
  12.8 0.3 %collective-permute-done.5.refs_3_ = bf16[32,1152]{1,0:T(8,128)(2,1)S(1)} collective-permute-done((bf16[32,1152]{1,0:T(8,128)(2,1)S(1)}, bf16[32,1152]{1,0:T(8,128)(2,1)S(1)}, u32[]{:S(2)}, u32[]{:S(2)}) %collective-permute-start.5) | collective-permute-done | bytes 73760 | tf_op jit(solution)/shard_map/ppermute | solution.py:49
  13.2 0.5 %shard_map.51 = (f32[32,1152]{1,0:T(8,128)S(1)}, bf16[16,1152]{1,0:T(8,128)(2,1)S(1)}, bf16[16,1152]{1,0:T(8,128)(2,1)S(1)}, bf16[32,1152]{1,0:T(8,128)(2,1)S(1)}, bf16[32,1152]{1,0:T(8,128)(2,1)S(1)}) custom-call(s32[1,64]{1,0:T(1,128)S(1)} %bitcast.2, s32[1,64]{1,0:T(1,128)S(1)} %collective-permute-done.far_ids_ref, ...), custom_call_target="tpu_custom_call" | custom-call | tf_op jit(solution)/shard_map/pallas_call | solution.py:58
  13.7 2.2 %collective-permute-start.10 = (bf16[32,1152]{1,0:T(8,128)(2,1)S(1)}, bf16[32,1152]{1,0:T(8,128)(2,1)S(1)}, u32[]{:S(2)}, u32[]{:S(2)}) collective-permute-start(bf16[32,1152]{1,0:T(8,128)(2,1)S(1)} %get-tuple-element.21), channel_id=1, source_target_pairs={{0,24},{1,25},{2,26},{3,27},{4,7},{5,6},{6,5},{7,4},{8,16},{9,17},... | collective-permute-start | bytes 221192 | tf_op jit(solution)/shard_map/ppermute | solution.py:49
  15.9 0.8 %collective-permute-start.11 = (bf16[32,1152]{1,0:T(8,128)(2,1)S(1)}, bf16[32,1152]{1,0:T(8,128)(2,1)S(1)}, u32[]{:S(2)}, u32[]{:S(2)}) collective-permute-start(bf16[32,1152]{1,0:T(8,128)(2,1)S(1)} %get-tuple-element.22), channel_id=1, source_target_pairs={{0,8},{1,9},{2,10},{3,11},{4,5},{5,4},{6,7},{7,6},{8,0},{9,1},{10,... | collective-permute-start | bytes 221192 | tf_op jit(solution)/shard_map/ppermute | solution.py:49
  16.8 1.1 %collective-permute-start.12 = (bf16[16,1152]{1,0:T(8,128)(2,1)S(1)}, bf16[16,1152]{1,0:T(8,128)(2,1)S(1)}, u32[]{:S(2)}, u32[]{:S(2)}) collective-permute-start(bf16[16,1152]{1,0:T(8,128)(2,1)S(1)} %get-tuple-element.24), channel_id=1, source_target_pairs={{0,16},{1,17},{2,18},{3,19},{4,6},{5,7},{6,4},{7,5},{8,24},{9,25},... | collective-permute-start | bytes 110600 | tf_op jit(solution)/shard_map/ppermute | solution.py:49
  17.9 1.1 %collective-permute-done.10.refs_0_ = bf16[32,1152]{1,0:T(8,128)(2,1)S(1)} collective-permute-done((bf16[32,1152]{1,0:T(8,128)(2,1)S(1)}, bf16[32,1152]{1,0:T(8,128)(2,1)S(1)}, u32[]{:S(2)}, u32[]{:S(2)}) %collective-permute-start.10) | collective-permute-done | bytes 73760 | tf_op jit(solution)/shard_map/ppermute | solution.py:49
  19.0 1.2 %collective-permute-done.11.refs_1_ = bf16[32,1152]{1,0:T(8,128)(2,1)S(1)} collective-permute-done((bf16[32,1152]{1,0:T(8,128)(2,1)S(1)}, bf16[32,1152]{1,0:T(8,128)(2,1)S(1)}, u32[]{:S(2)}, u32[]{:S(2)}) %collective-permute-start.11) | collective-permute-done | bytes 73760 | tf_op jit(solution)/shard_map/ppermute | solution.py:49
  20.4 1.0 %collective-permute-done.9.cross_ref = bf16[16,1152]{1,0:T(8,128)(2,1)S(1)} collective-permute-done((bf16[16,1152]{1,0:T(8,128)(2,1)S(1)}, bf16[16,1152]{1,0:T(8,128)(2,1)S(1)}, u32[]{:S(2)}, u32[]{:S(2)}) %collective-permute-start.9) | collective-permute-done | bytes 36896 | tf_op jit(solution)/shard_map/ppermute | solution.py:49
  21.3 0.1 shard_map.52
  21.5 0.1 collective-permute-done.13.got_ref
  21.6 0.8 %shard_map.54 = (f32[16,1152]{1,0:T(8,128)}, f32[16,1152]{1,0:T(8,128)}) custom-call(f32[32,1152]{1,0:T(8,128)S(1)} %get-tuple-element.17.unit_ref, f32[32,1]{1,0:T(8,128)S(1)} %get-tuple-element.18.inverse_ref, f32[16,1152]{1,0:T(8,128)S(1)} %get-tuple-element.19.rest_ref, f32[16,1152]{1,0:T(8,128)S(1)} %get-tuple-element.23.keep_ref, ...), custom_call_target="tpu_custom_call" | custom-call | tf_op jit(solution)/shard_map/pallas_call | solution.py:58
  (15 shorter events, 0.2 us)
Async XLA Ops:
  0.6 1.4 %copy-start.1 = (bf16[16,1152]{1,0:T(8,128)(2,1)S(1)}, bf16[16,1152]{1,0:T(8,128)(2,1)}, u32[]{:S(2)}) copy-start(bf16[16,1152]{1,0:T(8,128)(2,1)} %param.3) | copy-start | bytes 110596
  0.6 1.6 %collective-permute-start.2 = (bf16[16,1152]{1,0:T(8,128)(2,1)}, bf16[16,1152]{1,0:T(8,128)(2,1)S(1)}, u32[]{:S(2)}, u32[]{:S(2)}) collective-permute-start(bf16[16,1152]{1,0:T(8,128)(2,1)} %param.3), channel_id=1, source_target_pairs={{0,4},{4,0},{8,12},{12,8},{16,20},{20,16},{24,28},{28,24},{1,5},{5... | collective-permute-start | bytes 110600 | tf_op jit(solution)/shard_map/ppermute | solution.py:37
  1.2 1.4 %collective-permute-start.1 = (bf16[16,1152]{1,0:T(8,128)(2,1)}, bf16[16,1152]{1,0:T(8,128)(2,1)S(1)}, u32[]{:S(2)}, u32[]{:S(2)}) collective-permute-start(bf16[16,1152]{1,0:T(8,128)(2,1)} %param.4), channel_id=1, source_target_pairs={{0,4},{4,0},{8,12},{12,8},{16,20},{20,16},{24,28},{28,24},{1,5},{5... | collective-permute-start | bytes 110600 | tf_op jit(solution)/shard_map/ppermute | solution.py:37
  2.7 9.0 %copy-start = (s32[64]{0:T(128)S(1)}, s32[64]{0:T(128)}, u32[]{:S(2)}) copy-start(s32[64]{0:T(128)} %param.5) | copy-start | bytes 772
  2.7 6.6 %collective-permute-start.4 = (bf16[32,1152]{1,0:T(8,128)(2,1)S(1)}, bf16[32,1152]{1,0:T(8,128)(2,1)S(1)}, u32[]{:S(2)}, u32[]{:S(2)}) collective-permute-start(bf16[32,1152]{1,0:T(8,128)(2,1)S(1)} %get-tuple-element.14.refs_0_), channel_id=1, source_target_pairs={{0,16},{1,17},{2,18},{3,19},{4,6},{5,7},{6,4},{7,5},{8,24},{9,25},... | collective-permute-start | bytes 221192 | tf_op jit(solution)/shard_map/ppermute | solution.py:49
  5.5 5.3 %collective-permute-start.3 = (bf16[32,1152]{1,0:T(8,128)(2,1)S(1)}, bf16[32,1152]{1,0:T(8,128)(2,1)S(1)}, u32[]{:S(2)}, u32[]{:S(2)}) collective-permute-start(bf16[32,1152]{1,0:T(8,128)(2,1)S(1)} %get-tuple-element.14.refs_0_), channel_id=1, source_target_pairs={{0,24},{1,25},{2,26},{3,27},{4,7},{5,6},{6,5},{7,4},{8,16},{9,17},... | collective-permute-start | bytes 221192 | tf_op jit(solution)/shard_map/ppermute | solution.py:49
  6.9 5.9 %collective-permute-start.8 = (bf16[32,1152]{1,0:T(8,128)(2,1)S(1)}, bf16[32,1152]{1,0:T(8,128)(2,1)S(1)}, u32[]{:S(2)}, u32[]{:S(2)}) collective-permute-start(bf16[32,1152]{1,0:T(8,128)(2,1)S(1)} %get-tuple-element.14.refs_0_), channel_id=1, source_target_pairs={{0,12},{1,13},{2,14},{3,15},{4,1},{5,0},{6,3},{7,2},{8,4},{9,5},{1... | collective-permute-start | bytes 221192 | tf_op jit(solution)/shard_map/ppermute | solution.py:49
  8.8 4.4 %collective-permute-start.5 = (bf16[32,1152]{1,0:T(8,128)(2,1)S(1)}, bf16[32,1152]{1,0:T(8,128)(2,1)S(1)}, u32[]{:S(2)}, u32[]{:S(2)}) collective-permute-start(bf16[32,1152]{1,0:T(8,128)(2,1)S(1)} %get-tuple-element.14.refs_0_), channel_id=1, source_target_pairs={{0,8},{1,9},{2,10},{3,11},{4,5},{5,4},{6,7},{7,6},{8,0},{9,1},{10,... | collective-permute-start | bytes 221192 | tf_op jit(solution)/shard_map/ppermute | solution.py:49
  9.3 3.8 %collective-permute-start.7 = (bf16[32,1152]{1,0:T(8,128)(2,1)S(1)}, bf16[32,1152]{1,0:T(8,128)(2,1)S(1)}, u32[]{:S(2)}, u32[]{:S(2)}) collective-permute-start(bf16[32,1152]{1,0:T(8,128)(2,1)S(1)} %collective-permute-done.4.refs_2_), channel_id=1, source_target_pairs={{0,4},{4,0},{8,12},{12,8},{16,20},{20,16},{24,28},{28,24},{1,5},{5... | collective-permute-start | bytes 221192 | tf_op jit(solution)/shard_map/ppermute | solution.py:37
  10.7 2.4 %collective-permute-start.6 = (bf16[32,1152]{1,0:T(8,128)(2,1)S(1)}, bf16[32,1152]{1,0:T(8,128)(2,1)S(1)}, u32[]{:S(2)}, u32[]{:S(2)}) collective-permute-start(bf16[32,1152]{1,0:T(8,128)(2,1)S(1)} %collective-permute-done.3.refs_1_), channel_id=1, source_target_pairs={{0,4},{4,0},{8,12},{12,8},{16,20},{20,16},{24,28},{28,24},{1,5},{5... | collective-permute-start | bytes 221192 | tf_op jit(solution)/shard_map/ppermute | solution.py:37
  11.7 1.1 %collective-permute-start = (s32[1,64]{1,0:T(1,128)S(1)}, s32[1,64]{1,0:T(1,128)S(1)}, u32[]{:S(2)}, u32[]{:S(2)}) collective-permute-start(s32[1,64]{1,0:T(1,128)S(1)} %bitcast.1), channel_id=1, source_target_pairs={{0,4},{4,0},{8,12},{12,8},{16,20},{20,16},{24,28},{28,24},{1,5},{5... | collective-permute-start | bytes 776 | tf_op jit(solution)/shard_map/ppermute | solution.py:37
  13.7 5.3 %collective-permute-start.10 = (bf16[32,1152]{1,0:T(8,128)(2,1)S(1)}, bf16[32,1152]{1,0:T(8,128)(2,1)S(1)}, u32[]{:S(2)}, u32[]{:S(2)}) collective-permute-start(bf16[32,1152]{1,0:T(8,128)(2,1)S(1)} %get-tuple-element.21), channel_id=1, source_target_pairs={{0,24},{1,25},{2,26},{3,27},{4,7},{5,6},{6,5},{7,4},{8,16},{9,17},... | collective-permute-start | bytes 221192 | tf_op jit(solution)/shard_map/ppermute | solution.py:49
  15.9 4.4 %collective-permute-start.11 = (bf16[32,1152]{1,0:T(8,128)(2,1)S(1)}, bf16[32,1152]{1,0:T(8,128)(2,1)S(1)}, u32[]{:S(2)}, u32[]{:S(2)}) collective-permute-start(bf16[32,1152]{1,0:T(8,128)(2,1)S(1)} %get-tuple-element.22), channel_id=1, source_target_pairs={{0,8},{1,9},{2,10},{3,11},{4,5},{5,4},{6,7},{7,6},{8,0},{9,1},{10,... | collective-permute-start | bytes 221192 | tf_op jit(solution)/shard_map/ppermute | solution.py:49
  16.7 4.6 %collective-permute-start.9 = (bf16[16,1152]{1,0:T(8,128)(2,1)S(1)}, bf16[16,1152]{1,0:T(8,128)(2,1)S(1)}, u32[]{:S(2)}, u32[]{:S(2)}) collective-permute-start(bf16[16,1152]{1,0:T(8,128)(2,1)S(1)} %get-tuple-element.16), channel_id=1, source_target_pairs={{0,20},{1,21},{2,22},{3,23},{4,2},{5,3},{6,0},{7,1},{8,28},{9,29},... | collective-permute-start | bytes 110600 | tf_op jit(solution)/shard_map/ppermute | solution.py:49
  16.8 4.7 %collective-permute-start.12 = (bf16[16,1152]{1,0:T(8,128)(2,1)S(1)}, bf16[16,1152]{1,0:T(8,128)(2,1)S(1)}, u32[]{:S(2)}, u32[]{:S(2)}) collective-permute-start(bf16[16,1152]{1,0:T(8,128)(2,1)S(1)} %get-tuple-element.24), channel_id=1, source_target_pairs={{0,16},{1,17},{2,18},{3,19},{4,6},{5,7},{6,4},{7,5},{8,24},{9,25},... | collective-permute-start | bytes 110600 | tf_op jit(solution)/shard_map/ppermute | solution.py:49
  20.3 1.3 %collective-permute-start.13 = (bf16[16,1152]{1,0:T(8,128)(2,1)S(1)}, bf16[16,1152]{1,0:T(8,128)(2,1)S(1)}, u32[]{:S(2)}, u32[]{:S(2)}) collective-permute-start(bf16[16,1152]{1,0:T(8,128)(2,1)S(1)} %get-tuple-element.25), channel_id=1, source_target_pairs={{0,4},{4,0},{8,12},{12,8},{16,20},{20,16},{24,28},{28,24},{1,5},{5... | collective-permute-start | bytes 110600 | tf_op jit(solution)/shard_map/ppermute | solution.py:37

commit v18 on v17

--- a/solution.py
+++ b/solution.py
@@ -37,15 +37,17 @@
     return lax.ppermute(block, "img", [(i, i ^ 1) for i in range(size)])
 
 
-def chip_swap(block, distance, cross=0):
+def chip_swap(block, txt_distance, img_distance, cross=0):
     n_img, n_txt = lax.axis_size("img"), lax.axis_size("txt")
     pairs = []
     for img in range(n_img):
         for txt in range(n_txt):
-            if img % 2 == 0 and distance < n_img // 2:
-                pairs.append((img * n_txt + txt, (img ^ (2 * distance) ^ cross) * n_txt + txt))
-            if img % 2 == 1 and distance < n_txt:
-                pairs.append((img * n_txt + txt, (img ^ cross) * n_txt + (txt ^ distance)))
+            if img % 2 == 0 and txt_distance < n_img // 2:
+                target = (img ^ (2 * txt_distance) ^ cross) * n_txt + txt
+                pairs.append((img * n_txt + txt, target))
+            if img % 2 == 1 and img_distance < n_txt:
+                target = (img ^ cross) * n_txt + (txt ^ img_distance)
+                pairs.append((img * n_txt + txt, target))
     return lax.ppermute(block, ("img", "txt"), pairs)
 
 
@@ -112,7 +114,7 @@
     return lax.dot_general(mine, other, (((1,), (1,)), ((), ())), preferred_element_type=f32)
 
 
-def pair_kernel(blocks, split, ids_ref, far_ids_ref, *refs):
+def pair_kernel(blocks, plan, ids_ref, far_ids_ref, *refs):
     mine_refs, other_refs = refs[:blocks], refs[blocks:2 * blocks]
     own_ref, same_ref, cross_ref, *send_refs = refs[2 * blocks:]
     height = own_ref.shape[0]
@@ -123,11 +125,18 @@
     other = jnp.concatenate([ref[...] for ref in other_refs], axis=0)
     part = jnp.dot(coeff, other, preferred_element_type=f32)
     own_ref[...] = part[:height]
-    whole = [k for k in range(1, blocks) if k != split]
-    for k, ref in zip(whole, send_refs):
-        ref[...] = part[k * height:(k + 1) * height].astype(bf16)
-    block = part[split * height:(split + 1) * height].astype(bf16)
-    even = is_even()
+    even = is_even()
+
+    def block_of(txt_distance, img_distance):
+        txt, img = [
+            part[(blocks - k) * height:(blocks - k + 1) * height] for k in (txt_distance, img_distance)
+        ]
+        return jnp.where(even, txt, img).astype(bf16)
+
+    *whole, split = plan
+    for distances, ref in zip(whole, send_refs):
+        ref[...] = block_of(*distances)
+    block = block_of(*split)
     same_ref[...] = jnp.where(even, block[:rows], block[rows:])
     cross_ref[...] = jnp.where(even, block[rows:], block[:rows])
 
@@ -171,18 +180,19 @@
     near = jnp.concatenate([text_embeds, image_embeds])
     mine, other = call(sides_kernel, [pair] * 2, [near, far_txt, far_img])
     order = list(range(blocks - 1, 0, -1))
-    mine = [mine] + [chip_swap(mine, k) for k in order]
-    other = [other, *[core_swap(block) for block in mine[1:-1]], chip_swap(mine[0], 1, cross=1)]
-    split = min(2, blocks - 1)
+    mine = [mine] + [chip_swap(mine, k, k) for k in order]
+    other = [other, *[core_swap(block) for block in mine[1:-1]], chip_swap(mine[0], 1, 1, cross=1)]
+    txt_plan = order[::-1]
+    img_plan = order[:1] + order[2:] + order[1:2]
+    plan = list(zip(txt_plan, img_plan))
     own, same, cross, *send = call(
-        functools.partial(pair_kernel, blocks, split),
+        functools.partial(pair_kernel, blocks, plan),
         [total] + [piece] * 2 + [pair] * (blocks - 2),
         [ids, core_swap(ids), *mine, *other],
     )
-    far = order.pop(split - 1)
-    got = [chip_swap(block, k) for k, block in zip(order, send)]
-    cross = chip_swap(cross, far, cross=1)
-    same = chip_swap(same, far)
+    got = [chip_swap(block, *distances) for distances, block in zip(plan, send)]
+    cross = chip_swap(cross, *plan[-1], cross=1)
+    same = chip_swap(same, *plan[-1])
     keep, send = call(sum_kernel, [single, piece], [own, *got])
     got = core_swap(send)
     column = jax.ShapeDtypeStruct((2 * rows, 1), f32)

time: 22.7 us -> 23.5 us (1.035)
  starting transfers between devices: 12.5 us -> 13.6 us
    ppermute x8, starting transfers between devices: 10.8 us -> 11.7 us  [chip_swap(): return lax.ppermute(block, ('img', 'txt'), pairs)]
  transfers between devices with their start and end apart: 14 -> 14, of which waited for: 9 -> 8; matrix products, arithmetic and copies ran while one was open for 3% -> 3% of each run, Pallas kernels for 1% -> 1%
where the time goes in v18:
time: 23.5 us; the launch traced here: 23.3 us
  starting transfers between devices  13.6 us (58%)
  waiting for transfers between devices  6.68 us (28%)
  Pallas kernels  1.58 us (7%)
  local copies, waits for them, and re-layouts  0.79 us (3%)
  between operations  0.68 us (3%)
    ppermute x8, starting transfers between devices, chip_swap(): return lax.ppermute(block, ('img', 'txt'), pairs)  11.7 us
    ppermute x8, waiting for transfers between devices, chip_swap(): return lax.ppermute(block, ('img', 'txt'), pairs)  4.99 us
    ppermute x6, starting transfers between devices, core_swap(): return lax.ppermute(block, 'img', [(i, i ^ 1) for i in range(size)])  1.84 us
    ppermute x6, waiting for transfers between devices, core_swap(): return lax.ppermute(block, 'img', [(i, i ^ 1) for i in range(size)])  1.69 us
    pallas_call x5, Pallas kernels, call(): pl.pallas_call(kernel, out_shape=outs, in_specs=[VMEM] * len(args), out_s...  1.58 us
    unnamed x5, local copies, waits for them, and re-layouts  0.78 us
  transfers between devices with their start and end apart: 14, of which 8 were waited for; matrix products, arithmetic and copies ran while one was open for 3% of the time, Pallas kernels for 1%

profile of v18, /device:TPU:0, one launch (start us, length us, event | category | flops | bytes accessed | tf_op | source)
XLA Modules:
  0.0 23.3 jit_solution(8160435948727886471)
XLA Ops:
  0.6 0.5 %collective-permute-start.2 = (bf16[16,1152]{1,0:T(8,128)(2,1)}, bf16[16,1152]{1,0:T(8,128)(2,1)S(1)}, u32[]{:S(2)}, u32[]{:S(2)}) collective-permute-start(bf16[16,1152]{1,0:T(8,128)(2,1)} %param.3), channel_id=1, source_target_pairs={{0,4},{4,0},{8,12},{12,8},{16,20},{20,16},{24,28},{28,24},{1,5},{5... | collective-permute-start | bytes 110600 | tf_op jit(solution)/shard_map/ppermute | solution.py:37
  1.2 0.8 %constant_dynamic-update-slice_fusion.1 = bf16[32,1152]{1,0:T(8,128)(2,1)S(1)} fusion(bf16[16,1152]{1,0:T(8,128)(2,1)} %param.4), kind=kLoop, calls=%fused_computation.1 | loop fusion | bytes 73728
  2.0 0.2 collective-permute-done.2.img_ref
  2.2 0.3 %collective-permute-done.1.txt_ref = bf16[16,1152]{1,0:T(8,128)(2,1)S(1)} collective-permute-done((bf16[16,1152]{1,0:T(8,128)(2,1)}, bf16[16,1152]{1,0:T(8,128)(2,1)S(1)}, u32[]{:S(2)}, u32[]{:S(2)}) %collective-permute-start.1) | collective-permute-done | bytes 36896 | tf_op jit(solution)/shard_map/ppermute | solution.py:37
  2.6 0.1 shard_map.50
  2.7 2.7 %collective-permute-start.4 = (bf16[32,1152]{1,0:T(8,128)(2,1)S(1)}, bf16[32,1152]{1,0:T(8,128)(2,1)S(1)}, u32[]{:S(2)}, u32[]{:S(2)}) collective-permute-start(bf16[32,1152]{1,0:T(8,128)(2,1)S(1)} %get-tuple-element.14.refs_0_), channel_id=1, source_target_pairs={{0,16},{1,17},{2,18},{3,19},{4,6},{5,7},{6,4},{7,5},{8,24},{9,25},... | collective-permute-start | bytes 221192 | tf_op jit(solution)/shard_map/ppermute | solution.py:51
  5.5 1.4 %collective-permute-start.3 = (bf16[32,1152]{1,0:T(8,128)(2,1)S(1)}, bf16[32,1152]{1,0:T(8,128)(2,1)S(1)}, u32[]{:S(2)}, u32[]{:S(2)}) collective-permute-start(bf16[32,1152]{1,0:T(8,128)(2,1)S(1)} %get-tuple-element.14.refs_0_), channel_id=1, source_target_pairs={{0,24},{1,25},{2,26},{3,27},{4,7},{5,6},{6,5},{7,4},{8,16},{9,17},... | collective-permute-start | bytes 221192 | tf_op jit(solution)/shard_map/ppermute | solution.py:51
  6.9 1.9 %collective-permute-start.8 = (bf16[32,1152]{1,0:T(8,128)(2,1)S(1)}, bf16[32,1152]{1,0:T(8,128)(2,1)S(1)}, u32[]{:S(2)}, u32[]{:S(2)}) collective-permute-start(bf16[32,1152]{1,0:T(8,128)(2,1)S(1)} %get-tuple-element.14.refs_0_), channel_id=1, source_target_pairs={{0,12},{1,13},{2,14},{3,15},{4,1},{5,0},{6,3},{7,2},{8,4},{9,5},{1... | collective-permute-start | bytes 221192 | tf_op jit(solution)/shard_map/ppermute | solution.py:51
  8.8 0.5 %collective-permute-start.5 = (bf16[32,1152]{1,0:T(8,128)(2,1)S(1)}, bf16[32,1152]{1,0:T(8,128)(2,1)S(1)}, u32[]{:S(2)}, u32[]{:S(2)}) collective-permute-start(bf16[32,1152]{1,0:T(8,128)(2,1)S(1)} %get-tuple-element.14.refs_0_), channel_id=1, source_target_pairs={{0,8},{1,9},{2,10},{3,11},{4,5},{5,4},{6,7},{7,6},{8,0},{9,1},{10,... | collective-permute-start | bytes 221192 | tf_op jit(solution)/shard_map/ppermute | solution.py:51
  9.3 1.4 %collective-permute-done.3.refs_1_ = bf16[32,1152]{1,0:T(8,128)(2,1)S(1)} collective-permute-done((bf16[32,1152]{1,0:T(8,128)(2,1)S(1)}, bf16[32,1152]{1,0:T(8,128)(2,1)S(1)}, u32[]{:S(2)}, u32[]{:S(2)}) %collective-permute-start.3) | collective-permute-done | bytes 73760 | tf_op jit(solution)/shard_map/ppermute | solution.py:51
  10.7 1.0 %collective-permute-start.6 = (bf16[32,1152]{1,0:T(8,128)(2,1)S(1)}, bf16[32,1152]{1,0:T(8,128)(2,1)S(1)}, u32[]{:S(2)}, u32[]{:S(2)}) collective-permute-start(bf16[32,1152]{1,0:T(8,128)(2,1)S(1)} %collective-permute-done.3.refs_1_), channel_id=1, source_target_pairs={{0,4},{4,0},{8,12},{12,8},{16,20},{20,16},{24,28},{28,24},{1,5},{5... | collective-permute-start | bytes 221192 | tf_op jit(solution)/shard_map/ppermute | solution.py:37
  11.7 1.1 %collective-permute-done.far_ids_ref = s32[1,64]{1,0:T(1,128)S(1)} collective-permute-done((s32[1,64]{1,0:T(1,128)S(1)}, s32[1,64]{1,0:T(1,128)S(1)}, u32[]{:S(2)}, u32[]{:S(2)}) %collective-permute-start) | collective-permute-done | bytes 288 | tf_op jit(solution)/shard_map/ppermute | solution.py:37
  12.8 0.3 %collective-permute-done.5.refs_3_ = bf16[32,1152]{1,0:T(8,128)(2,1)S(1)} collective-permute-done((bf16[32,1152]{1,0:T(8,128)(2,1)S(1)}, bf16[32,1152]{1,0:T(8,128)(2,1)S(1)}, u32[]{:S(2)}, u32[]{:S(2)}) %collective-permute-start.5) | collective-permute-done | bytes 73760 | tf_op jit(solution)/shard_map/ppermute | solution.py:51
  13.2 0.5 %shard_map.51 = (f32[32,1152]{1,0:T(8,128)S(1)}, bf16[16,1152]{1,0:T(8,128)(2,1)S(1)}, bf16[16,1152]{1,0:T(8,128)(2,1)S(1)}, bf16[32,1152]{1,0:T(8,128)(2,1)S(1)}, bf16[32,1152]{1,0:T(8,128)(2,1)S(1)}) custom-call(s32[1,64]{1,0:T(1,128)S(1)} %bitcast.2, s32[1,64]{1,0:T(1,128)S(1)} %collective-permute-done.far_ids_ref, ...), custom_call_target="tpu_custom_call" | custom-call | tf_op jit(solution)/shard_map/pallas_call | solution.py:60
  13.7 1.2 %collective-permute-start.10 = (bf16[32,1152]{1,0:T(8,128)(2,1)S(1)}, bf16[32,1152]{1,0:T(8,128)(2,1)S(1)}, u32[]{:S(2)}, u32[]{:S(2)}) collective-permute-start(bf16[32,1152]{1,0:T(8,128)(2,1)S(1)} %get-tuple-element.21), channel_id=1, source_target_pairs={{0,8},{1,9},{2,10},{3,11},{4,7},{5,6},{6,5},{7,4},{8,0},{9,1},{10,... | collective-permute-start | bytes 221192 | tf_op jit(solution)/shard_map/ppermute | solution.py:51
  14.9 1.5 %collective-permute-start.11 = (bf16[32,1152]{1,0:T(8,128)(2,1)S(1)}, bf16[32,1152]{1,0:T(8,128)(2,1)S(1)}, u32[]{:S(2)}, u32[]{:S(2)}) collective-permute-start(bf16[32,1152]{1,0:T(8,128)(2,1)S(1)} %get-tuple-element.22), channel_id=1, source_target_pairs={{0,16},{1,17},{2,18},{3,19},{4,5},{5,4},{6,7},{7,6},{8,24},{9,25},... | collective-permute-start | bytes 221192 | tf_op jit(solution)/shard_map/ppermute | solution.py:51
  16.5 1.2 %collective-permute-start.9 = (bf16[16,1152]{1,0:T(8,128)(2,1)S(1)}, bf16[16,1152]{1,0:T(8,128)(2,1)S(1)}, u32[]{:S(2)}, u32[]{:S(2)}) collective-permute-start(bf16[16,1152]{1,0:T(8,128)(2,1)S(1)} %get-tuple-element.16), channel_id=1, source_target_pairs={{0,28},{1,29},{2,30},{3,31},{4,2},{5,3},{6,0},{7,1},{8,20},{9,21},... | collective-permute-start | bytes 110600 | tf_op jit(solution)/shard_map/ppermute | solution.py:51
  17.7 1.2 %collective-permute-start.12 = (bf16[16,1152]{1,0:T(8,128)(2,1)S(1)}, bf16[16,1152]{1,0:T(8,128)(2,1)S(1)}, u32[]{:S(2)}, u32[]{:S(2)}) collective-permute-start(bf16[16,1152]{1,0:T(8,128)(2,1)S(1)} %get-tuple-element.24), channel_id=1, source_target_pairs={{0,24},{1,25},{2,26},{3,27},{4,6},{5,7},{6,4},{7,5},{8,16},{9,17},... | collective-permute-start | bytes 110600 | tf_op jit(solution)/shard_map/ppermute | solution.py:51
  18.8 0.5 %collective-permute-done.11.refs_1_ = bf16[32,1152]{1,0:T(8,128)(2,1)S(1)} collective-permute-done((bf16[32,1152]{1,0:T(8,128)(2,1)S(1)}, bf16[32,1152]{1,0:T(8,128)(2,1)S(1)}, u32[]{:S(2)}, u32[]{:S(2)}) %collective-permute-start.11) | collective-permute-done | bytes 73760 | tf_op jit(solution)/shard_map/ppermute | solution.py:51
  19.3 0.3 %collective-permute-start.13 = (bf16[16,1152]{1,0:T(8,128)(2,1)S(1)}, bf16[16,1152]{1,0:T(8,128)(2,1)S(1)}, u32[]{:S(2)}, u32[]{:S(2)}) collective-permute-start(bf16[16,1152]{1,0:T(8,128)(2,1)S(1)} %get-tuple-element.25), channel_id=1, source_target_pairs={{0,4},{4,0},{8,12},{12,8},{16,20},{20,16},{24,28},{28,24},{1,5},{5... | collective-permute-start | bytes 110600 | tf_op jit(solution)/shard_map/ppermute | solution.py:37
  19.6 1.1 %collective-permute-done.9.cross_ref = bf16[16,1152]{1,0:T(8,128)(2,1)S(1)} collective-permute-done((bf16[16,1152]{1,0:T(8,128)(2,1)S(1)}, bf16[16,1152]{1,0:T(8,128)(2,1)S(1)}, u32[]{:S(2)}, u32[]{:S(2)}) %collective-permute-start.9) | collective-permute-done | bytes 36896 | tf_op jit(solution)/shard_map/ppermute | solution.py:51
  20.8 0.1 shard_map.52
  20.9 1.7 %collective-permute-done.12.same_ref = bf16[16,1152]{1,0:T(8,128)(2,1)S(1)} collective-permute-done((bf16[16,1152]{1,0:T(8,128)(2,1)S(1)}, bf16[16,1152]{1,0:T(8,128)(2,1)S(1)}, u32[]{:S(2)}, u32[]{:S(2)}) %collective-permute-start.12) | collective-permute-done | bytes 36896 | tf_op jit(solution)/shard_map/ppermute | solution.py:51
  22.5 0.8 %shard_map.54 = (f32[16,1152]{1,0:T(8,128)}, f32[16,1152]{1,0:T(8,128)}) custom-call(f32[32,1152]{1,0:T(8,128)S(1)} %get-tuple-element.17.unit_ref, f32[32,1]{1,0:T(8,128)S(1)} %get-tuple-element.18.inverse_ref, f32[16,1152]{1,0:T(8,128)S(1)} %get-tuple-element.19.rest_ref, f32[16,1152]{1,0:T(8,128)S(1)} %get-tuple-element.23.keep_ref, ...), custom_call_target="tpu_custom_call" | custom-call | tf_op jit(solution)/shard_map/pallas_call | solution.py:60
  (15 shorter events, 0.2 us)
Async XLA Ops:
  0.6 1.4 %copy-start.1 = (bf16[16,1152]{1,0:T(8,128)(2,1)S(1)}, bf16[16,1152]{1,0:T(8,128)(2,1)}, u32[]{:S(2)}) copy-start(bf16[16,1152]{1,0:T(8,128)(2,1)} %param.3) | copy-start | bytes 110596
  0.6 1.6 %collective-permute-start.2 = (bf16[16,1152]{1,0:T(8,128)(2,1)}, bf16[16,1152]{1,0:T(8,128)(2,1)S(1)}, u32[]{:S(2)}, u32[]{:S(2)}) collective-permute-start(bf16[16,1152]{1,0:T(8,128)(2,1)} %param.3), channel_id=1, source_target_pairs={{0,4},{4,0},{8,12},{12,8},{16,20},{20,16},{24,28},{28,24},{1,5},{5... | collective-permute-start | bytes 110600 | tf_op jit(solution)/shard_map/ppermute | solution.py:37
  1.2 1.4 %collective-permute-start.1 = (bf16[16,1152]{1,0:T(8,128)(2,1)}, bf16[16,1152]{1,0:T(8,128)(2,1)S(1)}, u32[]{:S(2)}, u32[]{:S(2)}) collective-permute-start(bf16[16,1152]{1,0:T(8,128)(2,1)} %param.4), channel_id=1, source_target_pairs={{0,4},{4,0},{8,12},{12,8},{16,20},{20,16},{24,28},{28,24},{1,5},{5... | collective-permute-start | bytes 110600 | tf_op jit(solution)/shard_map/ppermute | solution.py:37
  2.7 9.0 %copy-start = (s32[64]{0:T(128)S(1)}, s32[64]{0:T(128)}, u32[]{:S(2)}) copy-start(s32[64]{0:T(128)} %param.5) | copy-start | bytes 772
  2.7 6.6 %collective-permute-start.4 = (bf16[32,1152]{1,0:T(8,128)(2,1)S(1)}, bf16[32,1152]{1,0:T(8,128)(2,1)S(1)}, u32[]{:S(2)}, u32[]{:S(2)}) collective-permute-start(bf16[32,1152]{1,0:T(8,128)(2,1)S(1)} %get-tuple-element.14.refs_0_), channel_id=1, source_target_pairs={{0,16},{1,17},{2,18},{3,19},{4,6},{5,7},{6,4},{7,5},{8,24},{9,25},... | collective-permute-start | bytes 221192 | tf_op jit(solution)/shard_map/ppermute | solution.py:51
  5.5 5.3 %collective-permute-start.3 = (bf16[32,1152]{1,0:T(8,128)(2,1)S(1)}, bf16[32,1152]{1,0:T(8,128)(2,1)S(1)}, u32[]{:S(2)}, u32[]{:S(2)}) collective-permute-start(bf16[32,1152]{1,0:T(8,128)(2,1)S(1)} %get-tuple-element.14.refs_0_), channel_id=1, source_target_pairs={{0,24},{1,25},{2,26},{3,27},{4,7},{5,6},{6,5},{7,4},{8,16},{9,17},... | collective-permute-start | bytes 221192 | tf_op jit(solution)/shard_map/ppermute | solution.py:51
  6.9 5.9 %collective-permute-start.8 = (bf16[32,1152]{1,0:T(8,128)(2,1)S(1)}, bf16[32,1152]{1,0:T(8,128)(2,1)S(1)}, u32[]{:S(2)}, u32[]{:S(2)}) collective-permute-start(bf16[32,1152]{1,0:T(8,128)(2,1)S(1)} %get-tuple-element.14.refs_0_), channel_id=1, source_target_pairs={{0,12},{1,13},{2,14},{3,15},{4,1},{5,0},{6,3},{7,2},{8,4},{9,5},{1... | collective-permute-start | bytes 221192 | tf_op jit(solution)/shard_map/ppermute | solution.py:51
  8.8 4.4 %collective-permute-start.5 = (bf16[32,1152]{1,0:T(8,128)(2,1)S(1)}, bf16[32,1152]{1,0:T(8,128)(2,1)S(1)}, u32[]{:S(2)}, u32[]{:S(2)}) collective-permute-start(bf16[32,1152]{1,0:T(8,128)(2,1)S(1)} %get-tuple-element.14.refs_0_), channel_id=1, source_target_pairs={{0,8},{1,9},{2,10},{3,11},{4,5},{5,4},{6,7},{7,6},{8,0},{9,1},{10,... | collective-permute-start | bytes 221192 | tf_op jit(solution)/shard_map/ppermute | solution.py:51
  9.3 3.8 %collective-permute-start.7 = (bf16[32,1152]{1,0:T(8,128)(2,1)S(1)}, bf16[32,1152]{1,0:T(8,128)(2,1)S(1)}, u32[]{:S(2)}, u32[]{:S(2)}) collective-permute-start(bf16[32,1152]{1,0:T(8,128)(2,1)S(1)} %collective-permute-done.4.refs_2_), channel_id=1, source_target_pairs={{0,4},{4,0},{8,12},{12,8},{16,20},{20,16},{24,28},{28,24},{1,5},{5... | collective-permute-start | bytes 221192 | tf_op jit(solution)/shard_map/ppermute | solution.py:37
  10.7 2.4 %collective-permute-start.6 = (bf16[32,1152]{1,0:T(8,128)(2,1)S(1)}, bf16[32,1152]{1,0:T(8,128)(2,1)S(1)}, u32[]{:S(2)}, u32[]{:S(2)}) collective-permute-start(bf16[32,1152]{1,0:T(8,128)(2,1)S(1)} %collective-permute-done.3.refs_1_), channel_id=1, source_target_pairs={{0,4},{4,0},{8,12},{12,8},{16,20},{20,16},{24,28},{28,24},{1,5},{5... | collective-permute-start | bytes 221192 | tf_op jit(solution)/shard_map/ppermute | solution.py:37
  11.7 1.1 %collective-permute-start = (s32[1,64]{1,0:T(1,128)S(1)}, s32[1,64]{1,0:T(1,128)S(1)}, u32[]{:S(2)}, u32[]{:S(2)}) collective-permute-start(s32[1,64]{1,0:T(1,128)S(1)} %bitcast.1), channel_id=1, source_target_pairs={{0,4},{4,0},{8,12},{12,8},{16,20},{20,16},{24,28},{28,24},{1,5},{5... | collective-permute-start | bytes 776 | tf_op jit(solution)/shard_map/ppermute | solution.py:37
  13.7 5.1 %collective-permute-start.10 = (bf16[32,1152]{1,0:T(8,128)(2,1)S(1)}, bf16[32,1152]{1,0:T(8,128)(2,1)S(1)}, u32[]{:S(2)}, u32[]{:S(2)}) collective-permute-start(bf16[32,1152]{1,0:T(8,128)(2,1)S(1)} %get-tuple-element.21), channel_id=1, source_target_pairs={{0,8},{1,9},{2,10},{3,11},{4,7},{5,6},{6,5},{7,4},{8,0},{9,1},{10,... | collective-permute-start | bytes 221192 | tf_op jit(solution)/shard_map/ppermute | solution.py:51
  14.9 4.4 %collective-permute-start.11 = (bf16[32,1152]{1,0:T(8,128)(2,1)S(1)}, bf16[32,1152]{1,0:T(8,128)(2,1)S(1)}, u32[]{:S(2)}, u32[]{:S(2)}) collective-permute-start(bf16[32,1152]{1,0:T(8,128)(2,1)S(1)} %get-tuple-element.22), channel_id=1, source_target_pairs={{0,16},{1,17},{2,18},{3,19},{4,5},{5,4},{6,7},{7,6},{8,24},{9,25},... | collective-permute-start | bytes 221192 | tf_op jit(solution)/shard_map/ppermute | solution.py:51
  16.5 4.3 %collective-permute-start.9 = (bf16[16,1152]{1,0:T(8,128)(2,1)S(1)}, bf16[16,1152]{1,0:T(8,128)(2,1)S(1)}, u32[]{:S(2)}, u32[]{:S(2)}) collective-permute-start(bf16[16,1152]{1,0:T(8,128)(2,1)S(1)} %get-tuple-element.16), channel_id=1, source_target_pairs={{0,28},{1,29},{2,30},{3,31},{4,2},{5,3},{6,0},{7,1},{8,20},{9,21},... | collective-permute-start | bytes 110600 | tf_op jit(solution)/shard_map/ppermute | solution.py:51
  17.7 4.9 %collective-permute-start.12 = (bf16[16,1152]{1,0:T(8,128)(2,1)S(1)}, bf16[16,1152]{1,0:T(8,128)(2,1)S(1)}, u32[]{:S(2)}, u32[]{:S(2)}) collective-permute-start(bf16[16,1152]{1,0:T(8,128)(2,1)S(1)} %get-tuple-element.24), channel_id=1, source_target_pairs={{0,24},{1,25},{2,26},{3,27},{4,6},{5,7},{6,4},{7,5},{8,16},{9,17},... | collective-permute-start | bytes 110600 | tf_op jit(solution)/shard_map/ppermute | solution.py:51
  19.3 3.2 %collective-permute-start.13 = (bf16[16,1152]{1,0:T(8,128)(2,1)S(1)}, bf16[16,1152]{1,0:T(8,128)(2,1)S(1)}, u32[]{:S(2)}, u32[]{:S(2)}) collective-permute-start(bf16[16,1152]{1,0:T(8,128)(2,1)S(1)} %get-tuple-element.25), channel_id=1, source_target_pairs={{0,4},{4,0},{8,12},{12,8},{16,20},{20,16},{24,28},{28,24},{1,5},{5... | collective-permute-start | bytes 110600 | tf_op jit(solution)/shard_map/ppermute | solution.py:37

commit v19 on v17

--- a/solution.py
+++ b/solution.py
@@ -37,16 +37,21 @@
     return lax.ppermute(block, "img", [(i, i ^ 1) for i in range(size)])
 
 
-def chip_swap(block, distance, cross=0):
+def chip_swap(block, distance, cross=lambda txt: 0):
     n_img, n_txt = lax.axis_size("img"), lax.axis_size("txt")
     pairs = []
     for img in range(n_img):
         for txt in range(n_txt):
+            other = cross(txt)
             if img % 2 == 0 and distance < n_img // 2:
-                pairs.append((img * n_txt + txt, (img ^ (2 * distance) ^ cross) * n_txt + txt))
+                pairs.append((img * n_txt + txt, (img ^ (2 * distance) ^ other) * n_txt + txt))
             if img % 2 == 1 and distance < n_txt:
-                pairs.append((img * n_txt + txt, (img ^ cross) * n_txt + (txt ^ distance)))
+                pairs.append((img * n_txt + txt, (img ^ other) * n_txt + (txt ^ distance)))
     return lax.ppermute(block, ("img", "txt"), pairs)
+
+
+def cross_first(distance):
+    return (lax.axis_index("txt") % 2 == 0) | (distance % 2 == 1)
 
 
 def is_even():
@@ -114,7 +119,7 @@
 
 def pair_kernel(blocks, split, ids_ref, far_ids_ref, *refs):
     mine_refs, other_refs = refs[:blocks], refs[blocks:2 * blocks]
-    own_ref, same_ref, cross_ref, *send_refs = refs[2 * blocks:]
+    own_ref, first_ref, second_ref, *send_refs = refs[2 * blocks:]
     height = own_ref.shape[0]
     rows = height // 2
     mine_ids, other_ids = side_ids(rows, ids_ref[...], far_ids_ref[...], blocks * height)
@@ -128,8 +133,9 @@
         ref[...] = part[k * height:(k + 1) * height].astype(bf16)
     block = part[split * height:(split + 1) * height].astype(bf16)
     even = is_even()
-    same_ref[...] = jnp.where(even, block[:rows], block[rows:])
-    cross_ref[...] = jnp.where(even, block[rows:], block[:rows])
+    first = jnp.logical_xor(even, cross_first(blocks - split))
+    first_ref[...] = jnp.where(first, block[:rows], block[rows:])
+    second_ref[...] = jnp.where(first, block[rows:], block[:rows])
 
 
 def sum_kernel(own_ref, *refs):
@@ -143,16 +149,20 @@
     send_ref[...] = jnp.where(even, total[rows:], total[:rows]).astype(bf16)
 
 
-def unit_kernel(raw_ref, cross_ref, unit_ref, inverse_ref, rest_ref):
+def unit_kernel(raw_ref, first_ref, unit_ref, inverse_ref, rest_ref):
     unit_ref[...], inverse_ref[...] = normalize(raw_ref[...])
-    rest_ref[...] = cross_ref[...].astype(f32)
-
-
-def out_kernel(unit_ref, inverse_ref, rest_ref, keep_ref, same_ref, got_ref, img_ref, txt_ref):
+    rest_ref[...] = first_ref[...].astype(f32)
+
+
+def out_kernel(
+    far, unit_ref, inverse_ref, first_ref, keep_ref, second_ref, got_ref, img_ref, txt_ref
+):
     rows = keep_ref.shape[0]
     even = is_even()
-    keep = keep_ref[...] + same_ref[...].astype(f32)
-    got = got_ref[...].astype(f32) + rest_ref[...]
+    first, second = first_ref[...], second_ref[...].astype(f32)
+    cross = cross_first(far)
+    keep = keep_ref[...] + jnp.where(cross, second, first)
+    got = got_ref[...].astype(f32) + jnp.where(cross, first, second)
     unit, inverse = unit_ref[...], inverse_ref[...]
     txt_ref[...] = back_norm(unit[:rows], inverse[:rows], jnp.where(even, keep, got))
     img_ref[...] = back_norm(unit[rows:], inverse[rows:], jnp.where(even, got, keep))
@@ -172,22 +182,23 @@
     mine, other = call(sides_kernel, [pair] * 2, [near, far_txt, far_img])
     order = list(range(blocks - 1, 0, -1))
     mine = [mine] + [chip_swap(mine, k) for k in order]
-    other = [other, *[core_swap(block) for block in mine[1:-1]], chip_swap(mine[0], 1, cross=1)]
+    other = [other, *[core_swap(block) for block in mine[1:-1]], chip_swap(mine[0], 1, lambda txt: 1)]
     split = min(2, blocks - 1)
-    own, same, cross, *send = call(
+    own, first, second, *send = call(
         functools.partial(pair_kernel, blocks, split),
         [total] + [piece] * 2 + [pair] * (blocks - 2),
         [ids, core_swap(ids), *mine, *other],
     )
     far = order.pop(split - 1)
     got = [chip_swap(block, k) for k, block in zip(order, send)]
-    cross = chip_swap(cross, far, cross=1)
-    same = chip_swap(same, far)
+    first = chip_swap(first, far, lambda txt: int(txt % 2 == 0 or far % 2 == 1))
+    second = chip_swap(second, far, lambda txt: int(txt % 2 == 1 and far % 2 == 0))
     keep, send = call(sum_kernel, [single, piece], [own, *got])
     got = core_swap(send)
     column = jax.ShapeDtypeStruct((2 * rows, 1), f32)
-    ready = call(unit_kernel, [total, column, single], [near, cross], cost=LONG)
-    return tuple(call(out_kernel, [single] * 2, [*ready, keep, same, got]))
+    ready = call(unit_kernel, [total, column, single], [near, first], cost=LONG)
+    kernel = functools.partial(out_kernel, far)
+    return tuple(call(kernel, [single] * 2, [*ready, keep, second, got]))
 
 
 def solution(mesh):

time: 22.7 us -> 22.7 us (level)
    ppermute x8, waiting for transfers between devices: 5.02 us -> 4.71 us  [chip_swap(): return lax.ppermute(block, ('img', 'txt'), pairs)]
    ppermute x6, waiting for transfers between devices: 1.79 us -> 2.1 us  [core_swap(): return lax.ppermute(block, 'img', [(i, i ^ 1) for i in range(size)])]
where the time goes in v19:
time: 22.7 us; the launch traced here: 22.4 us
  starting transfers between devices  12.5 us (55%)
  waiting for transfers between devices  6.81 us (30%)
  Pallas kernels  1.58 us (7%)
  local copies, waits for them, and re-layouts  0.79 us (3%)
  between operations  0.7 us (3%)
    ppermute x8, starting transfers between devices, chip_swap(): return lax.ppermute(block, ('img', 'txt'), pairs)  10.8 us
    ppermute x8, waiting for transfers between devices, chip_swap(): return lax.ppermute(block, ('img', 'txt'), pairs)  4.71 us
    ppermute x6, waiting for transfers between devices, core_swap(): return lax.ppermute(block, 'img', [(i, i ^ 1) for i in range(size)])  2.1 us
    ppermute x6, starting transfers between devices, core_swap(): return lax.ppermute(block, 'img', [(i, i ^ 1) for i in range(size)])  1.63 us
    pallas_call x5, Pallas kernels, call(): pl.pallas_call(kernel, out_shape=outs, in_specs=[VMEM] * len(args), out_s...  1.58 us
    unnamed x5, local copies, waits for them, and re-layouts  0.78 us
  transfers between devices with their start and end apart: 14, of which 9 were waited for; matrix products, arithmetic and copies ran while one was open for 3% of the time, Pallas kernels for 1%

profile of v19, /device:TPU:0, one launch (start us, length us, event | category | flops | bytes accessed | tf_op | source)
XLA Modules:
  0.0 22.4 jit_solution(13154955137661857625)
XLA Ops:
  0.6 0.5 %collective-permute-start.2 = (bf16[16,1152]{1,0:T(8,128)(2,1)}, bf16[16,1152]{1,0:T(8,128)(2,1)S(1)}, u32[]{:S(2)}, u32[]{:S(2)}) collective-permute-start(bf16[16,1152]{1,0:T(8,128)(2,1)} %param.3), channel_id=1, source_target_pairs={{0,4},{4,0},{8,12},{12,8},{16,20},{20,16},{24,28},{28,24},{1,5},{5... | collective-permute-start | bytes 110600 | tf_op jit(solution)/shard_map/ppermute | solution.py:37
  1.2 0.1 collective-permute-start.1
  1.2 0.8 %constant_dynamic-update-slice_fusion.1 = bf16[32,1152]{1,0:T(8,128)(2,1)S(1)} fusion(bf16[16,1152]{1,0:T(8,128)(2,1)} %param.4), kind=kLoop, calls=%fused_computation.1 | loop fusion | bytes 73728
  2.0 0.2 collective-permute-done.2.img_ref
  2.2 0.3 %collective-permute-done.1.txt_ref = bf16[16,1152]{1,0:T(8,128)(2,1)S(1)} collective-permute-done((bf16[16,1152]{1,0:T(8,128)(2,1)}, bf16[16,1152]{1,0:T(8,128)(2,1)S(1)}, u32[]{:S(2)}, u32[]{:S(2)}) %collective-permute-start.1) | collective-permute-done | bytes 36896 | tf_op jit(solution)/shard_map/ppermute | solution.py:37
  2.6 0.1 shard_map.50
  2.7 2.7 %collective-permute-start.4 = (bf16[32,1152]{1,0:T(8,128)(2,1)S(1)}, bf16[32,1152]{1,0:T(8,128)(2,1)S(1)}, u32[]{:S(2)}, u32[]{:S(2)}) collective-permute-start(bf16[32,1152]{1,0:T(8,128)(2,1)S(1)} %get-tuple-element.14.refs_0_), channel_id=1, source_target_pairs={{0,16},{1,17},{2,18},{3,19},{4,6},{5,7},{6,4},{7,5},{8,24},{9,25},... | collective-permute-start | bytes 221192 | tf_op jit(solution)/shard_map/ppermute | solution.py:50
  5.5 1.4 %collective-permute-start.3 = (bf16[32,1152]{1,0:T(8,128)(2,1)S(1)}, bf16[32,1152]{1,0:T(8,128)(2,1)S(1)}, u32[]{:S(2)}, u32[]{:S(2)}) collective-permute-start(bf16[32,1152]{1,0:T(8,128)(2,1)S(1)} %get-tuple-element.14.refs_0_), channel_id=1, source_target_pairs={{0,24},{1,25},{2,26},{3,27},{4,7},{5,6},{6,5},{7,4},{8,16},{9,17},... | collective-permute-start | bytes 221192 | tf_op jit(solution)/shard_map/ppermute | solution.py:50
  6.9 1.9 %collective-permute-start.8 = (bf16[32,1152]{1,0:T(8,128)(2,1)S(1)}, bf16[32,1152]{1,0:T(8,128)(2,1)S(1)}, u32[]{:S(2)}, u32[]{:S(2)}) collective-permute-start(bf16[32,1152]{1,0:T(8,128)(2,1)S(1)} %get-tuple-element.14.refs_0_), channel_id=1, source_target_pairs={{0,12},{1,13},{2,14},{3,15},{4,1},{5,0},{6,3},{7,2},{8,4},{9,5},{1... | collective-permute-start | bytes 221192 | tf_op jit(solution)/shard_map/ppermute | solution.py:50
  8.8 0.5 %collective-permute-start.5 = (bf16[32,1152]{1,0:T(8,128)(2,1)S(1)}, bf16[32,1152]{1,0:T(8,128)(2,1)S(1)}, u32[]{:S(2)}, u32[]{:S(2)}) collective-permute-start(bf16[32,1152]{1,0:T(8,128)(2,1)S(1)} %get-tuple-element.14.refs_0_), channel_id=1, source_target_pairs={{0,8},{1,9},{2,10},{3,11},{4,5},{5,4},{6,7},{7,6},{8,0},{9,1},{10,... | collective-permute-start | bytes 221192 | tf_op jit(solution)/shard_map/ppermute | solution.py:50
  9.3 1.4 %collective-permute-done.3.refs_1_ = bf16[32,1152]{1,0:T(8,128)(2,1)S(1)} collective-permute-done((bf16[32,1152]{1,0:T(8,128)(2,1)S(1)}, bf16[32,1152]{1,0:T(8,128)(2,1)S(1)}, u32[]{:S(2)}, u32[]{:S(2)}) %collective-permute-start.3) | collective-permute-done | bytes 73760 | tf_op jit(solution)/shard_map/ppermute | solution.py:50
  10.7 1.0 %collective-permute-start.6 = (bf16[32,1152]{1,0:T(8,128)(2,1)S(1)}, bf16[32,1152]{1,0:T(8,128)(2,1)S(1)}, u32[]{:S(2)}, u32[]{:S(2)}) collective-permute-start(bf16[32,1152]{1,0:T(8,128)(2,1)S(1)} %collective-permute-done.3.refs_1_), channel_id=1, source_target_pairs={{0,4},{4,0},{8,12},{12,8},{16,20},{20,16},{24,28},{28,24},{1,5},{5... | collective-permute-start | bytes 221192 | tf_op jit(solution)/shard_map/ppermute | solution.py:37
  11.7 1.1 %collective-permute-done.far_ids_ref = s32[1,64]{1,0:T(1,128)S(1)} collective-permute-done((s32[1,64]{1,0:T(1,128)S(1)}, s32[1,64]{1,0:T(1,128)S(1)}, u32[]{:S(2)}, u32[]{:S(2)}) %collective-permute-start) | collective-permute-done | bytes 288 | tf_op jit(solution)/shard_map/ppermute | solution.py:37
  12.8 0.3 %collective-permute-done.5.refs_3_ = bf16[32,1152]{1,0:T(8,128)(2,1)S(1)} collective-permute-done((bf16[32,1152]{1,0:T(8,128)(2,1)S(1)}, bf16[32,1152]{1,0:T(8,128)(2,1)S(1)}, u32[]{:S(2)}, u32[]{:S(2)}) %collective-permute-start.5) | collective-permute-done | bytes 73760 | tf_op jit(solution)/shard_map/ppermute | solution.py:50
  13.2 0.5 %shard_map.51 = (f32[32,1152]{1,0:T(8,128)S(1)}, bf16[16,1152]{1,0:T(8,128)(2,1)S(1)}, bf16[16,1152]{1,0:T(8,128)(2,1)S(1)}, bf16[32,1152]{1,0:T(8,128)(2,1)S(1)}, bf16[32,1152]{1,0:T(8,128)(2,1)S(1)}) custom-call(s32[1,64]{1,0:T(1,128)S(1)} %bitcast.2, s32[1,64]{1,0:T(1,128)S(1)} %collective-permute-done.far_ids_ref, ...), custom_call_target="tpu_custom_call" | custom-call | tf_op jit(solution)/shard_map/pallas_call | solution.py:63
  13.7 2.2 %collective-permute-start.10 = (bf16[32,1152]{1,0:T(8,128)(2,1)S(1)}, bf16[32,1152]{1,0:T(8,128)(2,1)S(1)}, u32[]{:S(2)}, u32[]{:S(2)}) collective-permute-start(bf16[32,1152]{1,0:T(8,128)(2,1)S(1)} %get-tuple-element.21), channel_id=1, source_target_pairs={{0,24},{1,25},{2,26},{3,27},{4,7},{5,6},{6,5},{7,4},{8,16},{9,17},... | collective-permute-start | bytes 221192 | tf_op jit(solution)/shard_map/ppermute | solution.py:50
  15.9 0.8 %collective-permute-start.11 = (bf16[32,1152]{1,0:T(8,128)(2,1)S(1)}, bf16[32,1152]{1,0:T(8,128)(2,1)S(1)}, u32[]{:S(2)}, u32[]{:S(2)}) collective-permute-start(bf16[32,1152]{1,0:T(8,128)(2,1)S(1)} %get-tuple-element.22), channel_id=1, source_target_pairs={{0,8},{1,9},{2,10},{3,11},{4,5},{5,4},{6,7},{7,6},{8,0},{9,1},{10,... | collective-permute-start | bytes 221192 | tf_op jit(solution)/shard_map/ppermute | solution.py:50
  16.8 1.1 %collective-permute-start.12 = (bf16[16,1152]{1,0:T(8,128)(2,1)S(1)}, bf16[16,1152]{1,0:T(8,128)(2,1)S(1)}, u32[]{:S(2)}, u32[]{:S(2)}) collective-permute-start(bf16[16,1152]{1,0:T(8,128)(2,1)S(1)} %get-tuple-element.24), channel_id=1, source_target_pairs={{0,16},{1,21},{2,18},{3,23},{4,6},{5,3},{6,4},{7,1},{8,24},{9,29},... | collective-permute-start | bytes 110600 | tf_op jit(solution)/shard_map/ppermute | solution.py:50
  17.9 1.1 %collective-permute-done.10.refs_0_ = bf16[32,1152]{1,0:T(8,128)(2,1)S(1)} collective-permute-done((bf16[32,1152]{1,0:T(8,128)(2,1)S(1)}, bf16[32,1152]{1,0:T(8,128)(2,1)S(1)}, u32[]{:S(2)}, u32[]{:S(2)}) %collective-permute-start.10) | collective-permute-done | bytes 73760 | tf_op jit(solution)/shard_map/ppermute | solution.py:50
  19.0 1.2 %collective-permute-done.11.refs_1_ = bf16[32,1152]{1,0:T(8,128)(2,1)S(1)} collective-permute-done((bf16[32,1152]{1,0:T(8,128)(2,1)S(1)}, bf16[32,1152]{1,0:T(8,128)(2,1)S(1)}, u32[]{:S(2)}, u32[]{:S(2)}) %collective-permute-start.11) | collective-permute-done | bytes 73760 | tf_op jit(solution)/shard_map/ppermute | solution.py:50
  20.4 0.7 %collective-permute-done.9.first_ref = bf16[16,1152]{1,0:T(8,128)(2,1)S(1)} collective-permute-done((bf16[16,1152]{1,0:T(8,128)(2,1)S(1)}, bf16[16,1152]{1,0:T(8,128)(2,1)S(1)}, u32[]{:S(2)}, u32[]{:S(2)}) %collective-permute-start.9) | collective-permute-done | bytes 36896 | tf_op jit(solution)/shard_map/ppermute | solution.py:50
  21.0 0.1 shard_map.52
  21.2 0.4 %collective-permute-done.13.got_ref = bf16[16,1152]{1,0:T(8,128)(2,1)S(1)} collective-permute-done((bf16[16,1152]{1,0:T(8,128)(2,1)S(1)}, bf16[16,1152]{1,0:T(8,128)(2,1)S(1)}, u32[]{:S(2)}, u32[]{:S(2)}) %collective-permute-start.13) | collective-permute-done | bytes 36896 | tf_op jit(solution)/shard_map/ppermute | solution.py:37
  21.6 0.8 %shard_map.54 = (f32[16,1152]{1,0:T(8,128)}, f32[16,1152]{1,0:T(8,128)}) custom-call(f32[32,1152]{1,0:T(8,128)S(1)} %get-tuple-element.17.unit_ref, f32[32,1]{1,0:T(8,128)S(1)} %get-tuple-element.18.inverse_ref, f32[16,1152]{1,0:T(8,128)S(1)} %get-tuple-element.19.first_ref, f32[16,1152]{1,0:T(8,128)S(1)} %get-tuple-element.23.keep_ref, ...), custom_call_target="tpu_custom_call" | custom-call | tf_op jit(solution)/shard_map/pallas_call | solution.py:63
  (15 shorter events, 0.2 us)
Async XLA Ops:
  0.6 1.4 %copy-start.1 = (bf16[16,1152]{1,0:T(8,128)(2,1)S(1)}, bf16[16,1152]{1,0:T(8,128)(2,1)}, u32[]{:S(2)}) copy-start(bf16[16,1152]{1,0:T(8,128)(2,1)} %param.3) | copy-start | bytes 110596
  0.6 1.6 %collective-permute-start.2 = (bf16[16,1152]{1,0:T(8,128)(2,1)}, bf16[16,1152]{1,0:T(8,128)(2,1)S(1)}, u32[]{:S(2)}, u32[]{:S(2)}) collective-permute-start(bf16[16,1152]{1,0:T(8,128)(2,1)} %param.3), channel_id=1, source_target_pairs={{0,4},{4,0},{8,12},{12,8},{16,20},{20,16},{24,28},{28,24},{1,5},{5... | collective-permute-start | bytes 110600 | tf_op jit(solution)/shard_map/ppermute | solution.py:37
  1.2 1.4 %collective-permute-start.1 = (bf16[16,1152]{1,0:T(8,128)(2,1)}, bf16[16,1152]{1,0:T(8,128)(2,1)S(1)}, u32[]{:S(2)}, u32[]{:S(2)}) collective-permute-start(bf16[16,1152]{1,0:T(8,128)(2,1)} %param.4), channel_id=1, source_target_pairs={{0,4},{4,0},{8,12},{12,8},{16,20},{20,16},{24,28},{28,24},{1,5},{5... | collective-permute-start | bytes 110600 | tf_op jit(solution)/shard_map/ppermute | solution.py:37
  2.7 9.0 %copy-start = (s32[64]{0:T(128)S(1)}, s32[64]{0:T(128)}, u32[]{:S(2)}) copy-start(s32[64]{0:T(128)} %param.5) | copy-start | bytes 772
  2.7 6.6 %collective-permute-start.4 = (bf16[32,1152]{1,0:T(8,128)(2,1)S(1)}, bf16[32,1152]{1,0:T(8,128)(2,1)S(1)}, u32[]{:S(2)}, u32[]{:S(2)}) collective-permute-start(bf16[32,1152]{1,0:T(8,128)(2,1)S(1)} %get-tuple-element.14.refs_0_), channel_id=1, source_target_pairs={{0,16},{1,17},{2,18},{3,19},{4,6},{5,7},{6,4},{7,5},{8,24},{9,25},... | collective-permute-start | bytes 221192 | tf_op jit(solution)/shard_map/ppermute | solution.py:50
  5.5 5.3 %collective-permute-start.3 = (bf16[32,1152]{1,0:T(8,128)(2,1)S(1)}, bf16[32,1152]{1,0:T(8,128)(2,1)S(1)}, u32[]{:S(2)}, u32[]{:S(2)}) collective-permute-start(bf16[32,1152]{1,0:T(8,128)(2,1)S(1)} %get-tuple-element.14.refs_0_), channel_id=1, source_target_pairs={{0,24},{1,25},{2,26},{3,27},{4,7},{5,6},{6,5},{7,4},{8,16},{9,17},... | collective-permute-start | bytes 221192 | tf_op jit(solution)/shard_map/ppermute | solution.py:50
  6.9 5.9 %collective-permute-start.8 = (bf16[32,1152]{1,0:T(8,128)(2,1)S(1)}, bf16[32,1152]{1,0:T(8,128)(2,1)S(1)}, u32[]{:S(2)}, u32[]{:S(2)}) collective-permute-start(bf16[32,1152]{1,0:T(8,128)(2,1)S(1)} %get-tuple-element.14.refs_0_), channel_id=1, source_target_pairs={{0,12},{1,13},{2,14},{3,15},{4,1},{5,0},{6,3},{7,2},{8,4},{9,5},{1... | collective-permute-start | bytes 221192 | tf_op jit(solution)/shard_map/ppermute | solution.py:50
  8.8 4.4 %collective-permute-start.5 = (bf16[32,1152]{1,0:T(8,128)(2,1)S(1)}, bf16[32,1152]{1,0:T(8,128)(2,1)S(1)}, u32[]{:S(2)}, u32[]{:S(2)}) collective-permute-start(bf16[32,1152]{1,0:T(8,128)(2,1)S(1)} %get-tuple-element.14.refs_0_), channel_id=1, source_target_pairs={{0,8},{1,9},{2,10},{3,11},{4,5},{5,4},{6,7},{7,6},{8,0},{9,1},{10,... | collective-permute-start | bytes 221192 | tf_op jit(solution)/shard_map/ppermute | solution.py:50
  9.3 3.8 %collective-permute-start.7 = (bf16[32,1152]{1,0:T(8,128)(2,1)S(1)}, bf16[32,1152]{1,0:T(8,128)(2,1)S(1)}, u32[]{:S(2)}, u32[]{:S(2)}) collective-permute-start(bf16[32,1152]{1,0:T(8,128)(2,1)S(1)} %collective-permute-done.4.refs_2_), channel_id=1, source_target_pairs={{0,4},{4,0},{8,12},{12,8},{16,20},{20,16},{24,28},{28,24},{1,5},{5... | collective-permute-start | bytes 221192 | tf_op jit(solution)/shard_map/ppermute | solution.py:37
  10.7 2.4 %collective-permute-start.6 = (bf16[32,1152]{1,0:T(8,128)(2,1)S(1)}, bf16[32,1152]{1,0:T(8,128)(2,1)S(1)}, u32[]{:S(2)}, u32[]{:S(2)}) collective-permute-start(bf16[32,1152]{1,0:T(8,128)(2,1)S(1)} %collective-permute-done.3.refs_1_), channel_id=1, source_target_pairs={{0,4},{4,0},{8,12},{12,8},{16,20},{20,16},{24,28},{28,24},{1,5},{5... | collective-permute-start | bytes 221192 | tf_op jit(solution)/shard_map/ppermute | solution.py:37
  11.7 1.1 %collective-permute-start = (s32[1,64]{1,0:T(1,128)S(1)}, s32[1,64]{1,0:T(1,128)S(1)}, u32[]{:S(2)}, u32[]{:S(2)}) collective-permute-start(s32[1,64]{1,0:T(1,128)S(1)} %bitcast.1), channel_id=1, source_target_pairs={{0,4},{4,0},{8,12},{12,8},{16,20},{20,16},{24,28},{28,24},{1,5},{5... | collective-permute-start | bytes 776 | tf_op jit(solution)/shard_map/ppermute | solution.py:37
  13.7 5.3 %collective-permute-start.10 = (bf16[32,1152]{1,0:T(8,128)(2,1)S(1)}, bf16[32,1152]{1,0:T(8,128)(2,1)S(1)}, u32[]{:S(2)}, u32[]{:S(2)}) collective-permute-start(bf16[32,1152]{1,0:T(8,128)(2,1)S(1)} %get-tuple-element.21), channel_id=1, source_target_pairs={{0,24},{1,25},{2,26},{3,27},{4,7},{5,6},{6,5},{7,4},{8,16},{9,17},... | collective-permute-start | bytes 221192 | tf_op jit(solution)/shard_map/ppermute | solution.py:50
  15.9 4.4 %collective-permute-start.11 = (bf16[32,1152]{1,0:T(8,128)(2,1)S(1)}, bf16[32,1152]{1,0:T(8,128)(2,1)S(1)}, u32[]{:S(2)}, u32[]{:S(2)}) collective-permute-start(bf16[32,1152]{1,0:T(8,128)(2,1)S(1)} %get-tuple-element.22), channel_id=1, source_target_pairs={{0,8},{1,9},{2,10},{3,11},{4,5},{5,4},{6,7},{7,6},{8,0},{9,1},{10,... | collective-permute-start | bytes 221192 | tf_op jit(solution)/shard_map/ppermute | solution.py:50
  16.7 4.3 %collective-permute-start.9 = (bf16[16,1152]{1,0:T(8,128)(2,1)S(1)}, bf16[16,1152]{1,0:T(8,128)(2,1)S(1)}, u32[]{:S(2)}, u32[]{:S(2)}) collective-permute-start(bf16[16,1152]{1,0:T(8,128)(2,1)S(1)} %get-tuple-element.16), channel_id=1, source_target_pairs={{0,20},{1,17},{2,22},{3,19},{4,2},{5,7},{6,0},{7,5},{8,28},{9,25},... | collective-permute-start | bytes 110600 | tf_op jit(solution)/shard_map/ppermute | solution.py:50
  16.8 4.3 %collective-permute-start.12 = (bf16[16,1152]{1,0:T(8,128)(2,1)S(1)}, bf16[16,1152]{1,0:T(8,128)(2,1)S(1)}, u32[]{:S(2)}, u32[]{:S(2)}) collective-permute-start(bf16[16,1152]{1,0:T(8,128)(2,1)S(1)} %get-tuple-element.24), channel_id=1, source_target_pairs={{0,16},{1,21},{2,18},{3,23},{4,6},{5,3},{6,4},{7,1},{8,24},{9,29},... | collective-permute-start | bytes 110600 | tf_op jit(solution)/shard_map/ppermute | solution.py:50
  20.3 1.3 %collective-permute-start.13 = (bf16[16,1152]{1,0:T(8,128)(2,1)S(1)}, bf16[16,1152]{1,0:T(8,128)(2,1)S(1)}, u32[]{:S(2)}, u32[]{:S(2)}) collective-permute-start(bf16[16,1152]{1,0:T(8,128)(2,1)S(1)} %get-tuple-element.25), channel_id=1, source_target_pairs={{0,4},{4,0},{8,12},{12,8},{16,20},{20,16},{24,28},{28,24},{1,5},{5... | collective-permute-start | bytes 110600 | tf_op jit(solution)/shard_map/ppermute | solution.py:37

commit v20 on v19

--- a/solution.py
+++ b/solution.py
@@ -183,7 +183,7 @@
     order = list(range(blocks - 1, 0, -1))
     mine = [mine] + [chip_swap(mine, k) for k in order]
     other = [other, *[core_swap(block) for block in mine[1:-1]], chip_swap(mine[0], 1, lambda txt: 1)]
-    split = min(2, blocks - 1)
+    split = blocks - 1
     own, first, second, *send = call(
         functools.partial(pair_kernel, blocks, split),
         [total] + [piece] * 2 + [pair] * (blocks - 2),

time: 22.7 us -> 22.5 us (level)
  no operation moved by 1% of the time
where the time goes in v20:
time: 22.5 us; the launch traced here: 22.3 us
  starting transfers between devices  12.7 us (56%)
  waiting for transfers between devices  6.6 us (29%)
  Pallas kernels  1.58 us (7%)
  local copies, waits for them, and re-layouts  0.79 us (4%)
  between operations  0.68 us (3%)
    ppermute x8, starting transfers between devices, chip_swap(): return lax.ppermute(block, ('img', 'txt'), pairs)  10.8 us
    ppermute x8, waiting for transfers between devices, chip_swap(): return lax.ppermute(block, ('img', 'txt'), pairs)  4.71 us
    ppermute x6, waiting for transfers between devices, core_swap(): return lax.ppermute(block, 'img', [(i, i ^ 1) for i in range(size)])  1.89 us
    ppermute x6, starting transfers between devices, core_swap(): return lax.ppermute(block, 'img', [(i, i ^ 1) for i in range(size)])  1.85 us
    pallas_call x5, Pallas kernels, call(): pl.pallas_call(kernel, out_shape=outs, in_specs=[VMEM] * len(args), out_s...  1.58 us
    unnamed x5, local copies, waits for them, and re-layouts  0.78 us
  transfers between devices with their start and end apart: 14, of which 9 were waited for; matrix products, arithmetic and copies ran while one was open for 3% of the time, Pallas kernels for 1%

profile of v20, /device:TPU:0, one launch (start us, length us, event | category | flops | bytes accessed | tf_op | source)
XLA Modules:
  0.0 22.3 jit_solution(9144399439502163375)
XLA Ops:
  0.6 0.5 %collective-permute-start.2 = (bf16[16,1152]{1,0:T(8,128)(2,1)}, bf16[16,1152]{1,0:T(8,128)(2,1)S(1)}, u32[]{:S(2)}, u32[]{:S(2)}) collective-permute-start(bf16[16,1152]{1,0:T(8,128)(2,1)} %param.3), channel_id=1, source_target_pairs={{0,4},{4,0},{8,12},{12,8},{16,20},{20,16},{24,28},{28,24},{1,5},{5... | collective-permute-start | bytes 110600 | tf_op jit(solution)/shard_map/ppermute | solution.py:37
  1.2 0.8 %constant_dynamic-update-slice_fusion.1 = bf16[32,1152]{1,0:T(8,128)(2,1)S(1)} fusion(bf16[16,1152]{1,0:T(8,128)(2,1)} %param.4), kind=kLoop, calls=%fused_computation.1 | loop fusion | bytes 73728
  2.0 0.2 collective-permute-done.2.img_ref
  2.2 0.3 %collective-permute-done.1.txt_ref = bf16[16,1152]{1,0:T(8,128)(2,1)S(1)} collective-permute-done((bf16[16,1152]{1,0:T(8,128)(2,1)}, bf16[16,1152]{1,0:T(8,128)(2,1)S(1)}, u32[]{:S(2)}, u32[]{:S(2)}) %collective-permute-start.1) | collective-permute-done | bytes 36896 | tf_op jit(solution)/shard_map/ppermute | solution.py:37
  2.6 0.1 shard_map.50
  2.7 2.7 %collective-permute-start.4 = (bf16[32,1152]{1,0:T(8,128)(2,1)S(1)}, bf16[32,1152]{1,0:T(8,128)(2,1)S(1)}, u32[]{:S(2)}, u32[]{:S(2)}) collective-permute-start(bf16[32,1152]{1,0:T(8,128)(2,1)S(1)} %get-tuple-element.14.refs_0_), channel_id=1, source_target_pairs={{0,16},{1,17},{2,18},{3,19},{4,6},{5,7},{6,4},{7,5},{8,24},{9,25},... | collective-permute-start | bytes 221192 | tf_op jit(solution)/shard_map/ppermute | solution.py:50
  5.5 1.4 %collective-permute-start.3 = (bf16[32,1152]{1,0:T(8,128)(2,1)S(1)}, bf16[32,1152]{1,0:T(8,128)(2,1)S(1)}, u32[]{:S(2)}, u32[]{:S(2)}) collective-permute-start(bf16[32,1152]{1,0:T(8,128)(2,1)S(1)} %get-tuple-element.14.refs_0_), channel_id=1, source_target_pairs={{0,24},{1,25},{2,26},{3,27},{4,7},{5,6},{6,5},{7,4},{8,16},{9,17},... | collective-permute-start | bytes 221192 | tf_op jit(solution)/shard_map/ppermute | solution.py:50
  6.9 1.9 %collective-permute-start.8 = (bf16[32,1152]{1,0:T(8,128)(2,1)S(1)}, bf16[32,1152]{1,0:T(8,128)(2,1)S(1)}, u32[]{:S(2)}, u32[]{:S(2)}) collective-permute-start(bf16[32,1152]{1,0:T(8,128)(2,1)S(1)} %get-tuple-element.14.refs_0_), channel_id=1, source_target_pairs={{0,12},{1,13},{2,14},{3,15},{4,1},{5,0},{6,3},{7,2},{8,4},{9,5},{1... | collective-permute-start | bytes 221192 | tf_op jit(solution)/shard_map/ppermute | solution.py:50
  8.8 0.5 %collective-permute-start.5 = (bf16[32,1152]{1,0:T(8,128)(2,1)S(1)}, bf16[32,1152]{1,0:T(8,128)(2,1)S(1)}, u32[]{:S(2)}, u32[]{:S(2)}) collective-permute-start(bf16[32,1152]{1,0:T(8,128)(2,1)S(1)} %get-tuple-element.14.refs_0_), channel_id=1, source_target_pairs={{0,8},{1,9},{2,10},{3,11},{4,5},{5,4},{6,7},{7,6},{8,0},{9,1},{10,... | collective-permute-start | bytes 221192 | tf_op jit(solution)/shard_map/ppermute | solution.py:50
  9.3 1.4 %collective-permute-done.3.refs_1_ = bf16[32,1152]{1,0:T(8,128)(2,1)S(1)} collective-permute-done((bf16[32,1152]{1,0:T(8,128)(2,1)S(1)}, bf16[32,1152]{1,0:T(8,128)(2,1)S(1)}, u32[]{:S(2)}, u32[]{:S(2)}) %collective-permute-start.3) | collective-permute-done | bytes 73760 | tf_op jit(solution)/shard_map/ppermute | solution.py:50
  10.7 1.0 %collective-permute-start.6 = (bf16[32,1152]{1,0:T(8,128)(2,1)S(1)}, bf16[32,1152]{1,0:T(8,128)(2,1)S(1)}, u32[]{:S(2)}, u32[]{:S(2)}) collective-permute-start(bf16[32,1152]{1,0:T(8,128)(2,1)S(1)} %collective-permute-done.3.refs_1_), channel_id=1, source_target_pairs={{0,4},{4,0},{8,12},{12,8},{16,20},{20,16},{24,28},{28,24},{1,5},{5... | collective-permute-start | bytes 221192 | tf_op jit(solution)/shard_map/ppermute | solution.py:37
  11.7 1.1 %collective-permute-done.far_ids_ref = s32[1,64]{1,0:T(1,128)S(1)} collective-permute-done((s32[1,64]{1,0:T(1,128)S(1)}, s32[1,64]{1,0:T(1,128)S(1)}, u32[]{:S(2)}, u32[]{:S(2)}) %collective-permute-start) | collective-permute-done | bytes 288 | tf_op jit(solution)/shard_map/ppermute | solution.py:37
  12.8 0.3 %collective-permute-done.5.refs_3_ = bf16[32,1152]{1,0:T(8,128)(2,1)S(1)} collective-permute-done((bf16[32,1152]{1,0:T(8,128)(2,1)S(1)}, bf16[32,1152]{1,0:T(8,128)(2,1)S(1)}, u32[]{:S(2)}, u32[]{:S(2)}) %collective-permute-start.5) | collective-permute-done | bytes 73760 | tf_op jit(solution)/shard_map/ppermute | solution.py:50
  13.2 0.5 %shard_map.51 = (f32[32,1152]{1,0:T(8,128)S(1)}, bf16[16,1152]{1,0:T(8,128)(2,1)S(1)}, bf16[16,1152]{1,0:T(8,128)(2,1)S(1)}, bf16[32,1152]{1,0:T(8,128)(2,1)S(1)}, bf16[32,1152]{1,0:T(8,128)(2,1)S(1)}) custom-call(s32[1,64]{1,0:T(1,128)S(1)} %bitcast.2, s32[1,64]{1,0:T(1,128)S(1)} %collective-permute-done.far_ids_ref, ...), custom_call_target="tpu_custom_call" | custom-call | tf_op jit(solution)/shard_map/pallas_call | solution.py:63
  13.7 2.2 %collective-permute-start.10 = (bf16[32,1152]{1,0:T(8,128)(2,1)S(1)}, bf16[32,1152]{1,0:T(8,128)(2,1)S(1)}, u32[]{:S(2)}, u32[]{:S(2)}) collective-permute-start(bf16[32,1152]{1,0:T(8,128)(2,1)S(1)} %get-tuple-element.21), channel_id=1, source_target_pairs={{0,24},{1,25},{2,26},{3,27},{4,7},{5,6},{6,5},{7,4},{8,16},{9,17},... | collective-permute-start | bytes 221192 | tf_op jit(solution)/shard_map/ppermute | solution.py:50
  15.9 0.5 %collective-permute-start.11 = (bf16[32,1152]{1,0:T(8,128)(2,1)S(1)}, bf16[32,1152]{1,0:T(8,128)(2,1)S(1)}, u32[]{:S(2)}, u32[]{:S(2)}) collective-permute-start(bf16[32,1152]{1,0:T(8,128)(2,1)S(1)} %get-tuple-element.22), channel_id=1, source_target_pairs={{0,16},{1,17},{2,18},{3,19},{4,6},{5,7},{6,4},{7,5},{8,24},{9,25},... | collective-permute-start | bytes 221192 | tf_op jit(solution)/shard_map/ppermute | solution.py:50
  16.4 1.0 %collective-permute-start.9 = (bf16[16,1152]{1,0:T(8,128)(2,1)S(1)}, bf16[16,1152]{1,0:T(8,128)(2,1)S(1)}, u32[]{:S(2)}, u32[]{:S(2)}) collective-permute-start(bf16[16,1152]{1,0:T(8,128)(2,1)S(1)} %get-tuple-element.16), channel_id=1, source_target_pairs={{0,12},{1,13},{2,14},{3,15},{4,1},{5,0},{6,3},{7,2},{8,4},{9,5},{1... | collective-permute-start | bytes 110600 | tf_op jit(solution)/shard_map/ppermute | solution.py:50
  17.4 0.5 %collective-permute-start.12 = (bf16[16,1152]{1,0:T(8,128)(2,1)S(1)}, bf16[16,1152]{1,0:T(8,128)(2,1)S(1)}, u32[]{:S(2)}, u32[]{:S(2)}) collective-permute-start(bf16[16,1152]{1,0:T(8,128)(2,1)S(1)} %get-tuple-element.24), channel_id=1, source_target_pairs={{0,8},{1,9},{2,10},{3,11},{4,5},{5,4},{6,7},{7,6},{8,0},{9,1},{10,... | collective-permute-start | bytes 110600 | tf_op jit(solution)/shard_map/ppermute | solution.py:50
  17.9 1.1 %collective-permute-done.10.refs_0_ = bf16[32,1152]{1,0:T(8,128)(2,1)S(1)} collective-permute-done((bf16[32,1152]{1,0:T(8,128)(2,1)S(1)}, bf16[32,1152]{1,0:T(8,128)(2,1)S(1)}, u32[]{:S(2)}, u32[]{:S(2)}) %collective-permute-start.10) | collective-permute-done | bytes 73760 | tf_op jit(solution)/shard_map/ppermute | solution.py:50
  19.0 1.2 %collective-permute-done.11.refs_1_ = bf16[32,1152]{1,0:T(8,128)(2,1)S(1)} collective-permute-done((bf16[32,1152]{1,0:T(8,128)(2,1)S(1)}, bf16[32,1152]{1,0:T(8,128)(2,1)S(1)}, u32[]{:S(2)}, u32[]{:S(2)}) %collective-permute-start.11) | collective-permute-done | bytes 73760 | tf_op jit(solution)/shard_map/ppermute | solution.py:50
  20.3 0.3 %collective-permute-start.13 = (bf16[16,1152]{1,0:T(8,128)(2,1)S(1)}, bf16[16,1152]{1,0:T(8,128)(2,1)S(1)}, u32[]{:S(2)}, u32[]{:S(2)}) collective-permute-start(bf16[16,1152]{1,0:T(8,128)(2,1)S(1)} %get-tuple-element.25), channel_id=1, source_target_pairs={{0,4},{4,0},{8,12},{12,8},{16,20},{20,16},{24,28},{28,24},{1,5},{5... | collective-permute-start | bytes 110600 | tf_op jit(solution)/shard_map/ppermute | solution.py:37
  20.7 0.7 %collective-permute-done.12.second_ref = bf16[16,1152]{1,0:T(8,128)(2,1)S(1)} collective-permute-done((bf16[16,1152]{1,0:T(8,128)(2,1)S(1)}, bf16[16,1152]{1,0:T(8,128)(2,1)S(1)}, u32[]{:S(2)}, u32[]{:S(2)}) %collective-permute-start.12) | collective-permute-done | bytes 36896 | tf_op jit(solution)/shard_map/ppermute | solution.py:50
  21.4 0.2 collective-permute-done.13.got_ref
  21.6 0.8 %shard_map.54 = (f32[16,1152]{1,0:T(8,128)}, f32[16,1152]{1,0:T(8,128)}) custom-call(f32[32,1152]{1,0:T(8,128)S(1)} %get-tuple-element.17.unit_ref, f32[32,1]{1,0:T(8,128)S(1)} %get-tuple-element.18.inverse_ref, f32[16,1152]{1,0:T(8,128)S(1)} %get-tuple-element.19.first_ref, f32[16,1152]{1,0:T(8,128)S(1)} %get-tuple-element.23.keep_ref, ...), custom_call_target="tpu_custom_call" | custom-call | tf_op jit(solution)/shard_map/pallas_call | solution.py:63
  (15 shorter events, 0.3 us)
Async XLA Ops:
  0.6 1.4 %copy-start.1 = (bf16[16,1152]{1,0:T(8,128)(2,1)S(1)}, bf16[16,1152]{1,0:T(8,128)(2,1)}, u32[]{:S(2)}) copy-start(bf16[16,1152]{1,0:T(8,128)(2,1)} %param.3) | copy-start | bytes 110596
  0.6 1.6 %collective-permute-start.2 = (bf16[16,1152]{1,0:T(8,128)(2,1)}, bf16[16,1152]{1,0:T(8,128)(2,1)S(1)}, u32[]{:S(2)}, u32[]{:S(2)}) collective-permute-start(bf16[16,1152]{1,0:T(8,128)(2,1)} %param.3), channel_id=1, source_target_pairs={{0,4},{4,0},{8,12},{12,8},{16,20},{20,16},{24,28},{28,24},{1,5},{5... | collective-permute-start | bytes 110600 | tf_op jit(solution)/shard_map/ppermute | solution.py:37
  1.2 1.4 %collective-permute-start.1 = (bf16[16,1152]{1,0:T(8,128)(2,1)}, bf16[16,1152]{1,0:T(8,128)(2,1)S(1)}, u32[]{:S(2)}, u32[]{:S(2)}) collective-permute-start(bf16[16,1152]{1,0:T(8,128)(2,1)} %param.4), channel_id=1, source_target_pairs={{0,4},{4,0},{8,12},{12,8},{16,20},{20,16},{24,28},{28,24},{1,5},{5... | collective-permute-start | bytes 110600 | tf_op jit(solution)/shard_map/ppermute | solution.py:37
  2.7 9.0 %copy-start = (s32[64]{0:T(128)S(1)}, s32[64]{0:T(128)}, u32[]{:S(2)}) copy-start(s32[64]{0:T(128)} %param.5) | copy-start | bytes 772
  2.7 6.6 %collective-permute-start.4 = (bf16[32,1152]{1,0:T(8,128)(2,1)S(1)}, bf16[32,1152]{1,0:T(8,128)(2,1)S(1)}, u32[]{:S(2)}, u32[]{:S(2)}) collective-permute-start(bf16[32,1152]{1,0:T(8,128)(2,1)S(1)} %get-tuple-element.14.refs_0_), channel_id=1, source_target_pairs={{0,16},{1,17},{2,18},{3,19},{4,6},{5,7},{6,4},{7,5},{8,24},{9,25},... | collective-permute-start | bytes 221192 | tf_op jit(solution)/shard_map/ppermute | solution.py:50
  5.5 5.3 %collective-permute-start.3 = (bf16[32,1152]{1,0:T(8,128)(2,1)S(1)}, bf16[32,1152]{1,0:T(8,128)(2,1)S(1)}, u32[]{:S(2)}, u32[]{:S(2)}) collective-permute-start(bf16[32,1152]{1,0:T(8,128)(2,1)S(1)} %get-tuple-element.14.refs_0_), channel_id=1, source_target_pairs={{0,24},{1,25},{2,26},{3,27},{4,7},{5,6},{6,5},{7,4},{8,16},{9,17},... | collective-permute-start | bytes 221192 | tf_op jit(solution)/shard_map/ppermute | solution.py:50
  6.9 5.9 %collective-permute-start.8 = (bf16[32,1152]{1,0:T(8,128)(2,1)S(1)}, bf16[32,1152]{1,0:T(8,128)(2,1)S(1)}, u32[]{:S(2)}, u32[]{:S(2)}) collective-permute-start(bf16[32,1152]{1,0:T(8,128)(2,1)S(1)} %get-tuple-element.14.refs_0_), channel_id=1, source_target_pairs={{0,12},{1,13},{2,14},{3,15},{4,1},{5,0},{6,3},{7,2},{8,4},{9,5},{1... | collective-permute-start | bytes 221192 | tf_op jit(solution)/shard_map/ppermute | solution.py:50
  8.8 4.4 %collective-permute-start.5 = (bf16[32,1152]{1,0:T(8,128)(2,1)S(1)}, bf16[32,1152]{1,0:T(8,128)(2,1)S(1)}, u32[]{:S(2)}, u32[]{:S(2)}) collective-permute-start(bf16[32,1152]{1,0:T(8,128)(2,1)S(1)} %get-tuple-element.14.refs_0_), channel_id=1, source_target_pairs={{0,8},{1,9},{2,10},{3,11},{4,5},{5,4},{6,7},{7,6},{8,0},{9,1},{10,... | collective-permute-start | bytes 221192 | tf_op jit(solution)/shard_map/ppermute | solution.py:50
  9.3 3.8 %collective-permute-start.7 = (bf16[32,1152]{1,0:T(8,128)(2,1)S(1)}, bf16[32,1152]{1,0:T(8,128)(2,1)S(1)}, u32[]{:S(2)}, u32[]{:S(2)}) collective-permute-start(bf16[32,1152]{1,0:T(8,128)(2,1)S(1)} %collective-permute-done.4.refs_2_), channel_id=1, source_target_pairs={{0,4},{4,0},{8,12},{12,8},{16,20},{20,16},{24,28},{28,24},{1,5},{5... | collective-permute-start | bytes 221192 | tf_op jit(solution)/shard_map/ppermute | solution.py:37
  10.7 2.4 %collective-permute-start.6 = (bf16[32,1152]{1,0:T(8,128)(2,1)S(1)}, bf16[32,1152]{1,0:T(8,128)(2,1)S(1)}, u32[]{:S(2)}, u32[]{:S(2)}) collective-permute-start(bf16[32,1152]{1,0:T(8,128)(2,1)S(1)} %collective-permute-done.3.refs_1_), channel_id=1, source_target_pairs={{0,4},{4,0},{8,12},{12,8},{16,20},{20,16},{24,28},{28,24},{1,5},{5... | collective-permute-start | bytes 221192 | tf_op jit(solution)/shard_map/ppermute | solution.py:37
  11.7 1.1 %collective-permute-start = (s32[1,64]{1,0:T(1,128)S(1)}, s32[1,64]{1,0:T(1,128)S(1)}, u32[]{:S(2)}, u32[]{:S(2)}) collective-permute-start(s32[1,64]{1,0:T(1,128)S(1)} %bitcast.1), channel_id=1, source_target_pairs={{0,4},{4,0},{8,12},{12,8},{16,20},{20,16},{24,28},{28,24},{1,5},{5... | collective-permute-start | bytes 776 | tf_op jit(solution)/shard_map/ppermute | solution.py:37
  13.7 5.3 %collective-permute-start.10 = (bf16[32,1152]{1,0:T(8,128)(2,1)S(1)}, bf16[32,1152]{1,0:T(8,128)(2,1)S(1)}, u32[]{:S(2)}, u32[]{:S(2)}) collective-permute-start(bf16[32,1152]{1,0:T(8,128)(2,1)S(1)} %get-tuple-element.21), channel_id=1, source_target_pairs={{0,24},{1,25},{2,26},{3,27},{4,7},{5,6},{6,5},{7,4},{8,16},{9,17},... | collective-permute-start | bytes 221192 | tf_op jit(solution)/shard_map/ppermute | solution.py:50
  15.9 4.4 %collective-permute-start.11 = (bf16[32,1152]{1,0:T(8,128)(2,1)S(1)}, bf16[32,1152]{1,0:T(8,128)(2,1)S(1)}, u32[]{:S(2)}, u32[]{:S(2)}) collective-permute-start(bf16[32,1152]{1,0:T(8,128)(2,1)S(1)} %get-tuple-element.22), channel_id=1, source_target_pairs={{0,16},{1,17},{2,18},{3,19},{4,6},{5,7},{6,4},{7,5},{8,24},{9,25},... | collective-permute-start | bytes 221192 | tf_op jit(solution)/shard_map/ppermute | solution.py:50
  16.4 4.2 %collective-permute-start.9 = (bf16[16,1152]{1,0:T(8,128)(2,1)S(1)}, bf16[16,1152]{1,0:T(8,128)(2,1)S(1)}, u32[]{:S(2)}, u32[]{:S(2)}) collective-permute-start(bf16[16,1152]{1,0:T(8,128)(2,1)S(1)} %get-tuple-element.16), channel_id=1, source_target_pairs={{0,12},{1,13},{2,14},{3,15},{4,1},{5,0},{6,3},{7,2},{8,4},{9,5},{1... | collective-permute-start | bytes 110600 | tf_op jit(solution)/shard_map/ppermute | solution.py:50
  17.4 4.0 %collective-permute-start.12 = (bf16[16,1152]{1,0:T(8,128)(2,1)S(1)}, bf16[16,1152]{1,0:T(8,128)(2,1)S(1)}, u32[]{:S(2)}, u32[]{:S(2)}) collective-permute-start(bf16[16,1152]{1,0:T(8,128)(2,1)S(1)} %get-tuple-element.24), channel_id=1, source_target_pairs={{0,8},{1,9},{2,10},{3,11},{4,5},{5,4},{6,7},{7,6},{8,0},{9,1},{10,... | collective-permute-start | bytes 110600 | tf_op jit(solution)/shard_map/ppermute | solution.py:50
  20.3 1.3 %collective-permute-start.13 = (bf16[16,1152]{1,0:T(8,128)(2,1)S(1)}, bf16[16,1152]{1,0:T(8,128)(2,1)S(1)}, u32[]{:S(2)}, u32[]{:S(2)}) collective-permute-start(bf16[16,1152]{1,0:T(8,128)(2,1)S(1)} %get-tuple-element.25), channel_id=1, source_target_pairs={{0,4},{4,0},{8,12},{12,8},{16,20},{20,16},{24,28},{28,24},{1,5},{5... | collective-permute-start | bytes 110600 | tf_op jit(solution)/shard_map/ppermute | solution.py:37

commit v21 on v20

--- a/solution.py
+++ b/solution.py
@@ -190,7 +190,7 @@
         [ids, core_swap(ids), *mine, *other],
     )
     far = order.pop(split - 1)
-    got = [chip_swap(block, k) for k, block in zip(order, send)]
+    got = [chip_swap(block, k) for k, block in zip(order, send)][::-1]
     first = chip_swap(first, far, lambda txt: int(txt % 2 == 0 or far % 2 == 1))
     second = chip_swap(second, far, lambda txt: int(txt % 2 == 1 and far % 2 == 0))
     keep, send = call(sum_kernel, [single, piece], [own, *got])

time: 22.5 us -> 22.8 us (1.013)
  waiting for transfers between devices: 6.6 us -> 7.01 us
where the time goes in v21:
time: 22.8 us; the launch traced here: 22.6 us
  starting transfers between devices  12.6 us (55%)
  waiting for transfers between devices  7.01 us (31%)
  Pallas kernels  1.58 us (7%)
  local copies, waits for them, and re-layouts  0.79 us (3%)
  between operations  0.7 us (3%)
    ppermute x8, starting transfers between devices, chip_swap(): return lax.ppermute(block, ('img', 'txt'), pairs)  10.9 us
    ppermute x8, waiting for transfers between devices, chip_swap(): return lax.ppermute(block, ('img', 'txt'), pairs)  4.92 us
    ppermute x6, waiting for transfers between devices, core_swap(): return lax.ppermute(block, 'img', [(i, i ^ 1) for i in range(size)])  2.09 us
    ppermute x6, starting transfers between devices, core_swap(): return lax.ppermute(block, 'img', [(i, i ^ 1) for i in range(size)])  1.63 us
    pallas_call x5, Pallas kernels, call(): pl.pallas_call(kernel, out_shape=outs, in_specs=[VMEM] * len(args), out_s...  1.58 us
    unnamed x5, local copies, waits for them, and re-layouts  0.78 us
  transfers between devices with their start and end apart: 14, of which 9 were waited for; matrix products, arithmetic and copies ran while one was open for 3% of the time, Pallas kernels for 1%

profile of v21, /device:TPU:0, one launch (start us, length us, event | category | flops | bytes accessed | tf_op | source)
XLA Modules:
  0.0 22.6 jit_solution(12522145168784080835)
XLA Ops:
  0.6 0.5 %collective-permute-start.2 = (bf16[16,1152]{1,0:T(8,128)(2,1)}, bf16[16,1152]{1,0:T(8,128)(2,1)S(1)}, u32[]{:S(2)}, u32[]{:S(2)}) collective-permute-start(bf16[16,1152]{1,0:T(8,128)(2,1)} %param.3), channel_id=1, source_target_pairs={{0,4},{4,0},{8,12},{12,8},{16,20},{20,16},{24,28},{28,24},{1,5},{5... | collective-permute-start | bytes 110600 | tf_op jit(solution)/shard_map/ppermute | solution.py:37
  1.2 0.8 %constant_dynamic-update-slice_fusion.1 = bf16[32,1152]{1,0:T(8,128)(2,1)S(1)} fusion(bf16[16,1152]{1,0:T(8,128)(2,1)} %param.4), kind=kLoop, calls=%fused_computation.1 | loop fusion | bytes 73728
  2.0 0.2 collective-permute-done.2.img_ref
  2.2 0.3 %collective-permute-done.1.txt_ref = bf16[16,1152]{1,0:T(8,128)(2,1)S(1)} collective-permute-done((bf16[16,1152]{1,0:T(8,128)(2,1)}, bf16[16,1152]{1,0:T(8,128)(2,1)S(1)}, u32[]{:S(2)}, u32[]{:S(2)}) %collective-permute-start.1) | collective-permute-done | bytes 36896 | tf_op jit(solution)/shard_map/ppermute | solution.py:37
  2.6 0.1 shard_map.50
  2.7 2.7 %collective-permute-start.4 = (bf16[32,1152]{1,0:T(8,128)(2,1)S(1)}, bf16[32,1152]{1,0:T(8,128)(2,1)S(1)}, u32[]{:S(2)}, u32[]{:S(2)}) collective-permute-start(bf16[32,1152]{1,0:T(8,128)(2,1)S(1)} %get-tuple-element.14.refs_0_), channel_id=1, source_target_pairs={{0,16},{1,17},{2,18},{3,19},{4,6},{5,7},{6,4},{7,5},{8,24},{9,25},... | collective-permute-start | bytes 221192 | tf_op jit(solution)/shard_map/ppermute | solution.py:50
  5.5 1.4 %collective-permute-start.3 = (bf16[32,1152]{1,0:T(8,128)(2,1)S(1)}, bf16[32,1152]{1,0:T(8,128)(2,1)S(1)}, u32[]{:S(2)}, u32[]{:S(2)}) collective-permute-start(bf16[32,1152]{1,0:T(8,128)(2,1)S(1)} %get-tuple-element.14.refs_0_), channel_id=1, source_target_pairs={{0,24},{1,25},{2,26},{3,27},{4,7},{5,6},{6,5},{7,4},{8,16},{9,17},... | collective-permute-start | bytes 221192 | tf_op jit(solution)/shard_map/ppermute | solution.py:50
  6.9 1.9 %collective-permute-start.8 = (bf16[32,1152]{1,0:T(8,128)(2,1)S(1)}, bf16[32,1152]{1,0:T(8,128)(2,1)S(1)}, u32[]{:S(2)}, u32[]{:S(2)}) collective-permute-start(bf16[32,1152]{1,0:T(8,128)(2,1)S(1)} %get-tuple-element.14.refs_0_), channel_id=1, source_target_pairs={{0,12},{1,13},{2,14},{3,15},{4,1},{5,0},{6,3},{7,2},{8,4},{9,5},{1... | collective-permute-start | bytes 221192 | tf_op jit(solution)/shard_map/ppermute | solution.py:50
  8.8 0.5 %collective-permute-start.5 = (bf16[32,1152]{1,0:T(8,128)(2,1)S(1)}, bf16[32,1152]{1,0:T(8,128)(2,1)S(1)}, u32[]{:S(2)}, u32[]{:S(2)}) collective-permute-start(bf16[32,1152]{1,0:T(8,128)(2,1)S(1)} %get-tuple-element.14.refs_0_), channel_id=1, source_target_pairs={{0,8},{1,9},{2,10},{3,11},{4,5},{5,4},{6,7},{7,6},{8,0},{9,1},{10,... | collective-permute-start | bytes 221192 | tf_op jit(solution)/shard_map/ppermute | solution.py:50
  9.3 1.4 %collective-permute-done.3.refs_1_ = bf16[32,1152]{1,0:T(8,128)(2,1)S(1)} collective-permute-done((bf16[32,1152]{1,0:T(8,128)(2,1)S(1)}, bf16[32,1152]{1,0:T(8,128)(2,1)S(1)}, u32[]{:S(2)}, u32[]{:S(2)}) %collective-permute-start.3) | collective-permute-done | bytes 73760 | tf_op jit(solution)/shard_map/ppermute | solution.py:50
  10.7 1.0 %collective-permute-start.6 = (bf16[32,1152]{1,0:T(8,128)(2,1)S(1)}, bf16[32,1152]{1,0:T(8,128)(2,1)S(1)}, u32[]{:S(2)}, u32[]{:S(2)}) collective-permute-start(bf16[32,1152]{1,0:T(8,128)(2,1)S(1)} %collective-permute-done.3.refs_1_), channel_id=1, source_target_pairs={{0,4},{4,0},{8,12},{12,8},{16,20},{20,16},{24,28},{28,24},{1,5},{5... | collective-permute-start | bytes 221192 | tf_op jit(solution)/shard_map/ppermute | solution.py:37
  11.7 1.1 %collective-permute-done.far_ids_ref = s32[1,64]{1,0:T(1,128)S(1)} collective-permute-done((s32[1,64]{1,0:T(1,128)S(1)}, s32[1,64]{1,0:T(1,128)S(1)}, u32[]{:S(2)}, u32[]{:S(2)}) %collective-permute-start) | collective-permute-done | bytes 288 | tf_op jit(solution)/shard_map/ppermute | solution.py:37
  12.8 0.3 %collective-permute-done.5.refs_3_ = bf16[32,1152]{1,0:T(8,128)(2,1)S(1)} collective-permute-done((bf16[32,1152]{1,0:T(8,128)(2,1)S(1)}, bf16[32,1152]{1,0:T(8,128)(2,1)S(1)}, u32[]{:S(2)}, u32[]{:S(2)}) %collective-permute-start.5) | collective-permute-done | bytes 73760 | tf_op jit(solution)/shard_map/ppermute | solution.py:50
  13.2 0.5 %shard_map.51 = (f32[32,1152]{1,0:T(8,128)S(1)}, bf16[16,1152]{1,0:T(8,128)(2,1)S(1)}, bf16[16,1152]{1,0:T(8,128)(2,1)S(1)}, bf16[32,1152]{1,0:T(8,128)(2,1)S(1)}, bf16[32,1152]{1,0:T(8,128)(2,1)S(1)}) custom-call(s32[1,64]{1,0:T(1,128)S(1)} %bitcast.2, s32[1,64]{1,0:T(1,128)S(1)} %collective-permute-done.far_ids_ref, ...), custom_call_target="tpu_custom_call" | custom-call | tf_op jit(solution)/shard_map/pallas_call | solution.py:63
  13.7 1.6 %collective-permute-start.10 = (bf16[32,1152]{1,0:T(8,128)(2,1)S(1)}, bf16[32,1152]{1,0:T(8,128)(2,1)S(1)}, u32[]{:S(2)}, u32[]{:S(2)}) collective-permute-start(bf16[32,1152]{1,0:T(8,128)(2,1)S(1)} %get-tuple-element.21), channel_id=1, source_target_pairs={{0,16},{1,17},{2,18},{3,19},{4,6},{5,7},{6,4},{7,5},{8,24},{9,25},... | collective-permute-start | bytes 221192 | tf_op jit(solution)/shard_map/ppermute | solution.py:50
  15.3 1.1 %collective-permute-start.11 = (bf16[32,1152]{1,0:T(8,128)(2,1)S(1)}, bf16[32,1152]{1,0:T(8,128)(2,1)S(1)}, u32[]{:S(2)}, u32[]{:S(2)}) collective-permute-start(bf16[32,1152]{1,0:T(8,128)(2,1)S(1)} %get-tuple-element.22), channel_id=1, source_target_pairs={{0,24},{1,25},{2,26},{3,27},{4,7},{5,6},{6,5},{7,4},{8,16},{9,17},... | collective-permute-start | bytes 221192 | tf_op jit(solution)/shard_map/ppermute | solution.py:50
  16.4 1.1 %collective-permute-start.9 = (bf16[16,1152]{1,0:T(8,128)(2,1)S(1)}, bf16[16,1152]{1,0:T(8,128)(2,1)S(1)}, u32[]{:S(2)}, u32[]{:S(2)}) collective-permute-start(bf16[16,1152]{1,0:T(8,128)(2,1)S(1)} %get-tuple-element.16), channel_id=1, source_target_pairs={{0,12},{1,13},{2,14},{3,15},{4,1},{5,0},{6,3},{7,2},{8,4},{9,5},{1... | collective-permute-start | bytes 110600 | tf_op jit(solution)/shard_map/ppermute | solution.py:50
  17.5 0.5 %collective-permute-start.12 = (bf16[16,1152]{1,0:T(8,128)(2,1)S(1)}, bf16[16,1152]{1,0:T(8,128)(2,1)S(1)}, u32[]{:S(2)}, u32[]{:S(2)}) collective-permute-start(bf16[16,1152]{1,0:T(8,128)(2,1)S(1)} %get-tuple-element.24), channel_id=1, source_target_pairs={{0,8},{1,9},{2,10},{3,11},{4,5},{5,4},{6,7},{7,6},{8,0},{9,1},{10,... | collective-permute-start | bytes 110600 | tf_op jit(solution)/shard_map/ppermute | solution.py:50
  18.0 0.1 collective-permute-done.10.refs_0_
  18.1 2.4 %collective-permute-done.11.refs_1_ = bf16[32,1152]{1,0:T(8,128)(2,1)S(1)} collective-permute-done((bf16[32,1152]{1,0:T(8,128)(2,1)S(1)}, bf16[32,1152]{1,0:T(8,128)(2,1)S(1)}, u32[]{:S(2)}, u32[]{:S(2)}) %collective-permute-start.11) | collective-permute-done | bytes 73760 | tf_op jit(solution)/shard_map/ppermute | solution.py:50
  20.7 0.1 shard_map.52
  20.8 0.7 %collective-permute-done.12.second_ref = bf16[16,1152]{1,0:T(8,128)(2,1)S(1)} collective-permute-done((bf16[16,1152]{1,0:T(8,128)(2,1)S(1)}, bf16[16,1152]{1,0:T(8,128)(2,1)S(1)}, u32[]{:S(2)}, u32[]{:S(2)}) %collective-permute-start.12) | collective-permute-done | bytes 36896 | tf_op jit(solution)/shard_map/ppermute | solution.py:50
  21.4 0.4 %collective-permute-done.13.got_ref = bf16[16,1152]{1,0:T(8,128)(2,1)S(1)} collective-permute-done((bf16[16,1152]{1,0:T(8,128)(2,1)S(1)}, bf16[16,1152]{1,0:T(8,128)(2,1)S(1)}, u32[]{:S(2)}, u32[]{:S(2)}) %collective-permute-start.13) | collective-permute-done | bytes 36896 | tf_op jit(solution)/shard_map/ppermute | solution.py:37
  21.9 0.8 %shard_map.54 = (f32[16,1152]{1,0:T(8,128)}, f32[16,1152]{1,0:T(8,128)}) custom-call(f32[32,1152]{1,0:T(8,128)S(1)} %get-tuple-element.17.unit_ref, f32[32,1]{1,0:T(8,128)S(1)} %get-tuple-element.18.inverse_ref, f32[16,1152]{1,0:T(8,128)S(1)} %get-tuple-element.19.first_ref, f32[16,1152]{1,0:T(8,128)S(1)} %get-tuple-element.23.keep_ref, ...), custom_call_target="tpu_custom_call" | custom-call | tf_op jit(solution)/shard_map/pallas_call | solution.py:63
  (15 shorter events, 0.2 us)
Async XLA Ops:
  0.6 1.4 %copy-start.1 = (bf16[16,1152]{1,0:T(8,128)(2,1)S(1)}, bf16[16,1152]{1,0:T(8,128)(2,1)}, u32[]{:S(2)}) copy-start(bf16[16,1152]{1,0:T(8,128)(2,1)} %param.3) | copy-start | bytes 110596
  0.6 1.6 %collective-permute-start.2 = (bf16[16,1152]{1,0:T(8,128)(2,1)}, bf16[16,1152]{1,0:T(8,128)(2,1)S(1)}, u32[]{:S(2)}, u32[]{:S(2)}) collective-permute-start(bf16[16,1152]{1,0:T(8,128)(2,1)} %param.3), channel_id=1, source_target_pairs={{0,4},{4,0},{8,12},{12,8},{16,20},{20,16},{24,28},{28,24},{1,5},{5... | collective-permute-start | bytes 110600 | tf_op jit(solution)/shard_map/ppermute | solution.py:37
  1.2 1.4 %collective-permute-start.1 = (bf16[16,1152]{1,0:T(8,128)(2,1)}, bf16[16,1152]{1,0:T(8,128)(2,1)S(1)}, u32[]{:S(2)}, u32[]{:S(2)}) collective-permute-start(bf16[16,1152]{1,0:T(8,128)(2,1)} %param.4), channel_id=1, source_target_pairs={{0,4},{4,0},{8,12},{12,8},{16,20},{20,16},{24,28},{28,24},{1,5},{5... | collective-permute-start | bytes 110600 | tf_op jit(solution)/shard_map/ppermute | solution.py:37
  2.7 9.0 %copy-start = (s32[64]{0:T(128)S(1)}, s32[64]{0:T(128)}, u32[]{:S(2)}) copy-start(s32[64]{0:T(128)} %param.5) | copy-start | bytes 772
  2.7 6.6 %collective-permute-start.4 = (bf16[32,1152]{1,0:T(8,128)(2,1)S(1)}, bf16[32,1152]{1,0:T(8,128)(2,1)S(1)}, u32[]{:S(2)}, u32[]{:S(2)}) collective-permute-start(bf16[32,1152]{1,0:T(8,128)(2,1)S(1)} %get-tuple-element.14.refs_0_), channel_id=1, source_target_pairs={{0,16},{1,17},{2,18},{3,19},{4,6},{5,7},{6,4},{7,5},{8,24},{9,25},... | collective-permute-start | bytes 221192 | tf_op jit(solution)/shard_map/ppermute | solution.py:50
  5.5 5.3 %collective-permute-start.3 = (bf16[32,1152]{1,0:T(8,128)(2,1)S(1)}, bf16[32,1152]{1,0:T(8,128)(2,1)S(1)}, u32[]{:S(2)}, u32[]{:S(2)}) collective-permute-start(bf16[32,1152]{1,0:T(8,128)(2,1)S(1)} %get-tuple-element.14.refs_0_), channel_id=1, source_target_pairs={{0,24},{1,25},{2,26},{3,27},{4,7},{5,6},{6,5},{7,4},{8,16},{9,17},... | collective-permute-start | bytes 221192 | tf_op jit(solution)/shard_map/ppermute | solution.py:50
  6.9 5.9 %collective-permute-start.8 = (bf16[32,1152]{1,0:T(8,128)(2,1)S(1)}, bf16[32,1152]{1,0:T(8,128)(2,1)S(1)}, u32[]{:S(2)}, u32[]{:S(2)}) collective-permute-start(bf16[32,1152]{1,0:T(8,128)(2,1)S(1)} %get-tuple-element.14.refs_0_), channel_id=1, source_target_pairs={{0,12},{1,13},{2,14},{3,15},{4,1},{5,0},{6,3},{7,2},{8,4},{9,5},{1... | collective-permute-start | bytes 221192 | tf_op jit(solution)/shard_map/ppermute | solution.py:50
  8.8 4.4 %collective-permute-start.5 = (bf16[32,1152]{1,0:T(8,128)(2,1)S(1)}, bf16[32,1152]{1,0:T(8,128)(2,1)S(1)}, u32[]{:S(2)}, u32[]{:S(2)}) collective-permute-start(bf16[32,1152]{1,0:T(8,128)(2,1)S(1)} %get-tuple-element.14.refs_0_), channel_id=1, source_target_pairs={{0,8},{1,9},{2,10},{3,11},{4,5},{5,4},{6,7},{7,6},{8,0},{9,1},{10,... | collective-permute-start | bytes 221192 | tf_op jit(solution)/shard_map/ppermute | solution.py:50
  9.3 3.8 %collective-permute-start.7 = (bf16[32,1152]{1,0:T(8,128)(2,1)S(1)}, bf16[32,1152]{1,0:T(8,128)(2,1)S(1)}, u32[]{:S(2)}, u32[]{:S(2)}) collective-permute-start(bf16[32,1152]{1,0:T(8,128)(2,1)S(1)} %collective-permute-done.4.refs_2_), channel_id=1, source_target_pairs={{0,4},{4,0},{8,12},{12,8},{16,20},{20,16},{24,28},{28,24},{1,5},{5... | collective-permute-start | bytes 221192 | tf_op jit(solution)/shard_map/ppermute | solution.py:37
  10.7 2.4 %collective-permute-start.6 = (bf16[32,1152]{1,0:T(8,128)(2,1)S(1)}, bf16[32,1152]{1,0:T(8,128)(2,1)S(1)}, u32[]{:S(2)}, u32[]{:S(2)}) collective-permute-start(bf16[32,1152]{1,0:T(8,128)(2,1)S(1)} %collective-permute-done.3.refs_1_), channel_id=1, source_target_pairs={{0,4},{4,0},{8,12},{12,8},{16,20},{20,16},{24,28},{28,24},{1,5},{5... | collective-permute-start | bytes 221192 | tf_op jit(solution)/shard_map/ppermute | solution.py:37
  11.7 1.1 %collective-permute-start = (s32[1,64]{1,0:T(1,128)S(1)}, s32[1,64]{1,0:T(1,128)S(1)}, u32[]{:S(2)}, u32[]{:S(2)}) collective-permute-start(s32[1,64]{1,0:T(1,128)S(1)} %bitcast.1), channel_id=1, source_target_pairs={{0,4},{4,0},{8,12},{12,8},{16,20},{20,16},{24,28},{28,24},{1,5},{5... | collective-permute-start | bytes 776 | tf_op jit(solution)/shard_map/ppermute | solution.py:37
  13.7 4.4 %collective-permute-start.10 = (bf16[32,1152]{1,0:T(8,128)(2,1)S(1)}, bf16[32,1152]{1,0:T(8,128)(2,1)S(1)}, u32[]{:S(2)}, u32[]{:S(2)}) collective-permute-start(bf16[32,1152]{1,0:T(8,128)(2,1)S(1)} %get-tuple-element.21), channel_id=1, source_target_pairs={{0,16},{1,17},{2,18},{3,19},{4,6},{5,7},{6,4},{7,5},{8,24},{9,25},... | collective-permute-start | bytes 221192 | tf_op jit(solution)/shard_map/ppermute | solution.py:50
  15.3 5.3 %collective-permute-start.11 = (bf16[32,1152]{1,0:T(8,128)(2,1)S(1)}, bf16[32,1152]{1,0:T(8,128)(2,1)S(1)}, u32[]{:S(2)}, u32[]{:S(2)}) collective-permute-start(bf16[32,1152]{1,0:T(8,128)(2,1)S(1)} %get-tuple-element.22), channel_id=1, source_target_pairs={{0,24},{1,25},{2,26},{3,27},{4,7},{5,6},{6,5},{7,4},{8,16},{9,17},... | collective-permute-start | bytes 221192 | tf_op jit(solution)/shard_map/ppermute | solution.py:50
  16.4 4.2 %collective-permute-start.9 = (bf16[16,1152]{1,0:T(8,128)(2,1)S(1)}, bf16[16,1152]{1,0:T(8,128)(2,1)S(1)}, u32[]{:S(2)}, u32[]{:S(2)}) collective-permute-start(bf16[16,1152]{1,0:T(8,128)(2,1)S(1)} %get-tuple-element.16), channel_id=1, source_target_pairs={{0,12},{1,13},{2,14},{3,15},{4,1},{5,0},{6,3},{7,2},{8,4},{9,5},{1... | collective-permute-start | bytes 110600 | tf_op jit(solution)/shard_map/ppermute | solution.py:50
  17.5 4.0 %collective-permute-start.12 = (bf16[16,1152]{1,0:T(8,128)(2,1)S(1)}, bf16[16,1152]{1,0:T(8,128)(2,1)S(1)}, u32[]{:S(2)}, u32[]{:S(2)}) collective-permute-start(bf16[16,1152]{1,0:T(8,128)(2,1)S(1)} %get-tuple-element.24), channel_id=1, source_target_pairs={{0,8},{1,9},{2,10},{3,11},{4,5},{5,4},{6,7},{7,6},{8,0},{9,1},{10,... | collective-permute-start | bytes 110600 | tf_op jit(solution)/shard_map/ppermute | solution.py:50
  20.6 1.3 %collective-permute-start.13 = (bf16[16,1152]{1,0:T(8,128)(2,1)S(1)}, bf16[16,1152]{1,0:T(8,128)(2,1)S(1)}, u32[]{:S(2)}, u32[]{:S(2)}) collective-permute-start(bf16[16,1152]{1,0:T(8,128)(2,1)S(1)} %get-tuple-element.25), channel_id=1, source_target_pairs={{0,4},{4,0},{8,12},{12,8},{16,20},{20,16},{24,28},{28,24},{1,5},{5... | collective-permute-start | bytes 110600 | tf_op jit(solution)/shard_map/ppermute | solution.py:37

commit v22 on v20

--- a/solution.py
+++ b/solution.py
@@ -91,7 +91,10 @@
     n_img = lax.axis_size("img")
     row = lax.broadcasted_iota(jnp.int32, (count, 1), 0)
     block, core, j = row // (2 * rows), row // rows % 2, row % rows
-    chip = jnp.where(block == 0, 0, count // (2 * rows) - block)
+    blocks = count // (2 * rows)
+    chip = jnp.where(block == 0, 0, blocks - block)
+    if blocks > 2:
+        chip = jnp.where(block == 1, blocks - 2, jnp.where(block == 2, blocks - 1, chip))
     txt_ids = (me_txt * n_img + (((me_img // 2) ^ chip) * 2 + core)) * rows + j
     source = (me_txt ^ chip) * rows + j
     here = lax.broadcasted_iota(jnp.int32, (count, ids.shape[1]), 1) == source
@@ -181,6 +184,7 @@
     near = jnp.concatenate([text_embeds, image_embeds])
     mine, other = call(sides_kernel, [pair] * 2, [near, far_txt, far_img])
     order = list(range(blocks - 1, 0, -1))
+    order[:2] = order[1::-1]
     mine = [mine] + [chip_swap(mine, k) for k in order]
     other = [other, *[core_swap(block) for block in mine[1:-1]], chip_swap(mine[0], 1, lambda txt: 1)]
     split = blocks - 1
@@ -191,6 +195,7 @@
     )
     far = order.pop(split - 1)
     got = [chip_swap(block, k) for k, block in zip(order, send)]
+    got[:2] = got[1::-1]
     first = chip_swap(first, far, lambda txt: int(txt % 2 == 0 or far % 2 == 1))
     second = chip_swap(second, far, lambda txt: int(txt % 2 == 1 and far % 2 == 0))
     keep, send = call(sum_kernel, [single, piece], [own, *got])

time: 22.5 us -> 22.6 us (level)
  starting transfers between devices: 12.7 us -> 13 us
  waiting for transfers between devices: 6.6 us -> 6.37 us
    ppermute x8, waiting for transfers between devices: 4.71 us -> 3.85 us  [chip_swap(): return lax.ppermute(block, ('img', 'txt'), pairs)]
    ppermute x6, waiting for transfers between devices: 1.89 us -> 2.51 us  [core_swap(): return lax.ppermute(block, 'img', [(i, i ^ 1) for i in range(size)])]
  transfers between devices with their start and end apart: 14 -> 14, of which waited for: 9 -> 8; matrix products, arithmetic and copies ran while one was open for 3% -> 3% of each run, Pallas kernels for 1% -> 1%
where the time goes in v22:
time: 22.6 us; the launch traced here: 22.4 us
  starting transfers between devices  13 us (58%)
  waiting for transfers between devices  6.37 us (28%)
  Pallas kernels  1.58 us (7%)
  local copies, waits for them, and re-layouts  0.79 us (3%)
  between operations  0.69 us (3%)
    ppermute x8, starting transfers between devices, chip_swap(): return lax.ppermute(block, ('img', 'txt'), pairs)  10.9 us
    ppermute x8, waiting for transfers between devices, chip_swap(): return lax.ppermute(block, ('img', 'txt'), pairs)  3.85 us
    ppermute x6, waiting for transfers between devices, core_swap(): return lax.ppermute(block, 'img', [(i, i ^ 1) for i in range(size)])  2.51 us
    ppermute x6, starting transfers between devices, core_swap(): return lax.ppermute(block, 'img', [(i, i ^ 1) for i in range(size)])  2.08 us
    pallas_call x5, Pallas kernels, call(): pl.pallas_call(kernel, out_shape=outs, in_specs=[VMEM] * len(args), out_s...  1.58 us
    unnamed x5, local copies, waits for them, and re-layouts  0.78 us
  transfers between devices with their start and end apart: 14, of which 8 were waited for; matrix products, arithmetic and copies ran while one was open for 3% of the time, Pallas kernels for 1%

profile of v22, /device:TPU:0, one launch (start us, length us, event | category | flops | bytes accessed | tf_op | source)
XLA Modules:
  0.0 22.4 jit_solution(18311120390885173681)
XLA Ops:
  0.6 0.5 %collective-permute-start.2 = (bf16[16,1152]{1,0:T(8,128)(2,1)}, bf16[16,1152]{1,0:T(8,128)(2,1)S(1)}, u32[]{:S(2)}, u32[]{:S(2)}) collective-permute-start(bf16[16,1152]{1,0:T(8,128)(2,1)} %param.3), channel_id=1, source_target_pairs={{0,4},{4,0},{8,12},{12,8},{16,20},{20,16},{24,28},{28,24},{1,5},{5... | collective-permute-start | bytes 110600 | tf_op jit(solution)/shard_map/ppermute | solution.py:37
  1.2 0.8 %constant_dynamic-update-slice_fusion.1 = bf16[32,1152]{1,0:T(8,128)(2,1)S(1)} fusion(bf16[16,1152]{1,0:T(8,128)(2,1)} %param.4), kind=kLoop, calls=%fused_computation.1 | loop fusion | bytes 73728
  2.0 0.2 collective-permute-done.2.img_ref
  2.2 0.3 %collective-permute-done.1.txt_ref = bf16[16,1152]{1,0:T(8,128)(2,1)S(1)} collective-permute-done((bf16[16,1152]{1,0:T(8,128)(2,1)}, bf16[16,1152]{1,0:T(8,128)(2,1)S(1)}, u32[]{:S(2)}, u32[]{:S(2)}) %collective-permute-start.1) | collective-permute-done | bytes 36896 | tf_op jit(solution)/shard_map/ppermute | solution.py:37
  2.6 0.1 shard_map.50
  2.7 3.7 %collective-permute-start.4 = (bf16[32,1152]{1,0:T(8,128)(2,1)S(1)}, bf16[32,1152]{1,0:T(8,128)(2,1)S(1)}, u32[]{:S(2)}, u32[]{:S(2)}) collective-permute-start(bf16[32,1152]{1,0:T(8,128)(2,1)S(1)} %get-tuple-element.14.refs_0_), channel_id=1, source_target_pairs={{0,24},{1,25},{2,26},{3,27},{4,7},{5,6},{6,5},{7,4},{8,16},{9,17},... | collective-permute-start | bytes 221192 | tf_op jit(solution)/shard_map/ppermute | solution.py:50
  6.4 0.5 %collective-permute-start.3 = (bf16[32,1152]{1,0:T(8,128)(2,1)S(1)}, bf16[32,1152]{1,0:T(8,128)(2,1)S(1)}, u32[]{:S(2)}, u32[]{:S(2)}) collective-permute-start(bf16[32,1152]{1,0:T(8,128)(2,1)S(1)} %get-tuple-element.14.refs_0_), channel_id=1, source_target_pairs={{0,16},{1,17},{2,18},{3,19},{4,6},{5,7},{6,4},{7,5},{8,24},{9,25},... | collective-permute-start | bytes 221192 | tf_op jit(solution)/shard_map/ppermute | solution.py:50
  6.9 1.8 %collective-permute-start.8 = (bf16[32,1152]{1,0:T(8,128)(2,1)S(1)}, bf16[32,1152]{1,0:T(8,128)(2,1)S(1)}, u32[]{:S(2)}, u32[]{:S(2)}) collective-permute-start(bf16[32,1152]{1,0:T(8,128)(2,1)S(1)} %get-tuple-element.14.refs_0_), channel_id=1, source_target_pairs={{0,12},{1,13},{2,14},{3,15},{4,1},{5,0},{6,3},{7,2},{8,4},{9,5},{1... | collective-permute-start | bytes 221192 | tf_op jit(solution)/shard_map/ppermute | solution.py:50
  8.7 0.5 %collective-permute-start.5 = (bf16[32,1152]{1,0:T(8,128)(2,1)S(1)}, bf16[32,1152]{1,0:T(8,128)(2,1)S(1)}, u32[]{:S(2)}, u32[]{:S(2)}) collective-permute-start(bf16[32,1152]{1,0:T(8,128)(2,1)S(1)} %get-tuple-element.14.refs_0_), channel_id=1, source_target_pairs={{0,8},{1,9},{2,10},{3,11},{4,5},{5,4},{6,7},{7,6},{8,0},{9,1},{10,... | collective-permute-start | bytes 221192 | tf_op jit(solution)/shard_map/ppermute | solution.py:50
  9.3 0.1 collective-permute-start.7
  9.4 1.4 %collective-permute-done.3.refs_1_ = bf16[32,1152]{1,0:T(8,128)(2,1)S(1)} collective-permute-done((bf16[32,1152]{1,0:T(8,128)(2,1)S(1)}, bf16[32,1152]{1,0:T(8,128)(2,1)S(1)}, u32[]{:S(2)}, u32[]{:S(2)}) %collective-permute-start.3) | collective-permute-done | bytes 73760 | tf_op jit(solution)/shard_map/ppermute | solution.py:50
  10.7 1.0 %collective-permute-start.6 = (bf16[32,1152]{1,0:T(8,128)(2,1)S(1)}, bf16[32,1152]{1,0:T(8,128)(2,1)S(1)}, u32[]{:S(2)}, u32[]{:S(2)}) collective-permute-start(bf16[32,1152]{1,0:T(8,128)(2,1)S(1)} %collective-permute-done.3.refs_1_), channel_id=1, source_target_pairs={{0,4},{4,0},{8,12},{12,8},{16,20},{20,16},{24,28},{28,24},{1,5},{5... | collective-permute-start | bytes 221192 | tf_op jit(solution)/shard_map/ppermute | solution.py:37
  11.8 1.1 %collective-permute-done.far_ids_ref = s32[1,64]{1,0:T(1,128)S(1)} collective-permute-done((s32[1,64]{1,0:T(1,128)S(1)}, s32[1,64]{1,0:T(1,128)S(1)}, u32[]{:S(2)}, u32[]{:S(2)}) %collective-permute-start) | collective-permute-done | bytes 288 | tf_op jit(solution)/shard_map/ppermute | solution.py:37
  12.9 0.1 collective-permute-done.5.refs_3_
  13.1 0.5 %shard_map.51 = (f32[32,1152]{1,0:T(8,128)S(1)}, bf16[16,1152]{1,0:T(8,128)(2,1)S(1)}, bf16[16,1152]{1,0:T(8,128)(2,1)S(1)}, bf16[32,1152]{1,0:T(8,128)(2,1)S(1)}, bf16[32,1152]{1,0:T(8,128)(2,1)S(1)}) custom-call(s32[1,64]{1,0:T(1,128)S(1)} %bitcast.2, s32[1,64]{1,0:T(1,128)S(1)} %collective-permute-done.far_ids_ref, ...), custom_call_target="tpu_custom_call" | custom-call | tf_op jit(solution)/shard_map/pallas_call | solution.py:63
  13.6 2.3 %collective-permute-start.10 = (bf16[32,1152]{1,0:T(8,128)(2,1)S(1)}, bf16[32,1152]{1,0:T(8,128)(2,1)S(1)}, u32[]{:S(2)}, u32[]{:S(2)}) collective-permute-start(bf16[32,1152]{1,0:T(8,128)(2,1)S(1)} %get-tuple-element.21), channel_id=1, source_target_pairs={{0,24},{1,25},{2,26},{3,27},{4,7},{5,6},{6,5},{7,4},{8,16},{9,17},... | collective-permute-start | bytes 221192 | tf_op jit(solution)/shard_map/ppermute | solution.py:50
  15.9 0.5 %collective-permute-start.11 = (bf16[32,1152]{1,0:T(8,128)(2,1)S(1)}, bf16[32,1152]{1,0:T(8,128)(2,1)S(1)}, u32[]{:S(2)}, u32[]{:S(2)}) collective-permute-start(bf16[32,1152]{1,0:T(8,128)(2,1)S(1)} %get-tuple-element.22), channel_id=1, source_target_pairs={{0,16},{1,17},{2,18},{3,19},{4,6},{5,7},{6,4},{7,5},{8,24},{9,25},... | collective-permute-start | bytes 221192 | tf_op jit(solution)/shard_map/ppermute | solution.py:50
  16.4 0.2 %collective-permute-start.9 = (bf16[16,1152]{1,0:T(8,128)(2,1)S(1)}, bf16[16,1152]{1,0:T(8,128)(2,1)S(1)}, u32[]{:S(2)}, u32[]{:S(2)}) collective-permute-start(bf16[16,1152]{1,0:T(8,128)(2,1)S(1)} %get-tuple-element.16), channel_id=1, source_target_pairs={{0,12},{1,13},{2,14},{3,15},{4,1},{5,0},{6,3},{7,2},{8,4},{9,5},{1... | collective-permute-start | bytes 110600 | tf_op jit(solution)/shard_map/ppermute | solution.py:50
  16.7 1.3 %collective-permute-start.12 = (bf16[16,1152]{1,0:T(8,128)(2,1)S(1)}, bf16[16,1152]{1,0:T(8,128)(2,1)S(1)}, u32[]{:S(2)}, u32[]{:S(2)}) collective-permute-start(bf16[16,1152]{1,0:T(8,128)(2,1)S(1)} %get-tuple-element.24), channel_id=1, source_target_pairs={{0,8},{1,9},{2,10},{3,11},{4,5},{5,4},{6,7},{7,6},{8,0},{9,1},{10,... | collective-permute-start | bytes 110600 | tf_op jit(solution)/shard_map/ppermute | solution.py:50
  18.0 1.0 %collective-permute-done.10.refs_0_ = bf16[32,1152]{1,0:T(8,128)(2,1)S(1)} collective-permute-done((bf16[32,1152]{1,0:T(8,128)(2,1)S(1)}, bf16[32,1152]{1,0:T(8,128)(2,1)S(1)}, u32[]{:S(2)}, u32[]{:S(2)}) %collective-permute-start.10) | collective-permute-done | bytes 73760 | tf_op jit(solution)/shard_map/ppermute | solution.py:50
  18.9 1.4 %collective-permute-done.11.refs_1_ = bf16[32,1152]{1,0:T(8,128)(2,1)S(1)} collective-permute-done((bf16[32,1152]{1,0:T(8,128)(2,1)S(1)}, bf16[32,1152]{1,0:T(8,128)(2,1)S(1)}, u32[]{:S(2)}, u32[]{:S(2)}) %collective-permute-start.11) | collective-permute-done | bytes 73760 | tf_op jit(solution)/shard_map/ppermute | solution.py:50
  20.3 0.3 %collective-permute-start.13 = (bf16[16,1152]{1,0:T(8,128)(2,1)S(1)}, bf16[16,1152]{1,0:T(8,128)(2,1)S(1)}, u32[]{:S(2)}, u32[]{:S(2)}) collective-permute-start(bf16[16,1152]{1,0:T(8,128)(2,1)S(1)} %get-tuple-element.25), channel_id=1, source_target_pairs={{0,4},{4,0},{8,12},{12,8},{16,20},{20,16},{24,28},{28,24},{1,5},{5... | collective-permute-start | bytes 110600 | tf_op jit(solution)/shard_map/ppermute | solution.py:37
  20.8 0.8 %collective-permute-done.13.got_ref = bf16[16,1152]{1,0:T(8,128)(2,1)S(1)} collective-permute-done((bf16[16,1152]{1,0:T(8,128)(2,1)S(1)}, bf16[16,1152]{1,0:T(8,128)(2,1)S(1)}, u32[]{:S(2)}, u32[]{:S(2)}) %collective-permute-start.13) | collective-permute-done | bytes 36896 | tf_op jit(solution)/shard_map/ppermute | solution.py:37
  21.6 0.8 %shard_map.54 = (f32[16,1152]{1,0:T(8,128)}, f32[16,1152]{1,0:T(8,128)}) custom-call(f32[32,1152]{1,0:T(8,128)S(1)} %get-tuple-element.17.unit_ref, f32[32,1]{1,0:T(8,128)S(1)} %get-tuple-element.18.inverse_ref, f32[16,1152]{1,0:T(8,128)S(1)} %get-tuple-element.19.first_ref, f32[16,1152]{1,0:T(8,128)S(1)} %get-tuple-element.23.keep_ref, ...), custom_call_target="tpu_custom_call" | custom-call | tf_op jit(solution)/shard_map/pallas_call | solution.py:63
  (15 shorter events, 0.3 us)
Async XLA Ops:
  0.6 1.4 %copy-start.1 = (bf16[16,1152]{1,0:T(8,128)(2,1)S(1)}, bf16[16,1152]{1,0:T(8,128)(2,1)}, u32[]{:S(2)}) copy-start(bf16[16,1152]{1,0:T(8,128)(2,1)} %param.3) | copy-start | bytes 110596
  0.6 1.6 %collective-permute-start.2 = (bf16[16,1152]{1,0:T(8,128)(2,1)}, bf16[16,1152]{1,0:T(8,128)(2,1)S(1)}, u32[]{:S(2)}, u32[]{:S(2)}) collective-permute-start(bf16[16,1152]{1,0:T(8,128)(2,1)} %param.3), channel_id=1, source_target_pairs={{0,4},{4,0},{8,12},{12,8},{16,20},{20,16},{24,28},{28,24},{1,5},{5... | collective-permute-start | bytes 110600 | tf_op jit(solution)/shard_map/ppermute | solution.py:37
  1.2 1.4 %collective-permute-start.1 = (bf16[16,1152]{1,0:T(8,128)(2,1)}, bf16[16,1152]{1,0:T(8,128)(2,1)S(1)}, u32[]{:S(2)}, u32[]{:S(2)}) collective-permute-start(bf16[16,1152]{1,0:T(8,128)(2,1)} %param.4), channel_id=1, source_target_pairs={{0,4},{4,0},{8,12},{12,8},{16,20},{20,16},{24,28},{28,24},{1,5},{5... | collective-permute-start | bytes 110600 | tf_op jit(solution)/shard_map/ppermute | solution.py:37
  2.7 9.1 %copy-start = (s32[64]{0:T(128)S(1)}, s32[64]{0:T(128)}, u32[]{:S(2)}) copy-start(s32[64]{0:T(128)} %param.5) | copy-start | bytes 772
  2.7 6.5 %collective-permute-start.4 = (bf16[32,1152]{1,0:T(8,128)(2,1)S(1)}, bf16[32,1152]{1,0:T(8,128)(2,1)S(1)}, u32[]{:S(2)}, u32[]{:S(2)}) collective-permute-start(bf16[32,1152]{1,0:T(8,128)(2,1)S(1)} %get-tuple-element.14.refs_0_), channel_id=1, source_target_pairs={{0,24},{1,25},{2,26},{3,27},{4,7},{5,6},{6,5},{7,4},{8,16},{9,17},... | collective-permute-start | bytes 221192 | tf_op jit(solution)/shard_map/ppermute | solution.py:50
  6.4 4.4 %collective-permute-start.3 = (bf16[32,1152]{1,0:T(8,128)(2,1)S(1)}, bf16[32,1152]{1,0:T(8,128)(2,1)S(1)}, u32[]{:S(2)}, u32[]{:S(2)}) collective-permute-start(bf16[32,1152]{1,0:T(8,128)(2,1)S(1)} %get-tuple-element.14.refs_0_), channel_id=1, source_target_pairs={{0,16},{1,17},{2,18},{3,19},{4,6},{5,7},{6,4},{7,5},{8,24},{9,25},... | collective-permute-start | bytes 221192 | tf_op jit(solution)/shard_map/ppermute | solution.py:50
  6.9 6.0 %collective-permute-start.8 = (bf16[32,1152]{1,0:T(8,128)(2,1)S(1)}, bf16[32,1152]{1,0:T(8,128)(2,1)S(1)}, u32[]{:S(2)}, u32[]{:S(2)}) collective-permute-start(bf16[32,1152]{1,0:T(8,128)(2,1)S(1)} %get-tuple-element.14.refs_0_), channel_id=1, source_target_pairs={{0,12},{1,13},{2,14},{3,15},{4,1},{5,0},{6,3},{7,2},{8,4},{9,5},{1... | collective-permute-start | bytes 221192 | tf_op jit(solution)/shard_map/ppermute | solution.py:50
  8.7 4.4 %collective-permute-start.5 = (bf16[32,1152]{1,0:T(8,128)(2,1)S(1)}, bf16[32,1152]{1,0:T(8,128)(2,1)S(1)}, u32[]{:S(2)}, u32[]{:S(2)}) collective-permute-start(bf16[32,1152]{1,0:T(8,128)(2,1)S(1)} %get-tuple-element.14.refs_0_), channel_id=1, source_target_pairs={{0,8},{1,9},{2,10},{3,11},{4,5},{5,4},{6,7},{7,6},{8,0},{9,1},{10,... | collective-permute-start | bytes 221192 | tf_op jit(solution)/shard_map/ppermute | solution.py:50
  9.3 3.8 %collective-permute-start.7 = (bf16[32,1152]{1,0:T(8,128)(2,1)S(1)}, bf16[32,1152]{1,0:T(8,128)(2,1)S(1)}, u32[]{:S(2)}, u32[]{:S(2)}) collective-permute-start(bf16[32,1152]{1,0:T(8,128)(2,1)S(1)} %collective-permute-done.4.refs_2_), channel_id=1, source_target_pairs={{0,4},{4,0},{8,12},{12,8},{16,20},{20,16},{24,28},{28,24},{1,5},{5... | collective-permute-start | bytes 221192 | tf_op jit(solution)/shard_map/ppermute | solution.py:37
  10.7 2.3 %collective-permute-start.6 = (bf16[32,1152]{1,0:T(8,128)(2,1)S(1)}, bf16[32,1152]{1,0:T(8,128)(2,1)S(1)}, u32[]{:S(2)}, u32[]{:S(2)}) collective-permute-start(bf16[32,1152]{1,0:T(8,128)(2,1)S(1)} %collective-permute-done.3.refs_1_), channel_id=1, source_target_pairs={{0,4},{4,0},{8,12},{12,8},{16,20},{20,16},{24,28},{28,24},{1,5},{5... | collective-permute-start | bytes 221192 | tf_op jit(solution)/shard_map/ppermute | solution.py:37
  11.8 1.1 %collective-permute-start = (s32[1,64]{1,0:T(1,128)S(1)}, s32[1,64]{1,0:T(1,128)S(1)}, u32[]{:S(2)}, u32[]{:S(2)}) collective-permute-start(s32[1,64]{1,0:T(1,128)S(1)} %bitcast.1), channel_id=1, source_target_pairs={{0,4},{4,0},{8,12},{12,8},{16,20},{20,16},{24,28},{28,24},{1,5},{5... | collective-permute-start | bytes 776 | tf_op jit(solution)/shard_map/ppermute | solution.py:37
  13.6 5.3 %collective-permute-start.10 = (bf16[32,1152]{1,0:T(8,128)(2,1)S(1)}, bf16[32,1152]{1,0:T(8,128)(2,1)S(1)}, u32[]{:S(2)}, u32[]{:S(2)}) collective-permute-start(bf16[32,1152]{1,0:T(8,128)(2,1)S(1)} %get-tuple-element.21), channel_id=1, source_target_pairs={{0,24},{1,25},{2,26},{3,27},{4,7},{5,6},{6,5},{7,4},{8,16},{9,17},... | collective-permute-start | bytes 221192 | tf_op jit(solution)/shard_map/ppermute | solution.py:50
  15.9 4.4 %collective-permute-start.11 = (bf16[32,1152]{1,0:T(8,128)(2,1)S(1)}, bf16[32,1152]{1,0:T(8,128)(2,1)S(1)}, u32[]{:S(2)}, u32[]{:S(2)}) collective-permute-start(bf16[32,1152]{1,0:T(8,128)(2,1)S(1)} %get-tuple-element.22), channel_id=1, source_target_pairs={{0,16},{1,17},{2,18},{3,19},{4,6},{5,7},{6,4},{7,5},{8,24},{9,25},... | collective-permute-start | bytes 221192 | tf_op jit(solution)/shard_map/ppermute | solution.py:50
  16.4 4.2 %collective-permute-start.9 = (bf16[16,1152]{1,0:T(8,128)(2,1)S(1)}, bf16[16,1152]{1,0:T(8,128)(2,1)S(1)}, u32[]{:S(2)}, u32[]{:S(2)}) collective-permute-start(bf16[16,1152]{1,0:T(8,128)(2,1)S(1)} %get-tuple-element.16), channel_id=1, source_target_pairs={{0,12},{1,13},{2,14},{3,15},{4,1},{5,0},{6,3},{7,2},{8,4},{9,5},{1... | collective-permute-start | bytes 110600 | tf_op jit(solution)/shard_map/ppermute | solution.py:50
  16.7 4.1 %collective-permute-start.12 = (bf16[16,1152]{1,0:T(8,128)(2,1)S(1)}, bf16[16,1152]{1,0:T(8,128)(2,1)S(1)}, u32[]{:S(2)}, u32[]{:S(2)}) collective-permute-start(bf16[16,1152]{1,0:T(8,128)(2,1)S(1)} %get-tuple-element.24), channel_id=1, source_target_pairs={{0,8},{1,9},{2,10},{3,11},{4,5},{5,4},{6,7},{7,6},{8,0},{9,1},{10,... | collective-permute-start | bytes 110600 | tf_op jit(solution)/shard_map/ppermute | solution.py:50
  20.3 1.3 %collective-permute-start.13 = (bf16[16,1152]{1,0:T(8,128)(2,1)S(1)}, bf16[16,1152]{1,0:T(8,128)(2,1)S(1)}, u32[]{:S(2)}, u32[]{:S(2)}) collective-permute-start(bf16[16,1152]{1,0:T(8,128)(2,1)S(1)} %get-tuple-element.25), channel_id=1, source_target_pairs={{0,4},{4,0},{8,12},{12,8},{16,20},{20,16},{24,28},{28,24},{1,5},{5... | collective-permute-start | bytes 110600 | tf_op jit(solution)/shard_map/ppermute | solution.py:37

commit v23 on v21

--- a/solution.py
+++ b/solution.py
@@ -37,17 +37,23 @@
     return lax.ppermute(block, "img", [(i, i ^ 1) for i in range(size)])
 
 
-def chip_swap(block, distance, cross=lambda txt: 0):
+def chip_swap(block, distances, cross=lambda txt: 0):
     n_img, n_txt = lax.axis_size("img"), lax.axis_size("txt")
+    along_img, along_txt = distances
     pairs = []
     for img in range(n_img):
         for txt in range(n_txt):
             other = cross(txt)
-            if img % 2 == 0 and distance < n_img // 2:
-                pairs.append((img * n_txt + txt, (img ^ (2 * distance) ^ other) * n_txt + txt))
-            if img % 2 == 1 and distance < n_txt:
-                pairs.append((img * n_txt + txt, (img ^ other) * n_txt + (txt ^ distance)))
+            if img % 2 == 0 and along_img < n_img // 2:
+                pairs.append((img * n_txt + txt, (img ^ (2 * along_img) ^ other) * n_txt + txt))
+            if img % 2 == 1 and along_txt < n_txt:
+                pairs.append((img * n_txt + txt, (img ^ other) * n_txt + (txt ^ along_txt)))
     return lax.ppermute(block, ("img", "txt"), pairs)
+
+
+def orders(blocks):
+    falling = list(range(blocks - 1, 0, -1))
+    return falling, falling[1::-1] + falling[2:]
 
 
 def cross_first(distance):
@@ -91,9 +97,14 @@
     n_img = lax.axis_size("img")
     row = lax.broadcasted_iota(jnp.int32, (count, 1), 0)
     block, core, j = row // (2 * rows), row // rows % 2, row % rows
-    chip = jnp.where(block == 0, 0, count // (2 * rows) - block)
-    txt_ids = (me_txt * n_img + (((me_img // 2) ^ chip) * 2 + core)) * rows + j
-    source = (me_txt ^ chip) * rows + j
+    chips = []
+    for order in orders(count // (2 * rows)):
+        chip = jnp.zeros_like(block)
+        for k, distance in enumerate(order):
+            chip = jnp.where(block == k + 1, distance, chip)
+        chips.append(chip)
+    txt_ids = (me_txt * n_img + (((me_img // 2) ^ chips[0]) * 2 + core)) * rows + j
+    source = (me_txt ^ chips[1]) * rows + j
     here = lax.broadcasted_iota(jnp.int32, (count, ids.shape[1]), 1) == source
     per_core = jnp.where(core == me_img % 2, ids, far_ids)
     img_ids = jnp.sum(jnp.where(here, per_core, 0), axis=1, keepdims=True)
@@ -117,7 +128,7 @@
     return lax.dot_general(mine, other, (((1,), (1,)), ((), ())), preferred_element_type=f32)
 
 
-def pair_kernel(blocks, split, ids_ref, far_ids_ref, *refs):
+def pair_kernel(blocks, plan, ids_ref, far_ids_ref, *refs):
     mine_refs, other_refs = refs[:blocks], refs[blocks:2 * blocks]
     own_ref, first_ref, second_ref, *send_refs = refs[2 * blocks:]
     height = own_ref.shape[0]
@@ -128,12 +139,21 @@
     other = jnp.concatenate([ref[...] for ref in other_refs], axis=0)
     part = jnp.dot(coeff, other, preferred_element_type=f32)
     own_ref[...] = part[:height]
-    whole = [k for k in range(1, blocks) if k != split]
-    for k, ref in zip(whole, send_refs):
-        ref[...] = part[k * height:(k + 1) * height].astype(bf16)
-    block = part[split * height:(split + 1) * height].astype(bf16)
-    even = is_even()
-    first = jnp.logical_xor(even, cross_first(blocks - split))
+    even = is_even()
+    txt_order, img_order = orders(blocks)
+
+    def block_of(distance):
+        txt, img = [
+            part[(order.index(distance) + 1) * height:(order.index(distance) + 2) * height]
+            for order in (txt_order, img_order)
+        ]
+        return jnp.where(even, txt, img).astype(bf16)
+
+    *whole, split = plan
+    for distance, ref in zip(whole, send_refs):
+        ref[...] = block_of(distance)
+    block = block_of(split)
+    first = jnp.logical_xor(even, cross_first(split))
     first_ref[...] = jnp.where(first, block[:rows], block[rows:])
     second_ref[...] = jnp.where(first, block[rows:], block[:rows])
 
@@ -180,19 +200,18 @@
     far_img = core_swap(image_embeds)
     near = jnp.concatenate([text_embeds, image_embeds])
     mine, other = call(sides_kernel, [pair] * 2, [near, far_txt, far_img])
-    order = list(range(blocks - 1, 0, -1))
-    mine = [mine] + [chip_swap(mine, k) for k in order]
-    other = [other, *[core_swap(block) for block in mine[1:-1]], chip_swap(mine[0], 1, lambda txt: 1)]
-    split = blocks - 1
+    mine = [mine] + [chip_swap(mine, distances) for distances in zip(*orders(blocks))]
+    other = [other, *[core_swap(block) for block in mine[1:-1]], chip_swap(mine[0], (1, 1), lambda txt: 1)]
+    plan = list(range(blocks - 1, 0, -1))
+    far = plan[-1]
     own, first, second, *send = call(
-        functools.partial(pair_kernel, blocks, split),
+        functools.partial(pair_kernel, blocks, plan),
         [total] + [piece] * 2 + [pair] * (blocks - 2),
         [ids, core_swap(ids), *mine, *other],
     )
-    far = order.pop(split - 1)
-    got = [chip_swap(block, k) for k, block in zip(order, send)][::-1]
-    first = chip_swap(first, far, lambda txt: int(txt % 2 == 0 or far % 2 == 1))
-    second = chip_swap(second, far, lambda txt: int(txt % 2 == 1 and far % 2 == 0))
+    got = [chip_swap(block, (k, k)) for k, block in zip(plan, send)]
+    first = chip_swap(first, (far, far), lambda txt: int(txt % 2 == 0 or far % 2 == 1))
+    second = chip_swap(second, (far, far), lambda txt: int(txt % 2 == 1 and far % 2 == 0))
     keep, send = call(sum_kernel, [single, piece], [own, *got])
     got = core_swap(send)
     column = jax.ShapeDtypeStruct((2 * rows, 1), f32)

time: 22.8 us -> 22.6 us (level)
  waiting for transfers between devices: 7.01 us -> 6.42 us
  starting transfers between devices: 12.6 us -> 12.9 us
    ppermute x6, starting transfers between devices: 1.63 us -> 2.07 us  [core_swap(): return lax.ppermute(block, 'img', [(i, i ^ 1) for i in range(size)])]
    ppermute x8, waiting for transfers between devices: 4.92 us -> 4.5 us  [chip_swap(): return lax.ppermute(block, ('img', 'txt'), pairs)]
where the time goes in v23:
time: 22.6 us; the launch traced here: 22.4 us
  starting transfers between devices  12.9 us (57%)
  waiting for transfers between devices  6.42 us (28%)
  Pallas kernels  1.58 us (7%)
  local copies, waits for them, and re-layouts  0.79 us (3%)
  between operations  0.68 us (3%)
    ppermute x8, starting transfers between devices, chip_swap(): return lax.ppermute(block, ('img', 'txt'), pairs)  10.8 us
    ppermute x8, waiting for transfers between devices, chip_swap(): return lax.ppermute(block, ('img', 'txt'), pairs)  4.5 us
    ppermute x6, starting transfers between devices, core_swap(): return lax.ppermute(block, 'img', [(i, i ^ 1) for i in range(size)])  2.07 us
    ppermute x6, waiting for transfers between devices, core_swap(): return lax.ppermute(block, 'img', [(i, i ^ 1) for i in range(size)])  1.92 us
    pallas_call x5, Pallas kernels, call(): pl.pallas_call(kernel, out_shape=outs, in_specs=[VMEM] * len(args), out_s...  1.58 us
    unnamed x5, local copies, waits for them, and re-layouts  0.78 us
  transfers between devices with their start and end apart: 14, of which 9 were waited for; matrix products, arithmetic and copies ran while one was open for 3% of the time, Pallas kernels for 1%

profile of v23, /device:TPU:0, one launch (start us, length us, event | category | flops | bytes accessed | tf_op | source)
XLA Modules:
  0.0 22.4 jit_solution(5150162505729902663)
XLA Ops:
  0.6 0.5 %collective-permute-start.2 = (bf16[16,1152]{1,0:T(8,128)(2,1)}, bf16[16,1152]{1,0:T(8,128)(2,1)S(1)}, u32[]{:S(2)}, u32[]{:S(2)}) collective-permute-start(bf16[16,1152]{1,0:T(8,128)(2,1)} %param.3), channel_id=1, source_target_pairs={{0,4},{4,0},{8,12},{12,8},{16,20},{20,16},{24,28},{28,24},{1,5},{5... | collective-permute-start | bytes 110600 | tf_op jit(solution)/shard_map/ppermute | solution.py:37
  1.2 0.8 %constant_dynamic-update-slice_fusion.1 = bf16[32,1152]{1,0:T(8,128)(2,1)S(1)} fusion(bf16[16,1152]{1,0:T(8,128)(2,1)} %param.4), kind=kLoop, calls=%fused_computation.1 | loop fusion | bytes 73728
  2.0 0.2 collective-permute-done.2.img_ref
  2.2 0.3 %collective-permute-done.1.txt_ref = bf16[16,1152]{1,0:T(8,128)(2,1)S(1)} collective-permute-done((bf16[16,1152]{1,0:T(8,128)(2,1)}, bf16[16,1152]{1,0:T(8,128)(2,1)S(1)}, u32[]{:S(2)}, u32[]{:S(2)}) %collective-permute-start.1) | collective-permute-done | bytes 36896 | tf_op jit(solution)/shard_map/ppermute | solution.py:37
  2.6 0.1 shard_map.50
  2.7 2.7 %collective-permute-start.4 = (bf16[32,1152]{1,0:T(8,128)(2,1)S(1)}, bf16[32,1152]{1,0:T(8,128)(2,1)S(1)}, u32[]{:S(2)}, u32[]{:S(2)}) collective-permute-start(bf16[32,1152]{1,0:T(8,128)(2,1)S(1)} %get-tuple-element.14.refs_0_), channel_id=1, source_target_pairs={{0,16},{1,17},{2,18},{3,19},{4,7},{5,6},{6,5},{7,4},{8,24},{9,25},... | collective-permute-start | bytes 221192 | tf_op jit(solution)/shard_map/ppermute | solution.py:51
  5.5 1.4 %collective-permute-start.3 = (bf16[32,1152]{1,0:T(8,128)(2,1)S(1)}, bf16[32,1152]{1,0:T(8,128)(2,1)S(1)}, u32[]{:S(2)}, u32[]{:S(2)}) collective-permute-start(bf16[32,1152]{1,0:T(8,128)(2,1)S(1)} %get-tuple-element.14.refs_0_), channel_id=1, source_target_pairs={{0,24},{1,25},{2,26},{3,27},{4,6},{5,7},{6,4},{7,5},{8,16},{9,17},... | collective-permute-start | bytes 221192 | tf_op jit(solution)/shard_map/ppermute | solution.py:51
  6.9 1.8 %collective-permute-start.8 = (bf16[32,1152]{1,0:T(8,128)(2,1)S(1)}, bf16[32,1152]{1,0:T(8,128)(2,1)S(1)}, u32[]{:S(2)}, u32[]{:S(2)}) collective-permute-start(bf16[32,1152]{1,0:T(8,128)(2,1)S(1)} %get-tuple-element.14.refs_0_), channel_id=1, source_target_pairs={{0,12},{1,13},{2,14},{3,15},{4,1},{5,0},{6,3},{7,2},{8,4},{9,5},{1... | collective-permute-start | bytes 221192 | tf_op jit(solution)/shard_map/ppermute | solution.py:51
  8.7 0.5 %collective-permute-start.5 = (bf16[32,1152]{1,0:T(8,128)(2,1)S(1)}, bf16[32,1152]{1,0:T(8,128)(2,1)S(1)}, u32[]{:S(2)}, u32[]{:S(2)}) collective-permute-start(bf16[32,1152]{1,0:T(8,128)(2,1)S(1)} %get-tuple-element.14.refs_0_), channel_id=1, source_target_pairs={{0,8},{1,9},{2,10},{3,11},{4,5},{5,4},{6,7},{7,6},{8,0},{9,1},{10,... | collective-permute-start | bytes 221192 | tf_op jit(solution)/shard_map/ppermute | solution.py:51
  9.4 1.4 %collective-permute-done.3.refs_1_ = bf16[32,1152]{1,0:T(8,128)(2,1)S(1)} collective-permute-done((bf16[32,1152]{1,0:T(8,128)(2,1)S(1)}, bf16[32,1152]{1,0:T(8,128)(2,1)S(1)}, u32[]{:S(2)}, u32[]{:S(2)}) %collective-permute-start.3) | collective-permute-done | bytes 73760 | tf_op jit(solution)/shard_map/ppermute | solution.py:51
  10.7 1.1 %collective-permute-start.6 = (bf16[32,1152]{1,0:T(8,128)(2,1)S(1)}, bf16[32,1152]{1,0:T(8,128)(2,1)S(1)}, u32[]{:S(2)}, u32[]{:S(2)}) collective-permute-start(bf16[32,1152]{1,0:T(8,128)(2,1)S(1)} %collective-permute-done.3.refs_1_), channel_id=1, source_target_pairs={{0,4},{4,0},{8,12},{12,8},{16,20},{20,16},{24,28},{28,24},{1,5},{5... | collective-permute-start | bytes 221192 | tf_op jit(solution)/shard_map/ppermute | solution.py:37
  11.8 1.1 %collective-permute-done.far_ids_ref = s32[1,64]{1,0:T(1,128)S(1)} collective-permute-done((s32[1,64]{1,0:T(1,128)S(1)}, s32[1,64]{1,0:T(1,128)S(1)}, u32[]{:S(2)}, u32[]{:S(2)}) %collective-permute-start) | collective-permute-done | bytes 288 | tf_op jit(solution)/shard_map/ppermute | solution.py:37
  12.9 0.1 collective-permute-done.5.refs_3_
  13.1 0.5 %shard_map.51 = (f32[32,1152]{1,0:T(8,128)S(1)}, bf16[16,1152]{1,0:T(8,128)(2,1)S(1)}, bf16[16,1152]{1,0:T(8,128)(2,1)S(1)}, bf16[32,1152]{1,0:T(8,128)(2,1)S(1)}, bf16[32,1152]{1,0:T(8,128)(2,1)S(1)}) custom-call(s32[1,64]{1,0:T(1,128)S(1)} %bitcast.2, s32[1,64]{1,0:T(1,128)S(1)} %collective-permute-done.far_ids_ref, ...), custom_call_target="tpu_custom_call" | custom-call | tf_op jit(solution)/shard_map/pallas_call | solution.py:69
  13.6 2.3 %collective-permute-start.10 = (bf16[32,1152]{1,0:T(8,128)(2,1)S(1)}, bf16[32,1152]{1,0:T(8,128)(2,1)S(1)}, u32[]{:S(2)}, u32[]{:S(2)}) collective-permute-start(bf16[32,1152]{1,0:T(8,128)(2,1)S(1)} %get-tuple-element.21), channel_id=1, source_target_pairs={{0,24},{1,25},{2,26},{3,27},{4,7},{5,6},{6,5},{7,4},{8,16},{9,17},... | collective-permute-start | bytes 221192 | tf_op jit(solution)/shard_map/ppermute | solution.py:51
  15.9 0.5 %collective-permute-start.11 = (bf16[32,1152]{1,0:T(8,128)(2,1)S(1)}, bf16[32,1152]{1,0:T(8,128)(2,1)S(1)}, u32[]{:S(2)}, u32[]{:S(2)}) collective-permute-start(bf16[32,1152]{1,0:T(8,128)(2,1)S(1)} %get-tuple-element.22), channel_id=1, source_target_pairs={{0,16},{1,17},{2,18},{3,19},{4,6},{5,7},{6,4},{7,5},{8,24},{9,25},... | collective-permute-start | bytes 221192 | tf_op jit(solution)/shard_map/ppermute | solution.py:51
  16.4 1.0 %collective-permute-start.9 = (bf16[16,1152]{1,0:T(8,128)(2,1)S(1)}, bf16[16,1152]{1,0:T(8,128)(2,1)S(1)}, u32[]{:S(2)}, u32[]{:S(2)}) collective-permute-start(bf16[16,1152]{1,0:T(8,128)(2,1)S(1)} %get-tuple-element.16), channel_id=1, source_target_pairs={{0,12},{1,13},{2,14},{3,15},{4,1},{5,0},{6,3},{7,2},{8,4},{9,5},{1... | collective-permute-start | bytes 110600 | tf_op jit(solution)/shard_map/ppermute | solution.py:51
  17.4 0.5 %collective-permute-start.12 = (bf16[16,1152]{1,0:T(8,128)(2,1)S(1)}, bf16[16,1152]{1,0:T(8,128)(2,1)S(1)}, u32[]{:S(2)}, u32[]{:S(2)}) collective-permute-start(bf16[16,1152]{1,0:T(8,128)(2,1)S(1)} %get-tuple-element.24), channel_id=1, source_target_pairs={{0,8},{1,9},{2,10},{3,11},{4,5},{5,4},{6,7},{7,6},{8,0},{9,1},{10,... | collective-permute-start | bytes 110600 | tf_op jit(solution)/shard_map/ppermute | solution.py:51
  17.9 1.0 %collective-permute-done.10.refs_0_ = bf16[32,1152]{1,0:T(8,128)(2,1)S(1)} collective-permute-done((bf16[32,1152]{1,0:T(8,128)(2,1)S(1)}, bf16[32,1152]{1,0:T(8,128)(2,1)S(1)}, u32[]{:S(2)}, u32[]{:S(2)}) %collective-permute-start.10) | collective-permute-done | bytes 73760 | tf_op jit(solution)/shard_map/ppermute | solution.py:51
  18.9 1.4 %collective-permute-done.11.refs_1_ = bf16[32,1152]{1,0:T(8,128)(2,1)S(1)} collective-permute-done((bf16[32,1152]{1,0:T(8,128)(2,1)S(1)}, bf16[32,1152]{1,0:T(8,128)(2,1)S(1)}, u32[]{:S(2)}, u32[]{:S(2)}) %collective-permute-start.11) | collective-permute-done | bytes 73760 | tf_op jit(solution)/shard_map/ppermute | solution.py:51
  20.3 0.3 %collective-permute-start.13 = (bf16[16,1152]{1,0:T(8,128)(2,1)S(1)}, bf16[16,1152]{1,0:T(8,128)(2,1)S(1)}, u32[]{:S(2)}, u32[]{:S(2)}) collective-permute-start(bf16[16,1152]{1,0:T(8,128)(2,1)S(1)} %get-tuple-element.25), channel_id=1, source_target_pairs={{0,4},{4,0},{8,12},{12,8},{16,20},{20,16},{24,28},{28,24},{1,5},{5... | collective-permute-start | bytes 110600 | tf_op jit(solution)/shard_map/ppermute | solution.py:37
  20.7 0.6 %collective-permute-done.12.second_ref = bf16[16,1152]{1,0:T(8,128)(2,1)S(1)} collective-permute-done((bf16[16,1152]{1,0:T(8,128)(2,1)S(1)}, bf16[16,1152]{1,0:T(8,128)(2,1)S(1)}, u32[]{:S(2)}, u32[]{:S(2)}) %collective-permute-start.12) | collective-permute-done | bytes 36896 | tf_op jit(solution)/shard_map/ppermute | solution.py:51
  21.4 0.2 %collective-permute-done.13.got_ref = bf16[16,1152]{1,0:T(8,128)(2,1)S(1)} collective-permute-done((bf16[16,1152]{1,0:T(8,128)(2,1)S(1)}, bf16[16,1152]{1,0:T(8,128)(2,1)S(1)}, u32[]{:S(2)}, u32[]{:S(2)}) %collective-permute-start.13) | collective-permute-done | bytes 36896 | tf_op jit(solution)/shard_map/ppermute | solution.py:37
  21.6 0.8 %shard_map.54 = (f32[16,1152]{1,0:T(8,128)}, f32[16,1152]{1,0:T(8,128)}) custom-call(f32[32,1152]{1,0:T(8,128)S(1)} %get-tuple-element.17.unit_ref, f32[32,1]{1,0:T(8,128)S(1)} %get-tuple-element.18.inverse_ref, f32[16,1152]{1,0:T(8,128)S(1)} %get-tuple-element.19.first_ref, f32[16,1152]{1,0:T(8,128)S(1)} %get-tuple-element.23.keep_ref, ...), custom_call_target="tpu_custom_call" | custom-call | tf_op jit(solution)/shard_map/pallas_call | solution.py:69
  (15 shorter events, 0.4 us)
Async XLA Ops:
  0.6 1.4 %copy-start.1 = (bf16[16,1152]{1,0:T(8,128)(2,1)S(1)}, bf16[16,1152]{1,0:T(8,128)(2,1)}, u32[]{:S(2)}) copy-start(bf16[16,1152]{1,0:T(8,128)(2,1)} %param.3) | copy-start | bytes 110596
  0.6 1.6 %collective-permute-start.2 = (bf16[16,1152]{1,0:T(8,128)(2,1)}, bf16[16,1152]{1,0:T(8,128)(2,1)S(1)}, u32[]{:S(2)}, u32[]{:S(2)}) collective-permute-start(bf16[16,1152]{1,0:T(8,128)(2,1)} %param.3), channel_id=1, source_target_pairs={{0,4},{4,0},{8,12},{12,8},{16,20},{20,16},{24,28},{28,24},{1,5},{5... | collective-permute-start | bytes 110600 | tf_op jit(solution)/shard_map/ppermute | solution.py:37
  1.2 1.4 %collective-permute-start.1 = (bf16[16,1152]{1,0:T(8,128)(2,1)}, bf16[16,1152]{1,0:T(8,128)(2,1)S(1)}, u32[]{:S(2)}, u32[]{:S(2)}) collective-permute-start(bf16[16,1152]{1,0:T(8,128)(2,1)} %param.4), channel_id=1, source_target_pairs={{0,4},{4,0},{8,12},{12,8},{16,20},{20,16},{24,28},{28,24},{1,5},{5... | collective-permute-start | bytes 110600 | tf_op jit(solution)/shard_map/ppermute | solution.py:37
  2.7 9.1 %copy-start = (s32[64]{0:T(128)S(1)}, s32[64]{0:T(128)}, u32[]{:S(2)}) copy-start(s32[64]{0:T(128)} %param.5) | copy-start | bytes 772
  2.7 6.5 %collective-permute-start.4 = (bf16[32,1152]{1,0:T(8,128)(2,1)S(1)}, bf16[32,1152]{1,0:T(8,128)(2,1)S(1)}, u32[]{:S(2)}, u32[]{:S(2)}) collective-permute-start(bf16[32,1152]{1,0:T(8,128)(2,1)S(1)} %get-tuple-element.14.refs_0_), channel_id=1, source_target_pairs={{0,16},{1,17},{2,18},{3,19},{4,7},{5,6},{6,5},{7,4},{8,24},{9,25},... | collective-permute-start | bytes 221192 | tf_op jit(solution)/shard_map/ppermute | solution.py:51
  5.5 5.3 %collective-permute-start.3 = (bf16[32,1152]{1,0:T(8,128)(2,1)S(1)}, bf16[32,1152]{1,0:T(8,128)(2,1)S(1)}, u32[]{:S(2)}, u32[]{:S(2)}) collective-permute-start(bf16[32,1152]{1,0:T(8,128)(2,1)S(1)} %get-tuple-element.14.refs_0_), channel_id=1, source_target_pairs={{0,24},{1,25},{2,26},{3,27},{4,6},{5,7},{6,4},{7,5},{8,16},{9,17},... | collective-permute-start | bytes 221192 | tf_op jit(solution)/shard_map/ppermute | solution.py:51
  6.9 6.0 %collective-permute-start.8 = (bf16[32,1152]{1,0:T(8,128)(2,1)S(1)}, bf16[32,1152]{1,0:T(8,128)(2,1)S(1)}, u32[]{:S(2)}, u32[]{:S(2)}) collective-permute-start(bf16[32,1152]{1,0:T(8,128)(2,1)S(1)} %get-tuple-element.14.refs_0_), channel_id=1, source_target_pairs={{0,12},{1,13},{2,14},{3,15},{4,1},{5,0},{6,3},{7,2},{8,4},{9,5},{1... | collective-permute-start | bytes 221192 | tf_op jit(solution)/shard_map/ppermute | solution.py:51
  8.7 4.4 %collective-permute-start.5 = (bf16[32,1152]{1,0:T(8,128)(2,1)S(1)}, bf16[32,1152]{1,0:T(8,128)(2,1)S(1)}, u32[]{:S(2)}, u32[]{:S(2)}) collective-permute-start(bf16[32,1152]{1,0:T(8,128)(2,1)S(1)} %get-tuple-element.14.refs_0_), channel_id=1, source_target_pairs={{0,8},{1,9},{2,10},{3,11},{4,5},{5,4},{6,7},{7,6},{8,0},{9,1},{10,... | collective-permute-start | bytes 221192 | tf_op jit(solution)/shard_map/ppermute | solution.py:51
  9.3 3.8 %collective-permute-start.7 = (bf16[32,1152]{1,0:T(8,128)(2,1)S(1)}, bf16[32,1152]{1,0:T(8,128)(2,1)S(1)}, u32[]{:S(2)}, u32[]{:S(2)}) collective-permute-start(bf16[32,1152]{1,0:T(8,128)(2,1)S(1)} %collective-permute-done.4.refs_2_), channel_id=1, source_target_pairs={{0,4},{4,0},{8,12},{12,8},{16,20},{20,16},{24,28},{28,24},{1,5},{5... | collective-permute-start | bytes 221192 | tf_op jit(solution)/shard_map/ppermute | solution.py:37
  10.7 2.4 %collective-permute-start.6 = (bf16[32,1152]{1,0:T(8,128)(2,1)S(1)}, bf16[32,1152]{1,0:T(8,128)(2,1)S(1)}, u32[]{:S(2)}, u32[]{:S(2)}) collective-permute-start(bf16[32,1152]{1,0:T(8,128)(2,1)S(1)} %collective-permute-done.3.refs_1_), channel_id=1, source_target_pairs={{0,4},{4,0},{8,12},{12,8},{16,20},{20,16},{24,28},{28,24},{1,5},{5... | collective-permute-start | bytes 221192 | tf_op jit(solution)/shard_map/ppermute | solution.py:37
  11.8 1.1 %collective-permute-start = (s32[1,64]{1,0:T(1,128)S(1)}, s32[1,64]{1,0:T(1,128)S(1)}, u32[]{:S(2)}, u32[]{:S(2)}) collective-permute-start(s32[1,64]{1,0:T(1,128)S(1)} %bitcast.1), channel_id=1, source_target_pairs={{0,4},{4,0},{8,12},{12,8},{16,20},{20,16},{24,28},{28,24},{1,5},{5... | collective-permute-start | bytes 776 | tf_op jit(solution)/shard_map/ppermute | solution.py:37
  13.6 5.3 %collective-permute-start.10 = (bf16[32,1152]{1,0:T(8,128)(2,1)S(1)}, bf16[32,1152]{1,0:T(8,128)(2,1)S(1)}, u32[]{:S(2)}, u32[]{:S(2)}) collective-permute-start(bf16[32,1152]{1,0:T(8,128)(2,1)S(1)} %get-tuple-element.21), channel_id=1, source_target_pairs={{0,24},{1,25},{2,26},{3,27},{4,7},{5,6},{6,5},{7,4},{8,16},{9,17},... | collective-permute-start | bytes 221192 | tf_op jit(solution)/shard_map/ppermute | solution.py:51
  15.9 4.4 %collective-permute-start.11 = (bf16[32,1152]{1,0:T(8,128)(2,1)S(1)}, bf16[32,1152]{1,0:T(8,128)(2,1)S(1)}, u32[]{:S(2)}, u32[]{:S(2)}) collective-permute-start(bf16[32,1152]{1,0:T(8,128)(2,1)S(1)} %get-tuple-element.22), channel_id=1, source_target_pairs={{0,16},{1,17},{2,18},{3,19},{4,6},{5,7},{6,4},{7,5},{8,24},{9,25},... | collective-permute-start | bytes 221192 | tf_op jit(solution)/shard_map/ppermute | solution.py:51
  16.4 4.2 %collective-permute-start.9 = (bf16[16,1152]{1,0:T(8,128)(2,1)S(1)}, bf16[16,1152]{1,0:T(8,128)(2,1)S(1)}, u32[]{:S(2)}, u32[]{:S(2)}) collective-permute-start(bf16[16,1152]{1,0:T(8,128)(2,1)S(1)} %get-tuple-element.16), channel_id=1, source_target_pairs={{0,12},{1,13},{2,14},{3,15},{4,1},{5,0},{6,3},{7,2},{8,4},{9,5},{1... | collective-permute-start | bytes 110600 | tf_op jit(solution)/shard_map/ppermute | solution.py:51
  17.4 4.0 %collective-permute-start.12 = (bf16[16,1152]{1,0:T(8,128)(2,1)S(1)}, bf16[16,1152]{1,0:T(8,128)(2,1)S(1)}, u32[]{:S(2)}, u32[]{:S(2)}) collective-permute-start(bf16[16,1152]{1,0:T(8,128)(2,1)S(1)} %get-tuple-element.24), channel_id=1, source_target_pairs={{0,8},{1,9},{2,10},{3,11},{4,5},{5,4},{6,7},{7,6},{8,0},{9,1},{10,... | collective-permute-start | bytes 110600 | tf_op jit(solution)/shard_map/ppermute | solution.py:51
  20.3 1.3 %collective-permute-start.13 = (bf16[16,1152]{1,0:T(8,128)(2,1)S(1)}, bf16[16,1152]{1,0:T(8,128)(2,1)S(1)}, u32[]{:S(2)}, u32[]{:S(2)}) collective-permute-start(bf16[16,1152]{1,0:T(8,128)(2,1)S(1)} %get-tuple-element.25), channel_id=1, source_target_pairs={{0,4},{4,0},{8,12},{12,8},{16,20},{20,16},{24,28},{28,24},{1,5},{5... | collective-permute-start | bytes 110600 | tf_op jit(solution)/shard_map/ppermute | solution.py:37

commit v24 on v23

--- a/solution.py
+++ b/solution.py
@@ -53,7 +53,7 @@
 
 def orders(blocks):
     falling = list(range(blocks - 1, 0, -1))
-    return falling, falling[1::-1] + falling[2:]
+    return falling[1::-1] + falling[2:], falling
 
 
 def cross_first(distance):

time: 22.6 us -> 22.5 us (level)
    ppermute x6, waiting for transfers between devices: 1.92 us -> 2.48 us  [core_swap(): return lax.ppermute(block, 'img', [(i, i ^ 1) for i in range(size)])]
    ppermute x8, waiting for transfers between devices: 4.5 us -> 4.04 us  [chip_swap(): return lax.ppermute(block, ('img', 'txt'), pairs)]
  transfers between devices with their start and end apart: 14 -> 14, of which waited for: 9 -> 8; matrix products, arithmetic and copies ran while one was open for 3% -> 3% of each run, Pallas kernels for 1% -> 1%
where the time goes in v24:
time: 22.5 us; the launch traced here: 22.3 us
  starting transfers between devices  12.8 us (57%)
  waiting for transfers between devices  6.52 us (29%)
  Pallas kernels  1.58 us (7%)
  local copies, waits for them, and re-layouts  0.79 us (4%)
  between operations  0.69 us (3%)
    ppermute x8, starting transfers between devices, chip_swap(): return lax.ppermute(block, ('img', 'txt'), pairs)  10.9 us
    ppermute x8, waiting for transfers between devices, chip_swap(): return lax.ppermute(block, ('img', 'txt'), pairs)  4.04 us
    ppermute x6, waiting for transfers between devices, core_swap(): return lax.ppermute(block, 'img', [(i, i ^ 1) for i in range(size)])  2.48 us
    ppermute x6, starting transfers between devices, core_swap(): return lax.ppermute(block, 'img', [(i, i ^ 1) for i in range(size)])  1.89 us
    pallas_call x5, Pallas kernels, call(): pl.pallas_call(kernel, out_shape=outs, in_specs=[VMEM] * len(args), out_s...  1.58 us
    unnamed x5, local copies, waits for them, and re-layouts  0.78 us
  transfers between devices with their start and end apart: 14, of which 8 were waited for; matrix products, arithmetic and copies ran while one was open for 3% of the time, Pallas kernels for 1%

profile of v24, /device:TPU:0, one launch (start us, length us, event | category | flops | bytes accessed | tf_op | source)
XLA Modules:
  0.0 22.3 jit_solution(7667798599131753156)
XLA Ops:
  0.6 0.5 %collective-permute-start.2 = (bf16[16,1152]{1,0:T(8,128)(2,1)}, bf16[16,1152]{1,0:T(8,128)(2,1)S(1)}, u32[]{:S(2)}, u32[]{:S(2)}) collective-permute-start(bf16[16,1152]{1,0:T(8,128)(2,1)} %param.3), channel_id=1, source_target_pairs={{0,4},{4,0},{8,12},{12,8},{16,20},{20,16},{24,28},{28,24},{1,5},{5... | collective-permute-start | bytes 110600 | tf_op jit(solution)/shard_map/ppermute | solution.py:37
  1.2 0.8 %constant_dynamic-update-slice_fusion.1 = bf16[32,1152]{1,0:T(8,128)(2,1)S(1)} fusion(bf16[16,1152]{1,0:T(8,128)(2,1)} %param.4), kind=kLoop, calls=%fused_computation.1 | loop fusion | bytes 73728
  2.0 0.2 collective-permute-done.2.img_ref
  2.2 0.3 %collective-permute-done.1.txt_ref = bf16[16,1152]{1,0:T(8,128)(2,1)S(1)} collective-permute-done((bf16[16,1152]{1,0:T(8,128)(2,1)}, bf16[16,1152]{1,0:T(8,128)(2,1)S(1)}, u32[]{:S(2)}, u32[]{:S(2)}) %collective-permute-start.1) | collective-permute-done | bytes 36896 | tf_op jit(solution)/shard_map/ppermute | solution.py:37
  2.6 0.1 shard_map.50
  2.7 3.7 %collective-permute-start.4 = (bf16[32,1152]{1,0:T(8,128)(2,1)S(1)}, bf16[32,1152]{1,0:T(8,128)(2,1)S(1)}, u32[]{:S(2)}, u32[]{:S(2)}) collective-permute-start(bf16[32,1152]{1,0:T(8,128)(2,1)S(1)} %get-tuple-element.14.refs_0_), channel_id=1, source_target_pairs={{0,24},{1,25},{2,26},{3,27},{4,6},{5,7},{6,4},{7,5},{8,16},{9,17},... | collective-permute-start | bytes 221192 | tf_op jit(solution)/shard_map/ppermute | solution.py:51
  6.4 0.5 %collective-permute-start.3 = (bf16[32,1152]{1,0:T(8,128)(2,1)S(1)}, bf16[32,1152]{1,0:T(8,128)(2,1)S(1)}, u32[]{:S(2)}, u32[]{:S(2)}) collective-permute-start(bf16[32,1152]{1,0:T(8,128)(2,1)S(1)} %get-tuple-element.14.refs_0_), channel_id=1, source_target_pairs={{0,16},{1,17},{2,18},{3,19},{4,7},{5,6},{6,5},{7,4},{8,24},{9,25},... | collective-permute-start | bytes 221192 | tf_op jit(solution)/shard_map/ppermute | solution.py:51
  6.9 1.9 %collective-permute-start.8 = (bf16[32,1152]{1,0:T(8,128)(2,1)S(1)}, bf16[32,1152]{1,0:T(8,128)(2,1)S(1)}, u32[]{:S(2)}, u32[]{:S(2)}) collective-permute-start(bf16[32,1152]{1,0:T(8,128)(2,1)S(1)} %get-tuple-element.14.refs_0_), channel_id=1, source_target_pairs={{0,12},{1,13},{2,14},{3,15},{4,1},{5,0},{6,3},{7,2},{8,4},{9,5},{1... | collective-permute-start | bytes 221192 | tf_op jit(solution)/shard_map/ppermute | solution.py:51
  8.8 0.5 %collective-permute-start.5 = (bf16[32,1152]{1,0:T(8,128)(2,1)S(1)}, bf16[32,1152]{1,0:T(8,128)(2,1)S(1)}, u32[]{:S(2)}, u32[]{:S(2)}) collective-permute-start(bf16[32,1152]{1,0:T(8,128)(2,1)S(1)} %get-tuple-element.14.refs_0_), channel_id=1, source_target_pairs={{0,8},{1,9},{2,10},{3,11},{4,5},{5,4},{6,7},{7,6},{8,0},{9,1},{10,... | collective-permute-start | bytes 221192 | tf_op jit(solution)/shard_map/ppermute | solution.py:51
  9.3 1.4 %collective-permute-done.3.refs_1_ = bf16[32,1152]{1,0:T(8,128)(2,1)S(1)} collective-permute-done((bf16[32,1152]{1,0:T(8,128)(2,1)S(1)}, bf16[32,1152]{1,0:T(8,128)(2,1)S(1)}, u32[]{:S(2)}, u32[]{:S(2)}) %collective-permute-start.3) | collective-permute-done | bytes 73760 | tf_op jit(solution)/shard_map/ppermute | solution.py:51
  10.7 0.9 %collective-permute-start.6 = (bf16[32,1152]{1,0:T(8,128)(2,1)S(1)}, bf16[32,1152]{1,0:T(8,128)(2,1)S(1)}, u32[]{:S(2)}, u32[]{:S(2)}) collective-permute-start(bf16[32,1152]{1,0:T(8,128)(2,1)S(1)} %collective-permute-done.3.refs_1_), channel_id=1, source_target_pairs={{0,4},{4,0},{8,12},{12,8},{16,20},{20,16},{24,28},{28,24},{1,5},{5... | collective-permute-start | bytes 221192 | tf_op jit(solution)/shard_map/ppermute | solution.py:37
  11.7 1.1 %collective-permute-done.far_ids_ref = s32[1,64]{1,0:T(1,128)S(1)} collective-permute-done((s32[1,64]{1,0:T(1,128)S(1)}, s32[1,64]{1,0:T(1,128)S(1)}, u32[]{:S(2)}, u32[]{:S(2)}) %collective-permute-start) | collective-permute-done | bytes 288 | tf_op jit(solution)/shard_map/ppermute | solution.py:37
  12.8 0.3 %collective-permute-done.5.refs_3_ = bf16[32,1152]{1,0:T(8,128)(2,1)S(1)} collective-permute-done((bf16[32,1152]{1,0:T(8,128)(2,1)S(1)}, bf16[32,1152]{1,0:T(8,128)(2,1)S(1)}, u32[]{:S(2)}, u32[]{:S(2)}) %collective-permute-start.5) | collective-permute-done | bytes 73760 | tf_op jit(solution)/shard_map/ppermute | solution.py:51
  13.2 0.5 %shard_map.51 = (f32[32,1152]{1,0:T(8,128)S(1)}, bf16[16,1152]{1,0:T(8,128)(2,1)S(1)}, bf16[16,1152]{1,0:T(8,128)(2,1)S(1)}, bf16[32,1152]{1,0:T(8,128)(2,1)S(1)}, bf16[32,1152]{1,0:T(8,128)(2,1)S(1)}) custom-call(s32[1,64]{1,0:T(1,128)S(1)} %bitcast.2, s32[1,64]{1,0:T(1,128)S(1)} %collective-permute-done.far_ids_ref, ...), custom_call_target="tpu_custom_call" | custom-call | tf_op jit(solution)/shard_map/pallas_call | solution.py:69
  13.7 2.2 %collective-permute-start.10 = (bf16[32,1152]{1,0:T(8,128)(2,1)S(1)}, bf16[32,1152]{1,0:T(8,128)(2,1)S(1)}, u32[]{:S(2)}, u32[]{:S(2)}) collective-permute-start(bf16[32,1152]{1,0:T(8,128)(2,1)S(1)} %get-tuple-element.21), channel_id=1, source_target_pairs={{0,24},{1,25},{2,26},{3,27},{4,7},{5,6},{6,5},{7,4},{8,16},{9,17},... | collective-permute-start | bytes 221192 | tf_op jit(solution)/shard_map/ppermute | solution.py:51
  15.9 0.5 %collective-permute-start.11 = (bf16[32,1152]{1,0:T(8,128)(2,1)S(1)}, bf16[32,1152]{1,0:T(8,128)(2,1)S(1)}, u32[]{:S(2)}, u32[]{:S(2)}) collective-permute-start(bf16[32,1152]{1,0:T(8,128)(2,1)S(1)} %get-tuple-element.22), channel_id=1, source_target_pairs={{0,16},{1,17},{2,18},{3,19},{4,6},{5,7},{6,4},{7,5},{8,24},{9,25},... | collective-permute-start | bytes 221192 | tf_op jit(solution)/shard_map/ppermute | solution.py:51
  16.4 0.3 %collective-permute-start.9 = (bf16[16,1152]{1,0:T(8,128)(2,1)S(1)}, bf16[16,1152]{1,0:T(8,128)(2,1)S(1)}, u32[]{:S(2)}, u32[]{:S(2)}) collective-permute-start(bf16[16,1152]{1,0:T(8,128)(2,1)S(1)} %get-tuple-element.16), channel_id=1, source_target_pairs={{0,12},{1,13},{2,14},{3,15},{4,1},{5,0},{6,3},{7,2},{8,4},{9,5},{1... | collective-permute-start | bytes 110600 | tf_op jit(solution)/shard_map/ppermute | solution.py:51
  16.7 1.3 %collective-permute-start.12 = (bf16[16,1152]{1,0:T(8,128)(2,1)S(1)}, bf16[16,1152]{1,0:T(8,128)(2,1)S(1)}, u32[]{:S(2)}, u32[]{:S(2)}) collective-permute-start(bf16[16,1152]{1,0:T(8,128)(2,1)S(1)} %get-tuple-element.24), channel_id=1, source_target_pairs={{0,8},{1,9},{2,10},{3,11},{4,5},{5,4},{6,7},{7,6},{8,0},{9,1},{10,... | collective-permute-start | bytes 110600 | tf_op jit(solution)/shard_map/ppermute | solution.py:51
  18.0 1.0 %collective-permute-done.10.refs_0_ = bf16[32,1152]{1,0:T(8,128)(2,1)S(1)} collective-permute-done((bf16[32,1152]{1,0:T(8,128)(2,1)S(1)}, bf16[32,1152]{1,0:T(8,128)(2,1)S(1)}, u32[]{:S(2)}, u32[]{:S(2)}) %collective-permute-start.10) | collective-permute-done | bytes 73760 | tf_op jit(solution)/shard_map/ppermute | solution.py:51
  19.0 1.2 %collective-permute-done.11.refs_1_ = bf16[32,1152]{1,0:T(8,128)(2,1)S(1)} collective-permute-done((bf16[32,1152]{1,0:T(8,128)(2,1)S(1)}, bf16[32,1152]{1,0:T(8,128)(2,1)S(1)}, u32[]{:S(2)}, u32[]{:S(2)}) %collective-permute-start.11) | collective-permute-done | bytes 73760 | tf_op jit(solution)/shard_map/ppermute | solution.py:51
  20.3 0.4 %collective-permute-start.13 = (bf16[16,1152]{1,0:T(8,128)(2,1)S(1)}, bf16[16,1152]{1,0:T(8,128)(2,1)S(1)}, u32[]{:S(2)}, u32[]{:S(2)}) collective-permute-start(bf16[16,1152]{1,0:T(8,128)(2,1)S(1)} %get-tuple-element.25), channel_id=1, source_target_pairs={{0,4},{4,0},{8,12},{12,8},{16,20},{20,16},{24,28},{28,24},{1,5},{5... | collective-permute-start | bytes 110600 | tf_op jit(solution)/shard_map/ppermute | solution.py:37
  20.7 0.1 shard_map.52
  20.8 0.8 %collective-permute-done.13.got_ref = bf16[16,1152]{1,0:T(8,128)(2,1)S(1)} collective-permute-done((bf16[16,1152]{1,0:T(8,128)(2,1)S(1)}, bf16[16,1152]{1,0:T(8,128)(2,1)S(1)}, u32[]{:S(2)}, u32[]{:S(2)}) %collective-permute-start.13) | collective-permute-done | bytes 36896 | tf_op jit(solution)/shard_map/ppermute | solution.py:37
  21.6 0.8 %shard_map.54 = (f32[16,1152]{1,0:T(8,128)}, f32[16,1152]{1,0:T(8,128)}) custom-call(f32[32,1152]{1,0:T(8,128)S(1)} %get-tuple-element.17.unit_ref, f32[32,1]{1,0:T(8,128)S(1)} %get-tuple-element.18.inverse_ref, f32[16,1152]{1,0:T(8,128)S(1)} %get-tuple-element.19.first_ref, f32[16,1152]{1,0:T(8,128)S(1)} %get-tuple-element.23.keep_ref, ...), custom_call_target="tpu_custom_call" | custom-call | tf_op jit(solution)/shard_map/pallas_call | solution.py:69
  (15 shorter events, 0.2 us)
Async XLA Ops:
  0.6 1.4 %copy-start.1 = (bf16[16,1152]{1,0:T(8,128)(2,1)S(1)}, bf16[16,1152]{1,0:T(8,128)(2,1)}, u32[]{:S(2)}) copy-start(bf16[16,1152]{1,0:T(8,128)(2,1)} %param.3) | copy-start | bytes 110596
  0.6 1.6 %collective-permute-start.2 = (bf16[16,1152]{1,0:T(8,128)(2,1)}, bf16[16,1152]{1,0:T(8,128)(2,1)S(1)}, u32[]{:S(2)}, u32[]{:S(2)}) collective-permute-start(bf16[16,1152]{1,0:T(8,128)(2,1)} %param.3), channel_id=1, source_target_pairs={{0,4},{4,0},{8,12},{12,8},{16,20},{20,16},{24,28},{28,24},{1,5},{5... | collective-permute-start | bytes 110600 | tf_op jit(solution)/shard_map/ppermute | solution.py:37
  1.2 1.4 %collective-permute-start.1 = (bf16[16,1152]{1,0:T(8,128)(2,1)}, bf16[16,1152]{1,0:T(8,128)(2,1)S(1)}, u32[]{:S(2)}, u32[]{:S(2)}) collective-permute-start(bf16[16,1152]{1,0:T(8,128)(2,1)} %param.4), channel_id=1, source_target_pairs={{0,4},{4,0},{8,12},{12,8},{16,20},{20,16},{24,28},{28,24},{1,5},{5... | collective-permute-start | bytes 110600 | tf_op jit(solution)/shard_map/ppermute | solution.py:37
  2.7 9.0 %copy-start = (s32[64]{0:T(128)S(1)}, s32[64]{0:T(128)}, u32[]{:S(2)}) copy-start(s32[64]{0:T(128)} %param.5) | copy-start | bytes 772
  2.7 6.6 %collective-permute-start.4 = (bf16[32,1152]{1,0:T(8,128)(2,1)S(1)}, bf16[32,1152]{1,0:T(8,128)(2,1)S(1)}, u32[]{:S(2)}, u32[]{:S(2)}) collective-permute-start(bf16[32,1152]{1,0:T(8,128)(2,1)S(1)} %get-tuple-element.14.refs_0_), channel_id=1, source_target_pairs={{0,24},{1,25},{2,26},{3,27},{4,6},{5,7},{6,4},{7,5},{8,16},{9,17},... | collective-permute-start | bytes 221192 | tf_op jit(solution)/shard_map/ppermute | solution.py:51
  6.4 4.4 %collective-permute-start.3 = (bf16[32,1152]{1,0:T(8,128)(2,1)S(1)}, bf16[32,1152]{1,0:T(8,128)(2,1)S(1)}, u32[]{:S(2)}, u32[]{:S(2)}) collective-permute-start(bf16[32,1152]{1,0:T(8,128)(2,1)S(1)} %get-tuple-element.14.refs_0_), channel_id=1, source_target_pairs={{0,16},{1,17},{2,18},{3,19},{4,7},{5,6},{6,5},{7,4},{8,24},{9,25},... | collective-permute-start | bytes 221192 | tf_op jit(solution)/shard_map/ppermute | solution.py:51
  6.9 5.9 %collective-permute-start.8 = (bf16[32,1152]{1,0:T(8,128)(2,1)S(1)}, bf16[32,1152]{1,0:T(8,128)(2,1)S(1)}, u32[]{:S(2)}, u32[]{:S(2)}) collective-permute-start(bf16[32,1152]{1,0:T(8,128)(2,1)S(1)} %get-tuple-element.14.refs_0_), channel_id=1, source_target_pairs={{0,12},{1,13},{2,14},{3,15},{4,1},{5,0},{6,3},{7,2},{8,4},{9,5},{1... | collective-permute-start | bytes 221192 | tf_op jit(solution)/shard_map/ppermute | solution.py:51
  8.8 4.4 %collective-permute-start.5 = (bf16[32,1152]{1,0:T(8,128)(2,1)S(1)}, bf16[32,1152]{1,0:T(8,128)(2,1)S(1)}, u32[]{:S(2)}, u32[]{:S(2)}) collective-permute-start(bf16[32,1152]{1,0:T(8,128)(2,1)S(1)} %get-tuple-element.14.refs_0_), channel_id=1, source_target_pairs={{0,8},{1,9},{2,10},{3,11},{4,5},{5,4},{6,7},{7,6},{8,0},{9,1},{10,... | collective-permute-start | bytes 221192 | tf_op jit(solution)/shard_map/ppermute | solution.py:51
  9.3 3.8 %collective-permute-start.7 = (bf16[32,1152]{1,0:T(8,128)(2,1)S(1)}, bf16[32,1152]{1,0:T(8,128)(2,1)S(1)}, u32[]{:S(2)}, u32[]{:S(2)}) collective-permute-start(bf16[32,1152]{1,0:T(8,128)(2,1)S(1)} %collective-permute-done.4.refs_2_), channel_id=1, source_target_pairs={{0,4},{4,0},{8,12},{12,8},{16,20},{20,16},{24,28},{28,24},{1,5},{5... | collective-permute-start | bytes 221192 | tf_op jit(solution)/shard_map/ppermute | solution.py:37
  10.7 2.4 %collective-permute-start.6 = (bf16[32,1152]{1,0:T(8,128)(2,1)S(1)}, bf16[32,1152]{1,0:T(8,128)(2,1)S(1)}, u32[]{:S(2)}, u32[]{:S(2)}) collective-permute-start(bf16[32,1152]{1,0:T(8,128)(2,1)S(1)} %collective-permute-done.3.refs_1_), channel_id=1, source_target_pairs={{0,4},{4,0},{8,12},{12,8},{16,20},{20,16},{24,28},{28,24},{1,5},{5... | collective-permute-start | bytes 221192 | tf_op jit(solution)/shard_map/ppermute | solution.py:37
  11.7 1.1 %collective-permute-start = (s32[1,64]{1,0:T(1,128)S(1)}, s32[1,64]{1,0:T(1,128)S(1)}, u32[]{:S(2)}, u32[]{:S(2)}) collective-permute-start(s32[1,64]{1,0:T(1,128)S(1)} %bitcast.1), channel_id=1, source_target_pairs={{0,4},{4,0},{8,12},{12,8},{16,20},{20,16},{24,28},{28,24},{1,5},{5... | collective-permute-start | bytes 776 | tf_op jit(solution)/shard_map/ppermute | solution.py:37
  13.7 5.3 %collective-permute-start.10 = (bf16[32,1152]{1,0:T(8,128)(2,1)S(1)}, bf16[32,1152]{1,0:T(8,128)(2,1)S(1)}, u32[]{:S(2)}, u32[]{:S(2)}) collective-permute-start(bf16[32,1152]{1,0:T(8,128)(2,1)S(1)} %get-tuple-element.21), channel_id=1, source_target_pairs={{0,24},{1,25},{2,26},{3,27},{4,7},{5,6},{6,5},{7,4},{8,16},{9,17},... | collective-permute-start | bytes 221192 | tf_op jit(solution)/shard_map/ppermute | solution.py:51
  15.9 4.4 %collective-permute-start.11 = (bf16[32,1152]{1,0:T(8,128)(2,1)S(1)}, bf16[32,1152]{1,0:T(8,128)(2,1)S(1)}, u32[]{:S(2)}, u32[]{:S(2)}) collective-permute-start(bf16[32,1152]{1,0:T(8,128)(2,1)S(1)} %get-tuple-element.22), channel_id=1, source_target_pairs={{0,16},{1,17},{2,18},{3,19},{4,6},{5,7},{6,4},{7,5},{8,24},{9,25},... | collective-permute-start | bytes 221192 | tf_op jit(solution)/shard_map/ppermute | solution.py:51
  16.4 4.2 %collective-permute-start.9 = (bf16[16,1152]{1,0:T(8,128)(2,1)S(1)}, bf16[16,1152]{1,0:T(8,128)(2,1)S(1)}, u32[]{:S(2)}, u32[]{:S(2)}) collective-permute-start(bf16[16,1152]{1,0:T(8,128)(2,1)S(1)} %get-tuple-element.16), channel_id=1, source_target_pairs={{0,12},{1,13},{2,14},{3,15},{4,1},{5,0},{6,3},{7,2},{8,4},{9,5},{1... | collective-permute-start | bytes 110600 | tf_op jit(solution)/shard_map/ppermute | solution.py:51
  16.7 4.1 %collective-permute-start.12 = (bf16[16,1152]{1,0:T(8,128)(2,1)S(1)}, bf16[16,1152]{1,0:T(8,128)(2,1)S(1)}, u32[]{:S(2)}, u32[]{:S(2)}) collective-permute-start(bf16[16,1152]{1,0:T(8,128)(2,1)S(1)} %get-tuple-element.24), channel_id=1, source_target_pairs={{0,8},{1,9},{2,10},{3,11},{4,5},{5,4},{6,7},{7,6},{8,0},{9,1},{10,... | collective-permute-start | bytes 110600 | tf_op jit(solution)/shard_map/ppermute | solution.py:51
  20.3 1.3 %collective-permute-start.13 = (bf16[16,1152]{1,0:T(8,128)(2,1)S(1)}, bf16[16,1152]{1,0:T(8,128)(2,1)S(1)}, u32[]{:S(2)}, u32[]{:S(2)}) collective-permute-start(bf16[16,1152]{1,0:T(8,128)(2,1)S(1)} %get-tuple-element.25), channel_id=1, source_target_pairs={{0,4},{4,0},{8,12},{12,8},{16,20},{20,16},{24,28},{28,24},{1,5},{5... | collective-permute-start | bytes 110600 | tf_op jit(solution)/shard_map/ppermute | solution.py:37

commit v25 on v24

--- a/solution.py
+++ b/solution.py
@@ -13,6 +13,7 @@
 f32 = jnp.float32
 bf16 = jnp.bfloat16
 VMEM = pl.BlockSpec(memory_space=pltpu.VMEM)
+LANES = 128
 LONG = pl.CostEstimate(flops=10**10, bytes_accessed=10**7, transcendentals=0)
 
 
@@ -52,8 +53,7 @@
 
 
 def orders(blocks):
-    falling = list(range(blocks - 1, 0, -1))
-    return falling[1::-1] + falling[2:], falling
+    return [*range(blocks - 2, 0, -1), blocks - 1]
 
 
 def cross_first(distance):
@@ -91,20 +91,46 @@
     other_ref[rows:, :] = jnp.where(even, far_img, own_txt)
 
 
+def pack_kernel(ids_ref, piece_ref, out_ref):
+    height, width = piece_ref.shape
+    tiles = width // LANES
+    count = ids_ref.shape[1]
+    for k in range(tiles):
+        out_ref[k * height:(k + 1) * height, :] = piece_ref[:, k * LANES:(k + 1) * LANES]
+    rest = out_ref.shape[0] - tiles * height
+    row = lax.broadcasted_iota(jnp.int32, (rest, LANES), 0)
+    code = jnp.zeros((rest, LANES), f32)
+    for k in range(0, count, LANES):
+        ids = ids_ref[:, k:k + LANES]
+        if ids.shape[1] < LANES:
+            ids = jnp.concatenate([ids, jnp.zeros((1, LANES - ids.shape[1]), ids.dtype)], axis=1)
+        code = jnp.where(row == 2 * k // LANES, (ids // 256).astype(f32), code)
+        code = jnp.where(row == 2 * k // LANES + 1, (ids % 256).astype(f32), code)
+    out_ref[tiles * height:, :] = code.astype(bf16)
+
+
+def unpack(ref, height, width, count):
+    tiles = width // LANES
+    piece = jnp.concatenate(
+        [ref[k * height:(k + 1) * height, :] for k in range(tiles)], axis=1
+    )
+    code = ref[tiles * height:, :].astype(f32)
+    ids = [code[k:k + 1] * 256.0 + code[k + 1:k + 2] for k in range(0, 2 * count // LANES or 2, 2)]
+    ids = jnp.concatenate(ids, axis=1)[:, :count].astype(jnp.int32)
+    return piece, ids
+
+
 def row_ids(rows, ids, far_ids, count):
     me_img = lax.axis_index("img")
     me_txt = lax.axis_index("txt")
     n_img = lax.axis_size("img")
     row = lax.broadcasted_iota(jnp.int32, (count, 1), 0)
     block, core, j = row // (2 * rows), row // rows % 2, row % rows
-    chips = []
-    for order in orders(count // (2 * rows)):
-        chip = jnp.zeros_like(block)
-        for k, distance in enumerate(order):
-            chip = jnp.where(block == k + 1, distance, chip)
-        chips.append(chip)
-    txt_ids = (me_txt * n_img + (((me_img // 2) ^ chips[0]) * 2 + core)) * rows + j
-    source = (me_txt ^ chips[1]) * rows + j
+    chip = jnp.zeros_like(block)
+    for k, distance in enumerate(orders(count // (2 * rows))):
+        chip = jnp.where(block == k + 1, distance, chip)
+    txt_ids = (me_txt * n_img + (((me_img // 2) ^ chip) * 2 + core)) * rows + j
+    source = (me_txt ^ chip) * rows + j
     here = lax.broadcasted_iota(jnp.int32, (count, ids.shape[1]), 1) == source
     per_core = jnp.where(core == me_img % 2, ids, far_ids)
     img_ids = jnp.sum(jnp.where(here, per_core, 0), axis=1, keepdims=True)
@@ -122,32 +148,34 @@
     return jnp.where(even, txt_ids, img_ids), other_ids
 
 
-def scores_of(mine_refs, other_refs):
+def scores_of(mine_refs, other):
     mine = jnp.concatenate([ref[...] for ref in mine_refs], axis=0)
+    return lax.dot_general(mine, other, (((1,), (1,)), ((), ())), preferred_element_type=f32)
+
+
+def most_kernel(blocks, *refs):
+    mine_refs, other_refs, (other_ref, scores_ref) = refs[:blocks], refs[blocks:-2], refs[-2:]
     other = jnp.concatenate([ref[...] for ref in other_refs], axis=0)
-    return lax.dot_general(mine, other, (((1,), (1,)), ((), ())), preferred_element_type=f32)
-
-
-def pair_kernel(blocks, plan, ids_ref, far_ids_ref, *refs):
-    mine_refs, other_refs = refs[:blocks], refs[blocks:2 * blocks]
-    own_ref, first_ref, second_ref, *send_refs = refs[2 * blocks:]
-    height = own_ref.shape[0]
+    other_ref[...] = other
+    scores_ref[...] = scores_of(mine_refs, other)
+
+
+def pair_kernel(blocks, plan, ids_ref, other_ref, scores_ref, last_ref, *refs):
+    mine_refs, (own_ref, first_ref, second_ref, *send_refs) = refs[:blocks], refs[blocks:]
+    height, width = own_ref.shape
     rows = height // 2
-    mine_ids, other_ids = side_ids(rows, ids_ref[...], far_ids_ref[...], blocks * height)
-    scores = scores_of(mine_refs, other_refs)
+    last, far_ids = unpack(last_ref, height, width, ids_ref.shape[1])
+    mine_ids, other_ids = side_ids(rows, ids_ref[...], far_ids, blocks * height)
+    scores = jnp.concatenate([scores_ref[...], scores_of(mine_refs, last)], axis=1)
     coeff = pair_coeff(scale_logit * scores + shift_logit, mine_ids == other_ids)
-    other = jnp.concatenate([ref[...] for ref in other_refs], axis=0)
+    other = jnp.concatenate([other_ref[...], last], axis=0)
     part = jnp.dot(coeff, other, preferred_element_type=f32)
     own_ref[...] = part[:height]
     even = is_even()
-    txt_order, img_order = orders(blocks)
 
     def block_of(distance):
-        txt, img = [
-            part[(order.index(distance) + 1) * height:(order.index(distance) + 2) * height]
-            for order in (txt_order, img_order)
-        ]
-        return jnp.where(even, txt, img).astype(bf16)
+        start = (orders(blocks).index(distance) + 1) * height
+        return part[start:start + height].astype(bf16)
 
     *whole, split = plan
     for distance, ref in zip(whole, send_refs):
@@ -199,15 +227,25 @@
     far_txt = core_swap(text_embeds)
     far_img = core_swap(image_embeds)
     near = jnp.concatenate([text_embeds, image_embeds])
-    mine, other = call(sides_kernel, [pair] * 2, [near, far_txt, far_img])
-    mine = [mine] + [chip_swap(mine, distances) for distances in zip(*orders(blocks))]
-    other = [other, *[core_swap(block) for block in mine[1:-1]], chip_swap(mine[0], (1, 1), lambda txt: 1)]
+    mine, *other = call(sides_kernel, [pair] * 2, [near, far_txt, far_img])
+    order = orders(blocks)
+    mine = [mine] + [chip_swap(mine, (k, k)) for k in order]
+    tiles = jax.ShapeDtypeStruct((2 * rows * (width // LANES) + 16, LANES), bf16)
+    (tiles,) = call(pack_kernel, [tiles], [ids, mine[-1]])
+    near_block = chip_swap(mine[0], (1, 1), lambda txt: 1)
+    other += [near_block if k == 1 else core_swap(x) for k, x in zip(order[:-1], mine[1:-1])]
+    count = blocks * 2 * rows
+    outs = [
+        jax.ShapeDtypeStruct((count - 2 * rows, width), bf16),
+        jax.ShapeDtypeStruct((count, count - 2 * rows), f32),
+    ]
+    most = call(functools.partial(most_kernel, blocks), outs, [*mine, *other], cost=LONG)
     plan = list(range(blocks - 1, 0, -1))
     far = plan[-1]
     own, first, second, *send = call(
         functools.partial(pair_kernel, blocks, plan),
         [total] + [piece] * 2 + [pair] * (blocks - 2),
-        [ids, core_swap(ids), *mine, *other],
+        [ids, *most, core_swap(tiles), *mine],
     )
     got = [chip_swap(block, (k, k)) for k, block in zip(plan, send)]
     first = chip_swap(first, (far, far), lambda txt: int(txt % 2 == 0 or far % 2 == 1))

time: 22.5 us -> 22.4 us (level)
  starting transfers between devices: 12.8 us -> 12.4 us
  Pallas kernels: 1.58 us -> 1.88 us
    ppermute x8, waiting for transfers between devices: 4.04 us -> 5.76 us  [chip_swap(): return lax.ppermute(block, ('img', 'txt'), pairs)]
    ppermute x6 -> x5, waiting for transfers between devices: 2.48 us -> 0.77 us  [core_swap(): return lax.ppermute(block, 'img', [(i, i ^ 1) for i in range(size)])]
    ppermute x8, starting transfers between devices: 10.9 us -> 10.5 us  [chip_swap(): return lax.ppermute(block, ('img', 'txt'), pairs)]
    pallas_call x5 -> x7, Pallas kernels: 1.58 us -> 1.88 us  [call(): pl.pallas_call(kernel, out_shape=outs, in_specs=[VMEM] * len(args), out_s...]
    ppermute x6 -> x5, starting transfers between devices: 1.89 us -> 1.9 us  [core_swap(): return lax.ppermute(block, 'img', [(i, i ^ 1) for i in range(size)])]
  transfers between devices with their start and end apart: 14 -> 13, of which waited for: 8 -> 8; matrix products, arithmetic and copies ran while one was open for 3% -> 4% of each run, Pallas kernels for 1% -> 2%
where the time goes in v25:
time: 22.4 us; the launch traced here: 22.2 us
  starting transfers between devices  12.4 us (55%)
  waiting for transfers between devices  6.53 us (29%)
  Pallas kernels  1.88 us (8%)
  local copies, waits for them, and re-layouts  0.79 us (4%)
  between operations  0.7 us (3%)
    ppermute x8, starting transfers between devices, chip_swap(): return lax.ppermute(block, ('img', 'txt'), pairs)  10.5 us
    ppermute x8, waiting for transfers between devices, chip_swap(): return lax.ppermute(block, ('img', 'txt'), pairs)  5.76 us
    ppermute x5, starting transfers between devices, core_swap(): return lax.ppermute(block, 'img', [(i, i ^ 1) for i in range(size)])  1.9 us
    pallas_call x7, Pallas kernels, call(): pl.pallas_call(kernel, out_shape=outs, in_specs=[VMEM] * len(args), out_s...  1.88 us
    unnamed x5, local copies, waits for them, and re-layouts  0.78 us
    ppermute x5, waiting for transfers between devices, core_swap(): return lax.ppermute(block, 'img', [(i, i ^ 1) for i in range(size)])  0.77 us
  transfers between devices with their start and end apart: 13, of which 8 were waited for; matrix products, arithmetic and copies ran while one was open for 4% of the time, Pallas kernels for 2%

profile of v25, /device:TPU:0, one launch (start us, length us, event | category | flops | bytes accessed | tf_op | source)
XLA Modules:
  0.0 22.2 jit_solution(252591572202410908)
XLA Ops:
  0.6 0.5 %collective-permute-start.1 = (bf16[16,1152]{1,0:T(8,128)(2,1)}, bf16[16,1152]{1,0:T(8,128)(2,1)S(1)}, u32[]{:S(2)}, u32[]{:S(2)}) collective-permute-start(bf16[16,1152]{1,0:T(8,128)(2,1)} %param.3), channel_id=1, source_target_pairs={{0,4},{4,0},{8,12},{12,8},{16,20},{20,16},{24,28},{28,24},{1,5},{5... | collective-permute-start | bytes 110600 | tf_op jit(solution)/shard_map/ppermute | solution.py:38
  1.2 0.8 %constant_dynamic-update-slice_fusion.1 = bf16[32,1152]{1,0:T(8,128)(2,1)S(1)} fusion(bf16[16,1152]{1,0:T(8,128)(2,1)} %param.4), kind=kLoop, calls=%fused_computation.1 | loop fusion | bytes 73728
  2.0 0.2 collective-permute-done.1.img_ref
  2.2 0.3 %collective-permute-done.txt_ref = bf16[16,1152]{1,0:T(8,128)(2,1)S(1)} collective-permute-done((bf16[16,1152]{1,0:T(8,128)(2,1)}, bf16[16,1152]{1,0:T(8,128)(2,1)S(1)}, u32[]{:S(2)}, u32[]{:S(2)}) %collective-permute-start) | collective-permute-done | bytes 36896 | tf_op jit(solution)/shard_map/ppermute | solution.py:38
  2.6 0.1 shard_map.50
  2.7 2.7 %collective-permute-start.2 = (bf16[32,1152]{1,0:T(8,128)(2,1)S(1)}, bf16[32,1152]{1,0:T(8,128)(2,1)S(1)}, u32[]{:S(2)}, u32[]{:S(2)}) collective-permute-start(bf16[32,1152]{1,0:T(8,128)(2,1)S(1)} %get-tuple-element.16.refs_0_), channel_id=1, source_target_pairs={{0,16},{1,17},{2,18},{3,19},{4,6},{5,7},{6,4},{7,5},{8,24},{9,25},... | collective-permute-start | bytes 221192 | tf_op jit(solution)/shard_map/ppermute | solution.py:52
  5.5 1.4 %collective-permute-start.4 = (bf16[32,1152]{1,0:T(8,128)(2,1)S(1)}, bf16[32,1152]{1,0:T(8,128)(2,1)S(1)}, u32[]{:S(2)}, u32[]{:S(2)}) collective-permute-start(bf16[32,1152]{1,0:T(8,128)(2,1)S(1)} %get-tuple-element.16.refs_0_), channel_id=1, source_target_pairs={{0,24},{1,25},{2,26},{3,27},{4,7},{5,6},{6,5},{7,4},{8,16},{9,17},... | collective-permute-start | bytes 221192 | tf_op jit(solution)/shard_map/ppermute | solution.py:52
  6.9 1.9 %collective-permute-start.6 = (bf16[32,1152]{1,0:T(8,128)(2,1)S(1)}, bf16[32,1152]{1,0:T(8,128)(2,1)S(1)}, u32[]{:S(2)}, u32[]{:S(2)}) collective-permute-start(bf16[32,1152]{1,0:T(8,128)(2,1)S(1)} %get-tuple-element.16.refs_0_), channel_id=1, source_target_pairs={{0,12},{1,13},{2,14},{3,15},{4,1},{5,0},{6,3},{7,2},{8,4},{9,5},{1... | collective-permute-start | bytes 221192 | tf_op jit(solution)/shard_map/ppermute | solution.py:52
  8.8 0.5 %collective-permute-start.3 = (bf16[32,1152]{1,0:T(8,128)(2,1)S(1)}, bf16[32,1152]{1,0:T(8,128)(2,1)S(1)}, u32[]{:S(2)}, u32[]{:S(2)}) collective-permute-start(bf16[32,1152]{1,0:T(8,128)(2,1)S(1)} %get-tuple-element.16.refs_0_), channel_id=1, source_target_pairs={{0,8},{1,9},{2,10},{3,11},{4,5},{5,4},{6,7},{7,6},{8,0},{9,1},{10,... | collective-permute-start | bytes 221192 | tf_op jit(solution)/shard_map/ppermute | solution.py:52
  9.3 1.4 %collective-permute-done.4.refs_3_.piece_ref = bf16[32,1152]{1,0:T(8,128)(2,1)S(1)} collective-permute-done((bf16[32,1152]{1,0:T(8,128)(2,1)S(1)}, bf16[32,1152]{1,0:T(8,128)(2,1)S(1)}, u32[]{:S(2)}, u32[]{:S(2)}) %collective-permute-start.4) | collective-permute-done | bytes 73760 | tf_op jit(solution)/shard_map/ppermute | solution.py:52
  10.8 1.0 %collective-permute-start.7 = (bf16[304,128]{1,0:T(8,128)(2,1)S(1)}, bf16[304,128]{1,0:T(8,128)(2,1)S(1)}, u32[]{:S(2)}, u32[]{:S(2)}) collective-permute-start(bf16[304,128]{1,0:T(8,128)(2,1)S(1)} %shard_map.52), channel_id=1, source_target_pairs={{0,4},{4,0},{8,12},{12,8},{16,20},{20,16},{24,28},{28,24},{1,5},{5... | collective-permute-start | bytes 233480 | tf_op jit(solution)/shard_map/ppermute | solution.py:38
  11.8 1.4 %collective-permute-done.3.refs_2_ = bf16[32,1152]{1,0:T(8,128)(2,1)S(1)} collective-permute-done((bf16[32,1152]{1,0:T(8,128)(2,1)S(1)}, bf16[32,1152]{1,0:T(8,128)(2,1)S(1)}, u32[]{:S(2)}, u32[]{:S(2)}) %collective-permute-start.3) | collective-permute-done | bytes 73760 | tf_op jit(solution)/shard_map/ppermute | solution.py:52
  13.2 0.2 %shard_map.51 = (bf16[96,1152]{1,0:T(8,128)(2,1)S(1)}, f32[128,96]{1,0:T(8,128)S(1)}) custom-call(bf16[32,1152]{1,0:T(8,128)(2,1)S(1)} %get-tuple-element.16.refs_0_, bf16[32,1152]{1,0:T(8,128)(2,1)S(1)} %collective-permute-done.2.refs_1_, bf16[32,1152]{1,0:T(8,128)(2,1)S(1)} %collective-permute-done.3.refs_2_, ...), custom_call_target="tpu_custom_call" | custom-call | flops 10000000000 | bytes 10000000 | tf_op jit(solution)/shard_map/pallas_call | solution.py:69
  13.4 0.6 %shard_map.53 = (f32[32,1152]{1,0:T(8,128)S(1)}, bf16[16,1152]{1,0:T(8,128)(2,1)S(1)}, bf16[16,1152]{1,0:T(8,128)(2,1)S(1)}, bf16[32,1152]{1,0:T(8,128)(2,1)S(1)}, bf16[32,1152]{1,0:T(8,128)(2,1)S(1)}) custom-call(s32[1,64]{1,0:T(1,128)S(1)} %bitcast.2, bf16[96,1152]{1,0:T(8,128)(2,1)S(1)} %get-tuple-element.18.other_ref, ...), custom_call_target="tpu_custom_call" | custom-call | tf_op jit(solution)/shard_map/pallas_call | solution.py:69
  14.0 1.8 %collective-permute-start.9 = (bf16[32,1152]{1,0:T(8,128)(2,1)S(1)}, bf16[32,1152]{1,0:T(8,128)(2,1)S(1)}, u32[]{:S(2)}, u32[]{:S(2)}) collective-permute-start(bf16[32,1152]{1,0:T(8,128)(2,1)S(1)} %get-tuple-element.25), channel_id=1, source_target_pairs={{0,24},{1,25},{2,26},{3,27},{4,7},{5,6},{6,5},{7,4},{8,16},{9,17},... | collective-permute-start | bytes 221192 | tf_op jit(solution)/shard_map/ppermute | solution.py:52
  15.8 0.5 %collective-permute-start.10 = (bf16[32,1152]{1,0:T(8,128)(2,1)S(1)}, bf16[32,1152]{1,0:T(8,128)(2,1)S(1)}, u32[]{:S(2)}, u32[]{:S(2)}) collective-permute-start(bf16[32,1152]{1,0:T(8,128)(2,1)S(1)} %get-tuple-element.26), channel_id=1, source_target_pairs={{0,16},{1,17},{2,18},{3,19},{4,6},{5,7},{6,4},{7,5},{8,24},{9,25},... | collective-permute-start | bytes 221192 | tf_op jit(solution)/shard_map/ppermute | solution.py:52
  16.3 1.0 %collective-permute-start.8 = (bf16[16,1152]{1,0:T(8,128)(2,1)S(1)}, bf16[16,1152]{1,0:T(8,128)(2,1)S(1)}, u32[]{:S(2)}, u32[]{:S(2)}) collective-permute-start(bf16[16,1152]{1,0:T(8,128)(2,1)S(1)} %get-tuple-element.20), channel_id=1, source_target_pairs={{0,12},{1,13},{2,14},{3,15},{4,1},{5,0},{6,3},{7,2},{8,4},{9,5},{1... | collective-permute-start | bytes 110600 | tf_op jit(solution)/shard_map/ppermute | solution.py:52
  17.3 0.5 %collective-permute-start.11 = (bf16[16,1152]{1,0:T(8,128)(2,1)S(1)}, bf16[16,1152]{1,0:T(8,128)(2,1)S(1)}, u32[]{:S(2)}, u32[]{:S(2)}) collective-permute-start(bf16[16,1152]{1,0:T(8,128)(2,1)S(1)} %get-tuple-element.28), channel_id=1, source_target_pairs={{0,8},{1,9},{2,10},{3,11},{4,5},{5,4},{6,7},{7,6},{8,0},{9,1},{10,... | collective-permute-start | bytes 110600 | tf_op jit(solution)/shard_map/ppermute | solution.py:52
  17.9 1.5 %collective-permute-done.9.refs_0_ = bf16[32,1152]{1,0:T(8,128)(2,1)S(1)} collective-permute-done((bf16[32,1152]{1,0:T(8,128)(2,1)S(1)}, bf16[32,1152]{1,0:T(8,128)(2,1)S(1)}, u32[]{:S(2)}, u32[]{:S(2)}) %collective-permute-start.9) | collective-permute-done | bytes 73760 | tf_op jit(solution)/shard_map/ppermute | solution.py:52
  19.3 0.9 %collective-permute-done.10.refs_1_ = bf16[32,1152]{1,0:T(8,128)(2,1)S(1)} collective-permute-done((bf16[32,1152]{1,0:T(8,128)(2,1)S(1)}, bf16[32,1152]{1,0:T(8,128)(2,1)S(1)}, u32[]{:S(2)}, u32[]{:S(2)}) %collective-permute-start.10) | collective-permute-done | bytes 73760 | tf_op jit(solution)/shard_map/ppermute | solution.py:52
  20.2 0.3 %collective-permute-start.12 = (bf16[16,1152]{1,0:T(8,128)(2,1)S(1)}, bf16[16,1152]{1,0:T(8,128)(2,1)S(1)}, u32[]{:S(2)}, u32[]{:S(2)}) collective-permute-start(bf16[16,1152]{1,0:T(8,128)(2,1)S(1)} %get-tuple-element.29), channel_id=1, source_target_pairs={{0,4},{4,0},{8,12},{12,8},{16,20},{20,16},{24,28},{28,24},{1,5},{5... | collective-permute-start | bytes 110600 | tf_op jit(solution)/shard_map/ppermute | solution.py:38
  20.6 0.7 %collective-permute-done.11.second_ref = bf16[16,1152]{1,0:T(8,128)(2,1)S(1)} collective-permute-done((bf16[16,1152]{1,0:T(8,128)(2,1)S(1)}, bf16[16,1152]{1,0:T(8,128)(2,1)S(1)}, u32[]{:S(2)}, u32[]{:S(2)}) %collective-permute-start.11) | collective-permute-done | bytes 36896 | tf_op jit(solution)/shard_map/ppermute | solution.py:52
  21.3 0.2 collective-permute-done.12.got_ref
  21.5 0.8 %shard_map.56 = (f32[16,1152]{1,0:T(8,128)}, f32[16,1152]{1,0:T(8,128)}) custom-call(f32[32,1152]{1,0:T(8,128)S(1)} %get-tuple-element.21.unit_ref, f32[32,1]{1,0:T(8,128)S(1)} %get-tuple-element.22.inverse_ref, f32[16,1152]{1,0:T(8,128)S(1)} %get-tuple-element.23.first_ref, f32[16,1152]{1,0:T(8,128)S(1)} %get-tuple-element.27.keep_ref, ...), custom_call_target="tpu_custom_call" | custom-call | tf_op jit(solution)/shard_map/pallas_call | solution.py:69
  (15 shorter events, 0.3 us)
Async XLA Ops:
  0.6 1.4 %copy-start.1 = (bf16[16,1152]{1,0:T(8,128)(2,1)S(1)}, bf16[16,1152]{1,0:T(8,128)(2,1)}, u32[]{:S(2)}) copy-start(bf16[16,1152]{1,0:T(8,128)(2,1)} %param.3) | copy-start | bytes 110596
  0.6 1.6 %collective-permute-start.1 = (bf16[16,1152]{1,0:T(8,128)(2,1)}, bf16[16,1152]{1,0:T(8,128)(2,1)S(1)}, u32[]{:S(2)}, u32[]{:S(2)}) collective-permute-start(bf16[16,1152]{1,0:T(8,128)(2,1)} %param.3), channel_id=1, source_target_pairs={{0,4},{4,0},{8,12},{12,8},{16,20},{20,16},{24,28},{28,24},{1,5},{5... | collective-permute-start | bytes 110600 | tf_op jit(solution)/shard_map/ppermute | solution.py:38
  1.2 1.4 %collective-permute-start = (bf16[16,1152]{1,0:T(8,128)(2,1)}, bf16[16,1152]{1,0:T(8,128)(2,1)S(1)}, u32[]{:S(2)}, u32[]{:S(2)}) collective-permute-start(bf16[16,1152]{1,0:T(8,128)(2,1)} %param.4), channel_id=1, source_target_pairs={{0,4},{4,0},{8,12},{12,8},{16,20},{20,16},{24,28},{28,24},{1,5},{5... | collective-permute-start | bytes 110600 | tf_op jit(solution)/shard_map/ppermute | solution.py:38
  2.7 8.0 %copy-start = (s32[64]{0:T(128)S(1)}, s32[64]{0:T(128)}, u32[]{:S(2)}) copy-start(s32[64]{0:T(128)} %param.5) | copy-start | bytes 772
  2.7 6.6 %collective-permute-start.2 = (bf16[32,1152]{1,0:T(8,128)(2,1)S(1)}, bf16[32,1152]{1,0:T(8,128)(2,1)S(1)}, u32[]{:S(2)}, u32[]{:S(2)}) collective-permute-start(bf16[32,1152]{1,0:T(8,128)(2,1)S(1)} %get-tuple-element.16.refs_0_), channel_id=1, source_target_pairs={{0,16},{1,17},{2,18},{3,19},{4,6},{5,7},{6,4},{7,5},{8,24},{9,25},... | collective-permute-start | bytes 221192 | tf_op jit(solution)/shard_map/ppermute | solution.py:52
  5.5 5.3 %collective-permute-start.4 = (bf16[32,1152]{1,0:T(8,128)(2,1)S(1)}, bf16[32,1152]{1,0:T(8,128)(2,1)S(1)}, u32[]{:S(2)}, u32[]{:S(2)}) collective-permute-start(bf16[32,1152]{1,0:T(8,128)(2,1)S(1)} %get-tuple-element.16.refs_0_), channel_id=1, source_target_pairs={{0,24},{1,25},{2,26},{3,27},{4,7},{5,6},{6,5},{7,4},{8,16},{9,17},... | collective-permute-start | bytes 221192 | tf_op jit(solution)/shard_map/ppermute | solution.py:52
  6.9 4.9 %collective-permute-start.6 = (bf16[32,1152]{1,0:T(8,128)(2,1)S(1)}, bf16[32,1152]{1,0:T(8,128)(2,1)S(1)}, u32[]{:S(2)}, u32[]{:S(2)}) collective-permute-start(bf16[32,1152]{1,0:T(8,128)(2,1)S(1)} %get-tuple-element.16.refs_0_), channel_id=1, source_target_pairs={{0,12},{1,13},{2,14},{3,15},{4,1},{5,0},{6,3},{7,2},{8,4},{9,5},{1... | collective-permute-start | bytes 221192 | tf_op jit(solution)/shard_map/ppermute | solution.py:52
  8.8 4.4 %collective-permute-start.3 = (bf16[32,1152]{1,0:T(8,128)(2,1)S(1)}, bf16[32,1152]{1,0:T(8,128)(2,1)S(1)}, u32[]{:S(2)}, u32[]{:S(2)}) collective-permute-start(bf16[32,1152]{1,0:T(8,128)(2,1)S(1)} %get-tuple-element.16.refs_0_), channel_id=1, source_target_pairs={{0,8},{1,9},{2,10},{3,11},{4,5},{5,4},{6,7},{7,6},{8,0},{9,1},{10,... | collective-permute-start | bytes 221192 | tf_op jit(solution)/shard_map/ppermute | solution.py:52
  9.3 3.8 %collective-permute-start.5 = (bf16[32,1152]{1,0:T(8,128)(2,1)S(1)}, bf16[32,1152]{1,0:T(8,128)(2,1)S(1)}, u32[]{:S(2)}, u32[]{:S(2)}) collective-permute-start(bf16[32,1152]{1,0:T(8,128)(2,1)S(1)} %collective-permute-done.2.refs_1_), channel_id=1, source_target_pairs={{0,4},{4,0},{8,12},{12,8},{16,20},{20,16},{24,28},{28,24},{1,5},{5... | collective-permute-start | bytes 221192 | tf_op jit(solution)/shard_map/ppermute | solution.py:38
  10.8 2.6 %collective-permute-start.7 = (bf16[304,128]{1,0:T(8,128)(2,1)S(1)}, bf16[304,128]{1,0:T(8,128)(2,1)S(1)}, u32[]{:S(2)}, u32[]{:S(2)}) collective-permute-start(bf16[304,128]{1,0:T(8,128)(2,1)S(1)} %shard_map.52), channel_id=1, source_target_pairs={{0,4},{4,0},{8,12},{12,8},{16,20},{20,16},{24,28},{28,24},{1,5},{5... | collective-permute-start | bytes 233480 | tf_op jit(solution)/shard_map/ppermute | solution.py:38
  14.0 5.3 %collective-permute-start.9 = (bf16[32,1152]{1,0:T(8,128)(2,1)S(1)}, bf16[32,1152]{1,0:T(8,128)(2,1)S(1)}, u32[]{:S(2)}, u32[]{:S(2)}) collective-permute-start(bf16[32,1152]{1,0:T(8,128)(2,1)S(1)} %get-tuple-element.25), channel_id=1, source_target_pairs={{0,24},{1,25},{2,26},{3,27},{4,7},{5,6},{6,5},{7,4},{8,16},{9,17},... | collective-permute-start | bytes 221192 | tf_op jit(solution)/shard_map/ppermute | solution.py:52
  15.8 4.4 %collective-permute-start.10 = (bf16[32,1152]{1,0:T(8,128)(2,1)S(1)}, bf16[32,1152]{1,0:T(8,128)(2,1)S(1)}, u32[]{:S(2)}, u32[]{:S(2)}) collective-permute-start(bf16[32,1152]{1,0:T(8,128)(2,1)S(1)} %get-tuple-element.26), channel_id=1, source_target_pairs={{0,16},{1,17},{2,18},{3,19},{4,6},{5,7},{6,4},{7,5},{8,24},{9,25},... | collective-permute-start | bytes 221192 | tf_op jit(solution)/shard_map/ppermute | solution.py:52
  16.3 4.2 %collective-permute-start.8 = (bf16[16,1152]{1,0:T(8,128)(2,1)S(1)}, bf16[16,1152]{1,0:T(8,128)(2,1)S(1)}, u32[]{:S(2)}, u32[]{:S(2)}) collective-permute-start(bf16[16,1152]{1,0:T(8,128)(2,1)S(1)} %get-tuple-element.20), channel_id=1, source_target_pairs={{0,12},{1,13},{2,14},{3,15},{4,1},{5,0},{6,3},{7,2},{8,4},{9,5},{1... | collective-permute-start | bytes 110600 | tf_op jit(solution)/shard_map/ppermute | solution.py:52
  17.3 4.0 %collective-permute-start.11 = (bf16[16,1152]{1,0:T(8,128)(2,1)S(1)}, bf16[16,1152]{1,0:T(8,128)(2,1)S(1)}, u32[]{:S(2)}, u32[]{:S(2)}) collective-permute-start(bf16[16,1152]{1,0:T(8,128)(2,1)S(1)} %get-tuple-element.28), channel_id=1, source_target_pairs={{0,8},{1,9},{2,10},{3,11},{4,5},{5,4},{6,7},{7,6},{8,0},{9,1},{10,... | collective-permute-start | bytes 110600 | tf_op jit(solution)/shard_map/ppermute | solution.py:52
  20.2 1.3 %collective-permute-start.12 = (bf16[16,1152]{1,0:T(8,128)(2,1)S(1)}, bf16[16,1152]{1,0:T(8,128)(2,1)S(1)}, u32[]{:S(2)}, u32[]{:S(2)}) collective-permute-start(bf16[16,1152]{1,0:T(8,128)(2,1)S(1)} %get-tuple-element.29), channel_id=1, source_target_pairs={{0,4},{4,0},{8,12},{12,8},{16,20},{20,16},{24,28},{28,24},{1,5},{5... | collective-permute-start | bytes 110600 | tf_op jit(solution)/shard_map/ppermute | solution.py:38

commit v26 on v16

--- a/solution.py
+++ b/solution.py
@@ -37,15 +37,16 @@
     return lax.ppermute(block, "img", [(i, i ^ 1) for i in range(size)])
 
 
-def chip_swap(block, distance, cross=0):
+def chip_swap(block, distance, cross=lambda txt: 0):
     n_img, n_txt = lax.axis_size("img"), lax.axis_size("txt")
     pairs = []
     for img in range(n_img):
         for txt in range(n_txt):
+            other = cross(txt)
             if img % 2 == 0 and distance < n_img // 2:
-                pairs.append((img * n_txt + txt, (img ^ (2 * distance) ^ cross) * n_txt + txt))
+                pairs.append((img * n_txt + txt, (img ^ (2 * distance) ^ other) * n_txt + txt))
             if img % 2 == 1 and distance < n_txt:
-                pairs.append((img * n_txt + txt, (img ^ cross) * n_txt + (txt ^ distance)))
+                pairs.append((img * n_txt + txt, (img ^ other) * n_txt + (txt ^ distance)))
     return lax.ppermute(block, ("img", "txt"), pairs)
 
 
@@ -112,9 +113,9 @@
     return lax.dot_general(mine, other, (((1,), (1,)), ((), ())), preferred_element_type=f32)
 
 
-def pair_kernel(blocks, split, ids_ref, far_ids_ref, *refs):
+def pair_kernel(blocks, ids_ref, far_ids_ref, *refs):
     mine_refs, other_refs = refs[:blocks], refs[blocks:2 * blocks]
-    own_ref, same_ref, cross_ref, *send_refs = refs[2 * blocks:]
+    own_ref, *send_refs = refs[2 * blocks:]
     height = own_ref.shape[0]
     rows = height // 2
     mine_ids, other_ids = side_ids(rows, ids_ref[...], far_ids_ref[...], blocks * height)
@@ -123,13 +124,8 @@
     other = jnp.concatenate([ref[...] for ref in other_refs], axis=0)
     part = jnp.dot(coeff, other, preferred_element_type=f32)
     own_ref[...] = part[:height]
-    whole = [k for k in range(1, blocks) if k != split]
-    for k, ref in zip(whole, send_refs):
-        ref[...] = part[k * height:(k + 1) * height].astype(bf16)
-    block = part[split * height:(split + 1) * height].astype(bf16)
-    even = is_even()
-    same_ref[...] = jnp.where(even, block[:rows], block[rows:])
-    cross_ref[...] = jnp.where(even, block[rows:], block[:rows])
+    for k, ref in enumerate(send_refs):
+        ref[...] = part[(k + 1) * height:(k + 2) * height].astype(bf16)
 
 
 def sum_kernel(own_ref, *refs):
@@ -143,24 +139,23 @@
     send_ref[...] = jnp.where(even, total[rows:], total[:rows]).astype(bf16)
 
 
-def keep_kernel(raw_ref, keep_ref, same_ref, grad_ref, unit_ref, inverse_ref):
+def keep_kernel(raw_ref, keep_ref, grad_ref, unit_ref, inverse_ref):
     rows = keep_ref.shape[0]
     even = is_even()
     unit, inverse = normalize(raw_ref[...])
     grad_ref[...] = back_norm(
         jnp.where(even, unit[:rows], unit[rows:]),
         jnp.where(even, inverse[:rows], inverse[rows:]),
-        keep_ref[...] + same_ref[...].astype(f32),
+        keep_ref[...],
     )
     unit_ref[...] = jnp.where(even, unit[rows:], unit[:rows])
     inverse_ref[...] = jnp.where(even, inverse[rows:], inverse[:rows])
 
 
-def out_kernel(grad_ref, unit_ref, inverse_ref, cross_ref, got_ref, img_ref, txt_ref):
+def out_kernel(grad_ref, unit_ref, inverse_ref, got_ref, img_ref, txt_ref):
     even = is_even()
-    total = got_ref[...].astype(f32) + cross_ref[...].astype(f32)
     keep = grad_ref[...]
-    got = back_norm(unit_ref[...], inverse_ref[...], total)
+    got = back_norm(unit_ref[...], inverse_ref[...], got_ref[...].astype(f32))
     txt_ref[...] = jnp.where(even, keep, got)
     img_ref[...] = jnp.where(even, got, keep)
 
@@ -179,22 +174,17 @@
     mine, other = call(sides_kernel, [pair] * 2, [near, far_txt, far_img])
     order = list(range(blocks - 1, 0, -1))
     mine = [mine] + [chip_swap(mine, k) for k in order]
-    other = [other, *[core_swap(block) for block in mine[1:-1]], chip_swap(mine[0], 1, cross=1)]
-    split = min(2, blocks - 1)
-    own, same, cross, *send = call(
-        functools.partial(pair_kernel, blocks, split),
-        [total] + [piece] * 2 + [pair] * (blocks - 2),
+    other = [other, *[core_swap(block) for block in mine[1:-1]], chip_swap(mine[0], 1, lambda txt: 1)]
+    own, *send = call(
+        functools.partial(pair_kernel, blocks),
+        [total] + [pair] * (blocks - 1),
         [ids, core_swap(ids), *mine, *other],
     )
-    far = order.pop(split - 1)
     got = [chip_swap(block, k) for k, block in zip(order, send)]
-    same = chip_swap(same, far)
-    cross = chip_swap(cross, far, cross=1)
     keep, send = call(sum_kernel, [single, piece], [own, *got])
-    got = core_swap(send)
     column = jax.ShapeDtypeStruct((rows, 1), f32)
-    kept = call(keep_kernel, [single, single, column], [near, keep, same], cost=LONG)
-    return tuple(call(out_kernel, [single] * 2, [*kept, cross, got]))
+    kept = call(keep_kernel, [single, single, column], [near, keep], cost=LONG)
+    return tuple(call(out_kernel, [single] * 2, [*kept, core_swap(send)]))
 
 
 def solution(mesh):

time: 23.1 us -> 23 us (level)
  starting transfers between devices: 12.9 us -> 11.8 us
  waiting for transfers between devices: 6.95 us -> 7.92 us
    ppermute x8 -> x7, starting transfers between devices: 11.2 us -> 10.2 us  [chip_swap(): return lax.ppermute(block, ('img', 'txt'), pairs)]
    ppermute x6, waiting for transfers between devices: 1.69 us -> 2.69 us  [core_swap(): return lax.ppermute(block, 'img', [(i, i ^ 1) for i in range(size)])]
    ppermute x8 -> x7, waiting for transfers between devices: 5.26 us -> 5.24 us  [chip_swap(): return lax.ppermute(block, ('img', 'txt'), pairs)]
  transfers between devices with their start and end apart: 14 -> 13, of which waited for: 9 -> 9; matrix products, arithmetic and copies ran while one was open for 3% -> 3% of each run, Pallas kernels for 1% -> 1%
where the time goes in v26:
time: 23 us; the launch traced here: 22.9 us
  starting transfers between devices  11.8 us (51%)
  waiting for transfers between devices  7.92 us (34%)
  Pallas kernels  1.66 us (7%)
  local copies, waits for them, and re-layouts  0.79 us (3%)
  between operations  0.69 us (3%)
    ppermute x7, starting transfers between devices, chip_swap(): return lax.ppermute(block, ('img', 'txt'), pairs)  10.2 us
    ppermute x7, waiting for transfers between devices, chip_swap(): return lax.ppermute(block, ('img', 'txt'), pairs)  5.24 us
    ppermute x6, waiting for transfers between devices, core_swap(): return lax.ppermute(block, 'img', [(i, i ^ 1) for i in range(size)])  2.69 us
    pallas_call x5, Pallas kernels, call(): pl.pallas_call(kernel, out_shape=outs, in_specs=[VMEM] * len(args), out_s...  1.66 us
    ppermute x6, starting transfers between devices, core_swap(): return lax.ppermute(block, 'img', [(i, i ^ 1) for i in range(size)])  1.63 us
    unnamed x5, local copies, waits for them, and re-layouts  0.78 us
  transfers between devices with their start and end apart: 13, of which 9 were waited for; matrix products, arithmetic and copies ran while one was open for 3% of the time, Pallas kernels for 1%

profile of v26, /device:TPU:0, one launch (start us, length us, event | category | flops | bytes accessed | tf_op | source)
XLA Modules:
  0.0 22.9 jit_solution(11354564916037544291)
XLA Ops:
  0.6 0.5 %collective-permute-start.2 = (bf16[16,1152]{1,0:T(8,128)(2,1)}, bf16[16,1152]{1,0:T(8,128)(2,1)S(1)}, u32[]{:S(2)}, u32[]{:S(2)}) collective-permute-start(bf16[16,1152]{1,0:T(8,128)(2,1)} %param.3), channel_id=1, source_target_pairs={{0,4},{4,0},{8,12},{12,8},{16,20},{20,16},{24,28},{28,24},{1,5},{5... | collective-permute-start | bytes 110600 | tf_op jit(solution)/shard_map/ppermute | solution.py:37
  1.2 0.1 collective-permute-start.1
  1.2 0.8 %constant_dynamic-update-slice_fusion.1 = bf16[32,1152]{1,0:T(8,128)(2,1)S(1)} fusion(bf16[16,1152]{1,0:T(8,128)(2,1)} %param.4), kind=kLoop, calls=%fused_computation.1 | loop fusion | bytes 73728
  2.0 0.2 collective-permute-done.2.img_ref
  2.2 0.3 %collective-permute-done.1.txt_ref = bf16[16,1152]{1,0:T(8,128)(2,1)S(1)} collective-permute-done((bf16[16,1152]{1,0:T(8,128)(2,1)}, bf16[16,1152]{1,0:T(8,128)(2,1)S(1)}, u32[]{:S(2)}, u32[]{:S(2)}) %collective-permute-start.1) | collective-permute-done | bytes 36896 | tf_op jit(solution)/shard_map/ppermute | solution.py:37
  2.6 0.1 shard_map.50
  2.7 2.7 %collective-permute-start.4 = (bf16[32,1152]{1,0:T(8,128)(2,1)S(1)}, bf16[32,1152]{1,0:T(8,128)(2,1)S(1)}, u32[]{:S(2)}, u32[]{:S(2)}) collective-permute-start(bf16[32,1152]{1,0:T(8,128)(2,1)S(1)} %get-tuple-element.13.refs_0_), channel_id=1, source_target_pairs={{0,16},{1,17},{2,18},{3,19},{4,6},{5,7},{6,4},{7,5},{8,24},{9,25},... | collective-permute-start | bytes 221192 | tf_op jit(solution)/shard_map/ppermute | solution.py:50
  5.5 1.4 %collective-permute-start.3 = (bf16[32,1152]{1,0:T(8,128)(2,1)S(1)}, bf16[32,1152]{1,0:T(8,128)(2,1)S(1)}, u32[]{:S(2)}, u32[]{:S(2)}) collective-permute-start(bf16[32,1152]{1,0:T(8,128)(2,1)S(1)} %get-tuple-element.13.refs_0_), channel_id=1, source_target_pairs={{0,24},{1,25},{2,26},{3,27},{4,7},{5,6},{6,5},{7,4},{8,16},{9,17},... | collective-permute-start | bytes 221192 | tf_op jit(solution)/shard_map/ppermute | solution.py:50
  6.9 1.9 %collective-permute-start.8 = (bf16[32,1152]{1,0:T(8,128)(2,1)S(1)}, bf16[32,1152]{1,0:T(8,128)(2,1)S(1)}, u32[]{:S(2)}, u32[]{:S(2)}) collective-permute-start(bf16[32,1152]{1,0:T(8,128)(2,1)S(1)} %get-tuple-element.13.refs_0_), channel_id=1, source_target_pairs={{0,12},{1,13},{2,14},{3,15},{4,1},{5,0},{6,3},{7,2},{8,4},{9,5},{1... | collective-permute-start | bytes 221192 | tf_op jit(solution)/shard_map/ppermute | solution.py:50
  8.8 0.5 %collective-permute-start.5 = (bf16[32,1152]{1,0:T(8,128)(2,1)S(1)}, bf16[32,1152]{1,0:T(8,128)(2,1)S(1)}, u32[]{:S(2)}, u32[]{:S(2)}) collective-permute-start(bf16[32,1152]{1,0:T(8,128)(2,1)S(1)} %get-tuple-element.13.refs_0_), channel_id=1, source_target_pairs={{0,8},{1,9},{2,10},{3,11},{4,5},{5,4},{6,7},{7,6},{8,0},{9,1},{10,... | collective-permute-start | bytes 221192 | tf_op jit(solution)/shard_map/ppermute | solution.py:50
  9.3 1.4 %collective-permute-done.3.refs_1_ = bf16[32,1152]{1,0:T(8,128)(2,1)S(1)} collective-permute-done((bf16[32,1152]{1,0:T(8,128)(2,1)S(1)}, bf16[32,1152]{1,0:T(8,128)(2,1)S(1)}, u32[]{:S(2)}, u32[]{:S(2)}) %collective-permute-start.3) | collective-permute-done | bytes 73760 | tf_op jit(solution)/shard_map/ppermute | solution.py:50
  10.7 1.0 %collective-permute-start.6 = (bf16[32,1152]{1,0:T(8,128)(2,1)S(1)}, bf16[32,1152]{1,0:T(8,128)(2,1)S(1)}, u32[]{:S(2)}, u32[]{:S(2)}) collective-permute-start(bf16[32,1152]{1,0:T(8,128)(2,1)S(1)} %collective-permute-done.3.refs_1_), channel_id=1, source_target_pairs={{0,4},{4,0},{8,12},{12,8},{16,20},{20,16},{24,28},{28,24},{1,5},{5... | collective-permute-start | bytes 221192 | tf_op jit(solution)/shard_map/ppermute | solution.py:37
  11.7 1.1 %collective-permute-done.far_ids_ref = s32[1,64]{1,0:T(1,128)S(1)} collective-permute-done((s32[1,64]{1,0:T(1,128)S(1)}, s32[1,64]{1,0:T(1,128)S(1)}, u32[]{:S(2)}, u32[]{:S(2)}) %collective-permute-start) | collective-permute-done | bytes 288 | tf_op jit(solution)/shard_map/ppermute | solution.py:37
  12.8 0.3 %collective-permute-done.5.refs_3_ = bf16[32,1152]{1,0:T(8,128)(2,1)S(1)} collective-permute-done((bf16[32,1152]{1,0:T(8,128)(2,1)S(1)}, bf16[32,1152]{1,0:T(8,128)(2,1)S(1)}, u32[]{:S(2)}, u32[]{:S(2)}) %collective-permute-start.5) | collective-permute-done | bytes 73760 | tf_op jit(solution)/shard_map/ppermute | solution.py:50
  13.2 0.5 %shard_map.51 = (f32[32,1152]{1,0:T(8,128)S(1)}, bf16[32,1152]{1,0:T(8,128)(2,1)S(1)}, bf16[32,1152]{1,0:T(8,128)(2,1)S(1)}, bf16[32,1152]{1,0:T(8,128)(2,1)S(1)}) custom-call(s32[1,64]{1,0:T(1,128)S(1)} %bitcast.2, s32[1,64]{1,0:T(1,128)S(1)} %collective-permute-done.far_ids_ref, bf16[32,1152]{1,0:T(8,128)(2,1)S(1)} %get-tuple-element.13.refs_0_, ...), custom_call_target="tpu_custom_call" | custom-call | tf_op jit(solution)/shard_map/pallas_call | solution.py:59
  13.7 2.2 %collective-permute-start.9 = (bf16[32,1152]{1,0:T(8,128)(2,1)S(1)}, bf16[32,1152]{1,0:T(8,128)(2,1)S(1)}, u32[]{:S(2)}, u32[]{:S(2)}) collective-permute-start(bf16[32,1152]{1,0:T(8,128)(2,1)S(1)} %get-tuple-element.16), channel_id=1, source_target_pairs={{0,24},{1,25},{2,26},{3,27},{4,7},{5,6},{6,5},{7,4},{8,16},{9,17},... | collective-permute-start | bytes 221192 | tf_op jit(solution)/shard_map/ppermute | solution.py:50
  15.9 0.5 %collective-permute-start.10 = (bf16[32,1152]{1,0:T(8,128)(2,1)S(1)}, bf16[32,1152]{1,0:T(8,128)(2,1)S(1)}, u32[]{:S(2)}, u32[]{:S(2)}) collective-permute-start(bf16[32,1152]{1,0:T(8,128)(2,1)S(1)} %get-tuple-element.17), channel_id=1, source_target_pairs={{0,16},{1,17},{2,18},{3,19},{4,6},{5,7},{6,4},{7,5},{8,24},{9,25},... | collective-permute-start | bytes 221192 | tf_op jit(solution)/shard_map/ppermute | solution.py:50
  16.4 0.8 %collective-permute-start.11 = (bf16[32,1152]{1,0:T(8,128)(2,1)S(1)}, bf16[32,1152]{1,0:T(8,128)(2,1)S(1)}, u32[]{:S(2)}, u32[]{:S(2)}) collective-permute-start(bf16[32,1152]{1,0:T(8,128)(2,1)S(1)} %get-tuple-element.18), channel_id=1, source_target_pairs={{0,8},{1,9},{2,10},{3,11},{4,5},{5,4},{6,7},{7,6},{8,0},{9,1},{10,... | collective-permute-start | bytes 221192 | tf_op jit(solution)/shard_map/ppermute | solution.py:50
  17.3 1.8 %collective-permute-done.9.refs_0_ = bf16[32,1152]{1,0:T(8,128)(2,1)S(1)} collective-permute-done((bf16[32,1152]{1,0:T(8,128)(2,1)S(1)}, bf16[32,1152]{1,0:T(8,128)(2,1)S(1)}, u32[]{:S(2)}, u32[]{:S(2)}) %collective-permute-start.9) | collective-permute-done | bytes 73760 | tf_op jit(solution)/shard_map/ppermute | solution.py:50
  19.0 1.2 %collective-permute-done.10.refs_1_ = bf16[32,1152]{1,0:T(8,128)(2,1)S(1)} collective-permute-done((bf16[32,1152]{1,0:T(8,128)(2,1)S(1)}, bf16[32,1152]{1,0:T(8,128)(2,1)S(1)}, u32[]{:S(2)}, u32[]{:S(2)}) %collective-permute-start.10) | collective-permute-done | bytes 73760 | tf_op jit(solution)/shard_map/ppermute | solution.py:50
  20.3 0.5 %collective-permute-done.11.refs_2_ = bf16[32,1152]{1,0:T(8,128)(2,1)S(1)} collective-permute-done((bf16[32,1152]{1,0:T(8,128)(2,1)S(1)}, bf16[32,1152]{1,0:T(8,128)(2,1)S(1)}, u32[]{:S(2)}, u32[]{:S(2)}) %collective-permute-start.11) | collective-permute-done | bytes 73760 | tf_op jit(solution)/shard_map/ppermute | solution.py:50
  20.9 0.2 shard_map.53
  21.1 1.0 %collective-permute-done.12.got_ref = bf16[16,1152]{1,0:T(8,128)(2,1)S(1)} collective-permute-done((bf16[16,1152]{1,0:T(8,128)(2,1)S(1)}, bf16[16,1152]{1,0:T(8,128)(2,1)S(1)}, u32[]{:S(2)}, u32[]{:S(2)}) %collective-permute-start.12) | collective-permute-done | bytes 36896 | tf_op jit(solution)/shard_map/ppermute | solution.py:37
  22.1 0.8 %shard_map.54 = (f32[16,1152]{1,0:T(8,128)}, f32[16,1152]{1,0:T(8,128)}) custom-call(f32[16,1152]{1,0:T(8,128)S(1)} %get-tuple-element.20.grad_ref, f32[16,1152]{1,0:T(8,128)S(1)} %get-tuple-element.21.unit_ref, f32[16,1]{1,0:T(8,128)S(1)} %get-tuple-element.22.inverse_ref, bf16[16,1152]{1,0:T(8,128)(2,1)S(1)} %collective-permute-done.12.got_ref), custom_call_target="tpu_custom_call" | custom-call | tf_op jit(solution)/shard_map/pallas_call | solution.py:59
  (13 shorter events, 0.2 us)
Async XLA Ops:
  0.6 1.4 %copy-start.1 = (bf16[16,1152]{1,0:T(8,128)(2,1)S(1)}, bf16[16,1152]{1,0:T(8,128)(2,1)}, u32[]{:S(2)}) copy-start(bf16[16,1152]{1,0:T(8,128)(2,1)} %param.3) | copy-start | bytes 110596
  0.6 1.6 %collective-permute-start.2 = (bf16[16,1152]{1,0:T(8,128)(2,1)}, bf16[16,1152]{1,0:T(8,128)(2,1)S(1)}, u32[]{:S(2)}, u32[]{:S(2)}) collective-permute-start(bf16[16,1152]{1,0:T(8,128)(2,1)} %param.3), channel_id=1, source_target_pairs={{0,4},{4,0},{8,12},{12,8},{16,20},{20,16},{24,28},{28,24},{1,5},{5... | collective-permute-start | bytes 110600 | tf_op jit(solution)/shard_map/ppermute | solution.py:37
  1.2 1.4 %collective-permute-start.1 = (bf16[16,1152]{1,0:T(8,128)(2,1)}, bf16[16,1152]{1,0:T(8,128)(2,1)S(1)}, u32[]{:S(2)}, u32[]{:S(2)}) collective-permute-start(bf16[16,1152]{1,0:T(8,128)(2,1)} %param.4), channel_id=1, source_target_pairs={{0,4},{4,0},{8,12},{12,8},{16,20},{20,16},{24,28},{28,24},{1,5},{5... | collective-permute-start | bytes 110600 | tf_op jit(solution)/shard_map/ppermute | solution.py:37
  2.7 9.0 %copy-start = (s32[64]{0:T(128)S(1)}, s32[64]{0:T(128)}, u32[]{:S(2)}) copy-start(s32[64]{0:T(128)} %param.5) | copy-start | bytes 772
  2.7 6.6 %collective-permute-start.4 = (bf16[32,1152]{1,0:T(8,128)(2,1)S(1)}, bf16[32,1152]{1,0:T(8,128)(2,1)S(1)}, u32[]{:S(2)}, u32[]{:S(2)}) collective-permute-start(bf16[32,1152]{1,0:T(8,128)(2,1)S(1)} %get-tuple-element.13.refs_0_), channel_id=1, source_target_pairs={{0,16},{1,17},{2,18},{3,19},{4,6},{5,7},{6,4},{7,5},{8,24},{9,25},... | collective-permute-start | bytes 221192 | tf_op jit(solution)/shard_map/ppermute | solution.py:50
  5.5 5.3 %collective-permute-start.3 = (bf16[32,1152]{1,0:T(8,128)(2,1)S(1)}, bf16[32,1152]{1,0:T(8,128)(2,1)S(1)}, u32[]{:S(2)}, u32[]{:S(2)}) collective-permute-start(bf16[32,1152]{1,0:T(8,128)(2,1)S(1)} %get-tuple-element.13.refs_0_), channel_id=1, source_target_pairs={{0,24},{1,25},{2,26},{3,27},{4,7},{5,6},{6,5},{7,4},{8,16},{9,17},... | collective-permute-start | bytes 221192 | tf_op jit(solution)/shard_map/ppermute | solution.py:50
  6.9 5.9 %collective-permute-start.8 = (bf16[32,1152]{1,0:T(8,128)(2,1)S(1)}, bf16[32,1152]{1,0:T(8,128)(2,1)S(1)}, u32[]{:S(2)}, u32[]{:S(2)}) collective-permute-start(bf16[32,1152]{1,0:T(8,128)(2,1)S(1)} %get-tuple-element.13.refs_0_), channel_id=1, source_target_pairs={{0,12},{1,13},{2,14},{3,15},{4,1},{5,0},{6,3},{7,2},{8,4},{9,5},{1... | collective-permute-start | bytes 221192 | tf_op jit(solution)/shard_map/ppermute | solution.py:50
  8.8 4.4 %collective-permute-start.5 = (bf16[32,1152]{1,0:T(8,128)(2,1)S(1)}, bf16[32,1152]{1,0:T(8,128)(2,1)S(1)}, u32[]{:S(2)}, u32[]{:S(2)}) collective-permute-start(bf16[32,1152]{1,0:T(8,128)(2,1)S(1)} %get-tuple-element.13.refs_0_), channel_id=1, source_target_pairs={{0,8},{1,9},{2,10},{3,11},{4,5},{5,4},{6,7},{7,6},{8,0},{9,1},{10,... | collective-permute-start | bytes 221192 | tf_op jit(solution)/shard_map/ppermute | solution.py:50
  9.3 3.8 %collective-permute-start.7 = (bf16[32,1152]{1,0:T(8,128)(2,1)S(1)}, bf16[32,1152]{1,0:T(8,128)(2,1)S(1)}, u32[]{:S(2)}, u32[]{:S(2)}) collective-permute-start(bf16[32,1152]{1,0:T(8,128)(2,1)S(1)} %collective-permute-done.4.refs_2_), channel_id=1, source_target_pairs={{0,4},{4,0},{8,12},{12,8},{16,20},{20,16},{24,28},{28,24},{1,5},{5... | collective-permute-start | bytes 221192 | tf_op jit(solution)/shard_map/ppermute | solution.py:37
  10.7 2.4 %collective-permute-start.6 = (bf16[32,1152]{1,0:T(8,128)(2,1)S(1)}, bf16[32,1152]{1,0:T(8,128)(2,1)S(1)}, u32[]{:S(2)}, u32[]{:S(2)}) collective-permute-start(bf16[32,1152]{1,0:T(8,128)(2,1)S(1)} %collective-permute-done.3.refs_1_), channel_id=1, source_target_pairs={{0,4},{4,0},{8,12},{12,8},{16,20},{20,16},{24,28},{28,24},{1,5},{5... | collective-permute-start | bytes 221192 | tf_op jit(solution)/shard_map/ppermute | solution.py:37
  11.7 1.1 %collective-permute-start = (s32[1,64]{1,0:T(1,128)S(1)}, s32[1,64]{1,0:T(1,128)S(1)}, u32[]{:S(2)}, u32[]{:S(2)}) collective-permute-start(s32[1,64]{1,0:T(1,128)S(1)} %bitcast.1), channel_id=1, source_target_pairs={{0,4},{4,0},{8,12},{12,8},{16,20},{20,16},{24,28},{28,24},{1,5},{5... | collective-permute-start | bytes 776 | tf_op jit(solution)/shard_map/ppermute | solution.py:37
  13.7 5.3 %collective-permute-start.9 = (bf16[32,1152]{1,0:T(8,128)(2,1)S(1)}, bf16[32,1152]{1,0:T(8,128)(2,1)S(1)}, u32[]{:S(2)}, u32[]{:S(2)}) collective-permute-start(bf16[32,1152]{1,0:T(8,128)(2,1)S(1)} %get-tuple-element.16), channel_id=1, source_target_pairs={{0,24},{1,25},{2,26},{3,27},{4,7},{5,6},{6,5},{7,4},{8,16},{9,17},... | collective-permute-start | bytes 221192 | tf_op jit(solution)/shard_map/ppermute | solution.py:50
  15.9 4.4 %collective-permute-start.10 = (bf16[32,1152]{1,0:T(8,128)(2,1)S(1)}, bf16[32,1152]{1,0:T(8,128)(2,1)S(1)}, u32[]{:S(2)}, u32[]{:S(2)}) collective-permute-start(bf16[32,1152]{1,0:T(8,128)(2,1)S(1)} %get-tuple-element.17), channel_id=1, source_target_pairs={{0,16},{1,17},{2,18},{3,19},{4,6},{5,7},{6,4},{7,5},{8,24},{9,25},... | collective-permute-start | bytes 221192 | tf_op jit(solution)/shard_map/ppermute | solution.py:50
  16.4 4.4 %collective-permute-start.11 = (bf16[32,1152]{1,0:T(8,128)(2,1)S(1)}, bf16[32,1152]{1,0:T(8,128)(2,1)S(1)}, u32[]{:S(2)}, u32[]{:S(2)}) collective-permute-start(bf16[32,1152]{1,0:T(8,128)(2,1)S(1)} %get-tuple-element.18), channel_id=1, source_target_pairs={{0,8},{1,9},{2,10},{3,11},{4,5},{5,4},{6,7},{7,6},{8,0},{9,1},{10,... | collective-permute-start | bytes 221192 | tf_op jit(solution)/shard_map/ppermute | solution.py:50
  20.8 1.3 %collective-permute-start.12 = (bf16[16,1152]{1,0:T(8,128)(2,1)S(1)}, bf16[16,1152]{1,0:T(8,128)(2,1)S(1)}, u32[]{:S(2)}, u32[]{:S(2)}) collective-permute-start(bf16[16,1152]{1,0:T(8,128)(2,1)S(1)} %get-tuple-element.23), channel_id=1, source_target_pairs={{0,4},{4,0},{8,12},{12,8},{16,20},{20,16},{24,28},{28,24},{1,5},{5... | collective-permute-start | bytes 110600 | tf_op jit(solution)/shard_map/ppermute | solution.py:37

commit v27 on v20

--- a/solution.py
+++ b/solution.py
@@ -35,6 +35,11 @@
 def core_swap(block):
     size = lax.axis_size("img")
     return lax.ppermute(block, "img", [(i, i ^ 1) for i in range(size)])
+
+
+def core_send(block, source):
+    size = lax.axis_size("img")
+    return lax.ppermute(block, "img", [(i, i ^ 1) for i in range(source, size, 2)])
 
 
 def chip_swap(block, distance, cross=lambda txt: 0):
@@ -72,17 +77,23 @@
     )(*args)
 
 
-def sides_kernel(own_ref, txt_ref, img_ref, mine_ref, other_ref):
+def mine_kernel(near_ref, txt_ref, img_ref, mine_ref):
     rows = txt_ref.shape[0]
     even = is_even()
-    own = normalize(own_ref[...])[0].astype(bf16)
-    own_txt, own_img = own[:rows], own[rows:]
-    far_txt = normalize(txt_ref[...])[0].astype(bf16)
-    far_img = normalize(img_ref[...])[0].astype(bf16)
-    mine_ref[:rows, :] = jnp.where(even, own_txt, far_img)
-    mine_ref[rows:, :] = jnp.where(even, far_txt, own_img)
-    other_ref[:rows, :] = jnp.where(even, own_img, far_txt)
-    other_ref[rows:, :] = jnp.where(even, far_img, own_txt)
+    first = jnp.where(even, near_ref[:rows, :], img_ref[...])
+    second = jnp.where(even, txt_ref[...], near_ref[rows:, :])
+    mine_ref[:rows, :] = normalize(first)[0].astype(bf16)
+    mine_ref[rows:, :] = normalize(second)[0].astype(bf16)
+
+
+def other_kernel(near_ref, txt_ref, img_ref, mine_ref, other_ref, out_ref):
+    rows = txt_ref.shape[0]
+    even = is_even()
+    first = jnp.where(even, near_ref[rows:, :], txt_ref[...])
+    second = jnp.where(even, img_ref[...], near_ref[:rows, :])
+    other_ref[:rows, :] = normalize(first)[0].astype(bf16)
+    other_ref[rows:, :] = normalize(second)[0].astype(bf16)
+    out_ref[...] = mine_ref[...]
 
 
 def row_ids(rows, ids, far_ids, count):
@@ -176,12 +187,13 @@
     piece = jax.ShapeDtypeStruct((rows, width), bf16)
     single = jax.ShapeDtypeStruct((rows, width), f32)
     ids = pair_ids.reshape(1, -1)
-    far_txt = core_swap(text_embeds)
-    far_img = core_swap(image_embeds)
+    far_txt, far_img = core_send(text_embeds, 1), core_send(image_embeds, 0)
+    late_txt, late_img = core_send(text_embeds, 0), core_send(image_embeds, 1)
     near = jnp.concatenate([text_embeds, image_embeds])
-    mine, other = call(sides_kernel, [pair] * 2, [near, far_txt, far_img])
+    (own,) = call(mine_kernel, [pair], [near, far_txt, far_img])
+    other, again = call(other_kernel, [pair] * 2, [near, late_txt, late_img, own])
     order = list(range(blocks - 1, 0, -1))
-    mine = [mine] + [chip_swap(mine, k) for k in order]
+    mine = [own] + [chip_swap(again if k == 1 else own, k) for k in order]
     other = [other, *[core_swap(block) for block in mine[1:-1]], chip_swap(mine[0], 1, lambda txt: 1)]
     split = blocks - 1
     own, first, second, *send = call(

time: 22.5 us -> 30 us (1.33)
  starting transfers between devices: 12.7 us -> 19.7 us
    ppermute x0 -> x4, starting transfers between devices: none -> 7.96 us  [core_send(): lax.ppermute(block, 'img', [(i, i ^ 1) for i in range(source, size, 2)])]
    ppermute x0 -> x4, waiting for transfers between devices: none -> 1.99 us  [core_send(): lax.ppermute(block, 'img', [(i, i ^ 1) for i in range(source, size, 2)])]
    ppermute x8, waiting for transfers between devices: 4.71 us -> 3.21 us  [chip_swap(): return lax.ppermute(block, ('img', 'txt'), pairs)]
    ppermute x8, starting transfers between devices: 10.8 us -> 9.46 us  [chip_swap(): return lax.ppermute(block, ('img', 'txt'), pairs)]
    ppermute x6 -> x4, starting transfers between devices: 1.85 us -> 2.25 us  [core_swap(): return lax.ppermute(block, 'img', [(i, i ^ 1) for i in range(size)])]
    ppermute x6 -> x4, waiting for transfers between devices: 1.89 us -> 1.57 us  [core_swap(): return lax.ppermute(block, 'img', [(i, i ^ 1) for i in range(size)])]
    pallas_call x5 -> x6, Pallas kernels: 1.58 us -> 1.67 us  [call(): pl.pallas_call(kernel, out_shape=outs, in_specs=[VMEM] * len(args), out_s...]
    unnamed x5 -> x7, local copies, waits for them, and re-layouts: 0.78 us -> 0.79 us
  transfers between devices with their start and end apart: 14 -> 16, of which waited for: 9 -> 7; matrix products, arithmetic and copies ran while one was open for 3% -> 3% of each run, Pallas kernels for 1% -> 1%
where the time goes in v27:
time: 30 us; the launch traced here: 29.7 us
  starting transfers between devices  19.7 us (66%)
  waiting for transfers between devices  6.76 us (23%)
  Pallas kernels  1.67 us (6%)
  local copies, waits for them, and re-layouts  0.8 us (3%)
  between operations  0.77 us (3%)
    ppermute x8, starting transfers between devices, chip_swap(): return lax.ppermute(block, ('img', 'txt'), pairs)  9.46 us
    ppermute x4, starting transfers between devices, core_send(): lax.ppermute(block, 'img', [(i, i ^ 1) for i in range(source, size, 2)])  7.96 us
    ppermute x8, waiting for transfers between devices, chip_swap(): return lax.ppermute(block, ('img', 'txt'), pairs)  3.21 us
    ppermute x4, starting transfers between devices, core_swap(): return lax.ppermute(block, 'img', [(i, i ^ 1) for i in range(size)])  2.25 us
    ppermute x4, waiting for transfers between devices, core_send(): lax.ppermute(block, 'img', [(i, i ^ 1) for i in range(source, size, 2)])  1.99 us
    pallas_call x6, Pallas kernels, call(): pl.pallas_call(kernel, out_shape=outs, in_specs=[VMEM] * len(args), out_s...  1.67 us
    ppermute x4, waiting for transfers between devices, core_swap(): return lax.ppermute(block, 'img', [(i, i ^ 1) for i in range(size)])  1.57 us
    unnamed x7, local copies, waits for them, and re-layouts  0.79 us
  transfers between devices with their start and end apart: 16, of which 7 were waited for; matrix products, arithmetic and copies ran while one was open for 3% of the time, Pallas kernels for 1%

profile of v27, /device:TPU:0, one launch (start us, length us, event | category | flops | bytes accessed | tf_op | source)
XLA Modules:
  0.0 29.7 jit_solution(2529041748358860085)
XLA Ops:
  0.6 2.4 %collective-permute-start.2 = (bf16[16,1152]{1,0:T(8,128)(2,1)}, bf16[16,1152]{1,0:T(8,128)(2,1)S(1)}, u32[]{:S(2)}, u32[]{:S(2)}) collective-permute-start(bf16[16,1152]{1,0:T(8,128)(2,1)} %param.3), channel_id=1, source_target_pairs={{0,4},{8,12},{16,20},{24,28},{1,5},{9,13},{17,21},{25,29},{2,6},{1... | collective-permute-start | bytes 110600 | tf_op jit(solution)/shard_map/ppermute | solution.py:42
  3.0 1.3 %collective-permute-start.1 = (bf16[16,1152]{1,0:T(8,128)(2,1)}, bf16[16,1152]{1,0:T(8,128)(2,1)S(1)}, u32[]{:S(2)}, u32[]{:S(2)}) collective-permute-start(bf16[16,1152]{1,0:T(8,128)(2,1)} %param.4), channel_id=1, source_target_pairs={{4,0},{12,8},{20,16},{28,24},{5,1},{13,9},{21,17},{29,25},{6,2},{1... | collective-permute-start | bytes 110600 | tf_op jit(solution)/shard_map/ppermute | solution.py:42
  4.3 0.8 %constant_dynamic-update-slice_fusion.1 = bf16[32,1152]{1,0:T(8,128)(2,1)S(1)} fusion(bf16[16,1152]{1,0:T(8,128)(2,1)} %param.4), kind=kLoop, calls=%fused_computation.1 | loop fusion | bytes 73728
  5.1 1.2 %collective-permute-done.1.txt_ref = bf16[16,1152]{1,0:T(8,128)(2,1)S(1)} collective-permute-done((bf16[16,1152]{1,0:T(8,128)(2,1)}, bf16[16,1152]{1,0:T(8,128)(2,1)S(1)}, u32[]{:S(2)}, u32[]{:S(2)}) %collective-permute-start.1) | collective-permute-done | bytes 36896 | tf_op jit(solution)/shard_map/ppermute | solution.py:42
  6.4 2.4 %collective-permute-start.4 = (bf16[32,1152]{1,0:T(8,128)(2,1)S(1)}, bf16[32,1152]{1,0:T(8,128)(2,1)S(1)}, u32[]{:S(2)}, u32[]{:S(2)}) collective-permute-start(bf16[32,1152]{1,0:T(8,128)(2,1)S(1)} %shard_map.50.mine_ref.refs_0_), channel_id=1, source_target_pairs={{0,16},{1,17},{2,18},{3,19},{4,6},{5,7},{6,4},{7,5},{8,24},{9,25},... | collective-permute-start | bytes 221192 | tf_op jit(solution)/shard_map/ppermute | solution.py:55
  8.9 1.4 %collective-permute-start.3 = (bf16[32,1152]{1,0:T(8,128)(2,1)S(1)}, bf16[32,1152]{1,0:T(8,128)(2,1)S(1)}, u32[]{:S(2)}, u32[]{:S(2)}) collective-permute-start(bf16[32,1152]{1,0:T(8,128)(2,1)S(1)} %shard_map.50.mine_ref.refs_0_), channel_id=1, source_target_pairs={{0,24},{1,25},{2,26},{3,27},{4,7},{5,6},{6,5},{7,4},{8,16},{9,17},... | collective-permute-start | bytes 221192 | tf_op jit(solution)/shard_map/ppermute | solution.py:55
  10.3 1.3 %collective-permute-start.6 = (bf16[16,1152]{1,0:T(8,128)(2,1)S(1)}, bf16[16,1152]{1,0:T(8,128)(2,1)S(1)}, u32[]{:S(2)}, u32[]{:S(2)}) collective-permute-start(bf16[16,1152]{1,0:T(8,128)(2,1)S(1)} %copy-done.1), channel_id=1, source_target_pairs={{4,0},{12,8},{20,16},{28,24},{5,1},{13,9},{21,17},{29,25},{6,2},{1... | collective-permute-start | bytes 110600 | tf_op jit(solution)/shard_map/ppermute | solution.py:42
  11.6 3.0 %collective-permute-start.5 = (bf16[16,1152]{1,0:T(8,128)(2,1)S(1)}, bf16[16,1152]{1,0:T(8,128)(2,1)S(1)}, u32[]{:S(2)}, u32[]{:S(2)}) collective-permute-start(bf16[16,1152]{1,0:T(8,128)(2,1)S(1)} %copy-done.2), channel_id=1, source_target_pairs={{0,4},{8,12},{16,20},{24,28},{1,5},{9,13},{17,21},{25,29},{2,6},{1... | collective-permute-start | bytes 110600 | tf_op jit(solution)/shard_map/ppermute | solution.py:42
  14.7 0.8 %collective-permute-done.5.txt_ref = bf16[16,1152]{1,0:T(8,128)(2,1)S(1)} collective-permute-done((bf16[16,1152]{1,0:T(8,128)(2,1)S(1)}, bf16[16,1152]{1,0:T(8,128)(2,1)S(1)}, u32[]{:S(2)}, u32[]{:S(2)}) %collective-permute-start.5) | collective-permute-done | bytes 36896 | tf_op jit(solution)/shard_map/ppermute | solution.py:42
  15.6 1.0 %collective-permute-start.7 = (bf16[32,1152]{1,0:T(8,128)(2,1)S(1)}, bf16[32,1152]{1,0:T(8,128)(2,1)S(1)}, u32[]{:S(2)}, u32[]{:S(2)}) collective-permute-start(bf16[32,1152]{1,0:T(8,128)(2,1)S(1)} %get-tuple-element.14), channel_id=1, source_target_pairs={{0,8},{1,9},{2,10},{3,11},{4,5},{5,4},{6,7},{7,6},{8,0},{9,1},{10,... | collective-permute-start | bytes 221192 | tf_op jit(solution)/shard_map/ppermute | solution.py:55
  16.6 0.7 %collective-permute-start.9 = (bf16[32,1152]{1,0:T(8,128)(2,1)S(1)}, bf16[32,1152]{1,0:T(8,128)(2,1)S(1)}, u32[]{:S(2)}, u32[]{:S(2)}) collective-permute-start(bf16[32,1152]{1,0:T(8,128)(2,1)S(1)} %collective-permute-done.4.refs_2_), channel_id=1, source_target_pairs={{0,4},{4,0},{8,12},{12,8},{16,20},{20,16},{24,28},{28,24},{1,5},{5... | collective-permute-start | bytes 221192 | tf_op jit(solution)/shard_map/ppermute | solution.py:37
  17.4 0.4 %collective-permute-start = (s32[1,64]{1,0:T(1,128)S(1)}, s32[1,64]{1,0:T(1,128)S(1)}, u32[]{:S(2)}, u32[]{:S(2)}) collective-permute-start(s32[1,64]{1,0:T(1,128)S(1)} %bitcast.1), channel_id=1, source_target_pairs={{0,4},{4,0},{8,12},{12,8},{16,20},{20,16},{24,28},{28,24},{1,5},{5... | collective-permute-start | bytes 776 | tf_op jit(solution)/shard_map/ppermute | solution.py:37
  17.8 0.8 %collective-permute-done.far_ids_ref = s32[1,64]{1,0:T(1,128)S(1)} collective-permute-done((s32[1,64]{1,0:T(1,128)S(1)}, s32[1,64]{1,0:T(1,128)S(1)}, u32[]{:S(2)}, u32[]{:S(2)}) %collective-permute-start) | collective-permute-done | bytes 288 | tf_op jit(solution)/shard_map/ppermute | solution.py:37
  18.7 1.4 %collective-permute-done.7.refs_3_ = bf16[32,1152]{1,0:T(8,128)(2,1)S(1)} collective-permute-done((bf16[32,1152]{1,0:T(8,128)(2,1)S(1)}, bf16[32,1152]{1,0:T(8,128)(2,1)S(1)}, u32[]{:S(2)}, u32[]{:S(2)}) %collective-permute-start.7) | collective-permute-done | bytes 73760 | tf_op jit(solution)/shard_map/ppermute | solution.py:55
  20.0 0.5 %shard_map.52 = (f32[32,1152]{1,0:T(8,128)S(1)}, bf16[16,1152]{1,0:T(8,128)(2,1)S(1)}, bf16[16,1152]{1,0:T(8,128)(2,1)S(1)}, bf16[32,1152]{1,0:T(8,128)(2,1)S(1)}, bf16[32,1152]{1,0:T(8,128)(2,1)S(1)}) custom-call(s32[1,64]{1,0:T(1,128)S(1)} %bitcast.2, s32[1,64]{1,0:T(1,128)S(1)} %collective-permute-done.far_ids_ref, ...), custom_call_target="tpu_custom_call" | custom-call | tf_op jit(solution)/shard_map/pallas_call | solution.py:68
  20.6 2.0 %collective-permute-start.12 = (bf16[32,1152]{1,0:T(8,128)(2,1)S(1)}, bf16[32,1152]{1,0:T(8,128)(2,1)S(1)}, u32[]{:S(2)}, u32[]{:S(2)}) collective-permute-start(bf16[32,1152]{1,0:T(8,128)(2,1)S(1)} %get-tuple-element.21), channel_id=1, source_target_pairs={{0,24},{1,25},{2,26},{3,27},{4,7},{5,6},{6,5},{7,4},{8,16},{9,17},... | collective-permute-start | bytes 221192 | tf_op jit(solution)/shard_map/ppermute | solution.py:55
  22.6 0.5 %collective-permute-start.13 = (bf16[32,1152]{1,0:T(8,128)(2,1)S(1)}, bf16[32,1152]{1,0:T(8,128)(2,1)S(1)}, u32[]{:S(2)}, u32[]{:S(2)}) collective-permute-start(bf16[32,1152]{1,0:T(8,128)(2,1)S(1)} %get-tuple-element.22), channel_id=1, source_target_pairs={{0,16},{1,17},{2,18},{3,19},{4,6},{5,7},{6,4},{7,5},{8,24},{9,25},... | collective-permute-start | bytes 221192 | tf_op jit(solution)/shard_map/ppermute | solution.py:55
  23.1 0.5 %collective-permute-start.11 = (bf16[16,1152]{1,0:T(8,128)(2,1)S(1)}, bf16[16,1152]{1,0:T(8,128)(2,1)S(1)}, u32[]{:S(2)}, u32[]{:S(2)}) collective-permute-start(bf16[16,1152]{1,0:T(8,128)(2,1)S(1)} %get-tuple-element.16), channel_id=1, source_target_pairs={{0,12},{1,13},{2,14},{3,15},{4,1},{5,0},{6,3},{7,2},{8,4},{9,5},{1... | collective-permute-start | bytes 110600 | tf_op jit(solution)/shard_map/ppermute | solution.py:55
  23.6 1.5 %collective-permute-start.14 = (bf16[16,1152]{1,0:T(8,128)(2,1)S(1)}, bf16[16,1152]{1,0:T(8,128)(2,1)S(1)}, u32[]{:S(2)}, u32[]{:S(2)}) collective-permute-start(bf16[16,1152]{1,0:T(8,128)(2,1)S(1)} %get-tuple-element.24), channel_id=1, source_target_pairs={{0,8},{1,9},{2,10},{3,11},{4,5},{5,4},{6,7},{7,6},{8,0},{9,1},{10,... | collective-permute-start | bytes 110600 | tf_op jit(solution)/shard_map/ppermute | solution.py:55
  25.1 0.8 %collective-permute-done.12.refs_0_ = bf16[32,1152]{1,0:T(8,128)(2,1)S(1)} collective-permute-done((bf16[32,1152]{1,0:T(8,128)(2,1)S(1)}, bf16[32,1152]{1,0:T(8,128)(2,1)S(1)}, u32[]{:S(2)}, u32[]{:S(2)}) %collective-permute-start.12) | collective-permute-done | bytes 73760 | tf_op jit(solution)/shard_map/ppermute | solution.py:55
  25.9 1.0 %collective-permute-done.13.refs_1_ = bf16[32,1152]{1,0:T(8,128)(2,1)S(1)} collective-permute-done((bf16[32,1152]{1,0:T(8,128)(2,1)S(1)}, bf16[32,1152]{1,0:T(8,128)(2,1)S(1)}, u32[]{:S(2)}, u32[]{:S(2)}) %collective-permute-start.13) | collective-permute-done | bytes 73760 | tf_op jit(solution)/shard_map/ppermute | solution.py:55
  27.0 1.1 %collective-permute-start.15 = (bf16[16,1152]{1,0:T(8,128)(2,1)S(1)}, bf16[16,1152]{1,0:T(8,128)(2,1)S(1)}, u32[]{:S(2)}, u32[]{:S(2)}) collective-permute-start(bf16[16,1152]{1,0:T(8,128)(2,1)S(1)} %get-tuple-element.25), channel_id=1, source_target_pairs={{0,4},{4,0},{8,12},{12,8},{16,20},{20,16},{24,28},{28,24},{1,5},{5... | collective-permute-start | bytes 110600 | tf_op jit(solution)/shard_map/ppermute | solution.py:37
  28.2 0.7 %collective-permute-done.15.got_ref = bf16[16,1152]{1,0:T(8,128)(2,1)S(1)} collective-permute-done((bf16[16,1152]{1,0:T(8,128)(2,1)S(1)}, bf16[16,1152]{1,0:T(8,128)(2,1)S(1)}, u32[]{:S(2)}, u32[]{:S(2)}) %collective-permute-start.15) | collective-permute-done | bytes 36896 | tf_op jit(solution)/shard_map/ppermute | solution.py:37
  28.9 0.8 %shard_map.55 = (f32[16,1152]{1,0:T(8,128)}, f32[16,1152]{1,0:T(8,128)}) custom-call(f32[32,1152]{1,0:T(8,128)S(1)} %get-tuple-element.17.unit_ref, f32[32,1]{1,0:T(8,128)S(1)} %get-tuple-element.18.inverse_ref, f32[16,1152]{1,0:T(8,128)S(1)} %get-tuple-element.19.first_ref, f32[16,1152]{1,0:T(8,128)S(1)} %get-tuple-element.23.keep_ref, ...), custom_call_target="tpu_custom_call" | custom-call | tf_op jit(solution)/shard_map/pallas_call | solution.py:68
  (22 shorter events, 0.5 us)
Async XLA Ops:
  0.6 4.5 %copy-start.1 = (bf16[16,1152]{1,0:T(8,128)(2,1)S(1)}, bf16[16,1152]{1,0:T(8,128)(2,1)}, u32[]{:S(2)}) copy-start(bf16[16,1152]{1,0:T(8,128)(2,1)} %param.3) | copy-start | bytes 110596
  0.6 4.5 %collective-permute-start.2 = (bf16[16,1152]{1,0:T(8,128)(2,1)}, bf16[16,1152]{1,0:T(8,128)(2,1)S(1)}, u32[]{:S(2)}, u32[]{:S(2)}) collective-permute-start(bf16[16,1152]{1,0:T(8,128)(2,1)} %param.3), channel_id=1, source_target_pairs={{0,4},{8,12},{16,20},{24,28},{1,5},{9,13},{17,21},{25,29},{2,6},{1... | collective-permute-start | bytes 110600 | tf_op jit(solution)/shard_map/ppermute | solution.py:42
  3.0 3.3 %collective-permute-start.1 = (bf16[16,1152]{1,0:T(8,128)(2,1)}, bf16[16,1152]{1,0:T(8,128)(2,1)S(1)}, u32[]{:S(2)}, u32[]{:S(2)}) collective-permute-start(bf16[16,1152]{1,0:T(8,128)(2,1)} %param.4), channel_id=1, source_target_pairs={{4,0},{12,8},{20,16},{28,24},{5,1},{13,9},{21,17},{29,25},{6,2},{1... | collective-permute-start | bytes 110600 | tf_op jit(solution)/shard_map/ppermute | solution.py:42
  5.1 6.5 %copy-start.2 = (bf16[16,1152]{1,0:T(8,128)(2,1)S(1)}, bf16[16,1152]{1,0:T(8,128)(2,1)}, u32[]{:S(2)}) copy-start(bf16[16,1152]{1,0:T(8,128)(2,1)} %param.4) | copy-start | bytes 110596
  6.4 10.2 %collective-permute-start.4 = (bf16[32,1152]{1,0:T(8,128)(2,1)S(1)}, bf16[32,1152]{1,0:T(8,128)(2,1)S(1)}, u32[]{:S(2)}, u32[]{:S(2)}) collective-permute-start(bf16[32,1152]{1,0:T(8,128)(2,1)S(1)} %shard_map.50.mine_ref.refs_0_), channel_id=1, source_target_pairs={{0,16},{1,17},{2,18},{3,19},{4,6},{5,7},{6,4},{7,5},{8,24},{9,25},... | collective-permute-start | bytes 221192 | tf_op jit(solution)/shard_map/ppermute | solution.py:55
  8.9 8.5 %collective-permute-start.3 = (bf16[32,1152]{1,0:T(8,128)(2,1)S(1)}, bf16[32,1152]{1,0:T(8,128)(2,1)S(1)}, u32[]{:S(2)}, u32[]{:S(2)}) collective-permute-start(bf16[32,1152]{1,0:T(8,128)(2,1)S(1)} %shard_map.50.mine_ref.refs_0_), channel_id=1, source_target_pairs={{0,24},{1,25},{2,26},{3,27},{4,7},{5,6},{6,5},{7,4},{8,16},{9,17},... | collective-permute-start | bytes 221192 | tf_op jit(solution)/shard_map/ppermute | solution.py:55
  10.3 4.4 %collective-permute-start.6 = (bf16[16,1152]{1,0:T(8,128)(2,1)S(1)}, bf16[16,1152]{1,0:T(8,128)(2,1)S(1)}, u32[]{:S(2)}, u32[]{:S(2)}) collective-permute-start(bf16[16,1152]{1,0:T(8,128)(2,1)S(1)} %copy-done.1), channel_id=1, source_target_pairs={{4,0},{12,8},{20,16},{28,24},{5,1},{13,9},{21,17},{29,25},{6,2},{1... | collective-permute-start | bytes 110600 | tf_op jit(solution)/shard_map/ppermute | solution.py:42
  11.6 3.9 %collective-permute-start.5 = (bf16[16,1152]{1,0:T(8,128)(2,1)S(1)}, bf16[16,1152]{1,0:T(8,128)(2,1)S(1)}, u32[]{:S(2)}, u32[]{:S(2)}) collective-permute-start(bf16[16,1152]{1,0:T(8,128)(2,1)S(1)} %copy-done.2), channel_id=1, source_target_pairs={{0,4},{8,12},{16,20},{24,28},{1,5},{9,13},{17,21},{25,29},{2,6},{1... | collective-permute-start | bytes 110600 | tf_op jit(solution)/shard_map/ppermute | solution.py:42
  14.6 5.4 %collective-permute-start.10 = (bf16[32,1152]{1,0:T(8,128)(2,1)S(1)}, bf16[32,1152]{1,0:T(8,128)(2,1)S(1)}, u32[]{:S(2)}, u32[]{:S(2)}) collective-permute-start(bf16[32,1152]{1,0:T(8,128)(2,1)S(1)} %shard_map.50.mine_ref.refs_0_), channel_id=1, source_target_pairs={{0,12},{1,13},{2,14},{3,15},{4,1},{5,0},{6,3},{7,2},{8,4},{9,5},{1... | collective-permute-start | bytes 221192 | tf_op jit(solution)/shard_map/ppermute | solution.py:55
  15.6 1.8 %copy-start = (s32[64]{0:T(128)S(1)}, s32[64]{0:T(128)}, u32[]{:S(2)}) copy-start(s32[64]{0:T(128)} %param.5) | copy-start | bytes 772
  15.6 4.4 %collective-permute-start.7 = (bf16[32,1152]{1,0:T(8,128)(2,1)S(1)}, bf16[32,1152]{1,0:T(8,128)(2,1)S(1)}, u32[]{:S(2)}, u32[]{:S(2)}) collective-permute-start(bf16[32,1152]{1,0:T(8,128)(2,1)S(1)} %get-tuple-element.14), channel_id=1, source_target_pairs={{0,8},{1,9},{2,10},{3,11},{4,5},{5,4},{6,7},{7,6},{8,0},{9,1},{10,... | collective-permute-start | bytes 221192 | tf_op jit(solution)/shard_map/ppermute | solution.py:55
  16.6 3.4 %collective-permute-start.9 = (bf16[32,1152]{1,0:T(8,128)(2,1)S(1)}, bf16[32,1152]{1,0:T(8,128)(2,1)S(1)}, u32[]{:S(2)}, u32[]{:S(2)}) collective-permute-start(bf16[32,1152]{1,0:T(8,128)(2,1)S(1)} %collective-permute-done.4.refs_2_), channel_id=1, source_target_pairs={{0,4},{4,0},{8,12},{12,8},{16,20},{20,16},{24,28},{28,24},{1,5},{5... | collective-permute-start | bytes 221192 | tf_op jit(solution)/shard_map/ppermute | solution.py:37
  17.3 2.7 %collective-permute-start.8 = (bf16[32,1152]{1,0:T(8,128)(2,1)S(1)}, bf16[32,1152]{1,0:T(8,128)(2,1)S(1)}, u32[]{:S(2)}, u32[]{:S(2)}) collective-permute-start(bf16[32,1152]{1,0:T(8,128)(2,1)S(1)} %collective-permute-done.3.refs_1_), channel_id=1, source_target_pairs={{0,4},{4,0},{8,12},{12,8},{16,20},{20,16},{24,28},{28,24},{1,5},{5... | collective-permute-start | bytes 221192 | tf_op jit(solution)/shard_map/ppermute | solution.py:37
  17.4 1.3 %collective-permute-start = (s32[1,64]{1,0:T(1,128)S(1)}, s32[1,64]{1,0:T(1,128)S(1)}, u32[]{:S(2)}, u32[]{:S(2)}) collective-permute-start(s32[1,64]{1,0:T(1,128)S(1)} %bitcast.1), channel_id=1, source_target_pairs={{0,4},{4,0},{8,12},{12,8},{16,20},{20,16},{24,28},{28,24},{1,5},{5... | collective-permute-start | bytes 776 | tf_op jit(solution)/shard_map/ppermute | solution.py:37
  20.6 5.3 %collective-permute-start.12 = (bf16[32,1152]{1,0:T(8,128)(2,1)S(1)}, bf16[32,1152]{1,0:T(8,128)(2,1)S(1)}, u32[]{:S(2)}, u32[]{:S(2)}) collective-permute-start(bf16[32,1152]{1,0:T(8,128)(2,1)S(1)} %get-tuple-element.21), channel_id=1, source_target_pairs={{0,24},{1,25},{2,26},{3,27},{4,7},{5,6},{6,5},{7,4},{8,16},{9,17},... | collective-permute-start | bytes 221192 | tf_op jit(solution)/shard_map/ppermute | solution.py:55
  22.6 4.4 %collective-permute-start.13 = (bf16[32,1152]{1,0:T(8,128)(2,1)S(1)}, bf16[32,1152]{1,0:T(8,128)(2,1)S(1)}, u32[]{:S(2)}, u32[]{:S(2)}) collective-permute-start(bf16[32,1152]{1,0:T(8,128)(2,1)S(1)} %get-tuple-element.22), channel_id=1, source_target_pairs={{0,16},{1,17},{2,18},{3,19},{4,6},{5,7},{6,4},{7,5},{8,24},{9,25},... | collective-permute-start | bytes 221192 | tf_op jit(solution)/shard_map/ppermute | solution.py:55
  23.1 5.0 %collective-permute-start.11 = (bf16[16,1152]{1,0:T(8,128)(2,1)S(1)}, bf16[16,1152]{1,0:T(8,128)(2,1)S(1)}, u32[]{:S(2)}, u32[]{:S(2)}) collective-permute-start(bf16[16,1152]{1,0:T(8,128)(2,1)S(1)} %get-tuple-element.16), channel_id=1, source_target_pairs={{0,12},{1,13},{2,14},{3,15},{4,1},{5,0},{6,3},{7,2},{8,4},{9,5},{1... | collective-permute-start | bytes 110600 | tf_op jit(solution)/shard_map/ppermute | solution.py:55
  23.6 4.5 %collective-permute-start.14 = (bf16[16,1152]{1,0:T(8,128)(2,1)S(1)}, bf16[16,1152]{1,0:T(8,128)(2,1)S(1)}, u32[]{:S(2)}, u32[]{:S(2)}) collective-permute-start(bf16[16,1152]{1,0:T(8,128)(2,1)S(1)} %get-tuple-element.24), channel_id=1, source_target_pairs={{0,8},{1,9},{2,10},{3,11},{4,5},{5,4},{6,7},{7,6},{8,0},{9,1},{10,... | collective-permute-start | bytes 110600 | tf_op jit(solution)/shard_map/ppermute | solution.py:55
  27.0 1.9 %collective-permute-start.15 = (bf16[16,1152]{1,0:T(8,128)(2,1)S(1)}, bf16[16,1152]{1,0:T(8,128)(2,1)S(1)}, u32[]{:S(2)}, u32[]{:S(2)}) collective-permute-start(bf16[16,1152]{1,0:T(8,128)(2,1)S(1)} %get-tuple-element.25), channel_id=1, source_target_pairs={{0,4},{4,0},{8,12},{12,8},{16,20},{20,16},{24,28},{28,24},{1,5},{5... | collective-permute-start | bytes 110600 | tf_op jit(solution)/shard_map/ppermute | solution.py:37

commit v28 on v24

--- a/solution.py
+++ b/solution.py
@@ -53,7 +53,7 @@
 
 def orders(blocks):
     falling = list(range(blocks - 1, 0, -1))
-    return falling[1::-1] + falling[2:], falling
+    return falling, falling
 
 
 def cross_first(distance):
@@ -142,18 +142,18 @@
     even = is_even()
     txt_order, img_order = orders(blocks)
 
-    def block_of(distance):
-        txt, img = [
-            part[(order.index(distance) + 1) * height:(order.index(distance) + 2) * height]
-            for order in (txt_order, img_order)
+    def block_of(distances):
+        starts = [
+            (order.index(k) + 1) * height for order, k in zip((txt_order, img_order), distances)
         ]
+        txt, img = [part[start:start + height] for start in starts]
         return jnp.where(even, txt, img).astype(bf16)
 
     *whole, split = plan
-    for distance, ref in zip(whole, send_refs):
-        ref[...] = block_of(distance)
+    for distances, ref in zip(whole, send_refs):
+        ref[...] = block_of(distances)
     block = block_of(split)
-    first = jnp.logical_xor(even, cross_first(split))
+    first = jnp.logical_xor(even, cross_first(split[0]))
     first_ref[...] = jnp.where(first, block[:rows], block[rows:])
     second_ref[...] = jnp.where(first, block[rows:], block[:rows])
 
@@ -169,23 +169,30 @@
     send_ref[...] = jnp.where(even, total[rows:], total[:rows]).astype(bf16)
 
 
-def unit_kernel(raw_ref, first_ref, unit_ref, inverse_ref, rest_ref):
-    unit_ref[...], inverse_ref[...] = normalize(raw_ref[...])
-    rest_ref[...] = first_ref[...].astype(f32)
-
-
-def out_kernel(
-    far, unit_ref, inverse_ref, first_ref, keep_ref, second_ref, got_ref, img_ref, txt_ref
+def keep_kernel(
+    far, raw_ref, keep_ref, first_ref, second_ref, grad_ref, unit_ref, inverse_ref, rest_ref
 ):
     rows = keep_ref.shape[0]
     even = is_even()
-    first, second = first_ref[...], second_ref[...].astype(f32)
+    unit, inverse = normalize(raw_ref[...])
+    first, second = first_ref[...].astype(f32), second_ref[...].astype(f32)
     cross = cross_first(far)
-    keep = keep_ref[...] + jnp.where(cross, second, first)
-    got = got_ref[...].astype(f32) + jnp.where(cross, first, second)
-    unit, inverse = unit_ref[...], inverse_ref[...]
-    txt_ref[...] = back_norm(unit[:rows], inverse[:rows], jnp.where(even, keep, got))
-    img_ref[...] = back_norm(unit[rows:], inverse[rows:], jnp.where(even, got, keep))
+    grad_ref[...] = back_norm(
+        jnp.where(even, unit[:rows], unit[rows:]),
+        jnp.where(even, inverse[:rows], inverse[rows:]),
+        keep_ref[...] + jnp.where(cross, second, first),
+    )
+    rest_ref[...] = jnp.where(cross, first, second)
+    unit_ref[...] = jnp.where(even, unit[rows:], unit[:rows])
+    inverse_ref[...] = jnp.where(even, inverse[rows:], inverse[:rows])
+
+
+def out_kernel(grad_ref, unit_ref, inverse_ref, rest_ref, got_ref, img_ref, txt_ref):
+    even = is_even()
+    keep = grad_ref[...]
+    got = back_norm(unit_ref[...], inverse_ref[...], got_ref[...].astype(f32) + rest_ref[...])
+    txt_ref[...] = jnp.where(even, keep, got)
+    img_ref[...] = jnp.where(even, got, keep)
 
 
 def local(image_embeds, text_embeds, pair_ids):
@@ -202,22 +209,24 @@
     mine, other = call(sides_kernel, [pair] * 2, [near, far_txt, far_img])
     mine = [mine] + [chip_swap(mine, distances) for distances in zip(*orders(blocks))]
     other = [other, *[core_swap(block) for block in mine[1:-1]], chip_swap(mine[0], (1, 1), lambda txt: 1)]
-    plan = list(range(blocks - 1, 0, -1))
-    far = plan[-1]
+    txt_plan = list(range(blocks - 1, 0, -1))
+    img_plan = txt_plan[1::-1] + txt_plan[2:]
+    plan = list(zip(txt_plan, img_plan))
+    far = plan[-1][0]
     own, first, second, *send = call(
         functools.partial(pair_kernel, blocks, plan),
         [total] + [piece] * 2 + [pair] * (blocks - 2),
         [ids, core_swap(ids), *mine, *other],
     )
-    got = [chip_swap(block, (k, k)) for k, block in zip(plan, send)]
+    got = [chip_swap(block, distances) for distances, block in zip(plan, send)]
     first = chip_swap(first, (far, far), lambda txt: int(txt % 2 == 0 or far % 2 == 1))
     second = chip_swap(second, (far, far), lambda txt: int(txt % 2 == 1 and far % 2 == 0))
     keep, send = call(sum_kernel, [single, piece], [own, *got])
     got = core_swap(send)
-    column = jax.ShapeDtypeStruct((2 * rows, 1), f32)
-    ready = call(unit_kernel, [total, column, single], [near, first], cost=LONG)
-    kernel = functools.partial(out_kernel, far)
-    return tuple(call(kernel, [single] * 2, [*ready, keep, second, got]))
+    column = jax.ShapeDtypeStruct((rows, 1), f32)
+    outs = [single, single, column, single]
+    kept = call(functools.partial(keep_kernel, far), outs, [near, keep, first, second], cost=LONG)
+    return tuple(call(out_kernel, [single] * 2, [*kept, got]))
 
 
 def solution(mesh):

time: 22.5 us -> 22.6 us (level)
    ppermute x8, waiting for transfers between devices: 4.04 us -> 4.89 us  [chip_swap(): return lax.ppermute(block, ('img', 'txt'), pairs)]
    ppermute x6, waiting for transfers between devices: 2.48 us -> 1.69 us  [core_swap(): return lax.ppermute(block, 'img', [(i, i ^ 1) for i in range(size)])]
where the time goes in v28:
time: 22.6 us; the launch traced here: 22.4 us
  starting transfers between devices  12.7 us (56%)
  waiting for transfers between devices  6.57 us (29%)
  Pallas kernels  1.66 us (7%)
  local copies, waits for them, and re-layouts  0.79 us (3%)
  between operations  0.69 us (3%)
    ppermute x8, starting transfers between devices, chip_swap(): return lax.ppermute(block, ('img', 'txt'), pairs)  10.9 us
    ppermute x8, waiting for transfers between devices, chip_swap(): return lax.ppermute(block, ('img', 'txt'), pairs)  4.89 us
    ppermute x6, starting transfers between devices, core_swap(): return lax.ppermute(block, 'img', [(i, i ^ 1) for i in range(size)])  1.78 us
    ppermute x6, waiting for transfers between devices, core_swap(): return lax.ppermute(block, 'img', [(i, i ^ 1) for i in range(size)])  1.69 us
    pallas_call x5, Pallas kernels, call(): pl.pallas_call(kernel, out_shape=outs, in_specs=[VMEM] * len(args), out_s...  1.66 us
    unnamed x5, local copies, waits for them, and re-layouts  0.78 us
  transfers between devices with their start and end apart: 14, of which 8 were waited for; matrix products, arithmetic and copies ran while one was open for 3% of the time, Pallas kernels for 1%

profile of v28, /device:TPU:0, one launch (start us, length us, event | category | flops | bytes accessed | tf_op | source)
XLA Modules:
  0.0 22.4 jit_solution(12390501036151071640)
XLA Ops:
  0.6 0.5 %collective-permute-start.2 = (bf16[16,1152]{1,0:T(8,128)(2,1)}, bf16[16,1152]{1,0:T(8,128)(2,1)S(1)}, u32[]{:S(2)}, u32[]{:S(2)}) collective-permute-start(bf16[16,1152]{1,0:T(8,128)(2,1)} %param.3), channel_id=1, source_target_pairs={{0,4},{4,0},{8,12},{12,8},{16,20},{20,16},{24,28},{28,24},{1,5},{5... | collective-permute-start | bytes 110600 | tf_op jit(solution)/shard_map/ppermute | solution.py:37
  1.2 0.8 %constant_dynamic-update-slice_fusion.1 = bf16[32,1152]{1,0:T(8,128)(2,1)S(1)} fusion(bf16[16,1152]{1,0:T(8,128)(2,1)} %param.4), kind=kLoop, calls=%fused_computation.1 | loop fusion | bytes 73728
  2.0 0.2 collective-permute-done.2.img_ref
  2.2 0.3 %collective-permute-done.1.txt_ref = bf16[16,1152]{1,0:T(8,128)(2,1)S(1)} collective-permute-done((bf16[16,1152]{1,0:T(8,128)(2,1)}, bf16[16,1152]{1,0:T(8,128)(2,1)S(1)}, u32[]{:S(2)}, u32[]{:S(2)}) %collective-permute-start.1) | collective-permute-done | bytes 36896 | tf_op jit(solution)/shard_map/ppermute | solution.py:37
  2.6 0.1 shard_map.50
  2.7 2.7 %collective-permute-start.4 = (bf16[32,1152]{1,0:T(8,128)(2,1)S(1)}, bf16[32,1152]{1,0:T(8,128)(2,1)S(1)}, u32[]{:S(2)}, u32[]{:S(2)}) collective-permute-start(bf16[32,1152]{1,0:T(8,128)(2,1)S(1)} %get-tuple-element.15.refs_0_), channel_id=1, source_target_pairs={{0,16},{1,17},{2,18},{3,19},{4,6},{5,7},{6,4},{7,5},{8,24},{9,25},... | collective-permute-start | bytes 221192 | tf_op jit(solution)/shard_map/ppermute | solution.py:51
  5.5 1.4 %collective-permute-start.3 = (bf16[32,1152]{1,0:T(8,128)(2,1)S(1)}, bf16[32,1152]{1,0:T(8,128)(2,1)S(1)}, u32[]{:S(2)}, u32[]{:S(2)}) collective-permute-start(bf16[32,1152]{1,0:T(8,128)(2,1)S(1)} %get-tuple-element.15.refs_0_), channel_id=1, source_target_pairs={{0,24},{1,25},{2,26},{3,27},{4,7},{5,6},{6,5},{7,4},{8,16},{9,17},... | collective-permute-start | bytes 221192 | tf_op jit(solution)/shard_map/ppermute | solution.py:51
  6.9 1.9 %collective-permute-start.8 = (bf16[32,1152]{1,0:T(8,128)(2,1)S(1)}, bf16[32,1152]{1,0:T(8,128)(2,1)S(1)}, u32[]{:S(2)}, u32[]{:S(2)}) collective-permute-start(bf16[32,1152]{1,0:T(8,128)(2,1)S(1)} %get-tuple-element.15.refs_0_), channel_id=1, source_target_pairs={{0,12},{1,13},{2,14},{3,15},{4,1},{5,0},{6,3},{7,2},{8,4},{9,5},{1... | collective-permute-start | bytes 221192 | tf_op jit(solution)/shard_map/ppermute | solution.py:51
  8.8 0.5 %collective-permute-start.5 = (bf16[32,1152]{1,0:T(8,128)(2,1)S(1)}, bf16[32,1152]{1,0:T(8,128)(2,1)S(1)}, u32[]{:S(2)}, u32[]{:S(2)}) collective-permute-start(bf16[32,1152]{1,0:T(8,128)(2,1)S(1)} %get-tuple-element.15.refs_0_), channel_id=1, source_target_pairs={{0,8},{1,9},{2,10},{3,11},{4,5},{5,4},{6,7},{7,6},{8,0},{9,1},{10,... | collective-permute-start | bytes 221192 | tf_op jit(solution)/shard_map/ppermute | solution.py:51
  9.3 1.4 %collective-permute-done.3.refs_1_ = bf16[32,1152]{1,0:T(8,128)(2,1)S(1)} collective-permute-done((bf16[32,1152]{1,0:T(8,128)(2,1)S(1)}, bf16[32,1152]{1,0:T(8,128)(2,1)S(1)}, u32[]{:S(2)}, u32[]{:S(2)}) %collective-permute-start.3) | collective-permute-done | bytes 73760 | tf_op jit(solution)/shard_map/ppermute | solution.py:51
  10.7 1.0 %collective-permute-start.6 = (bf16[32,1152]{1,0:T(8,128)(2,1)S(1)}, bf16[32,1152]{1,0:T(8,128)(2,1)S(1)}, u32[]{:S(2)}, u32[]{:S(2)}) collective-permute-start(bf16[32,1152]{1,0:T(8,128)(2,1)S(1)} %collective-permute-done.3.refs_1_), channel_id=1, source_target_pairs={{0,4},{4,0},{8,12},{12,8},{16,20},{20,16},{24,28},{28,24},{1,5},{5... | collective-permute-start | bytes 221192 | tf_op jit(solution)/shard_map/ppermute | solution.py:37
  11.7 1.1 %collective-permute-done.far_ids_ref = s32[1,64]{1,0:T(1,128)S(1)} collective-permute-done((s32[1,64]{1,0:T(1,128)S(1)}, s32[1,64]{1,0:T(1,128)S(1)}, u32[]{:S(2)}, u32[]{:S(2)}) %collective-permute-start) | collective-permute-done | bytes 288 | tf_op jit(solution)/shard_map/ppermute | solution.py:37
  12.8 0.3 %collective-permute-done.5.refs_3_ = bf16[32,1152]{1,0:T(8,128)(2,1)S(1)} collective-permute-done((bf16[32,1152]{1,0:T(8,128)(2,1)S(1)}, bf16[32,1152]{1,0:T(8,128)(2,1)S(1)}, u32[]{:S(2)}, u32[]{:S(2)}) %collective-permute-start.5) | collective-permute-done | bytes 73760 | tf_op jit(solution)/shard_map/ppermute | solution.py:51
  13.2 0.5 %shard_map.51 = (f32[32,1152]{1,0:T(8,128)S(1)}, bf16[16,1152]{1,0:T(8,128)(2,1)S(1)}, bf16[16,1152]{1,0:T(8,128)(2,1)S(1)}, bf16[32,1152]{1,0:T(8,128)(2,1)S(1)}, bf16[32,1152]{1,0:T(8,128)(2,1)S(1)}) custom-call(s32[1,64]{1,0:T(1,128)S(1)} %bitcast.2, s32[1,64]{1,0:T(1,128)S(1)} %collective-permute-done.far_ids_ref, ...), custom_call_target="tpu_custom_call" | custom-call | tf_op jit(solution)/shard_map/pallas_call | solution.py:69
  13.7 2.2 %collective-permute-start.9 = (bf16[32,1152]{1,0:T(8,128)(2,1)S(1)}, bf16[32,1152]{1,0:T(8,128)(2,1)S(1)}, u32[]{:S(2)}, u32[]{:S(2)}) collective-permute-start(bf16[32,1152]{1,0:T(8,128)(2,1)S(1)} %get-tuple-element.18), channel_id=1, source_target_pairs={{0,24},{1,25},{2,26},{3,27},{4,6},{5,7},{6,4},{7,5},{8,16},{9,17},... | collective-permute-start | bytes 221192 | tf_op jit(solution)/shard_map/ppermute | solution.py:51
  15.9 0.5 %collective-permute-start.10 = (bf16[32,1152]{1,0:T(8,128)(2,1)S(1)}, bf16[32,1152]{1,0:T(8,128)(2,1)S(1)}, u32[]{:S(2)}, u32[]{:S(2)}) collective-permute-start(bf16[32,1152]{1,0:T(8,128)(2,1)S(1)} %get-tuple-element.19), channel_id=1, source_target_pairs={{0,16},{1,17},{2,18},{3,19},{4,7},{5,6},{6,5},{7,4},{8,24},{9,25},... | collective-permute-start | bytes 221192 | tf_op jit(solution)/shard_map/ppermute | solution.py:51
  16.4 1.1 %collective-permute-start.11 = (bf16[16,1152]{1,0:T(8,128)(2,1)S(1)}, bf16[16,1152]{1,0:T(8,128)(2,1)S(1)}, u32[]{:S(2)}, u32[]{:S(2)}) collective-permute-start(bf16[16,1152]{1,0:T(8,128)(2,1)S(1)} %get-tuple-element.21), channel_id=1, source_target_pairs={{0,12},{1,13},{2,14},{3,15},{4,1},{5,0},{6,3},{7,2},{8,4},{9,5},{1... | collective-permute-start | bytes 110600 | tf_op jit(solution)/shard_map/ppermute | solution.py:51
  17.5 0.5 %collective-permute-start.12 = (bf16[16,1152]{1,0:T(8,128)(2,1)S(1)}, bf16[16,1152]{1,0:T(8,128)(2,1)S(1)}, u32[]{:S(2)}, u32[]{:S(2)}) collective-permute-start(bf16[16,1152]{1,0:T(8,128)(2,1)S(1)} %get-tuple-element.22), channel_id=1, source_target_pairs={{0,8},{1,9},{2,10},{3,11},{4,5},{5,4},{6,7},{7,6},{8,0},{9,1},{10,... | collective-permute-start | bytes 110600 | tf_op jit(solution)/shard_map/ppermute | solution.py:51
  18.0 1.0 %collective-permute-done.9.refs_0_ = bf16[32,1152]{1,0:T(8,128)(2,1)S(1)} collective-permute-done((bf16[32,1152]{1,0:T(8,128)(2,1)S(1)}, bf16[32,1152]{1,0:T(8,128)(2,1)S(1)}, u32[]{:S(2)}, u32[]{:S(2)}) %collective-permute-start.9) | collective-permute-done | bytes 73760 | tf_op jit(solution)/shard_map/ppermute | solution.py:51
  19.0 1.2 %collective-permute-done.10.refs_1_ = bf16[32,1152]{1,0:T(8,128)(2,1)S(1)} collective-permute-done((bf16[32,1152]{1,0:T(8,128)(2,1)S(1)}, bf16[32,1152]{1,0:T(8,128)(2,1)S(1)}, u32[]{:S(2)}, u32[]{:S(2)}) %collective-permute-start.10) | collective-permute-done | bytes 73760 | tf_op jit(solution)/shard_map/ppermute | solution.py:51
  20.3 0.2 %collective-permute-start.13 = (bf16[16,1152]{1,0:T(8,128)(2,1)S(1)}, bf16[16,1152]{1,0:T(8,128)(2,1)S(1)}, u32[]{:S(2)}, u32[]{:S(2)}) collective-permute-start(bf16[16,1152]{1,0:T(8,128)(2,1)S(1)} %get-tuple-element.27), channel_id=1, source_target_pairs={{0,4},{4,0},{8,12},{12,8},{16,20},{20,16},{24,28},{28,24},{1,5},{5... | collective-permute-start | bytes 110600 | tf_op jit(solution)/shard_map/ppermute | solution.py:37
  20.5 0.9 %collective-permute-done.12.second_ref = bf16[16,1152]{1,0:T(8,128)(2,1)S(1)} collective-permute-done((bf16[16,1152]{1,0:T(8,128)(2,1)S(1)}, bf16[16,1152]{1,0:T(8,128)(2,1)S(1)}, u32[]{:S(2)}, u32[]{:S(2)}) %collective-permute-start.12) | collective-permute-done | bytes 36896 | tf_op jit(solution)/shard_map/ppermute | solution.py:51
  21.4 0.2 shard_map.53
  21.7 0.8 %shard_map.54 = (f32[16,1152]{1,0:T(8,128)}, f32[16,1152]{1,0:T(8,128)}) custom-call(f32[16,1152]{1,0:T(8,128)S(1)} %get-tuple-element.23.grad_ref, f32[16,1152]{1,0:T(8,128)S(1)} %get-tuple-element.24.unit_ref, f32[16,1]{1,0:T(8,128)S(1)} %get-tuple-element.25.inverse_ref, f32[16,1152]{1,0:T(8,128)S(1)} %get-tuple-element.26.rest_ref, ...), custom_call_target="tpu_custom_call" | custom-call | tf_op jit(solution)/shard_map/pallas_call | solution.py:69
  (15 shorter events, 0.2 us)
Async XLA Ops:
  0.6 1.4 %copy-start.1 = (bf16[16,1152]{1,0:T(8,128)(2,1)S(1)}, bf16[16,1152]{1,0:T(8,128)(2,1)}, u32[]{:S(2)}) copy-start(bf16[16,1152]{1,0:T(8,128)(2,1)} %param.3) | copy-start | bytes 110596
  0.6 1.6 %collective-permute-start.2 = (bf16[16,1152]{1,0:T(8,128)(2,1)}, bf16[16,1152]{1,0:T(8,128)(2,1)S(1)}, u32[]{:S(2)}, u32[]{:S(2)}) collective-permute-start(bf16[16,1152]{1,0:T(8,128)(2,1)} %param.3), channel_id=1, source_target_pairs={{0,4},{4,0},{8,12},{12,8},{16,20},{20,16},{24,28},{28,24},{1,5},{5... | collective-permute-start | bytes 110600 | tf_op jit(solution)/shard_map/ppermute | solution.py:37
  1.2 1.4 %collective-permute-start.1 = (bf16[16,1152]{1,0:T(8,128)(2,1)}, bf16[16,1152]{1,0:T(8,128)(2,1)S(1)}, u32[]{:S(2)}, u32[]{:S(2)}) collective-permute-start(bf16[16,1152]{1,0:T(8,128)(2,1)} %param.4), channel_id=1, source_target_pairs={{0,4},{4,0},{8,12},{12,8},{16,20},{20,16},{24,28},{28,24},{1,5},{5... | collective-permute-start | bytes 110600 | tf_op jit(solution)/shard_map/ppermute | solution.py:37
  2.7 9.0 %copy-start = (s32[64]{0:T(128)S(1)}, s32[64]{0:T(128)}, u32[]{:S(2)}) copy-start(s32[64]{0:T(128)} %param.5) | copy-start | bytes 772
  2.7 6.6 %collective-permute-start.4 = (bf16[32,1152]{1,0:T(8,128)(2,1)S(1)}, bf16[32,1152]{1,0:T(8,128)(2,1)S(1)}, u32[]{:S(2)}, u32[]{:S(2)}) collective-permute-start(bf16[32,1152]{1,0:T(8,128)(2,1)S(1)} %get-tuple-element.15.refs_0_), channel_id=1, source_target_pairs={{0,16},{1,17},{2,18},{3,19},{4,6},{5,7},{6,4},{7,5},{8,24},{9,25},... | collective-permute-start | bytes 221192 | tf_op jit(solution)/shard_map/ppermute | solution.py:51
  5.5 5.3 %collective-permute-start.3 = (bf16[32,1152]{1,0:T(8,128)(2,1)S(1)}, bf16[32,1152]{1,0:T(8,128)(2,1)S(1)}, u32[]{:S(2)}, u32[]{:S(2)}) collective-permute-start(bf16[32,1152]{1,0:T(8,128)(2,1)S(1)} %get-tuple-element.15.refs_0_), channel_id=1, source_target_pairs={{0,24},{1,25},{2,26},{3,27},{4,7},{5,6},{6,5},{7,4},{8,16},{9,17},... | collective-permute-start | bytes 221192 | tf_op jit(solution)/shard_map/ppermute | solution.py:51
  6.9 5.9 %collective-permute-start.8 = (bf16[32,1152]{1,0:T(8,128)(2,1)S(1)}, bf16[32,1152]{1,0:T(8,128)(2,1)S(1)}, u32[]{:S(2)}, u32[]{:S(2)}) collective-permute-start(bf16[32,1152]{1,0:T(8,128)(2,1)S(1)} %get-tuple-element.15.refs_0_), channel_id=1, source_target_pairs={{0,12},{1,13},{2,14},{3,15},{4,1},{5,0},{6,3},{7,2},{8,4},{9,5},{1... | collective-permute-start | bytes 221192 | tf_op jit(solution)/shard_map/ppermute | solution.py:51
  8.8 4.4 %collective-permute-start.5 = (bf16[32,1152]{1,0:T(8,128)(2,1)S(1)}, bf16[32,1152]{1,0:T(8,128)(2,1)S(1)}, u32[]{:S(2)}, u32[]{:S(2)}) collective-permute-start(bf16[32,1152]{1,0:T(8,128)(2,1)S(1)} %get-tuple-element.15.refs_0_), channel_id=1, source_target_pairs={{0,8},{1,9},{2,10},{3,11},{4,5},{5,4},{6,7},{7,6},{8,0},{9,1},{10,... | collective-permute-start | bytes 221192 | tf_op jit(solution)/shard_map/ppermute | solution.py:51
  9.3 3.8 %collective-permute-start.7 = (bf16[32,1152]{1,0:T(8,128)(2,1)S(1)}, bf16[32,1152]{1,0:T(8,128)(2,1)S(1)}, u32[]{:S(2)}, u32[]{:S(2)}) collective-permute-start(bf16[32,1152]{1,0:T(8,128)(2,1)S(1)} %collective-permute-done.4.refs_2_), channel_id=1, source_target_pairs={{0,4},{4,0},{8,12},{12,8},{16,20},{20,16},{24,28},{28,24},{1,5},{5... | collective-permute-start | bytes 221192 | tf_op jit(solution)/shard_map/ppermute | solution.py:37
  10.7 2.4 %collective-permute-start.6 = (bf16[32,1152]{1,0:T(8,128)(2,1)S(1)}, bf16[32,1152]{1,0:T(8,128)(2,1)S(1)}, u32[]{:S(2)}, u32[]{:S(2)}) collective-permute-start(bf16[32,1152]{1,0:T(8,128)(2,1)S(1)} %collective-permute-done.3.refs_1_), channel_id=1, source_target_pairs={{0,4},{4,0},{8,12},{12,8},{16,20},{20,16},{24,28},{28,24},{1,5},{5... | collective-permute-start | bytes 221192 | tf_op jit(solution)/shard_map/ppermute | solution.py:37
  11.7 1.1 %collective-permute-start = (s32[1,64]{1,0:T(1,128)S(1)}, s32[1,64]{1,0:T(1,128)S(1)}, u32[]{:S(2)}, u32[]{:S(2)}) collective-permute-start(s32[1,64]{1,0:T(1,128)S(1)} %bitcast.1), channel_id=1, source_target_pairs={{0,4},{4,0},{8,12},{12,8},{16,20},{20,16},{24,28},{28,24},{1,5},{5... | collective-permute-start | bytes 776 | tf_op jit(solution)/shard_map/ppermute | solution.py:37
  13.7 5.3 %collective-permute-start.9 = (bf16[32,1152]{1,0:T(8,128)(2,1)S(1)}, bf16[32,1152]{1,0:T(8,128)(2,1)S(1)}, u32[]{:S(2)}, u32[]{:S(2)}) collective-permute-start(bf16[32,1152]{1,0:T(8,128)(2,1)S(1)} %get-tuple-element.18), channel_id=1, source_target_pairs={{0,24},{1,25},{2,26},{3,27},{4,6},{5,7},{6,4},{7,5},{8,16},{9,17},... | collective-permute-start | bytes 221192 | tf_op jit(solution)/shard_map/ppermute | solution.py:51
  15.9 4.4 %collective-permute-start.10 = (bf16[32,1152]{1,0:T(8,128)(2,1)S(1)}, bf16[32,1152]{1,0:T(8,128)(2,1)S(1)}, u32[]{:S(2)}, u32[]{:S(2)}) collective-permute-start(bf16[32,1152]{1,0:T(8,128)(2,1)S(1)} %get-tuple-element.19), channel_id=1, source_target_pairs={{0,16},{1,17},{2,18},{3,19},{4,7},{5,6},{6,5},{7,4},{8,24},{9,25},... | collective-permute-start | bytes 221192 | tf_op jit(solution)/shard_map/ppermute | solution.py:51
  16.4 4.1 %collective-permute-start.11 = (bf16[16,1152]{1,0:T(8,128)(2,1)S(1)}, bf16[16,1152]{1,0:T(8,128)(2,1)S(1)}, u32[]{:S(2)}, u32[]{:S(2)}) collective-permute-start(bf16[16,1152]{1,0:T(8,128)(2,1)S(1)} %get-tuple-element.21), channel_id=1, source_target_pairs={{0,12},{1,13},{2,14},{3,15},{4,1},{5,0},{6,3},{7,2},{8,4},{9,5},{1... | collective-permute-start | bytes 110600 | tf_op jit(solution)/shard_map/ppermute | solution.py:51
  17.5 4.0 %collective-permute-start.12 = (bf16[16,1152]{1,0:T(8,128)(2,1)S(1)}, bf16[16,1152]{1,0:T(8,128)(2,1)S(1)}, u32[]{:S(2)}, u32[]{:S(2)}) collective-permute-start(bf16[16,1152]{1,0:T(8,128)(2,1)S(1)} %get-tuple-element.22), channel_id=1, source_target_pairs={{0,8},{1,9},{2,10},{3,11},{4,5},{5,4},{6,7},{7,6},{8,0},{9,1},{10,... | collective-permute-start | bytes 110600 | tf_op jit(solution)/shard_map/ppermute | solution.py:51
  20.3 1.4 %collective-permute-start.13 = (bf16[16,1152]{1,0:T(8,128)(2,1)S(1)}, bf16[16,1152]{1,0:T(8,128)(2,1)S(1)}, u32[]{:S(2)}, u32[]{:S(2)}) collective-permute-start(bf16[16,1152]{1,0:T(8,128)(2,1)S(1)} %get-tuple-element.27), channel_id=1, source_target_pairs={{0,4},{4,0},{8,12},{12,8},{16,20},{20,16},{24,28},{28,24},{1,5},{5... | collective-permute-start | bytes 110600 | tf_op jit(solution)/shard_map/ppermute | solution.py:37

commit v29 on v20

--- a/solution.py
+++ b/solution.py
@@ -37,12 +37,12 @@
     return lax.ppermute(block, "img", [(i, i ^ 1) for i in range(size)])
 
 
-def chip_swap(block, distance, cross=lambda txt: 0):
+def chip_swap(block, distance, cross=lambda img, txt: 0):
     n_img, n_txt = lax.axis_size("img"), lax.axis_size("txt")
     pairs = []
     for img in range(n_img):
         for txt in range(n_txt):
-            other = cross(txt)
+            other = cross(img, txt)
             if img % 2 == 0 and distance < n_img // 2:
                 pairs.append((img * n_txt + txt, (img ^ (2 * distance) ^ other) * n_txt + txt))
             if img % 2 == 1 and distance < n_txt:
@@ -50,8 +50,12 @@
     return lax.ppermute(block, ("img", "txt"), pairs)
 
 
-def cross_first(distance):
-    return (lax.axis_index("txt") % 2 == 0) | (distance % 2 == 1)
+def cross_first(img, txt, distance):
+    return (txt + img % 2 * distance) % 2 == 0
+
+
+def gets_cross_first():
+    return lax.axis_index("txt") % 2 == 0
 
 
 def is_even():
@@ -133,7 +137,8 @@
         ref[...] = part[k * height:(k + 1) * height].astype(bf16)
     block = part[split * height:(split + 1) * height].astype(bf16)
     even = is_even()
-    first = jnp.logical_xor(even, cross_first(blocks - split))
+    crosses = cross_first(lax.axis_index("img"), lax.axis_index("txt"), blocks - split)
+    first = jnp.logical_xor(even, crosses)
     first_ref[...] = jnp.where(first, block[:rows], block[rows:])
     second_ref[...] = jnp.where(first, block[rows:], block[:rows])
 
@@ -155,12 +160,12 @@
 
 
 def out_kernel(
-    far, unit_ref, inverse_ref, first_ref, keep_ref, second_ref, got_ref, img_ref, txt_ref
+    unit_ref, inverse_ref, first_ref, keep_ref, second_ref, got_ref, img_ref, txt_ref
 ):
     rows = keep_ref.shape[0]
     even = is_even()
     first, second = first_ref[...], second_ref[...].astype(f32)
-    cross = cross_first(far)
+    cross = gets_cross_first()
     keep = keep_ref[...] + jnp.where(cross, second, first)
     got = got_ref[...].astype(f32) + jnp.where(cross, first, second)
     unit, inverse = unit_ref[...], inverse_ref[...]
@@ -182,7 +187,7 @@
     mine, other = call(sides_kernel, [pair] * 2, [near, far_txt, far_img])
     order = list(range(blocks - 1, 0, -1))
     mine = [mine] + [chip_swap(mine, k) for k in order]
-    other = [other, *[core_swap(block) for block in mine[1:-1]], chip_swap(mine[0], 1, lambda txt: 1)]
+    other = [other, *[core_swap(block) for block in mine[1:-1]], chip_swap(mine[0], 1, lambda img, txt: 1)]
     split = blocks - 1
     own, first, second, *send = call(
         functools.partial(pair_kernel, blocks, split),
@@ -191,14 +196,13 @@
     )
     far = order.pop(split - 1)
     got = [chip_swap(block, k) for k, block in zip(order, send)]
-    first = chip_swap(first, far, lambda txt: int(txt % 2 == 0 or far % 2 == 1))
-    second = chip_swap(second, far, lambda txt: int(txt % 2 == 1 and far % 2 == 0))
+    first = chip_swap(first, far, lambda img, txt: int(cross_first(img, txt, far)))
+    second = chip_swap(second, far, lambda img, txt: int(not cross_first(img, txt, far)))
     keep, send = call(sum_kernel, [single, piece], [own, *got])
     got = core_swap(send)
     column = jax.ShapeDtypeStruct((2 * rows, 1), f32)
     ready = call(unit_kernel, [total, column, single], [near, first], cost=LONG)
-    kernel = functools.partial(out_kernel, far)
-    return tuple(call(kernel, [single] * 2, [*ready, keep, second, got]))
+    return tuple(call(out_kernel, [single] * 2, [*ready, keep, second, got]))
 
 
 def solution(mesh):

time: 22.5 us -> 22.5 us (level)
  no operation moved by 1% of the time
where the time goes in v29:
time: 22.5 us; the launch traced here: 22.4 us
  starting transfers between devices  12.7 us (56%)
  waiting for transfers between devices  6.56 us (29%)
  Pallas kernels  1.58 us (7%)
  local copies, waits for them, and re-layouts  0.79 us (4%)
  between operations  0.68 us (3%)
    ppermute x8, starting transfers between devices, chip_swap(): return lax.ppermute(block, ('img', 'txt'), pairs)  10.8 us
    ppermute x8, waiting for transfers between devices, chip_swap(): return lax.ppermute(block, ('img', 'txt'), pairs)  4.67 us
    ppermute x6, starting transfers between devices, core_swap(): return lax.ppermute(block, 'img', [(i, i ^ 1) for i in range(size)])  1.89 us
    ppermute x6, waiting for transfers between devices, core_swap(): return lax.ppermute(block, 'img', [(i, i ^ 1) for i in range(size)])  1.89 us
    pallas_call x5, Pallas kernels, call(): pl.pallas_call(kernel, out_shape=outs, in_specs=[VMEM] * len(args), out_s...  1.58 us
    unnamed x5, local copies, waits for them, and re-layouts  0.78 us
  transfers between devices with their start and end apart: 14, of which 9 were waited for; matrix products, arithmetic and copies ran while one was open for 3% of the time, Pallas kernels for 1%

profile of v29, /device:TPU:0, one launch (start us, length us, event | category | flops | bytes accessed | tf_op | source)
XLA Modules:
  0.0 22.4 jit_solution(14441618215776165598)
XLA Ops:
  0.6 0.5 %collective-permute-start.2 = (bf16[16,1152]{1,0:T(8,128)(2,1)}, bf16[16,1152]{1,0:T(8,128)(2,1)S(1)}, u32[]{:S(2)}, u32[]{:S(2)}) collective-permute-start(bf16[16,1152]{1,0:T(8,128)(2,1)} %param.3), channel_id=1, source_target_pairs={{0,4},{4,0},{8,12},{12,8},{16,20},{20,16},{24,28},{28,24},{1,5},{5... | collective-permute-start | bytes 110600 | tf_op jit(solution)/shard_map/ppermute | solution.py:37
  1.2 0.8 %constant_dynamic-update-slice_fusion.1 = bf16[32,1152]{1,0:T(8,128)(2,1)S(1)} fusion(bf16[16,1152]{1,0:T(8,128)(2,1)} %param.4), kind=kLoop, calls=%fused_computation.1 | loop fusion | bytes 73728
  2.0 0.2 collective-permute-done.2.img_ref
  2.2 0.3 %collective-permute-done.1.txt_ref = bf16[16,1152]{1,0:T(8,128)(2,1)S(1)} collective-permute-done((bf16[16,1152]{1,0:T(8,128)(2,1)}, bf16[16,1152]{1,0:T(8,128)(2,1)S(1)}, u32[]{:S(2)}, u32[]{:S(2)}) %collective-permute-start.1) | collective-permute-done | bytes 36896 | tf_op jit(solution)/shard_map/ppermute | solution.py:37
  2.6 0.1 shard_map.50
  2.7 2.7 %collective-permute-start.4 = (bf16[32,1152]{1,0:T(8,128)(2,1)S(1)}, bf16[32,1152]{1,0:T(8,128)(2,1)S(1)}, u32[]{:S(2)}, u32[]{:S(2)}) collective-permute-start(bf16[32,1152]{1,0:T(8,128)(2,1)S(1)} %get-tuple-element.14.refs_0_), channel_id=1, source_target_pairs={{0,16},{1,17},{2,18},{3,19},{4,6},{5,7},{6,4},{7,5},{8,24},{9,25},... | collective-permute-start | bytes 221192 | tf_op jit(solution)/shard_map/ppermute | solution.py:50
  5.5 1.4 %collective-permute-start.3 = (bf16[32,1152]{1,0:T(8,128)(2,1)S(1)}, bf16[32,1152]{1,0:T(8,128)(2,1)S(1)}, u32[]{:S(2)}, u32[]{:S(2)}) collective-permute-start(bf16[32,1152]{1,0:T(8,128)(2,1)S(1)} %get-tuple-element.14.refs_0_), channel_id=1, source_target_pairs={{0,24},{1,25},{2,26},{3,27},{4,7},{5,6},{6,5},{7,4},{8,16},{9,17},... | collective-permute-start | bytes 221192 | tf_op jit(solution)/shard_map/ppermute | solution.py:50
  6.9 1.9 %collective-permute-start.8 = (bf16[32,1152]{1,0:T(8,128)(2,1)S(1)}, bf16[32,1152]{1,0:T(8,128)(2,1)S(1)}, u32[]{:S(2)}, u32[]{:S(2)}) collective-permute-start(bf16[32,1152]{1,0:T(8,128)(2,1)S(1)} %get-tuple-element.14.refs_0_), channel_id=1, source_target_pairs={{0,12},{1,13},{2,14},{3,15},{4,1},{5,0},{6,3},{7,2},{8,4},{9,5},{1... | collective-permute-start | bytes 221192 | tf_op jit(solution)/shard_map/ppermute | solution.py:50
  8.8 0.5 %collective-permute-start.5 = (bf16[32,1152]{1,0:T(8,128)(2,1)S(1)}, bf16[32,1152]{1,0:T(8,128)(2,1)S(1)}, u32[]{:S(2)}, u32[]{:S(2)}) collective-permute-start(bf16[32,1152]{1,0:T(8,128)(2,1)S(1)} %get-tuple-element.14.refs_0_), channel_id=1, source_target_pairs={{0,8},{1,9},{2,10},{3,11},{4,5},{5,4},{6,7},{7,6},{8,0},{9,1},{10,... | collective-permute-start | bytes 221192 | tf_op jit(solution)/shard_map/ppermute | solution.py:50
  9.3 1.4 %collective-permute-done.3.refs_1_ = bf16[32,1152]{1,0:T(8,128)(2,1)S(1)} collective-permute-done((bf16[32,1152]{1,0:T(8,128)(2,1)S(1)}, bf16[32,1152]{1,0:T(8,128)(2,1)S(1)}, u32[]{:S(2)}, u32[]{:S(2)}) %collective-permute-start.3) | collective-permute-done | bytes 73760 | tf_op jit(solution)/shard_map/ppermute | solution.py:50
  10.7 1.0 %collective-permute-start.6 = (bf16[32,1152]{1,0:T(8,128)(2,1)S(1)}, bf16[32,1152]{1,0:T(8,128)(2,1)S(1)}, u32[]{:S(2)}, u32[]{:S(2)}) collective-permute-start(bf16[32,1152]{1,0:T(8,128)(2,1)S(1)} %collective-permute-done.3.refs_1_), channel_id=1, source_target_pairs={{0,4},{4,0},{8,12},{12,8},{16,20},{20,16},{24,28},{28,24},{1,5},{5... | collective-permute-start | bytes 221192 | tf_op jit(solution)/shard_map/ppermute | solution.py:37
  11.7 1.1 %collective-permute-done.far_ids_ref = s32[1,64]{1,0:T(1,128)S(1)} collective-permute-done((s32[1,64]{1,0:T(1,128)S(1)}, s32[1,64]{1,0:T(1,128)S(1)}, u32[]{:S(2)}, u32[]{:S(2)}) %collective-permute-start) | collective-permute-done | bytes 288 | tf_op jit(solution)/shard_map/ppermute | solution.py:37
  12.8 0.3 %collective-permute-done.5.refs_3_ = bf16[32,1152]{1,0:T(8,128)(2,1)S(1)} collective-permute-done((bf16[32,1152]{1,0:T(8,128)(2,1)S(1)}, bf16[32,1152]{1,0:T(8,128)(2,1)S(1)}, u32[]{:S(2)}, u32[]{:S(2)}) %collective-permute-start.5) | collective-permute-done | bytes 73760 | tf_op jit(solution)/shard_map/ppermute | solution.py:50
  13.2 0.5 %shard_map.51 = (f32[32,1152]{1,0:T(8,128)S(1)}, bf16[16,1152]{1,0:T(8,128)(2,1)S(1)}, bf16[16,1152]{1,0:T(8,128)(2,1)S(1)}, bf16[32,1152]{1,0:T(8,128)(2,1)S(1)}, bf16[32,1152]{1,0:T(8,128)(2,1)S(1)}) custom-call(s32[1,64]{1,0:T(1,128)S(1)} %bitcast.2, s32[1,64]{1,0:T(1,128)S(1)} %collective-permute-done.far_ids_ref, ...), custom_call_target="tpu_custom_call" | custom-call | tf_op jit(solution)/shard_map/pallas_call | solution.py:67
  13.7 2.2 %collective-permute-start.10 = (bf16[32,1152]{1,0:T(8,128)(2,1)S(1)}, bf16[32,1152]{1,0:T(8,128)(2,1)S(1)}, u32[]{:S(2)}, u32[]{:S(2)}) collective-permute-start(bf16[32,1152]{1,0:T(8,128)(2,1)S(1)} %get-tuple-element.21), channel_id=1, source_target_pairs={{0,24},{1,25},{2,26},{3,27},{4,7},{5,6},{6,5},{7,4},{8,16},{9,17},... | collective-permute-start | bytes 221192 | tf_op jit(solution)/shard_map/ppermute | solution.py:50
  15.9 0.5 %collective-permute-start.11 = (bf16[32,1152]{1,0:T(8,128)(2,1)S(1)}, bf16[32,1152]{1,0:T(8,128)(2,1)S(1)}, u32[]{:S(2)}, u32[]{:S(2)}) collective-permute-start(bf16[32,1152]{1,0:T(8,128)(2,1)S(1)} %get-tuple-element.22), channel_id=1, source_target_pairs={{0,16},{1,17},{2,18},{3,19},{4,6},{5,7},{6,4},{7,5},{8,24},{9,25},... | collective-permute-start | bytes 221192 | tf_op jit(solution)/shard_map/ppermute | solution.py:50
  16.4 1.0 %collective-permute-start.9 = (bf16[16,1152]{1,0:T(8,128)(2,1)S(1)}, bf16[16,1152]{1,0:T(8,128)(2,1)S(1)}, u32[]{:S(2)}, u32[]{:S(2)}) collective-permute-start(bf16[16,1152]{1,0:T(8,128)(2,1)S(1)} %get-tuple-element.16), channel_id=1, source_target_pairs={{0,12},{1,9},{2,14},{3,11},{4,5},{5,0},{6,7},{7,2},{8,4},{9,1},{10... | collective-permute-start | bytes 110600 | tf_op jit(solution)/shard_map/ppermute | solution.py:50
  17.4 0.5 %collective-permute-start.12 = (bf16[16,1152]{1,0:T(8,128)(2,1)S(1)}, bf16[16,1152]{1,0:T(8,128)(2,1)S(1)}, u32[]{:S(2)}, u32[]{:S(2)}) collective-permute-start(bf16[16,1152]{1,0:T(8,128)(2,1)S(1)} %get-tuple-element.24), channel_id=1, source_target_pairs={{0,8},{1,13},{2,10},{3,15},{4,1},{5,4},{6,3},{7,6},{8,0},{9,5},{10... | collective-permute-start | bytes 110600 | tf_op jit(solution)/shard_map/ppermute | solution.py:50
  17.9 1.1 %collective-permute-done.10.refs_0_ = bf16[32,1152]{1,0:T(8,128)(2,1)S(1)} collective-permute-done((bf16[32,1152]{1,0:T(8,128)(2,1)S(1)}, bf16[32,1152]{1,0:T(8,128)(2,1)S(1)}, u32[]{:S(2)}, u32[]{:S(2)}) %collective-permute-start.10) | collective-permute-done | bytes 73760 | tf_op jit(solution)/shard_map/ppermute | solution.py:50
  19.0 1.2 %collective-permute-done.11.refs_1_ = bf16[32,1152]{1,0:T(8,128)(2,1)S(1)} collective-permute-done((bf16[32,1152]{1,0:T(8,128)(2,1)S(1)}, bf16[32,1152]{1,0:T(8,128)(2,1)S(1)}, u32[]{:S(2)}, u32[]{:S(2)}) %collective-permute-start.11) | collective-permute-done | bytes 73760 | tf_op jit(solution)/shard_map/ppermute | solution.py:50
  20.3 0.3 %collective-permute-start.13 = (bf16[16,1152]{1,0:T(8,128)(2,1)S(1)}, bf16[16,1152]{1,0:T(8,128)(2,1)S(1)}, u32[]{:S(2)}, u32[]{:S(2)}) collective-permute-start(bf16[16,1152]{1,0:T(8,128)(2,1)S(1)} %get-tuple-element.25), channel_id=1, source_target_pairs={{0,4},{4,0},{8,12},{12,8},{16,20},{20,16},{24,28},{28,24},{1,5},{5... | collective-permute-start | bytes 110600 | tf_op jit(solution)/shard_map/ppermute | solution.py:37
  20.7 0.6 %collective-permute-done.12.second_ref = bf16[16,1152]{1,0:T(8,128)(2,1)S(1)} collective-permute-done((bf16[16,1152]{1,0:T(8,128)(2,1)S(1)}, bf16[16,1152]{1,0:T(8,128)(2,1)S(1)}, u32[]{:S(2)}, u32[]{:S(2)}) %collective-permute-start.12) | collective-permute-done | bytes 36896 | tf_op jit(solution)/shard_map/ppermute | solution.py:50
  21.4 0.2 collective-permute-done.13.got_ref
  21.6 0.8 %shard_map.54 = (f32[16,1152]{1,0:T(8,128)}, f32[16,1152]{1,0:T(8,128)}) custom-call(f32[32,1152]{1,0:T(8,128)S(1)} %get-tuple-element.17.unit_ref, f32[32,1]{1,0:T(8,128)S(1)} %get-tuple-element.18.inverse_ref, f32[16,1152]{1,0:T(8,128)S(1)} %get-tuple-element.19.first_ref, f32[16,1152]{1,0:T(8,128)S(1)} %get-tuple-element.23.keep_ref, ...), custom_call_target="tpu_custom_call" | custom-call | tf_op jit(solution)/shard_map/pallas_call | solution.py:67
  (15 shorter events, 0.3 us)
Async XLA Ops:
  0.6 1.4 %copy-start.1 = (bf16[16,1152]{1,0:T(8,128)(2,1)S(1)}, bf16[16,1152]{1,0:T(8,128)(2,1)}, u32[]{:S(2)}) copy-start(bf16[16,1152]{1,0:T(8,128)(2,1)} %param.3) | copy-start | bytes 110596
  0.6 1.6 %collective-permute-start.2 = (bf16[16,1152]{1,0:T(8,128)(2,1)}, bf16[16,1152]{1,0:T(8,128)(2,1)S(1)}, u32[]{:S(2)}, u32[]{:S(2)}) collective-permute-start(bf16[16,1152]{1,0:T(8,128)(2,1)} %param.3), channel_id=1, source_target_pairs={{0,4},{4,0},{8,12},{12,8},{16,20},{20,16},{24,28},{28,24},{1,5},{5... | collective-permute-start | bytes 110600 | tf_op jit(solution)/shard_map/ppermute | solution.py:37
  1.2 1.4 %collective-permute-start.1 = (bf16[16,1152]{1,0:T(8,128)(2,1)}, bf16[16,1152]{1,0:T(8,128)(2,1)S(1)}, u32[]{:S(2)}, u32[]{:S(2)}) collective-permute-start(bf16[16,1152]{1,0:T(8,128)(2,1)} %param.4), channel_id=1, source_target_pairs={{0,4},{4,0},{8,12},{12,8},{16,20},{20,16},{24,28},{28,24},{1,5},{5... | collective-permute-start | bytes 110600 | tf_op jit(solution)/shard_map/ppermute | solution.py:37
  2.7 9.0 %copy-start = (s32[64]{0:T(128)S(1)}, s32[64]{0:T(128)}, u32[]{:S(2)}) copy-start(s32[64]{0:T(128)} %param.5) | copy-start | bytes 772
  2.7 6.6 %collective-permute-start.4 = (bf16[32,1152]{1,0:T(8,128)(2,1)S(1)}, bf16[32,1152]{1,0:T(8,128)(2,1)S(1)}, u32[]{:S(2)}, u32[]{:S(2)}) collective-permute-start(bf16[32,1152]{1,0:T(8,128)(2,1)S(1)} %get-tuple-element.14.refs_0_), channel_id=1, source_target_pairs={{0,16},{1,17},{2,18},{3,19},{4,6},{5,7},{6,4},{7,5},{8,24},{9,25},... | collective-permute-start | bytes 221192 | tf_op jit(solution)/shard_map/ppermute | solution.py:50
  5.5 5.3 %collective-permute-start.3 = (bf16[32,1152]{1,0:T(8,128)(2,1)S(1)}, bf16[32,1152]{1,0:T(8,128)(2,1)S(1)}, u32[]{:S(2)}, u32[]{:S(2)}) collective-permute-start(bf16[32,1152]{1,0:T(8,128)(2,1)S(1)} %get-tuple-element.14.refs_0_), channel_id=1, source_target_pairs={{0,24},{1,25},{2,26},{3,27},{4,7},{5,6},{6,5},{7,4},{8,16},{9,17},... | collective-permute-start | bytes 221192 | tf_op jit(solution)/shard_map/ppermute | solution.py:50
  6.9 5.9 %collective-permute-start.8 = (bf16[32,1152]{1,0:T(8,128)(2,1)S(1)}, bf16[32,1152]{1,0:T(8,128)(2,1)S(1)}, u32[]{:S(2)}, u32[]{:S(2)}) collective-permute-start(bf16[32,1152]{1,0:T(8,128)(2,1)S(1)} %get-tuple-element.14.refs_0_), channel_id=1, source_target_pairs={{0,12},{1,13},{2,14},{3,15},{4,1},{5,0},{6,3},{7,2},{8,4},{9,5},{1... | collective-permute-start | bytes 221192 | tf_op jit(solution)/shard_map/ppermute | solution.py:50
  8.8 4.4 %collective-permute-start.5 = (bf16[32,1152]{1,0:T(8,128)(2,1)S(1)}, bf16[32,1152]{1,0:T(8,128)(2,1)S(1)}, u32[]{:S(2)}, u32[]{:S(2)}) collective-permute-start(bf16[32,1152]{1,0:T(8,128)(2,1)S(1)} %get-tuple-element.14.refs_0_), channel_id=1, source_target_pairs={{0,8},{1,9},{2,10},{3,11},{4,5},{5,4},{6,7},{7,6},{8,0},{9,1},{10,... | collective-permute-start | bytes 221192 | tf_op jit(solution)/shard_map/ppermute | solution.py:50
  9.3 3.8 %collective-permute-start.7 = (bf16[32,1152]{1,0:T(8,128)(2,1)S(1)}, bf16[32,1152]{1,0:T(8,128)(2,1)S(1)}, u32[]{:S(2)}, u32[]{:S(2)}) collective-permute-start(bf16[32,1152]{1,0:T(8,128)(2,1)S(1)} %collective-permute-done.4.refs_2_), channel_id=1, source_target_pairs={{0,4},{4,0},{8,12},{12,8},{16,20},{20,16},{24,28},{28,24},{1,5},{5... | collective-permute-start | bytes 221192 | tf_op jit(solution)/shard_map/ppermute | solution.py:37
  10.7 2.4 %collective-permute-start.6 = (bf16[32,1152]{1,0:T(8,128)(2,1)S(1)}, bf16[32,1152]{1,0:T(8,128)(2,1)S(1)}, u32[]{:S(2)}, u32[]{:S(2)}) collective-permute-start(bf16[32,1152]{1,0:T(8,128)(2,1)S(1)} %collective-permute-done.3.refs_1_), channel_id=1, source_target_pairs={{0,4},{4,0},{8,12},{12,8},{16,20},{20,16},{24,28},{28,24},{1,5},{5... | collective-permute-start | bytes 221192 | tf_op jit(solution)/shard_map/ppermute | solution.py:37
  11.7 1.1 %collective-permute-start = (s32[1,64]{1,0:T(1,128)S(1)}, s32[1,64]{1,0:T(1,128)S(1)}, u32[]{:S(2)}, u32[]{:S(2)}) collective-permute-start(s32[1,64]{1,0:T(1,128)S(1)} %bitcast.1), channel_id=1, source_target_pairs={{0,4},{4,0},{8,12},{12,8},{16,20},{20,16},{24,28},{28,24},{1,5},{5... | collective-permute-start | bytes 776 | tf_op jit(solution)/shard_map/ppermute | solution.py:37
  13.7 5.3 %collective-permute-start.10 = (bf16[32,1152]{1,0:T(8,128)(2,1)S(1)}, bf16[32,1152]{1,0:T(8,128)(2,1)S(1)}, u32[]{:S(2)}, u32[]{:S(2)}) collective-permute-start(bf16[32,1152]{1,0:T(8,128)(2,1)S(1)} %get-tuple-element.21), channel_id=1, source_target_pairs={{0,24},{1,25},{2,26},{3,27},{4,7},{5,6},{6,5},{7,4},{8,16},{9,17},... | collective-permute-start | bytes 221192 | tf_op jit(solution)/shard_map/ppermute | solution.py:50
  15.9 4.4 %collective-permute-start.11 = (bf16[32,1152]{1,0:T(8,128)(2,1)S(1)}, bf16[32,1152]{1,0:T(8,128)(2,1)S(1)}, u32[]{:S(2)}, u32[]{:S(2)}) collective-permute-start(bf16[32,1152]{1,0:T(8,128)(2,1)S(1)} %get-tuple-element.22), channel_id=1, source_target_pairs={{0,16},{1,17},{2,18},{3,19},{4,6},{5,7},{6,4},{7,5},{8,24},{9,25},... | collective-permute-start | bytes 221192 | tf_op jit(solution)/shard_map/ppermute | solution.py:50
  16.4 4.2 %collective-permute-start.9 = (bf16[16,1152]{1,0:T(8,128)(2,1)S(1)}, bf16[16,1152]{1,0:T(8,128)(2,1)S(1)}, u32[]{:S(2)}, u32[]{:S(2)}) collective-permute-start(bf16[16,1152]{1,0:T(8,128)(2,1)S(1)} %get-tuple-element.16), channel_id=1, source_target_pairs={{0,12},{1,9},{2,14},{3,11},{4,5},{5,0},{6,7},{7,2},{8,4},{9,1},{10... | collective-permute-start | bytes 110600 | tf_op jit(solution)/shard_map/ppermute | solution.py:50
  17.4 4.0 %collective-permute-start.12 = (bf16[16,1152]{1,0:T(8,128)(2,1)S(1)}, bf16[16,1152]{1,0:T(8,128)(2,1)S(1)}, u32[]{:S(2)}, u32[]{:S(2)}) collective-permute-start(bf16[16,1152]{1,0:T(8,128)(2,1)S(1)} %get-tuple-element.24), channel_id=1, source_target_pairs={{0,8},{1,13},{2,10},{3,15},{4,1},{5,4},{6,3},{7,6},{8,0},{9,5},{10... | collective-permute-start | bytes 110600 | tf_op jit(solution)/shard_map/ppermute | solution.py:50
  20.3 1.3 %collective-permute-start.13 = (bf16[16,1152]{1,0:T(8,128)(2,1)S(1)}, bf16[16,1152]{1,0:T(8,128)(2,1)S(1)}, u32[]{:S(2)}, u32[]{:S(2)}) collective-permute-start(bf16[16,1152]{1,0:T(8,128)(2,1)S(1)} %get-tuple-element.25), channel_id=1, source_target_pairs={{0,4},{4,0},{8,12},{12,8},{16,20},{20,16},{24,28},{28,24},{1,5},{5... | collective-permute-start | bytes 110600 | tf_op jit(solution)/shard_map/ppermute | solution.py:37

commit v30 on v29

--- a/solution.py
+++ b/solution.py
@@ -154,23 +154,44 @@
     send_ref[...] = jnp.where(even, total[rows:], total[:rows]).astype(bf16)
 
 
-def unit_kernel(raw_ref, first_ref, unit_ref, inverse_ref, rest_ref):
-    unit_ref[...], inverse_ref[...] = normalize(raw_ref[...])
-    rest_ref[...] = first_ref[...].astype(f32)
-
-
-def out_kernel(
-    unit_ref, inverse_ref, first_ref, keep_ref, second_ref, got_ref, img_ref, txt_ref
+def keep_kernel(
+    raw_ref, keep_ref, first_ref, second_ref, grad_ref, unit_ref, inverse_ref, rest_ref
 ):
     rows = keep_ref.shape[0]
     even = is_even()
-    first, second = first_ref[...], second_ref[...].astype(f32)
+    unit, inverse = normalize(raw_ref[...])
+    first, second = first_ref[...].astype(f32), second_ref[...].astype(f32)
     cross = gets_cross_first()
-    keep = keep_ref[...] + jnp.where(cross, second, first)
-    got = got_ref[...].astype(f32) + jnp.where(cross, first, second)
-    unit, inverse = unit_ref[...], inverse_ref[...]
-    txt_ref[...] = back_norm(unit[:rows], inverse[:rows], jnp.where(even, keep, got))
-    img_ref[...] = back_norm(unit[rows:], inverse[rows:], jnp.where(even, got, keep))
+    grad_ref[...] = back_norm(
+        jnp.where(even, unit[:rows], unit[rows:]),
+        jnp.where(even, inverse[:rows], inverse[rows:]),
+        keep_ref[...] + jnp.where(cross, second, first),
+    )
+    rest_ref[...] = jnp.where(cross, first, second)
+    unit_ref[...] = jnp.where(even, unit[rows:], unit[:rows])
+    inverse_ref[...] = jnp.where(even, inverse[rows:], inverse[:rows])
+
+
+def out_kernel(
+    grad_ref, unit_ref, inverse_ref, rest_ref, got_ref, img_ref, txt_ref, other_ref, sems
+):
+    def write(keep_out, got_out):
+        kept = pltpu.make_async_copy(grad_ref, keep_out, sems.at[0])
+        kept.start()
+        total = got_ref[...].astype(f32) + rest_ref[...]
+        other_ref[...] = back_norm(unit_ref[...], inverse_ref[...], total)
+        other = pltpu.make_async_copy(other_ref, got_out, sems.at[1])
+        other.start()
+        kept.wait()
+        other.wait()
+
+    @pl.when(is_even())
+    def _():
+        write(txt_ref, img_ref)
+
+    @pl.when(jnp.logical_not(is_even()))
+    def _():
+        write(img_ref, txt_ref)
 
 
 def local(image_embeds, text_embeds, pair_ids):
@@ -200,9 +221,18 @@
     second = chip_swap(second, far, lambda img, txt: int(not cross_first(img, txt, far)))
     keep, send = call(sum_kernel, [single, piece], [own, *got])
     got = core_swap(send)
-    column = jax.ShapeDtypeStruct((2 * rows, 1), f32)
-    ready = call(unit_kernel, [total, column, single], [near, first], cost=LONG)
-    return tuple(call(out_kernel, [single] * 2, [*ready, keep, second, got]))
+    column = jax.ShapeDtypeStruct((rows, 1), f32)
+    outs = [single, single, column, single]
+    kept = call(keep_kernel, outs, [near, keep, first, second], cost=LONG)
+    return tuple(
+        pl.pallas_call(
+            out_kernel,
+            out_shape=[single] * 2,
+            in_specs=[VMEM] * 5,
+            out_specs=[pl.BlockSpec(memory_space=pl.ANY)] * 2,
+            scratch_shapes=[pltpu.VMEM((rows, width), f32), pltpu.SemaphoreType.DMA((2,))],
+        )(*kept, got)
+    )
 
 
 def solution(mesh):

time: 22.5 us -> 26.6 us (1.18)
  local copies, waits for them, and re-layouts: 0.79 us -> 3.86 us
  Pallas kernels: 1.58 us -> 2.6 us
    unnamed x5 -> x15, local copies, waits for them, and re-layouts: 0.78 us -> 3.85 us
    pallas_call x0 -> x1, Pallas kernels: none -> 1.71 us  [local(): pl.pallas_call(out_kernel, out_shape=[single] * 2, in_specs=[VMEM] * 5, o...]
    pallas_call x5 -> x4, Pallas kernels: 1.58 us -> 0.9 us  [call(): pl.pallas_call(kernel, out_shape=outs, in_specs=[VMEM] * len(args), out_s...]
  transfers between devices with their start and end apart: 14 -> 14, of which waited for: 9 -> 8; matrix products, arithmetic and copies ran while one was open for 3% -> 3% of each run, Pallas kernels for 1% -> 1%
where the time goes in v30:
time: 26.6 us; the launch traced here: 26.4 us
  starting transfers between devices  12.7 us (48%)
  waiting for transfers between devices  6.47 us (24%)
  local copies, waits for them, and re-layouts  3.86 us (15%)
  Pallas kernels  2.6 us (10%)
  between operations  0.69 us (3%)
    ppermute x8, starting transfers between devices, chip_swap(): return lax.ppermute(block, ('img', 'txt'), pairs)  10.8 us
    ppermute x8, waiting for transfers between devices, chip_swap(): return lax.ppermute(block, ('img', 'txt'), pairs)  4.78 us
    unnamed x15, local copies, waits for them, and re-layouts  3.85 us
    ppermute x6, starting transfers between devices, core_swap(): return lax.ppermute(block, 'img', [(i, i ^ 1) for i in range(size)])  1.89 us
    pallas_call x1, Pallas kernels, local(): pl.pallas_call(out_kernel, out_shape=[single] * 2, in_specs=[VMEM] * 5, o...  1.71 us
    ppermute x6, waiting for transfers between devices, core_swap(): return lax.ppermute(block, 'img', [(i, i ^ 1) for i in range(size)])  1.69 us
    pallas_call x4, Pallas kernels, call(): pl.pallas_call(kernel, out_shape=outs, in_specs=[VMEM] * len(args), out_s...  0.9 us
  transfers between devices with their start and end apart: 14, of which 8 were waited for; matrix products, arithmetic and copies ran while one was open for 3% of the time, Pallas kernels for 1%

profile of v30, /device:TPU:0, one launch (start us, length us, event | category | flops | bytes accessed | tf_op | source)
XLA Modules:
  0.0 26.4 jit_solution(18066281416886502797)
XLA Ops:
  0.6 0.5 %collective-permute-start.2 = (bf16[16,1152]{1,0:T(8,128)(2,1)}, bf16[16,1152]{1,0:T(8,128)(2,1)S(1)}, u32[]{:S(2)}, u32[]{:S(2)}) collective-permute-start(bf16[16,1152]{1,0:T(8,128)(2,1)} %param.3), channel_id=1, source_target_pairs={{0,4},{4,0},{8,12},{12,8},{16,20},{20,16},{24,28},{28,24},{1,5},{5... | collective-permute-start | bytes 110600 | tf_op jit(solution)/shard_map/ppermute | solution.py:37
  1.2 0.8 %constant_dynamic-update-slice_fusion.1 = bf16[32,1152]{1,0:T(8,128)(2,1)S(1)} fusion(bf16[16,1152]{1,0:T(8,128)(2,1)} %param.4), kind=kLoop, calls=%fused_computation.1 | loop fusion | bytes 73728
  2.2 0.3 %collective-permute-done.1.txt_ref = bf16[16,1152]{1,0:T(8,128)(2,1)S(1)} collective-permute-done((bf16[16,1152]{1,0:T(8,128)(2,1)}, bf16[16,1152]{1,0:T(8,128)(2,1)S(1)}, u32[]{:S(2)}, u32[]{:S(2)}) %collective-permute-start.1) | collective-permute-done | bytes 36896 | tf_op jit(solution)/shard_map/ppermute | solution.py:37
  2.7 2.7 %collective-permute-start.4 = (bf16[32,1152]{1,0:T(8,128)(2,1)S(1)}, bf16[32,1152]{1,0:T(8,128)(2,1)S(1)}, u32[]{:S(2)}, u32[]{:S(2)}) collective-permute-start(bf16[32,1152]{1,0:T(8,128)(2,1)S(1)} %get-tuple-element.15.refs_0_), channel_id=1, source_target_pairs={{0,16},{1,17},{2,18},{3,19},{4,6},{5,7},{6,4},{7,5},{8,24},{9,25},... | collective-permute-start | bytes 221192 | tf_op jit(solution)/shard_map/ppermute | solution.py:50
  5.5 1.4 %collective-permute-start.3 = (bf16[32,1152]{1,0:T(8,128)(2,1)S(1)}, bf16[32,1152]{1,0:T(8,128)(2,1)S(1)}, u32[]{:S(2)}, u32[]{:S(2)}) collective-permute-start(bf16[32,1152]{1,0:T(8,128)(2,1)S(1)} %get-tuple-element.15.refs_0_), channel_id=1, source_target_pairs={{0,24},{1,25},{2,26},{3,27},{4,7},{5,6},{6,5},{7,4},{8,16},{9,17},... | collective-permute-start | bytes 221192 | tf_op jit(solution)/shard_map/ppermute | solution.py:50
  6.9 1.9 %collective-permute-start.8 = (bf16[32,1152]{1,0:T(8,128)(2,1)S(1)}, bf16[32,1152]{1,0:T(8,128)(2,1)S(1)}, u32[]{:S(2)}, u32[]{:S(2)}) collective-permute-start(bf16[32,1152]{1,0:T(8,128)(2,1)S(1)} %get-tuple-element.15.refs_0_), channel_id=1, source_target_pairs={{0,12},{1,13},{2,14},{3,15},{4,1},{5,0},{6,3},{7,2},{8,4},{9,5},{1... | collective-permute-start | bytes 221192 | tf_op jit(solution)/shard_map/ppermute | solution.py:50
  8.8 0.5 %collective-permute-start.5 = (bf16[32,1152]{1,0:T(8,128)(2,1)S(1)}, bf16[32,1152]{1,0:T(8,128)(2,1)S(1)}, u32[]{:S(2)}, u32[]{:S(2)}) collective-permute-start(bf16[32,1152]{1,0:T(8,128)(2,1)S(1)} %get-tuple-element.15.refs_0_), channel_id=1, source_target_pairs={{0,8},{1,9},{2,10},{3,11},{4,5},{5,4},{6,7},{7,6},{8,0},{9,1},{10,... | collective-permute-start | bytes 221192 | tf_op jit(solution)/shard_map/ppermute | solution.py:50
  9.3 1.4 %collective-permute-done.3.refs_1_ = bf16[32,1152]{1,0:T(8,128)(2,1)S(1)} collective-permute-done((bf16[32,1152]{1,0:T(8,128)(2,1)S(1)}, bf16[32,1152]{1,0:T(8,128)(2,1)S(1)}, u32[]{:S(2)}, u32[]{:S(2)}) %collective-permute-start.3) | collective-permute-done | bytes 73760 | tf_op jit(solution)/shard_map/ppermute | solution.py:50
  10.7 1.0 %collective-permute-start.6 = (bf16[32,1152]{1,0:T(8,128)(2,1)S(1)}, bf16[32,1152]{1,0:T(8,128)(2,1)S(1)}, u32[]{:S(2)}, u32[]{:S(2)}) collective-permute-start(bf16[32,1152]{1,0:T(8,128)(2,1)S(1)} %collective-permute-done.3.refs_1_), channel_id=1, source_target_pairs={{0,4},{4,0},{8,12},{12,8},{16,20},{20,16},{24,28},{28,24},{1,5},{5... | collective-permute-start | bytes 221192 | tf_op jit(solution)/shard_map/ppermute | solution.py:37
  11.7 1.1 %collective-permute-done.far_ids_ref = s32[1,64]{1,0:T(1,128)S(1)} collective-permute-done((s32[1,64]{1,0:T(1,128)S(1)}, s32[1,64]{1,0:T(1,128)S(1)}, u32[]{:S(2)}, u32[]{:S(2)}) %collective-permute-start) | collective-permute-done | bytes 288 | tf_op jit(solution)/shard_map/ppermute | solution.py:37
  13.2 0.5 %shard_map.51 = (f32[32,1152]{1,0:T(8,128)S(1)}, bf16[16,1152]{1,0:T(8,128)(2,1)S(1)}, bf16[16,1152]{1,0:T(8,128)(2,1)S(1)}, bf16[32,1152]{1,0:T(8,128)(2,1)S(1)}, bf16[32,1152]{1,0:T(8,128)(2,1)S(1)}) custom-call(s32[1,64]{1,0:T(1,128)S(1)} %bitcast.2, s32[1,64]{1,0:T(1,128)S(1)} %collective-permute-done.far_ids_ref, ...), custom_call_target="tpu_custom_call" | custom-call | tf_op jit(solution)/shard_map/pallas_call | solution.py:67
  13.7 2.2 %collective-permute-start.9 = (bf16[32,1152]{1,0:T(8,128)(2,1)S(1)}, bf16[32,1152]{1,0:T(8,128)(2,1)S(1)}, u32[]{:S(2)}, u32[]{:S(2)}) collective-permute-start(bf16[32,1152]{1,0:T(8,128)(2,1)S(1)} %get-tuple-element.18), channel_id=1, source_target_pairs={{0,24},{1,25},{2,26},{3,27},{4,7},{5,6},{6,5},{7,4},{8,16},{9,17},... | collective-permute-start | bytes 221192 | tf_op jit(solution)/shard_map/ppermute | solution.py:50
  15.9 0.5 %collective-permute-start.10 = (bf16[32,1152]{1,0:T(8,128)(2,1)S(1)}, bf16[32,1152]{1,0:T(8,128)(2,1)S(1)}, u32[]{:S(2)}, u32[]{:S(2)}) collective-permute-start(bf16[32,1152]{1,0:T(8,128)(2,1)S(1)} %get-tuple-element.19), channel_id=1, source_target_pairs={{0,16},{1,17},{2,18},{3,19},{4,6},{5,7},{6,4},{7,5},{8,24},{9,25},... | collective-permute-start | bytes 221192 | tf_op jit(solution)/shard_map/ppermute | solution.py:50
  16.4 1.0 %collective-permute-start.11 = (bf16[16,1152]{1,0:T(8,128)(2,1)S(1)}, bf16[16,1152]{1,0:T(8,128)(2,1)S(1)}, u32[]{:S(2)}, u32[]{:S(2)}) collective-permute-start(bf16[16,1152]{1,0:T(8,128)(2,1)S(1)} %get-tuple-element.21), channel_id=1, source_target_pairs={{0,12},{1,9},{2,14},{3,11},{4,5},{5,0},{6,7},{7,2},{8,4},{9,1},{10... | collective-permute-start | bytes 110600 | tf_op jit(solution)/shard_map/ppermute | solution.py:50
  17.4 0.5 %collective-permute-start.12 = (bf16[16,1152]{1,0:T(8,128)(2,1)S(1)}, bf16[16,1152]{1,0:T(8,128)(2,1)S(1)}, u32[]{:S(2)}, u32[]{:S(2)}) collective-permute-start(bf16[16,1152]{1,0:T(8,128)(2,1)S(1)} %get-tuple-element.22), channel_id=1, source_target_pairs={{0,8},{1,13},{2,10},{3,15},{4,1},{5,4},{6,3},{7,6},{8,0},{9,5},{10... | collective-permute-start | bytes 110600 | tf_op jit(solution)/shard_map/ppermute | solution.py:50
  17.9 1.1 %collective-permute-done.9.refs_0_ = bf16[32,1152]{1,0:T(8,128)(2,1)S(1)} collective-permute-done((bf16[32,1152]{1,0:T(8,128)(2,1)S(1)}, bf16[32,1152]{1,0:T(8,128)(2,1)S(1)}, u32[]{:S(2)}, u32[]{:S(2)}) %collective-permute-start.9) | collective-permute-done | bytes 73760 | tf_op jit(solution)/shard_map/ppermute | solution.py:50
  19.0 1.2 %collective-permute-done.10.refs_1_ = bf16[32,1152]{1,0:T(8,128)(2,1)S(1)} collective-permute-done((bf16[32,1152]{1,0:T(8,128)(2,1)S(1)}, bf16[32,1152]{1,0:T(8,128)(2,1)S(1)}, u32[]{:S(2)}, u32[]{:S(2)}) %collective-permute-start.10) | collective-permute-done | bytes 73760 | tf_op jit(solution)/shard_map/ppermute | solution.py:50
  20.6 0.7 %collective-permute-done.12.second_ref = bf16[16,1152]{1,0:T(8,128)(2,1)S(1)} collective-permute-done((bf16[16,1152]{1,0:T(8,128)(2,1)S(1)}, bf16[16,1152]{1,0:T(8,128)(2,1)S(1)}, u32[]{:S(2)}, u32[]{:S(2)}) %collective-permute-start.12) | collective-permute-done | bytes 36896 | tf_op jit(solution)/shard_map/ppermute | solution.py:50
  21.6 0.6 %copy-done = f32[16,1152]{1,0:T(8,128)} copy-done((f32[16,1152]{1,0:T(8,128)}, f32[16,1152]{1,0:T(8,128)S(1)}, u32[]{:S(2)}) %copy-start) | copy-done | bytes 73752
  22.2 0.6 %copy-done.1 = f32[16,1152]{1,0:T(8,128)} copy-done((f32[16,1152]{1,0:T(8,128)}, f32[16,1152]{1,0:T(8,128)S(1)}, u32[]{:S(2)}) %copy-start.1) | copy-done | bytes 73752
  22.8 0.6 %copy-done.2 = f32[16,1152]{1,0:T(8,128)} copy-done((f32[16,1152]{1,0:T(8,128)}, f32[16,1152]{1,0:T(8,128)S(1)}, u32[]{:S(2)}) %copy-start.2) | copy-done | bytes 73752
  23.4 0.6 %copy-done.3 = f32[16,1]{1,0:T(8,128)} copy-done((f32[16,1]{1,0:T(8,128)}, f32[16,1]{1,0:T(8,128)S(1)}, u32[]{:S(2)}) %copy-start.3) | copy-done | bytes 88
  24.1 0.6 %copy-done.6 = bf16[16,1152]{1,0:T(8,128)(2,1)} copy-done((bf16[16,1152]{1,0:T(8,128)(2,1)}, bf16[16,1152]{1,0:T(8,128)(2,1)S(1)}, u32[]{:S(2)}) %copy-start.6) | copy-done | bytes 36888
  24.7 1.7 %shard_map.54 = (f32[16,1152]{1,0:T(8,128)}, f32[16,1152]{1,0:T(8,128)}) custom-call(f32[16,1152]{1,0:T(8,128)} %copy-done, f32[16,1152]{1,0:T(8,128)} %copy-done.1, f32[16,1]{1,0:T(8,128)} %copy-done.3, f32[16,1152]{1,0:T(8,128)} %copy-done.2, bf16[16,1152]{1,0:T(8,128)(2,1)} %copy-done.6), custom_call_target="tpu_custom_call" | custom-call | tf_op jit(solution)/shard_map/pallas_call | solution.py:228
  (25 shorter events, 1.4 us)
Async XLA Ops:
  0.6 1.4 %copy-start.5 = (bf16[16,1152]{1,0:T(8,128)(2,1)S(1)}, bf16[16,1152]{1,0:T(8,128)(2,1)}, u32[]{:S(2)}) copy-start(bf16[16,1152]{1,0:T(8,128)(2,1)} %param.3) | copy-start | bytes 110596
  0.6 1.6 %collective-permute-start.2 = (bf16[16,1152]{1,0:T(8,128)(2,1)}, bf16[16,1152]{1,0:T(8,128)(2,1)S(1)}, u32[]{:S(2)}, u32[]{:S(2)}) collective-permute-start(bf16[16,1152]{1,0:T(8,128)(2,1)} %param.3), channel_id=1, source_target_pairs={{0,4},{4,0},{8,12},{12,8},{16,20},{20,16},{24,28},{28,24},{1,5},{5... | collective-permute-start | bytes 110600 | tf_op jit(solution)/shard_map/ppermute | solution.py:37
  1.2 1.4 %collective-permute-start.1 = (bf16[16,1152]{1,0:T(8,128)(2,1)}, bf16[16,1152]{1,0:T(8,128)(2,1)S(1)}, u32[]{:S(2)}, u32[]{:S(2)}) collective-permute-start(bf16[16,1152]{1,0:T(8,128)(2,1)} %param.4), channel_id=1, source_target_pairs={{0,4},{4,0},{8,12},{12,8},{16,20},{20,16},{24,28},{28,24},{1,5},{5... | collective-permute-start | bytes 110600 | tf_op jit(solution)/shard_map/ppermute | solution.py:37
  2.7 9.0 %copy-start.4 = (s32[64]{0:T(128)S(1)}, s32[64]{0:T(128)}, u32[]{:S(2)}) copy-start(s32[64]{0:T(128)} %param.5) | copy-start | bytes 772
  2.7 6.6 %collective-permute-start.4 = (bf16[32,1152]{1,0:T(8,128)(2,1)S(1)}, bf16[32,1152]{1,0:T(8,128)(2,1)S(1)}, u32[]{:S(2)}, u32[]{:S(2)}) collective-permute-start(bf16[32,1152]{1,0:T(8,128)(2,1)S(1)} %get-tuple-element.15.refs_0_), channel_id=1, source_target_pairs={{0,16},{1,17},{2,18},{3,19},{4,6},{5,7},{6,4},{7,5},{8,24},{9,25},... | collective-permute-start | bytes 221192 | tf_op jit(solution)/shard_map/ppermute | solution.py:50
  5.5 5.3 %collective-permute-start.3 = (bf16[32,1152]{1,0:T(8,128)(2,1)S(1)}, bf16[32,1152]{1,0:T(8,128)(2,1)S(1)}, u32[]{:S(2)}, u32[]{:S(2)}) collective-permute-start(bf16[32,1152]{1,0:T(8,128)(2,1)S(1)} %get-tuple-element.15.refs_0_), channel_id=1, source_target_pairs={{0,24},{1,25},{2,26},{3,27},{4,7},{5,6},{6,5},{7,4},{8,16},{9,17},... | collective-permute-start | bytes 221192 | tf_op jit(solution)/shard_map/ppermute | solution.py:50
  6.9 5.9 %collective-permute-start.8 = (bf16[32,1152]{1,0:T(8,128)(2,1)S(1)}, bf16[32,1152]{1,0:T(8,128)(2,1)S(1)}, u32[]{:S(2)}, u32[]{:S(2)}) collective-permute-start(bf16[32,1152]{1,0:T(8,128)(2,1)S(1)} %get-tuple-element.15.refs_0_), channel_id=1, source_target_pairs={{0,12},{1,13},{2,14},{3,15},{4,1},{5,0},{6,3},{7,2},{8,4},{9,5},{1... | collective-permute-start | bytes 221192 | tf_op jit(solution)/shard_map/ppermute | solution.py:50
  8.8 4.4 %collective-permute-start.5 = (bf16[32,1152]{1,0:T(8,128)(2,1)S(1)}, bf16[32,1152]{1,0:T(8,128)(2,1)S(1)}, u32[]{:S(2)}, u32[]{:S(2)}) collective-permute-start(bf16[32,1152]{1,0:T(8,128)(2,1)S(1)} %get-tuple-element.15.refs_0_), channel_id=1, source_target_pairs={{0,8},{1,9},{2,10},{3,11},{4,5},{5,4},{6,7},{7,6},{8,0},{9,1},{10,... | collective-permute-start | bytes 221192 | tf_op jit(solution)/shard_map/ppermute | solution.py:50
  9.3 3.8 %collective-permute-start.7 = (bf16[32,1152]{1,0:T(8,128)(2,1)S(1)}, bf16[32,1152]{1,0:T(8,128)(2,1)S(1)}, u32[]{:S(2)}, u32[]{:S(2)}) collective-permute-start(bf16[32,1152]{1,0:T(8,128)(2,1)S(1)} %collective-permute-done.4.refs_2_), channel_id=1, source_target_pairs={{0,4},{4,0},{8,12},{12,8},{16,20},{20,16},{24,28},{28,24},{1,5},{5... | collective-permute-start | bytes 221192 | tf_op jit(solution)/shard_map/ppermute | solution.py:37
  10.7 2.4 %collective-permute-start.6 = (bf16[32,1152]{1,0:T(8,128)(2,1)S(1)}, bf16[32,1152]{1,0:T(8,128)(2,1)S(1)}, u32[]{:S(2)}, u32[]{:S(2)}) collective-permute-start(bf16[32,1152]{1,0:T(8,128)(2,1)S(1)} %collective-permute-done.3.refs_1_), channel_id=1, source_target_pairs={{0,4},{4,0},{8,12},{12,8},{16,20},{20,16},{24,28},{28,24},{1,5},{5... | collective-permute-start | bytes 221192 | tf_op jit(solution)/shard_map/ppermute | solution.py:37
  11.7 1.1 %collective-permute-start = (s32[1,64]{1,0:T(1,128)S(1)}, s32[1,64]{1,0:T(1,128)S(1)}, u32[]{:S(2)}, u32[]{:S(2)}) collective-permute-start(s32[1,64]{1,0:T(1,128)S(1)} %bitcast.1), channel_id=1, source_target_pairs={{0,4},{4,0},{8,12},{12,8},{16,20},{20,16},{24,28},{28,24},{1,5},{5... | collective-permute-start | bytes 776 | tf_op jit(solution)/shard_map/ppermute | solution.py:37
  13.7 5.3 %collective-permute-start.9 = (bf16[32,1152]{1,0:T(8,128)(2,1)S(1)}, bf16[32,1152]{1,0:T(8,128)(2,1)S(1)}, u32[]{:S(2)}, u32[]{:S(2)}) collective-permute-start(bf16[32,1152]{1,0:T(8,128)(2,1)S(1)} %get-tuple-element.18), channel_id=1, source_target_pairs={{0,24},{1,25},{2,26},{3,27},{4,7},{5,6},{6,5},{7,4},{8,16},{9,17},... | collective-permute-start | bytes 221192 | tf_op jit(solution)/shard_map/ppermute | solution.py:50
  15.9 4.4 %collective-permute-start.10 = (bf16[32,1152]{1,0:T(8,128)(2,1)S(1)}, bf16[32,1152]{1,0:T(8,128)(2,1)S(1)}, u32[]{:S(2)}, u32[]{:S(2)}) collective-permute-start(bf16[32,1152]{1,0:T(8,128)(2,1)S(1)} %get-tuple-element.19), channel_id=1, source_target_pairs={{0,16},{1,17},{2,18},{3,19},{4,6},{5,7},{6,4},{7,5},{8,24},{9,25},... | collective-permute-start | bytes 221192 | tf_op jit(solution)/shard_map/ppermute | solution.py:50
  16.4 4.2 %collective-permute-start.11 = (bf16[16,1152]{1,0:T(8,128)(2,1)S(1)}, bf16[16,1152]{1,0:T(8,128)(2,1)S(1)}, u32[]{:S(2)}, u32[]{:S(2)}) collective-permute-start(bf16[16,1152]{1,0:T(8,128)(2,1)S(1)} %get-tuple-element.21), channel_id=1, source_target_pairs={{0,12},{1,9},{2,14},{3,11},{4,5},{5,0},{6,7},{7,2},{8,4},{9,1},{10... | collective-permute-start | bytes 110600 | tf_op jit(solution)/shard_map/ppermute | solution.py:50
  17.4 4.0 %collective-permute-start.12 = (bf16[16,1152]{1,0:T(8,128)(2,1)S(1)}, bf16[16,1152]{1,0:T(8,128)(2,1)S(1)}, u32[]{:S(2)}, u32[]{:S(2)}) collective-permute-start(bf16[16,1152]{1,0:T(8,128)(2,1)S(1)} %get-tuple-element.22), channel_id=1, source_target_pairs={{0,8},{1,13},{2,10},{3,15},{4,1},{5,4},{6,3},{7,6},{8,0},{9,5},{10... | collective-permute-start | bytes 110600 | tf_op jit(solution)/shard_map/ppermute | solution.py:50
  20.3 3.8 %collective-permute-start.13 = (bf16[16,1152]{1,0:T(8,128)(2,1)S(1)}, bf16[16,1152]{1,0:T(8,128)(2,1)S(1)}, u32[]{:S(2)}, u32[]{:S(2)}) collective-permute-start(bf16[16,1152]{1,0:T(8,128)(2,1)S(1)} %get-tuple-element.27), channel_id=1, source_target_pairs={{0,4},{4,0},{8,12},{12,8},{16,20},{20,16},{24,28},{28,24},{1,5},{5... | collective-permute-start | bytes 110600 | tf_op jit(solution)/shard_map/ppermute | solution.py:37
  21.6 0.6 %copy-start = (f32[16,1152]{1,0:T(8,128)}, f32[16,1152]{1,0:T(8,128)S(1)}, u32[]{:S(2)}) copy-start(f32[16,1152]{1,0:T(8,128)S(1)} %get-tuple-element.23.grad_ref) | copy-start | bytes 221188
  22.2 0.6 %copy-start.1 = (f32[16,1152]{1,0:T(8,128)}, f32[16,1152]{1,0:T(8,128)S(1)}, u32[]{:S(2)}) copy-start(f32[16,1152]{1,0:T(8,128)S(1)} %get-tuple-element.24.unit_ref) | copy-start | bytes 221188
  22.8 0.6 %copy-start.2 = (f32[16,1152]{1,0:T(8,128)}, f32[16,1152]{1,0:T(8,128)S(1)}, u32[]{:S(2)}) copy-start(f32[16,1152]{1,0:T(8,128)S(1)} %get-tuple-element.26.rest_ref) | copy-start | bytes 221188
  23.4 0.6 %copy-start.3 = (f32[16,1]{1,0:T(8,128)}, f32[16,1]{1,0:T(8,128)S(1)}, u32[]{:S(2)}) copy-start(f32[16,1]{1,0:T(8,128)S(1)} %get-tuple-element.25.inverse_ref) | copy-start | bytes 196
  24.1 0.6 %copy-start.6 = (bf16[16,1152]{1,0:T(8,128)(2,1)}, bf16[16,1152]{1,0:T(8,128)(2,1)S(1)}, u32[]{:S(2)}) copy-start(bf16[16,1152]{1,0:T(8,128)(2,1)S(1)} %collective-permute-done.13.got_ref) | copy-start | bytes 110596

commit v31 on v29

--- a/solution.py
+++ b/solution.py
@@ -51,11 +51,11 @@
 
 
 def cross_first(img, txt, distance):
-    return (txt + img % 2 * distance) % 2 == 0
+    return (txt + img % 2 * distance) % 2 == 1
 
 
 def gets_cross_first():
-    return lax.axis_index("txt") % 2 == 0
+    return lax.axis_index("txt") % 2 == 1
 
 
 def is_even():

time: 22.5 us -> 22.5 us (level)
  waiting for transfers between devices: 6.56 us -> 7.11 us
  starting transfers between devices: 12.7 us -> 12.2 us
    ppermute x8, starting transfers between devices: 10.8 us -> 10.4 us  [chip_swap(): return lax.ppermute(block, ('img', 'txt'), pairs)]
    ppermute x6, waiting for transfers between devices: 1.89 us -> 2.27 us  [core_swap(): return lax.ppermute(block, 'img', [(i, i ^ 1) for i in range(size)])]
where the time goes in v31:
time: 22.5 us; the launch traced here: 22.4 us
  starting transfers between devices  12.2 us (54%)
  waiting for transfers between devices  7.11 us (32%)
  Pallas kernels  1.58 us (7%)
  local copies, waits for them, and re-layouts  0.79 us (4%)
  between operations  0.68 us (3%)
    ppermute x8, starting transfers between devices, chip_swap(): return lax.ppermute(block, ('img', 'txt'), pairs)  10.4 us
    ppermute x8, waiting for transfers between devices, chip_swap(): return lax.ppermute(block, ('img', 'txt'), pairs)  4.84 us
    ppermute x6, waiting for transfers between devices, core_swap(): return lax.ppermute(block, 'img', [(i, i ^ 1) for i in range(size)])  2.27 us
    ppermute x6, starting transfers between devices, core_swap(): return lax.ppermute(block, 'img', [(i, i ^ 1) for i in range(size)])  1.82 us
    pallas_call x5, Pallas kernels, call(): pl.pallas_call(kernel, out_shape=outs, in_specs=[VMEM] * len(args), out_s...  1.58 us
    unnamed x5, local copies, waits for them, and re-layouts  0.78 us
  transfers between devices with their start and end apart: 14, of which 9 were waited for; matrix products, arithmetic and copies ran while one was open for 3% of the time, Pallas kernels for 1%

profile of v31, /device:TPU:0, one launch (start us, length us, event | category | flops | bytes accessed | tf_op | source)
XLA Modules:
  0.0 22.4 jit_solution(7675426740758420715)
XLA Ops:
  0.6 0.5 %collective-permute-start.2 = (bf16[16,1152]{1,0:T(8,128)(2,1)}, bf16[16,1152]{1,0:T(8,128)(2,1)S(1)}, u32[]{:S(2)}, u32[]{:S(2)}) collective-permute-start(bf16[16,1152]{1,0:T(8,128)(2,1)} %param.3), channel_id=1, source_target_pairs={{0,4},{4,0},{8,12},{12,8},{16,20},{20,16},{24,28},{28,24},{1,5},{5... | collective-permute-start | bytes 110600 | tf_op jit(solution)/shard_map/ppermute | solution.py:37
  1.2 0.8 %constant_dynamic-update-slice_fusion.1 = bf16[32,1152]{1,0:T(8,128)(2,1)S(1)} fusion(bf16[16,1152]{1,0:T(8,128)(2,1)} %param.4), kind=kLoop, calls=%fused_computation.1 | loop fusion | bytes 73728
  2.0 0.2 collective-permute-done.2.img_ref
  2.2 0.3 %collective-permute-done.1.txt_ref = bf16[16,1152]{1,0:T(8,128)(2,1)S(1)} collective-permute-done((bf16[16,1152]{1,0:T(8,128)(2,1)}, bf16[16,1152]{1,0:T(8,128)(2,1)S(1)}, u32[]{:S(2)}, u32[]{:S(2)}) %collective-permute-start.1) | collective-permute-done | bytes 36896 | tf_op jit(solution)/shard_map/ppermute | solution.py:37
  2.6 0.1 shard_map.50
  2.7 2.7 %collective-permute-start.4 = (bf16[32,1152]{1,0:T(8,128)(2,1)S(1)}, bf16[32,1152]{1,0:T(8,128)(2,1)S(1)}, u32[]{:S(2)}, u32[]{:S(2)}) collective-permute-start(bf16[32,1152]{1,0:T(8,128)(2,1)S(1)} %get-tuple-element.14.refs_0_), channel_id=1, source_target_pairs={{0,16},{1,17},{2,18},{3,19},{4,6},{5,7},{6,4},{7,5},{8,24},{9,25},... | collective-permute-start | bytes 221192 | tf_op jit(solution)/shard_map/ppermute | solution.py:50
  5.5 1.4 %collective-permute-start.3 = (bf16[32,1152]{1,0:T(8,128)(2,1)S(1)}, bf16[32,1152]{1,0:T(8,128)(2,1)S(1)}, u32[]{:S(2)}, u32[]{:S(2)}) collective-permute-start(bf16[32,1152]{1,0:T(8,128)(2,1)S(1)} %get-tuple-element.14.refs_0_), channel_id=1, source_target_pairs={{0,24},{1,25},{2,26},{3,27},{4,7},{5,6},{6,5},{7,4},{8,16},{9,17},... | collective-permute-start | bytes 221192 | tf_op jit(solution)/shard_map/ppermute | solution.py:50
  6.9 1.9 %collective-permute-start.8 = (bf16[32,1152]{1,0:T(8,128)(2,1)S(1)}, bf16[32,1152]{1,0:T(8,128)(2,1)S(1)}, u32[]{:S(2)}, u32[]{:S(2)}) collective-permute-start(bf16[32,1152]{1,0:T(8,128)(2,1)S(1)} %get-tuple-element.14.refs_0_), channel_id=1, source_target_pairs={{0,12},{1,13},{2,14},{3,15},{4,1},{5,0},{6,3},{7,2},{8,4},{9,5},{1... | collective-permute-start | bytes 221192 | tf_op jit(solution)/shard_map/ppermute | solution.py:50
  8.8 0.5 %collective-permute-start.5 = (bf16[32,1152]{1,0:T(8,128)(2,1)S(1)}, bf16[32,1152]{1,0:T(8,128)(2,1)S(1)}, u32[]{:S(2)}, u32[]{:S(2)}) collective-permute-start(bf16[32,1152]{1,0:T(8,128)(2,1)S(1)} %get-tuple-element.14.refs_0_), channel_id=1, source_target_pairs={{0,8},{1,9},{2,10},{3,11},{4,5},{5,4},{6,7},{7,6},{8,0},{9,1},{10,... | collective-permute-start | bytes 221192 | tf_op jit(solution)/shard_map/ppermute | solution.py:50
  9.3 1.4 %collective-permute-done.3.refs_1_ = bf16[32,1152]{1,0:T(8,128)(2,1)S(1)} collective-permute-done((bf16[32,1152]{1,0:T(8,128)(2,1)S(1)}, bf16[32,1152]{1,0:T(8,128)(2,1)S(1)}, u32[]{:S(2)}, u32[]{:S(2)}) %collective-permute-start.3) | collective-permute-done | bytes 73760 | tf_op jit(solution)/shard_map/ppermute | solution.py:50
  10.7 1.0 %collective-permute-start.6 = (bf16[32,1152]{1,0:T(8,128)(2,1)S(1)}, bf16[32,1152]{1,0:T(8,128)(2,1)S(1)}, u32[]{:S(2)}, u32[]{:S(2)}) collective-permute-start(bf16[32,1152]{1,0:T(8,128)(2,1)S(1)} %collective-permute-done.3.refs_1_), channel_id=1, source_target_pairs={{0,4},{4,0},{8,12},{12,8},{16,20},{20,16},{24,28},{28,24},{1,5},{5... | collective-permute-start | bytes 221192 | tf_op jit(solution)/shard_map/ppermute | solution.py:37
  11.7 1.1 %collective-permute-done.far_ids_ref = s32[1,64]{1,0:T(1,128)S(1)} collective-permute-done((s32[1,64]{1,0:T(1,128)S(1)}, s32[1,64]{1,0:T(1,128)S(1)}, u32[]{:S(2)}, u32[]{:S(2)}) %collective-permute-start) | collective-permute-done | bytes 288 | tf_op jit(solution)/shard_map/ppermute | solution.py:37
  12.8 0.3 %collective-permute-done.5.refs_3_ = bf16[32,1152]{1,0:T(8,128)(2,1)S(1)} collective-permute-done((bf16[32,1152]{1,0:T(8,128)(2,1)S(1)}, bf16[32,1152]{1,0:T(8,128)(2,1)S(1)}, u32[]{:S(2)}, u32[]{:S(2)}) %collective-permute-start.5) | collective-permute-done | bytes 73760 | tf_op jit(solution)/shard_map/ppermute | solution.py:50
  13.2 0.5 %shard_map.51 = (f32[32,1152]{1,0:T(8,128)S(1)}, bf16[16,1152]{1,0:T(8,128)(2,1)S(1)}, bf16[16,1152]{1,0:T(8,128)(2,1)S(1)}, bf16[32,1152]{1,0:T(8,128)(2,1)S(1)}, bf16[32,1152]{1,0:T(8,128)(2,1)S(1)}) custom-call(s32[1,64]{1,0:T(1,128)S(1)} %bitcast.2, s32[1,64]{1,0:T(1,128)S(1)} %collective-permute-done.far_ids_ref, ...), custom_call_target="tpu_custom_call" | custom-call | tf_op jit(solution)/shard_map/pallas_call | solution.py:67
  13.7 2.2 %collective-permute-start.10 = (bf16[32,1152]{1,0:T(8,128)(2,1)S(1)}, bf16[32,1152]{1,0:T(8,128)(2,1)S(1)}, u32[]{:S(2)}, u32[]{:S(2)}) collective-permute-start(bf16[32,1152]{1,0:T(8,128)(2,1)S(1)} %get-tuple-element.21), channel_id=1, source_target_pairs={{0,24},{1,25},{2,26},{3,27},{4,7},{5,6},{6,5},{7,4},{8,16},{9,17},... | collective-permute-start | bytes 221192 | tf_op jit(solution)/shard_map/ppermute | solution.py:50
  15.9 0.5 %collective-permute-start.11 = (bf16[32,1152]{1,0:T(8,128)(2,1)S(1)}, bf16[32,1152]{1,0:T(8,128)(2,1)S(1)}, u32[]{:S(2)}, u32[]{:S(2)}) collective-permute-start(bf16[32,1152]{1,0:T(8,128)(2,1)S(1)} %get-tuple-element.22), channel_id=1, source_target_pairs={{0,16},{1,17},{2,18},{3,19},{4,6},{5,7},{6,4},{7,5},{8,24},{9,25},... | collective-permute-start | bytes 221192 | tf_op jit(solution)/shard_map/ppermute | solution.py:50
  16.4 0.8 %collective-permute-start.9 = (bf16[16,1152]{1,0:T(8,128)(2,1)S(1)}, bf16[16,1152]{1,0:T(8,128)(2,1)S(1)}, u32[]{:S(2)}, u32[]{:S(2)}) collective-permute-start(bf16[16,1152]{1,0:T(8,128)(2,1)S(1)} %get-tuple-element.16), channel_id=1, source_target_pairs={{0,8},{1,13},{2,10},{3,15},{4,1},{5,4},{6,3},{7,6},{8,0},{9,5},{10... | collective-permute-start | bytes 110600 | tf_op jit(solution)/shard_map/ppermute | solution.py:50
  17.3 0.2 collective-permute-start.12
  17.5 1.5 %collective-permute-done.10.refs_0_ = bf16[32,1152]{1,0:T(8,128)(2,1)S(1)} collective-permute-done((bf16[32,1152]{1,0:T(8,128)(2,1)S(1)}, bf16[32,1152]{1,0:T(8,128)(2,1)S(1)}, u32[]{:S(2)}, u32[]{:S(2)}) %collective-permute-start.10) | collective-permute-done | bytes 73760 | tf_op jit(solution)/shard_map/ppermute | solution.py:50
  19.0 1.2 %collective-permute-done.11.refs_1_ = bf16[32,1152]{1,0:T(8,128)(2,1)S(1)} collective-permute-done((bf16[32,1152]{1,0:T(8,128)(2,1)S(1)}, bf16[32,1152]{1,0:T(8,128)(2,1)S(1)}, u32[]{:S(2)}, u32[]{:S(2)}) %collective-permute-start.11) | collective-permute-done | bytes 73760 | tf_op jit(solution)/shard_map/ppermute | solution.py:50
  20.3 0.3 %collective-permute-start.13 = (bf16[16,1152]{1,0:T(8,128)(2,1)S(1)}, bf16[16,1152]{1,0:T(8,128)(2,1)S(1)}, u32[]{:S(2)}, u32[]{:S(2)}) collective-permute-start(bf16[16,1152]{1,0:T(8,128)(2,1)S(1)} %get-tuple-element.25), channel_id=1, source_target_pairs={{0,4},{4,0},{8,12},{12,8},{16,20},{20,16},{24,28},{28,24},{1,5},{5... | collective-permute-start | bytes 110600 | tf_op jit(solution)/shard_map/ppermute | solution.py:37
  20.7 0.3 %collective-permute-done.12.second_ref = bf16[16,1152]{1,0:T(8,128)(2,1)S(1)} collective-permute-done((bf16[16,1152]{1,0:T(8,128)(2,1)S(1)}, bf16[16,1152]{1,0:T(8,128)(2,1)S(1)}, u32[]{:S(2)}, u32[]{:S(2)}) %collective-permute-start.12) | collective-permute-done | bytes 36896 | tf_op jit(solution)/shard_map/ppermute | solution.py:50
  21.0 0.6 %collective-permute-done.13.got_ref = bf16[16,1152]{1,0:T(8,128)(2,1)S(1)} collective-permute-done((bf16[16,1152]{1,0:T(8,128)(2,1)S(1)}, bf16[16,1152]{1,0:T(8,128)(2,1)S(1)}, u32[]{:S(2)}, u32[]{:S(2)}) %collective-permute-start.13) | collective-permute-done | bytes 36896 | tf_op jit(solution)/shard_map/ppermute | solution.py:37
  21.6 0.8 %shard_map.54 = (f32[16,1152]{1,0:T(8,128)}, f32[16,1152]{1,0:T(8,128)}) custom-call(f32[32,1152]{1,0:T(8,128)S(1)} %get-tuple-element.17.unit_ref, f32[32,1]{1,0:T(8,128)S(1)} %get-tuple-element.18.inverse_ref, f32[16,1152]{1,0:T(8,128)S(1)} %get-tuple-element.19.first_ref, f32[16,1152]{1,0:T(8,128)S(1)} %get-tuple-element.23.keep_ref, ...), custom_call_target="tpu_custom_call" | custom-call | tf_op jit(solution)/shard_map/pallas_call | solution.py:67
  (15 shorter events, 0.3 us)
Async XLA Ops:
  0.6 1.4 %copy-start.1 = (bf16[16,1152]{1,0:T(8,128)(2,1)S(1)}, bf16[16,1152]{1,0:T(8,128)(2,1)}, u32[]{:S(2)}) copy-start(bf16[16,1152]{1,0:T(8,128)(2,1)} %param.3) | copy-start | bytes 110596
  0.6 1.6 %collective-permute-start.2 = (bf16[16,1152]{1,0:T(8,128)(2,1)}, bf16[16,1152]{1,0:T(8,128)(2,1)S(1)}, u32[]{:S(2)}, u32[]{:S(2)}) collective-permute-start(bf16[16,1152]{1,0:T(8,128)(2,1)} %param.3), channel_id=1, source_target_pairs={{0,4},{4,0},{8,12},{12,8},{16,20},{20,16},{24,28},{28,24},{1,5},{5... | collective-permute-start | bytes 110600 | tf_op jit(solution)/shard_map/ppermute | solution.py:37
  1.2 1.4 %collective-permute-start.1 = (bf16[16,1152]{1,0:T(8,128)(2,1)}, bf16[16,1152]{1,0:T(8,128)(2,1)S(1)}, u32[]{:S(2)}, u32[]{:S(2)}) collective-permute-start(bf16[16,1152]{1,0:T(8,128)(2,1)} %param.4), channel_id=1, source_target_pairs={{0,4},{4,0},{8,12},{12,8},{16,20},{20,16},{24,28},{28,24},{1,5},{5... | collective-permute-start | bytes 110600 | tf_op jit(solution)/shard_map/ppermute | solution.py:37
  2.7 9.0 %copy-start = (s32[64]{0:T(128)S(1)}, s32[64]{0:T(128)}, u32[]{:S(2)}) copy-start(s32[64]{0:T(128)} %param.5) | copy-start | bytes 772
  2.7 6.6 %collective-permute-start.4 = (bf16[32,1152]{1,0:T(8,128)(2,1)S(1)}, bf16[32,1152]{1,0:T(8,128)(2,1)S(1)}, u32[]{:S(2)}, u32[]{:S(2)}) collective-permute-start(bf16[32,1152]{1,0:T(8,128)(2,1)S(1)} %get-tuple-element.14.refs_0_), channel_id=1, source_target_pairs={{0,16},{1,17},{2,18},{3,19},{4,6},{5,7},{6,4},{7,5},{8,24},{9,25},... | collective-permute-start | bytes 221192 | tf_op jit(solution)/shard_map/ppermute | solution.py:50
  5.5 5.3 %collective-permute-start.3 = (bf16[32,1152]{1,0:T(8,128)(2,1)S(1)}, bf16[32,1152]{1,0:T(8,128)(2,1)S(1)}, u32[]{:S(2)}, u32[]{:S(2)}) collective-permute-start(bf16[32,1152]{1,0:T(8,128)(2,1)S(1)} %get-tuple-element.14.refs_0_), channel_id=1, source_target_pairs={{0,24},{1,25},{2,26},{3,27},{4,7},{5,6},{6,5},{7,4},{8,16},{9,17},... | collective-permute-start | bytes 221192 | tf_op jit(solution)/shard_map/ppermute | solution.py:50
  6.9 5.9 %collective-permute-start.8 = (bf16[32,1152]{1,0:T(8,128)(2,1)S(1)}, bf16[32,1152]{1,0:T(8,128)(2,1)S(1)}, u32[]{:S(2)}, u32[]{:S(2)}) collective-permute-start(bf16[32,1152]{1,0:T(8,128)(2,1)S(1)} %get-tuple-element.14.refs_0_), channel_id=1, source_target_pairs={{0,12},{1,13},{2,14},{3,15},{4,1},{5,0},{6,3},{7,2},{8,4},{9,5},{1... | collective-permute-start | bytes 221192 | tf_op jit(solution)/shard_map/ppermute | solution.py:50
  8.8 4.4 %collective-permute-start.5 = (bf16[32,1152]{1,0:T(8,128)(2,1)S(1)}, bf16[32,1152]{1,0:T(8,128)(2,1)S(1)}, u32[]{:S(2)}, u32[]{:S(2)}) collective-permute-start(bf16[32,1152]{1,0:T(8,128)(2,1)S(1)} %get-tuple-element.14.refs_0_), channel_id=1, source_target_pairs={{0,8},{1,9},{2,10},{3,11},{4,5},{5,4},{6,7},{7,6},{8,0},{9,1},{10,... | collective-permute-start | bytes 221192 | tf_op jit(solution)/shard_map/ppermute | solution.py:50
  9.3 3.8 %collective-permute-start.7 = (bf16[32,1152]{1,0:T(8,128)(2,1)S(1)}, bf16[32,1152]{1,0:T(8,128)(2,1)S(1)}, u32[]{:S(2)}, u32[]{:S(2)}) collective-permute-start(bf16[32,1152]{1,0:T(8,128)(2,1)S(1)} %collective-permute-done.4.refs_2_), channel_id=1, source_target_pairs={{0,4},{4,0},{8,12},{12,8},{16,20},{20,16},{24,28},{28,24},{1,5},{5... | collective-permute-start | bytes 221192 | tf_op jit(solution)/shard_map/ppermute | solution.py:37
  10.7 2.4 %collective-permute-start.6 = (bf16[32,1152]{1,0:T(8,128)(2,1)S(1)}, bf16[32,1152]{1,0:T(8,128)(2,1)S(1)}, u32[]{:S(2)}, u32[]{:S(2)}) collective-permute-start(bf16[32,1152]{1,0:T(8,128)(2,1)S(1)} %collective-permute-done.3.refs_1_), channel_id=1, source_target_pairs={{0,4},{4,0},{8,12},{12,8},{16,20},{20,16},{24,28},{28,24},{1,5},{5... | collective-permute-start | bytes 221192 | tf_op jit(solution)/shard_map/ppermute | solution.py:37
  11.7 1.1 %collective-permute-start = (s32[1,64]{1,0:T(1,128)S(1)}, s32[1,64]{1,0:T(1,128)S(1)}, u32[]{:S(2)}, u32[]{:S(2)}) collective-permute-start(s32[1,64]{1,0:T(1,128)S(1)} %bitcast.1), channel_id=1, source_target_pairs={{0,4},{4,0},{8,12},{12,8},{16,20},{20,16},{24,28},{28,24},{1,5},{5... | collective-permute-start | bytes 776 | tf_op jit(solution)/shard_map/ppermute | solution.py:37
  13.7 5.3 %collective-permute-start.10 = (bf16[32,1152]{1,0:T(8,128)(2,1)S(1)}, bf16[32,1152]{1,0:T(8,128)(2,1)S(1)}, u32[]{:S(2)}, u32[]{:S(2)}) collective-permute-start(bf16[32,1152]{1,0:T(8,128)(2,1)S(1)} %get-tuple-element.21), channel_id=1, source_target_pairs={{0,24},{1,25},{2,26},{3,27},{4,7},{5,6},{6,5},{7,4},{8,16},{9,17},... | collective-permute-start | bytes 221192 | tf_op jit(solution)/shard_map/ppermute | solution.py:50
  15.9 4.4 %collective-permute-start.11 = (bf16[32,1152]{1,0:T(8,128)(2,1)S(1)}, bf16[32,1152]{1,0:T(8,128)(2,1)S(1)}, u32[]{:S(2)}, u32[]{:S(2)}) collective-permute-start(bf16[32,1152]{1,0:T(8,128)(2,1)S(1)} %get-tuple-element.22), channel_id=1, source_target_pairs={{0,16},{1,17},{2,18},{3,19},{4,6},{5,7},{6,4},{7,5},{8,24},{9,25},... | collective-permute-start | bytes 221192 | tf_op jit(solution)/shard_map/ppermute | solution.py:50
  16.4 4.1 %collective-permute-start.9 = (bf16[16,1152]{1,0:T(8,128)(2,1)S(1)}, bf16[16,1152]{1,0:T(8,128)(2,1)S(1)}, u32[]{:S(2)}, u32[]{:S(2)}) collective-permute-start(bf16[16,1152]{1,0:T(8,128)(2,1)S(1)} %get-tuple-element.16), channel_id=1, source_target_pairs={{0,8},{1,13},{2,10},{3,15},{4,1},{5,4},{6,3},{7,6},{8,0},{9,5},{10... | collective-permute-start | bytes 110600 | tf_op jit(solution)/shard_map/ppermute | solution.py:50
  17.3 3.7 %collective-permute-start.12 = (bf16[16,1152]{1,0:T(8,128)(2,1)S(1)}, bf16[16,1152]{1,0:T(8,128)(2,1)S(1)}, u32[]{:S(2)}, u32[]{:S(2)}) collective-permute-start(bf16[16,1152]{1,0:T(8,128)(2,1)S(1)} %get-tuple-element.24), channel_id=1, source_target_pairs={{0,12},{1,9},{2,14},{3,11},{4,5},{5,0},{6,7},{7,2},{8,4},{9,1},{10... | collective-permute-start | bytes 110600 | tf_op jit(solution)/shard_map/ppermute | solution.py:50
  20.3 1.3 %collective-permute-start.13 = (bf16[16,1152]{1,0:T(8,128)(2,1)S(1)}, bf16[16,1152]{1,0:T(8,128)(2,1)S(1)}, u32[]{:S(2)}, u32[]{:S(2)}) collective-permute-start(bf16[16,1152]{1,0:T(8,128)(2,1)S(1)} %get-tuple-element.25), channel_id=1, source_target_pairs={{0,4},{4,0},{8,12},{12,8},{16,20},{20,16},{24,28},{28,24},{1,5},{5... | collective-permute-start | bytes 110600 | tf_op jit(solution)/shard_map/ppermute | solution.py:37
